TPU v7x, 32 devices: a whole 2x2x4 slice. The times are simulated.
32 devices in a mesh: dp: 8 (over y, x, core), context: 4 (over z).
Axes of the slice: x: 2, y: 2, z: 4, core: 2. Of those that a mesh axis runs over, the one named last changes fastest.
Arguments:
- span_order: int32 [8, 4], P('dp'), may hold values from 0 to 3, each once within a row
- queries: bfloat16 [12288, 1024], P(('dp', 'context')), may hold values from -9 to 9
- keys: bfloat16 [12288, 128], P(('dp', 'context')), may hold values from -6 to 6
- values: bfloat16 [12288, 128], P(('dp', 'context')), may hold values from -6 to 6
- out_grad: bfloat16 [12288, 1024], P(('dp', 'context')), may hold values from -6 to 6
- activations: bfloat16 [12288, 8192], P(('dp', 'context')), may hold values from -6 to 6
- error_feedback: float32 [8, 4, 8192, 256], P('dp', 'context')
Outputs:
- query_grad: bfloat16 [12288, 1024], P(('dp', 'context'))
- key_grad: bfloat16 [12288, 128], P(('dp', 'context'))
- value_grad: bfloat16 [12288, 128], P(('dp', 'context'))
- payload: float32 [8192, 256], P(('dp', 'context'))
- block_scale: float32 [256], replicated
Inputs may be any that keep to these rules, and one draw needn't show every extreme that they name: `span_order`: each row is a permutation: the indices of context hold the blocks of a sequence in the order that the row gives.
All inputs are finite; a program needn't handle non-finite values.
Results may differ from a plain program's by a relative error of at most 0.0061.
Values may be sent and summed in bfloat16 or wider, within the bound.
No kernel may reach another device: no remote copies, remote signals or barrier semaphores. Data moves between devices by JAX's collectives and lax.ppermute only.
A program may use at most 128 MiB of HBM per device.

v0:
```python
import jax
import jax.numpy as jnp
from jax import lax
from jax.sharding import PartitionSpec as P

QROWS = 32


def head_backward(query_head, all_keys, all_values, grad_head, query_positions, key_positions):
    inverse = 1.0 / query_head.shape[1] ** 0.5
    scores = jnp.dot(query_head, all_keys.T, preferred_element_type=jnp.float32) * inverse
    allowed = key_positions[None, :] <= query_positions[:, None]
    scores = jnp.where(allowed, scores, -jnp.inf)
    row_top = jnp.max(scores, axis=1, keepdims=True)
    expo_terms = jnp.exp(scores - row_top)
    probs = expo_terms / jnp.sum(expo_terms, axis=1, keepdims=True)
    prob_grad = jnp.dot(grad_head, all_values.T, preferred_element_type=jnp.float32)
    row_delta = jnp.sum(probs * prob_grad, axis=1, keepdims=True)
    score_grad = (probs * (prob_grad - row_delta)).astype(jnp.bfloat16)
    probs_low = probs.astype(jnp.bfloat16)
    query_part = jnp.dot(score_grad, all_keys, preferred_element_type=jnp.float32) * inverse
    key_part = jnp.dot(score_grad.T, query_head, preferred_element_type=jnp.float32) * inverse
    value_part = jnp.dot(probs_low.T, grad_head, preferred_element_type=jnp.float32)
    return (query_part, key_part, value_part)


def local(span_order, queries, keys, values, out_grad, activations, error_feedback):
    rows_local = queries.shape[0]
    head_dim = keys.shape[1]
    head_count = queries.shape[1] // head_dim
    context_index = lax.axis_index("context")
    offsets = jnp.arange(rows_local, dtype=jnp.int32)
    span_row = span_order[0]
    query_positions = span_row[context_index] * rows_local + offsets
    key_positions = (span_row[:, None] * rows_local + offsets[None, :]).reshape(-1)
    all_keys, all_values = (
        lax.all_gather(keys, "context", axis=0, tiled=True),
        lax.all_gather(values, "context", axis=0, tiled=True),
    )

    def one_head(totals, head_index):
        column_start = head_index * head_dim
        query_head = lax.dynamic_slice_in_dim(queries, column_start, head_dim, 1)
        grad_head = lax.dynamic_slice_in_dim(out_grad, column_start, head_dim, 1)
        query_part, key_part, value_part = head_backward(
            query_head, all_keys, all_values, grad_head, query_positions, key_positions
        )
        return ((totals[0] + key_part, totals[1] + value_part), query_part.astype(jnp.bfloat16))

    zero_rows = jnp.zeros((all_keys.shape[0], head_dim), jnp.float32)
    (key_terms, value_terms), query_parts = lax.scan(
        one_head, (zero_rows, zero_rows), jnp.arange(head_count, dtype=jnp.int32)
    )
    query_grad = jnp.transpose(query_parts, (1, 0, 2)).reshape(rows_local, head_count * head_dim)
    key_sum, value_sum = (
        lax.psum_scatter(key_terms, "context", scatter_dimension=0, tiled=True),
        lax.psum_scatter(value_terms, "context", scatter_dimension=0, tiled=True),
    )
    key_grad = key_sum.astype(jnp.bfloat16)
    value_grad = value_sum.astype(jnp.bfloat16)
    pair_grads = jnp.concatenate([key_grad, value_grad], axis=1)
    corrected = (
        lax.dot_general(
            activations, pair_grads, (((0,), (0,)), ((), ())), preferred_element_type=jnp.float32
        )
        + error_feedback[0, 0]
    )
    model_rows = corrected.shape[0]
    pair_width = corrected.shape[1]
    local_top = jnp.max(jnp.abs(corrected).reshape(model_rows // QROWS, QROWS * pair_width), axis=1)
    block_max = lax.pmax(local_top, ("dp", "context"))
    block_scale = block_max + 1e-06
    row_factor = jnp.repeat(7.0 / block_scale, QROWS)
    normalized = lax.optimization_barrier((corrected * row_factor[:, None]).astype(jnp.bfloat16))
    terms = normalized.astype(jnp.float32)
    payload = lax.psum_scatter(terms, ("dp", "context"), scatter_dimension=0, tiled=True)
    return (query_grad, key_grad, value_grad, payload, block_scale)


def solution(mesh):
    return jax.shard_map(
        local,
        mesh=mesh,
        in_specs=(
            P("dp", None),
            P(("dp", "context"), None),
            P(("dp", "context"), None),
            P(("dp", "context"), None),
            P(("dp", "context"), None),
            P(("dp", "context"), None),
            P("dp", "context", None, None),
        ),
        out_specs=(
            P(("dp", "context"), None),
            P(("dp", "context"), None),
            P(("dp", "context"), None),
            P(("dp", "context"), None),
            P(),
        ),
        check_vma=False,
    )
```

profile of v0, /device:TPU:0, one launch (start us, length us, event | category | flops | bytes accessed | tf_op | source)
XLA Modules:
  0.0 428.5 jit_solution(14213727847953316521)
XLA Ops:
  9.1 16.4 %all_gather.6 = bf16[1536,128]{1,0:T(8,128)(2,1)S(1)} all-gather(bf16[384,128]{1,0:T(8,128)(2,1)} %param.11), channel_id=1, replica_groups=mesh['dp'=8,'context'=4] {'context'}, dimensions={0}, use_global_device_ids=true | all-gather | bytes 491520 | tf_op jit(solution)/shard_map/all_gather | solution.py:37
  25.6 15.8 %all_gather.7 = bf16[1536,128]{1,0:T(8,128)(2,1)S(1)} all-gather(bf16[384,128]{1,0:T(8,128)(2,1)} %param.12), channel_id=1, replica_groups=mesh['dp'=8,'context'=4] {'context'}, dimensions={0}, use_global_device_ids=true | all-gather | bytes 491520 | tf_op jit(solution)/shard_map/all_gather | solution.py:38
  41.4 83.0 %while.15 = (s32[]{:T(128)}, f32[1536,128]{1,0:T(8,128)S(1)}, f32[1536,128]{1,0:T(8,128)S(1)}, bf16[8,384,128]{2,1,0:T(8,128)(2,1)S(1)}, s32[8]{0:T(128)S(1)}, /...) while((s32[]{:T(128)}, f32[1536,128]{1,0:T(8,128)S(1)}, ...), condition=%wide.region_4.5_spmd.clone, body=%wide.region_0.4_spmd.clone.sunk | while | flops 766673664 | bytes 24915712 | solution.py:51
  45.3 1.9 convolution_add_fusion.2
  49.5 1.7 fusion.58
  55.7 1.9 convolution_add_fusion.2
  57.6 1.6 multiply_reduce_fusion.2
  59.9 1.7 fusion.58
  66.1 1.9 convolution_add_fusion.2
  70.3 1.7 fusion.58
  76.4 1.9 convolution_add_fusion.2
  78.4 1.6 multiply_reduce_fusion.2
  80.6 1.7 fusion.58
  86.8 1.9 convolution_add_fusion.2
  88.7 1.6 multiply_reduce_fusion.2
  91.0 1.7 fusion.58
  97.2 1.9 convolution_add_fusion.2
  101.4 1.7 fusion.58
  107.6 1.9 convolution_add_fusion.2
  111.8 1.7 fusion.58
  117.9 1.9 convolution_add_fusion.2
  119.9 1.6 multiply_reduce_fusion.2
  122.1 1.7 fusion.58
  126.1 9.0 %copy.16 = f32[1,1,8192,256]{2,3,1,0:T(8,128)} copy(f32[1,1,8192,256]{3,2,1,0:T(8,128)} %param.15) | data formatting | bytes 16777216 | tf_op args[6]
  135.0 14.6 %reduce-scatter.4.cloned.1.call-done = f32[384,128]{1,0:T(8,128)} async-done(((f32[1536,128]{1,0:T(8,128)}), f32[384,128]{1,0:T(8,128)}) %reduce-scatter.4.cloned.1.call-update) | async-done | bytes 196624 | tf_op jit(solution)/shard_map/reduce_scatter | solution.py:56
  150.6 23.9 %reduce-scatter.6.cloned.1.call-done = f32[384,128]{1,0:T(8,128)} async-done(((f32[1536,128]{1,0:T(8,128)}), f32[384,128]{1,0:T(8,128)}) %reduce-scatter.6.cloned.1.call-update) | async-done | bytes 196624 | tf_op jit(solution)/shard_map/reduce_scatter | solution.py:57
  175.5 10.8 %abs_reduce_fusion = (f32[8192]{0:T(1024)S(1)}, f32[8192,256]{0,1:T(8,128)}) fusion(f32[1,1,8192,256]{2,3,1,0:T(8,128)} %copy.16, bf16[384,8192]{1,0:T(8,128)(2,1)} %param.14, bf16[384,128]{1,0:T(8,128)(2,1)S(1)} %convert_element_type.22, bf16[384,128]{1,0:T(8,128)(2,1)S(1)} %convert_element_type.21), kind=kOutput, calls=%fused_computation.31 | convolution fusion | flops 1617289216 | bytes 23298048 | tf_op jit(solution)/shard_map/dot_general | solution.py:63
  186.5 38.7 %pmax.7 = f32[256]{0:T(256)S(1)} all-reduce(f32[256]{0:T(256)S(1)} %reduce_max.27), channel_id=1, replica_groups=mesh['dp'=8,'context'=4] {'dp','context'}, use_global_device_ids=true, to_apply=%region_9.10 | all-reduce | flops 256 | bytes 2048 | tf_op jit(solution)/shard_map/pmax | solution.py:71
  226.0 4.1 multiply_convert_fusion.1
  230.1 4.2 convert_element_type.24
  235.3 184.8 %reduce-scatter.8.cloned.1.call-done = f32[256,256]{0,1:T(8,128)} async-done(((f32[8192,256]{0,1:T(8,128)}), f32[256,256]{0,1:T(8,128)}) %reduce-scatter.8.cloned.1.call-update) | async-done | bytes 262160 | tf_op jit(solution)/shard_map/reduce_scatter | solution.py:76
  420.2 1.8 copy.17
  (96 shorter events, 49.3 us)
Async XLA Ops:
  7.2 142.5 %reduce-scatter.4.cloned.1.call-start = ((), (), s32[]{:S(2)}) async-start(), calls=%async_computation.3 | async-start | bytes 983040 | tf_op jit(solution)/shard_map/reduce_scatter | solution.py:56
  124.4 0.9 copy-start
  124.4 1.2 copy-start.1
  125.3 49.3 %reduce-scatter.6.cloned.1.call-start = ((), (), s32[]{:S(2)}) async-start(), calls=%async_computation.4 | async-start | bytes 983040 | tf_op jit(solution)/shard_map/reduce_scatter | solution.py:57
  126.0 294.1 %reduce-scatter.8.cloned.1.call-start = ((), (), s32[]{:S(2)}) async-start(), calls=%async_computation.5 | async-start | bytes 8650752 | tf_op jit(solution)/shard_map/reduce_scatter | solution.py:76
  150.6 35.8 %copy-start.2 = (bf16[384,128]{1,0:T(8,128)(2,1)}, bf16[384,128]{1,0:T(8,128)(2,1)S(1)}, u32[]{:S(2)}) copy-start(bf16[384,128]{1,0:T(8,128)(2,1)S(1)} %convert_element_type.21) | copy-start | bytes 294916
  175.5 10.9 %copy-start.3 = (bf16[384,128]{1,0:T(8,128)(2,1)}, bf16[384,128]{1,0:T(8,128)(2,1)S(1)}, u32[]{:S(2)}) copy-start(bf16[384,128]{1,0:T(8,128)(2,1)S(1)} %convert_element_type.22) | copy-start | bytes 294916
Sparse Core Ops, SparseCore 0:
  125.4 24.2 reduce-scatter.3
  151.9 22.5 reduce-scatter.5
  234.4 185.6 reduce-scatter.7
where the time goes:
time: 430 us; the launch traced here: 428 us
  waiting for transfers between devices  224 us (52%)
  blocking collectives  70.9 us (16%)
  matrix products  68.7 us (16%)
  other arithmetic  27.4 us (6%)
  local copies, waits for them, and re-layouts  17.9 us (4%)
  between operations  13.9 us (3%)
  loops' own time  5.67 us (1%)
    reduce_scatter x1, waiting for transfers between devices, local(): lax.psum_scatter(terms, ('dp', 'context'), scatter_dimension=0, tiled=True)  185 us
    pmax x1, blocking collectives, local(): block_max = lax.pmax(local_top, ('dp', 'context'))  38.7 us
    reduce_scatter x1, waiting for transfers between devices, local(): lax.psum_scatter(value_terms, 'context', scatter_dimension=0, tiled=True)  23.9 us
    all_gather x1, blocking collectives, local(): lax.all_gather(keys, 'context', axis=0, tiled=True)  16.4 us
    all_gather x1, blocking collectives, local(): lax.all_gather(values, 'context', axis=0, tiled=True)  15.8 us
    dot_general x8, matrix products, head_backward(): jnp.dot(probs_low.T, grad_head, preferred_element_type=jnp.float32)  15.3 us
    reduce_scatter x1, waiting for transfers between devices, local(): lax.psum_scatter(key_terms, 'context', scatter_dimension=0, tiled=True)  14.6 us
    dot_general x8, matrix products, head_backward(): jnp.dot(score_grad.T, query_head, preferred_element_type=jnp.float32)  13.5 us
  transfers between devices with their start and end apart: 3, of which 3 were waited for; matrix products, arithmetic and copies ran while one was open for 3% of the time, Pallas kernels for 0%

commit v1 on v0

v1 whole, which is shorter than its diff:
```python
import functools

import jax
import jax.numpy as jnp
from jax import lax
from jax.experimental import pallas as pl
from jax.experimental.pallas import tpu as pltpu
from jax.sharding import PartitionSpec as P

QROWS = 32
LOG2E = 1.4426950408889634
FAR = 1e30
MIB = 1024 * 1024


def xor_perm(size, mask):
    return [(i, i ^ mask) for i in range(size)]


def attention_kernel(n_blocks, keep_ref, q_ref, do_ref, *refs):
    k_refs, v_refs = refs[:n_blocks], refs[n_blocks : 2 * n_blocks]
    dq_ref, own_ref, other_ref, k_all, v_all, q_cat, do_cat, p_buf, ds_buf, dk_acc, dv_acc = refs[2 * n_blocks :]
    rows, hd = k_refs[0].shape
    inverse = 1.0 / hd**0.5
    factor = inverse * LOG2E
    step = pl.program_id(0)
    width = 256
    f32 = jnp.float32

    @pl.when(step == 0)
    def _():
        for b in range(n_blocks):
            k_all[b * rows : (b + 1) * rows, :] = k_refs[b][...]
            v_all[b * rows : (b + 1) * rows, :] = v_refs[b][...]
        dk_acc[...] = jnp.zeros_like(dk_acc)
        dv_acc[...] = jnp.zeros_like(dv_acc)

    for h in range(2):
        q_cat[h * rows : (h + 1) * rows, :] = q_ref[:, h * hd : (h + 1) * hd]
        do_cat[h * rows : (h + 1) * rows, :] = do_ref[:, h * hd : (h + 1) * hd]

    for t in range(2 * rows // width):
        lanes = slice(t * width, (t + 1) * width)
        qc, dc = q_cat[lanes, :], do_cat[lanes, :]
        nt = (((1,), (1,)), ((), ()))
        s = [
            lax.dot_general(k_all[b * rows : (b + 1) * rows, :], qc, nt, preferred_element_type=f32)
            for b in range(n_blocks)
        ]
        dp = [
            lax.dot_general(v_all[b * rows : (b + 1) * rows, :], dc, nt, preferred_element_type=f32)
            for b in range(n_blocks)
        ]
        key_at = lax.broadcasted_iota(jnp.int32, (rows, width), 0)
        query_at = lax.broadcasted_iota(jnp.int32, (rows, width), 1) + t * width
        query_at = jnp.where(query_at >= rows, query_at - rows, query_at)
        s[0] = jnp.where(key_at <= query_at, s[0], -FAR)
        top = jnp.max(s[0], axis=0, keepdims=True)
        for b in range(1, n_blocks):
            block_top = jnp.max(s[b], axis=0, keepdims=True)
            top = jnp.maximum(top, jnp.where(keep_ref[b] > 0, block_top, -FAR))
        top = top * factor
        e, total, weighted = [], 0.0, 0.0
        for b in range(n_blocks):
            shift = top if b == 0 else jnp.where(keep_ref[b] > 0, top, FAR)
            e_b = jnp.exp2(s[b] * factor - shift)
            total = total + jnp.sum(e_b, axis=0, keepdims=True)
            weighted = weighted + jnp.sum(e_b * dp[b], axis=0, keepdims=True)
            e.append(e_b)
        inv = 1.0 / total
        delta = weighted * inv
        for b in range(n_blocks):
            p = e[b] * inv
            p_buf[b * rows : (b + 1) * rows, lanes] = p.astype(jnp.bfloat16)
            ds_buf[b * rows : (b + 1) * rows, lanes] = (p * (dp[b] - delta)).astype(jnp.bfloat16)

    dk_acc[...] += jnp.dot(ds_buf[...], q_cat[...], preferred_element_type=f32)
    dv_acc[...] += jnp.dot(p_buf[...], do_cat[...], preferred_element_type=f32)
    dq = lax.dot_general(ds_buf[...], k_all[...], (((0,), (0,)), ((), ())), preferred_element_type=f32) * inverse
    for h in range(2):
        dq_ref[:, h * hd : (h + 1) * hd] = dq[h * rows : (h + 1) * rows, :].astype(jnp.bfloat16)

    @pl.when(step == pl.num_programs(0) - 1)
    def _():
        own_ref[:, :hd] = dk_acc[:rows, :] * inverse
        own_ref[:, hd:] = dv_acc[:rows, :]
        for b in range(1, n_blocks):
            part = slice(b * rows, (b + 1) * rows)
            other_ref[b - 1, :, :hd] = (dk_acc[part, :] * inverse).astype(jnp.bfloat16)
            other_ref[b - 1, :, hd:] = dv_acc[part, :].astype(jnp.bfloat16)


def attention(keep, queries, out_grad, k_blocks, v_blocks):
    n = len(k_blocks)
    rows, hd = k_blocks[0].shape
    heads = queries.shape[1] // hd
    whole = pl.BlockSpec((rows, hd), lambda i, *_: (0, 0))
    pair = pl.BlockSpec((rows, 2 * hd), lambda i, *_: (0, i))
    bf16, f32 = jnp.bfloat16, jnp.float32
    return pl.pallas_call(
        functools.partial(attention_kernel, n),
        grid_spec=pltpu.PrefetchScalarGridSpec(
            num_scalar_prefetch=1,
            grid=(heads // 2,),
            in_specs=[pair, pair] + [whole] * (2 * n),
            out_specs=[
                pair,
                pl.BlockSpec((rows, 2 * hd), lambda i, *_: (0, 0)),
                pl.BlockSpec((n - 1, rows, 2 * hd), lambda i, *_: (0, 0, 0)),
            ],
            scratch_shapes=[
                pltpu.VMEM((n * rows, hd), bf16),
                pltpu.VMEM((n * rows, hd), bf16),
                pltpu.VMEM((2 * rows, hd), bf16),
                pltpu.VMEM((2 * rows, hd), bf16),
                pltpu.VMEM((n * rows, 2 * rows), bf16),
                pltpu.VMEM((n * rows, 2 * rows), bf16),
                pltpu.VMEM((n * rows, hd), f32),
                pltpu.VMEM((n * rows, hd), f32),
            ],
        ),
        out_shape=[
            jax.ShapeDtypeStruct(queries.shape, bf16),
            jax.ShapeDtypeStruct((rows, 2 * hd), f32),
            jax.ShapeDtypeStruct((n - 1, rows, 2 * hd), bf16),
        ],
        compiler_params=pltpu.CompilerParams(vmem_limit_bytes=48 * MIB),
        cost_estimate=pl.CostEstimate(
            flops=10 * rows * n * rows * hd * heads, bytes_accessed=6 * rows * heads * hd, transcendentals=n * rows * rows * heads
        ),
        name="attention_backward",
    )(keep, queries, out_grad, *k_blocks, *v_blocks)


def corrected_kernel(n_parts, shrink, with_grads, side_ref, *refs):
    own_ref, part_refs = refs[0], refs[1 : n_parts + 1]
    a_ref, e_ref, *outs = refs[n_parts + 1 :]
    if with_grads:
        low_ref, high_ref, top_ref, kg_ref, vg_ref, grads = outs
    else:
        low_ref, high_ref, top_ref, grads = outs
    hd = low_ref.shape[-1]

    @pl.when(pl.program_id(0) == 0)
    def _():
        total = own_ref[...]
        for part in part_refs:
            total = total + part[...].astype(jnp.float32)
        total = total.astype(jnp.bfloat16)
        grads[...] = total
        if with_grads:
            kg_ref[...] = total[:, :hd]
            vg_ref[...] = total[:, hd:]

    c = lax.dot_general(a_ref[...], grads[...], (((0,), (0,)), ((), ())), preferred_element_type=jnp.float32)
    c = c + e_ref[...]
    tile = c.shape[0]
    mags = jnp.max(jnp.abs(c).reshape(tile // QROWS, QROWS, c.shape[1]), axis=1)
    top_ref[0] = jnp.max(mags.T, axis=0, keepdims=True)
    low = (c * shrink).astype(jnp.bfloat16)
    low_ref[0] = low[:, :hd]
    high_ref[0] = low[:, hd:]


def corrected_tiles(side, own, parts, activations, errors, n_dp, shrink, with_grads):
    rows, width = own.shape
    model = activations.shape[1]
    tile = model // n_dp
    hd = width // 2
    whole = pl.BlockSpec((rows, width), lambda i, side: (0, 0))
    half = pl.BlockSpec((1, tile, hd), lambda i, side: (i, 0, 0))
    bf16, f32 = jnp.bfloat16, jnp.float32
    out_specs = [half, half, pl.BlockSpec((1, 1, tile // QROWS), lambda i, side: (i, 0, 0))]
    out_shape = [
        jax.ShapeDtypeStruct((n_dp // 2, tile, hd), bf16),
        jax.ShapeDtypeStruct((n_dp // 2, tile, hd), bf16),
        jax.ShapeDtypeStruct((n_dp // 2, 1, tile // QROWS), f32),
    ]
    if with_grads:
        out_specs += [pl.BlockSpec((rows, hd), lambda i, side: (0, 0))] * 2
        out_shape += [jax.ShapeDtypeStruct((rows, hd), bf16)] * 2
    return pl.pallas_call(
        functools.partial(corrected_kernel, len(parts), shrink, with_grads),
        grid_spec=pltpu.PrefetchScalarGridSpec(
            num_scalar_prefetch=1,
            grid=(n_dp // 2,),
            in_specs=[whole] * (1 + len(parts))
            + [
                pl.BlockSpec((rows, tile), lambda i, side: (0, 2 * i + side[0])),
                pl.BlockSpec((tile, width), lambda i, side: (2 * i + side[0], 0)),
            ],
            out_specs=out_specs,
            scratch_shapes=[pltpu.VMEM((rows, width), bf16)],
        ),
        out_shape=out_shape,
        compiler_params=pltpu.CompilerParams(vmem_limit_bytes=48 * MIB),
        cost_estimate=pl.CostEstimate(
            flops=rows * width * model, bytes_accessed=rows * model + 3 * width * model, transcendentals=0
        ),
        name="corrected_tiles",
    )(side, own, *parts, activations, errors)


def add_low(a, b):
    return (a.astype(jnp.float32) + b.astype(jnp.float32)).astype(jnp.bfloat16)


def local(n_dp, n_ctx, span_order, queries, keys, values, out_grad, activations, error_feedback):
    hd = keys.shape[1]
    me_dp, me_ctx = lax.axis_index("dp"), lax.axis_index("context")
    dp_bits = n_dp.bit_length() - 1

    def swap_dp(x, bit):
        return lax.ppermute(x, "dp", xor_perm(n_dp, 1 << bit))

    def swap_ctx(x, mask):
        return lax.ppermute(x, "context", xor_perm(n_ctx, mask))

    k_blocks = [keys] + [swap_ctx(keys, b) for b in range(1, n_ctx)]
    v_blocks = [values] + [swap_ctx(values, b) for b in range(1, n_ctx)]
    spans = span_order[0]
    block_spans = spans[me_ctx ^ jnp.arange(n_ctx, dtype=jnp.int32)]
    keep = (block_spans < block_spans[0]).astype(jnp.int32)
    query_grad, own, others = attention(keep, queries, out_grad, k_blocks, v_blocks)

    parts = [swap_ctx(others[b - 1], b) for b in range(1, n_ctx)]
    shrink = 1.0 / (n_dp * n_ctx)
    errors = error_feedback[0, 0]
    side = (me_dp & 1).astype(jnp.int32)
    send_low, send_high, send_top, key_grad, value_grad = corrected_tiles(
        (1 - side)[None], own, parts, activations, errors, n_dp, shrink, True
    )
    got = (swap_dp(send_low, 0), swap_dp(send_high, 0))
    keep_low, keep_high, keep_top = corrected_tiles(
        side[None], own, parts, activations, errors, n_dp, shrink, False
    )

    send_top, keep_top = send_top[:, 0], keep_top[:, 0]
    first = jnp.where(side == 0, keep_top, send_top)
    second = jnp.where(side == 0, send_top, keep_top)
    tops = jnp.stack([first, second], axis=1).reshape(-1)
    for bit in range(dp_bits):
        tops = jnp.maximum(tops, swap_dp(tops, bit))
    mask = 1
    while mask < n_ctx:
        tops = jnp.maximum(tops, swap_ctx(tops, mask))
        mask *= 2
    block_scale = tops + 1e-06

    results = []
    for half, (kept, received) in enumerate(zip((keep_low, keep_high), got)):
        current = add_low(kept, received)
        bits = list(range(1, dp_bits))
        current = current.reshape((2,) * len(bits) + current.shape[1:])
        order = bits if half == 0 else bits[::-1]
        left = bits[::-1]
        for bit in order:
            axis = left.index(bit)
            mine = (me_dp >> bit) & 1
            away = lax.dynamic_index_in_dim(current, 1 - mine, axis, keepdims=False)
            stay = lax.dynamic_index_in_dim(current, mine, axis, keepdims=False)
            current = add_low(stay, swap_dp(away, bit))
            left.remove(bit)
        chunks = current.reshape(n_ctx, -1, hd)
        total = lax.dynamic_index_in_dim(chunks, me_ctx, 0, keepdims=False).astype(jnp.float32)
        for b in range(1, n_ctx):
            away = lax.dynamic_index_in_dim(chunks, me_ctx ^ b, 0, keepdims=False)
            total = total + swap_ctx(away, b).astype(jnp.float32)
        results.append(total)
    own_blocks = block_scale.shape[0] // (n_dp * n_ctx)
    own_scale = lax.dynamic_slice_in_dim(block_scale, (me_dp * n_ctx + me_ctx) * own_blocks, own_blocks)
    row_factor = jnp.repeat((7.0 / shrink) / own_scale, QROWS)
    payload = jnp.concatenate(results, axis=1) * row_factor[:, None]
    return (query_grad, key_grad, value_grad, payload, block_scale)


def solution(mesh):
    tokens = P(("dp", "context"), None)
    return jax.shard_map(
        functools.partial(local, mesh.shape["dp"], mesh.shape["context"]),
        mesh=mesh,
        in_specs=(P("dp", None), tokens, tokens, tokens, tokens, tokens, P("dp", "context", None, None)),
        out_specs=(tokens, tokens, tokens, tokens, P()),
        check_vma=False,
    )
```

time: 430 us -> 135 us (0.31)
  waiting for transfers between devices: 224 us -> 56 us
  blocking collectives: 70.9 us -> 0 us
  matrix products: 68.7 us -> 0 us
  starting transfers between devices: 0.12 us -> 37.2 us
  Pallas kernels: 0 us -> 30.7 us
  other arithmetic: 27.4 us -> 3.58 us
  between operations: 13.9 us -> 0.83 us
  local copies, waits for them, and re-layouts: 17.9 us -> 6.76 us
  loops' own time: 5.67 us -> 0 us
    reduce_scatter x3 -> x0, waiting for transfers between devices: 223 us -> none  [the longest x1 185 us: local(): lax.psum_scatter(terms, ('dp', 'context'), scatter_dimension=0, tiled=True)]
    dot_general x41 -> x0, matrix products: 68.7 us -> none  [the longest x8 15.3 us: head_backward(): jnp.dot(probs_low.T, grad_head, preferred_element_type=jnp.float32)]
    ppermute x0 -> x26, waiting for transfers between devices: none -> 56 us  [the longest x17 30.3 us: swap_ctx(): return lax.ppermute(x, 'context', xor_perm(n_ctx, mask))]
    pmax x1 -> x0, blocking collectives: 38.7 us -> none  [local(): block_max = lax.pmax(local_top, ('dp', 'context'))]
    ppermute x0 -> x26, starting transfers between devices: none -> 37.2 us  [the longest x17 29.2 us: swap_ctx(): return lax.ppermute(x, 'context', xor_perm(n_ctx, mask))]
    all_gather x2 -> x0, blocking collectives: 32.2 us -> none  [the longest x1 16.4 us: local(): lax.all_gather(keys, 'context', axis=0, tiled=True)]
    pallas_call x0 -> x3, Pallas kernels: none -> 30.7 us  [the longest x1 20.2 us: attention(): pl.pallas_call(functools.partial(attention_kernel, n), grid_spec=pltpu.Pr...]
    convert_element_type x12 -> x6, other arithmetic: 15.3 us -> 2.58 us  [the longest x5 2.54 us: add_low(): return (a.astype(jnp.float32) + b.astype(jnp.float32)).astype(jnp.bfloat16)]
  transfers between devices with their start and end apart: 3 -> 26, of which waited for: 3 -> 12; matrix products, arithmetic and copies ran while one was open for 3% -> 2% of each run, Pallas kernels for 0% -> 4%
where the time goes in v1:
time: 135 us
  waiting for transfers between devices  56 us (41%)
  starting transfers between devices  37.2 us (28%)
  Pallas kernels  30.7 us (23%)
  local copies, waits for them, and re-layouts  6.76 us (5%)
  other arithmetic  3.58 us (3%)
    ppermute x17, waiting for transfers between devices, swap_ctx(): return lax.ppermute(x, 'context', xor_perm(n_ctx, mask))  30.3 us
    ppermute x17, starting transfers between devices, swap_ctx(): return lax.ppermute(x, 'context', xor_perm(n_ctx, mask))  29.2 us
    ppermute x9, waiting for transfers between devices, swap_dp(): return lax.ppermute(x, 'dp', xor_perm(n_dp, 1 << bit))  25.7 us
    pallas_call x1, Pallas kernels, attention(): pl.pallas_call(functools.partial(attention_kernel, n), grid_spec=pltpu.Pr...  20.2 us
    pallas_call x2, Pallas kernels, corrected_tiles(): pl.pallas_call(functools.partial(corrected_kernel, len(parts), shrink, wi...  10.5 us
    ppermute x9, starting transfers between devices, swap_dp(): return lax.ppermute(x, 'dp', xor_perm(n_dp, 1 << bit))  7.94 us
    unnamed x12, local copies, waits for them, and re-layouts  4.06 us
  transfers between devices with their start and end apart: 26, of which 12 were waited for; matrix products, arithmetic and copies ran while one was open for 2% of the time, Pallas kernels for 4%

profile of v1, /device:TPU:0, one launch (start us, length us, event | category | flops | bytes accessed | tf_op | source)
XLA Modules:
  0.0 135.0 jit_solution(1691732355282140549)
XLA Ops:
  0.6 3.1 %collective-permute-start = (bf16[384,128]{1,0:T(8,128)(2,1)}, bf16[384,128]{1,0:T(8,128)(2,1)S(1)}, u32[]{:S(2)}, u32[]{:S(2)}) collective-permute-start(bf16[384,128]{1,0:T(8,128)(2,1)} %refs_0_.1), channel_id=1, source_target_pairs={{0,1},{1,0},{2,3},{3,2},{4,5},{5,4},{6,7},{7,6},{8,9},{9,8},{10,11... | collective-permute-start | bytes 294920 | tf_op jit(solution)/shard_map/ppermute | solution.py:217
  3.7 2.6 %collective-permute-start.1 = (bf16[384,128]{1,0:T(8,128)(2,1)}, bf16[384,128]{1,0:T(8,128)(2,1)S(1)}, u32[]{:S(2)}, u32[]{:S(2)}) collective-permute-start(bf16[384,128]{1,0:T(8,128)(2,1)} %refs_0_.1), channel_id=1, source_target_pairs={{0,2},{1,3},{2,0},{3,1},{4,6},{5,7},{6,4},{7,5},{8,10},{9,11},{10,... | collective-permute-start | bytes 294920 | tf_op jit(solution)/shard_map/ppermute | solution.py:217
  7.2 3.5 %collective-permute-start.4 = (bf16[384,128]{1,0:T(8,128)(2,1)}, bf16[384,128]{1,0:T(8,128)(2,1)S(1)}, u32[]{:S(2)}, u32[]{:S(2)}) collective-permute-start(bf16[384,128]{1,0:T(8,128)(2,1)} %refs_4_.3), channel_id=1, source_target_pairs={{0,2},{1,3},{2,0},{3,1},{4,6},{5,7},{6,4},{7,5},{8,10},{9,11},{10,... | collective-permute-start | bytes 294920 | tf_op jit(solution)/shard_map/ppermute | solution.py:217
  11.6 3.0 %collective-permute-done.1.refs_2_ = bf16[384,128]{1,0:T(8,128)(2,1)S(1)} collective-permute-done((bf16[384,128]{1,0:T(8,128)(2,1)}, bf16[384,128]{1,0:T(8,128)(2,1)S(1)}, u32[]{:S(2)}, u32[]{:S(2)}) %collective-permute-start.1) | collective-permute-done | bytes 98336 | tf_op jit(solution)/shard_map/ppermute | solution.py:217
  14.6 8.2 %collective-permute-done.4.refs_6_ = bf16[384,128]{1,0:T(8,128)(2,1)S(1)} collective-permute-done((bf16[384,128]{1,0:T(8,128)(2,1)}, bf16[384,128]{1,0:T(8,128)(2,1)S(1)}, u32[]{:S(2)}, u32[]{:S(2)}) %collective-permute-start.4) | collective-permute-done | bytes 98336 | tf_op jit(solution)/shard_map/ppermute | solution.py:217
  22.8 1.1 copy-done.1
  24.0 1.1 copy-done.2
  26.9 20.2 %attention_backward.1 = (bf16[384,1024]{1,0:T(8,128)(2,1)}, f32[384,256]{1,0:T(8,128)S(1)}, bf16[3,384,256]{2,1,0:T(8,128)(2,1)S(1)}) custom-call(s32[4]{0:T(128)S(1)} %compare_convert_fusion.keep_ref, bf16[384,1024]{1,0:T(8,128)(2,1)S(1)} %copy-done.1, bf16[384,1024]{1,0:T(8,128)(2,1)S(1)} %copy-done.2, bf16[384,128]{1,0:T(8,128)(2,1)S(1)} %copy-done.3, ...), custom_call_target="tpu_custom_call" | custom-call | flops 6039797760 | bytes 2359296 | tf_op jit(solution)/shard_map/attention_backward/pallas_call | solution.py:100
  47.1 1.7 %collective-permute-start.6 = (bf16[384,256]{1,0:T(8,128)(2,1)S(1)}, bf16[384,256]{1,0:T(8,128)(2,1)S(1)}, u32[]{:S(2)}, u32[]{:S(2)}) collective-permute-start(bf16[384,256]{1,0:T(8,128)(2,1)S(1)} %get-tuple-element.29), channel_id=1, source_target_pairs={{0,1},{1,0},{2,3},{3,2},{4,5},{5,4},{6,7},{7,6},{8,9},{9,8},{10,11... | collective-permute-start | bytes 589832 | tf_op jit(solution)/shard_map/ppermute | solution.py:217
  48.8 1.4 %collective-permute-start.7 = (bf16[384,256]{1,0:T(8,128)(2,1)S(1)}, bf16[384,256]{1,0:T(8,128)(2,1)S(1)}, u32[]{:S(2)}, u32[]{:S(2)}) collective-permute-start(bf16[384,256]{1,0:T(8,128)(2,1)S(1)} %get-tuple-element.28), channel_id=1, source_target_pairs={{0,2},{1,3},{2,0},{3,1},{4,6},{5,7},{6,4},{7,5},{8,10},{9,11},{10,... | collective-permute-start | bytes 589832 | tf_op jit(solution)/shard_map/ppermute | solution.py:217
  50.2 1.4 %collective-permute-start.8 = (bf16[384,256]{1,0:T(8,128)(2,1)S(1)}, bf16[384,256]{1,0:T(8,128)(2,1)S(1)}, u32[]{:S(2)}, u32[]{:S(2)}) collective-permute-start(bf16[384,256]{1,0:T(8,128)(2,1)S(1)} %get-tuple-element.27), channel_id=1, source_target_pairs={{0,3},{1,2},{2,1},{3,0},{4,7},{5,6},{6,5},{7,4},{8,11},{9,10},{10,... | collective-permute-start | bytes 589832 | tf_op jit(solution)/shard_map/ppermute | solution.py:217
  51.6 3.8 %collective-permute-done.6.refs_1_ = bf16[384,256]{1,0:T(8,128)(2,1)S(1)} collective-permute-done((bf16[384,256]{1,0:T(8,128)(2,1)S(1)}, bf16[384,256]{1,0:T(8,128)(2,1)S(1)}, u32[]{:S(2)}, u32[]{:S(2)}) %collective-permute-start.6) | collective-permute-done | bytes 196640 | tf_op jit(solution)/shard_map/ppermute | solution.py:217
  55.4 10.1 %collective-permute-done.7.refs_2_ = bf16[384,256]{1,0:T(8,128)(2,1)S(1)} collective-permute-done((bf16[384,256]{1,0:T(8,128)(2,1)S(1)}, bf16[384,256]{1,0:T(8,128)(2,1)S(1)}, u32[]{:S(2)}, u32[]{:S(2)}) %collective-permute-start.7) | collective-permute-done | bytes 196640 | tf_op jit(solution)/shard_map/ppermute | solution.py:217
  65.5 5.5 %corrected_tiles.2 = (bf16[4,1024,128]{2,1,0:T(8,128)(2,1)S(1)}, bf16[4,1024,128]{2,1,0:T(8,128)(2,1)S(1)}, f32[4,1,32]{2,1,0:T(1,128)S(1)}, bf16[384,128]{1,0:T(8,128)(2,1)}, bf16[384,128]{1,0:T(8,128)(2,1)}) custom-call(s32[1]{0:T(128)} %bitcast.3.side_ref, f32[384,256]{1,0:T(8,128)S(1)} %get-tuple-element.17.refs_0_, ...), custom_call_target="tpu_custom_call" | custom-call | flops 805306368 | bytes 9437184 | tf_op jit(solution)/shard_map/corrected_tiles/pallas_call | solution.py:182
  71.5 5.0 %corrected_tiles.3 = (bf16[4,1024,128]{2,1,0:T(8,128)(2,1)S(1)}, bf16[4,1024,128]{2,1,0:T(8,128)(2,1)S(1)}, f32[4,1,32]{2,1,0:T(1,128)S(1)}) custom-call(s32[1]{0:T(128)} %bitcast.8.side_ref, f32[384,256]{1,0:T(8,128)S(1)} %get-tuple-element.17.refs_0_, bf16[384,256]{1,0:T(8,128)(2,1)S(1)} %collective-permute-done.6.refs_1_, ...), custom_call_target="tpu_custom_call" | custom-call | flops 805306368 | bytes 9437184 | tf_op jit(solution)/shard_map/corrected_tiles/pallas_call | solution.py:182
  76.5 2.1 %add_convert_fusion = (bf16[4,1024,128]{2,1,0:T(8,128)(2,1)S(1)}, bf16[4,1024,128]{2,1,0:T(8,128)(2,1)S(1)}) fusion(bf16[4,1024,128]{2,1,0:T(8,128)(2,1)} %collective-permute-done.15, bf16[4,1024,128]{2,1,0:T(8,128)(2,1)S(1)} %get-tuple-element.23, bf16[4,1024,128]{2,1,0:T(8,128)(2,1)} %collective-permute-done.9, bf16[4,1024,128]{2,1,0:T(8,128)(2,1)S(1)} %get-tuple-element.21), kind=kLoop, calls=%fused_computation.1 | loop fusion | flops 4194304 | bytes 6291456 | tf_op jit(solution)/shard_map/convert_element_type | solution.py:205
  79.5 1.5 %collective-permute-start.10 = (bf16[2,1024,128]{2,1,0:T(8,128)(2,1)}, bf16[2,1024,128]{2,1,0:T(8,128)(2,1)S(1)}, u32[]{:S(2)}, u32[]{:S(2)}) collective-permute-start(bf16[2,1024,128]{2,1,0:T(8,128)(2,1)} %dynamic-slice_bitcast_fusion.1), channel_id=1, source_target_pairs={{0,8},{4,12},{8,0},{12,4},{16,24},{20,28},{24,16},{28,20},{1,9},{5... | collective-permute-start | bytes 1572872 | tf_op jit(solution)/shard_map/ppermute | solution.py:214
  81.1 1.1 collective-permute-done.21
  82.7 10.8 %collective-permute-done.22 = f32[256]{0:T(256)S(1)} collective-permute-done((f32[256]{0:T(256)S(1)}, f32[256]{0:T(256)S(1)}, u32[]{:S(2)}, u32[]{:S(2)}) %collective-permute-start.22) | collective-permute-done | bytes 1056 | tf_op jit(solution)/shard_map/ppermute | solution.py:214
  93.6 1.5 %collective-permute-start.23 = (f32[256]{0:T(256)S(1)}, f32[256]{0:T(256)S(1)}, u32[]{:S(2)}, u32[]{:S(2)}) collective-permute-start(f32[256]{0:T(256)S(1)} %max.16), channel_id=1, source_target_pairs={{0,16},{4,20},{8,24},{12,28},{16,0},{20,4},{24,8},{28,12},{1,17},{... | collective-permute-start | bytes 3080 | tf_op jit(solution)/shard_map/ppermute | solution.py:214
  95.1 2.0 %collective-permute-done.23 = f32[256]{0:T(256)S(1)} collective-permute-done((f32[256]{0:T(256)S(1)}, f32[256]{0:T(256)S(1)}, u32[]{:S(2)}, u32[]{:S(2)}) %collective-permute-start.23) | collective-permute-done | bytes 1056 | tf_op jit(solution)/shard_map/ppermute | solution.py:214
  97.2 2.7 %collective-permute-start.24 = (f32[256]{0:T(256)S(1)}, f32[256]{0:T(256)S(1)}, u32[]{:S(2)}, u32[]{:S(2)}) collective-permute-start(f32[256]{0:T(256)S(1)} %max.17), channel_id=1, source_target_pairs={{0,1},{1,0},{2,3},{3,2},{4,5},{5,4},{6,7},{7,6},{8,9},{9,8},{10,11... | collective-permute-start | bytes 3080 | tf_op jit(solution)/shard_map/ppermute | solution.py:217
  99.8 1.5 %collective-permute-done.24 = f32[256]{0:T(256)S(1)} collective-permute-done((f32[256]{0:T(256)S(1)}, f32[256]{0:T(256)S(1)}, u32[]{:S(2)}, u32[]{:S(2)}) %collective-permute-start.24) | collective-permute-done | bytes 1056 | tf_op jit(solution)/shard_map/ppermute | solution.py:217
  101.4 3.0 %collective-permute-start.25 = (f32[256]{0:T(256)S(1)}, f32[256]{0:T(256)S(1)}, u32[]{:S(2)}, u32[]{:S(2)}) collective-permute-start(f32[256]{0:T(256)S(1)} %max.18), channel_id=1, source_target_pairs={{0,2},{1,3},{2,0},{3,1},{4,6},{5,7},{6,4},{7,5},{8,10},{9,11},{10,... | collective-permute-start | bytes 3080 | tf_op jit(solution)/shard_map/ppermute | solution.py:217
  105.1 1.5 %collective-permute-start.16 = (bf16[2,1024,128]{2,1,0:T(8,128)(2,1)}, bf16[2,1024,128]{2,1,0:T(8,128)(2,1)S(1)}, u32[]{:S(2)}, u32[]{:S(2)}) collective-permute-start(bf16[2,1024,128]{2,1,0:T(8,128)(2,1)} %dynamic-slice_bitcast_fusion), channel_id=1, source_target_pairs={{0,16},{4,20},{8,24},{12,28},{16,0},{20,4},{24,8},{28,12},{1,17},{... | collective-permute-start | bytes 1572872 | tf_op jit(solution)/shard_map/ppermute | solution.py:214
  107.9 10.6 %collective-permute-done.16 = bf16[2,1024,128]{2,1,0:T(8,128)(2,1)S(1)} collective-permute-done((bf16[2,1024,128]{2,1,0:T(8,128)(2,1)}, bf16[2,1024,128]{2,1,0:T(8,128)(2,1)S(1)}, u32[]{:S(2)}, u32[]{:S(2)}) %collective-permute-start.16) | collective-permute-done | bytes 524320 | tf_op jit(solution)/shard_map/ppermute | solution.py:214
  118.7 1.6 %collective-permute-start.17 = (bf16[1024,128]{1,0:T(8,128)(2,1)S(1)}, bf16[1024,128]{1,0:T(8,128)(2,1)S(1)}, u32[]{:S(2)}, u32[]{:S(2)}) collective-permute-start(bf16[1024,128]{1,0:T(8,128)(2,1)S(1)} %dynamic-slice_bitcast_fusion.2), channel_id=1, source_target_pairs={{0,8},{4,12},{8,0},{12,4},{16,24},{20,28},{24,16},{28,20},{1,9},{5... | collective-permute-start | bytes 786440 | tf_op jit(solution)/shard_map/ppermute | solution.py:214
  121.8 1.7 %collective-permute-start.13 = (bf16[256,128]{1,0:T(8,128)(2,1)S(1)}, bf16[256,128]{1,0:T(8,128)(2,1)S(1)}, u32[]{:S(2)}, u32[]{:S(2)}) collective-permute-start(bf16[256,128]{1,0:T(8,128)(2,1)S(1)} %get-tuple-element.32), channel_id=1, source_target_pairs={{0,2},{1,3},{2,0},{3,1},{4,6},{5,7},{6,4},{7,5},{8,10},{9,11},{10,... | collective-permute-start | bytes 196616 | tf_op jit(solution)/shard_map/ppermute | solution.py:217
  123.5 2.4 %collective-permute-start.14 = (bf16[256,128]{1,0:T(8,128)(2,1)S(1)}, bf16[256,128]{1,0:T(8,128)(2,1)S(1)}, u32[]{:S(2)}, u32[]{:S(2)}) collective-permute-start(bf16[256,128]{1,0:T(8,128)(2,1)S(1)} %get-tuple-element.31), channel_id=1, source_target_pairs={{0,3},{1,2},{2,1},{3,0},{4,7},{5,6},{6,5},{7,4},{8,11},{9,10},{10,... | collective-permute-start | bytes 196616 | tf_op jit(solution)/shard_map/ppermute | solution.py:217
  126.1 2.0 %collective-permute-start.19 = (bf16[256,128]{1,0:T(8,128)(2,1)S(1)}, bf16[256,128]{1,0:T(8,128)(2,1)S(1)}, u32[]{:S(2)}, u32[]{:S(2)}) collective-permute-start(bf16[256,128]{1,0:T(8,128)(2,1)S(1)} %get-tuple-element.35), channel_id=1, source_target_pairs={{0,2},{1,3},{2,0},{3,1},{4,6},{5,7},{6,4},{7,5},{8,10},{9,11},{10,... | collective-permute-start | bytes 196616 | tf_op jit(solution)/shard_map/ppermute | solution.py:217
  128.1 2.4 %collective-permute-start.20 = (bf16[256,128]{1,0:T(8,128)(2,1)S(1)}, bf16[256,128]{1,0:T(8,128)(2,1)S(1)}, u32[]{:S(2)}, u32[]{:S(2)}) collective-permute-start(bf16[256,128]{1,0:T(8,128)(2,1)S(1)} %get-tuple-element.34), channel_id=1, source_target_pairs={{0,3},{1,2},{2,1},{3,0},{4,7},{5,6},{6,5},{7,4},{8,11},{9,10},{10,... | collective-permute-start | bytes 196616 | tf_op jit(solution)/shard_map/ppermute | solution.py:217
  131.3 2.8 %collective-permute-done.20 = bf16[256,128]{1,0:T(8,128)(2,1)S(1)} collective-permute-done((bf16[256,128]{1,0:T(8,128)(2,1)S(1)}, bf16[256,128]{1,0:T(8,128)(2,1)S(1)}, u32[]{:S(2)}, u32[]{:S(2)}) %collective-permute-start.20) | collective-permute-done | bytes 65568 | tf_op jit(solution)/shard_map/ppermute | solution.py:217
  (65 shorter events, 11.2 us)
Async XLA Ops:
  0.6 10.1 %copy-start = (s32[1,4]{1,0:T(1,128)S(1)}, s32[1,4]{1,0:T(1,128)}, u32[]{:S(2)}) copy-start(s32[1,4]{1,0:T(1,128)} %param.7) | copy-start | bytes 52
  0.6 10.7 %collective-permute-start = (bf16[384,128]{1,0:T(8,128)(2,1)}, bf16[384,128]{1,0:T(8,128)(2,1)S(1)}, u32[]{:S(2)}, u32[]{:S(2)}) collective-permute-start(bf16[384,128]{1,0:T(8,128)(2,1)} %refs_0_.1), channel_id=1, source_target_pairs={{0,1},{1,0},{2,3},{3,2},{4,5},{5,4},{6,7},{7,6},{8,9},{9,8},{10,11... | collective-permute-start | bytes 294920 | tf_op jit(solution)/shard_map/ppermute | solution.py:217
  3.7 10.9 %collective-permute-start.1 = (bf16[384,128]{1,0:T(8,128)(2,1)}, bf16[384,128]{1,0:T(8,128)(2,1)S(1)}, u32[]{:S(2)}, u32[]{:S(2)}) collective-permute-start(bf16[384,128]{1,0:T(8,128)(2,1)} %refs_0_.1), channel_id=1, source_target_pairs={{0,2},{1,3},{2,0},{3,1},{4,6},{5,7},{6,4},{7,5},{8,10},{9,11},{10,... | collective-permute-start | bytes 294920 | tf_op jit(solution)/shard_map/ppermute | solution.py:217
  6.3 8.3 %collective-permute-start.2 = (bf16[384,128]{1,0:T(8,128)(2,1)}, bf16[384,128]{1,0:T(8,128)(2,1)S(1)}, u32[]{:S(2)}, u32[]{:S(2)}) collective-permute-start(bf16[384,128]{1,0:T(8,128)(2,1)} %refs_0_.1), channel_id=1, source_target_pairs={{0,3},{1,2},{2,1},{3,0},{4,7},{5,6},{6,5},{7,4},{8,11},{9,10},{10,... | collective-permute-start | bytes 294920 | tf_op jit(solution)/shard_map/ppermute | solution.py:217
  6.3 8.3 %collective-permute-start.3 = (bf16[384,128]{1,0:T(8,128)(2,1)}, bf16[384,128]{1,0:T(8,128)(2,1)S(1)}, u32[]{:S(2)}, u32[]{:S(2)}) collective-permute-start(bf16[384,128]{1,0:T(8,128)(2,1)} %refs_4_.3), channel_id=1, source_target_pairs={{0,1},{1,0},{2,3},{3,2},{4,5},{5,4},{6,7},{7,6},{8,9},{9,8},{10,11... | collective-permute-start | bytes 294920 | tf_op jit(solution)/shard_map/ppermute | solution.py:217
  7.2 15.6 %collective-permute-start.4 = (bf16[384,128]{1,0:T(8,128)(2,1)}, bf16[384,128]{1,0:T(8,128)(2,1)S(1)}, u32[]{:S(2)}, u32[]{:S(2)}) collective-permute-start(bf16[384,128]{1,0:T(8,128)(2,1)} %refs_4_.3), channel_id=1, source_target_pairs={{0,2},{1,3},{2,0},{3,1},{4,6},{5,7},{6,4},{7,5},{8,10},{9,11},{10,... | collective-permute-start | bytes 294920 | tf_op jit(solution)/shard_map/ppermute | solution.py:217
  11.4 11.4 %collective-permute-start.5 = (bf16[384,128]{1,0:T(8,128)(2,1)}, bf16[384,128]{1,0:T(8,128)(2,1)S(1)}, u32[]{:S(2)}, u32[]{:S(2)}) collective-permute-start(bf16[384,128]{1,0:T(8,128)(2,1)} %refs_4_.3), channel_id=1, source_target_pairs={{0,3},{1,2},{2,1},{3,0},{4,7},{5,6},{6,5},{7,4},{8,11},{9,10},{10,... | collective-permute-start | bytes 294920 | tf_op jit(solution)/shard_map/ppermute | solution.py:217
  22.8 1.1 copy-start.1
  23.9 1.1 copy-start.2
  25.1 0.9 copy-start.3
  26.0 0.9 copy-start.4
  47.1 8.3 %collective-permute-start.6 = (bf16[384,256]{1,0:T(8,128)(2,1)S(1)}, bf16[384,256]{1,0:T(8,128)(2,1)S(1)}, u32[]{:S(2)}, u32[]{:S(2)}) collective-permute-start(bf16[384,256]{1,0:T(8,128)(2,1)S(1)} %get-tuple-element.29), channel_id=1, source_target_pairs={{0,1},{1,0},{2,3},{3,2},{4,5},{5,4},{6,7},{7,6},{8,9},{9,8},{10,11... | collective-permute-start | bytes 589832 | tf_op jit(solution)/shard_map/ppermute | solution.py:217
  48.8 16.7 %collective-permute-start.7 = (bf16[384,256]{1,0:T(8,128)(2,1)S(1)}, bf16[384,256]{1,0:T(8,128)(2,1)S(1)}, u32[]{:S(2)}, u32[]{:S(2)}) collective-permute-start(bf16[384,256]{1,0:T(8,128)(2,1)S(1)} %get-tuple-element.28), channel_id=1, source_target_pairs={{0,2},{1,3},{2,0},{3,1},{4,6},{5,7},{6,4},{7,5},{8,10},{9,11},{10,... | collective-permute-start | bytes 589832 | tf_op jit(solution)/shard_map/ppermute | solution.py:217
  50.2 15.3 %collective-permute-start.8 = (bf16[384,256]{1,0:T(8,128)(2,1)S(1)}, bf16[384,256]{1,0:T(8,128)(2,1)S(1)}, u32[]{:S(2)}, u32[]{:S(2)}) collective-permute-start(bf16[384,256]{1,0:T(8,128)(2,1)S(1)} %get-tuple-element.27), channel_id=1, source_target_pairs={{0,3},{1,2},{2,1},{3,0},{4,7},{5,6},{6,5},{7,4},{8,11},{9,10},{10,... | collective-permute-start | bytes 589832 | tf_op jit(solution)/shard_map/ppermute | solution.py:217
  71.0 5.5 %collective-permute-start.15 = (bf16[4,1024,128]{2,1,0:T(8,128)(2,1)S(1)}, bf16[4,1024,128]{2,1,0:T(8,128)(2,1)}, u32[]{:S(2)}, u32[]{:S(2)}) collective-permute-start(bf16[4,1024,128]{2,1,0:T(8,128)(2,1)S(1)} %get-tuple-element.24), channel_id=1, source_target_pairs={{0,4},{4,0},{8,12},{12,8},{16,20},{20,16},{24,28},{28,24},{1,5},{5... | collective-permute-start | bytes 3145736 | tf_op jit(solution)/shard_map/ppermute | solution.py:214
  71.0 5.5 %collective-permute-start.9 = (bf16[4,1024,128]{2,1,0:T(8,128)(2,1)S(1)}, bf16[4,1024,128]{2,1,0:T(8,128)(2,1)}, u32[]{:S(2)}, u32[]{:S(2)}) collective-permute-start(bf16[4,1024,128]{2,1,0:T(8,128)(2,1)S(1)} %get-tuple-element.22), channel_id=1, source_target_pairs={{0,4},{4,0},{8,12},{12,8},{16,20},{20,16},{24,28},{28,24},{1,5},{5... | collective-permute-start | bytes 3145736 | tf_op jit(solution)/shard_map/ppermute | solution.py:214
  79.5 27.5 %collective-permute-start.10 = (bf16[2,1024,128]{2,1,0:T(8,128)(2,1)}, bf16[2,1024,128]{2,1,0:T(8,128)(2,1)S(1)}, u32[]{:S(2)}, u32[]{:S(2)}) collective-permute-start(bf16[2,1024,128]{2,1,0:T(8,128)(2,1)} %dynamic-slice_bitcast_fusion.1), channel_id=1, source_target_pairs={{0,8},{4,12},{8,0},{12,4},{16,24},{20,28},{24,16},{28,20},{1,9},{5... | collective-permute-start | bytes 1572872 | tf_op jit(solution)/shard_map/ppermute | solution.py:214
  81.1 1.1 collective-permute-start.21
  82.2 11.4 %collective-permute-start.22 = (f32[256]{0:T(256)S(1)}, f32[256]{0:T(256)S(1)}, u32[]{:S(2)}, u32[]{:S(2)}) collective-permute-start(f32[256]{0:T(256)S(1)} %max.15), channel_id=1, source_target_pairs={{0,8},{4,12},{8,0},{12,4},{16,24},{20,28},{24,16},{28,20},{1,9},{5... | collective-permute-start | bytes 3080 | tf_op jit(solution)/shard_map/ppermute | solution.py:214
  93.6 3.6 %collective-permute-start.23 = (f32[256]{0:T(256)S(1)}, f32[256]{0:T(256)S(1)}, u32[]{:S(2)}, u32[]{:S(2)}) collective-permute-start(f32[256]{0:T(256)S(1)} %max.16), channel_id=1, source_target_pairs={{0,16},{4,20},{8,24},{12,28},{16,0},{20,4},{24,8},{28,12},{1,17},{... | collective-permute-start | bytes 3080 | tf_op jit(solution)/shard_map/ppermute | solution.py:214
  97.2 4.2 %collective-permute-start.24 = (f32[256]{0:T(256)S(1)}, f32[256]{0:T(256)S(1)}, u32[]{:S(2)}, u32[]{:S(2)}) collective-permute-start(f32[256]{0:T(256)S(1)} %max.17), channel_id=1, source_target_pairs={{0,1},{1,0},{2,3},{3,2},{4,5},{5,4},{6,7},{7,6},{8,9},{9,8},{10,11... | collective-permute-start | bytes 3080 | tf_op jit(solution)/shard_map/ppermute | solution.py:217
  101.4 5.3 %collective-permute-start.25 = (f32[256]{0:T(256)S(1)}, f32[256]{0:T(256)S(1)}, u32[]{:S(2)}, u32[]{:S(2)}) collective-permute-start(f32[256]{0:T(256)S(1)} %max.18), channel_id=1, source_target_pairs={{0,2},{1,3},{2,0},{3,1},{4,6},{5,7},{6,4},{7,5},{8,10},{9,11},{10,... | collective-permute-start | bytes 3080 | tf_op jit(solution)/shard_map/ppermute | solution.py:217
  105.1 13.4 %collective-permute-start.16 = (bf16[2,1024,128]{2,1,0:T(8,128)(2,1)}, bf16[2,1024,128]{2,1,0:T(8,128)(2,1)S(1)}, u32[]{:S(2)}, u32[]{:S(2)}) collective-permute-start(bf16[2,1024,128]{2,1,0:T(8,128)(2,1)} %dynamic-slice_bitcast_fusion), channel_id=1, source_target_pairs={{0,16},{4,20},{8,24},{12,28},{16,0},{20,4},{24,8},{28,12},{1,17},{... | collective-permute-start | bytes 1572872 | tf_op jit(solution)/shard_map/ppermute | solution.py:214
  106.7 12.0 %copy-start.5 = (f32[256]{0:T(256)}, f32[256]{0:T(256)S(1)}, u32[]{:S(2)}) copy-start(f32[256]{0:T(256)S(1)} %maximum_add_fusion) | copy-start | bytes 3076
  107.1 14.2 %collective-permute-start.11 = (bf16[1024,128]{1,0:T(8,128)(2,1)S(1)}, bf16[1024,128]{1,0:T(8,128)(2,1)S(1)}, u32[]{:S(2)}, u32[]{:S(2)}) collective-permute-start(bf16[1024,128]{1,0:T(8,128)(2,1)S(1)} %dynamic-slice_bitcast_fusion.3), channel_id=1, source_target_pairs={{0,16},{4,20},{8,24},{12,28},{16,0},{20,4},{24,8},{28,12},{1,17},{... | collective-permute-start | bytes 786440 | tf_op jit(solution)/shard_map/ppermute | solution.py:214
  118.7 7.2 %collective-permute-start.17 = (bf16[1024,128]{1,0:T(8,128)(2,1)S(1)}, bf16[1024,128]{1,0:T(8,128)(2,1)S(1)}, u32[]{:S(2)}, u32[]{:S(2)}) collective-permute-start(bf16[1024,128]{1,0:T(8,128)(2,1)S(1)} %dynamic-slice_bitcast_fusion.2), channel_id=1, source_target_pairs={{0,8},{4,12},{8,0},{12,4},{16,24},{20,28},{24,16},{28,20},{1,9},{5... | collective-permute-start | bytes 786440 | tf_op jit(solution)/shard_map/ppermute | solution.py:214
  121.4 6.6 %collective-permute-start.12 = (bf16[256,128]{1,0:T(8,128)(2,1)S(1)}, bf16[256,128]{1,0:T(8,128)(2,1)S(1)}, u32[]{:S(2)}, u32[]{:S(2)}) collective-permute-start(bf16[256,128]{1,0:T(8,128)(2,1)S(1)} %get-tuple-element.30), channel_id=1, source_target_pairs={{0,1},{1,0},{2,3},{3,2},{4,5},{5,4},{6,7},{7,6},{8,9},{9,8},{10,11... | collective-permute-start | bytes 196616 | tf_op jit(solution)/shard_map/ppermute | solution.py:217
  121.8 8.7 %collective-permute-start.13 = (bf16[256,128]{1,0:T(8,128)(2,1)S(1)}, bf16[256,128]{1,0:T(8,128)(2,1)S(1)}, u32[]{:S(2)}, u32[]{:S(2)}) collective-permute-start(bf16[256,128]{1,0:T(8,128)(2,1)S(1)} %get-tuple-element.32), channel_id=1, source_target_pairs={{0,2},{1,3},{2,0},{3,1},{4,6},{5,7},{6,4},{7,5},{8,10},{9,11},{10,... | collective-permute-start | bytes 196616 | tf_op jit(solution)/shard_map/ppermute | solution.py:217
  123.5 7.0 %collective-permute-start.14 = (bf16[256,128]{1,0:T(8,128)(2,1)S(1)}, bf16[256,128]{1,0:T(8,128)(2,1)S(1)}, u32[]{:S(2)}, u32[]{:S(2)}) collective-permute-start(bf16[256,128]{1,0:T(8,128)(2,1)S(1)} %get-tuple-element.31), channel_id=1, source_target_pairs={{0,3},{1,2},{2,1},{3,0},{4,7},{5,6},{6,5},{7,4},{8,11},{9,10},{10,... | collective-permute-start | bytes 196616 | tf_op jit(solution)/shard_map/ppermute | solution.py:217
  126.0 4.5 %collective-permute-start.18 = (bf16[256,128]{1,0:T(8,128)(2,1)S(1)}, bf16[256,128]{1,0:T(8,128)(2,1)S(1)}, u32[]{:S(2)}, u32[]{:S(2)}) collective-permute-start(bf16[256,128]{1,0:T(8,128)(2,1)S(1)} %get-tuple-element.33), channel_id=1, source_target_pairs={{0,1},{1,0},{2,3},{3,2},{4,5},{5,4},{6,7},{7,6},{8,9},{9,8},{10,11... | collective-permute-start | bytes 196616 | tf_op jit(solution)/shard_map/ppermute | solution.py:217
  126.1 5.2 %collective-permute-start.19 = (bf16[256,128]{1,0:T(8,128)(2,1)S(1)}, bf16[256,128]{1,0:T(8,128)(2,1)S(1)}, u32[]{:S(2)}, u32[]{:S(2)}) collective-permute-start(bf16[256,128]{1,0:T(8,128)(2,1)S(1)} %get-tuple-element.35), channel_id=1, source_target_pairs={{0,2},{1,3},{2,0},{3,1},{4,6},{5,7},{6,4},{7,5},{8,10},{9,11},{10,... | collective-permute-start | bytes 196616 | tf_op jit(solution)/shard_map/ppermute | solution.py:217
  128.1 6.1 %collective-permute-start.20 = (bf16[256,128]{1,0:T(8,128)(2,1)S(1)}, bf16[256,128]{1,0:T(8,128)(2,1)S(1)}, u32[]{:S(2)}, u32[]{:S(2)}) collective-permute-start(bf16[256,128]{1,0:T(8,128)(2,1)S(1)} %get-tuple-element.34), channel_id=1, source_target_pairs={{0,3},{1,2},{2,1},{3,0},{4,7},{5,6},{6,5},{7,4},{8,11},{9,10},{10,... | collective-permute-start | bytes 196616 | tf_op jit(solution)/shard_map/ppermute | solution.py:217

commit v2 on v0

v2 whole, which is shorter than its diff:
```python
import functools

import jax
import jax.numpy as jnp
from jax import lax
from jax.experimental import pallas as pl
from jax.experimental.pallas import tpu as pltpu
from jax.sharding import PartitionSpec as P

QROWS = 32
LOG2E = 1.4426950408889634
FAR = 1e30
MIB = 1024 * 1024
BF16, F32 = jnp.bfloat16, jnp.float32


def xor_perm(size, mask):
    return [(i, i ^ mask) for i in range(size)]


def whole(shape):
    return pl.BlockSpec(shape, lambda *_: (0,) * len(shape))


def params(mib):
    return pltpu.CompilerParams(vmem_limit_bytes=mib * MIB)


def prepare_kernel(q_ref, do_ref, a_ref, q_out, do_out, a_out):
    q_out[...] = q_ref[...]
    do_out[...] = do_ref[...]
    a_out[...] = a_ref[...].T


def prepare(queries, out_grad, activations, hd):
    rows, columns = queries.shape
    heads = columns // hd
    model = activations.shape[1]
    tile = model // heads
    head = pl.BlockSpec((rows, hd), lambda i: (0, i))
    stacked = pl.BlockSpec((rows, hd), lambda i: (i, 0))
    return pl.pallas_call(
        prepare_kernel,
        grid=(heads,),
        in_specs=[head, head, pl.BlockSpec((rows, tile), lambda i: (0, i))],
        out_specs=[stacked, stacked, pl.BlockSpec((tile, rows), lambda i: (i, 0))],
        out_shape=[
            jax.ShapeDtypeStruct((heads * rows, hd), BF16),
            jax.ShapeDtypeStruct((heads * rows, hd), BF16),
            jax.ShapeDtypeStruct((model, rows), BF16),
        ],
        compiler_params=params(12),
        cost_estimate=pl.CostEstimate(flops=0, bytes_accessed=4 * rows * (model + 2 * columns), transcendentals=0),
        name="prepare",
    )(queries, out_grad, activations)


def attention_kernel(n_blocks, me_ref, span_ref, q_ref, do_ref, *refs):
    kv_refs = refs[:n_blocks]
    dq_ref, own_ref, *rest = refs[n_blocks:]
    other_refs = rest[: n_blocks - 1]
    k_all, v_all, p_buf, ds_buf, dk_acc, dv_acc = rest[n_blocks - 1 :]
    rows, hd = dk_acc.shape[0] // n_blocks, dk_acc.shape[1]
    inverse = 1.0 / hd**0.5
    factor = inverse * LOG2E
    step = pl.program_id(0)
    width = 256
    me = me_ref[0]
    keep = [None] + [span_ref[me ^ b] < span_ref[me] for b in range(1, n_blocks)]

    @pl.when(step == 0)
    def _():
        for b in range(n_blocks):
            k_all[b * rows : (b + 1) * rows, :] = kv_refs[b][:, :hd]
            v_all[b * rows : (b + 1) * rows, :] = kv_refs[b][:, hd:]
        dk_acc[...] = jnp.zeros_like(dk_acc)
        dv_acc[...] = jnp.zeros_like(dv_acc)

    for t in range(2 * rows // width):
        lanes = slice(t * width, (t + 1) * width)
        qc, dc = q_ref[lanes, :], do_ref[lanes, :]
        nt = (((1,), (1,)), ((), ()))
        s = [
            lax.dot_general(k_all[b * rows : (b + 1) * rows, :], qc, nt, preferred_element_type=F32)
            for b in range(n_blocks)
        ]
        dp = [
            lax.dot_general(v_all[b * rows : (b + 1) * rows, :], dc, nt, preferred_element_type=F32)
            for b in range(n_blocks)
        ]
        key_at = lax.broadcasted_iota(jnp.int32, (rows, width), 0)
        query_at = lax.broadcasted_iota(jnp.int32, (rows, width), 1) + t * width
        query_at = jnp.where(query_at >= rows, query_at - rows, query_at)
        s[0] = jnp.where(key_at <= query_at, s[0], -FAR)
        top = jnp.max(s[0], axis=0, keepdims=True)
        for b in range(1, n_blocks):
            block_top = jnp.max(s[b], axis=0, keepdims=True)
            top = jnp.maximum(top, jnp.where(keep[b], block_top, -FAR))
        top = top * factor
        e, total, weighted = [], 0.0, 0.0
        for b in range(n_blocks):
            shift = top if b == 0 else jnp.where(keep[b], top, FAR)
            e_b = jnp.exp2(s[b] * factor - shift)
            total = total + jnp.sum(e_b, axis=0, keepdims=True)
            weighted = weighted + jnp.sum(e_b * dp[b], axis=0, keepdims=True)
            e.append(e_b)
        inv = 1.0 / total
        delta = weighted * inv
        for b in range(n_blocks):
            p = e[b] * inv
            p_buf[b * rows : (b + 1) * rows, lanes] = p.astype(BF16)
            ds_buf[b * rows : (b + 1) * rows, lanes] = (p * (dp[b] - delta)).astype(BF16)

    dk_acc[...] += jnp.dot(ds_buf[...], q_ref[...], preferred_element_type=F32)
    dv_acc[...] += jnp.dot(p_buf[...], do_ref[...], preferred_element_type=F32)
    dq = lax.dot_general(ds_buf[...], k_all[...], (((0,), (0,)), ((), ())), preferred_element_type=F32) * inverse
    for h in range(2):
        dq_ref[:, h * hd : (h + 1) * hd] = dq[h * rows : (h + 1) * rows, :].astype(BF16)

    @pl.when(step == pl.num_programs(0) - 1)
    def _():
        own_ref[:, :hd] = dk_acc[:rows, :] * inverse
        own_ref[:, hd:] = dv_acc[:rows, :]
        for b in range(1, n_blocks):
            part = slice(b * rows, (b + 1) * rows)
            other_refs[b - 1][:, :hd] = (dk_acc[part, :] * inverse).astype(BF16)
            other_refs[b - 1][:, hd:] = dv_acc[part, :].astype(BF16)


def attention(me, spans, stacked_q, stacked_do, kv_blocks):
    n = len(kv_blocks)
    rows, hd = kv_blocks[0].shape[0], stacked_q.shape[1]
    heads = stacked_q.shape[0] // rows
    pair = pl.BlockSpec((2 * rows, hd), lambda i, *_: (i, 0))
    return pl.pallas_call(
        functools.partial(attention_kernel, n),
        grid_spec=pltpu.PrefetchScalarGridSpec(
            num_scalar_prefetch=2,
            grid=(heads // 2,),
            in_specs=[pair, pair] + [whole((rows, 2 * hd))] * n,
            out_specs=[pl.BlockSpec((rows, 2 * hd), lambda i, *_: (0, i))] + [whole((rows, 2 * hd))] * n,
            scratch_shapes=[
                pltpu.VMEM((n * rows, hd), BF16),
                pltpu.VMEM((n * rows, hd), BF16),
                pltpu.VMEM((n * rows, 2 * rows), BF16),
                pltpu.VMEM((n * rows, 2 * rows), BF16),
                pltpu.VMEM((n * rows, hd), F32),
                pltpu.VMEM((n * rows, hd), F32),
            ],
        ),
        out_shape=[jax.ShapeDtypeStruct((rows, heads * hd), BF16), jax.ShapeDtypeStruct((rows, 2 * hd), F32)]
        + [jax.ShapeDtypeStruct((rows, 2 * hd), BF16)] * (n - 1),
        compiler_params=params(36),
        cost_estimate=pl.CostEstimate(
            flops=10 * rows * n * rows * hd * heads,
            bytes_accessed=6 * rows * heads * hd,
            transcendentals=n * rows * rows * heads,
        ),
        name="attention_backward",
    )(me, spans, stacked_q, stacked_do, *kv_blocks)


def tile_of(step, me_dp, bits, flip):
    dest = me_dp ^ flip
    for j in range(1, bits):
        stays = (step >> (bits - 1 - j)) & 1
        dest = dest ^ ((1 - stays) << j)
    return dest


def reversed_step(step, bits):
    out = 0
    for j in range(1, bits):
        out = out + (((step >> (bits - 1 - j)) & 1) << (j - 1))
    return out


def corrected_tile(shrink, chosen, row, grads, a_ref, e_ref, top_ref):
    _, n_ctx, _, rows_set, rows = a_ref.shape
    tall = n_ctx * rows_set
    a = a_ref[0, :, 0].reshape(tall, rows)
    e = e_ref[0, :, 0].reshape(tall, e_ref.shape[4])
    c = jnp.dot(a, grads, preferred_element_type=F32) + e

    @pl.when(pl.program_id(0) == 0)
    def _():
        top_ref[...] = jnp.zeros_like(top_ref)

    mags = jnp.max(jnp.abs(c).reshape(tall // QROWS, QROWS, c.shape[1]), axis=1)
    mags = jnp.max(mags, axis=1, keepdims=True)
    per_set = rows_set // QROWS
    lanes = top_ref.shape[1]
    block = lax.broadcasted_iota(jnp.int32, (tall // QROWS, lanes), 0)
    lane = lax.broadcasted_iota(jnp.int32, (tall // QROWS, lanes), 1)
    shift = per_set.bit_length() - 1
    place = ((block >> shift) * (lanes // n_ctx)) + chosen * per_set + (block & (per_set - 1))
    top_ref[pl.ds(row, 1), :] = jnp.max(jnp.where(lane == place, mags, 0.0), axis=0, keepdims=True)
    return c * shrink


def send_kernel(n_parts, bits, shrink, chosen, with_grads, me_ref, own_ref, *refs):
    part_refs = refs[:n_parts]
    a_ref, e_ref, out_ref, top_ref, *grad_refs, grads = refs[n_parts:]
    step = pl.program_id(0)

    @pl.when(step == 0)
    def _():
        total = own_ref[...].astype(F32)
        for part in part_refs:
            total = total + part[...].astype(F32)
        total = total.astype(BF16)
        grads[...] = total
        if with_grads:
            hd = total.shape[1] // 2
            grad_refs[0][...] = total[:, :hd]
            grad_refs[1][...] = total[:, hd:]
            grad_refs[2][...] = total

    dest = tile_of(step, me_ref[0], bits, 1)
    out_ref[0] = corrected_tile(shrink, chosen, dest, grads[...], a_ref, e_ref, top_ref).astype(BF16)


def keep_kernel(bits, shrink, chosen, me_ref, grads, got_ref, a_ref, e_ref, low_away, low_stay, high_away, high_stay, top_ref):
    step = pl.program_id(0)
    half = low_away.shape[0]
    hd = low_away.shape[2]
    dest = tile_of(step, me_ref[0], bits, 0)
    c = corrected_tile(shrink, chosen, dest, grads[...], a_ref, e_ref, top_ref)
    c = (c + got_ref[0].astype(F32)).astype(BF16)
    back = reversed_step(step, bits)
    for at, part, away, stay in ((step, c[:, :hd], low_away, low_stay), (back, c[:, hd:], high_away, high_stay)):

        @pl.when(at < half)
        def _():
            away[at] = part

        @pl.when(at >= half)
        def _():
            stay[at - half] = part


def tile_specs(bits, flip, chosen, a, e):
    def block(x):
        _, n_ctx, _, rows_set, width = x.shape
        return pl.BlockSpec(
            (1, n_ctx, 1, rows_set, width), lambda i, me: (tile_of(i, me[0], bits, flip), 0, chosen, 0, 0)
        )

    return [block(a), block(e)]


def tile_cost(a, e):
    n_dp, n_ctx, sets, rows_set, rows = a.shape
    tall = n_dp // 2 * n_ctx * rows_set
    width = e.shape[4]
    return pl.CostEstimate(
        flops=2 * tall * rows * width, bytes_accessed=tall * (2 * rows + 6 * width), transcendentals=0
    )


def send_tiles(me, own, parts, a, e, chosen, shrink, with_grads):
    n_dp, n_ctx, sets, rows_set, rows = a.shape
    bits = n_dp.bit_length() - 1
    width = e.shape[4]
    tall = n_ctx * rows_set
    lanes = sets * tall // QROWS
    grad_shapes = [(rows, width // 2), (rows, width // 2), (rows, width)] if with_grads else []
    return pl.pallas_call(
        functools.partial(send_kernel, len(parts), bits, shrink, chosen, with_grads),
        grid_spec=pltpu.PrefetchScalarGridSpec(
            num_scalar_prefetch=1,
            grid=(n_dp // 2,),
            in_specs=[whole((rows, width))] * (1 + len(parts)) + tile_specs(bits, 1, chosen, a, e),
            out_specs=[pl.BlockSpec((1, tall, width), lambda i, me: (i, 0, 0)), whole((n_dp, lanes))]
            + [whole(s) for s in grad_shapes],
            scratch_shapes=[pltpu.VMEM((rows, width), BF16)],
        ),
        out_shape=[jax.ShapeDtypeStruct((n_dp // 2, tall, width), BF16), jax.ShapeDtypeStruct((n_dp, lanes), F32)]
        + [jax.ShapeDtypeStruct(s, BF16) for s in grad_shapes],
        compiler_params=params(16),
        cost_estimate=tile_cost(a, e),
        name="send_tiles",
    )(me, own, *parts, a, e)


def keep_tiles(me, grads, got, a, e, chosen, shrink):
    n_dp, n_ctx, sets, rows_set, rows = a.shape
    bits = n_dp.bit_length() - 1
    width = e.shape[4]
    tall = n_ctx * rows_set
    lanes = sets * tall // QROWS
    half = (n_dp // 4, tall, width // 2)
    return pl.pallas_call(
        functools.partial(keep_kernel, bits, shrink, chosen),
        grid_spec=pltpu.PrefetchScalarGridSpec(
            num_scalar_prefetch=1,
            grid=(n_dp // 2,),
            in_specs=[whole((rows, width)), pl.BlockSpec((1, tall, width), lambda i, me: (i, 0, 0))]
            + tile_specs(bits, 0, chosen, a, e),
            out_specs=[whole(half)] * 4 + [whole((n_dp, lanes))],
        ),
        out_shape=[jax.ShapeDtypeStruct(half, BF16)] * 4 + [jax.ShapeDtypeStruct((n_dp, lanes), F32)],
        compiler_params=params(16),
        cost_estimate=tile_cost(a, e),
        name="keep_tiles",
    )(me, grads, got, a, e)


def largest(tops, top_out):
    if tops:
        top = tops[0][...]
        for other in tops[1:]:
            top = jnp.maximum(top, other[...])
        top_out[0][...] = top


def add_kernel(n_tops, *refs):
    low, low_got, high, high_got = refs[:4]
    tops = refs[4 : 4 + n_tops]
    low_away, low_stay, high_away, high_stay, *top_out = refs[4 + n_tops :]
    half = low_away.shape[0]
    for mine, got, away, stay in ((low, low_got, low_away, low_stay), (high, high_got, high_away, high_stay)):
        away[...] = (mine[:half].astype(F32) + got[:half].astype(F32)).astype(BF16)
        stay[...] = (mine[half:].astype(F32) + got[half:].astype(F32)).astype(BF16)
    largest(tops, top_out)


def add_stage(low, low_got, high, high_got, tops):
    m, tall, hd = low.shape
    half = jax.ShapeDtypeStruct((m // 2, tall, hd), BF16)
    return pl.pallas_call(
        functools.partial(add_kernel, len(tops)),
        out_shape=[half] * 4 + [jax.ShapeDtypeStruct(top.shape, F32) for top in tops[:1]],
        compiler_params=params(16),
        cost_estimate=pl.CostEstimate(flops=2 * low.size, bytes_accessed=12 * low.size, transcendentals=0),
        name="add_stage",
    )(low, low_got, high, high_got, *tops)


def last_kernel(n_ctx, n_tops, me_ref, *refs):
    low, low_got, high, high_got = refs[:4]
    tops = refs[4 : 4 + n_tops]
    outs, top_out = refs[4 + n_tops : 4 + n_tops + n_ctx], refs[4 + n_tops + n_ctx :]
    hd = low.shape[2]
    rows_set = low.shape[1] // n_ctx
    for b in range(n_ctx):
        part = pl.ds(pl.multiple_of((me_ref[0] ^ b) * rows_set, rows_set), rows_set)
        for at, mine, got in ((0, low, low_got), (hd, high, high_got)):
            total = mine[0, part, :].astype(F32) + got[0, part, :].astype(F32)
            outs[b][:, at : at + hd] = total.astype(outs[b].dtype)
    largest(tops, top_out)


def last_stage(me_ctx, low, low_got, high, high_got, tops, n_ctx):
    _, tall, hd = low.shape
    shape = (tall // n_ctx, 2 * hd)
    return pl.pallas_call(
        functools.partial(last_kernel, n_ctx, len(tops)),
        grid_spec=pltpu.PrefetchScalarGridSpec(
            num_scalar_prefetch=1,
            grid=(1,),
            in_specs=[whole(low.shape)] * 4 + [whole(top.shape) for top in tops],
            out_specs=[whole(shape)] * n_ctx + [whole(top.shape) for top in tops[:1]],
        ),
        out_shape=[jax.ShapeDtypeStruct(shape, F32)]
        + [jax.ShapeDtypeStruct(shape, BF16)] * (n_ctx - 1)
        + [jax.ShapeDtypeStruct(top.shape, F32) for top in tops[:1]],
        compiler_params=params(16),
        cost_estimate=pl.CostEstimate(flops=2 * low.size, bytes_accessed=12 * low.size, transcendentals=0),
        name="last_stage",
    )(me_ctx, low, low_got, high, high_got, *tops)


def final_kernel(sets, n_ctx, gain, me_dp_ref, me_ctx_ref, *refs):
    groups = [refs[chosen * n_ctx : (chosen + 1) * n_ctx] for chosen in range(sets)]
    tops = refs[sets * n_ctx : sets * n_ctx + n_ctx]
    out_ref, scale_ref = refs[sets * n_ctx + n_ctx :]
    scale = tops[0][...]
    for other in tops[1:]:
        scale = jnp.maximum(scale, other[...])
    scale_ref[...] = scale + 1e-06
    factors = gain / scale_ref[pl.ds(me_dp_ref[0], 1), :]
    lane = lax.broadcasted_iota(jnp.int32, factors.shape, 1)
    rows_set = groups[0][0].shape[0]
    per_set = rows_set // QROWS
    first = me_ctx_ref[0] * (sets * per_set)
    for chosen, group in enumerate(groups):
        for r in range(per_set):
            part = slice(r * QROWS, (r + 1) * QROWS)
            total = group[0][part, :]
            for other in group[1:]:
                total = total + other[part, :].astype(F32)
            mine = jnp.where(lane == first + (chosen * per_set + r), factors, 0.0)
            at = chosen * rows_set + r * QROWS
            out_ref[at : at + QROWS, :] = total * jnp.sum(mine, axis=1, keepdims=True)


def final_stage(me_dp, me_ctx, groups, tops, gain):
    sets, n_ctx = len(groups), len(groups[0])
    rows_set, width = groups[0][0].shape
    return pl.pallas_call(
        functools.partial(final_kernel, sets, n_ctx, gain),
        grid_spec=pltpu.PrefetchScalarGridSpec(
            num_scalar_prefetch=2,
            grid=(1,),
            in_specs=[whole((rows_set, width))] * (sets * n_ctx) + [whole(tops[0].shape)] * n_ctx,
            out_specs=[whole((sets * rows_set, width)), whole(tops[0].shape)],
        ),
        out_shape=[
            jax.ShapeDtypeStruct((sets * rows_set, width), F32),
            jax.ShapeDtypeStruct(tops[0].shape, F32),
        ],
        compiler_params=params(8),
        cost_estimate=pl.CostEstimate(
            flops=4 * sets * rows_set * width, bytes_accessed=16 * sets * rows_set * width, transcendentals=0
        ),
        name="final_stage",
    )(me_dp, me_ctx, *[x for group in groups for x in group], *tops)


def local(n_dp, n_ctx, sets, span_order, queries, keys, values, out_grad, activations, error_feedback):
    rows, hd = keys.shape
    model = activations.shape[1]
    rows_set = model // (n_dp * n_ctx * sets)
    me_dp = lax.axis_index("dp").astype(jnp.int32)[None]
    me_ctx = lax.axis_index("context").astype(jnp.int32)[None]
    bits = n_dp.bit_length() - 1

    def swap_dp(x, mask):
        return lax.ppermute(x, "dp", xor_perm(n_dp, mask))

    def swap_ctx(x, mask):
        return lax.ppermute(x, "context", xor_perm(n_ctx, mask))

    pairs = jnp.concatenate([keys, values], axis=1)
    kv_blocks = [pairs] + [swap_ctx(pairs, b) for b in range(1, n_ctx)]
    stacked_q, stacked_do, acts = prepare(queries, out_grad, activations, hd)
    query_grad, own, *others = attention(me_ctx, span_order[0], stacked_q, stacked_do, kv_blocks)
    parts = [swap_ctx(other, b + 1) for b, other in enumerate(others)]

    shrink = 1.0 / (n_dp * n_ctx)
    acts = acts.reshape(n_dp, n_ctx, sets, rows_set, rows)
    errors = error_feedback.reshape(n_dp, n_ctx, sets, rows_set, 2 * hd)
    got, tops = [], []
    for chosen in range(sets):
        if chosen == 0:
            out, top, key_grad, value_grad, grads = send_tiles(me_dp, own, parts, acts, errors, 0, shrink, True)
        else:
            out, top = send_tiles(me_dp, grads, [], acts, errors, chosen, shrink, False)
        got.append(swap_dp(out, 1))
        tops.append(top)

    halves = []
    for chosen in range(sets):
        *half, top = keep_tiles(me_dp, grads, got[chosen], acts, errors, chosen, shrink)
        halves.append(half)
        tops.append(top)
    top = functools.reduce(jnp.maximum, tops)

    groups = []
    for chosen in range(sets):
        low_away, low, high_away, high = halves[chosen]
        for stage in range(1, bits):
            low_got = swap_dp(low_away, 1 << stage)
            high_got = swap_dp(high_away, 1 << (bits - stage))
            tops = []
            if chosen == sets - 1:
                masks = [1] if stage == 1 else range(2, n_dp, 2) if stage == 2 else []
                tops = [top] + [swap_dp(top, mask) for mask in masks]
            if stage < bits - 1:
                low_away, low, high_away, high, *top_out = add_stage(low, low_got, high, high_got, tops)
            else:
                outs = last_stage(me_ctx, low, low_got, high, high_got, tops, n_ctx)
                mine, *away = outs[:n_ctx]
                top_out = outs[n_ctx:]
            if tops:
                top = top_out[0]
        groups.append([mine] + [swap_ctx(part, b + 1) for b, part in enumerate(away)])
    tops = [top] + [swap_ctx(top, b) for b in range(1, n_ctx)]
    payload, scale = final_stage(me_dp, me_ctx, groups, tops, 7.0 / shrink)
    return query_grad, key_grad, value_grad, payload, scale.reshape(-1)


def solution(mesh):
    tokens = P(("dp", "context"), None)
    return jax.shard_map(
        functools.partial(local, mesh.shape["dp"], mesh.shape["context"], 2),
        mesh=mesh,
        in_specs=(P("dp", None), tokens, tokens, tokens, tokens, tokens, P("dp", "context", None, None)),
        out_specs=(tokens, tokens, tokens, tokens, P()),
        check_vma=False,
    )
```

time: 430 us -> 124 us (0.29)
  waiting for transfers between devices: 224 us -> 35.6 us
  blocking collectives: 70.9 us -> 0 us
  matrix products: 68.7 us -> 0 us
  starting transfers between devices: 0.12 us -> 36.7 us
  Pallas kernels: 0 us -> 33.5 us
  other arithmetic: 27.4 us -> 0.01 us
  between operations: 13.9 us -> 0.75 us
  loops' own time: 5.67 us -> 0 us
    reduce_scatter x3 -> x0, waiting for transfers between devices: 223 us -> none  [the longest x1 185 us: local(): lax.psum_scatter(terms, ('dp', 'context'), scatter_dimension=0, tiled=True)]
    dot_general x41 -> x0, matrix products: 68.7 us -> none  [the longest x8 15.3 us: head_backward(): jnp.dot(probs_low.T, grad_head, preferred_element_type=jnp.float32)]
    pmax x1 -> x0, blocking collectives: 38.7 us -> none  [local(): block_max = lax.pmax(local_top, ('dp', 'context'))]
    ppermute x0 -> x29, starting transfers between devices: none -> 36.7 us  [the longest x15 24.8 us: swap_ctx(): return lax.ppermute(x, 'context', xor_perm(n_ctx, mask))]
    ppermute x0 -> x29, waiting for transfers between devices: none -> 35.6 us  [the longest x15 22.8 us: swap_ctx(): return lax.ppermute(x, 'context', xor_perm(n_ctx, mask))]
    pallas_call x0 -> x11, Pallas kernels: none -> 33.5 us  [the longest x1 19.9 us: attention(): pl.pallas_call(functools.partial(attention_kernel, n), grid_spec=pltpu.Pr...]
    all_gather x2 -> x0, blocking collectives: 32.2 us -> none  [the longest x1 16.4 us: local(): lax.all_gather(keys, 'context', axis=0, tiled=True)]
    convert_element_type x12 -> x0, other arithmetic: 15.3 us -> none  [the longest x8 5.1 us: head_backward(): score_grad = (probs * (prob_grad - row_delta)).astype(jnp.bfloat16)]
  transfers between devices with their start and end apart: 3 -> 29, of which waited for: 3 -> 16; matrix products, arithmetic and copies ran while one was open for 3% -> 0% of each run, Pallas kernels for 0% -> 8%
where the time goes in v2:
time: 124 us
  starting transfers between devices  36.7 us (30%)
  waiting for transfers between devices  35.6 us (29%)
  Pallas kernels  33.5 us (27%)
  local copies, waits for them, and re-layouts  17.1 us (14%)
    ppermute x15, starting transfers between devices, swap_ctx(): return lax.ppermute(x, 'context', xor_perm(n_ctx, mask))  24.8 us
    ppermute x15, waiting for transfers between devices, swap_ctx(): return lax.ppermute(x, 'context', xor_perm(n_ctx, mask))  22.8 us
    pallas_call x1, Pallas kernels, attention(): pl.pallas_call(functools.partial(attention_kernel, n), grid_spec=pltpu.Pr...  19.9 us
    unnamed x17, local copies, waits for them, and re-layouts  15.6 us
    ppermute x14, waiting for transfers between devices, swap_dp(): return lax.ppermute(x, 'dp', xor_perm(n_dp, mask))  12.8 us
    ppermute x14, starting transfers between devices, swap_dp(): return lax.ppermute(x, 'dp', xor_perm(n_dp, mask))  11.9 us
    pallas_call x2, Pallas kernels, send_tiles(): pl.pallas_call(functools.partial(send_kernel, len(parts), bits, shrink, c...  4.75 us
    pallas_call x2, Pallas kernels, keep_tiles(): pl.pallas_call(functools.partial(keep_kernel, bits, shrink, chosen), grid...  4.52 us
  transfers between devices with their start and end apart: 29, of which 16 were waited for; matrix products, arithmetic and copies ran while one was open for 0% of the time, Pallas kernels for 8%

profile of v2, /device:TPU:0, one launch (start us, length us, event | category | flops | bytes accessed | tf_op | source)
XLA Modules:
  0.0 123.6 jit_solution(1072273744859761159)
XLA Ops:
  2.5 3.1 %collective-permute-start = (bf16[384,256]{1,0:T(8,128)(2,1)S(1)}, bf16[384,256]{1,0:T(8,128)(2,1)S(1)}, u32[]{:S(2)}, u32[]{:S(2)}) collective-permute-start(bf16[384,256]{1,0:T(8,128)(2,1)S(1)} %constant_dynamic-update-slice_fusion.refs_0_), channel_id=1, source_target_pairs={{0,1},{1,0},{2,3},{3,2},{4,5},{5,4},{6,7},{7,6},{8,9},{9,8},{10,11... | collective-permute-start | bytes 589832 | tf_op jit(solution)/shard_map/ppermute | solution.py:433
  5.6 2.6 %collective-permute-start.1 = (bf16[384,256]{1,0:T(8,128)(2,1)S(1)}, bf16[384,256]{1,0:T(8,128)(2,1)S(1)}, u32[]{:S(2)}, u32[]{:S(2)}) collective-permute-start(bf16[384,256]{1,0:T(8,128)(2,1)S(1)} %constant_dynamic-update-slice_fusion.refs_0_), channel_id=1, source_target_pairs={{0,2},{1,3},{2,0},{3,1},{4,6},{5,7},{6,4},{7,5},{8,10},{9,11},{10,... | collective-permute-start | bytes 589832 | tf_op jit(solution)/shard_map/ppermute | solution.py:433
  8.2 2.8 %copy-done.4 = bf16[384,8192]{1,0:T(8,128)(2,1)S(1)} copy-done((bf16[384,8192]{1,0:T(8,128)(2,1)S(1)}, bf16[384,8192]{1,0:T(8,128)(2,1)}, u32[]{:S(2)}) %copy-start.4) | copy-done | bytes 6291480
  13.2 3.1 %prepare.1 = (bf16[3072,128]{1,0:T(8,128)(2,1)S(1)}, bf16[3072,128]{1,0:T(8,128)(2,1)S(1)}, bf16[8192,384]{1,0:T(8,128)(2,1)S(1)}) custom-call(bf16[384,1024]{1,0:T(8,128)(2,1)S(1)} %copy-done.5, bf16[384,1024]{1,0:T(8,128)(2,1)S(1)} %copy-done.6, bf16[384,8192]{1,0:T(8,128)(2,1)S(1)} %copy-done.4), custom_call_target="tpu_custom_call" | custom-call | bytes 15728640 | tf_op jit(solution)/shard_map/prepare/pallas_call | solution.py:42
  16.3 2.7 %copy-done.2 = bf16[8192,384]{1,0:T(8,128)(2,1)} copy-done((bf16[8192,384]{1,0:T(8,128)(2,1)}, bf16[8192,384]{1,0:T(8,128)(2,1)S(1)}, u32[]{:S(2)}) %copy-start.2) | copy-done | bytes 6291480
  19.0 3.8 %collective-permute-done.1.refs_2_ = bf16[384,256]{1,0:T(8,128)(2,1)S(1)} collective-permute-done((bf16[384,256]{1,0:T(8,128)(2,1)S(1)}, bf16[384,256]{1,0:T(8,128)(2,1)S(1)}, u32[]{:S(2)}, u32[]{:S(2)}) %collective-permute-start.1) | collective-permute-done | bytes 196640 | tf_op jit(solution)/shard_map/ppermute | solution.py:433
  22.7 19.9 %attention_backward.1 = (bf16[384,1024]{1,0:T(8,128)(2,1)}, f32[384,256]{1,0:T(8,128)S(1)}, bf16[384,256]{1,0:T(8,128)(2,1)S(1)}, bf16[384,256]{1,0:T(8,128)(2,1)S(1)}, bf16[384,256]{1,0:T(8,128)(2,1)S(1)}) custom-call(s32[1]{0:T(128)} %bitcast.me_ref.me_ctx_ref, s32[4]{0:T(128)S(1)} %bitcast.13, bf16[3072,128]{1,0:T(8,128)(2,1)S(1)} %get-tuple-element.50.q_ref, ...), custom_call_target="tpu_custom_call" | custom-call | flops 6039797760 | bytes 2359296 | tf_op jit(solution)/shard_map/attention_backward/pallas_call | solution.py:135
  42.7 3.4 %collective-permute-start.3 = (bf16[384,256]{1,0:T(8,128)(2,1)S(1)}, bf16[384,256]{1,0:T(8,128)(2,1)S(1)}, u32[]{:S(2)}, u32[]{:S(2)}) collective-permute-start(bf16[384,256]{1,0:T(8,128)(2,1)S(1)} %get-tuple-element.54), channel_id=1, source_target_pairs={{0,1},{1,0},{2,3},{3,2},{4,5},{5,4},{6,7},{7,6},{8,9},{9,8},{10,11... | collective-permute-start | bytes 589832 | tf_op jit(solution)/shard_map/ppermute | solution.py:433
  47.0 1.5 %collective-permute-start.5 = (bf16[384,256]{1,0:T(8,128)(2,1)S(1)}, bf16[384,256]{1,0:T(8,128)(2,1)S(1)}, u32[]{:S(2)}, u32[]{:S(2)}) collective-permute-start(bf16[384,256]{1,0:T(8,128)(2,1)S(1)} %get-tuple-element.56), channel_id=1, source_target_pairs={{0,3},{1,2},{2,1},{3,0},{4,7},{5,6},{6,5},{7,4},{8,11},{9,10},{10,... | collective-permute-start | bytes 589832 | tf_op jit(solution)/shard_map/ppermute | solution.py:433
  48.5 3.8 %collective-permute-done.3.refs_0_ = bf16[384,256]{1,0:T(8,128)(2,1)S(1)} collective-permute-done((bf16[384,256]{1,0:T(8,128)(2,1)S(1)}, bf16[384,256]{1,0:T(8,128)(2,1)S(1)}, u32[]{:S(2)}, u32[]{:S(2)}) %collective-permute-start.3) | collective-permute-done | bytes 196640 | tf_op jit(solution)/shard_map/ppermute | solution.py:433
  52.3 10.4 %collective-permute-done.4.refs_1_ = bf16[384,256]{1,0:T(8,128)(2,1)S(1)} collective-permute-done((bf16[384,256]{1,0:T(8,128)(2,1)S(1)}, bf16[384,256]{1,0:T(8,128)(2,1)S(1)}, u32[]{:S(2)}, u32[]{:S(2)}) %collective-permute-start.4) | collective-permute-done | bytes 196640 | tf_op jit(solution)/shard_map/ppermute | solution.py:433
  62.7 3.4 %copy-done = f32[1,1,8192,256]{3,2,1,0:T(8,128)S(1)} copy-done((f32[1,1,8192,256]{3,2,1,0:T(8,128)S(1)}, f32[1,1,8192,256]{3,2,1,0:T(8,128)}, u32[]{:S(2)}) %copy-start) | copy-done | bytes 8388632
  66.1 2.8 %copy-done.3 = bf16[8192,384]{1,0:T(8,128)(2,1)S(1)} copy-done((bf16[8192,384]{1,0:T(8,128)(2,1)S(1)}, bf16[8192,384]{1,0:T(8,128)(2,1)}, u32[]{:S(2)}) %copy-start.3) | copy-done | bytes 6291480
  68.9 2.7 %send_tiles.2 = (bf16[4,512,256]{2,1,0:T(8,128)(2,1)S(1)}, f32[8,32]{1,0:T(8,128)S(1)}, bf16[384,128]{1,0:T(8,128)(2,1)}, bf16[384,128]{1,0:T(8,128)(2,1)}, bf16[384,256]{1,0:T(8,128)(2,1)S(1)}) custom-call(s32[1]{0:T(128)} %bitcast.2.me_ref.me_dp_ref, f32[384,256]{1,0:T(8,128)S(1)} %get-tuple-element.53.own_ref, ...), custom_call_target="tpu_custom_call" | custom-call | flops 402653184 | bytes 4718592 | tf_op jit(solution)/shard_map/send_tiles/pallas_call | solution.py:268
  72.3 2.1 %send_tiles.3 = (bf16[4,512,256]{2,1,0:T(8,128)(2,1)S(1)}, f32[8,32]{1,0:T(8,128)S(1)}) custom-call(s32[1]{0:T(128)} %bitcast.2.me_ref.me_dp_ref, bf16[384,256]{1,0:T(8,128)(2,1)S(1)} %get-tuple-element.60.grads.own_ref, bf16[8,4,2,128,384]{4,3,2,1,0:T(8,128)(2,1)S(1)} %bitcast.10, f32[8,4,2,128,256]{4,3,2,1,0:T(8,128)S(1)} %bitcast.6), custom_call_target="tpu_custom_call" | custom-call | flops 402653184 | bytes 4718592 | tf_op jit(solution)/shard_map/send_tiles/pallas_call | solution.py:268
  74.5 2.3 %keep_tiles.2 = (bf16[2,512,128]{2,1,0:T(8,128)(2,1)S(1)}, bf16[2,512,128]{2,1,0:T(8,128)(2,1)S(1)}, bf16[2,512,128]{2,1,0:T(8,128)(2,1)S(1)}, bf16[2,512,128]{2,1,0:T(8,128)(2,1)S(1)}, f32[8,32]{1,0:T(8,128)S(1)}) custom-call(s32[1]{0:T(128)} %bitcast.2.me_ref.me_dp_ref, bf16[384,256]{1,0:T(8,128)(2,1)S(1)} %get-tuple-element.60.grads.own_ref, ...), custom_call_target="tpu_custom_call" | custom-call | flops 402653184 | bytes 4718592 | tf_op jit(solution)/shard_map/keep_tiles/pallas_call | solution.py:293
  76.7 1.6 %collective-permute-start.7 = (bf16[2,512,128]{2,1,0:T(8,128)(2,1)S(1)}, bf16[2,512,128]{2,1,0:T(8,128)(2,1)S(1)}, u32[]{:S(2)}, u32[]{:S(2)}) collective-permute-start(bf16[2,512,128]{2,1,0:T(8,128)(2,1)S(1)} %get-tuple-element.63), channel_id=1, source_target_pairs={{0,8},{4,12},{8,0},{12,4},{16,24},{20,28},{24,16},{28,20},{1,9},{5... | collective-permute-start | bytes 786440 | tf_op jit(solution)/shard_map/ppermute | solution.py:430
  78.3 1.5 %collective-permute-start.8 = (bf16[2,512,128]{2,1,0:T(8,128)(2,1)S(1)}, bf16[2,512,128]{2,1,0:T(8,128)(2,1)S(1)}, u32[]{:S(2)}, u32[]{:S(2)}) collective-permute-start(bf16[2,512,128]{2,1,0:T(8,128)(2,1)S(1)} %get-tuple-element.65), channel_id=1, source_target_pairs={{0,16},{4,20},{8,24},{12,28},{16,0},{20,4},{24,8},{28,12},{1,17},{... | collective-permute-start | bytes 786440 | tf_op jit(solution)/shard_map/ppermute | solution.py:430
  79.8 2.2 %keep_tiles.3 = (bf16[2,512,128]{2,1,0:T(8,128)(2,1)S(1)}, bf16[2,512,128]{2,1,0:T(8,128)(2,1)S(1)}, bf16[2,512,128]{2,1,0:T(8,128)(2,1)S(1)}, bf16[2,512,128]{2,1,0:T(8,128)(2,1)S(1)}, f32[8,32]{1,0:T(8,128)S(1)}) custom-call(s32[1]{0:T(128)} %bitcast.2.me_ref.me_dp_ref, bf16[384,256]{1,0:T(8,128)(2,1)S(1)} %get-tuple-element.60.grads.own_ref, ...), custom_call_target="tpu_custom_call" | custom-call | flops 402653184 | bytes 4718592 | tf_op jit(solution)/shard_map/keep_tiles/pallas_call | solution.py:293
  83.2 2.7 %collective-permute-done.7.refs_1_ = bf16[2,512,128]{2,1,0:T(8,128)(2,1)S(1)} collective-permute-done((bf16[2,512,128]{2,1,0:T(8,128)(2,1)S(1)}, bf16[2,512,128]{2,1,0:T(8,128)(2,1)S(1)}, u32[]{:S(2)}, u32[]{:S(2)}) %collective-permute-start.7) | collective-permute-done | bytes 262176 | tf_op jit(solution)/shard_map/ppermute | solution.py:430
  85.9 1.5 %collective-permute-done.8.refs_3_ = bf16[2,512,128]{2,1,0:T(8,128)(2,1)S(1)} collective-permute-done((bf16[2,512,128]{2,1,0:T(8,128)(2,1)S(1)}, bf16[2,512,128]{2,1,0:T(8,128)(2,1)S(1)}, u32[]{:S(2)}, u32[]{:S(2)}) %collective-permute-start.8) | collective-permute-done | bytes 262176 | tf_op jit(solution)/shard_map/ppermute | solution.py:430
  87.6 1.6 %collective-permute-start.9 = (bf16[1,512,128]{2,1,0:T(8,128)(2,1)S(1)}, bf16[1,512,128]{2,1,0:T(8,128)(2,1)S(1)}, u32[]{:S(2)}, u32[]{:S(2)}) collective-permute-start(bf16[1,512,128]{2,1,0:T(8,128)(2,1)S(1)} %get-tuple-element.67), channel_id=1, source_target_pairs={{0,16},{4,20},{8,24},{12,28},{16,0},{20,4},{24,8},{28,12},{1,17},{... | collective-permute-start | bytes 393224 | tf_op jit(solution)/shard_map/ppermute | solution.py:430
  91.5 1.5 %collective-permute-done.16.refs_3_ = bf16[2,512,128]{2,1,0:T(8,128)(2,1)S(1)} collective-permute-done((bf16[2,512,128]{2,1,0:T(8,128)(2,1)S(1)}, bf16[2,512,128]{2,1,0:T(8,128)(2,1)S(1)}, u32[]{:S(2)}, u32[]{:S(2)}) %collective-permute-start.16) | collective-permute-done | bytes 262176 | tf_op jit(solution)/shard_map/ppermute | solution.py:430
  93.2 1.6 %collective-permute-start.18 = (bf16[1,512,128]{2,1,0:T(8,128)(2,1)S(1)}, bf16[1,512,128]{2,1,0:T(8,128)(2,1)S(1)}, u32[]{:S(2)}, u32[]{:S(2)}) collective-permute-start(bf16[1,512,128]{2,1,0:T(8,128)(2,1)S(1)} %get-tuple-element.84), channel_id=1, source_target_pairs={{0,16},{4,20},{8,24},{12,28},{16,0},{20,4},{24,8},{28,12},{1,17},{... | collective-permute-start | bytes 393224 | tf_op jit(solution)/shard_map/ppermute | solution.py:430
  95.8 2.7 %collective-permute-start.11 = (bf16[128,256]{1,0:T(8,128)(2,1)S(1)}, bf16[128,256]{1,0:T(8,128)(2,1)S(1)}, u32[]{:S(2)}, u32[]{:S(2)}) collective-permute-start(bf16[128,256]{1,0:T(8,128)(2,1)S(1)} %get-tuple-element.71), channel_id=1, source_target_pairs={{0,1},{1,0},{2,3},{3,2},{4,5},{5,4},{6,7},{7,6},{8,9},{9,8},{10,11... | collective-permute-start | bytes 196616 | tf_op jit(solution)/shard_map/ppermute | solution.py:433
  100.5 1.6 %collective-permute-done.20.refs_5_ = f32[8,32]{1,0:T(8,128)S(1)} collective-permute-done((f32[8,32]{1,0:T(8,128)S(1)}, f32[8,32]{1,0:T(8,128)S(1)}, u32[]{:S(2)}, u32[]{:S(2)}) %collective-permute-start.20) | collective-permute-done | bytes 1056 | tf_op jit(solution)/shard_map/ppermute | solution.py:430
  102.1 1.4 %collective-permute-start.22 = (f32[8,32]{1,0:T(8,128)S(1)}, f32[8,32]{1,0:T(8,128)S(1)}, u32[]{:S(2)}, u32[]{:S(2)}) collective-permute-start(f32[8,32]{1,0:T(8,128)S(1)} %get-tuple-element.87.refs_4_), channel_id=1, source_target_pairs={{0,24},{4,28},{8,16},{12,20},{16,8},{20,12},{24,0},{28,4},{1,25},{... | collective-permute-start | bytes 3080 | tf_op jit(solution)/shard_map/ppermute | solution.py:430
  103.6 3.1 %collective-permute-done.22.refs_7_ = f32[8,32]{1,0:T(8,128)S(1)} collective-permute-done((f32[8,32]{1,0:T(8,128)S(1)}, f32[8,32]{1,0:T(8,128)S(1)}, u32[]{:S(2)}, u32[]{:S(2)}) %collective-permute-start.22) | collective-permute-done | bytes 1056 | tf_op jit(solution)/shard_map/ppermute | solution.py:430
  107.1 2.7 %collective-permute-start.27 = (f32[8,32]{1,0:T(8,128)S(1)}, f32[8,32]{1,0:T(8,128)S(1)}, u32[]{:S(2)}, u32[]{:S(2)}) collective-permute-start(f32[8,32]{1,0:T(8,128)S(1)} %get-tuple-element.92.refs_8_), channel_id=1, source_target_pairs={{0,2},{1,3},{2,0},{3,1},{4,6},{5,7},{6,4},{7,5},{8,10},{9,11},{10,... | collective-permute-start | bytes 3080 | tf_op jit(solution)/shard_map/ppermute | solution.py:433
  111.6 2.0 %collective-permute-start.13 = (bf16[128,256]{1,0:T(8,128)(2,1)S(1)}, bf16[128,256]{1,0:T(8,128)(2,1)S(1)}, u32[]{:S(2)}, u32[]{:S(2)}) collective-permute-start(bf16[128,256]{1,0:T(8,128)(2,1)S(1)} %get-tuple-element.73), channel_id=1, source_target_pairs={{0,3},{1,2},{2,1},{3,0},{4,7},{5,6},{6,5},{7,4},{8,11},{9,10},{10,... | collective-permute-start | bytes 196616 | tf_op jit(solution)/shard_map/ppermute | solution.py:433
  116.0 2.0 %collective-permute-start.25 = (bf16[128,256]{1,0:T(8,128)(2,1)S(1)}, bf16[128,256]{1,0:T(8,128)(2,1)S(1)}, u32[]{:S(2)}, u32[]{:S(2)}) collective-permute-start(bf16[128,256]{1,0:T(8,128)(2,1)S(1)} %get-tuple-element.91), channel_id=1, source_target_pairs={{0,3},{1,2},{2,1},{3,0},{4,7},{5,6},{6,5},{7,4},{8,11},{9,10},{10,... | collective-permute-start | bytes 196616 | tf_op jit(solution)/shard_map/ppermute | solution.py:433
  118.8 2.1 %collective-permute-done.24.refs_6_ = bf16[128,256]{1,0:T(8,128)(2,1)S(1)} collective-permute-done((bf16[128,256]{1,0:T(8,128)(2,1)S(1)}, bf16[128,256]{1,0:T(8,128)(2,1)S(1)}, u32[]{:S(2)}, u32[]{:S(2)}) %collective-permute-start.24) | collective-permute-done | bytes 65568 | tf_op jit(solution)/shard_map/ppermute | solution.py:433
  (57 shorter events, 20.7 us)
Async XLA Ops:
  0.6 22.1 %copy-start.7 = (s32[1,4]{1,0:T(1,128)S(1)}, s32[1,4]{1,0:T(1,128)}, u32[]{:S(2)}) copy-start(s32[1,4]{1,0:T(1,128)} %param.7) | copy-start | bytes 52
  2.5 16.5 %collective-permute-start = (bf16[384,256]{1,0:T(8,128)(2,1)S(1)}, bf16[384,256]{1,0:T(8,128)(2,1)S(1)}, u32[]{:S(2)}, u32[]{:S(2)}) collective-permute-start(bf16[384,256]{1,0:T(8,128)(2,1)S(1)} %constant_dynamic-update-slice_fusion.refs_0_), channel_id=1, source_target_pairs={{0,1},{1,0},{2,3},{3,2},{4,5},{5,4},{6,7},{7,6},{8,9},{9,8},{10,11... | collective-permute-start | bytes 589832 | tf_op jit(solution)/shard_map/ppermute | solution.py:433
  5.6 17.2 %collective-permute-start.1 = (bf16[384,256]{1,0:T(8,128)(2,1)S(1)}, bf16[384,256]{1,0:T(8,128)(2,1)S(1)}, u32[]{:S(2)}, u32[]{:S(2)}) collective-permute-start(bf16[384,256]{1,0:T(8,128)(2,1)S(1)} %constant_dynamic-update-slice_fusion.refs_0_), channel_id=1, source_target_pairs={{0,2},{1,3},{2,0},{3,1},{4,6},{5,7},{6,4},{7,5},{8,10},{9,11},{10,... | collective-permute-start | bytes 589832 | tf_op jit(solution)/shard_map/ppermute | solution.py:433
  8.2 14.6 %collective-permute-start.2 = (bf16[384,256]{1,0:T(8,128)(2,1)S(1)}, bf16[384,256]{1,0:T(8,128)(2,1)S(1)}, u32[]{:S(2)}, u32[]{:S(2)}) collective-permute-start(bf16[384,256]{1,0:T(8,128)(2,1)S(1)} %constant_dynamic-update-slice_fusion.refs_0_), channel_id=1, source_target_pairs={{0,3},{1,2},{2,1},{3,0},{4,7},{5,6},{6,5},{7,4},{8,11},{9,10},{10,... | collective-permute-start | bytes 589832 | tf_op jit(solution)/shard_map/ppermute | solution.py:433
  42.7 9.6 %collective-permute-start.3 = (bf16[384,256]{1,0:T(8,128)(2,1)S(1)}, bf16[384,256]{1,0:T(8,128)(2,1)S(1)}, u32[]{:S(2)}, u32[]{:S(2)}) collective-permute-start(bf16[384,256]{1,0:T(8,128)(2,1)S(1)} %get-tuple-element.54), channel_id=1, source_target_pairs={{0,1},{1,0},{2,3},{3,2},{4,5},{5,4},{6,7},{7,6},{8,9},{9,8},{10,11... | collective-permute-start | bytes 589832 | tf_op jit(solution)/shard_map/ppermute | solution.py:433
  46.0 16.7 %collective-permute-start.4 = (bf16[384,256]{1,0:T(8,128)(2,1)S(1)}, bf16[384,256]{1,0:T(8,128)(2,1)S(1)}, u32[]{:S(2)}, u32[]{:S(2)}) collective-permute-start(bf16[384,256]{1,0:T(8,128)(2,1)S(1)} %get-tuple-element.55), channel_id=1, source_target_pairs={{0,2},{1,3},{2,0},{3,1},{4,6},{5,7},{6,4},{7,5},{8,10},{9,11},{10,... | collective-permute-start | bytes 589832 | tf_op jit(solution)/shard_map/ppermute | solution.py:433
  47.0 15.7 %collective-permute-start.5 = (bf16[384,256]{1,0:T(8,128)(2,1)S(1)}, bf16[384,256]{1,0:T(8,128)(2,1)S(1)}, u32[]{:S(2)}, u32[]{:S(2)}) collective-permute-start(bf16[384,256]{1,0:T(8,128)(2,1)S(1)} %get-tuple-element.56), channel_id=1, source_target_pairs={{0,3},{1,2},{2,1},{3,0},{4,7},{5,6},{6,5},{7,4},{8,11},{9,10},{10,... | collective-permute-start | bytes 589832 | tf_op jit(solution)/shard_map/ppermute | solution.py:433
  62.7 3.4 %copy-start = (f32[1,1,8192,256]{3,2,1,0:T(8,128)S(1)}, f32[1,1,8192,256]{3,2,1,0:T(8,128)}, u32[]{:S(2)}) copy-start(f32[1,1,8192,256]{3,2,1,0:T(8,128)} %param.13) | copy-start | bytes 25165828
  68.9 3.5 %copy-start.1 = (f32[1,1,8192,256]{3,2,1,0:T(8,128)S(1)}, f32[1,1,8192,256]{3,2,1,0:T(8,128)}, u32[]{:S(2)}) copy-start(f32[1,1,8192,256]{3,2,1,0:T(8,128)} %param.13) | copy-start | bytes 25165828
  71.6 2.9 %collective-permute-start.6 = (bf16[4,512,256]{2,1,0:T(8,128)(2,1)S(1)}, bf16[4,512,256]{2,1,0:T(8,128)(2,1)S(1)}, u32[]{:S(2)}, u32[]{:S(2)}) collective-permute-start(bf16[4,512,256]{2,1,0:T(8,128)(2,1)S(1)} %get-tuple-element.61), channel_id=1, source_target_pairs={{0,4},{4,0},{8,12},{12,8},{16,20},{20,16},{24,28},{28,24},{1,5},{5... | collective-permute-start | bytes 3145736 | tf_op jit(solution)/shard_map/ppermute | solution.py:430
  74.4 5.4 %collective-permute-start.14 = (bf16[4,512,256]{2,1,0:T(8,128)(2,1)S(1)}, bf16[4,512,256]{2,1,0:T(8,128)(2,1)S(1)}, u32[]{:S(2)}, u32[]{:S(2)}) collective-permute-start(bf16[4,512,256]{2,1,0:T(8,128)(2,1)S(1)} %get-tuple-element.74), channel_id=1, source_target_pairs={{0,4},{4,0},{8,12},{12,8},{16,20},{20,16},{24,28},{28,24},{1,5},{5... | collective-permute-start | bytes 3145736 | tf_op jit(solution)/shard_map/ppermute | solution.py:430
  76.7 9.2 %collective-permute-start.7 = (bf16[2,512,128]{2,1,0:T(8,128)(2,1)S(1)}, bf16[2,512,128]{2,1,0:T(8,128)(2,1)S(1)}, u32[]{:S(2)}, u32[]{:S(2)}) collective-permute-start(bf16[2,512,128]{2,1,0:T(8,128)(2,1)S(1)} %get-tuple-element.63), channel_id=1, source_target_pairs={{0,8},{4,12},{8,0},{12,4},{16,24},{20,28},{24,16},{28,20},{1,9},{5... | collective-permute-start | bytes 786440 | tf_op jit(solution)/shard_map/ppermute | solution.py:430
  78.3 9.1 %collective-permute-start.8 = (bf16[2,512,128]{2,1,0:T(8,128)(2,1)S(1)}, bf16[2,512,128]{2,1,0:T(8,128)(2,1)S(1)}, u32[]{:S(2)}, u32[]{:S(2)}) collective-permute-start(bf16[2,512,128]{2,1,0:T(8,128)(2,1)S(1)} %get-tuple-element.65), channel_id=1, source_target_pairs={{0,16},{4,20},{8,24},{12,28},{16,0},{20,4},{24,8},{28,12},{1,17},{... | collective-permute-start | bytes 786440 | tf_op jit(solution)/shard_map/ppermute | solution.py:430
  82.1 9.4 %collective-permute-start.15 = (bf16[2,512,128]{2,1,0:T(8,128)(2,1)S(1)}, bf16[2,512,128]{2,1,0:T(8,128)(2,1)S(1)}, u32[]{:S(2)}, u32[]{:S(2)}) collective-permute-start(bf16[2,512,128]{2,1,0:T(8,128)(2,1)S(1)} %get-tuple-element.76), channel_id=1, source_target_pairs={{0,8},{4,12},{8,0},{12,4},{16,24},{20,28},{24,16},{28,20},{1,9},{5... | collective-permute-start | bytes 786440 | tf_op jit(solution)/shard_map/ppermute | solution.py:430
  82.7 10.4 %collective-permute-start.16 = (bf16[2,512,128]{2,1,0:T(8,128)(2,1)S(1)}, bf16[2,512,128]{2,1,0:T(8,128)(2,1)S(1)}, u32[]{:S(2)}, u32[]{:S(2)}) collective-permute-start(bf16[2,512,128]{2,1,0:T(8,128)(2,1)S(1)} %get-tuple-element.78), channel_id=1, source_target_pairs={{0,16},{4,20},{8,24},{12,28},{16,0},{20,4},{24,8},{28,12},{1,17},{... | collective-permute-start | bytes 786440 | tf_op jit(solution)/shard_map/ppermute | solution.py:430
  87.6 8.1 %collective-permute-start.9 = (bf16[1,512,128]{2,1,0:T(8,128)(2,1)S(1)}, bf16[1,512,128]{2,1,0:T(8,128)(2,1)S(1)}, u32[]{:S(2)}, u32[]{:S(2)}) collective-permute-start(bf16[1,512,128]{2,1,0:T(8,128)(2,1)S(1)} %get-tuple-element.67), channel_id=1, source_target_pairs={{0,16},{4,20},{8,24},{12,28},{16,0},{20,4},{24,8},{28,12},{1,17},{... | collective-permute-start | bytes 393224 | tf_op jit(solution)/shard_map/ppermute | solution.py:430
  89.2 6.6 %collective-permute-start.10 = (bf16[1,512,128]{2,1,0:T(8,128)(2,1)S(1)}, bf16[1,512,128]{2,1,0:T(8,128)(2,1)S(1)}, u32[]{:S(2)}, u32[]{:S(2)}) collective-permute-start(bf16[1,512,128]{2,1,0:T(8,128)(2,1)S(1)} %get-tuple-element.69), channel_id=1, source_target_pairs={{0,8},{4,12},{8,0},{12,4},{16,24},{20,28},{24,16},{28,20},{1,9},{5... | collective-permute-start | bytes 393224 | tf_op jit(solution)/shard_map/ppermute | solution.py:430
  89.7 1.2 collective-permute-start.17
  93.2 13.4 %collective-permute-start.18 = (bf16[1,512,128]{2,1,0:T(8,128)(2,1)S(1)}, bf16[1,512,128]{2,1,0:T(8,128)(2,1)S(1)}, u32[]{:S(2)}, u32[]{:S(2)}) collective-permute-start(bf16[1,512,128]{2,1,0:T(8,128)(2,1)S(1)} %get-tuple-element.84), channel_id=1, source_target_pairs={{0,16},{4,20},{8,24},{12,28},{16,0},{20,4},{24,8},{28,12},{1,17},{... | collective-permute-start | bytes 393224 | tf_op jit(solution)/shard_map/ppermute | solution.py:430
  94.8 11.9 %collective-permute-start.19 = (bf16[1,512,128]{2,1,0:T(8,128)(2,1)S(1)}, bf16[1,512,128]{2,1,0:T(8,128)(2,1)S(1)}, u32[]{:S(2)}, u32[]{:S(2)}) collective-permute-start(bf16[1,512,128]{2,1,0:T(8,128)(2,1)S(1)} %get-tuple-element.86), channel_id=1, source_target_pairs={{0,8},{4,12},{8,0},{12,4},{16,24},{20,28},{24,16},{28,20},{1,9},{5... | collective-permute-start | bytes 393224 | tf_op jit(solution)/shard_map/ppermute | solution.py:430
  95.8 20.2 %collective-permute-start.11 = (bf16[128,256]{1,0:T(8,128)(2,1)S(1)}, bf16[128,256]{1,0:T(8,128)(2,1)S(1)}, u32[]{:S(2)}, u32[]{:S(2)}) collective-permute-start(bf16[128,256]{1,0:T(8,128)(2,1)S(1)} %get-tuple-element.71), channel_id=1, source_target_pairs={{0,1},{1,0},{2,3},{3,2},{4,5},{5,4},{6,7},{7,6},{8,9},{9,8},{10,11... | collective-permute-start | bytes 196616 | tf_op jit(solution)/shard_map/ppermute | solution.py:433
  98.5 3.6 %collective-permute-start.20 = (f32[8,32]{1,0:T(8,128)S(1)}, f32[8,32]{1,0:T(8,128)S(1)}, u32[]{:S(2)}, u32[]{:S(2)}) collective-permute-start(f32[8,32]{1,0:T(8,128)S(1)} %get-tuple-element.87.refs_4_), channel_id=1, source_target_pairs={{0,8},{4,12},{8,0},{12,4},{16,24},{20,28},{24,16},{28,20},{1,9},{5... | collective-permute-start | bytes 3080 | tf_op jit(solution)/shard_map/ppermute | solution.py:430
  99.6 3.9 %collective-permute-start.21 = (f32[8,32]{1,0:T(8,128)S(1)}, f32[8,32]{1,0:T(8,128)S(1)}, u32[]{:S(2)}, u32[]{:S(2)}) collective-permute-start(f32[8,32]{1,0:T(8,128)S(1)} %get-tuple-element.87.refs_4_), channel_id=1, source_target_pairs={{0,16},{4,20},{8,24},{12,28},{16,0},{20,4},{24,8},{28,12},{1,17},{... | collective-permute-start | bytes 3080 | tf_op jit(solution)/shard_map/ppermute | solution.py:430
  102.1 4.5 %collective-permute-start.22 = (f32[8,32]{1,0:T(8,128)S(1)}, f32[8,32]{1,0:T(8,128)S(1)}, u32[]{:S(2)}, u32[]{:S(2)}) collective-permute-start(f32[8,32]{1,0:T(8,128)S(1)} %get-tuple-element.87.refs_4_), channel_id=1, source_target_pairs={{0,24},{4,28},{8,16},{12,20},{16,8},{20,12},{24,0},{28,4},{1,25},{... | collective-permute-start | bytes 3080 | tf_op jit(solution)/shard_map/ppermute | solution.py:430
  106.7 4.8 %collective-permute-start.26 = (f32[8,32]{1,0:T(8,128)S(1)}, f32[8,32]{1,0:T(8,128)S(1)}, u32[]{:S(2)}, u32[]{:S(2)}) collective-permute-start(f32[8,32]{1,0:T(8,128)S(1)} %get-tuple-element.92.refs_8_), channel_id=1, source_target_pairs={{0,1},{1,0},{2,3},{3,2},{4,5},{5,4},{6,7},{7,6},{8,9},{9,8},{10,11... | collective-permute-start | bytes 3080 | tf_op jit(solution)/shard_map/ppermute | solution.py:433
  107.1 6.5 %collective-permute-start.27 = (f32[8,32]{1,0:T(8,128)S(1)}, f32[8,32]{1,0:T(8,128)S(1)}, u32[]{:S(2)}, u32[]{:S(2)}) collective-permute-start(f32[8,32]{1,0:T(8,128)S(1)} %get-tuple-element.92.refs_8_), channel_id=1, source_target_pairs={{0,2},{1,3},{2,0},{3,1},{4,6},{5,7},{6,4},{7,5},{8,10},{9,11},{10,... | collective-permute-start | bytes 3080 | tf_op jit(solution)/shard_map/ppermute | solution.py:433
  109.8 5.5 %collective-permute-start.28 = (f32[8,32]{1,0:T(8,128)S(1)}, f32[8,32]{1,0:T(8,128)S(1)}, u32[]{:S(2)}, u32[]{:S(2)}) collective-permute-start(f32[8,32]{1,0:T(8,128)S(1)} %get-tuple-element.92.refs_8_), channel_id=1, source_target_pairs={{0,3},{1,2},{2,1},{3,0},{4,7},{5,6},{6,5},{7,4},{8,11},{9,10},{10,... | collective-permute-start | bytes 3080 | tf_op jit(solution)/shard_map/ppermute | solution.py:433
  111.2 7.0 %collective-permute-start.12 = (bf16[128,256]{1,0:T(8,128)(2,1)S(1)}, bf16[128,256]{1,0:T(8,128)(2,1)S(1)}, u32[]{:S(2)}, u32[]{:S(2)}) collective-permute-start(bf16[128,256]{1,0:T(8,128)(2,1)S(1)} %get-tuple-element.72), channel_id=1, source_target_pairs={{0,2},{1,3},{2,0},{3,1},{4,6},{5,7},{6,4},{7,5},{8,10},{9,11},{10,... | collective-permute-start | bytes 196616 | tf_op jit(solution)/shard_map/ppermute | solution.py:433
  111.6 6.6 %collective-permute-start.13 = (bf16[128,256]{1,0:T(8,128)(2,1)S(1)}, bf16[128,256]{1,0:T(8,128)(2,1)S(1)}, u32[]{:S(2)}, u32[]{:S(2)}) collective-permute-start(bf16[128,256]{1,0:T(8,128)(2,1)S(1)} %get-tuple-element.73), channel_id=1, source_target_pairs={{0,3},{1,2},{2,1},{3,0},{4,7},{5,6},{6,5},{7,4},{8,11},{9,10},{10,... | collective-permute-start | bytes 196616 | tf_op jit(solution)/shard_map/ppermute | solution.py:433
  113.6 5.2 %collective-permute-start.23 = (bf16[128,256]{1,0:T(8,128)(2,1)S(1)}, bf16[128,256]{1,0:T(8,128)(2,1)S(1)}, u32[]{:S(2)}, u32[]{:S(2)}) collective-permute-start(bf16[128,256]{1,0:T(8,128)(2,1)S(1)} %get-tuple-element.89), channel_id=1, source_target_pairs={{0,1},{1,0},{2,3},{3,2},{4,5},{5,4},{6,7},{7,6},{8,9},{9,8},{10,11... | collective-permute-start | bytes 196616 | tf_op jit(solution)/shard_map/ppermute | solution.py:433
  115.3 5.6 %collective-permute-start.24 = (bf16[128,256]{1,0:T(8,128)(2,1)S(1)}, bf16[128,256]{1,0:T(8,128)(2,1)S(1)}, u32[]{:S(2)}, u32[]{:S(2)}) collective-permute-start(bf16[128,256]{1,0:T(8,128)(2,1)S(1)} %get-tuple-element.90), channel_id=1, source_target_pairs={{0,2},{1,3},{2,0},{3,1},{4,6},{5,7},{6,4},{7,5},{8,10},{9,11},{10,... | collective-permute-start | bytes 196616 | tf_op jit(solution)/shard_map/ppermute | solution.py:433
  116.0 6.2 %collective-permute-start.25 = (bf16[128,256]{1,0:T(8,128)(2,1)S(1)}, bf16[128,256]{1,0:T(8,128)(2,1)S(1)}, u32[]{:S(2)}, u32[]{:S(2)}) collective-permute-start(bf16[128,256]{1,0:T(8,128)(2,1)S(1)} %get-tuple-element.91), channel_id=1, source_target_pairs={{0,3},{1,2},{2,1},{3,0},{4,7},{5,6},{6,5},{7,4},{8,11},{9,10},{10,... | collective-permute-start | bytes 196616 | tf_op jit(solution)/shard_map/ppermute | solution.py:433
  (5 other events, 10.5 us)

commit v3 on v2

v3 whole, which is shorter than its diff:
```python
import functools

import jax
import jax.numpy as jnp
from jax import lax
from jax.experimental import pallas as pl
from jax.experimental.pallas import tpu as pltpu
from jax.sharding import PartitionSpec as P

QROWS = 32
LOG2E = 1.4426950408889634
FAR = 1e30
MIB = 1024 * 1024
BF16, F32 = jnp.bfloat16, jnp.float32


def xor_perm(size, mask):
    return [(i, i ^ mask) for i in range(size)]


def whole(shape):
    return pl.BlockSpec(shape, lambda *_: (0,) * len(shape))


def params(mib):
    return pltpu.CompilerParams(vmem_limit_bytes=mib * MIB)


def prepare_kernel(q_ref, do_ref, a_ref, e_ref, q_out, do_out, a_out, e_out):
    q_out[...] = q_ref[...]
    do_out[...] = do_ref[...]
    a_out[...] = a_ref[...].T
    e_out[...] = e_ref[...]


def prepare(queries, out_grad, activations, errors, hd):
    rows, columns = queries.shape
    heads = columns // hd
    model = activations.shape[1]
    tile = model // heads
    width = errors.shape[1]
    head = pl.BlockSpec((rows, hd), lambda i: (0, i))
    stacked = pl.BlockSpec((rows, hd), lambda i: (i, 0))
    error_tile = pl.BlockSpec((tile, width), lambda i: (i, 0))
    return pl.pallas_call(
        prepare_kernel,
        grid=(heads,),
        in_specs=[head, head, pl.BlockSpec((rows, tile), lambda i: (0, i)), error_tile],
        out_specs=[stacked, stacked, pl.BlockSpec((tile, rows), lambda i: (i, 0)), error_tile],
        out_shape=[
            jax.ShapeDtypeStruct((heads * rows, hd), BF16),
            jax.ShapeDtypeStruct((heads * rows, hd), BF16),
            jax.ShapeDtypeStruct((model, rows), BF16),
            jax.ShapeDtypeStruct((model, width), F32),
        ],
        compiler_params=params(56),
        cost_estimate=pl.CostEstimate(
            flops=0, bytes_accessed=4 * rows * (model + 2 * columns) + 8 * model * width, transcendentals=0
        ),
        name="prepare",
    )(queries, out_grad, activations, errors)


CHUNK = 256


def key_value(refs):
    if len(refs) == 2:
        return refs[0][...], refs[1][...]
    hd = refs[0].shape[1] // 2
    return refs[0][:, :hd], refs[0][:, hd:]


def score_chunk(k, v, q_ref, do_ref, at, own, first_lane):
    nt = (((1,), (1,)), ((), ()))
    lanes = pl.ds(at, CHUNK)
    s = lax.dot_general(k, q_ref[lanes, :], nt, preferred_element_type=F32)
    dp = lax.dot_general(v, do_ref[lanes, :], nt, preferred_element_type=F32)
    if own:
        rows = k.shape[0]
        key_at = lax.broadcasted_iota(jnp.int32, s.shape, 0)
        query_at = lax.broadcasted_iota(jnp.int32, s.shape, 1) + first_lane
        query_at = jnp.where(query_at >= rows, query_at - rows, query_at)
        s = jnp.where(key_at <= query_at, s, -FAR)
    return s, dp


def counted(b, me_ref, span_ref):
    me = me_ref[0]
    return span_ref[me ^ b] < span_ref[me]


def stats_kernel(b, me_ref, span_ref, q_ref, do_ref, *refs):
    if b == 0:
        kv, out = refs[:2], refs[2]
    else:
        kv, before, out = refs[:1], refs[1], refs[2]
    hd = q_ref.shape[1]

    def run():
        k, v = key_value(kv)
        pair = 2 * k.shape[0]
        factor = LOG2E / hd**0.5

        def heads(i, carry):
            for t in range(pair // CHUNK):
                at = pl.multiple_of(i * pair + t * CHUNK, CHUNK)
                lanes = pl.ds(at, CHUNK)
                s, dp = score_chunk(k, v, q_ref, do_ref, at, b == 0, t * CHUNK)
                top = jnp.max(s, axis=0, keepdims=True) * factor
                e = jnp.exp2(s * factor - top)
                total = jnp.sum(e, axis=0, keepdims=True)
                weighted = jnp.sum(e * dp, axis=0, keepdims=True)
                if b > 0:
                    old = before[0:1, lanes]
                    both = jnp.maximum(old, top)
                    old_part, new_part = jnp.exp2(old - both), jnp.exp2(top - both)
                    total = before[1:2, lanes] * old_part + total * new_part
                    weighted = before[2:3, lanes] * old_part + weighted * new_part
                    top = both
                out[0:1, lanes] = top
                out[1:2, lanes] = total
                out[2:3, lanes] = weighted
            return carry

        lax.fori_loop(0, q_ref.shape[0] // pair, heads, 0)

    if b == 0:
        run()
    else:
        keep = counted(b, me_ref, span_ref)
        pl.when(keep)(run)

        @pl.when(jnp.logical_not(keep))
        def _():
            out[...] = before[...]


def block_gradients(own, stats, q_ref, do_ref, kv, p_buf, ds_buf, dk, dv, ds_at):
    k, v = key_value(kv)
    hd = q_ref.shape[1]
    pair = 2 * k.shape[0]
    factor = LOG2E / hd**0.5
    dk[...] = jnp.zeros_like(dk)
    dv[...] = jnp.zeros_like(dv)

    def heads(i, carry):
        for t in range(pair // CHUNK):
            at = pl.multiple_of(i * pair + t * CHUNK, CHUNK)
            lanes = pl.ds(at, CHUNK)
            s, dp = score_chunk(k, v, q_ref, do_ref, at, own, t * CHUNK)
            total = stats[1:2, lanes]
            level = stats[0:1, lanes] + jnp.log(total) * LOG2E
            p = jnp.exp2(s * factor - level)
            ds = (p * (dp - stats[2:3, lanes] / total)).astype(BF16)
            p_buf[:, t * CHUNK : (t + 1) * CHUNK] = p.astype(BF16)
            ds_buf[:, t * CHUNK : (t + 1) * CHUNK] = ds
            ds_at(lanes, ds)
        part = pl.ds(pl.multiple_of(i * pair, pair), pair)
        dk[...] += jnp.dot(ds_buf[...], q_ref[part, :], preferred_element_type=F32)
        dv[...] += jnp.dot(p_buf[...], do_ref[part, :], preferred_element_type=F32)
        return carry

    lax.fori_loop(0, q_ref.shape[0] // pair, heads, 0)
    inverse = 1.0 / hd**0.5
    return dk[...] * inverse, dv[...]


def other_kernel(b, me_ref, span_ref, stats, q_ref, do_ref, kv, out_ref, ds_out, p_buf, ds_buf, dk, dv):
    keep = counted(b, me_ref, span_ref)
    hd = q_ref.shape[1]

    @pl.when(keep)
    def _():
        def ds_at(lanes, ds):
            ds_out[:, lanes] = ds

        dk_sum, dv_sum = block_gradients(False, stats, q_ref, do_ref, (kv,), p_buf, ds_buf, dk, dv, ds_at)
        out_ref[:, :hd] = dk_sum.astype(BF16)
        out_ref[:, hd:] = dv_sum.astype(BF16)

    @pl.when(jnp.logical_not(keep))
    def _():
        out_ref[...] = jnp.zeros_like(out_ref)
        ds_out[...] = jnp.zeros_like(ds_out)


def own_kernel(n, me_ref, span_ref, stats, q_ref, do_ref, k_ref, v_ref, *refs):
    kv_refs, ds_refs = refs[: n - 1], refs[n - 1 : 2 * n - 2]
    out_ref, dq_ref, ds_own, p_buf, ds_buf, dk, dv = refs[2 * n - 2 :]
    rows, hd = k_ref.shape

    def ds_at(lanes, ds):
        ds_own[:, lanes] = ds

    dk_sum, dv_sum = block_gradients(True, stats, q_ref, do_ref, (k_ref, v_ref), p_buf, ds_buf, dk, dv, ds_at)
    out_ref[:, :hd] = dk_sum
    out_ref[:, hd:] = dv_sum
    tn = (((0,), (0,)), ((), ()))

    def head(h, carry):
        lanes = pl.ds(pl.multiple_of(h * rows, 128), rows)
        dq = lax.dot_general(ds_own[:, lanes], k_ref[...], tn, preferred_element_type=F32)
        for kv, ds in zip(kv_refs, ds_refs):
            dq = dq + lax.dot_general(ds[:, lanes], kv[:, :hd], tn, preferred_element_type=F32)
        dq_ref[:, pl.ds(pl.multiple_of(h * hd, hd), hd)] = (dq / hd**0.5).astype(BF16)
        return carry

    lax.fori_loop(0, q_ref.shape[0] // rows, head, 0)


def block_call(kernel, name, products, operands, me, spans, stacked_q, out_shape, scratch):
    tall, hd = stacked_q.shape
    rows = operands[-1].shape[0] if name == "block_stats" else out_shape[0].shape[0]
    return pl.pallas_call(
        kernel,
        grid_spec=pltpu.PrefetchScalarGridSpec(
            num_scalar_prefetch=2,
            grid=(1,),
            in_specs=[whole(x.shape) for x in operands],
            out_specs=[whole(x.shape) for x in out_shape],
            scratch_shapes=scratch,
        ),
        out_shape=out_shape,
        compiler_params=params(24),
        cost_estimate=pl.CostEstimate(
            flops=4 * products * rows * tall * hd, bytes_accessed=8 * tall * hd, transcendentals=rows * tall
        ),
        name=name,
    )(me, spans, *operands)


def attention(me, spans, stacked_q, stacked_do, keys, values, received, swap):
    n = len(received) + 1
    rows, hd = keys.shape
    tall = stacked_q.shape[0]
    stats_shape = [jax.ShapeDtypeStruct((8, tall), F32)]

    def stats_call(b, operands):
        return block_call(
            functools.partial(stats_kernel, b), "block_stats", 2, operands, me, spans, stacked_q, stats_shape, []
        )[0]

    stats = stats_call(0, [stacked_q, stacked_do, keys, values])
    for b, kv in enumerate(received, 1):
        stats = stats_call(b, [stacked_q, stacked_do, kv, stats])
    pair_scratch = [
        pltpu.VMEM((rows, 2 * rows), BF16),
        pltpu.VMEM((rows, 2 * rows), BF16),
        pltpu.VMEM((rows, hd), F32),
        pltpu.VMEM((rows, hd), F32),
    ]
    parts, score_grads = [None] * (n - 1), [None] * (n - 1)
    for b in range(n - 1, 0, -1):
        part, score_grads[b - 1] = block_call(
            functools.partial(other_kernel, b),
            "block_gradients",
            4,
            [stats, stacked_q, stacked_do, received[b - 1]],
            me,
            spans,
            stacked_q,
            [jax.ShapeDtypeStruct((rows, 2 * hd), BF16), jax.ShapeDtypeStruct((rows, tall), BF16)],
            pair_scratch,
        )
        parts[b - 1] = swap(part, b)
    own, query_grad = block_call(
        functools.partial(own_kernel, n),
        "own_gradients",
        8,
        [stats, stacked_q, stacked_do, keys, values, *received, *score_grads],
        me,
        spans,
        stacked_q,
        [jax.ShapeDtypeStruct((rows, 2 * hd), F32), jax.ShapeDtypeStruct((rows, tall // rows * hd), BF16)],
        [pltpu.VMEM((rows, tall), BF16)] + pair_scratch,
    )
    return query_grad, own, parts


def tile_of(step, me_dp, bits, flip):
    mask = flip
    for j in range(1, bits):
        if not (step >> (bits - 1 - j)) & 1:
            mask |= 1 << j
    return me_dp ^ mask


def reversed_step(step, bits):
    return sum(((step >> (bits - 1 - j)) & 1) << (j - 1) for j in range(1, bits))


def corrected_tile(chosen, dest, grads, a_ref, e_ref, top_ref):
    _, n_ctx, _, rows_set, rows = a_ref.shape
    tall = n_ctx * rows_set
    a = a_ref[dest, :, chosen].reshape(tall, rows)
    e = e_ref[dest, :, chosen].reshape(tall, e_ref.shape[4])
    c = jnp.dot(a, grads, preferred_element_type=F32) + e

    mags = jnp.max(jnp.abs(c).reshape(tall // QROWS, QROWS, c.shape[1]), axis=1)
    mags = jnp.max(mags, axis=1, keepdims=True)
    per_set = rows_set // QROWS
    lanes = top_ref.shape[1]
    block = lax.broadcasted_iota(jnp.int32, (tall // QROWS, lanes), 0)
    lane = lax.broadcasted_iota(jnp.int32, (tall // QROWS, lanes), 1)
    shift = per_set.bit_length() - 1
    place = ((block >> shift) * (lanes // n_ctx)) + chosen * per_set + (block & (per_set - 1))
    top_ref[pl.ds(dest, 1), :] = jnp.max(jnp.where(lane == place, mags, 0.0), axis=0, keepdims=True)
    return c


def send_kernel(n_parts, bits, shrink, chosen, with_grads, me_ref, own_ref, *refs):
    part_refs = refs[:n_parts]
    a_ref, e_ref, out_ref, top_ref, *grad_refs = refs[n_parts:]
    if with_grads:
        total = own_ref[...]
        for part in part_refs:
            total = total + part[...].astype(F32)
        total = total.astype(BF16)
        hd = total.shape[1] // 2
        grad_refs[0][...] = total[:, :hd]
        grad_refs[1][...] = total[:, hd:]
        grad_refs[2][...] = total
    else:
        total = own_ref[...]
    top_ref[...] = jnp.zeros_like(top_ref)
    for step in range(out_ref.shape[0]):
        dest = tile_of(step, me_ref[0], bits, 1)
        c = corrected_tile(chosen, dest, total, a_ref, e_ref, top_ref)
        out_ref[step] = (c * shrink).astype(BF16)


def keep_kernel(bits, shrink, chosen, me_ref, grads, got_ref, a_ref, e_ref, *outs):
    low_away, low_stay, high_away, high_stay, top_ref = outs
    half = low_away.shape[0]
    hd = low_away.shape[2]
    total = grads[...]
    top_ref[...] = jnp.zeros_like(top_ref)
    for step in range(2 * half):
        dest = tile_of(step, me_ref[0], bits, 0)
        c = corrected_tile(chosen, dest, total, a_ref, e_ref, top_ref)
        c = (c * shrink + got_ref[step].astype(F32)).astype(BF16)
        back = reversed_step(step, bits)
        for at, part, away, stay in ((step, c[:, :hd], low_away, low_stay), (back, c[:, hd:], high_away, high_stay)):
            if at < half:
                away[at] = part
            else:
                stay[at - half] = part


def tile_call(kernel, name, me, operands, out_shape, a, e):
    n_dp, n_ctx, _, rows_set, rows = a.shape
    tall = n_dp // 2 * n_ctx * rows_set
    width = e.shape[4]
    return pl.pallas_call(
        kernel,
        grid_spec=pltpu.PrefetchScalarGridSpec(
            num_scalar_prefetch=1,
            grid=(1,),
            in_specs=[whole(x.shape) for x in operands] + [whole(a.shape), whole(e.shape)],
            out_specs=[whole(x.shape) for x in out_shape],
        ),
        out_shape=out_shape,
        compiler_params=params(28),
        cost_estimate=pl.CostEstimate(
            flops=2 * tall * rows * width, bytes_accessed=tall * (2 * rows + 6 * width), transcendentals=0
        ),
        name=name,
    )(me, *operands, a, e)


def send_tiles(me, own, parts, a, e, chosen, shrink, with_grads):
    n_dp, n_ctx, sets, rows_set, rows = a.shape
    bits = n_dp.bit_length() - 1
    width = e.shape[4]
    tall = n_ctx * rows_set
    out_shape = [
        jax.ShapeDtypeStruct((n_dp // 2, tall, width), BF16),
        jax.ShapeDtypeStruct((n_dp, sets * tall // QROWS), F32),
    ]
    if with_grads:
        out_shape += [jax.ShapeDtypeStruct((rows, columns), BF16) for columns in (width // 2, width // 2, width)]
    kernel = functools.partial(send_kernel, len(parts), bits, shrink, chosen, with_grads)
    return tile_call(kernel, "send_tiles", me, [own, *parts], out_shape, a, e)


def keep_tiles(me, grads, got, a, e, chosen, shrink):
    n_dp, n_ctx, sets, rows_set, rows = a.shape
    bits = n_dp.bit_length() - 1
    tall = n_ctx * rows_set
    half = jax.ShapeDtypeStruct((n_dp // 4, tall, e.shape[4] // 2), BF16)
    out_shape = [half] * 4 + [jax.ShapeDtypeStruct((n_dp, sets * tall // QROWS), F32)]
    kernel = functools.partial(keep_kernel, bits, shrink, chosen)
    return tile_call(kernel, "keep_tiles", me, [grads, got], out_shape, a, e)


def largest(tops, top_out):
    if tops:
        top = tops[0][...]
        for other in tops[1:]:
            top = jnp.maximum(top, other[...])
        top_out[0][...] = top


def add_kernel(n_tops, *refs):
    low, low_got, high, high_got = refs[:4]
    tops = refs[4 : 4 + n_tops]
    low_away, low_stay, high_away, high_stay, *top_out = refs[4 + n_tops :]
    half = low_away.shape[0]
    for mine, got, away, stay in ((low, low_got, low_away, low_stay), (high, high_got, high_away, high_stay)):
        away[...] = (mine[:half].astype(F32) + got[:half].astype(F32)).astype(BF16)
        stay[...] = (mine[half:].astype(F32) + got[half:].astype(F32)).astype(BF16)
    largest(tops, top_out)


def add_stage(low, low_got, high, high_got, tops):
    m, tall, hd = low.shape
    half = jax.ShapeDtypeStruct((m // 2, tall, hd), BF16)
    return pl.pallas_call(
        functools.partial(add_kernel, len(tops)),
        out_shape=[half] * 4 + [jax.ShapeDtypeStruct(top.shape, F32) for top in tops[:1]],
        compiler_params=params(16),
        cost_estimate=pl.CostEstimate(flops=2 * low.size, bytes_accessed=12 * low.size, transcendentals=0),
        name="add_stage",
    )(low, low_got, high, high_got, *tops)


def last_kernel(n_ctx, n_tops, me_ref, *refs):
    low, low_got, high, high_got = refs[:4]
    tops = refs[4 : 4 + n_tops]
    outs, top_out = refs[4 + n_tops : 4 + n_tops + n_ctx], refs[4 + n_tops + n_ctx :]
    hd = low.shape[2]
    rows_set = low.shape[1] // n_ctx
    for b in range(n_ctx):
        part = pl.ds(pl.multiple_of((me_ref[0] ^ b) * rows_set, rows_set), rows_set)
        for at, mine, got in ((0, low, low_got), (hd, high, high_got)):
            total = mine[0, part, :].astype(F32) + got[0, part, :].astype(F32)
            outs[b][:, at : at + hd] = total.astype(outs[b].dtype)
    largest(tops, top_out)


def last_stage(me_ctx, low, low_got, high, high_got, tops, n_ctx):
    _, tall, hd = low.shape
    shape = (tall // n_ctx, 2 * hd)
    return pl.pallas_call(
        functools.partial(last_kernel, n_ctx, len(tops)),
        grid_spec=pltpu.PrefetchScalarGridSpec(
            num_scalar_prefetch=1,
            grid=(1,),
            in_specs=[whole(low.shape)] * 4 + [whole(top.shape) for top in tops],
            out_specs=[whole(shape)] * n_ctx + [whole(top.shape) for top in tops[:1]],
        ),
        out_shape=[jax.ShapeDtypeStruct(shape, F32)]
        + [jax.ShapeDtypeStruct(shape, BF16)] * (n_ctx - 1)
        + [jax.ShapeDtypeStruct(top.shape, F32) for top in tops[:1]],
        compiler_params=params(16),
        cost_estimate=pl.CostEstimate(flops=2 * low.size, bytes_accessed=12 * low.size, transcendentals=0),
        name="last_stage",
    )(me_ctx, low, low_got, high, high_got, *tops)


def final_kernel(sets, n_ctx, gain, me_dp_ref, me_ctx_ref, *refs):
    groups = [refs[chosen * n_ctx : (chosen + 1) * n_ctx] for chosen in range(sets)]
    tops = refs[sets * n_ctx : sets * n_ctx + n_ctx]
    out_ref, scale_ref = refs[sets * n_ctx + n_ctx :]
    scale = tops[0][...]
    for other in tops[1:]:
        scale = jnp.maximum(scale, other[...])
    scale_ref[...] = scale + 1e-06
    factors = gain / scale_ref[pl.ds(me_dp_ref[0], 1), :]
    lane = lax.broadcasted_iota(jnp.int32, factors.shape, 1)
    rows_set = groups[0][0].shape[0]
    per_set = rows_set // QROWS
    first = me_ctx_ref[0] * (sets * per_set)
    for chosen, group in enumerate(groups):
        for r in range(per_set):
            part = slice(r * QROWS, (r + 1) * QROWS)
            total = group[0][part, :]
            for other in group[1:]:
                total = total + other[part, :].astype(F32)
            mine = jnp.where(lane == first + (chosen * per_set + r), factors, 0.0)
            at = chosen * rows_set + r * QROWS
            out_ref[at : at + QROWS, :] = total * jnp.sum(mine, axis=1, keepdims=True)


def final_stage(me_dp, me_ctx, groups, tops, gain):
    sets, n_ctx = len(groups), len(groups[0])
    rows_set, width = groups[0][0].shape
    return pl.pallas_call(
        functools.partial(final_kernel, sets, n_ctx, gain),
        grid_spec=pltpu.PrefetchScalarGridSpec(
            num_scalar_prefetch=2,
            grid=(1,),
            in_specs=[whole((rows_set, width))] * (sets * n_ctx) + [whole(tops[0].shape)] * n_ctx,
            out_specs=[whole((sets * rows_set, width)), whole(tops[0].shape)],
        ),
        out_shape=[
            jax.ShapeDtypeStruct((sets * rows_set, width), F32),
            jax.ShapeDtypeStruct(tops[0].shape, F32),
        ],
        compiler_params=params(8),
        cost_estimate=pl.CostEstimate(
            flops=4 * sets * rows_set * width, bytes_accessed=16 * sets * rows_set * width, transcendentals=0
        ),
        name="final_stage",
    )(me_dp, me_ctx, *[x for group in groups for x in group], *tops)


def local(n_dp, n_ctx, sets, span_order, queries, keys, values, out_grad, activations, error_feedback):
    rows, hd = keys.shape
    model = activations.shape[1]
    rows_set = model // (n_dp * n_ctx * sets)
    me_dp = lax.axis_index("dp").astype(jnp.int32)[None]
    me_ctx = lax.axis_index("context").astype(jnp.int32)[None]
    bits = n_dp.bit_length() - 1

    def swap_dp(x, mask):
        return lax.ppermute(x, "dp", xor_perm(n_dp, mask))

    def swap_ctx(x, mask):
        return lax.ppermute(x, "context", xor_perm(n_ctx, mask))

    pairs = jnp.concatenate([keys, values], axis=1)
    received = [swap_ctx(pairs, b) for b in range(1, n_ctx)]
    stacked_q, stacked_do, acts, errors = prepare(queries, out_grad, activations, error_feedback[0, 0], hd)
    query_grad, own, parts = attention(
        me_ctx, span_order[0], stacked_q, stacked_do, keys, values, received, swap_ctx
    )

    shrink = 1.0 / (n_dp * n_ctx)
    acts = acts.reshape(n_dp, n_ctx, sets, rows_set, rows)
    errors = errors.reshape(n_dp, n_ctx, sets, rows_set, 2 * hd)
    got, tops = [], []
    for chosen in range(sets):
        if chosen == 0:
            out, top, key_grad, value_grad, grads = send_tiles(me_dp, own, parts, acts, errors, 0, shrink, True)
        else:
            out, top = send_tiles(me_dp, grads, [], acts, errors, chosen, shrink, False)
        got.append(swap_dp(out, 1))
        tops.append(top)

    halves = []
    for chosen in range(sets):
        *half, top = keep_tiles(me_dp, grads, got[chosen], acts, errors, chosen, shrink)
        halves.append(half)
        tops.append(top)
    top = functools.reduce(jnp.maximum, tops)

    groups = []
    for chosen in range(sets):
        low_away, low, high_away, high = halves[chosen]
        for stage in range(1, bits):
            low_got = swap_dp(low_away, 1 << stage)
            high_got = swap_dp(high_away, 1 << (bits - stage))
            tops = []
            if chosen == sets - 1:
                masks = [1] if stage == 1 else range(2, n_dp, 2) if stage == 2 else []
                tops = [top] + [swap_dp(top, mask) for mask in masks]
            if stage < bits - 1:
                low_away, low, high_away, high, *top_out = add_stage(low, low_got, high, high_got, tops)
            else:
                outs = last_stage(me_ctx, low, low_got, high, high_got, tops, n_ctx)
                mine, *away = outs[:n_ctx]
                top_out = outs[n_ctx:]
            if tops:
                top = top_out[0]
        groups.append([mine] + [swap_ctx(part, b + 1) for b, part in enumerate(away)])
    tops = [top] + [swap_ctx(top, b) for b in range(1, n_ctx)]
    payload, scale = final_stage(me_dp, me_ctx, groups, tops, 7.0 / shrink)
    return query_grad, key_grad, value_grad, payload, scale.reshape(-1)


def solution(mesh):
    tokens = P(("dp", "context"), None)
    return jax.shard_map(
        functools.partial(local, mesh.shape["dp"], mesh.shape["context"], 2),
        mesh=mesh,
        in_specs=(P("dp", None), tokens, tokens, tokens, tokens, tokens, P("dp", "context", None, None)),
        out_specs=(tokens, tokens, tokens, tokens, P()),
        check_vma=False,
    )
```

time: 124 us -> 116 us (0.935)
  starting transfers between devices: 36.7 us -> 49.6 us
  local copies, waits for them, and re-layouts: 17.1 us -> 4.76 us
  waiting for transfers between devices: 35.6 us -> 24.8 us
    ppermute x15, waiting for transfers between devices: 22.8 us -> 5.65 us  [swap_ctx(): return lax.ppermute(x, 'context', xor_perm(n_ctx, mask))]
    unnamed x17 -> x19, local copies, waits for them, and re-layouts: 15.6 us -> 3.2 us
    ppermute x15, starting transfers between devices: 24.8 us -> 35.9 us  [swap_ctx(): return lax.ppermute(x, 'context', xor_perm(n_ctx, mask))]
    pallas_call x1, Pallas kernels: 3.06 us -> 13.7 us  [prepare(): pl.pallas_call(prepare_kernel, grid=(heads,), in_specs=[head, head, pl.Bl...]
    pallas_call x5 -> x12, Pallas kernels: 29.2 us -> 19.5 us  [the longest x8 15.8 us: block_call(): pl.pallas_call(kernel, grid_spec=pltpu.PrefetchScalarGridSpec(num_scalar_...]
    ppermute x14, waiting for transfers between devices: 12.8 us -> 19.2 us  [swap_dp(): return lax.ppermute(x, 'dp', xor_perm(n_dp, mask))]
    ppermute x14, starting transfers between devices: 11.9 us -> 13.7 us  [swap_dp(): return lax.ppermute(x, 'dp', xor_perm(n_dp, mask))]
  transfers between devices with their start and end apart: 29 -> 29, of which waited for: 16 -> 14; matrix products, arithmetic and copies ran while one was open for 0% -> 0% of each run, Pallas kernels for 8% -> 27%
where the time goes in v3:
time: 116 us; the launch traced here: 115 us
  starting transfers between devices  49.6 us (43%)
  Pallas kernels  34.5 us (30%)
  waiting for transfers between devices  24.8 us (21%)
  local copies, waits for them, and re-layouts  4.76 us (4%)
    ppermute x15, starting transfers between devices, swap_ctx(): return lax.ppermute(x, 'context', xor_perm(n_ctx, mask))  35.9 us
    ppermute x14, waiting for transfers between devices, swap_dp(): return lax.ppermute(x, 'dp', xor_perm(n_dp, mask))  19.2 us
    pallas_call x8, Pallas kernels, block_call(): pl.pallas_call(kernel, grid_spec=pltpu.PrefetchScalarGridSpec(num_scalar_...  15.8 us
    pallas_call x1, Pallas kernels, prepare(): pl.pallas_call(prepare_kernel, grid=(heads,), in_specs=[head, head, pl.Bl...  13.7 us
    ppermute x14, starting transfers between devices, swap_dp(): return lax.ppermute(x, 'dp', xor_perm(n_dp, mask))  13.7 us
    ppermute x15, waiting for transfers between devices, swap_ctx(): return lax.ppermute(x, 'context', xor_perm(n_ctx, mask))  5.65 us
    pallas_call x4, Pallas kernels, tile_call(): pl.pallas_call(kernel, grid_spec=pltpu.PrefetchScalarGridSpec(num_scalar_...  3.71 us
    unnamed x19, local copies, waits for them, and re-layouts  3.2 us
  transfers between devices with their start and end apart: 29, of which 14 were waited for; matrix products, arithmetic and copies ran while one was open for 0% of the time, Pallas kernels for 27%

profile of v3, /device:TPU:0, one launch (start us, length us, event | category | flops | bytes accessed | tf_op | source)
XLA Modules:
  0.0 114.5 jit_solution(11580044868162417375)
XLA Ops:
  2.5 3.1 %collective-permute-start.2 = (bf16[384,256]{1,0:T(8,128)(2,1)S(1)}, bf16[384,256]{1,0:T(8,128)(2,1)S(1)}, u32[]{:S(2)}, u32[]{:S(2)}) collective-permute-start(bf16[384,256]{1,0:T(8,128)(2,1)S(1)} %constant_dynamic-update-slice_fusion), channel_id=1, source_target_pairs={{0,1},{1,0},{2,3},{3,2},{4,5},{5,4},{6,7},{7,6},{8,9},{9,8},{10,11... | collective-permute-start | bytes 589832 | tf_op jit(solution)/shard_map/ppermute | solution.py:521
  5.6 2.6 %collective-permute-start.1 = (bf16[384,256]{1,0:T(8,128)(2,1)S(1)}, bf16[384,256]{1,0:T(8,128)(2,1)S(1)}, u32[]{:S(2)}, u32[]{:S(2)}) collective-permute-start(bf16[384,256]{1,0:T(8,128)(2,1)S(1)} %constant_dynamic-update-slice_fusion), channel_id=1, source_target_pairs={{0,2},{1,3},{2,0},{3,1},{4,6},{5,7},{6,4},{7,5},{8,10},{9,11},{10,... | collective-permute-start | bytes 589832 | tf_op jit(solution)/shard_map/ppermute | solution.py:521
  8.2 13.7 %prepare.1 = (bf16[3072,128]{1,0:T(8,128)(2,1)}, bf16[3072,128]{1,0:T(8,128)(2,1)}, bf16[8192,384]{1,0:T(8,128)(2,1)}, f32[8192,256]{1,0:T(8,128)}) custom-call(bf16[384,1024]{1,0:T(8,128)(2,1)} %q_ref.1, bf16[384,1024]{1,0:T(8,128)(2,1)} %do_ref.1, bf16[384,8192]{1,0:T(8,128)(2,1)} %a_ref.1, f32[8192,256]{1,0:T(8,128)} %bitcast.26), custom_call_target="tpu_custom_call" | custom-call | bytes 32505856 | tf_op jit(solution)/shard_map/prepare/pallas_call | solution.py:45
  21.9 1.1 copy-done
  23.1 1.1 copy-done.1
  24.2 2.9 %block_stats.4.refs_1_ = f32[8,3072]{1,0:T(8,128)S(1)} custom-call(s32[1]{0:T(128)} %bitcast.me_ref.me_ctx_ref, s32[4]{0:T(128)S(1)} %bitcast.18, bf16[3072,128]{1,0:T(8,128)(2,1)S(1)} %copy-done, bf16[3072,128]{1,0:T(8,128)(2,1)S(1)} %copy-done.1, bf16[384,128]{1,0:T(8,128)(2,1)S(1)} %copy-done.2, bf16[384,128]{1,0:T(8,128)(2,1)S(1)} %copy-done.3), custom_call_target="tpu_custom_call" | custom-call | flops 1207959552 | bytes 3145728 | tf_op jit(solution)/shard_map/block_stats/pallas_call | solution.py:215
  29.5 12.0 %collective-permute-start.5 = (bf16[384,256]{1,0:T(8,128)(2,1)S(1)}, bf16[384,256]{1,0:T(8,128)(2,1)S(1)}, u32[]{:S(2)}, u32[]{:S(2)}) collective-permute-start(bf16[384,256]{1,0:T(8,128)(2,1)S(1)} %get-tuple-element.63), channel_id=1, source_target_pairs={{0,3},{1,2},{2,1},{3,0},{4,7},{5,6},{6,5},{7,4},{8,11},{9,10},{10,... | collective-permute-start | bytes 589832 | tf_op jit(solution)/shard_map/ppermute | solution.py:521
  42.3 3.8 %collective-permute-start.4 = (bf16[384,256]{1,0:T(8,128)(2,1)S(1)}, bf16[384,256]{1,0:T(8,128)(2,1)S(1)}, u32[]{:S(2)}, u32[]{:S(2)}) collective-permute-start(bf16[384,256]{1,0:T(8,128)(2,1)S(1)} %get-tuple-element.62), channel_id=1, source_target_pairs={{0,2},{1,3},{2,0},{3,1},{4,6},{5,7},{6,4},{7,5},{8,10},{9,11},{10,... | collective-permute-start | bytes 589832 | tf_op jit(solution)/shard_map/ppermute | solution.py:521
  47.0 3.0 %collective-permute-start.3 = (bf16[384,256]{1,0:T(8,128)(2,1)S(1)}, bf16[384,256]{1,0:T(8,128)(2,1)S(1)}, u32[]{:S(2)}, u32[]{:S(2)}) collective-permute-start(bf16[384,256]{1,0:T(8,128)(2,1)S(1)} %get-tuple-element.61), channel_id=1, source_target_pairs={{0,1},{1,0},{2,3},{3,2},{4,5},{5,4},{6,7},{7,6},{8,9},{9,8},{10,11... | collective-permute-start | bytes 589832 | tf_op jit(solution)/shard_map/ppermute | solution.py:521
  50.0 8.9 %own_gradients.1 = (f32[384,256]{1,0:T(8,128)S(1)}, bf16[384,1024]{1,0:T(8,128)(2,1)}) custom-call(s32[1]{0:T(128)} %bitcast.me_ref.me_ctx_ref, s32[4]{0:T(128)S(1)} %bitcast.25, f32[8,3072]{1,0:T(8,128)S(1)} %block_stats.7.stats, bf16[3072,128]{1,0:T(8,128)(2,1)S(1)} %copy-done, bf16[3072,128]{1,0:T(8,128)(2,1)S(1)} %copy-done.1, ...), custom_call_target="tpu_custom_call" | custom-call | flops 4831838208 | bytes 3145728 | tf_op jit(solution)/shard_map/own_gradients/pallas_call | solution.py:215
  61.4 2.1 %collective-permute-done.14.got_ref = bf16[4,512,256]{2,1,0:T(8,128)(2,1)S(1)} collective-permute-done((bf16[4,512,256]{2,1,0:T(8,128)(2,1)S(1)}, bf16[4,512,256]{2,1,0:T(8,128)(2,1)S(1)}, u32[]{:S(2)}, u32[]{:S(2)}) %collective-permute-start.14) | collective-permute-done | bytes 1048608 | tf_op jit(solution)/shard_map/ppermute | solution.py:518
  65.2 2.5 %collective-permute-start.16 = (bf16[2,512,128]{2,1,0:T(8,128)(2,1)S(1)}, bf16[2,512,128]{2,1,0:T(8,128)(2,1)S(1)}, u32[]{:S(2)}, u32[]{:S(2)}) collective-permute-start(bf16[2,512,128]{2,1,0:T(8,128)(2,1)S(1)} %get-tuple-element.86), channel_id=1, source_target_pairs={{0,16},{4,20},{8,24},{12,28},{16,0},{20,4},{24,8},{28,12},{1,17},{... | collective-permute-start | bytes 786440 | tf_op jit(solution)/shard_map/ppermute | solution.py:518
  68.7 1.5 %collective-permute-start.7 = (bf16[2,512,128]{2,1,0:T(8,128)(2,1)S(1)}, bf16[2,512,128]{2,1,0:T(8,128)(2,1)S(1)}, u32[]{:S(2)}, u32[]{:S(2)}) collective-permute-start(bf16[2,512,128]{2,1,0:T(8,128)(2,1)S(1)} %get-tuple-element.71), channel_id=1, source_target_pairs={{0,8},{4,12},{8,0},{12,4},{16,24},{20,28},{24,16},{28,20},{1,9},{5... | collective-permute-start | bytes 786440 | tf_op jit(solution)/shard_map/ppermute | solution.py:518
  70.3 1.2 %collective-permute-done.17.refs_5_ = f32[8,32]{1,0:T(8,128)S(1)} collective-permute-done((f32[8,32]{1,0:T(8,128)S(1)}, f32[8,32]{1,0:T(8,128)S(1)}, u32[]{:S(2)}, u32[]{:S(2)}) %collective-permute-start.17) | collective-permute-done | bytes 1056 | tf_op jit(solution)/shard_map/ppermute | solution.py:518
  71.4 2.3 %collective-permute-done.15.refs_1_ = bf16[2,512,128]{2,1,0:T(8,128)(2,1)S(1)} collective-permute-done((bf16[2,512,128]{2,1,0:T(8,128)(2,1)S(1)}, bf16[2,512,128]{2,1,0:T(8,128)(2,1)S(1)}, u32[]{:S(2)}, u32[]{:S(2)}) %collective-permute-start.15) | collective-permute-done | bytes 262176 | tf_op jit(solution)/shard_map/ppermute | solution.py:518
  73.7 1.1 collective-permute-done.16.refs_3_
  75.0 2.1 %collective-permute-start.18 = (bf16[1,512,128]{2,1,0:T(8,128)(2,1)S(1)}, bf16[1,512,128]{2,1,0:T(8,128)(2,1)S(1)}, u32[]{:S(2)}, u32[]{:S(2)}) collective-permute-start(bf16[1,512,128]{2,1,0:T(8,128)(2,1)S(1)} %get-tuple-element.92), channel_id=1, source_target_pairs={{0,16},{4,20},{8,24},{12,28},{16,0},{20,4},{24,8},{28,12},{1,17},{... | collective-permute-start | bytes 393224 | tf_op jit(solution)/shard_map/ppermute | solution.py:518
  77.1 1.5 %collective-permute-start.19 = (bf16[1,512,128]{2,1,0:T(8,128)(2,1)S(1)}, bf16[1,512,128]{2,1,0:T(8,128)(2,1)S(1)}, u32[]{:S(2)}, u32[]{:S(2)}) collective-permute-start(bf16[1,512,128]{2,1,0:T(8,128)(2,1)S(1)} %get-tuple-element.94), channel_id=1, source_target_pairs={{0,8},{4,12},{8,0},{12,4},{16,24},{20,28},{24,16},{28,20},{1,9},{5... | collective-permute-start | bytes 393224 | tf_op jit(solution)/shard_map/ppermute | solution.py:518
  79.3 1.1 collective-permute-done.8.refs_3_
  80.6 2.1 %collective-permute-start.9 = (bf16[1,512,128]{2,1,0:T(8,128)(2,1)S(1)}, bf16[1,512,128]{2,1,0:T(8,128)(2,1)S(1)}, u32[]{:S(2)}, u32[]{:S(2)}) collective-permute-start(bf16[1,512,128]{2,1,0:T(8,128)(2,1)S(1)} %get-tuple-element.75), channel_id=1, source_target_pairs={{0,16},{4,20},{8,24},{12,28},{16,0},{20,4},{24,8},{28,12},{1,17},{... | collective-permute-start | bytes 393224 | tf_op jit(solution)/shard_map/ppermute | solution.py:518
  82.7 1.5 %collective-permute-start.10 = (bf16[1,512,128]{2,1,0:T(8,128)(2,1)S(1)}, bf16[1,512,128]{2,1,0:T(8,128)(2,1)S(1)}, u32[]{:S(2)}, u32[]{:S(2)}) collective-permute-start(bf16[1,512,128]{2,1,0:T(8,128)(2,1)S(1)} %get-tuple-element.77), channel_id=1, source_target_pairs={{0,8},{4,12},{8,0},{12,4},{16,24},{20,28},{24,16},{28,20},{1,9},{5... | collective-permute-start | bytes 393224 | tf_op jit(solution)/shard_map/ppermute | solution.py:518
  84.3 4.4 %collective-permute-done.22.refs_7_ = f32[8,32]{1,0:T(8,128)S(1)} collective-permute-done((f32[8,32]{1,0:T(8,128)S(1)}, f32[8,32]{1,0:T(8,128)S(1)}, u32[]{:S(2)}, u32[]{:S(2)}) %collective-permute-start.22) | collective-permute-done | bytes 1056 | tf_op jit(solution)/shard_map/ppermute | solution.py:518
  89.2 3.1 %collective-permute-done.21.refs_6_ = f32[8,32]{1,0:T(8,128)S(1)} collective-permute-done((f32[8,32]{1,0:T(8,128)S(1)}, f32[8,32]{1,0:T(8,128)S(1)}, u32[]{:S(2)}, u32[]{:S(2)}) %collective-permute-start.21) | collective-permute-done | bytes 1056 | tf_op jit(solution)/shard_map/ppermute | solution.py:518
  92.9 3.0 %collective-permute-done.20.refs_5_ = f32[8,32]{1,0:T(8,128)S(1)} collective-permute-done((f32[8,32]{1,0:T(8,128)S(1)}, f32[8,32]{1,0:T(8,128)S(1)}, u32[]{:S(2)}, u32[]{:S(2)}) %collective-permute-start.20) | collective-permute-done | bytes 1056 | tf_op jit(solution)/shard_map/ppermute | solution.py:518
  96.0 1.1 collective-permute-start.23
  97.3 2.2 %collective-permute-start.27 = (f32[8,32]{1,0:T(8,128)S(1)}, f32[8,32]{1,0:T(8,128)S(1)}, u32[]{:S(2)}, u32[]{:S(2)}) collective-permute-start(f32[8,32]{1,0:T(8,128)S(1)} %get-tuple-element.100.refs_8_), channel_id=1, source_target_pairs={{0,2},{1,3},{2,0},{3,1},{4,6},{5,7},{6,4},{7,5},{8,10},{9,11},{10,... | collective-permute-start | bytes 3080 | tf_op jit(solution)/shard_map/ppermute | solution.py:521
  99.5 2.0 %collective-permute-start.26 = (f32[8,32]{1,0:T(8,128)S(1)}, f32[8,32]{1,0:T(8,128)S(1)}, u32[]{:S(2)}, u32[]{:S(2)}) collective-permute-start(f32[8,32]{1,0:T(8,128)S(1)} %get-tuple-element.100.refs_8_), channel_id=1, source_target_pairs={{0,1},{1,0},{2,3},{3,2},{4,5},{5,4},{6,7},{7,6},{8,9},{9,8},{10,11... | collective-permute-start | bytes 3080 | tf_op jit(solution)/shard_map/ppermute | solution.py:521
  102.6 1.5 %collective-permute-start.25 = (bf16[128,256]{1,0:T(8,128)(2,1)S(1)}, bf16[128,256]{1,0:T(8,128)(2,1)S(1)}, u32[]{:S(2)}, u32[]{:S(2)}) collective-permute-start(bf16[128,256]{1,0:T(8,128)(2,1)S(1)} %get-tuple-element.99), channel_id=1, source_target_pairs={{0,3},{1,2},{2,1},{3,0},{4,7},{5,6},{6,5},{7,4},{8,11},{9,10},{10,... | collective-permute-start | bytes 196616 | tf_op jit(solution)/shard_map/ppermute | solution.py:521
  105.1 1.9 %collective-permute-start.12 = (bf16[128,256]{1,0:T(8,128)(2,1)S(1)}, bf16[128,256]{1,0:T(8,128)(2,1)S(1)}, u32[]{:S(2)}, u32[]{:S(2)}) collective-permute-start(bf16[128,256]{1,0:T(8,128)(2,1)S(1)} %get-tuple-element.80), channel_id=1, source_target_pairs={{0,2},{1,3},{2,0},{3,1},{4,6},{5,7},{6,4},{7,5},{8,10},{9,11},{10,... | collective-permute-start | bytes 196616 | tf_op jit(solution)/shard_map/ppermute | solution.py:521
  107.0 1.5 %collective-permute-start.13 = (bf16[128,256]{1,0:T(8,128)(2,1)S(1)}, bf16[128,256]{1,0:T(8,128)(2,1)S(1)}, u32[]{:S(2)}, u32[]{:S(2)}) collective-permute-start(bf16[128,256]{1,0:T(8,128)(2,1)S(1)} %get-tuple-element.81), channel_id=1, source_target_pairs={{0,3},{1,2},{2,1},{3,0},{4,7},{5,6},{6,5},{7,4},{8,11},{9,10},{10,... | collective-permute-start | bytes 196616 | tf_op jit(solution)/shard_map/ppermute | solution.py:521
  109.1 2.0 %collective-permute-done.12.refs_2_ = bf16[128,256]{1,0:T(8,128)(2,1)S(1)} collective-permute-done((bf16[128,256]{1,0:T(8,128)(2,1)S(1)}, bf16[128,256]{1,0:T(8,128)(2,1)S(1)}, u32[]{:S(2)}, u32[]{:S(2)}) %collective-permute-start.12) | collective-permute-done | bytes 65568 | tf_op jit(solution)/shard_map/ppermute | solution.py:521
  111.0 2.1 %collective-permute-done.13.refs_3_ = bf16[128,256]{1,0:T(8,128)(2,1)S(1)} collective-permute-done((bf16[128,256]{1,0:T(8,128)(2,1)S(1)}, bf16[128,256]{1,0:T(8,128)(2,1)S(1)}, u32[]{:S(2)}, u32[]{:S(2)}) %collective-permute-start.13) | collective-permute-done | bytes 65568 | tf_op jit(solution)/shard_map/ppermute | solution.py:521
  (68 shorter events, 17.6 us)
Async XLA Ops:
  2.5 24.6 %collective-permute-start.2 = (bf16[384,256]{1,0:T(8,128)(2,1)S(1)}, bf16[384,256]{1,0:T(8,128)(2,1)S(1)}, u32[]{:S(2)}, u32[]{:S(2)}) collective-permute-start(bf16[384,256]{1,0:T(8,128)(2,1)S(1)} %constant_dynamic-update-slice_fusion), channel_id=1, source_target_pairs={{0,1},{1,0},{2,3},{3,2},{4,5},{5,4},{6,7},{7,6},{8,9},{9,8},{10,11... | collective-permute-start | bytes 589832 | tf_op jit(solution)/shard_map/ppermute | solution.py:521
  5.6 22.1 %collective-permute-start.1 = (bf16[384,256]{1,0:T(8,128)(2,1)S(1)}, bf16[384,256]{1,0:T(8,128)(2,1)S(1)}, u32[]{:S(2)}, u32[]{:S(2)}) collective-permute-start(bf16[384,256]{1,0:T(8,128)(2,1)S(1)} %constant_dynamic-update-slice_fusion), channel_id=1, source_target_pairs={{0,2},{1,3},{2,0},{3,1},{4,6},{5,7},{6,4},{7,5},{8,10},{9,11},{10,... | collective-permute-start | bytes 589832 | tf_op jit(solution)/shard_map/ppermute | solution.py:521
  8.1 20.1 %collective-permute-start = (bf16[384,256]{1,0:T(8,128)(2,1)S(1)}, bf16[384,256]{1,0:T(8,128)(2,1)S(1)}, u32[]{:S(2)}, u32[]{:S(2)}) collective-permute-start(bf16[384,256]{1,0:T(8,128)(2,1)S(1)} %constant_dynamic-update-slice_fusion), channel_id=1, source_target_pairs={{0,3},{1,2},{2,1},{3,0},{4,7},{5,6},{6,5},{7,4},{8,11},{9,10},{10,... | collective-permute-start | bytes 589832 | tf_op jit(solution)/shard_map/ppermute | solution.py:521
  8.2 13.8 %copy-start.2 = (bf16[384,128]{1,0:T(8,128)(2,1)S(1)}, bf16[384,128]{1,0:T(8,128)(2,1)}, u32[]{:S(2)}) copy-start(bf16[384,128]{1,0:T(8,128)(2,1)} %k_ref.1) | copy-start | bytes 294916
  8.2 13.8 %copy-start.3 = (bf16[384,128]{1,0:T(8,128)(2,1)S(1)}, bf16[384,128]{1,0:T(8,128)(2,1)}, u32[]{:S(2)}) copy-start(bf16[384,128]{1,0:T(8,128)(2,1)} %v_ref.1) | copy-start | bytes 294916
  8.2 13.8 %copy-start.4 = (s32[1,4]{1,0:T(1,128)S(1)}, s32[1,4]{1,0:T(1,128)}, u32[]{:S(2)}) copy-start(s32[1,4]{1,0:T(1,128)} %param.7) | copy-start | bytes 52
  29.5 29.4 %collective-permute-start.5 = (bf16[384,256]{1,0:T(8,128)(2,1)S(1)}, bf16[384,256]{1,0:T(8,128)(2,1)S(1)}, u32[]{:S(2)}, u32[]{:S(2)}) collective-permute-start(bf16[384,256]{1,0:T(8,128)(2,1)S(1)} %get-tuple-element.63), channel_id=1, source_target_pairs={{0,3},{1,2},{2,1},{3,0},{4,7},{5,6},{6,5},{7,4},{8,11},{9,10},{10,... | collective-permute-start | bytes 589832 | tf_op jit(solution)/shard_map/ppermute | solution.py:521
  42.3 16.6 %collective-permute-start.4 = (bf16[384,256]{1,0:T(8,128)(2,1)S(1)}, bf16[384,256]{1,0:T(8,128)(2,1)S(1)}, u32[]{:S(2)}, u32[]{:S(2)}) collective-permute-start(bf16[384,256]{1,0:T(8,128)(2,1)S(1)} %get-tuple-element.62), channel_id=1, source_target_pairs={{0,2},{1,3},{2,0},{3,1},{4,6},{5,7},{6,4},{7,5},{8,10},{9,11},{10,... | collective-permute-start | bytes 589832 | tf_op jit(solution)/shard_map/ppermute | solution.py:521
  47.0 11.9 %collective-permute-start.3 = (bf16[384,256]{1,0:T(8,128)(2,1)S(1)}, bf16[384,256]{1,0:T(8,128)(2,1)S(1)}, u32[]{:S(2)}, u32[]{:S(2)}) collective-permute-start(bf16[384,256]{1,0:T(8,128)(2,1)S(1)} %get-tuple-element.61), channel_id=1, source_target_pairs={{0,1},{1,0},{2,3},{3,2},{4,5},{5,4},{6,7},{7,6},{8,9},{9,8},{10,11... | collective-permute-start | bytes 589832 | tf_op jit(solution)/shard_map/ppermute | solution.py:521
  60.8 2.7 %collective-permute-start.14 = (bf16[4,512,256]{2,1,0:T(8,128)(2,1)S(1)}, bf16[4,512,256]{2,1,0:T(8,128)(2,1)S(1)}, u32[]{:S(2)}, u32[]{:S(2)}) collective-permute-start(bf16[4,512,256]{2,1,0:T(8,128)(2,1)S(1)} %get-tuple-element.82), channel_id=1, source_target_pairs={{0,4},{4,0},{8,12},{12,8},{16,20},{20,16},{24,28},{28,24},{1,5},{5... | collective-permute-start | bytes 3145736 | tf_op jit(solution)/shard_map/ppermute | solution.py:518
  60.9 6.8 %collective-permute-start.6 = (bf16[4,512,256]{2,1,0:T(8,128)(2,1)S(1)}, bf16[4,512,256]{2,1,0:T(8,128)(2,1)S(1)}, u32[]{:S(2)}, u32[]{:S(2)}) collective-permute-start(bf16[4,512,256]{2,1,0:T(8,128)(2,1)S(1)} %get-tuple-element.69), channel_id=1, source_target_pairs={{0,4},{4,0},{8,12},{12,8},{16,20},{20,16},{24,28},{28,24},{1,5},{5... | collective-permute-start | bytes 3145736 | tf_op jit(solution)/shard_map/ppermute | solution.py:518
  64.5 9.2 %collective-permute-start.15 = (bf16[2,512,128]{2,1,0:T(8,128)(2,1)S(1)}, bf16[2,512,128]{2,1,0:T(8,128)(2,1)S(1)}, u32[]{:S(2)}, u32[]{:S(2)}) collective-permute-start(bf16[2,512,128]{2,1,0:T(8,128)(2,1)S(1)} %get-tuple-element.84), channel_id=1, source_target_pairs={{0,8},{4,12},{8,0},{12,4},{16,24},{20,28},{24,16},{28,20},{1,9},{5... | collective-permute-start | bytes 786440 | tf_op jit(solution)/shard_map/ppermute | solution.py:518
  65.2 9.7 %collective-permute-start.16 = (bf16[2,512,128]{2,1,0:T(8,128)(2,1)S(1)}, bf16[2,512,128]{2,1,0:T(8,128)(2,1)S(1)}, u32[]{:S(2)}, u32[]{:S(2)}) collective-permute-start(bf16[2,512,128]{2,1,0:T(8,128)(2,1)S(1)} %get-tuple-element.86), channel_id=1, source_target_pairs={{0,16},{4,20},{8,24},{12,28},{16,0},{20,4},{24,8},{28,12},{1,17},{... | collective-permute-start | bytes 786440 | tf_op jit(solution)/shard_map/ppermute | solution.py:518
  68.7 10.7 %collective-permute-start.7 = (bf16[2,512,128]{2,1,0:T(8,128)(2,1)S(1)}, bf16[2,512,128]{2,1,0:T(8,128)(2,1)S(1)}, u32[]{:S(2)}, u32[]{:S(2)}) collective-permute-start(bf16[2,512,128]{2,1,0:T(8,128)(2,1)S(1)} %get-tuple-element.71), channel_id=1, source_target_pairs={{0,8},{4,12},{8,0},{12,4},{16,24},{20,28},{24,16},{28,20},{1,9},{5... | collective-permute-start | bytes 786440 | tf_op jit(solution)/shard_map/ppermute | solution.py:518
  70.2 10.3 %collective-permute-start.8 = (bf16[2,512,128]{2,1,0:T(8,128)(2,1)S(1)}, bf16[2,512,128]{2,1,0:T(8,128)(2,1)S(1)}, u32[]{:S(2)}, u32[]{:S(2)}) collective-permute-start(bf16[2,512,128]{2,1,0:T(8,128)(2,1)S(1)} %get-tuple-element.73), channel_id=1, source_target_pairs={{0,16},{4,20},{8,24},{12,28},{16,0},{20,4},{24,8},{28,12},{1,17},{... | collective-permute-start | bytes 786440 | tf_op jit(solution)/shard_map/ppermute | solution.py:518
  70.2 1.2 %collective-permute-start.17 = (f32[8,32]{1,0:T(8,128)S(1)}, f32[8,32]{1,0:T(8,128)S(1)}, u32[]{:S(2)}, u32[]{:S(2)}) collective-permute-start(f32[8,32]{1,0:T(8,128)S(1)} %maximum_maximum_fusion.refs_4_), channel_id=1, source_target_pairs={{0,4},{4,0},{8,12},{12,8},{16,20},{20,16},{24,28},{28,24},{1,5},{5... | collective-permute-start | bytes 3080 | tf_op jit(solution)/shard_map/ppermute | solution.py:518
  75.0 20.9 %collective-permute-start.18 = (bf16[1,512,128]{2,1,0:T(8,128)(2,1)S(1)}, bf16[1,512,128]{2,1,0:T(8,128)(2,1)S(1)}, u32[]{:S(2)}, u32[]{:S(2)}) collective-permute-start(bf16[1,512,128]{2,1,0:T(8,128)(2,1)S(1)} %get-tuple-element.92), channel_id=1, source_target_pairs={{0,16},{4,20},{8,24},{12,28},{16,0},{20,4},{24,8},{28,12},{1,17},{... | collective-permute-start | bytes 393224 | tf_op jit(solution)/shard_map/ppermute | solution.py:518
  77.1 18.8 %collective-permute-start.19 = (bf16[1,512,128]{2,1,0:T(8,128)(2,1)S(1)}, bf16[1,512,128]{2,1,0:T(8,128)(2,1)S(1)}, u32[]{:S(2)}, u32[]{:S(2)}) collective-permute-start(bf16[1,512,128]{2,1,0:T(8,128)(2,1)S(1)} %get-tuple-element.94), channel_id=1, source_target_pairs={{0,8},{4,12},{8,0},{12,4},{16,24},{20,28},{24,16},{28,20},{1,9},{5... | collective-permute-start | bytes 393224 | tf_op jit(solution)/shard_map/ppermute | solution.py:518
  80.6 18.9 %collective-permute-start.9 = (bf16[1,512,128]{2,1,0:T(8,128)(2,1)S(1)}, bf16[1,512,128]{2,1,0:T(8,128)(2,1)S(1)}, u32[]{:S(2)}, u32[]{:S(2)}) collective-permute-start(bf16[1,512,128]{2,1,0:T(8,128)(2,1)S(1)} %get-tuple-element.75), channel_id=1, source_target_pairs={{0,16},{4,20},{8,24},{12,28},{16,0},{20,4},{24,8},{28,12},{1,17},{... | collective-permute-start | bytes 393224 | tf_op jit(solution)/shard_map/ppermute | solution.py:518
  82.7 18.8 %collective-permute-start.10 = (bf16[1,512,128]{2,1,0:T(8,128)(2,1)S(1)}, bf16[1,512,128]{2,1,0:T(8,128)(2,1)S(1)}, u32[]{:S(2)}, u32[]{:S(2)}) collective-permute-start(bf16[1,512,128]{2,1,0:T(8,128)(2,1)S(1)} %get-tuple-element.77), channel_id=1, source_target_pairs={{0,8},{4,12},{8,0},{12,4},{16,24},{20,28},{24,16},{28,20},{1,9},{5... | collective-permute-start | bytes 393224 | tf_op jit(solution)/shard_map/ppermute | solution.py:518
  84.2 4.5 %collective-permute-start.22 = (f32[8,32]{1,0:T(8,128)S(1)}, f32[8,32]{1,0:T(8,128)S(1)}, u32[]{:S(2)}, u32[]{:S(2)}) collective-permute-start(f32[8,32]{1,0:T(8,128)S(1)} %get-tuple-element.95.refs_4_), channel_id=1, source_target_pairs={{0,24},{4,28},{8,16},{12,20},{16,8},{20,12},{24,0},{28,4},{1,25},{... | collective-permute-start | bytes 3080 | tf_op jit(solution)/shard_map/ppermute | solution.py:518
  88.7 3.6 %collective-permute-start.21 = (f32[8,32]{1,0:T(8,128)S(1)}, f32[8,32]{1,0:T(8,128)S(1)}, u32[]{:S(2)}, u32[]{:S(2)}) collective-permute-start(f32[8,32]{1,0:T(8,128)S(1)} %get-tuple-element.95.refs_4_), channel_id=1, source_target_pairs={{0,16},{4,20},{8,24},{12,28},{16,0},{20,4},{24,8},{28,12},{1,17},{... | collective-permute-start | bytes 3080 | tf_op jit(solution)/shard_map/ppermute | solution.py:518
  92.3 3.6 %collective-permute-start.20 = (f32[8,32]{1,0:T(8,128)S(1)}, f32[8,32]{1,0:T(8,128)S(1)}, u32[]{:S(2)}, u32[]{:S(2)}) collective-permute-start(f32[8,32]{1,0:T(8,128)S(1)} %get-tuple-element.95.refs_4_), channel_id=1, source_target_pairs={{0,8},{4,12},{8,0},{12,4},{16,24},{20,28},{24,16},{28,20},{1,9},{5... | collective-permute-start | bytes 3080 | tf_op jit(solution)/shard_map/ppermute | solution.py:518
  96.0 11.0 %collective-permute-start.23 = (bf16[128,256]{1,0:T(8,128)(2,1)S(1)}, bf16[128,256]{1,0:T(8,128)(2,1)S(1)}, u32[]{:S(2)}, u32[]{:S(2)}) collective-permute-start(bf16[128,256]{1,0:T(8,128)(2,1)S(1)} %get-tuple-element.97), channel_id=1, source_target_pairs={{0,1},{1,0},{2,3},{3,2},{4,5},{5,4},{6,7},{7,6},{8,9},{9,8},{10,11... | collective-permute-start | bytes 196616 | tf_op jit(solution)/shard_map/ppermute | solution.py:521
  97.1 5.5 %collective-permute-start.28 = (f32[8,32]{1,0:T(8,128)S(1)}, f32[8,32]{1,0:T(8,128)S(1)}, u32[]{:S(2)}, u32[]{:S(2)}) collective-permute-start(f32[8,32]{1,0:T(8,128)S(1)} %get-tuple-element.100.refs_8_), channel_id=1, source_target_pairs={{0,3},{1,2},{2,1},{3,0},{4,7},{5,6},{6,5},{7,4},{8,11},{9,10},{10,... | collective-permute-start | bytes 3080 | tf_op jit(solution)/shard_map/ppermute | solution.py:521
  97.3 6.8 %collective-permute-start.27 = (f32[8,32]{1,0:T(8,128)S(1)}, f32[8,32]{1,0:T(8,128)S(1)}, u32[]{:S(2)}, u32[]{:S(2)}) collective-permute-start(f32[8,32]{1,0:T(8,128)S(1)} %get-tuple-element.100.refs_8_), channel_id=1, source_target_pairs={{0,2},{1,3},{2,0},{3,1},{4,6},{5,7},{6,4},{7,5},{8,10},{9,11},{10,... | collective-permute-start | bytes 3080 | tf_op jit(solution)/shard_map/ppermute | solution.py:521
  99.5 5.6 %collective-permute-start.26 = (f32[8,32]{1,0:T(8,128)S(1)}, f32[8,32]{1,0:T(8,128)S(1)}, u32[]{:S(2)}, u32[]{:S(2)}) collective-permute-start(f32[8,32]{1,0:T(8,128)S(1)} %get-tuple-element.100.refs_8_), channel_id=1, source_target_pairs={{0,1},{1,0},{2,3},{3,2},{4,5},{5,4},{6,7},{7,6},{8,9},{9,8},{10,11... | collective-permute-start | bytes 3080 | tf_op jit(solution)/shard_map/ppermute | solution.py:521
  101.5 7.0 %collective-permute-start.24 = (bf16[128,256]{1,0:T(8,128)(2,1)S(1)}, bf16[128,256]{1,0:T(8,128)(2,1)S(1)}, u32[]{:S(2)}, u32[]{:S(2)}) collective-permute-start(bf16[128,256]{1,0:T(8,128)(2,1)S(1)} %get-tuple-element.98), channel_id=1, source_target_pairs={{0,2},{1,3},{2,0},{3,1},{4,6},{5,7},{6,4},{7,5},{8,10},{9,11},{10,... | collective-permute-start | bytes 196616 | tf_op jit(solution)/shard_map/ppermute | solution.py:521
  102.6 6.2 %collective-permute-start.25 = (bf16[128,256]{1,0:T(8,128)(2,1)S(1)}, bf16[128,256]{1,0:T(8,128)(2,1)S(1)}, u32[]{:S(2)}, u32[]{:S(2)}) collective-permute-start(bf16[128,256]{1,0:T(8,128)(2,1)S(1)} %get-tuple-element.99), channel_id=1, source_target_pairs={{0,3},{1,2},{2,1},{3,0},{4,7},{5,6},{6,5},{7,4},{8,11},{9,10},{10,... | collective-permute-start | bytes 196616 | tf_op jit(solution)/shard_map/ppermute | solution.py:521
  104.1 5.0 %collective-permute-start.11 = (bf16[128,256]{1,0:T(8,128)(2,1)S(1)}, bf16[128,256]{1,0:T(8,128)(2,1)S(1)}, u32[]{:S(2)}, u32[]{:S(2)}) collective-permute-start(bf16[128,256]{1,0:T(8,128)(2,1)S(1)} %get-tuple-element.79), channel_id=1, source_target_pairs={{0,1},{1,0},{2,3},{3,2},{4,5},{5,4},{6,7},{7,6},{8,9},{9,8},{10,11... | collective-permute-start | bytes 196616 | tf_op jit(solution)/shard_map/ppermute | solution.py:521
  105.1 5.9 %collective-permute-start.12 = (bf16[128,256]{1,0:T(8,128)(2,1)S(1)}, bf16[128,256]{1,0:T(8,128)(2,1)S(1)}, u32[]{:S(2)}, u32[]{:S(2)}) collective-permute-start(bf16[128,256]{1,0:T(8,128)(2,1)S(1)} %get-tuple-element.80), channel_id=1, source_target_pairs={{0,2},{1,3},{2,0},{3,1},{4,6},{5,7},{6,4},{7,5},{8,10},{9,11},{10,... | collective-permute-start | bytes 196616 | tf_op jit(solution)/shard_map/ppermute | solution.py:521
  107.0 6.1 %collective-permute-start.13 = (bf16[128,256]{1,0:T(8,128)(2,1)S(1)}, bf16[128,256]{1,0:T(8,128)(2,1)S(1)}, u32[]{:S(2)}, u32[]{:S(2)}) collective-permute-start(bf16[128,256]{1,0:T(8,128)(2,1)S(1)} %get-tuple-element.81), channel_id=1, source_target_pairs={{0,3},{1,2},{2,1},{3,0},{4,7},{5,6},{6,5},{7,4},{8,11},{9,10},{10,... | collective-permute-start | bytes 196616 | tf_op jit(solution)/shard_map/ppermute | solution.py:521
  (6 other events, 45.9 us)

commit v4 on v0

v4 whole, which is shorter than its diff:
```python
import functools

import jax
import jax.numpy as jnp
from jax import lax
from jax.experimental import pallas as pl
from jax.experimental.pallas import tpu as pltpu
from jax.sharding import PartitionSpec as P

QROWS = 32
LOG2E = 1.4426950408889634
FAR = 1e30
MIB = 1024 * 1024
CHUNK = 256
TOP_ROWS, TOP_LANES = 16, 128
BF16, F32 = jnp.bfloat16, jnp.float32
BF16_MAX = float(jnp.finfo(jnp.bfloat16).max)
NT = (((1,), (1,)), ((), ()))
TN = (((0,), (0,)), ((), ()))


def xor_perm(size, mask):
    return [(i, i ^ mask) for i in range(size)]


def whole(x):
    return pl.BlockSpec(x.shape, lambda *_: (0,) * len(x.shape))


def shape(dims, dtype=BF16):
    return jax.ShapeDtypeStruct(dims, dtype)


def whole_call(kernel, name, scalars, operands, out_shape, mib, cost, scratch=()):
    return pl.pallas_call(
        kernel,
        grid_spec=pltpu.PrefetchScalarGridSpec(
            num_scalar_prefetch=len(scalars),
            grid=(1,),
            in_specs=[whole(x) for x in operands],
            out_specs=[whole(x) for x in out_shape],
            scratch_shapes=list(scratch),
        ),
        out_shape=out_shape,
        compiler_params=pltpu.CompilerParams(vmem_limit_bytes=mib * MIB),
        cost_estimate=pl.CostEstimate(flops=cost[0], bytes_accessed=cost[1], transcendentals=0),
        name=name,
    )(*scalars, *operands)


def join_kernel(k_ref, v_ref, out_ref):
    hd = k_ref.shape[1]
    out_ref[:, :hd] = k_ref[...]
    out_ref[:, hd:] = v_ref[...]


def join(keys, values):
    rows, hd = keys.shape
    out = [shape((rows, 2 * hd))]
    return whole_call(join_kernel, "join_keys_values", [], [keys, values], out, 4, (0, 8 * rows * hd))[0]


def prepare_kernel(pieces, a_hbm, e_hbm, a_out, e_out, a_buf, a_sems, e_sems):
    model = a_buf.shape[1]
    tile = model // pieces
    parts = [pl.ds(i * tile, tile) for i in range(pieces)]
    a_copies = [pltpu.make_async_copy(a_hbm.at[:, p], a_buf.at[:, p], a_sems.at[i]) for i, p in enumerate(parts)]
    e_copies = [pltpu.make_async_copy(e_hbm.at[p, :], e_out.at[p, :], e_sems.at[i]) for i, p in enumerate(parts)]
    for copy in a_copies + e_copies:
        copy.start()
    for copy, part in zip(a_copies, parts):
        copy.wait()
        a_out[part, :] = a_buf[:, part].T
    for copy in e_copies:
        copy.wait()


def prepare(activations, errors):
    rows, model = activations.shape
    pieces = 8
    hbm = pl.BlockSpec(memory_space=pltpu.HBM)
    outs = [shape((model, rows)), shape(errors.shape, F32)]
    return pl.pallas_call(
        functools.partial(prepare_kernel, pieces),
        in_specs=[hbm, hbm],
        out_specs=[pl.BlockSpec(memory_space=pltpu.VMEM)] * 2,
        out_shape=outs,
        scratch_shapes=[
            pltpu.VMEM((rows, model), BF16),
            pltpu.SemaphoreType.DMA((pieces,)),
            pltpu.SemaphoreType.DMA((pieces,)),
        ],
        compiler_params=pltpu.CompilerParams(vmem_limit_bytes=28 * MIB),
        cost_estimate=pl.CostEstimate(
            flops=0, bytes_accessed=2 * rows * model + 4 * errors.size, transcendentals=0
        ),
        name="prepare",
    )(activations, errors)


def key_value(refs):
    if len(refs) == 2:
        return refs[0][...], refs[1][...]
    hd = refs[0].shape[1] // 2
    return refs[0][:, :hd], refs[0][:, hd:]


def head_pair(ref, i, hd):
    at = i * (2 * hd)
    first = ref[:, pl.ds(pl.multiple_of(at, hd), hd)]
    second = ref[:, pl.ds(pl.multiple_of(at + hd, hd), hd)]
    return jnp.concatenate([first, second], axis=0)


def score_chunk(k, v, q, do, own, first_lane):
    s = lax.dot_general(k, q, NT, preferred_element_type=F32)
    dp = lax.dot_general(v, do, NT, preferred_element_type=F32)
    if own:
        rows = k.shape[0]
        key_at = lax.broadcasted_iota(jnp.int32, s.shape, 0)
        query_at = lax.broadcasted_iota(jnp.int32, s.shape, 1) + first_lane
        query_at = jnp.where(query_at >= rows, query_at - rows, query_at)
        s = jnp.where(key_at <= query_at, s, -FAR)
    return s, dp


def counted(b, me_ref, span_ref):
    me = me_ref[0]
    return span_ref[me ^ b] < span_ref[me]


def stats_kernel(b, me_ref, span_ref, q_ref, do_ref, *refs):
    if b == 0:
        kv, out = refs[:2], refs[2]
    else:
        kv, before, out = refs[:1], refs[1], refs[2]

    def run():
        k, v = key_value(kv)
        rows, hd = k.shape
        pair = 2 * rows
        factor = LOG2E / hd**0.5

        def heads(i, carry):
            q, do = head_pair(q_ref, i, hd), head_pair(do_ref, i, hd)
            for t in range(pair // CHUNK):
                part = slice(t * CHUNK, (t + 1) * CHUNK)
                lanes = pl.ds(pl.multiple_of(i * pair + t * CHUNK, CHUNK), CHUNK)
                s, dp = score_chunk(k, v, q[part], do[part], b == 0, t * CHUNK)
                top = jnp.max(s, axis=0, keepdims=True) * factor
                e = jnp.exp2(s * factor - top)
                total = jnp.sum(e, axis=0, keepdims=True)
                weighted = jnp.sum(e * dp, axis=0, keepdims=True)
                if b > 0:
                    old = before[0:1, lanes]
                    both = jnp.maximum(old, top)
                    old_part, new_part = jnp.exp2(old - both), jnp.exp2(top - both)
                    total = before[1:2, lanes] * old_part + total * new_part
                    weighted = before[2:3, lanes] * old_part + weighted * new_part
                    top = both
                out[0:1, lanes] = top
                out[1:2, lanes] = total
                out[2:3, lanes] = weighted
            return carry

        lax.fori_loop(0, q_ref.shape[1] // (2 * hd), heads, 0)

    if b == 0:
        run()
    else:
        keep = counted(b, me_ref, span_ref)
        pl.when(keep)(run)

        @pl.when(jnp.logical_not(keep))
        def _():
            out[...] = before[...]


def block_gradients(own, stats, q_ref, do_ref, kv, p_buf, ds_ref, ds_step, dk, dv, after):
    k, v = key_value(kv)
    rows, hd = k.shape
    pair = 2 * rows
    factor = LOG2E / hd**0.5
    dk[...] = jnp.zeros_like(dk)
    dv[...] = jnp.zeros_like(dv)

    def heads(i, carry):
        q, do = head_pair(q_ref, i, hd), head_pair(do_ref, i, hd)
        for t in range(pair // CHUNK):
            part = slice(t * CHUNK, (t + 1) * CHUNK)
            lanes = pl.ds(pl.multiple_of(i * pair + t * CHUNK, CHUNK), CHUNK)
            s, dp = score_chunk(k, v, q[part], do[part], own, t * CHUNK)
            total = stats[1:2, lanes]
            level = stats[0:1, lanes] + jnp.log(total) * LOG2E
            p = jnp.exp2(s * factor - level)
            p_buf[:, part] = p.astype(BF16)
            ds = (p * (dp - stats[2:3, lanes] / total)).astype(BF16)
            ds_ref[:, pl.ds(pl.multiple_of(i * ds_step + t * CHUNK, CHUNK), CHUNK)] = ds
        ds = ds_ref[:, pl.ds(pl.multiple_of(i * ds_step, CHUNK), pair)]
        dk[...] += jnp.dot(ds, q, preferred_element_type=F32)
        dv[...] += jnp.dot(p_buf[...], do, preferred_element_type=F32)
        after(i, ds)
        return carry

    lax.fori_loop(0, q_ref.shape[1] // (2 * hd), heads, 0)
    inverse = 1.0 / hd**0.5
    return dk[...] * inverse, dv[...]


def other_kernel(b, me_ref, span_ref, stats, q_ref, do_ref, kv, out_ref, ds_out, p_buf, dk, dv):
    keep = counted(b, me_ref, span_ref)
    rows, hd = dk.shape

    @pl.when(keep)
    def _():
        dk_sum, dv_sum = block_gradients(
            False, stats, q_ref, do_ref, (kv,), p_buf, ds_out, 2 * rows, dk, dv, lambda i, ds: None
        )
        out_ref[:, :hd] = dk_sum.astype(BF16)
        out_ref[:, hd:] = dv_sum.astype(BF16)

    @pl.when(jnp.logical_not(keep))
    def _():
        out_ref[...] = jnp.zeros_like(out_ref)
        ds_out[...] = jnp.zeros_like(ds_out)


def own_kernel(n, me_ref, span_ref, stats, q_ref, do_ref, k_ref, v_ref, *refs):
    kv_refs, ds_refs = refs[: n - 1], refs[n - 1 : 2 * n - 2]
    out_ref, dq_ref, ds_buf, p_buf, dk, dv = refs[2 * n - 2 :]
    rows, hd = k_ref.shape
    pair = 2 * rows

    def query_part(i, ds):
        lanes = pl.ds(pl.multiple_of(i * pair, CHUNK), pair)
        dq = lax.dot_general(ds, k_ref[...], TN, preferred_element_type=F32)
        for kv, other in zip(kv_refs, ds_refs):
            dq = dq + lax.dot_general(other[:, lanes], kv[:, :hd], TN, preferred_element_type=F32)
        dq = (dq / hd**0.5).astype(BF16)
        for h in range(2):
            at = pl.multiple_of(i * (2 * hd) + h * hd, hd)
            dq_ref[:, pl.ds(at, hd)] = dq[h * rows : (h + 1) * rows]

    dk_sum, dv_sum = block_gradients(
        True, stats, q_ref, do_ref, (k_ref, v_ref), p_buf, ds_buf, 0, dk, dv, query_part
    )
    out_ref[:, :hd] = dk_sum
    out_ref[:, hd:] = dv_sum


def attention(me, spans, queries, out_grad, keys, values, received, swap):
    n = len(received) + 1
    rows, hd = keys.shape
    columns = queries.shape[1]
    tall = columns // hd * rows
    product = 2 * rows * tall * hd
    scalars = [me, spans]

    def stats_call(b, operands):
        outs = [shape((8, tall), F32)]
        cost = (4 * product, 8 * rows * columns)
        return whole_call(functools.partial(stats_kernel, b), "block_stats", scalars, operands, outs, 20, cost)[0]

    stats = stats_call(0, [queries, out_grad, keys, values])
    for b, kv in enumerate(received, 1):
        stats = stats_call(b, [queries, out_grad, kv, stats])
    p_buf = pltpu.VMEM((rows, 2 * rows), BF16)
    sums = [pltpu.VMEM((rows, hd), F32)] * 2
    parts, score_grads = [None] * (n - 1), [None] * (n - 1)
    for b in range(n - 1, 0, -1):
        part, score_grads[b - 1] = whole_call(
            functools.partial(other_kernel, b),
            "block_gradients",
            scalars,
            [stats, queries, out_grad, received[b - 1]],
            [shape((rows, 2 * hd)), shape((rows, tall))],
            24,
            (8 * product, 16 * rows * columns),
            [p_buf, *sums],
        )
        parts[b - 1] = swap(part, b)
    own, query_grad = whole_call(
        functools.partial(own_kernel, n),
        "own_gradients",
        scalars,
        [stats, queries, out_grad, keys, values, *received, *score_grads],
        [shape((rows, 2 * hd), F32), shape((rows, columns))],
        32,
        (16 * product, 16 * rows * columns),
        [p_buf, p_buf, *sums],
    )
    return query_grad, own, parts


def pack_top(top):
    high = jnp.minimum(top, BF16_MAX).astype(BF16)
    rest = top - high.astype(F32)
    middle = rest.astype(BF16)
    low = (rest - middle.astype(F32)).astype(BF16)
    return jnp.concatenate([high, middle, low], axis=0)


def unpack_top(ref, at):
    parts = [ref[at + i * TOP_ROWS : at + (i + 1) * TOP_ROWS, :TOP_LANES].astype(F32) for i in range(3)]
    return parts[0] + (parts[1] + parts[2])


def tile_of(step, me_dp, bits, flip):
    mask = flip
    for j in range(1, bits):
        if not (step >> (bits - 1 - j)) & 1:
            mask |= 1 << j
    return me_dp ^ mask


def reversed_step(step, bits):
    return sum(((step >> (bits - 1 - j)) & 1) << (j - 1) for j in range(1, bits))


def corrected_tile(chosen, dest, grads, a_ref, e_ref, top_ref):
    _, n_ctx, sets, rows_set, rows = a_ref.shape
    tall = n_ctx * rows_set
    a = a_ref[dest, :, chosen].reshape(tall, rows)
    e = e_ref[dest, :, chosen].reshape(tall, e_ref.shape[4])
    c = jnp.dot(a, grads, preferred_element_type=F32) + e

    mags = jnp.max(jnp.abs(c).reshape(tall // QROWS, QROWS, c.shape[1]), axis=1)
    mags = jnp.max(mags, axis=1, keepdims=True)
    per_set = rows_set // QROWS
    block = lax.broadcasted_iota(jnp.int32, (tall // QROWS, TOP_LANES), 0)
    lane = lax.broadcasted_iota(jnp.int32, (tall // QROWS, TOP_LANES), 1)
    shift = per_set.bit_length() - 1
    place = ((block >> shift) * (sets * per_set)) + chosen * per_set + (block & (per_set - 1))
    top = jnp.max(jnp.where(lane == place, mags, 0.0), axis=0, keepdims=True)
    top_ref[pl.ds(dest, 1), :] = jnp.maximum(top_ref[pl.ds(dest, 1), :], top)
    return c


def first_send_kernel(bits, shrink, n_parts, me_ref, own_ref, *refs):
    part_refs = refs[:n_parts]
    a_ref, e_ref, out_ref, top_ref, kg_ref, vg_ref, grads_ref = refs[n_parts:]
    total = own_ref[...]
    for part in part_refs:
        total = total + part[...].astype(F32)
    total = total.astype(BF16)
    hd = total.shape[1] // 2
    kg_ref[...] = total[:, :hd]
    vg_ref[...] = total[:, hd:]
    grads_ref[...] = total
    top_ref[...] = jnp.zeros_like(top_ref)
    send_rows(bits, shrink, 0, me_ref, total, a_ref, e_ref, out_ref, top_ref)


def next_send_kernel(bits, shrink, chosen, me_ref, grads_ref, before_ref, a_ref, e_ref, out_ref, top_ref):
    top_ref[...] = before_ref[...]
    send_rows(bits, shrink, chosen, me_ref, grads_ref[...], a_ref, e_ref, out_ref, top_ref)


def send_rows(bits, shrink, chosen, me_ref, total, a_ref, e_ref, out_ref, top_ref):
    for step in range(out_ref.shape[0]):
        dest = tile_of(step, me_ref[0], bits, 1)
        c = corrected_tile(chosen, dest, total, a_ref, e_ref, top_ref)
        out_ref[step] = (c * shrink).astype(BF16)


def keep_kernel(bits, shrink, chosen, me_ref, grads, got_ref, before_ref, a_ref, e_ref, *outs):
    low_away, low_stay, high_away, high_stay, top_ref = outs
    steps, tall, width = got_ref.shape
    half = steps // 2
    hd = width // 2
    total = grads[...]
    top_ref[...] = before_ref[...]
    for step in range(steps):
        dest = tile_of(step, me_ref[0], bits, 0)
        c = corrected_tile(chosen, dest, total, a_ref, e_ref, top_ref)
        c = (c * shrink + got_ref[step].astype(F32)).astype(BF16)
        back = reversed_step(step, bits)
        for at, part, away, stay in ((step, c[:, :hd], low_away, low_stay), (back, c[:, hd:], high_away, high_stay)):
            if at < half:
                away[at * tall : (at + 1) * tall, :] = part
            else:
                stay[(at - half) * tall : (at - half + 1) * tall, :] = part
    low_away[half * tall :, :] = pack_top(top_ref[...])


def largest(top_ref, low_got, at, others):
    top = jnp.maximum(top_ref[...], unpack_top(low_got, at))
    for other in others:
        top = jnp.maximum(top, other[...])
    return top


def add_kernel(n_others, low, low_got, high, high_got, top_ref, *refs):
    others = refs[:n_others]
    low_away, low_stay, high_away, high_stay, top_out = refs[n_others:]
    size = low.shape[0]
    half = size // 2
    for mine, got, away, stay in ((low, low_got, low_away, low_stay), (high, high_got, high_away, high_stay)):
        away[:half, :] = (mine[:half, :].astype(F32) + got[:half, :].astype(F32)).astype(BF16)
        stay[...] = (mine[half:, :].astype(F32) + got[half:size, :].astype(F32)).astype(BF16)
    top = largest(top_ref, low_got, size, others)
    low_away[half:, :] = pack_top(top)
    top_out[...] = top


def last_kernel(n_ctx, n_others, me_ref, low, low_got, high, high_got, top_ref, *refs):
    others = refs[:n_others]
    *outs, top_out = refs[n_others:]
    size, hd = low.shape
    rows_set = size // n_ctx
    top = largest(top_ref, low_got, size, others)
    packed = pack_top(top)
    for b in range(n_ctx):
        part = pl.ds(pl.multiple_of((me_ref[0] ^ b) * rows_set, rows_set), rows_set)
        for at, mine, got in ((0, low, low_got), (hd, high, high_got)):
            total = mine[part, :].astype(F32) + got[part, :].astype(F32)
            outs[b][:rows_set, at : at + hd] = total.astype(outs[b].dtype)
        if b > 0:
            outs[b][rows_set:, :TOP_LANES] = packed
            outs[b][rows_set:, TOP_LANES:] = jnp.zeros_like(packed)
    top_out[...] = top


def final_kernel(sets, n_ctx, gain, me_dp_ref, me_ctx_ref, *refs):
    groups = [refs[chosen * n_ctx : (chosen + 1) * n_ctx] for chosen in range(sets)]
    top_ref, out_ref, scale_ref, all_tops = refs[sets * n_ctx :]
    n_dp, lanes = scale_ref.shape
    rows_set = groups[0][0].shape[0]
    scale = top_ref[...]
    for other in groups[-1][1:]:
        scale = jnp.maximum(scale, unpack_top(other, rows_set))
    scale = scale + 1e-06
    all_tops[...] = scale
    scale_ref[...] = scale[:n_dp, :lanes]
    factors = gain / all_tops[pl.ds(me_dp_ref[0], 1), :]
    lane = lax.broadcasted_iota(jnp.int32, factors.shape, 1)
    per_set = rows_set // QROWS
    first = me_ctx_ref[0] * (sets * per_set)
    for chosen, group in enumerate(groups):
        for r in range(per_set):
            part = slice(r * QROWS, (r + 1) * QROWS)
            total = group[0][part, :]
            for other in group[1:]:
                total = total + other[part, :].astype(F32)
            mine = jnp.where(lane == first + (chosen * per_set + r), factors, 0.0)
            at = chosen * rows_set + r * QROWS
            out_ref[at : at + QROWS, :] = total * jnp.sum(mine, axis=1, keepdims=True)


def local(n_dp, n_ctx, sets, span_order, queries, keys, values, out_grad, activations, error_feedback):
    rows, hd = keys.shape
    width = 2 * hd
    model = activations.shape[1]
    rows_set = model // (n_dp * n_ctx * sets)
    tall = n_ctx * rows_set
    me_dp = lax.axis_index("dp").astype(jnp.int32)[None]
    me_ctx = lax.axis_index("context").astype(jnp.int32)[None]
    bits = n_dp.bit_length() - 1
    packed_rows = 3 * TOP_ROWS

    def swap_dp(x, mask):
        return lax.ppermute(x, "dp", xor_perm(n_dp, mask))

    def swap_ctx(x, mask):
        return lax.ppermute(x, "context", xor_perm(n_ctx, mask))

    pairs = join(keys, values)
    received = [swap_ctx(pairs, b) for b in range(1, n_ctx)]
    acts, errors = prepare(activations, error_feedback[0, 0])
    query_grad, own, parts = attention(me_ctx, span_order[0], queries, out_grad, keys, values, received, swap_ctx)

    shrink = 1.0 / (n_dp * n_ctx)
    acts = acts.reshape(n_dp, n_ctx, sets, rows_set, rows)
    errors = errors.reshape(n_dp, n_ctx, sets, rows_set, width)
    tops = shape((TOP_ROWS, TOP_LANES), F32)
    steps = n_dp // 2
    cost = (2 * steps * tall * rows * width, steps * tall * (2 * rows + 6 * width))
    message = shape((steps, tall, width))
    got = []
    for chosen in range(sets):
        if chosen == 0:
            out, top, key_grad, value_grad, grads = whole_call(
                functools.partial(first_send_kernel, bits, shrink, n_ctx - 1),
                "send_tiles",
                [me_dp],
                [own, *parts, acts, errors],
                [message, tops, shape((rows, hd)), shape((rows, hd)), shape((rows, width))],
                28,
                cost,
            )
        else:
            out, top = whole_call(
                functools.partial(next_send_kernel, bits, shrink, chosen),
                "send_tiles",
                [me_dp],
                [grads, top, acts, errors],
                [message, tops],
                28,
                cost,
            )
        got.append(swap_dp(out, 1))

    halves = []
    for chosen in range(sets):
        half = steps // 2 * tall
        *arrays, top = whole_call(
            functools.partial(keep_kernel, bits, shrink, chosen),
            "keep_tiles",
            [me_dp],
            [grads, got[chosen], top, acts, errors],
            [shape((half + packed_rows, hd))] + [shape((half, hd))] * 3 + [tops],
            28,
            cost,
        )
        halves.append((arrays, top))

    groups = []
    for chosen in range(sets):
        (low_away, low, high_away, high), top = halves[chosen]
        for stage in range(1, bits):
            low_got = swap_dp(low_away, 1 << stage)
            high_got = swap_dp(high_away, 1 << (bits - stage))
            others = [swap_dp(top, mask) for mask in (1, 3)] if chosen == sets - 1 and stage == 1 else []
            operands = [low, low_got, high, high_got, top, *others]
            size = low.shape[0]
            cost = (4 * size * hd, 12 * size * hd)
            if stage < bits - 1:
                low_away, low, high_away, high, top = whole_call(
                    functools.partial(add_kernel, len(others)),
                    "add_stage",
                    [],
                    operands,
                    [shape((size // 2 + packed_rows, hd))] + [shape((size // 2, hd))] * 3 + [tops],
                    16,
                    cost,
                )
            else:
                mine, *away, top = whole_call(
                    functools.partial(last_kernel, n_ctx, len(others)),
                    "last_stage",
                    [me_ctx],
                    operands,
                    [shape((rows_set, width), F32)] + [shape((rows_set + packed_rows, width))] * (n_ctx - 1) + [tops],
                    16,
                    cost,
                )
        groups.append([mine] + [swap_ctx(part, b + 1) for b, part in enumerate(away)])
    payload, scale = whole_call(
        functools.partial(final_kernel, sets, n_ctx, 7.0 / shrink),
        "final_stage",
        [me_dp, me_ctx],
        [x for group in groups for x in group] + [top],
        [shape((sets * rows_set, width), F32), shape((n_dp, sets * tall // QROWS), F32)],
        8,
        (4 * sets * tall * width, 16 * sets * rows_set * width),
        [pltpu.VMEM((TOP_ROWS, TOP_LANES), F32)],
    )
    return query_grad, key_grad, value_grad, payload, scale.reshape(-1)


def solution(mesh):
    tokens = P(("dp", "context"), None)
    return jax.shard_map(
        functools.partial(local, mesh.shape["dp"], mesh.shape["context"], 2),
        mesh=mesh,
        in_specs=(P("dp", None), tokens, tokens, tokens, tokens, tokens, P("dp", "context", None, None)),
        out_specs=(tokens, tokens, tokens, tokens, P()),
        check_vma=False,
    )
```

time: 430 us -> 104 us (0.24)
  waiting for transfers between devices: 224 us -> 25.9 us
  blocking collectives: 70.9 us -> 0 us
  matrix products: 68.7 us -> 0 us
  Pallas kernels: 0 us -> 43.3 us
  other arithmetic: 27.4 us -> 0 us
  starting transfers between devices: 0.12 us -> 27.3 us
  between operations: 13.9 us -> 0.83 us
  local copies, waits for them, and re-layouts: 17.9 us -> 5.22 us
  loops' own time: 5.67 us -> 0 us
    reduce_scatter x3 -> x0, waiting for transfers between devices: 223 us -> none  [the longest x1 185 us: local(): lax.psum_scatter(terms, ('dp', 'context'), scatter_dimension=0, tiled=True)]
    dot_general x41 -> x0, matrix products: 68.7 us -> none  [the longest x8 15.3 us: head_backward(): jnp.dot(probs_low.T, grad_head, preferred_element_type=jnp.float32)]
    pallas_call x0 -> x19, Pallas kernels: none -> 43.3 us  [the longest x18 39 us: whole_call(): pl.pallas_call(kernel, grid_spec=pltpu.PrefetchScalarGridSpec(num_scalar_...]
    pmax x1 -> x0, blocking collectives: 38.7 us -> none  [local(): block_max = lax.pmax(local_top, ('dp', 'context'))]
    all_gather x2 -> x0, blocking collectives: 32.2 us -> none  [the longest x1 16.4 us: local(): lax.all_gather(keys, 'context', axis=0, tiled=True)]
    ppermute x0 -> x24, starting transfers between devices: none -> 27.3 us  [the longest x12 16.7 us: swap_ctx(): return lax.ppermute(x, 'context', xor_perm(n_ctx, mask))]
    ppermute x0 -> x24, waiting for transfers between devices: none -> 25.9 us  [the longest x12 15.8 us: swap_ctx(): return lax.ppermute(x, 'context', xor_perm(n_ctx, mask))]
    convert_element_type x12 -> x0, other arithmetic: 15.3 us -> none  [the longest x8 5.1 us: head_backward(): score_grad = (probs * (prob_grad - row_delta)).astype(jnp.bfloat16)]
  transfers between devices with their start and end apart: 3 -> 24, of which waited for: 3 -> 8; matrix products, arithmetic and copies ran while one was open for 3% -> 0% of each run, Pallas kernels for 0% -> 33%
where the time goes in v4:
time: 104 us; the launch traced here: 103 us
  Pallas kernels  43.3 us (42%)
  starting transfers between devices  27.3 us (26%)
  waiting for transfers between devices  25.9 us (25%)
  local copies, waits for them, and re-layouts  5.22 us (5%)
    pallas_call x18, Pallas kernels, whole_call(): pl.pallas_call(kernel, grid_spec=pltpu.PrefetchScalarGridSpec(num_scalar_...  39 us
    ppermute x12, starting transfers between devices, swap_ctx(): return lax.ppermute(x, 'context', xor_perm(n_ctx, mask))  16.7 us
    ppermute x12, waiting for transfers between devices, swap_ctx(): return lax.ppermute(x, 'context', xor_perm(n_ctx, mask))  15.8 us
    ppermute x12, starting transfers between devices, swap_dp(): return lax.ppermute(x, 'dp', xor_perm(n_dp, mask))  10.6 us
    ppermute x12, waiting for transfers between devices, swap_dp(): return lax.ppermute(x, 'dp', xor_perm(n_dp, mask))  10 us
    unnamed x16, local copies, waits for them, and re-layouts  4.59 us
    pallas_call x1, Pallas kernels, prepare(): pl.pallas_call(functools.partial(prepare_kernel, pieces), in_specs=[hbm,...  4.27 us
  transfers between devices with their start and end apart: 24, of which 8 were waited for; matrix products, arithmetic and copies ran while one was open for 0% of the time, Pallas kernels for 33%

profile of v4, /device:TPU:0, one launch (start us, length us, event | category | flops | bytes accessed | tf_op | source)
XLA Modules:
  0.0 102.5 jit_solution(10071634489783546453)
XLA Ops:
  2.5 3.1 %collective-permute-start.2 = (bf16[384,256]{1,0:T(8,128)(2,1)S(1)}, bf16[384,256]{1,0:T(8,128)(2,1)S(1)}, u32[]{:S(2)}, u32[]{:S(2)}) collective-permute-start(bf16[384,256]{1,0:T(8,128)(2,1)S(1)} %join_keys_values.1), channel_id=1, source_target_pairs={{0,1},{1,0},{2,3},{3,2},{4,5},{5,4},{6,7},{7,6},{8,9},{9,8},{10,11... | collective-permute-start | bytes 589832 | tf_op jit(solution)/shard_map/ppermute | solution.py:465
  5.5 2.5 %collective-permute-start = (bf16[384,256]{1,0:T(8,128)(2,1)S(1)}, bf16[384,256]{1,0:T(8,128)(2,1)S(1)}, u32[]{:S(2)}, u32[]{:S(2)}) collective-permute-start(bf16[384,256]{1,0:T(8,128)(2,1)S(1)} %join_keys_values.1), channel_id=1, source_target_pairs={{0,3},{1,2},{2,1},{3,0},{4,7},{5,6},{6,5},{7,4},{8,11},{9,10},{10,... | collective-permute-start | bytes 589832 | tf_op jit(solution)/shard_map/ppermute | solution.py:465
  8.1 2.8 %copy-done = bf16[384,8192]{1,0:T(8,128)(2,1)S(1)} copy-done((bf16[384,8192]{1,0:T(8,128)(2,1)S(1)}, bf16[384,8192]{1,0:T(8,128)(2,1)}, u32[]{:S(2)}) %copy-start) | copy-done | bytes 6291480
  10.9 4.3 %prepare.1 = (bf16[8192,384]{1,0:T(8,128)(2,1)S(1)}, f32[8192,256]{1,0:T(8,128)S(1)}) custom-call(bf16[384,8192]{1,0:T(8,128)(2,1)S(1)} %copy-done, f32[8192,256]{1,0:T(8,128)} %bitcast.22), custom_call_target="tpu_custom_call" | custom-call | bytes 14680064 | tf_op jit(solution)/shard_map/prepare/pallas_call | solution.py:83
  15.3 2.9 %block_stats.4.refs_1_ = f32[8,3072]{1,0:T(8,128)S(1)} custom-call(s32[1]{0:T(128)} %bitcast.me_ref.me_ctx_ref, s32[4]{0:T(128)S(1)} %bitcast.14, bf16[384,1024]{1,0:T(8,128)(2,1)S(1)} %copy-done.5, bf16[384,1024]{1,0:T(8,128)(2,1)S(1)} %copy-done.6, bf16[384,128]{1,0:T(8,128)(2,1)S(1)} %copy-done.2, bf16[384,128]{1,0:T(8,128)(2,1)S(1)} %copy-done.4), custom_call_target="tpu_custom_call" | custom-call | flops 1207959552 | bytes 3145728 | tf_op jit(solution)/shard_map/block_stats/pallas_call | solution.py:35
  18.2 3.2 %block_stats.5.refs_1_ = f32[8,3072]{1,0:T(8,128)S(1)} custom-call(s32[1]{0:T(128)} %bitcast.me_ref.me_ctx_ref, s32[4]{0:T(128)S(1)} %bitcast.15, bf16[384,1024]{1,0:T(8,128)(2,1)S(1)} %copy-done.5, bf16[384,1024]{1,0:T(8,128)(2,1)S(1)} %copy-done.6, bf16[384,256]{1,0:T(8,128)(2,1)S(1)} %collective-permute-done.2.refs_0_.kv, f32[8,3072]{1,0:T(8,128)S(1)} %block_stats.4.refs_1_), custom_call_target="tpu_custom_call" | custom-call | flops 1207959552 | bytes 3145728 | tf_op jit(solution)/shard_map/block_stats/pallas_call | solution.py:35
  21.5 3.9 %collective-permute-done.1.refs_0_.kv.refs_1_ = bf16[384,256]{1,0:T(8,128)(2,1)S(1)} collective-permute-done((bf16[384,256]{1,0:T(8,128)(2,1)S(1)}, bf16[384,256]{1,0:T(8,128)(2,1)S(1)}, u32[]{:S(2)}, u32[]{:S(2)}) %collective-permute-start.1) | collective-permute-done | bytes 196640 | tf_op jit(solution)/shard_map/ppermute | solution.py:465
  25.4 3.2 %block_stats.6.refs_1_ = f32[8,3072]{1,0:T(8,128)S(1)} custom-call(s32[1]{0:T(128)} %bitcast.me_ref.me_ctx_ref, s32[4]{0:T(128)S(1)} %bitcast.16, bf16[384,1024]{1,0:T(8,128)(2,1)S(1)} %copy-done.5, bf16[384,1024]{1,0:T(8,128)(2,1)S(1)} %copy-done.6, bf16[384,256]{1,0:T(8,128)(2,1)S(1)} %collective-permute-done.1.refs_0_.kv.refs_1_, ...), custom_call_target="tpu_custom_call" | custom-call | flops 1207959552 | bytes 3145728 | tf_op jit(solution)/shard_map/block_stats/pallas_call | solution.py:35
  28.6 3.2 %block_stats.7.stats = f32[8,3072]{1,0:T(8,128)S(1)} custom-call(s32[1]{0:T(128)} %bitcast.me_ref.me_ctx_ref, s32[4]{0:T(128)S(1)} %bitcast.17, bf16[384,1024]{1,0:T(8,128)(2,1)S(1)} %copy-done.5, bf16[384,1024]{1,0:T(8,128)(2,1)S(1)} %copy-done.6, bf16[384,256]{1,0:T(8,128)(2,1)S(1)} %collective-permute-done.refs_0_.kv.refs_2_, ...), custom_call_target="tpu_custom_call" | custom-call | flops 1207959552 | bytes 3145728 | tf_op jit(solution)/shard_map/block_stats/pallas_call | solution.py:35
  31.9 4.4 %block_gradients.3 = (bf16[384,256]{1,0:T(8,128)(2,1)S(1)}, bf16[384,3072]{1,0:T(8,128)(2,1)S(1)}) custom-call(s32[1]{0:T(128)} %bitcast.me_ref.me_ctx_ref, s32[4]{0:T(128)S(1)} %bitcast.18, f32[8,3072]{1,0:T(8,128)S(1)} %block_stats.7.stats, bf16[384,1024]{1,0:T(8,128)(2,1)S(1)} %copy-done.5, bf16[384,1024]{1,0:T(8,128)(2,1)S(1)} %copy-done.6, ...), custom_call_target="tpu_custom_call" | custom-call | flops 2415919104 | bytes 6291456 | tf_op jit(solution)/shard_map/block_gradients/pallas_call | solution.py:35
  36.3 4.4 %block_gradients.4 = (bf16[384,256]{1,0:T(8,128)(2,1)S(1)}, bf16[384,3072]{1,0:T(8,128)(2,1)S(1)}) custom-call(s32[1]{0:T(128)} %bitcast.me_ref.me_ctx_ref, s32[4]{0:T(128)S(1)} %bitcast.19, f32[8,3072]{1,0:T(8,128)S(1)} %block_stats.7.stats, bf16[384,1024]{1,0:T(8,128)(2,1)S(1)} %copy-done.5, bf16[384,1024]{1,0:T(8,128)(2,1)S(1)} %copy-done.6, ...), custom_call_target="tpu_custom_call" | custom-call | flops 2415919104 | bytes 6291456 | tf_op jit(solution)/shard_map/block_gradients/pallas_call | solution.py:35
  40.8 4.6 %block_gradients.5 = (bf16[384,256]{1,0:T(8,128)(2,1)S(1)}, bf16[384,3072]{1,0:T(8,128)(2,1)S(1)}) custom-call(s32[1]{0:T(128)} %bitcast.me_ref.me_ctx_ref, s32[4]{0:T(128)S(1)} %bitcast.20, f32[8,3072]{1,0:T(8,128)S(1)} %block_stats.7.stats, bf16[384,1024]{1,0:T(8,128)(2,1)S(1)} %copy-done.5, bf16[384,1024]{1,0:T(8,128)(2,1)S(1)} %copy-done.6, ...), custom_call_target="tpu_custom_call" | custom-call | flops 2415919104 | bytes 6291456 | tf_op jit(solution)/shard_map/block_gradients/pallas_call | solution.py:35
  46.1 7.3 %own_gradients.1 = (f32[384,256]{1,0:T(8,128)S(1)}, bf16[384,1024]{1,0:T(8,128)(2,1)}) custom-call(s32[1]{0:T(128)} %bitcast.me_ref.me_ctx_ref, s32[4]{0:T(128)S(1)} %bitcast.21, f32[8,3072]{1,0:T(8,128)S(1)} %block_stats.7.stats, bf16[384,1024]{1,0:T(8,128)(2,1)S(1)} %copy-done.5, bf16[384,1024]{1,0:T(8,128)(2,1)S(1)} %copy-done.6, ...), custom_call_target="tpu_custom_call" | custom-call | flops 4831838208 | bytes 6291456 | tf_op jit(solution)/shard_map/own_gradients/pallas_call | solution.py:35
  53.4 1.9 %collective-permute-done.4.refs_1_ = bf16[384,256]{1,0:T(8,128)(2,1)S(1)} collective-permute-done((bf16[384,256]{1,0:T(8,128)(2,1)S(1)}, bf16[384,256]{1,0:T(8,128)(2,1)S(1)}, u32[]{:S(2)}, u32[]{:S(2)}) %collective-permute-start.4) | collective-permute-done | bytes 196640 | tf_op jit(solution)/shard_map/ppermute | solution.py:465
  55.3 1.3 %send_tiles.2 = (bf16[4,512,256]{2,1,0:T(8,128)(2,1)S(1)}, f32[16,128]{1,0:T(8,128)S(1)}, bf16[384,128]{1,0:T(8,128)(2,1)}, bf16[384,128]{1,0:T(8,128)(2,1)}, bf16[384,256]{1,0:T(8,128)(2,1)S(1)}) custom-call(s32[1]{0:T(128)} %bitcast.2.me_ref.me_dp_ref, f32[384,256]{1,0:T(8,128)S(1)} %get-tuple-element.57.own_ref, ...), custom_call_target="tpu_custom_call" | custom-call | flops 402653184 | bytes 4718592 | tf_op jit(solution)/shard_map/send_tiles/pallas_call | solution.py:35
  58.1 1.2 %collective-permute-done.6.got_ref = bf16[4,512,256]{2,1,0:T(8,128)(2,1)S(1)} collective-permute-done((bf16[4,512,256]{2,1,0:T(8,128)(2,1)S(1)}, bf16[4,512,256]{2,1,0:T(8,128)(2,1)S(1)}, u32[]{:S(2)}, u32[]{:S(2)}) %collective-permute-start.6) | collective-permute-done | bytes 1048608 | tf_op jit(solution)/shard_map/ppermute | solution.py:462
  60.2 1.6 %collective-permute-start.7 = (bf16[1072,128]{1,0:T(8,128)(2,1)S(1)}, bf16[1072,128]{1,0:T(8,128)(2,1)S(1)}, u32[]{:S(2)}, u32[]{:S(2)}) collective-permute-start(bf16[1072,128]{1,0:T(8,128)(2,1)S(1)} %get-tuple-element.70), channel_id=1, source_target_pairs={{0,8},{4,12},{8,0},{12,4},{16,24},{20,28},{24,16},{28,20},{1,9},{5... | collective-permute-start | bytes 823304 | tf_op jit(solution)/shard_map/ppermute | solution.py:462
  61.8 1.5 %collective-permute-start.8 = (bf16[1024,128]{1,0:T(8,128)(2,1)S(1)}, bf16[1024,128]{1,0:T(8,128)(2,1)S(1)}, u32[]{:S(2)}, u32[]{:S(2)}) collective-permute-start(bf16[1024,128]{1,0:T(8,128)(2,1)S(1)} %get-tuple-element.72), channel_id=1, source_target_pairs={{0,16},{4,20},{8,24},{12,28},{16,0},{20,4},{24,8},{28,12},{1,17},{... | collective-permute-start | bytes 786440 | tf_op jit(solution)/shard_map/ppermute | solution.py:462
  65.3 5.7 %collective-permute-done.8.high_got = bf16[1024,128]{1,0:T(8,128)(2,1)S(1)} collective-permute-done((bf16[1024,128]{1,0:T(8,128)(2,1)S(1)}, bf16[1024,128]{1,0:T(8,128)(2,1)S(1)}, u32[]{:S(2)}, u32[]{:S(2)}) %collective-permute-start.8) | collective-permute-done | bytes 262176 | tf_op jit(solution)/shard_map/ppermute | solution.py:462
  71.1 1.6 %collective-permute-start.9 = (bf16[560,128]{1,0:T(8,128)(2,1)S(1)}, bf16[560,128]{1,0:T(8,128)(2,1)S(1)}, u32[]{:S(2)}, u32[]{:S(2)}) collective-permute-start(bf16[560,128]{1,0:T(8,128)(2,1)S(1)} %get-tuple-element.75), channel_id=1, source_target_pairs={{0,16},{4,20},{8,24},{12,28},{16,0},{20,4},{24,8},{28,12},{1,17},{... | collective-permute-start | bytes 430088 | tf_op jit(solution)/shard_map/ppermute | solution.py:462
  73.3 1.2 %collective-permute-done.17.refs_0_ = f32[16,128]{1,0:T(8,128)S(1)} collective-permute-done((f32[16,128]{1,0:T(8,128)S(1)}, f32[16,128]{1,0:T(8,128)S(1)}, u32[]{:S(2)}, u32[]{:S(2)}) %collective-permute-start.17) | collective-permute-done | bytes 8224 | tf_op jit(solution)/shard_map/ppermute | solution.py:462
  74.4 1.3 %collective-permute-start.18 = (f32[16,128]{1,0:T(8,128)S(1)}, f32[16,128]{1,0:T(8,128)S(1)}, u32[]{:S(2)}, u32[]{:S(2)}) collective-permute-start(f32[16,128]{1,0:T(8,128)S(1)} %get-tuple-element.88.top_ref), channel_id=1, source_target_pairs={{0,12},{4,8},{8,4},{12,0},{16,28},{20,24},{24,20},{28,16},{1,13},{... | collective-permute-start | bytes 24584 | tf_op jit(solution)/shard_map/ppermute | solution.py:462
  75.7 1.9 %collective-permute-done.18.refs_1_ = f32[16,128]{1,0:T(8,128)S(1)} collective-permute-done((f32[16,128]{1,0:T(8,128)S(1)}, f32[16,128]{1,0:T(8,128)S(1)}, u32[]{:S(2)}, u32[]{:S(2)}) %collective-permute-start.18) | collective-permute-done | bytes 8224 | tf_op jit(solution)/shard_map/ppermute | solution.py:462
  77.8 1.0 collective-permute-start.19
  78.7 1.5 %collective-permute-start.20 = (bf16[512,128]{1,0:T(8,128)(2,1)S(1)}, bf16[512,128]{1,0:T(8,128)(2,1)S(1)}, u32[]{:S(2)}, u32[]{:S(2)}) collective-permute-start(bf16[512,128]{1,0:T(8,128)(2,1)S(1)} %get-tuple-element.92), channel_id=1, source_target_pairs={{0,8},{4,12},{8,0},{12,4},{16,24},{20,28},{24,16},{28,20},{1,9},{5... | collective-permute-start | bytes 393224 | tf_op jit(solution)/shard_map/ppermute | solution.py:462
  80.8 2.3 %collective-permute-start.11 = (bf16[176,256]{1,0:T(8,128)(2,1)S(1)}, bf16[176,256]{1,0:T(8,128)(2,1)S(1)}, u32[]{:S(2)}, u32[]{:S(2)}) collective-permute-start(bf16[176,256]{1,0:T(8,128)(2,1)S(1)} %get-tuple-element.80), channel_id=1, source_target_pairs={{0,1},{1,0},{2,3},{3,2},{4,5},{5,4},{6,7},{7,6},{8,9},{9,8},{10,11... | collective-permute-start | bytes 270344 | tf_op jit(solution)/shard_map/ppermute | solution.py:465
  83.2 1.9 %collective-permute-start.12 = (bf16[176,256]{1,0:T(8,128)(2,1)S(1)}, bf16[176,256]{1,0:T(8,128)(2,1)S(1)}, u32[]{:S(2)}, u32[]{:S(2)}) collective-permute-start(bf16[176,256]{1,0:T(8,128)(2,1)S(1)} %get-tuple-element.81), channel_id=1, source_target_pairs={{0,2},{1,3},{2,0},{3,1},{4,6},{5,7},{6,4},{7,5},{8,10},{9,11},{10,... | collective-permute-start | bytes 270344 | tf_op jit(solution)/shard_map/ppermute | solution.py:465
  85.1 1.5 %collective-permute-start.13 = (bf16[176,256]{1,0:T(8,128)(2,1)S(1)}, bf16[176,256]{1,0:T(8,128)(2,1)S(1)}, u32[]{:S(2)}, u32[]{:S(2)}) collective-permute-start(bf16[176,256]{1,0:T(8,128)(2,1)S(1)} %get-tuple-element.82), channel_id=1, source_target_pairs={{0,3},{1,2},{2,1},{3,0},{4,7},{5,6},{6,5},{7,4},{8,11},{9,10},{10,... | collective-permute-start | bytes 270344 | tf_op jit(solution)/shard_map/ppermute | solution.py:465
  87.3 2.4 %collective-permute-start.22 = (bf16[176,256]{1,0:T(8,128)(2,1)S(1)}, bf16[176,256]{1,0:T(8,128)(2,1)S(1)}, u32[]{:S(2)}, u32[]{:S(2)}) collective-permute-start(bf16[176,256]{1,0:T(8,128)(2,1)S(1)} %get-tuple-element.96), channel_id=1, source_target_pairs={{0,2},{1,3},{2,0},{3,1},{4,6},{5,7},{6,4},{7,5},{8,10},{9,11},{10,... | collective-permute-start | bytes 270344 | tf_op jit(solution)/shard_map/ppermute | solution.py:465
  89.6 1.5 %collective-permute-start.23 = (bf16[176,256]{1,0:T(8,128)(2,1)S(1)}, bf16[176,256]{1,0:T(8,128)(2,1)S(1)}, u32[]{:S(2)}, u32[]{:S(2)}) collective-permute-start(bf16[176,256]{1,0:T(8,128)(2,1)S(1)} %get-tuple-element.97), channel_id=1, source_target_pairs={{0,3},{1,2},{2,1},{3,0},{4,7},{5,6},{6,5},{7,4},{8,11},{9,10},{10,... | collective-permute-start | bytes 270344 | tf_op jit(solution)/shard_map/ppermute | solution.py:465
  91.1 2.8 %collective-permute-done.13.refs_3_ = bf16[176,256]{1,0:T(8,128)(2,1)S(1)} collective-permute-done((bf16[176,256]{1,0:T(8,128)(2,1)S(1)}, bf16[176,256]{1,0:T(8,128)(2,1)S(1)}, u32[]{:S(2)}, u32[]{:S(2)}) %collective-permute-start.13) | collective-permute-done | bytes 90144 | tf_op jit(solution)/shard_map/ppermute | solution.py:465
  93.9 7.2 %collective-permute-done.22.refs_6_ = bf16[176,256]{1,0:T(8,128)(2,1)S(1)} collective-permute-done((bf16[176,256]{1,0:T(8,128)(2,1)S(1)}, bf16[176,256]{1,0:T(8,128)(2,1)S(1)}, u32[]{:S(2)}, u32[]{:S(2)}) %collective-permute-start.22) | collective-permute-done | bytes 90144 | tf_op jit(solution)/shard_map/ppermute | solution.py:465
  (52 shorter events, 10.8 us)
Async XLA Ops:
  0.6 0.9 copy-start.1
  1.5 0.9 copy-start.3
  2.5 15.8 %collective-permute-start.2 = (bf16[384,256]{1,0:T(8,128)(2,1)S(1)}, bf16[384,256]{1,0:T(8,128)(2,1)S(1)}, u32[]{:S(2)}, u32[]{:S(2)}) collective-permute-start(bf16[384,256]{1,0:T(8,128)(2,1)S(1)} %join_keys_values.1), channel_id=1, source_target_pairs={{0,1},{1,0},{2,3},{3,2},{4,5},{5,4},{6,7},{7,6},{8,9},{9,8},{10,11... | collective-permute-start | bytes 589832 | tf_op jit(solution)/shard_map/ppermute | solution.py:465
  5.5 23.1 %collective-permute-start = (bf16[384,256]{1,0:T(8,128)(2,1)S(1)}, bf16[384,256]{1,0:T(8,128)(2,1)S(1)}, u32[]{:S(2)}, u32[]{:S(2)}) collective-permute-start(bf16[384,256]{1,0:T(8,128)(2,1)S(1)} %join_keys_values.1), channel_id=1, source_target_pairs={{0,3},{1,2},{2,1},{3,0},{4,7},{5,6},{6,5},{7,4},{8,11},{9,10},{10,... | collective-permute-start | bytes 589832 | tf_op jit(solution)/shard_map/ppermute | solution.py:465
  8.0 17.4 %collective-permute-start.1 = (bf16[384,256]{1,0:T(8,128)(2,1)S(1)}, bf16[384,256]{1,0:T(8,128)(2,1)S(1)}, u32[]{:S(2)}, u32[]{:S(2)}) collective-permute-start(bf16[384,256]{1,0:T(8,128)(2,1)S(1)} %join_keys_values.1), channel_id=1, source_target_pairs={{0,2},{1,3},{2,0},{3,1},{4,6},{5,7},{6,4},{7,5},{8,10},{9,11},{10,... | collective-permute-start | bytes 589832 | tf_op jit(solution)/shard_map/ppermute | solution.py:465
  8.1 2.8 %copy-start = (bf16[384,8192]{1,0:T(8,128)(2,1)S(1)}, bf16[384,8192]{1,0:T(8,128)(2,1)}, u32[]{:S(2)}) copy-start(bf16[384,8192]{1,0:T(8,128)(2,1)} %a_hbm.1) | copy-start | bytes 18874372
  10.9 4.3 %copy-start.2 = (bf16[384,128]{1,0:T(8,128)(2,1)S(1)}, bf16[384,128]{1,0:T(8,128)(2,1)}, u32[]{:S(2)}) copy-start(bf16[384,128]{1,0:T(8,128)(2,1)} %k_ref.3) | copy-start | bytes 294916
  10.9 4.3 %copy-start.4 = (bf16[384,128]{1,0:T(8,128)(2,1)S(1)}, bf16[384,128]{1,0:T(8,128)(2,1)}, u32[]{:S(2)}) copy-start(bf16[384,128]{1,0:T(8,128)(2,1)} %v_ref.3) | copy-start | bytes 294916
  10.9 4.3 %copy-start.5 = (bf16[384,1024]{1,0:T(8,128)(2,1)S(1)}, bf16[384,1024]{1,0:T(8,128)(2,1)}, u32[]{:S(2)}) copy-start(bf16[384,1024]{1,0:T(8,128)(2,1)} %q_ref.15) | copy-start | bytes 2359300
  10.9 4.3 %copy-start.6 = (bf16[384,1024]{1,0:T(8,128)(2,1)S(1)}, bf16[384,1024]{1,0:T(8,128)(2,1)}, u32[]{:S(2)}) copy-start(bf16[384,1024]{1,0:T(8,128)(2,1)} %do_ref.15) | copy-start | bytes 2359300
  10.9 4.3 %copy-start.7 = (s32[1,4]{1,0:T(1,128)S(1)}, s32[1,4]{1,0:T(1,128)}, u32[]{:S(2)}) copy-start(s32[1,4]{1,0:T(1,128)} %param.7) | copy-start | bytes 52
  36.3 17.2 %collective-permute-start.3 = (bf16[384,256]{1,0:T(8,128)(2,1)S(1)}, bf16[384,256]{1,0:T(8,128)(2,1)S(1)}, u32[]{:S(2)}, u32[]{:S(2)}) collective-permute-start(bf16[384,256]{1,0:T(8,128)(2,1)S(1)} %get-tuple-element.58), channel_id=1, source_target_pairs={{0,1},{1,0},{2,3},{3,2},{4,5},{5,4},{6,7},{7,6},{8,9},{9,8},{10,11... | collective-permute-start | bytes 589832 | tf_op jit(solution)/shard_map/ppermute | solution.py:465
  40.7 14.6 %collective-permute-start.4 = (bf16[384,256]{1,0:T(8,128)(2,1)S(1)}, bf16[384,256]{1,0:T(8,128)(2,1)S(1)}, u32[]{:S(2)}, u32[]{:S(2)}) collective-permute-start(bf16[384,256]{1,0:T(8,128)(2,1)S(1)} %get-tuple-element.59), channel_id=1, source_target_pairs={{0,2},{1,3},{2,0},{3,1},{4,6},{5,7},{6,4},{7,5},{8,10},{9,11},{10,... | collective-permute-start | bytes 589832 | tf_op jit(solution)/shard_map/ppermute | solution.py:465
  45.4 10.0 %collective-permute-start.5 = (bf16[384,256]{1,0:T(8,128)(2,1)S(1)}, bf16[384,256]{1,0:T(8,128)(2,1)S(1)}, u32[]{:S(2)}, u32[]{:S(2)}) collective-permute-start(bf16[384,256]{1,0:T(8,128)(2,1)S(1)} %get-tuple-element.60), channel_id=1, source_target_pairs={{0,3},{1,2},{2,1},{3,0},{4,7},{5,6},{6,5},{7,4},{8,11},{9,10},{10,... | collective-permute-start | bytes 589832 | tf_op jit(solution)/shard_map/ppermute | solution.py:465
  56.6 2.7 %collective-permute-start.6 = (bf16[4,512,256]{2,1,0:T(8,128)(2,1)S(1)}, bf16[4,512,256]{2,1,0:T(8,128)(2,1)S(1)}, u32[]{:S(2)}, u32[]{:S(2)}) collective-permute-start(bf16[4,512,256]{2,1,0:T(8,128)(2,1)S(1)} %get-tuple-element.66), channel_id=1, source_target_pairs={{0,4},{4,0},{8,12},{12,8},{16,20},{20,16},{24,28},{28,24},{1,5},{5... | collective-permute-start | bytes 3145736 | tf_op jit(solution)/shard_map/ppermute | solution.py:462
  57.5 5.9 %collective-permute-start.14 = (bf16[4,512,256]{2,1,0:T(8,128)(2,1)S(1)}, bf16[4,512,256]{2,1,0:T(8,128)(2,1)S(1)}, u32[]{:S(2)}, u32[]{:S(2)}) collective-permute-start(bf16[4,512,256]{2,1,0:T(8,128)(2,1)S(1)} %get-tuple-element.83), channel_id=1, source_target_pairs={{0,4},{4,0},{8,12},{12,8},{16,20},{20,16},{24,28},{28,24},{1,5},{5... | collective-permute-start | bytes 3145736 | tf_op jit(solution)/shard_map/ppermute | solution.py:462
  60.2 10.8 %collective-permute-start.7 = (bf16[1072,128]{1,0:T(8,128)(2,1)S(1)}, bf16[1072,128]{1,0:T(8,128)(2,1)S(1)}, u32[]{:S(2)}, u32[]{:S(2)}) collective-permute-start(bf16[1072,128]{1,0:T(8,128)(2,1)S(1)} %get-tuple-element.70), channel_id=1, source_target_pairs={{0,8},{4,12},{8,0},{12,4},{16,24},{20,28},{24,16},{28,20},{1,9},{5... | collective-permute-start | bytes 823304 | tf_op jit(solution)/shard_map/ppermute | solution.py:462
  61.8 9.2 %collective-permute-start.8 = (bf16[1024,128]{1,0:T(8,128)(2,1)S(1)}, bf16[1024,128]{1,0:T(8,128)(2,1)S(1)}, u32[]{:S(2)}, u32[]{:S(2)}) collective-permute-start(bf16[1024,128]{1,0:T(8,128)(2,1)S(1)} %get-tuple-element.72), channel_id=1, source_target_pairs={{0,16},{4,20},{8,24},{12,28},{16,0},{20,4},{24,8},{28,12},{1,17},{... | collective-permute-start | bytes 786440 | tf_op jit(solution)/shard_map/ppermute | solution.py:462
  64.3 13.4 %collective-permute-start.15 = (bf16[1072,128]{1,0:T(8,128)(2,1)S(1)}, bf16[1072,128]{1,0:T(8,128)(2,1)S(1)}, u32[]{:S(2)}, u32[]{:S(2)}) collective-permute-start(bf16[1072,128]{1,0:T(8,128)(2,1)S(1)} %get-tuple-element.85), channel_id=1, source_target_pairs={{0,8},{4,12},{8,0},{12,4},{16,24},{20,28},{24,16},{28,20},{1,9},{5... | collective-permute-start | bytes 823304 | tf_op jit(solution)/shard_map/ppermute | solution.py:462
  64.8 12.8 %collective-permute-start.16 = (bf16[1024,128]{1,0:T(8,128)(2,1)S(1)}, bf16[1024,128]{1,0:T(8,128)(2,1)S(1)}, u32[]{:S(2)}, u32[]{:S(2)}) collective-permute-start(bf16[1024,128]{1,0:T(8,128)(2,1)S(1)} %get-tuple-element.87), channel_id=1, source_target_pairs={{0,16},{4,20},{8,24},{12,28},{16,0},{20,4},{24,8},{28,12},{1,17},{... | collective-permute-start | bytes 786440 | tf_op jit(solution)/shard_map/ppermute | solution.py:462
  71.1 9.1 %collective-permute-start.9 = (bf16[560,128]{1,0:T(8,128)(2,1)S(1)}, bf16[560,128]{1,0:T(8,128)(2,1)S(1)}, u32[]{:S(2)}, u32[]{:S(2)}) collective-permute-start(bf16[560,128]{1,0:T(8,128)(2,1)S(1)} %get-tuple-element.75), channel_id=1, source_target_pairs={{0,16},{4,20},{8,24},{12,28},{16,0},{20,4},{24,8},{28,12},{1,17},{... | collective-permute-start | bytes 430088 | tf_op jit(solution)/shard_map/ppermute | solution.py:462
  72.7 7.5 %collective-permute-start.10 = (bf16[512,128]{1,0:T(8,128)(2,1)S(1)}, bf16[512,128]{1,0:T(8,128)(2,1)S(1)}, u32[]{:S(2)}, u32[]{:S(2)}) collective-permute-start(bf16[512,128]{1,0:T(8,128)(2,1)S(1)} %get-tuple-element.77), channel_id=1, source_target_pairs={{0,8},{4,12},{8,0},{12,4},{16,24},{20,28},{24,16},{28,20},{1,9},{5... | collective-permute-start | bytes 393224 | tf_op jit(solution)/shard_map/ppermute | solution.py:462
  73.3 1.2 %collective-permute-start.17 = (f32[16,128]{1,0:T(8,128)S(1)}, f32[16,128]{1,0:T(8,128)S(1)}, u32[]{:S(2)}, u32[]{:S(2)}) collective-permute-start(f32[16,128]{1,0:T(8,128)S(1)} %get-tuple-element.88.top_ref), channel_id=1, source_target_pairs={{0,4},{4,0},{8,12},{12,8},{16,20},{20,16},{24,28},{28,24},{1,5},{5... | collective-permute-start | bytes 24584 | tf_op jit(solution)/shard_map/ppermute | solution.py:462
  74.4 3.2 %collective-permute-start.18 = (f32[16,128]{1,0:T(8,128)S(1)}, f32[16,128]{1,0:T(8,128)S(1)}, u32[]{:S(2)}, u32[]{:S(2)}) collective-permute-start(f32[16,128]{1,0:T(8,128)S(1)} %get-tuple-element.88.top_ref), channel_id=1, source_target_pairs={{0,12},{4,8},{8,4},{12,0},{16,28},{20,24},{24,20},{28,16},{1,13},{... | collective-permute-start | bytes 24584 | tf_op jit(solution)/shard_map/ppermute | solution.py:462
  77.8 8.8 %collective-permute-start.19 = (bf16[560,128]{1,0:T(8,128)(2,1)S(1)}, bf16[560,128]{1,0:T(8,128)(2,1)S(1)}, u32[]{:S(2)}, u32[]{:S(2)}) collective-permute-start(bf16[560,128]{1,0:T(8,128)(2,1)S(1)} %get-tuple-element.90), channel_id=1, source_target_pairs={{0,16},{4,20},{8,24},{12,28},{16,0},{20,4},{24,8},{28,12},{1,17},{... | collective-permute-start | bytes 430088 | tf_op jit(solution)/shard_map/ppermute | solution.py:462
  78.7 7.8 %collective-permute-start.20 = (bf16[512,128]{1,0:T(8,128)(2,1)S(1)}, bf16[512,128]{1,0:T(8,128)(2,1)S(1)}, u32[]{:S(2)}, u32[]{:S(2)}) collective-permute-start(bf16[512,128]{1,0:T(8,128)(2,1)S(1)} %get-tuple-element.92), channel_id=1, source_target_pairs={{0,8},{4,12},{8,0},{12,4},{16,24},{20,28},{24,16},{28,20},{1,9},{5... | collective-permute-start | bytes 393224 | tf_op jit(solution)/shard_map/ppermute | solution.py:462
  80.8 8.8 %collective-permute-start.11 = (bf16[176,256]{1,0:T(8,128)(2,1)S(1)}, bf16[176,256]{1,0:T(8,128)(2,1)S(1)}, u32[]{:S(2)}, u32[]{:S(2)}) collective-permute-start(bf16[176,256]{1,0:T(8,128)(2,1)S(1)} %get-tuple-element.80), channel_id=1, source_target_pairs={{0,1},{1,0},{2,3},{3,2},{4,5},{5,4},{6,7},{7,6},{8,9},{9,8},{10,11... | collective-permute-start | bytes 270344 | tf_op jit(solution)/shard_map/ppermute | solution.py:465
  83.2 7.9 %collective-permute-start.12 = (bf16[176,256]{1,0:T(8,128)(2,1)S(1)}, bf16[176,256]{1,0:T(8,128)(2,1)S(1)}, u32[]{:S(2)}, u32[]{:S(2)}) collective-permute-start(bf16[176,256]{1,0:T(8,128)(2,1)S(1)} %get-tuple-element.81), channel_id=1, source_target_pairs={{0,2},{1,3},{2,0},{3,1},{4,6},{5,7},{6,4},{7,5},{8,10},{9,11},{10,... | collective-permute-start | bytes 270344 | tf_op jit(solution)/shard_map/ppermute | solution.py:465
  85.1 8.8 %collective-permute-start.13 = (bf16[176,256]{1,0:T(8,128)(2,1)S(1)}, bf16[176,256]{1,0:T(8,128)(2,1)S(1)}, u32[]{:S(2)}, u32[]{:S(2)}) collective-permute-start(bf16[176,256]{1,0:T(8,128)(2,1)S(1)} %get-tuple-element.82), channel_id=1, source_target_pairs={{0,3},{1,2},{2,1},{3,0},{4,7},{5,6},{6,5},{7,4},{8,11},{9,10},{10,... | collective-permute-start | bytes 270344 | tf_op jit(solution)/shard_map/ppermute | solution.py:465
  86.6 7.2 %collective-permute-start.21 = (bf16[176,256]{1,0:T(8,128)(2,1)S(1)}, bf16[176,256]{1,0:T(8,128)(2,1)S(1)}, u32[]{:S(2)}, u32[]{:S(2)}) collective-permute-start(bf16[176,256]{1,0:T(8,128)(2,1)S(1)} %get-tuple-element.95), channel_id=1, source_target_pairs={{0,1},{1,0},{2,3},{3,2},{4,5},{5,4},{6,7},{7,6},{8,9},{9,8},{10,11... | collective-permute-start | bytes 270344 | tf_op jit(solution)/shard_map/ppermute | solution.py:465
  87.3 13.8 %collective-permute-start.22 = (bf16[176,256]{1,0:T(8,128)(2,1)S(1)}, bf16[176,256]{1,0:T(8,128)(2,1)S(1)}, u32[]{:S(2)}, u32[]{:S(2)}) collective-permute-start(bf16[176,256]{1,0:T(8,128)(2,1)S(1)} %get-tuple-element.96), channel_id=1, source_target_pairs={{0,2},{1,3},{2,0},{3,1},{4,6},{5,7},{6,4},{7,5},{8,10},{9,11},{10,... | collective-permute-start | bytes 270344 | tf_op jit(solution)/shard_map/ppermute | solution.py:465
  89.6 11.4 %collective-permute-start.23 = (bf16[176,256]{1,0:T(8,128)(2,1)S(1)}, bf16[176,256]{1,0:T(8,128)(2,1)S(1)}, u32[]{:S(2)}, u32[]{:S(2)}) collective-permute-start(bf16[176,256]{1,0:T(8,128)(2,1)S(1)} %get-tuple-element.97), channel_id=1, source_target_pairs={{0,3},{1,2},{2,1},{3,0},{4,7},{5,6},{6,5},{7,4},{8,11},{9,10},{10,... | collective-permute-start | bytes 270344 | tf_op jit(solution)/shard_map/ppermute | solution.py:465

commit v5 on v4

--- a/solution.py
+++ b/solution.py
@@ -12,7 +12,7 @@
 FAR = 1e30
 MIB = 1024 * 1024
 CHUNK = 256
-TOP_ROWS, TOP_LANES = 16, 128
+TOP_ROWS, TOP_LANES, PACK_LANES = 16, 128, 32
 BF16, F32 = jnp.bfloat16, jnp.float32
 BF16_MAX = float(jnp.finfo(jnp.bfloat16).max)
 NT = (((1,), (1,)), ((), ()))
@@ -31,13 +31,17 @@
     return jax.ShapeDtypeStruct(dims, dtype)
 
 
-def whole_call(kernel, name, scalars, operands, out_shape, mib, cost, scratch=()):
+def whole_call(kernel, name, scalars, operands, out_shape, mib, cost, scratch=(), after=()):
+    def body(*refs):
+        first = len(scalars) + len(operands)
+        kernel(*refs[:first], *refs[first + len(after) :])
+
     return pl.pallas_call(
-        kernel,
+        body,
         grid_spec=pltpu.PrefetchScalarGridSpec(
             num_scalar_prefetch=len(scalars),
             grid=(1,),
-            in_specs=[whole(x) for x in operands],
+            in_specs=[whole(x) for x in operands] + [pl.BlockSpec(memory_space=pl.ANY)] * len(after),
             out_specs=[whole(x) for x in out_shape],
             scratch_shapes=list(scratch),
         ),
@@ -45,22 +49,36 @@
         compiler_params=pltpu.CompilerParams(vmem_limit_bytes=mib * MIB),
         cost_estimate=pl.CostEstimate(flops=cost[0], bytes_accessed=cost[1], transcendentals=0),
         name=name,
-    )(*scalars, *operands)
-
-
-def join_kernel(k_ref, v_ref, out_ref):
-    hd = k_ref.shape[1]
-    out_ref[:, :hd] = k_ref[...]
-    out_ref[:, hd:] = v_ref[...]
-
-
-def join(keys, values):
-    rows, hd = keys.shape
-    out = [shape((rows, 2 * hd))]
-    return whole_call(join_kernel, "join_keys_values", [], [keys, values], out, 4, (0, 8 * rows * hd))[0]
-
-
-def prepare_kernel(pieces, a_hbm, e_hbm, a_out, e_out, a_buf, a_sems, e_sems):
+    )(*scalars, *operands, *after)
+
+
+def copy_all(pairs_of_refs, sems):
+    copies = [pltpu.make_async_copy(src, dst, sems.at[i]) for i, (src, dst) in enumerate(pairs_of_refs)]
+    for copy in copies:
+        copy.start()
+    for copy in copies:
+        copy.wait()
+
+
+def join_kernel(k_hbm, v_hbm, out_ref, sems):
+    hd = k_hbm.shape[1]
+    copy_all([(k_hbm, out_ref.at[:, pl.ds(0, hd)]), (v_hbm, out_ref.at[:, pl.ds(hd, hd)])], sems)
+
+
+def load_call(kernel, name, operands, out_shape, mib):
+    return pl.pallas_call(
+        kernel,
+        in_specs=[pl.BlockSpec(memory_space=pltpu.HBM)] * 2,
+        out_specs=[pl.BlockSpec(memory_space=pltpu.VMEM)] * len(out_shape),
+        out_shape=out_shape,
+        scratch_shapes=[pltpu.SemaphoreType.DMA((2,))],
+        compiler_params=pltpu.CompilerParams(vmem_limit_bytes=mib * MIB),
+        cost_estimate=pl.CostEstimate(flops=0, bytes_accessed=4 * operands[0].size, transcendentals=0),
+        name=name,
+    )(*operands)
+
+
+def prepare_kernel(pieces, a_hbm, e_hbm, _, a_out, e_out, a_buf, a_sems, e_sems):
     model = a_buf.shape[1]
     tile = model // pieces
     parts = [pl.ds(i * tile, tile) for i in range(pieces)]
@@ -75,14 +93,14 @@
         copy.wait()
 
 
-def prepare(activations, errors):
+def prepare(activations, errors, after):
     rows, model = activations.shape
     pieces = 8
     hbm = pl.BlockSpec(memory_space=pltpu.HBM)
     outs = [shape((model, rows)), shape(errors.shape, F32)]
     return pl.pallas_call(
         functools.partial(prepare_kernel, pieces),
-        in_specs=[hbm, hbm],
+        in_specs=[hbm, hbm, pl.BlockSpec(memory_space=pl.ANY)],
         out_specs=[pl.BlockSpec(memory_space=pltpu.VMEM)] * 2,
         out_shape=outs,
         scratch_shapes=[
@@ -95,14 +113,12 @@
             flops=0, bytes_accessed=2 * rows * model + 4 * errors.size, transcendentals=0
         ),
         name="prepare",
-    )(activations, errors)
-
-
-def key_value(refs):
-    if len(refs) == 2:
-        return refs[0][...], refs[1][...]
-    hd = refs[0].shape[1] // 2
-    return refs[0][:, :hd], refs[0][:, hd:]
+    )(activations, errors, *after)
+
+
+def key_value(ref):
+    hd = ref.shape[1] // 2
+    return ref[:, :hd], ref[:, hd:]
 
 
 def head_pair(ref, i, hd):
@@ -129,11 +145,8 @@
     return span_ref[me ^ b] < span_ref[me]
 
 
-def stats_kernel(b, me_ref, span_ref, q_ref, do_ref, *refs):
-    if b == 0:
-        kv, out = refs[:2], refs[2]
-    else:
-        kv, before, out = refs[:1], refs[1], refs[2]
+def stats_kernel(b, me_ref, span_ref, q_ref, do_ref, kv, *refs):
+    before, out = refs[0], refs[-1]
 
     def run():
         k, v = key_value(kv)
@@ -163,7 +176,7 @@
                 out[2:3, lanes] = weighted
             return carry
 
-        lax.fori_loop(0, q_ref.shape[1] // (2 * hd), heads, 0)
+        lax.fori_loop(0, q_ref.shape[1] // (2 * hd), heads, 0, unroll=True)
 
     if b == 0:
         run()
@@ -176,7 +189,7 @@
             out[...] = before[...]
 
 
-def block_gradients(own, stats, q_ref, do_ref, kv, p_buf, ds_ref, ds_step, dk, dv, after):
+def block_gradients(own, stats, q_ref, do_ref, kv, p_buf, ds_ref, dk, dv):
     k, v = key_value(kv)
     rows, hd = k.shape
     pair = 2 * rows
@@ -195,14 +208,13 @@
             p = jnp.exp2(s * factor - level)
             p_buf[:, part] = p.astype(BF16)
             ds = (p * (dp - stats[2:3, lanes] / total)).astype(BF16)
-            ds_ref[:, pl.ds(pl.multiple_of(i * ds_step + t * CHUNK, CHUNK), CHUNK)] = ds
-        ds = ds_ref[:, pl.ds(pl.multiple_of(i * ds_step, CHUNK), pair)]
+            ds_ref[:, lanes] = ds
+        ds = ds_ref[:, pl.ds(pl.multiple_of(i * pair, CHUNK), pair)]
         dk[...] += jnp.dot(ds, q, preferred_element_type=F32)
         dv[...] += jnp.dot(p_buf[...], do, preferred_element_type=F32)
-        after(i, ds)
         return carry
 
-    lax.fori_loop(0, q_ref.shape[1] // (2 * hd), heads, 0)
+    lax.fori_loop(0, q_ref.shape[1] // (2 * hd), heads, 0, unroll=True)
     inverse = 1.0 / hd**0.5
     return dk[...] * inverse, dv[...]
 
@@ -213,9 +225,7 @@
 
     @pl.when(keep)
     def _():
-        dk_sum, dv_sum = block_gradients(
-            False, stats, q_ref, do_ref, (kv,), p_buf, ds_out, 2 * rows, dk, dv, lambda i, ds: None
-        )
+        dk_sum, dv_sum = block_gradients(False, stats, q_ref, do_ref, kv, p_buf, ds_out, dk, dv)
         out_ref[:, :hd] = dk_sum.astype(BF16)
         out_ref[:, hd:] = dv_sum.astype(BF16)
 
@@ -225,32 +235,30 @@
         ds_out[...] = jnp.zeros_like(ds_out)
 
 
-def own_kernel(n, me_ref, span_ref, stats, q_ref, do_ref, k_ref, v_ref, *refs):
-    kv_refs, ds_refs = refs[: n - 1], refs[n - 1 : 2 * n - 2]
-    out_ref, dq_ref, ds_buf, p_buf, dk, dv = refs[2 * n - 2 :]
-    rows, hd = k_ref.shape
-    pair = 2 * rows
-
-    def query_part(i, ds):
-        lanes = pl.ds(pl.multiple_of(i * pair, CHUNK), pair)
-        dq = lax.dot_general(ds, k_ref[...], TN, preferred_element_type=F32)
-        for kv, other in zip(kv_refs, ds_refs):
-            dq = dq + lax.dot_general(other[:, lanes], kv[:, :hd], TN, preferred_element_type=F32)
-        dq = (dq / hd**0.5).astype(BF16)
-        for h in range(2):
-            at = pl.multiple_of(i * (2 * hd) + h * hd, hd)
-            dq_ref[:, pl.ds(at, hd)] = dq[h * rows : (h + 1) * rows]
-
-    dk_sum, dv_sum = block_gradients(
-        True, stats, q_ref, do_ref, (k_ref, v_ref), p_buf, ds_buf, 0, dk, dv, query_part
-    )
+def own_kernel(me_ref, span_ref, stats, q_ref, do_ref, kv, out_ref, ds_out, p_buf, dk, dv):
+    hd = dk.shape[1]
+    dk_sum, dv_sum = block_gradients(True, stats, q_ref, do_ref, kv, p_buf, ds_out, dk, dv)
     out_ref[:, :hd] = dk_sum
     out_ref[:, hd:] = dv_sum
 
 
-def attention(me, spans, queries, out_grad, keys, values, received, swap):
-    n = len(received) + 1
-    rows, hd = keys.shape
+def query_kernel(n, *refs):
+    kv_refs, ds_refs, dq_ref = refs[:n], refs[n : 2 * n], refs[2 * n]
+    rows, hd = kv_refs[0].shape[0], kv_refs[0].shape[1] // 2
+    for h in range(dq_ref.shape[1] // hd):
+        dq = 0.0
+        for kv, ds in zip(kv_refs, ds_refs):
+            part = ds[:, h * rows : (h + 1) * rows]
+            dq = dq + lax.dot_general(part, kv[:, :hd], TN, preferred_element_type=F32)
+        dq_ref[:, h * hd : (h + 1) * hd] = (dq / hd**0.5).astype(BF16)
+
+
+def relay_kernel(block_ref, out_ref):
+    out_ref[...] = block_ref[...]
+
+
+def attention(me, spans, queries, out_grad, pairs, swap, n):
+    rows, hd = pairs.shape[0], pairs.shape[1] // 2
     columns = queries.shape[1]
     tall = columns // hd * rows
     product = 2 * rows * tall * hd
@@ -261,12 +269,25 @@
         cost = (4 * product, 8 * rows * columns)
         return whole_call(functools.partial(stats_kernel, b), "block_stats", scalars, operands, outs, 20, cost)[0]
 
-    stats = stats_call(0, [queries, out_grad, keys, values])
-    for b, kv in enumerate(received, 1):
-        stats = stats_call(b, [queries, out_grad, kv, stats])
+    blocks = [pairs] + [None] * (n - 1)
+    for b in range(1, n):
+        if b & (b - 1) == 0:
+            blocks[b] = swap(pairs, b)
+    stats = stats_call(0, [queries, out_grad, pairs])
+    for b in range(1, n):
+        if blocks[b] is None:
+            handed = blocks[b & (b - 1)]
+            if b == 3:
+                cost = (0, 8 * rows * hd)
+                handed = whole_call(relay_kernel, "relay", [], [handed], [shape(handed.shape)], 4, cost, [], first)[0]
+            blocks[b] = swap(handed, b & -b)
+        stats = stats_call(b, [queries, out_grad, blocks[b], stats])
+        if b == 1:
+            first = [stats]
+    received = blocks[1:]
     p_buf = pltpu.VMEM((rows, 2 * rows), BF16)
     sums = [pltpu.VMEM((rows, hd), F32)] * 2
-    parts, score_grads = [None] * (n - 1), [None] * (n - 1)
+    parts, score_grads, before = [None] * (n - 1), [None] * (n - 1), []
     for b in range(n - 1, 0, -1):
         part, score_grads[b - 1] = whole_call(
             functools.partial(other_kernel, b),
@@ -277,32 +298,53 @@
             24,
             (8 * product, 16 * rows * columns),
             [p_buf, *sums],
+            before,
         )
         parts[b - 1] = swap(part, b)
-    own, query_grad = whole_call(
-        functools.partial(own_kernel, n),
+        before = [part]
+    own, own_score_grad = whole_call(
+        own_kernel,
         "own_gradients",
         scalars,
-        [stats, queries, out_grad, keys, values, *received, *score_grads],
-        [shape((rows, 2 * hd), F32), shape((rows, columns))],
-        32,
-        (16 * product, 16 * rows * columns),
-        [p_buf, p_buf, *sums],
+        [stats, queries, out_grad, pairs],
+        [shape((rows, 2 * hd), F32), shape((rows, tall))],
+        24,
+        (8 * product, 16 * rows * columns),
+        [p_buf, *sums],
+        before,
     )
-    return query_grad, own, parts
+    return own, parts, blocks, [own_score_grad, *score_grads], before
+
+
+def query_gradients(blocks, score_grads, columns, after):
+    n = len(blocks)
+    rows, width = blocks[0].shape
+    return whole_call(
+        functools.partial(query_kernel, n),
+        "query_gradients",
+        [],
+        [*blocks, *score_grads],
+        [shape((rows, columns))],
+        24,
+        (2 * n * rows * rows * columns, 16 * rows * columns),
+        [],
+        after,
+    )[0]
 
 
 def pack_top(top):
-    high = jnp.minimum(top, BF16_MAX).astype(BF16)
-    rest = top - high.astype(F32)
-    middle = rest.astype(BF16)
-    low = (rest - middle.astype(F32)).astype(BF16)
-    return jnp.concatenate([high, middle, low], axis=0)
+    high = jnp.minimum(top, BF16_MAX).astype(BF16).astype(F32)
+    rest = top - high
+    middle = rest.astype(BF16).astype(F32)
+    low = rest - middle
+    return (high + pltpu.roll(middle, PACK_LANES, 1) + pltpu.roll(low, 2 * PACK_LANES, 1)).astype(BF16)
 
 
 def unpack_top(ref, at):
-    parts = [ref[at + i * TOP_ROWS : at + (i + 1) * TOP_ROWS, :TOP_LANES].astype(F32) for i in range(3)]
-    return parts[0] + (parts[1] + parts[2])
+    x = ref[at : at + TOP_ROWS, :].astype(F32)
+    total = x + (pltpu.roll(x, TOP_LANES - PACK_LANES, 1) + pltpu.roll(x, TOP_LANES - 2 * PACK_LANES, 1))
+    lane = lax.broadcasted_iota(jnp.int32, x.shape, 1)
+    return jnp.where(lane < PACK_LANES, total, 0.0)
 
 
 def tile_of(step, me_dp, bits, flip):
@@ -380,55 +422,58 @@
                 away[at * tall : (at + 1) * tall, :] = part
             else:
                 stay[(at - half) * tall : (at - half + 1) * tall, :] = part
-    low_away[half * tall :, :] = pack_top(top_ref[...])
-
-
-def largest(top_ref, low_got, at, others):
-    top = jnp.maximum(top_ref[...], unpack_top(low_got, at))
-    for other in others:
-        top = jnp.maximum(top, other[...])
-    return top
-
-
-def add_kernel(n_others, low, low_got, high, high_got, top_ref, *refs):
-    others = refs[:n_others]
-    low_away, low_stay, high_away, high_stay, top_out = refs[n_others:]
+    if low_away.shape[0] > half * tall:
+        low_away[half * tall :, :] = pack_top(top_ref[...])
+
+
+def largest(tops, low_got, size):
+    found = [top[...] for top in tops]
+    if low_got.shape[0] > size:
+        found.append(unpack_top(low_got, size))
+    return functools.reduce(jnp.maximum, found)
+
+
+def add_kernel(n_tops, low, low_got, high, high_got, *refs):
+    tops = refs[:n_tops]
+    low_away, low_stay, high_away, high_stay, *top_out = refs[n_tops:]
     size = low.shape[0]
     half = size // 2
     for mine, got, away, stay in ((low, low_got, low_away, low_stay), (high, high_got, high_away, high_stay)):
         away[:half, :] = (mine[:half, :].astype(F32) + got[:half, :].astype(F32)).astype(BF16)
         stay[...] = (mine[half:, :].astype(F32) + got[half:size, :].astype(F32)).astype(BF16)
-    top = largest(top_ref, low_got, size, others)
-    low_away[half:, :] = pack_top(top)
-    top_out[...] = top
-
-
-def last_kernel(n_ctx, n_others, me_ref, low, low_got, high, high_got, top_ref, *refs):
-    others = refs[:n_others]
-    *outs, top_out = refs[n_others:]
+    if tops:
+        top = largest(tops, low_got, size)
+        top_out[0][...] = top
+        if low_away.shape[0] > half:
+            low_away[half:, :] = pack_top(top)
+
+
+def last_kernel(n_ctx, n_tops, me_ref, low, low_got, high, high_got, *refs):
+    tops = refs[:n_tops]
+    outs, top_out = refs[n_tops : n_tops + n_ctx], refs[n_tops + n_ctx :]
     size, hd = low.shape
     rows_set = size // n_ctx
-    top = largest(top_ref, low_got, size, others)
-    packed = pack_top(top)
+    if tops:
+        top = largest(tops, low_got, size)
+        top_out[0][...] = top
+        packed = pack_top(top)
     for b in range(n_ctx):
         part = pl.ds(pl.multiple_of((me_ref[0] ^ b) * rows_set, rows_set), rows_set)
-        for at, mine, got in ((0, low, low_got), (hd, high, high_got)):
+        for at, mine, got in ((0, low, low_got), (rows_set, high, high_got)):
             total = mine[part, :].astype(F32) + got[part, :].astype(F32)
-            outs[b][:rows_set, at : at + hd] = total.astype(outs[b].dtype)
-        if b > 0:
-            outs[b][rows_set:, :TOP_LANES] = packed
-            outs[b][rows_set:, TOP_LANES:] = jnp.zeros_like(packed)
-    top_out[...] = top
+            outs[b][at : at + rows_set, :] = total.astype(outs[b].dtype)
+        if b > 0 and tops:
+            outs[b][2 * rows_set :, :] = packed
 
 
 def final_kernel(sets, n_ctx, gain, me_dp_ref, me_ctx_ref, *refs):
     groups = [refs[chosen * n_ctx : (chosen + 1) * n_ctx] for chosen in range(sets)]
     top_ref, out_ref, scale_ref, all_tops = refs[sets * n_ctx :]
     n_dp, lanes = scale_ref.shape
-    rows_set = groups[0][0].shape[0]
+    rows_set, hd = groups[0][0].shape[0] // 2, groups[0][0].shape[1]
     scale = top_ref[...]
     for other in groups[-1][1:]:
-        scale = jnp.maximum(scale, unpack_top(other, rows_set))
+        scale = jnp.maximum(scale, unpack_top(other, 2 * rows_set))
     scale = scale + 1e-06
     all_tops[...] = scale
     scale_ref[...] = scale[:n_dp, :lanes]
@@ -438,13 +483,15 @@
     first = me_ctx_ref[0] * (sets * per_set)
     for chosen, group in enumerate(groups):
         for r in range(per_set):
-            part = slice(r * QROWS, (r + 1) * QROWS)
-            total = group[0][part, :]
-            for other in group[1:]:
-                total = total + other[part, :].astype(F32)
             mine = jnp.where(lane == first + (chosen * per_set + r), factors, 0.0)
+            factor = jnp.sum(mine, axis=1, keepdims=True)
             at = chosen * rows_set + r * QROWS
-            out_ref[at : at + QROWS, :] = total * jnp.sum(mine, axis=1, keepdims=True)
+            for h in range(2):
+                part = slice(h * rows_set + r * QROWS, h * rows_set + (r + 1) * QROWS)
+                total = group[0][part, :]
+                for other in group[1:]:
+                    total = total + other[part, :].astype(F32)
+                out_ref[at : at + QROWS, h * hd : (h + 1) * hd] = total * factor
 
 
 def local(n_dp, n_ctx, sets, span_order, queries, keys, values, out_grad, activations, error_feedback):
@@ -456,7 +503,6 @@
     me_dp = lax.axis_index("dp").astype(jnp.int32)[None]
     me_ctx = lax.axis_index("context").astype(jnp.int32)[None]
     bits = n_dp.bit_length() - 1
-    packed_rows = 3 * TOP_ROWS
 
     def swap_dp(x, mask):
         return lax.ppermute(x, "dp", xor_perm(n_dp, mask))
@@ -464,10 +510,11 @@
     def swap_ctx(x, mask):
         return lax.ppermute(x, "context", xor_perm(n_ctx, mask))
 
-    pairs = join(keys, values)
-    received = [swap_ctx(pairs, b) for b in range(1, n_ctx)]
-    acts, errors = prepare(activations, error_feedback[0, 0])
-    query_grad, own, parts = attention(me_ctx, span_order[0], queries, out_grad, keys, values, received, swap_ctx)
+    pairs = load_call(join_kernel, "join_keys_values", [keys, values], [shape((rows, width))], 4)[0]
+    own, parts, blocks, score_grads, last_part = attention(
+        me_ctx, span_order[0], queries, out_grad, pairs, swap_ctx, n_ctx
+    )
+    acts, errors = prepare(activations, error_feedback[0, 0], last_part)
 
     shrink = 1.0 / (n_dp * n_ctx)
     acts = acts.reshape(n_dp, n_ctx, sets, rows_set, rows)
@@ -503,53 +550,64 @@
     halves = []
     for chosen in range(sets):
         half = steps // 2 * tall
+        extra = TOP_ROWS if chosen == sets - 1 else 0
         *arrays, top = whole_call(
             functools.partial(keep_kernel, bits, shrink, chosen),
             "keep_tiles",
             [me_dp],
             [grads, got[chosen], top, acts, errors],
-            [shape((half + packed_rows, hd))] + [shape((half, hd))] * 3 + [tops],
+            [shape((half + extra, hd))] + [shape((half, hd))] * 3 + [tops],
             28,
             cost,
         )
-        halves.append((arrays, top))
-
+        halves.append(arrays)
+
+    gathered = [top, swap_dp(top, 1), swap_dp(top, 3)]
+    query_grad = query_gradients(blocks, score_grads, queries.shape[1], [top])
     groups = []
     for chosen in range(sets):
-        (low_away, low, high_away, high), top = halves[chosen]
+        low_away, low, high_away, high = halves[chosen]
+        extra = TOP_ROWS if chosen == sets - 1 else 0
         for stage in range(1, bits):
             low_got = swap_dp(low_away, 1 << stage)
             high_got = swap_dp(high_away, 1 << (bits - stage))
-            others = [swap_dp(top, mask) for mask in (1, 3)] if chosen == sets - 1 and stage == 1 else []
-            operands = [low, low_got, high, high_got, top, *others]
+            with_tops = extra > 0 or (chosen == 0 and stage == 1)
+            operands = [low, low_got, high, high_got] + (gathered if with_tops else [])
+            n_tops = len(operands) - 4
             size = low.shape[0]
             cost = (4 * size * hd, 12 * size * hd)
             if stage < bits - 1:
-                low_away, low, high_away, high, top = whole_call(
-                    functools.partial(add_kernel, len(others)),
+                low_away, low, high_away, high, *top_out = whole_call(
+                    functools.partial(add_kernel, n_tops),
                     "add_stage",
                     [],
                     operands,
-                    [shape((size // 2 + packed_rows, hd))] + [shape((size // 2, hd))] * 3 + [tops],
+                    [shape((size // 2 + extra, hd))] + [shape((size // 2, hd))] * 3 + [tops] * with_tops,
+                    16,
+                    cost,
+                    after=[query_grad] if chosen == 0 and stage == 1 else [],
+                )
+            else:
+                outs = whole_call(
+                    functools.partial(last_kernel, n_ctx, n_tops),
+                    "last_stage",
+                    [me_ctx],
+                    operands,
+                    [shape((2 * rows_set, hd), F32)]
+                    + [shape((2 * rows_set + extra, hd))] * (n_ctx - 1)
+                    + [tops] * with_tops,
                     16,
                     cost,
                 )
-            else:
-                mine, *away, top = whole_call(
-                    functools.partial(last_kernel, n_ctx, len(others)),
-                    "last_stage",
-                    [me_ctx],
-                    operands,
-                    [shape((rows_set, width), F32)] + [shape((rows_set + packed_rows, width))] * (n_ctx - 1) + [tops],
-                    16,
-                    cost,
-                )
-        groups.append([mine] + [swap_ctx(part, b + 1) for b, part in enumerate(away)])
+                mine, away, top_out = outs[0], outs[1:n_ctx], outs[n_ctx:]
+            if with_tops:
+                gathered = list(top_out)
+        groups.append([mine] + [swap_ctx(away[b - 1], b) for b in range(n_ctx - 1, 0, -1)])
     payload, scale = whole_call(
         functools.partial(final_kernel, sets, n_ctx, 7.0 / shrink),
         "final_stage",
         [me_dp, me_ctx],
-        [x for group in groups for x in group] + [top],
+        [x for group in groups for x in group] + gathered,
         [shape((sets * rows_set, width), F32), shape((n_dp, sets * tall // QROWS), F32)],
         8,
         (4 * sets * tall * width, 16 * sets * rows_set * width),

time: 104 us -> 96.8 us (0.931)
  Pallas kernels: 43.3 us -> 32.1 us
  local copies, waits for them, and re-layouts: 5.22 us -> 9.42 us
  starting transfers between devices: 27.3 us -> 29.8 us
  waiting for transfers between devices: 25.9 us -> 23.9 us
    pallas_call x18 -> x20, Pallas kernels: 39 us -> 28.2 us  [the longest x19 28.1 us: whole_call(): pl.pallas_call(body, grid_spec=pltpu.PrefetchScalarGridSpec(num_scalar_pr...]
    unnamed x16 -> x32, local copies, waits for them, and re-layouts: 4.59 us -> 8.79 us
    ppermute x12, waiting for transfers between devices: 15.8 us -> 12.3 us  [swap_ctx(): return lax.ppermute(x, 'context', xor_perm(n_ctx, mask))]
    ppermute x12, starting transfers between devices: 16.7 us -> 20 us  [swap_ctx(): return lax.ppermute(x, 'context', xor_perm(n_ctx, mask))]
    ppermute x12, waiting for transfers between devices: 10 us -> 11.5 us  [swap_dp(): return lax.ppermute(x, 'dp', xor_perm(n_dp, mask))]
  transfers between devices with their start and end apart: 24 -> 24, of which waited for: 8 -> 7; matrix products, arithmetic and copies ran while one was open for 0% -> 0% of each run, Pallas kernels for 33% -> 25%
where the time goes in v5:
time: 96.8 us; the launch traced here: 96.2 us
  Pallas kernels  32.1 us (33%)
  starting transfers between devices  29.8 us (31%)
  waiting for transfers between devices  23.9 us (25%)
  local copies, waits for them, and re-layouts  9.42 us (10%)
    pallas_call x19, Pallas kernels, whole_call(): pl.pallas_call(body, grid_spec=pltpu.PrefetchScalarGridSpec(num_scalar_pr...  28.1 us
    ppermute x12, starting transfers between devices, swap_ctx(): return lax.ppermute(x, 'context', xor_perm(n_ctx, mask))  20 us
    ppermute x12, waiting for transfers between devices, swap_ctx(): return lax.ppermute(x, 'context', xor_perm(n_ctx, mask))  12.3 us
    ppermute x12, waiting for transfers between devices, swap_dp(): return lax.ppermute(x, 'dp', xor_perm(n_dp, mask))  11.5 us
    ppermute x12, starting transfers between devices, swap_dp(): return lax.ppermute(x, 'dp', xor_perm(n_dp, mask))  9.8 us
    unnamed x32, local copies, waits for them, and re-layouts  8.79 us
    pallas_call x1, Pallas kernels, prepare(): pl.pallas_call(functools.partial(prepare_kernel, pieces), in_specs=[hbm,...  3.97 us
  transfers between devices with their start and end apart: 24, of which 7 were waited for; matrix products, arithmetic and copies ran while one was open for 0% of the time, Pallas kernels for 25%

profile of v5, /device:TPU:0, one launch (start us, length us, event | category | flops | bytes accessed | tf_op | source)
XLA Modules:
  0.0 96.2 jit_solution(16297649428314484461)
XLA Ops:
  2.5 3.1 %collective-permute-start = (bf16[384,256]{1,0:T(8,128)(2,1)S(1)}, bf16[384,256]{1,0:T(8,128)(2,1)S(1)}, u32[]{:S(2)}, u32[]{:S(2)}) collective-permute-start(bf16[384,256]{1,0:T(8,128)(2,1)S(1)} %join_keys_values.1.refs_4_.refs_5_.refs_0_), channel_id=1, source_target_pairs={{0,1},{1,0},{2,3},{3,2},{4,5},{5,4},{6,7},{7,6},{8,9},{9,8},{10,11... | collective-permute-start | bytes 589832 | tf_op jit(solution)/shard_map/ppermute | solution.py:511
  5.6 2.6 %collective-permute-start.1 = (bf16[384,256]{1,0:T(8,128)(2,1)S(1)}, bf16[384,256]{1,0:T(8,128)(2,1)S(1)}, u32[]{:S(2)}, u32[]{:S(2)}) collective-permute-start(bf16[384,256]{1,0:T(8,128)(2,1)S(1)} %join_keys_values.1.refs_4_.refs_5_.refs_0_), channel_id=1, source_target_pairs={{0,2},{1,3},{2,0},{3,1},{4,6},{5,7},{6,4},{7,5},{8,10},{9,11},{10,... | collective-permute-start | bytes 589832 | tf_op jit(solution)/shard_map/ppermute | solution.py:511
  8.2 1.1 %copy-done.3 = bf16[384,1024]{1,0:T(8,128)(2,1)S(1)} copy-done((bf16[384,1024]{1,0:T(8,128)(2,1)S(1)}, bf16[384,1024]{1,0:T(8,128)(2,1)}, u32[]{:S(2)}) %copy-start.3) | copy-done | bytes 786456
  9.3 1.1 %copy-done.7 = bf16[384,1024]{1,0:T(8,128)(2,1)S(1)} copy-done((bf16[384,1024]{1,0:T(8,128)(2,1)S(1)}, bf16[384,1024]{1,0:T(8,128)(2,1)}, u32[]{:S(2)}) %copy-start.7) | copy-done | bytes 786456
  11.1 2.3 %block_stats.4.refs_5_ = f32[8,3072]{1,0:T(8,128)S(1)} custom-call(s32[1]{0:T(128)} %bitcast.refs_0_.refs_1_, s32[4]{0:T(128)S(1)} %bitcast.16, bf16[384,1024]{1,0:T(8,128)(2,1)S(1)} %copy-done.3, bf16[384,1024]{1,0:T(8,128)(2,1)S(1)} %copy-done.7, bf16[384,256]{1,0:T(8,128)(2,1)S(1)} %join_keys_values.1.refs_4_.refs_5_.refs_0_), custom_call_target="tpu_custom_call" | custom-call | flops 1207959552 | bytes 3145728 | tf_op jit(solution)/shard_map/block_stats/pallas_call | solution.py:39
  13.4 1.1 %collective-permute-done.refs_4_.refs_5_.refs_1_ = bf16[384,256]{1,0:T(8,128)(2,1)S(1)} collective-permute-done((bf16[384,256]{1,0:T(8,128)(2,1)S(1)}, bf16[384,256]{1,0:T(8,128)(2,1)S(1)}, u32[]{:S(2)}, u32[]{:S(2)}) %collective-permute-start) | collective-permute-done | bytes 196640 | tf_op jit(solution)/shard_map/ppermute | solution.py:511
  14.6 1.1 %copy-done.4 = bf16[384,1024]{1,0:T(8,128)(2,1)S(1)} copy-done((bf16[384,1024]{1,0:T(8,128)(2,1)S(1)}, bf16[384,1024]{1,0:T(8,128)(2,1)}, u32[]{:S(2)}) %copy-start.4) | copy-done | bytes 786456
  15.7 1.1 %copy-done.8 = bf16[384,1024]{1,0:T(8,128)(2,1)S(1)} copy-done((bf16[384,1024]{1,0:T(8,128)(2,1)S(1)}, bf16[384,1024]{1,0:T(8,128)(2,1)}, u32[]{:S(2)}) %copy-start.8) | copy-done | bytes 786456
  17.5 2.6 %block_stats.5.refs_1_.refs_5_ = f32[8,3072]{1,0:T(8,128)S(1)} custom-call(s32[1]{0:T(128)} %bitcast.refs_0_.refs_1_, s32[4]{0:T(128)S(1)} %bitcast.17, bf16[384,1024]{1,0:T(8,128)(2,1)S(1)} %copy-done.4, bf16[384,1024]{1,0:T(8,128)(2,1)S(1)} %copy-done.8, bf16[384,256]{1,0:T(8,128)(2,1)S(1)} %collective-permute-done.refs_4_.refs_5_.refs_1_, ...), custom_call_target="tpu_custom_call" | custom-call | flops 1207959552 | bytes 3145728 | tf_op jit(solution)/shard_map/block_stats/pallas_call | solution.py:39
  20.9 5.2 %collective-permute-done.2.refs_4_.refs_5_.refs_3_ = bf16[384,256]{1,0:T(8,128)(2,1)S(1)} collective-permute-done((bf16[384,256]{1,0:T(8,128)(2,1)S(1)}, bf16[384,256]{1,0:T(8,128)(2,1)S(1)}, u32[]{:S(2)}, u32[]{:S(2)}) %collective-permute-start.2) | collective-permute-done | bytes 196640 | tf_op jit(solution)/shard_map/ppermute | solution.py:511
  26.1 2.6 %block_stats.7.refs_2_ = f32[8,3072]{1,0:T(8,128)S(1)} custom-call(s32[1]{0:T(128)} %bitcast.refs_0_.refs_1_, s32[4]{0:T(128)S(1)} %bitcast.19, bf16[384,1024]{1,0:T(8,128)(2,1)S(1)} %copy-done.5, bf16[384,1024]{1,0:T(8,128)(2,1)S(1)} %copy-done.9, bf16[384,256]{1,0:T(8,128)(2,1)S(1)} %collective-permute-done.2.refs_4_.refs_5_.refs_3_, ...), custom_call_target="tpu_custom_call" | custom-call | flops 1207959552 | bytes 3145728 | tf_op jit(solution)/shard_map/block_stats/pallas_call | solution.py:39
  28.7 3.2 %block_gradients.3 = (bf16[384,256]{1,0:T(8,128)(2,1)S(1)}, bf16[384,3072]{1,0:T(8,128)(2,1)S(1)}) custom-call(s32[1]{0:T(128)} %bitcast.refs_0_.refs_1_, s32[4]{0:T(128)S(1)} %bitcast.20, f32[8,3072]{1,0:T(8,128)S(1)} %block_stats.7.refs_2_, bf16[384,1024]{1,0:T(8,128)(2,1)S(1)} %copy-done.5, bf16[384,1024]{1,0:T(8,128)(2,1)S(1)} %copy-done.9, ...), custom_call_target="tpu_custom_call" | custom-call | flops 2415919104 | bytes 6291456 | tf_op jit(solution)/shard_map/block_gradients/pallas_call | solution.py:39
  32.9 4.0 %collective-permute-start.4 = (bf16[384,256]{1,0:T(8,128)(2,1)S(1)}, bf16[384,256]{1,0:T(8,128)(2,1)S(1)}, u32[]{:S(2)}, u32[]{:S(2)}) collective-permute-start(bf16[384,256]{1,0:T(8,128)(2,1)S(1)} %get-tuple-element.54.refs_6_), channel_id=1, source_target_pairs={{0,2},{1,3},{2,0},{3,1},{4,6},{5,7},{6,4},{7,5},{8,10},{9,11},{10,... | collective-permute-start | bytes 589832 | tf_op jit(solution)/shard_map/ppermute | solution.py:511
  36.9 3.2 %block_gradients.5 = (bf16[384,256]{1,0:T(8,128)(2,1)S(1)}, bf16[384,3072]{1,0:T(8,128)(2,1)S(1)}) custom-call(s32[1]{0:T(128)} %bitcast.refs_0_.refs_1_, s32[4]{0:T(128)S(1)} %bitcast.22, f32[8,3072]{1,0:T(8,128)S(1)} %block_stats.7.refs_2_, bf16[384,1024]{1,0:T(8,128)(2,1)S(1)} %copy-done.6, bf16[384,1024]{1,0:T(8,128)(2,1)S(1)} %copy-done.10, ...), custom_call_target="tpu_custom_call" | custom-call | flops 2415919104 | bytes 6291456 | tf_op jit(solution)/shard_map/block_gradients/pallas_call | solution.py:39
  40.2 4.0 %prepare.1 = (bf16[8192,384]{1,0:T(8,128)(2,1)S(1)}, f32[8192,256]{1,0:T(8,128)S(1)}) custom-call(bf16[384,8192]{1,0:T(8,128)(2,1)S(1)} %bitcast.15, f32[8192,256]{1,0:T(8,128)} %bitcast.24, bf16[384,256]{1,0:T(8,128)(2,1)S(1)} %get-tuple-element.55.refs_6_._), custom_call_target="tpu_custom_call" | custom-call | bytes 14680064 | tf_op jit(solution)/shard_map/prepare/pallas_call | solution.py:101
  44.2 3.2 %own_gradients.1 = (f32[384,256]{1,0:T(8,128)S(1)}, bf16[384,3072]{1,0:T(8,128)(2,1)S(1)}) custom-call(s32[1]{0:T(128)} %bitcast.refs_0_.refs_1_, s32[4]{0:T(128)S(1)} %bitcast.23, f32[8,3072]{1,0:T(8,128)S(1)} %block_stats.7.refs_2_, bf16[384,1024]{1,0:T(8,128)(2,1)S(1)} %copy-done.6, bf16[384,1024]{1,0:T(8,128)(2,1)S(1)} %copy-done.10, ...), custom_call_target="tpu_custom_call" | custom-call | flops 2415919104 | bytes 6291456 | tf_op jit(solution)/shard_map/own_gradients/pallas_call | solution.py:39
  47.4 2.1 %collective-permute-done.4.refs_3_ = bf16[384,256]{1,0:T(8,128)(2,1)S(1)} collective-permute-done((bf16[384,256]{1,0:T(8,128)(2,1)S(1)}, bf16[384,256]{1,0:T(8,128)(2,1)S(1)}, u32[]{:S(2)}, u32[]{:S(2)}) %collective-permute-start.4) | collective-permute-done | bytes 196640 | tf_op jit(solution)/shard_map/ppermute | solution.py:511
  49.5 1.3 %send_tiles.2 = (bf16[4,512,256]{2,1,0:T(8,128)(2,1)S(1)}, f32[16,128]{1,0:T(8,128)S(1)}, bf16[384,128]{1,0:T(8,128)(2,1)}, bf16[384,128]{1,0:T(8,128)(2,1)}, bf16[384,256]{1,0:T(8,128)(2,1)S(1)}) custom-call(s32[1]{0:T(128)} %bitcast.2.refs_0_, f32[384,256]{1,0:T(8,128)S(1)} %get-tuple-element.60.refs_1_, ...), custom_call_target="tpu_custom_call" | custom-call | flops 402653184 | bytes 4718592 | tf_op jit(solution)/shard_map/send_tiles/pallas_call | solution.py:39
  52.2 1.2 %collective-permute-done.7.refs_2_ = bf16[4,512,256]{2,1,0:T(8,128)(2,1)S(1)} collective-permute-done((bf16[4,512,256]{2,1,0:T(8,128)(2,1)S(1)}, bf16[4,512,256]{2,1,0:T(8,128)(2,1)S(1)}, u32[]{:S(2)}, u32[]{:S(2)}) %collective-permute-start.7) | collective-permute-done | bytes 1048608 | tf_op jit(solution)/shard_map/ppermute | solution.py:508
  54.4 1.2 %collective-permute-start.8 = (bf16[1024,128]{1,0:T(8,128)(2,1)S(1)}, bf16[1024,128]{1,0:T(8,128)(2,1)S(1)}, u32[]{:S(2)}, u32[]{:S(2)}) collective-permute-start(bf16[1024,128]{1,0:T(8,128)(2,1)S(1)} %get-tuple-element.73), channel_id=1, source_target_pairs={{0,8},{4,12},{8,0},{12,4},{16,24},{20,28},{24,16},{28,20},{1,9},{5... | collective-permute-start | bytes 786440 | tf_op jit(solution)/shard_map/ppermute | solution.py:508
  57.8 1.7 %collective-permute-start.18 = (bf16[1024,128]{1,0:T(8,128)(2,1)S(1)}, bf16[1024,128]{1,0:T(8,128)(2,1)S(1)}, u32[]{:S(2)}, u32[]{:S(2)}) collective-permute-start(bf16[1024,128]{1,0:T(8,128)(2,1)S(1)} %get-tuple-element.87), channel_id=1, source_target_pairs={{0,16},{4,20},{8,24},{12,28},{16,0},{20,4},{24,8},{28,12},{1,17},{... | collective-permute-start | bytes 786440 | tf_op jit(solution)/shard_map/ppermute | solution.py:508
  59.6 8.3 %collective-permute-done.11.refs_6_ = f32[16,128]{1,0:T(8,128)S(1)} collective-permute-done((f32[16,128]{1,0:T(8,128)S(1)}, f32[16,128]{1,0:T(8,128)S(1)}, u32[]{:S(2)}, u32[]{:S(2)}) %collective-permute-start.11) | collective-permute-done | bytes 8224 | tf_op jit(solution)/shard_map/ppermute | solution.py:508
  68.8 3.8 %query_gradients.1.refs_7_ = bf16[384,1024]{1,0:T(8,128)(2,1)} custom-call(bf16[384,256]{1,0:T(8,128)(2,1)S(1)} %join_keys_values.1.refs_4_.refs_5_.refs_0_, bf16[384,256]{1,0:T(8,128)(2,1)S(1)} %collective-permute-done.refs_4_.refs_5_.refs_1_, bf16[384,256]{1,0:T(8,128)(2,1)S(1)} %collective-permute-done.1.refs_0_.refs_4_.refs_5_.refs_2_, ...), custom_call_target="tpu_custom_call" | custom-call | flops 1207959552 | bytes 6291456 | tf_op jit(solution)/shard_map/query_gradients/pallas_call | solution.py:39
  72.6 1.1 %copy-done = bf16[384,1024]{1,0:T(8,128)(2,1)S(1)} copy-done((bf16[384,1024]{1,0:T(8,128)(2,1)S(1)}, bf16[384,1024]{1,0:T(8,128)(2,1)}, u32[]{:S(2)}) %copy-start) | copy-done | bytes 786456
  74.2 1.3 %collective-permute-start.13 = (bf16[512,128]{1,0:T(8,128)(2,1)S(1)}, bf16[512,128]{1,0:T(8,128)(2,1)S(1)}, u32[]{:S(2)}, u32[]{:S(2)}) collective-permute-start(bf16[512,128]{1,0:T(8,128)(2,1)S(1)} %get-tuple-element.79), channel_id=1, source_target_pairs={{0,8},{4,12},{8,0},{12,4},{16,24},{20,28},{24,16},{28,20},{1,9},{5... | collective-permute-start | bytes 393224 | tf_op jit(solution)/shard_map/ppermute | solution.py:508
  75.8 1.7 %collective-permute-start.19 = (bf16[528,128]{1,0:T(8,128)(2,1)S(1)}, bf16[528,128]{1,0:T(8,128)(2,1)S(1)}, u32[]{:S(2)}, u32[]{:S(2)}) collective-permute-start(bf16[528,128]{1,0:T(8,128)(2,1)S(1)} %get-tuple-element.90), channel_id=1, source_target_pairs={{0,16},{4,20},{8,24},{12,28},{16,0},{20,4},{24,8},{28,12},{1,17},{... | collective-permute-start | bytes 405512 | tf_op jit(solution)/shard_map/ppermute | solution.py:508
  78.3 2.0 %collective-permute-done.12.refs_2_ = bf16[512,128]{1,0:T(8,128)(2,1)S(1)} collective-permute-done((bf16[512,128]{1,0:T(8,128)(2,1)S(1)}, bf16[512,128]{1,0:T(8,128)(2,1)S(1)}, u32[]{:S(2)}, u32[]{:S(2)}) %collective-permute-start.12) | collective-permute-done | bytes 131104 | tf_op jit(solution)/shard_map/ppermute | solution.py:508
  80.4 3.5 %collective-permute-start.14 = (bf16[256,128]{1,0:T(8,128)(2,1)S(1)}, bf16[256,128]{1,0:T(8,128)(2,1)S(1)}, u32[]{:S(2)}, u32[]{:S(2)}) collective-permute-start(bf16[256,128]{1,0:T(8,128)(2,1)S(1)} %get-tuple-element.81), channel_id=1, source_target_pairs={{0,3},{1,2},{2,1},{3,0},{4,7},{5,6},{6,5},{7,4},{8,11},{9,10},{10,... | collective-permute-start | bytes 196616 | tf_op jit(solution)/shard_map/ppermute | solution.py:511
  84.1 1.6 %collective-permute-start.21 = (bf16[272,128]{1,0:T(8,128)(2,1)S(1)}, bf16[272,128]{1,0:T(8,128)(2,1)S(1)}, u32[]{:S(2)}, u32[]{:S(2)}) collective-permute-start(bf16[272,128]{1,0:T(8,128)(2,1)S(1)} %get-tuple-element.95), channel_id=1, source_target_pairs={{0,3},{1,2},{2,1},{3,0},{4,7},{5,6},{6,5},{7,4},{8,11},{9,10},{10,... | collective-permute-start | bytes 208904 | tf_op jit(solution)/shard_map/ppermute | solution.py:511
  85.8 2.8 %collective-permute-start.23 = (bf16[272,128]{1,0:T(8,128)(2,1)S(1)}, bf16[272,128]{1,0:T(8,128)(2,1)S(1)}, u32[]{:S(2)}, u32[]{:S(2)}) collective-permute-start(bf16[272,128]{1,0:T(8,128)(2,1)S(1)} %get-tuple-element.97), channel_id=1, source_target_pairs={{0,1},{1,0},{2,3},{3,2},{4,5},{5,4},{6,7},{7,6},{8,9},{9,8},{10,11... | collective-permute-start | bytes 208904 | tf_op jit(solution)/shard_map/ppermute | solution.py:511
  88.7 2.0 %collective-permute-start.16 = (bf16[256,128]{1,0:T(8,128)(2,1)S(1)}, bf16[256,128]{1,0:T(8,128)(2,1)S(1)}, u32[]{:S(2)}, u32[]{:S(2)}) collective-permute-start(bf16[256,128]{1,0:T(8,128)(2,1)S(1)} %get-tuple-element.83), channel_id=1, source_target_pairs={{0,1},{1,0},{2,3},{3,2},{4,5},{5,4},{6,7},{7,6},{8,9},{9,8},{10,11... | collective-permute-start | bytes 196616 | tf_op jit(solution)/shard_map/ppermute | solution.py:511
  90.7 3.9 %collective-permute-done.15.refs_4_ = bf16[256,128]{1,0:T(8,128)(2,1)S(1)} collective-permute-done((bf16[256,128]{1,0:T(8,128)(2,1)S(1)}, bf16[256,128]{1,0:T(8,128)(2,1)S(1)}, u32[]{:S(2)}, u32[]{:S(2)}) %collective-permute-start.15) | collective-permute-done | bytes 65568 | tf_op jit(solution)/shard_map/ppermute | solution.py:511
  (71 shorter events, 13.9 us)
Async XLA Ops:
  2.4 17.8 %copy-start.13 = (s32[1,4]{1,0:T(1,128)S(1)}, s32[1,4]{1,0:T(1,128)}, u32[]{:S(2)}) copy-start(s32[1,4]{1,0:T(1,128)} %param.7) | copy-start | bytes 52
  2.5 12.1 %collective-permute-start = (bf16[384,256]{1,0:T(8,128)(2,1)S(1)}, bf16[384,256]{1,0:T(8,128)(2,1)S(1)}, u32[]{:S(2)}, u32[]{:S(2)}) collective-permute-start(bf16[384,256]{1,0:T(8,128)(2,1)S(1)} %join_keys_values.1.refs_4_.refs_5_.refs_0_), channel_id=1, source_target_pairs={{0,1},{1,0},{2,3},{3,2},{4,5},{5,4},{6,7},{7,6},{8,9},{9,8},{10,11... | collective-permute-start | bytes 589832 | tf_op jit(solution)/shard_map/ppermute | solution.py:511
  5.6 14.6 %collective-permute-start.1 = (bf16[384,256]{1,0:T(8,128)(2,1)S(1)}, bf16[384,256]{1,0:T(8,128)(2,1)S(1)}, u32[]{:S(2)}, u32[]{:S(2)}) collective-permute-start(bf16[384,256]{1,0:T(8,128)(2,1)S(1)} %join_keys_values.1.refs_4_.refs_5_.refs_0_), channel_id=1, source_target_pairs={{0,2},{1,3},{2,0},{3,1},{4,6},{5,7},{6,4},{7,5},{8,10},{9,11},{10,... | collective-permute-start | bytes 589832 | tf_op jit(solution)/shard_map/ppermute | solution.py:511
  11.1 9.2 %copy-start.5 = (bf16[384,1024]{1,0:T(8,128)(2,1)S(1)}, bf16[384,1024]{1,0:T(8,128)(2,1)}, u32[]{:S(2)}) copy-start(bf16[384,1024]{1,0:T(8,128)(2,1)} %refs_3_.15) | copy-start | bytes 2359300
  11.1 9.2 %copy-start.9 = (bf16[384,1024]{1,0:T(8,128)(2,1)S(1)}, bf16[384,1024]{1,0:T(8,128)(2,1)}, u32[]{:S(2)}) copy-start(bf16[384,1024]{1,0:T(8,128)(2,1)} %refs_4_.7) | copy-start | bytes 2359300
  20.2 5.9 %collective-permute-start.2 = (bf16[384,256]{1,0:T(8,128)(2,1)S(1)}, bf16[384,256]{1,0:T(8,128)(2,1)S(1)}, u32[]{:S(2)}, u32[]{:S(2)}) collective-permute-start(bf16[384,256]{1,0:T(8,128)(2,1)S(1)} %relay.1), channel_id=1, source_target_pairs={{0,1},{1,0},{2,3},{3,2},{4,5},{5,4},{6,7},{7,6},{8,9},{9,8},{10,11... | collective-permute-start | bytes 589832 | tf_op jit(solution)/shard_map/ppermute | solution.py:511
  20.9 11.1 %copy-start.6 = (bf16[384,1024]{1,0:T(8,128)(2,1)S(1)}, bf16[384,1024]{1,0:T(8,128)(2,1)}, u32[]{:S(2)}) copy-start(bf16[384,1024]{1,0:T(8,128)(2,1)} %refs_3_.15) | copy-start | bytes 2359300
  20.9 11.1 %copy-start.10 = (bf16[384,1024]{1,0:T(8,128)(2,1)S(1)}, bf16[384,1024]{1,0:T(8,128)(2,1)}, u32[]{:S(2)}) copy-start(bf16[384,1024]{1,0:T(8,128)(2,1)} %refs_4_.7) | copy-start | bytes 2359300
  31.9 15.5 %collective-permute-start.5 = (bf16[384,256]{1,0:T(8,128)(2,1)S(1)}, bf16[384,256]{1,0:T(8,128)(2,1)S(1)}, u32[]{:S(2)}, u32[]{:S(2)}) collective-permute-start(bf16[384,256]{1,0:T(8,128)(2,1)S(1)} %get-tuple-element.53.refs_6_), channel_id=1, source_target_pairs={{0,3},{1,2},{2,1},{3,0},{4,7},{5,6},{6,5},{7,4},{8,11},{9,10},{10,... | collective-permute-start | bytes 589832 | tf_op jit(solution)/shard_map/ppermute | solution.py:511
  32.0 8.2 %slice-start = ((s8[6291456]{0:T(1024)(128)(4,1)}), s8[4194304]{0:T(1024)(128)(4,1)S(1)}, s32[]{:S(2)}) async-start(s8[6291456]{0:T(1024)(128)(4,1)} %bitcast.14), calls=%async_computation | async-start | bytes 8388608
  32.9 7.3 %slice-start.1 = ((s8[6291456]{0:T(1024)(128)(4,1)}), s8[2097152]{0:T(1024)(128)(4,1)S(1)}, s32[]{:S(2)}) async-start(s8[6291456]{0:T(1024)(128)(4,1)} %bitcast.14), calls=%async_computation.1 | async-start | bytes 4194304
  32.9 16.6 %collective-permute-start.4 = (bf16[384,256]{1,0:T(8,128)(2,1)S(1)}, bf16[384,256]{1,0:T(8,128)(2,1)S(1)}, u32[]{:S(2)}, u32[]{:S(2)}) collective-permute-start(bf16[384,256]{1,0:T(8,128)(2,1)S(1)} %get-tuple-element.54.refs_6_), channel_id=1, source_target_pairs={{0,2},{1,3},{2,0},{3,1},{4,6},{5,7},{6,4},{7,5},{8,10},{9,11},{10,... | collective-permute-start | bytes 589832 | tf_op jit(solution)/shard_map/ppermute | solution.py:511
  40.1 9.4 %collective-permute-start.3 = (bf16[384,256]{1,0:T(8,128)(2,1)S(1)}, bf16[384,256]{1,0:T(8,128)(2,1)S(1)}, u32[]{:S(2)}, u32[]{:S(2)}) collective-permute-start(bf16[384,256]{1,0:T(8,128)(2,1)S(1)} %get-tuple-element.55.refs_6_._), channel_id=1, source_target_pairs={{0,1},{1,0},{2,3},{3,2},{4,5},{5,4},{6,7},{7,6},{8,9},{9,8},{10,11... | collective-permute-start | bytes 589832 | tf_op jit(solution)/shard_map/ppermute | solution.py:511
  50.8 2.7 %collective-permute-start.7 = (bf16[4,512,256]{2,1,0:T(8,128)(2,1)S(1)}, bf16[4,512,256]{2,1,0:T(8,128)(2,1)S(1)}, u32[]{:S(2)}, u32[]{:S(2)}) collective-permute-start(bf16[4,512,256]{2,1,0:T(8,128)(2,1)S(1)} %get-tuple-element.66), channel_id=1, source_target_pairs={{0,4},{4,0},{8,12},{12,8},{16,20},{20,16},{24,28},{28,24},{1,5},{5... | collective-permute-start | bytes 3145736 | tf_op jit(solution)/shard_map/ppermute | solution.py:508
  51.7 4.4 %collective-permute-start.6 = (bf16[4,512,256]{2,1,0:T(8,128)(2,1)S(1)}, bf16[4,512,256]{2,1,0:T(8,128)(2,1)S(1)}, u32[]{:S(2)}, u32[]{:S(2)}) collective-permute-start(bf16[4,512,256]{2,1,0:T(8,128)(2,1)S(1)} %get-tuple-element.65), channel_id=1, source_target_pairs={{0,4},{4,0},{8,12},{12,8},{16,20},{20,16},{24,28},{28,24},{1,5},{5... | collective-permute-start | bytes 3145736 | tf_op jit(solution)/shard_map/ppermute | solution.py:508
  54.4 18.2 %collective-permute-start.8 = (bf16[1024,128]{1,0:T(8,128)(2,1)S(1)}, bf16[1024,128]{1,0:T(8,128)(2,1)S(1)}, u32[]{:S(2)}, u32[]{:S(2)}) collective-permute-start(bf16[1024,128]{1,0:T(8,128)(2,1)S(1)} %get-tuple-element.73), channel_id=1, source_target_pairs={{0,8},{4,12},{8,0},{12,4},{16,24},{20,28},{24,16},{28,20},{1,9},{5... | collective-permute-start | bytes 786440 | tf_op jit(solution)/shard_map/ppermute | solution.py:508
  55.6 17.0 %collective-permute-start.9 = (bf16[1024,128]{1,0:T(8,128)(2,1)S(1)}, bf16[1024,128]{1,0:T(8,128)(2,1)S(1)}, u32[]{:S(2)}, u32[]{:S(2)}) collective-permute-start(bf16[1024,128]{1,0:T(8,128)(2,1)S(1)} %get-tuple-element.75), channel_id=1, source_target_pairs={{0,16},{4,20},{8,24},{12,28},{16,0},{20,4},{24,8},{28,12},{1,17},{... | collective-permute-start | bytes 786440 | tf_op jit(solution)/shard_map/ppermute | solution.py:508
  57.1 18.5 %collective-permute-start.17 = (bf16[1040,128]{1,0:T(8,128)(2,1)S(1)}, bf16[1040,128]{1,0:T(8,128)(2,1)S(1)}, u32[]{:S(2)}, u32[]{:S(2)}) collective-permute-start(bf16[1040,128]{1,0:T(8,128)(2,1)S(1)} %get-tuple-element.85), channel_id=1, source_target_pairs={{0,8},{4,12},{8,0},{12,4},{16,24},{20,28},{24,16},{28,20},{1,9},{5... | collective-permute-start | bytes 798728 | tf_op jit(solution)/shard_map/ppermute | solution.py:508
  57.8 17.7 %collective-permute-start.18 = (bf16[1024,128]{1,0:T(8,128)(2,1)S(1)}, bf16[1024,128]{1,0:T(8,128)(2,1)S(1)}, u32[]{:S(2)}, u32[]{:S(2)}) collective-permute-start(bf16[1024,128]{1,0:T(8,128)(2,1)S(1)} %get-tuple-element.87), channel_id=1, source_target_pairs={{0,16},{4,20},{8,24},{12,28},{16,0},{20,4},{24,8},{28,12},{1,17},{... | collective-permute-start | bytes 786440 | tf_op jit(solution)/shard_map/ppermute | solution.py:508
  59.6 8.3 %collective-permute-start.11 = (f32[16,128]{1,0:T(8,128)S(1)}, f32[16,128]{1,0:T(8,128)S(1)}, u32[]{:S(2)}, u32[]{:S(2)}) collective-permute-start(f32[16,128]{1,0:T(8,128)S(1)} %get-tuple-element.69.refs_8_.refs_4_), channel_id=1, source_target_pairs={{0,12},{4,8},{8,4},{12,0},{16,28},{20,24},{24,20},{28,16},{1,13},{... | collective-permute-start | bytes 24584 | tf_op jit(solution)/shard_map/ppermute | solution.py:508
  67.9 4.7 %collective-permute-start.10 = (f32[16,128]{1,0:T(8,128)S(1)}, f32[16,128]{1,0:T(8,128)S(1)}, u32[]{:S(2)}, u32[]{:S(2)}) collective-permute-start(f32[16,128]{1,0:T(8,128)S(1)} %get-tuple-element.69.refs_8_.refs_4_), channel_id=1, source_target_pairs={{0,4},{4,0},{8,12},{12,8},{16,20},{20,16},{24,28},{28,24},{1,5},{5... | collective-permute-start | bytes 24584 | tf_op jit(solution)/shard_map/ppermute | solution.py:508
  72.6 1.1 %copy-start = (bf16[384,1024]{1,0:T(8,128)(2,1)S(1)}, bf16[384,1024]{1,0:T(8,128)(2,1)}, u32[]{:S(2)}) copy-start(bf16[384,1024]{1,0:T(8,128)(2,1)} %query_gradients.1.refs_7_) | copy-start | bytes 2359300
  73.9 6.4 %collective-permute-start.12 = (bf16[512,128]{1,0:T(8,128)(2,1)S(1)}, bf16[512,128]{1,0:T(8,128)(2,1)S(1)}, u32[]{:S(2)}, u32[]{:S(2)}) collective-permute-start(bf16[512,128]{1,0:T(8,128)(2,1)S(1)} %get-tuple-element.77), channel_id=1, source_target_pairs={{0,16},{4,20},{8,24},{12,28},{16,0},{20,4},{24,8},{28,12},{1,17},{... | collective-permute-start | bytes 393224 | tf_op jit(solution)/shard_map/ppermute | solution.py:508
  74.2 6.1 %collective-permute-start.13 = (bf16[512,128]{1,0:T(8,128)(2,1)S(1)}, bf16[512,128]{1,0:T(8,128)(2,1)S(1)}, u32[]{:S(2)}, u32[]{:S(2)}) collective-permute-start(bf16[512,128]{1,0:T(8,128)(2,1)S(1)} %get-tuple-element.79), channel_id=1, source_target_pairs={{0,8},{4,12},{8,0},{12,4},{16,24},{20,28},{24,16},{28,20},{1,9},{5... | collective-permute-start | bytes 393224 | tf_op jit(solution)/shard_map/ppermute | solution.py:508
  75.8 8.2 %collective-permute-start.19 = (bf16[528,128]{1,0:T(8,128)(2,1)S(1)}, bf16[528,128]{1,0:T(8,128)(2,1)S(1)}, u32[]{:S(2)}, u32[]{:S(2)}) collective-permute-start(bf16[528,128]{1,0:T(8,128)(2,1)S(1)} %get-tuple-element.90), channel_id=1, source_target_pairs={{0,16},{4,20},{8,24},{12,28},{16,0},{20,4},{24,8},{28,12},{1,17},{... | collective-permute-start | bytes 405512 | tf_op jit(solution)/shard_map/ppermute | solution.py:508
  77.5 6.5 %collective-permute-start.20 = (bf16[512,128]{1,0:T(8,128)(2,1)S(1)}, bf16[512,128]{1,0:T(8,128)(2,1)S(1)}, u32[]{:S(2)}, u32[]{:S(2)}) collective-permute-start(bf16[512,128]{1,0:T(8,128)(2,1)S(1)} %get-tuple-element.92), channel_id=1, source_target_pairs={{0,8},{4,12},{8,0},{12,4},{16,24},{20,28},{24,16},{28,20},{1,9},{5... | collective-permute-start | bytes 393224 | tf_op jit(solution)/shard_map/ppermute | solution.py:508
  80.4 8.3 %collective-permute-start.14 = (bf16[256,128]{1,0:T(8,128)(2,1)S(1)}, bf16[256,128]{1,0:T(8,128)(2,1)S(1)}, u32[]{:S(2)}, u32[]{:S(2)}) collective-permute-start(bf16[256,128]{1,0:T(8,128)(2,1)S(1)} %get-tuple-element.81), channel_id=1, source_target_pairs={{0,3},{1,2},{2,1},{3,0},{4,7},{5,6},{6,5},{7,4},{8,11},{9,10},{10,... | collective-permute-start | bytes 196616 | tf_op jit(solution)/shard_map/ppermute | solution.py:511
  84.1 10.5 %collective-permute-start.21 = (bf16[272,128]{1,0:T(8,128)(2,1)S(1)}, bf16[272,128]{1,0:T(8,128)(2,1)S(1)}, u32[]{:S(2)}, u32[]{:S(2)}) collective-permute-start(bf16[272,128]{1,0:T(8,128)(2,1)S(1)} %get-tuple-element.95), channel_id=1, source_target_pairs={{0,3},{1,2},{2,1},{3,0},{4,7},{5,6},{6,5},{7,4},{8,11},{9,10},{10,... | collective-permute-start | bytes 208904 | tf_op jit(solution)/shard_map/ppermute | solution.py:511
  85.7 8.9 %collective-permute-start.22 = (bf16[272,128]{1,0:T(8,128)(2,1)S(1)}, bf16[272,128]{1,0:T(8,128)(2,1)S(1)}, u32[]{:S(2)}, u32[]{:S(2)}) collective-permute-start(bf16[272,128]{1,0:T(8,128)(2,1)S(1)} %get-tuple-element.96), channel_id=1, source_target_pairs={{0,2},{1,3},{2,0},{3,1},{4,6},{5,7},{6,4},{7,5},{8,10},{9,11},{10,... | collective-permute-start | bytes 208904 | tf_op jit(solution)/shard_map/ppermute | solution.py:511
  85.8 8.9 %collective-permute-start.23 = (bf16[272,128]{1,0:T(8,128)(2,1)S(1)}, bf16[272,128]{1,0:T(8,128)(2,1)S(1)}, u32[]{:S(2)}, u32[]{:S(2)}) collective-permute-start(bf16[272,128]{1,0:T(8,128)(2,1)S(1)} %get-tuple-element.97), channel_id=1, source_target_pairs={{0,1},{1,0},{2,3},{3,2},{4,5},{5,4},{6,7},{7,6},{8,9},{9,8},{10,11... | collective-permute-start | bytes 208904 | tf_op jit(solution)/shard_map/ppermute | solution.py:511
  88.6 6.0 %collective-permute-start.15 = (bf16[256,128]{1,0:T(8,128)(2,1)S(1)}, bf16[256,128]{1,0:T(8,128)(2,1)S(1)}, u32[]{:S(2)}, u32[]{:S(2)}) collective-permute-start(bf16[256,128]{1,0:T(8,128)(2,1)S(1)} %get-tuple-element.82), channel_id=1, source_target_pairs={{0,2},{1,3},{2,0},{3,1},{4,6},{5,7},{6,4},{7,5},{8,10},{9,11},{10,... | collective-permute-start | bytes 196616 | tf_op jit(solution)/shard_map/ppermute | solution.py:511
  88.7 5.9 %collective-permute-start.16 = (bf16[256,128]{1,0:T(8,128)(2,1)S(1)}, bf16[256,128]{1,0:T(8,128)(2,1)S(1)}, u32[]{:S(2)}, u32[]{:S(2)}) collective-permute-start(bf16[256,128]{1,0:T(8,128)(2,1)S(1)} %get-tuple-element.83), channel_id=1, source_target_pairs={{0,1},{1,0},{2,3},{3,2},{4,5},{5,4},{6,7},{7,6},{8,9},{9,8},{10,11... | collective-permute-start | bytes 196616 | tf_op jit(solution)/shard_map/ppermute | solution.py:511
  (8 other events, 7.6 us)

commit v6 on v5

--- a/solution.py
+++ b/solution.py
@@ -108,7 +108,7 @@
             pltpu.SemaphoreType.DMA((pieces,)),
             pltpu.SemaphoreType.DMA((pieces,)),
         ],
-        compiler_params=pltpu.CompilerParams(vmem_limit_bytes=28 * MIB),
+        compiler_params=pltpu.CompilerParams(vmem_limit_bytes=24 * MIB),
         cost_estimate=pl.CostEstimate(
             flops=0, bytes_accessed=2 * rows * model + 4 * errors.size, transcendentals=0
         ),
@@ -140,53 +140,64 @@
     return s, dp
 
 
-def counted(b, me_ref, span_ref):
+def counted(b, flags):
+    lane = lax.broadcasted_iota(jnp.int32, flags.shape, 1)
+    return jnp.max(jnp.where(lane == b, flags[...], 0.0)) > 0.5
+
+
+def stats_of_block(b, q_ref, do_ref, kv, before, out):
+    k, v = key_value(kv)
+    rows, hd = k.shape
+    pair = 2 * rows
+    factor = LOG2E / hd**0.5
+
+    def heads(i, carry):
+        q, do = head_pair(q_ref, i, hd), head_pair(do_ref, i, hd)
+        for t in range(pair // CHUNK):
+            part = slice(t * CHUNK, (t + 1) * CHUNK)
+            lanes = pl.ds(pl.multiple_of(i * pair + t * CHUNK, CHUNK), CHUNK)
+            s, dp = score_chunk(k, v, q[part], do[part], b == 0, t * CHUNK)
+            top = jnp.max(s, axis=0, keepdims=True) * factor
+            e = jnp.exp2(s * factor - top)
+            total = jnp.sum(e, axis=0, keepdims=True)
+            weighted = jnp.sum(e * dp, axis=0, keepdims=True)
+            if b > 0:
+                old = before[0:1, lanes]
+                both = jnp.maximum(old, top)
+                old_part, new_part = jnp.exp2(old - both), jnp.exp2(top - both)
+                total = before[1:2, lanes] * old_part + total * new_part
+                weighted = before[2:3, lanes] * old_part + weighted * new_part
+                top = both
+            out[0:1, lanes] = top
+            out[1:2, lanes] = total
+            out[2:3, lanes] = weighted
+        return carry
+
+    lax.fori_loop(0, q_ref.shape[1] // (2 * hd), heads, 0, unroll=True)
+
+
+def first_stats_kernel(n, me_ref, span_ref, q_ref, do_ref, kv, out, q_out, do_out, flags):
     me = me_ref[0]
-    return span_ref[me ^ b] < span_ref[me]
-
-
-def stats_kernel(b, me_ref, span_ref, q_ref, do_ref, kv, *refs):
-    before, out = refs[0], refs[-1]
-
-    def run():
-        k, v = key_value(kv)
-        rows, hd = k.shape
-        pair = 2 * rows
-        factor = LOG2E / hd**0.5
-
-        def heads(i, carry):
-            q, do = head_pair(q_ref, i, hd), head_pair(do_ref, i, hd)
-            for t in range(pair // CHUNK):
-                part = slice(t * CHUNK, (t + 1) * CHUNK)
-                lanes = pl.ds(pl.multiple_of(i * pair + t * CHUNK, CHUNK), CHUNK)
-                s, dp = score_chunk(k, v, q[part], do[part], b == 0, t * CHUNK)
-                top = jnp.max(s, axis=0, keepdims=True) * factor
-                e = jnp.exp2(s * factor - top)
-                total = jnp.sum(e, axis=0, keepdims=True)
-                weighted = jnp.sum(e * dp, axis=0, keepdims=True)
-                if b > 0:
-                    old = before[0:1, lanes]
-                    both = jnp.maximum(old, top)
-                    old_part, new_part = jnp.exp2(old - both), jnp.exp2(top - both)
-                    total = before[1:2, lanes] * old_part + total * new_part
-                    weighted = before[2:3, lanes] * old_part + weighted * new_part
-                    top = both
-                out[0:1, lanes] = top
-                out[1:2, lanes] = total
-                out[2:3, lanes] = weighted
-            return carry
-
-        lax.fori_loop(0, q_ref.shape[1] // (2 * hd), heads, 0, unroll=True)
-
-    if b == 0:
-        run()
-    else:
-        keep = counted(b, me_ref, span_ref)
-        pl.when(keep)(run)
-
-        @pl.when(jnp.logical_not(keep))
-        def _():
-            out[...] = before[...]
+    lane = lax.broadcasted_iota(jnp.int32, flags.shape, 1)
+    found = jnp.zeros(flags.shape, F32)
+    for b in range(1, n):
+        found = jnp.where((lane == b) & (span_ref[me ^ b] < span_ref[me]), 1.0, found)
+    flags[...] = found
+    q_out[...] = q_ref[...]
+    do_out[...] = do_ref[...]
+    stats_of_block(0, q_ref, do_ref, kv, None, out)
+
+
+def next_stats_kernel(b, flags, q_ref, do_ref, kv, before, out):
+    keep = counted(b, flags)
+
+    @pl.when(keep)
+    def _():
+        stats_of_block(b, q_ref, do_ref, kv, before, out)
+
+    @pl.when(jnp.logical_not(keep))
+    def _():
+        out[...] = before[...]
 
 
 def block_gradients(own, stats, q_ref, do_ref, kv, p_buf, ds_ref, dk, dv):
@@ -219,8 +230,8 @@
     return dk[...] * inverse, dv[...]
 
 
-def other_kernel(b, me_ref, span_ref, stats, q_ref, do_ref, kv, out_ref, ds_out, p_buf, dk, dv):
-    keep = counted(b, me_ref, span_ref)
+def other_kernel(b, flags, stats, q_ref, do_ref, kv, out_ref, ds_out, p_buf, dk, dv):
+    keep = counted(b, flags)
     rows, hd = dk.shape
 
     @pl.when(keep)
@@ -235,7 +246,7 @@
         ds_out[...] = jnp.zeros_like(ds_out)
 
 
-def own_kernel(me_ref, span_ref, stats, q_ref, do_ref, kv, out_ref, ds_out, p_buf, dk, dv):
+def own_kernel(stats, q_ref, do_ref, kv, out_ref, ds_out, p_buf, dk, dv):
     hd = dk.shape[1]
     dk_sum, dv_sum = block_gradients(True, stats, q_ref, do_ref, kv, p_buf, ds_out, dk, dv)
     out_ref[:, :hd] = dk_sum
@@ -243,7 +254,8 @@
 
 
 def query_kernel(n, *refs):
-    kv_refs, ds_refs, dq_ref = refs[:n], refs[n : 2 * n], refs[2 * n]
+    kv_refs, ds_refs, dq_ref, mark_ref = refs[:n], refs[n : 2 * n], refs[2 * n], refs[2 * n + 1]
+    mark_ref[...] = jnp.zeros_like(mark_ref)
     rows, hd = kv_refs[0].shape[0], kv_refs[0].shape[1] // 2
     for h in range(dq_ref.shape[1] // hd):
         dq = 0.0
@@ -253,37 +265,38 @@
         dq_ref[:, h * hd : (h + 1) * hd] = (dq / hd**0.5).astype(BF16)
 
 
-def relay_kernel(block_ref, out_ref):
-    out_ref[...] = block_ref[...]
-
-
 def attention(me, spans, queries, out_grad, pairs, swap, n):
     rows, hd = pairs.shape[0], pairs.shape[1] // 2
     columns = queries.shape[1]
     tall = columns // hd * rows
     product = 2 * rows * tall * hd
-    scalars = [me, spans]
-
-    def stats_call(b, operands):
-        outs = [shape((8, tall), F32)]
-        cost = (4 * product, 8 * rows * columns)
-        return whole_call(functools.partial(stats_kernel, b), "block_stats", scalars, operands, outs, 20, cost)[0]
-
-    blocks = [pairs] + [None] * (n - 1)
+    cost = (4 * product, 8 * rows * columns)
+
+    blocks = [pairs]
     for b in range(1, n):
-        if b & (b - 1) == 0:
-            blocks[b] = swap(pairs, b)
-    stats = stats_call(0, [queries, out_grad, pairs])
+        blocks.append(swap(blocks[b & (b - 1)], b & -b))
+    stats_shape = shape((8, tall), F32)
+    stats, queries, out_grad, flags = whole_call(
+        functools.partial(first_stats_kernel, n),
+        "first_stats",
+        [me, spans],
+        [queries, out_grad, pairs],
+        [stats_shape, shape(queries.shape), shape(out_grad.shape), shape((8, 128), F32)],
+        14,
+        cost,
+    )
     for b in range(1, n):
-        if blocks[b] is None:
-            handed = blocks[b & (b - 1)]
-            if b == 3:
-                cost = (0, 8 * rows * hd)
-                handed = whole_call(relay_kernel, "relay", [], [handed], [shape(handed.shape)], 4, cost, [], first)[0]
-            blocks[b] = swap(handed, b & -b)
-        stats = stats_call(b, [queries, out_grad, blocks[b], stats])
-        if b == 1:
-            first = [stats]
+        stats = whole_call(
+            functools.partial(next_stats_kernel, b),
+            "next_stats",
+            [],
+            [flags, queries, out_grad, blocks[b], stats],
+            [stats_shape],
+            12,
+            cost,
+            [],
+            blocks[2:3] if b == 1 else [],
+        )[0]
     received = blocks[1:]
     p_buf = pltpu.VMEM((rows, 2 * rows), BF16)
     sums = [pltpu.VMEM((rows, hd), F32)] * 2
@@ -292,10 +305,10 @@
         part, score_grads[b - 1] = whole_call(
             functools.partial(other_kernel, b),
             "block_gradients",
-            scalars,
-            [stats, queries, out_grad, received[b - 1]],
+            [],
+            [flags, stats, queries, out_grad, received[b - 1]],
             [shape((rows, 2 * hd)), shape((rows, tall))],
-            24,
+            14,
             (8 * product, 16 * rows * columns),
             [p_buf, *sums],
             before,
@@ -305,10 +318,10 @@
     own, own_score_grad = whole_call(
         own_kernel,
         "own_gradients",
-        scalars,
+        [],
         [stats, queries, out_grad, pairs],
         [shape((rows, 2 * hd), F32), shape((rows, tall))],
-        24,
+        14,
         (8 * product, 16 * rows * columns),
         [p_buf, *sums],
         before,
@@ -324,12 +337,12 @@
         "query_gradients",
         [],
         [*blocks, *score_grads],
-        [shape((rows, columns))],
-        24,
+        [shape((rows, columns)), shape((8, 128), F32)],
+        5 + 3 * n,
         (2 * n * rows * rows * columns, 16 * rows * columns),
         [],
         after,
-    )[0]
+    )
 
 
 def pack_top(top):
@@ -341,7 +354,7 @@
 
 
 def unpack_top(ref, at):
-    x = ref[at : at + TOP_ROWS, :].astype(F32)
+    x = ref[at : at + TOP_ROWS, :TOP_LANES].astype(F32)
     total = x + (pltpu.roll(x, TOP_LANES - PACK_LANES, 1) + pltpu.roll(x, TOP_LANES - 2 * PACK_LANES, 1))
     lane = lax.broadcasted_iota(jnp.int32, x.shape, 1)
     return jnp.where(lane < PACK_LANES, total, 0.0)
@@ -376,6 +389,18 @@
     top = jnp.max(jnp.where(lane == place, mags, 0.0), axis=0, keepdims=True)
     top_ref[pl.ds(dest, 1), :] = jnp.maximum(top_ref[pl.ds(dest, 1), :], top)
     return c
+
+
+def send_rows(bits, shrink, chosen, me_ref, total, a_ref, e_ref, out_ref, top_ref, packed):
+    tall = a_ref.shape[1] * a_ref.shape[3]
+    steps = a_ref.shape[0] // 2
+    for step in range(steps):
+        dest = tile_of(step, me_ref[0], bits, 1)
+        c = corrected_tile(chosen, dest, total, a_ref, e_ref, top_ref)
+        out_ref[step * tall : (step + 1) * tall, :] = (c * shrink).astype(BF16)
+    if packed:
+        out_ref[steps * tall :, :TOP_LANES] = pack_top(top_ref[...])
+        out_ref[steps * tall :, TOP_LANES:] = jnp.zeros((TOP_ROWS, out_ref.shape[1] - TOP_LANES), BF16)
 
 
 def first_send_kernel(bits, shrink, n_parts, me_ref, own_ref, *refs):
@@ -390,40 +415,42 @@
     vg_ref[...] = total[:, hd:]
     grads_ref[...] = total
     top_ref[...] = jnp.zeros_like(top_ref)
-    send_rows(bits, shrink, 0, me_ref, total, a_ref, e_ref, out_ref, top_ref)
-
-
-def next_send_kernel(bits, shrink, chosen, me_ref, grads_ref, before_ref, a_ref, e_ref, out_ref, top_ref):
+    send_rows(bits, shrink, 0, me_ref, total, a_ref, e_ref, out_ref, top_ref, False)
+
+
+def next_send_kernel(bits, shrink, chosen, packed, me_ref, grads_ref, before_ref, a_ref, e_ref, out_ref, top_ref):
     top_ref[...] = before_ref[...]
-    send_rows(bits, shrink, chosen, me_ref, grads_ref[...], a_ref, e_ref, out_ref, top_ref)
-
-
-def send_rows(bits, shrink, chosen, me_ref, total, a_ref, e_ref, out_ref, top_ref):
-    for step in range(out_ref.shape[0]):
-        dest = tile_of(step, me_ref[0], bits, 1)
-        c = corrected_tile(chosen, dest, total, a_ref, e_ref, top_ref)
-        out_ref[step] = (c * shrink).astype(BF16)
-
-
-def keep_kernel(bits, shrink, chosen, me_ref, grads, got_ref, before_ref, a_ref, e_ref, *outs):
-    low_away, low_stay, high_away, high_stay, top_ref = outs
-    steps, tall, width = got_ref.shape
+    send_rows(bits, shrink, chosen, me_ref, grads_ref[...], a_ref, e_ref, out_ref, top_ref, packed)
+
+
+def kept_kernel(bits, shrink, me_ref, grads_ref, before_ref, a_ref, e_ref, *outs):
+    *kept, top_ref = outs
+    top_ref[...] = before_ref[...]
+    total = grads_ref[...]
+    for chosen, out_ref in enumerate(kept):
+        for step in range(out_ref.shape[0]):
+            dest = tile_of(step, me_ref[0], bits, 0)
+            out_ref[step] = corrected_tile(chosen, dest, total, a_ref, e_ref, top_ref) * shrink
+
+
+def split_kernel(bits, n_tops, kept, got, *refs):
+    steps, tall, width = kept.shape
     half = steps // 2
     hd = width // 2
-    total = grads[...]
-    top_ref[...] = before_ref[...]
+    tops = refs[:n_tops]
+    low_away, low_stay, high_away, high_stay, *top_out = refs[n_tops:]
     for step in range(steps):
-        dest = tile_of(step, me_ref[0], bits, 0)
-        c = corrected_tile(chosen, dest, total, a_ref, e_ref, top_ref)
-        c = (c * shrink + got_ref[step].astype(F32)).astype(BF16)
+        c = (kept[step] + got[step * tall : (step + 1) * tall, :].astype(F32)).astype(BF16)
         back = reversed_step(step, bits)
         for at, part, away, stay in ((step, c[:, :hd], low_away, low_stay), (back, c[:, hd:], high_away, high_stay)):
             if at < half:
                 away[at * tall : (at + 1) * tall, :] = part
             else:
                 stay[(at - half) * tall : (at - half + 1) * tall, :] = part
-    if low_away.shape[0] > half * tall:
-        low_away[half * tall :, :] = pack_top(top_ref[...])
+    if tops:
+        top = largest(tops, got, steps * tall)
+        top_out[0][...] = top
+        low_away[half * tall :, :] = pack_top(top)
 
 
 def largest(tops, low_got, size):
@@ -522,48 +549,54 @@
     tops = shape((TOP_ROWS, TOP_LANES), F32)
     steps = n_dp // 2
     cost = (2 * steps * tall * rows * width, steps * tall * (2 * rows + 6 * width))
-    message = shape((steps, tall, width))
-    got = []
-    for chosen in range(sets):
-        if chosen == 0:
-            out, top, key_grad, value_grad, grads = whole_call(
-                functools.partial(first_send_kernel, bits, shrink, n_ctx - 1),
-                "send_tiles",
-                [me_dp],
-                [own, *parts, acts, errors],
-                [message, tops, shape((rows, hd)), shape((rows, hd)), shape((rows, width))],
-                28,
-                cost,
-            )
-        else:
-            out, top = whole_call(
-                functools.partial(next_send_kernel, bits, shrink, chosen),
-                "send_tiles",
-                [me_dp],
-                [grads, top, acts, errors],
-                [message, tops],
-                28,
-                cost,
-            )
+    out, top, key_grad, value_grad, grads = whole_call(
+        functools.partial(first_send_kernel, bits, shrink, n_ctx - 1),
+        "send_tiles",
+        [me_dp],
+        [own, *parts, acts, errors],
+        [shape((steps * tall, width)), tops, shape((rows, hd)), shape((rows, hd)), shape((rows, width))],
+        22,
+        cost,
+    )
+    got = [swap_dp(out, 1)]
+    *kept, top = whole_call(
+        functools.partial(kept_kernel, bits, shrink),
+        "kept_tiles",
+        [me_dp],
+        [grads, top, acts, errors],
+        [shape((steps, tall, width), F32)] * sets + [tops],
+        24,
+        (sets * cost[0], sets * cost[1]),
+    )
+    for chosen in range(1, sets):
+        extra = TOP_ROWS if chosen == sets - 1 else 0
+        out, top = whole_call(
+            functools.partial(next_send_kernel, bits, shrink, chosen, extra > 0),
+            "send_tiles",
+            [me_dp],
+            [grads, top, acts, errors],
+            [shape((steps * tall + extra, width)), tops],
+            22,
+            cost,
+        )
         got.append(swap_dp(out, 1))
 
     halves = []
     for chosen in range(sets):
         half = steps // 2 * tall
-        extra = TOP_ROWS if chosen == sets - 1 else 0
-        *arrays, top = whole_call(
-            functools.partial(keep_kernel, bits, shrink, chosen),
-            "keep_tiles",
-            [me_dp],
-            [grads, got[chosen], top, acts, errors],
-            [shape((half + extra, hd))] + [shape((half, hd))] * 3 + [tops],
-            28,
-            cost,
+        last = chosen == sets - 1
+        arrays = whole_call(
+            functools.partial(split_kernel, bits, int(last)),
+            "split_tiles",
+            [],
+            [kept[chosen], got[chosen]] + [top] * last,
+            [shape((half + TOP_ROWS * last, hd))] + [shape((half, hd))] * 3 + [tops] * last,
+            10,
+            (4 * half * width, 12 * half * width),
         )
-        halves.append(arrays)
-
-    gathered = [top, swap_dp(top, 1), swap_dp(top, 3)]
-    query_grad = query_gradients(blocks, score_grads, queries.shape[1], [top])
+        halves.append(arrays[:4])
+    gathered = [arrays[4]]
+    query_grad, mark = query_gradients(blocks, score_grads, queries.shape[1], [arrays[1]])
     groups = []
     for chosen in range(sets):
         low_away, low, high_away, high = halves[chosen]
@@ -571,7 +604,7 @@
         for stage in range(1, bits):
             low_got = swap_dp(low_away, 1 << stage)
             high_got = swap_dp(high_away, 1 << (bits - stage))
-            with_tops = extra > 0 or (chosen == 0 and stage == 1)
+            with_tops = extra > 0
             operands = [low, low_got, high, high_got] + (gathered if with_tops else [])
             n_tops = len(operands) - 4
             size = low.shape[0]
@@ -583,9 +616,9 @@
                     [],
                     operands,
                     [shape((size // 2 + extra, hd))] + [shape((size // 2, hd))] * 3 + [tops] * with_tops,
-                    16,
+                    8,
                     cost,
-                    after=[query_grad] if chosen == 0 and stage == 1 else [],
+                    after=[mark] if chosen == 0 and stage == 1 else [],
                 )
             else:
                 outs = whole_call(
@@ -596,7 +629,7 @@
                     [shape((2 * rows_set, hd), F32)]
                     + [shape((2 * rows_set + extra, hd))] * (n_ctx - 1)
                     + [tops] * with_tops,
-                    16,
+                    8,
                     cost,
                 )
                 mine, away, top_out = outs[0], outs[1:n_ctx], outs[n_ctx:]

time: 96.8 us -> 85.8 us (0.89)
  waiting for transfers between devices: 23.9 us -> 16.7 us
  local copies, waits for them, and re-layouts: 9.42 us -> 6.78 us
  starting transfers between devices: 29.8 us -> 28.4 us
    ppermute x12 -> x10, waiting for transfers between devices: 11.5 us -> 5.21 us  [swap_dp(): return lax.ppermute(x, 'dp', xor_perm(n_dp, mask))]
    ppermute x12, starting transfers between devices: 20 us -> 16.9 us  [swap_ctx(): return lax.ppermute(x, 'context', xor_perm(n_ctx, mask))]
    unnamed x32 -> x22, local copies, waits for them, and re-layouts: 8.79 us -> 6.15 us
    ppermute x12 -> x10, starting transfers between devices: 9.8 us -> 11.5 us  [swap_dp(): return lax.ppermute(x, 'dp', xor_perm(n_dp, mask))]
    pallas_call x19, Pallas kernels: 28.1 us -> 29.4 us  [whole_call(): pl.pallas_call(body, grid_spec=pltpu.PrefetchScalarGridSpec(num_scalar_pr...]
  transfers between devices with their start and end apart: 24 -> 22, of which waited for: 7 -> 8; matrix products, arithmetic and copies ran while one was open for 0% -> 0% of each run, Pallas kernels for 25% -> 30%
where the time goes in v6:
time: 85.8 us; the launch traced here: 85.6 us
  Pallas kernels  32.9 us (38%)
  starting transfers between devices  28.4 us (33%)
  waiting for transfers between devices  16.7 us (19%)
  local copies, waits for them, and re-layouts  6.78 us (8%)
  between operations  0.86 us (1%)
    pallas_call x19, Pallas kernels, whole_call(): pl.pallas_call(body, grid_spec=pltpu.PrefetchScalarGridSpec(num_scalar_pr...  29.4 us
    ppermute x12, starting transfers between devices, swap_ctx(): return lax.ppermute(x, 'context', xor_perm(n_ctx, mask))  16.9 us
    ppermute x10, starting transfers between devices, swap_dp(): return lax.ppermute(x, 'dp', xor_perm(n_dp, mask))  11.5 us
    ppermute x12, waiting for transfers between devices, swap_ctx(): return lax.ppermute(x, 'context', xor_perm(n_ctx, mask))  11.4 us
    unnamed x22, local copies, waits for them, and re-layouts  6.15 us
    ppermute x10, waiting for transfers between devices, swap_dp(): return lax.ppermute(x, 'dp', xor_perm(n_dp, mask))  5.21 us
    pallas_call x1, Pallas kernels, prepare(): pl.pallas_call(functools.partial(prepare_kernel, pieces), in_specs=[hbm,...  3.51 us
  transfers between devices with their start and end apart: 22, of which 8 were waited for; matrix products, arithmetic and copies ran while one was open for 0% of the time, Pallas kernels for 30%

profile of v6, /device:TPU:0, one launch (start us, length us, event | category | flops | bytes accessed | tf_op | source)
XLA Modules:
  0.0 85.6 jit_solution(16487813599012178343)
XLA Ops:
  2.5 4.1 %collective-permute-start.1 = (bf16[384,256]{1,0:T(8,128)(2,1)S(1)}, bf16[384,256]{1,0:T(8,128)(2,1)S(1)}, u32[]{:S(2)}, u32[]{:S(2)}) collective-permute-start(bf16[384,256]{1,0:T(8,128)(2,1)S(1)} %join_keys_values.1.refs_4_.refs_3_.refs_0_), channel_id=1, source_target_pairs={{0,2},{1,3},{2,0},{3,1},{4,6},{5,7},{6,4},{7,5},{8,10},{9,11},{10,... | collective-permute-start | bytes 589832 | tf_op jit(solution)/shard_map/ppermute | solution.py:538
  6.6 1.6 %collective-permute-start = (bf16[384,256]{1,0:T(8,128)(2,1)S(1)}, bf16[384,256]{1,0:T(8,128)(2,1)S(1)}, u32[]{:S(2)}, u32[]{:S(2)}) collective-permute-start(bf16[384,256]{1,0:T(8,128)(2,1)S(1)} %join_keys_values.1.refs_4_.refs_3_.refs_0_), channel_id=1, source_target_pairs={{0,1},{1,0},{2,3},{3,2},{4,5},{5,4},{6,7},{7,6},{8,9},{9,8},{10,11... | collective-permute-start | bytes 589832 | tf_op jit(solution)/shard_map/ppermute | solution.py:538
  9.3 1.1 %copy-done.5 = bf16[384,1024]{1,0:T(8,128)(2,1)S(1)} copy-done((bf16[384,1024]{1,0:T(8,128)(2,1)S(1)}, bf16[384,1024]{1,0:T(8,128)(2,1)}, u32[]{:S(2)}) %copy-start.5) | copy-done | bytes 786456
  11.1 2.4 %first_stats.1 = (f32[8,3072]{1,0:T(8,128)S(1)}, bf16[384,1024]{1,0:T(8,128)(2,1)S(1)}, bf16[384,1024]{1,0:T(8,128)(2,1)S(1)}, f32[8,128]{1,0:T(8,128)S(1)}) custom-call(s32[1]{0:T(128)} %bitcast.refs_0_.refs_1_, s32[4]{0:T(128)S(1)} %bitcast.17, bf16[384,1024]{1,0:T(8,128)(2,1)S(1)} %copy-done.4, bf16[384,1024]{1,0:T(8,128)(2,1)S(1)} %copy-done.5, ...), custom_call_target="tpu_custom_call" | custom-call | flops 1207959552 | bytes 3145728 | tf_op jit(solution)/shard_map/first_stats/pallas_call | solution.py:39
  13.5 2.3 %collective-permute-done.1.refs_5_.refs_3_.refs_4_.refs_2_ = bf16[384,256]{1,0:T(8,128)(2,1)S(1)} collective-permute-done((bf16[384,256]{1,0:T(8,128)(2,1)S(1)}, bf16[384,256]{1,0:T(8,128)(2,1)S(1)}, u32[]{:S(2)}, u32[]{:S(2)}) %collective-permute-start.1) | collective-permute-done | bytes 196640 | tf_op jit(solution)/shard_map/ppermute | solution.py:538
  16.4 2.2 %next_stats.3.refs_4_ = f32[8,3072]{1,0:T(8,128)S(1)} custom-call(f32[8,128]{1,0:T(8,128)S(1)} %get-tuple-element.60.refs_0_, bf16[384,1024]{1,0:T(8,128)(2,1)S(1)} %get-tuple-element.61.refs_1_.refs_2_, bf16[384,1024]{1,0:T(8,128)(2,1)S(1)} %get-tuple-element.62.refs_2_.refs_3_, bf16[384,256]{1,0:T(8,128)(2,1)S(1)} %collective-permute-done.refs_3_.refs_4_.refs_1_, ...), custom_call_target="tpu_custom_call" | custom-call | flops 1207959552 | bytes 3145728 | tf_op jit(solution)/shard_map/next_stats/pallas_call | solution.py:39
  18.6 2.2 %next_stats.4.refs_4_ = f32[8,3072]{1,0:T(8,128)S(1)} custom-call(f32[8,128]{1,0:T(8,128)S(1)} %get-tuple-element.60.refs_0_, bf16[384,1024]{1,0:T(8,128)(2,1)S(1)} %get-tuple-element.61.refs_1_.refs_2_, bf16[384,1024]{1,0:T(8,128)(2,1)S(1)} %get-tuple-element.62.refs_2_.refs_3_, bf16[384,256]{1,0:T(8,128)(2,1)S(1)} %collective-permute-done.1.refs_5_.refs_3_.refs_4_.refs_2_, ...), custom_call_target="tpu_custom_call" | custom-call | flops 1207959552 | bytes 3145728 | tf_op jit(solution)/shard_map/next_stats/pallas_call | solution.py:39
  21.8 2.2 %next_stats.5.refs_1_.refs_0_ = f32[8,3072]{1,0:T(8,128)S(1)} custom-call(f32[8,128]{1,0:T(8,128)S(1)} %get-tuple-element.60.refs_0_, bf16[384,1024]{1,0:T(8,128)(2,1)S(1)} %get-tuple-element.61.refs_1_.refs_2_, bf16[384,1024]{1,0:T(8,128)(2,1)S(1)} %get-tuple-element.62.refs_2_.refs_3_, bf16[384,256]{1,0:T(8,128)(2,1)S(1)} %collective-permute-done.2.refs_3_.refs_4_, ...), custom_call_target="tpu_custom_call" | custom-call | flops 1207959552 | bytes 3145728 | tf_op jit(solution)/shard_map/next_stats/pallas_call | solution.py:39
  24.1 2.8 %block_gradients.3 = (bf16[384,256]{1,0:T(8,128)(2,1)S(1)}, bf16[384,3072]{1,0:T(8,128)(2,1)S(1)}) custom-call(f32[8,128]{1,0:T(8,128)S(1)} %get-tuple-element.60.refs_0_, f32[8,3072]{1,0:T(8,128)S(1)} %next_stats.5.refs_1_.refs_0_, bf16[384,1024]{1,0:T(8,128)(2,1)S(1)} %get-tuple-element.61.refs_1_.refs_2_, ...), custom_call_target="tpu_custom_call" | custom-call | flops 2415919104 | bytes 6291456 | tf_op jit(solution)/shard_map/block_gradients/pallas_call | solution.py:39
  26.9 2.9 %block_gradients.4 = (bf16[384,256]{1,0:T(8,128)(2,1)S(1)}, bf16[384,3072]{1,0:T(8,128)(2,1)S(1)}) custom-call(f32[8,128]{1,0:T(8,128)S(1)} %get-tuple-element.60.refs_0_, f32[8,3072]{1,0:T(8,128)S(1)} %next_stats.5.refs_1_.refs_0_, bf16[384,1024]{1,0:T(8,128)(2,1)S(1)} %get-tuple-element.61.refs_1_.refs_2_, ...), custom_call_target="tpu_custom_call" | custom-call | flops 2415919104 | bytes 6291456 | tf_op jit(solution)/shard_map/block_gradients/pallas_call | solution.py:39
  30.5 2.8 %block_gradients.5 = (bf16[384,256]{1,0:T(8,128)(2,1)S(1)}, bf16[384,3072]{1,0:T(8,128)(2,1)S(1)}) custom-call(f32[8,128]{1,0:T(8,128)S(1)} %get-tuple-element.60.refs_0_, f32[8,3072]{1,0:T(8,128)S(1)} %next_stats.5.refs_1_.refs_0_, bf16[384,1024]{1,0:T(8,128)(2,1)S(1)} %get-tuple-element.61.refs_1_.refs_2_, ...), custom_call_target="tpu_custom_call" | custom-call | flops 2415919104 | bytes 6291456 | tf_op jit(solution)/shard_map/block_gradients/pallas_call | solution.py:39
  33.3 1.4 %copy-done = bf16[384,3072]{1,0:T(8,128)(2,1)} copy-done((bf16[384,3072]{1,0:T(8,128)(2,1)}, bf16[384,3072]{1,0:T(8,128)(2,1)S(1)}, u32[]{:S(2)}) %copy-start) | copy-done | bytes 2359320
  34.7 1.3 %collective-permute-start.3 = (bf16[384,256]{1,0:T(8,128)(2,1)S(1)}, bf16[384,256]{1,0:T(8,128)(2,1)S(1)}, u32[]{:S(2)}, u32[]{:S(2)}) collective-permute-start(bf16[384,256]{1,0:T(8,128)(2,1)S(1)} %get-tuple-element.66.refs_4_._), channel_id=1, source_target_pairs={{0,1},{1,0},{2,3},{3,2},{4,5},{5,4},{6,7},{7,6},{8,9},{9,8},{10,11... | collective-permute-start | bytes 589832 | tf_op jit(solution)/shard_map/ppermute | solution.py:538
  36.1 3.5 %prepare.1 = (bf16[8192,384]{1,0:T(8,128)(2,1)S(1)}, f32[8192,256]{1,0:T(8,128)S(1)}) custom-call(bf16[384,8192]{1,0:T(8,128)(2,1)S(1)} %bitcast.16, f32[8192,256]{1,0:T(8,128)S(1)} %bitcast.14, bf16[384,256]{1,0:T(8,128)(2,1)S(1)} %get-tuple-element.66.refs_4_._), custom_call_target="tpu_custom_call" | custom-call | bytes 14680064 | tf_op jit(solution)/shard_map/prepare/pallas_call | solution.py:101
  39.6 2.6 %own_gradients.1 = (f32[384,256]{1,0:T(8,128)S(1)}, bf16[384,3072]{1,0:T(8,128)(2,1)S(1)}) custom-call(f32[8,3072]{1,0:T(8,128)S(1)} %next_stats.5.refs_1_.refs_0_, bf16[384,1024]{1,0:T(8,128)(2,1)S(1)} %get-tuple-element.61.refs_1_.refs_2_, bf16[384,1024]{1,0:T(8,128)(2,1)S(1)} %get-tuple-element.62.refs_2_.refs_3_, ...), custom_call_target="tpu_custom_call" | custom-call | flops 2415919104 | bytes 6291456 | tf_op jit(solution)/shard_map/own_gradients/pallas_call | solution.py:39
  42.2 4.9 %collective-permute-done.4.refs_3_ = bf16[384,256]{1,0:T(8,128)(2,1)S(1)} collective-permute-done((bf16[384,256]{1,0:T(8,128)(2,1)S(1)}, bf16[384,256]{1,0:T(8,128)(2,1)S(1)}, u32[]{:S(2)}, u32[]{:S(2)}) %collective-permute-start.4) | collective-permute-done | bytes 196640 | tf_op jit(solution)/shard_map/ppermute | solution.py:538
  47.2 1.3 %send_tiles.2 = (bf16[2048,256]{1,0:T(8,128)(2,1)S(1)}, f32[16,128]{1,0:T(8,128)S(1)}, bf16[384,128]{1,0:T(8,128)(2,1)}, bf16[384,128]{1,0:T(8,128)(2,1)}, bf16[384,256]{1,0:T(8,128)(2,1)S(1)}) custom-call(s32[1]{0:T(128)} %bitcast.2.refs_0_, f32[384,256]{1,0:T(8,128)S(1)} %get-tuple-element.71.refs_1_, bf16[384,256]{1,0:T(8,128)(2,1)S(1)} %collective-permute-done.3.refs_2_, ...), custom_call_target="tpu_custom_call" | custom-call | flops 402653184 | bytes 4718592 | tf_op jit(solution)/shard_map/send_tiles/pallas_call | solution.py:39
  48.4 1.4 %kept_tiles.1 = (f32[4,512,256]{2,1,0:T(8,128)S(1)}, f32[4,512,256]{2,1,0:T(8,128)S(1)}, f32[16,128]{1,0:T(8,128)S(1)}) custom-call(s32[1]{0:T(128)} %bitcast.2.refs_0_, bf16[384,256]{1,0:T(8,128)(2,1)S(1)} %get-tuple-element.74.refs_1_, f32[16,128]{1,0:T(8,128)S(1)} %get-tuple-element.75.refs_2_, bf16[8,4,2,128,384]{4,3,2,1,0:T(8,128)(2,1)S(1)} %bitcast.10, ...), custom_call_target="tpu_custom_call" | custom-call | flops 805306368 | bytes 9437184 | tf_op jit(solution)/shard_map/kept_tiles/pallas_call | solution.py:39
  52.2 1.6 %collective-permute-start.9 = (bf16[1024,128]{1,0:T(8,128)(2,1)S(1)}, bf16[1024,128]{1,0:T(8,128)(2,1)S(1)}, u32[]{:S(2)}, u32[]{:S(2)}) collective-permute-start(bf16[1024,128]{1,0:T(8,128)(2,1)S(1)} %get-tuple-element.89), channel_id=1, source_target_pairs={{0,16},{4,20},{8,24},{12,28},{16,0},{20,4},{24,8},{28,12},{1,17},{... | collective-permute-start | bytes 786440 | tf_op jit(solution)/shard_map/ppermute | solution.py:535
  54.3 1.7 %collective-permute-start.15 = (bf16[1040,128]{1,0:T(8,128)(2,1)S(1)}, bf16[1040,128]{1,0:T(8,128)(2,1)S(1)}, u32[]{:S(2)}, u32[]{:S(2)}) collective-permute-start(bf16[1040,128]{1,0:T(8,128)(2,1)S(1)} %get-tuple-element.99), channel_id=1, source_target_pairs={{0,8},{4,12},{8,0},{12,4},{16,24},{20,28},{24,16},{28,20},{1,9},{5... | collective-permute-start | bytes 798728 | tf_op jit(solution)/shard_map/ppermute | solution.py:535
  56.3 3.6 %query_gradients.1 = (bf16[384,1024]{1,0:T(8,128)(2,1)}, f32[8,128]{1,0:T(8,128)S(1)}) custom-call(bf16[384,256]{1,0:T(8,128)(2,1)S(1)} %join_keys_values.1.refs_4_.refs_3_.refs_0_, bf16[384,256]{1,0:T(8,128)(2,1)S(1)} %collective-permute-done.refs_3_.refs_4_.refs_1_, bf16[384,256]{1,0:T(8,128)(2,1)S(1)} %collective-permute-done.1.refs_5_.refs_3_.refs_4_.refs_2_, ...), custom_call_target="tpu_custom_call" | custom-call | flops 1207959552 | bytes 6291456 | tf_op jit(solution)/shard_map/query_gradients/pallas_call | solution.py:39
  61.6 1.7 %collective-permute-start.10 = (bf16[512,128]{1,0:T(8,128)(2,1)S(1)}, bf16[512,128]{1,0:T(8,128)(2,1)S(1)}, u32[]{:S(2)}, u32[]{:S(2)}) collective-permute-start(bf16[512,128]{1,0:T(8,128)(2,1)S(1)} %get-tuple-element.92), channel_id=1, source_target_pairs={{0,16},{4,20},{8,24},{12,28},{16,0},{20,4},{24,8},{28,12},{1,17},{... | collective-permute-start | bytes 393224 | tf_op jit(solution)/shard_map/ppermute | solution.py:535
  63.3 1.6 %collective-permute-start.11 = (bf16[512,128]{1,0:T(8,128)(2,1)S(1)}, bf16[512,128]{1,0:T(8,128)(2,1)S(1)}, u32[]{:S(2)}, u32[]{:S(2)}) collective-permute-start(bf16[512,128]{1,0:T(8,128)(2,1)S(1)} %get-tuple-element.94), channel_id=1, source_target_pairs={{0,8},{4,12},{8,0},{12,4},{16,24},{20,28},{24,16},{28,20},{1,9},{5... | collective-permute-start | bytes 393224 | tf_op jit(solution)/shard_map/ppermute | solution.py:535
  64.9 2.2 %collective-permute-done.16.refs_3_ = bf16[1024,128]{1,0:T(8,128)(2,1)S(1)} collective-permute-done((bf16[1024,128]{1,0:T(8,128)(2,1)S(1)}, bf16[1024,128]{1,0:T(8,128)(2,1)S(1)}, u32[]{:S(2)}, u32[]{:S(2)}) %collective-permute-start.16) | collective-permute-done | bytes 262176 | tf_op jit(solution)/shard_map/ppermute | solution.py:535
  67.3 1.7 %collective-permute-start.17 = (bf16[528,128]{1,0:T(8,128)(2,1)S(1)}, bf16[528,128]{1,0:T(8,128)(2,1)S(1)}, u32[]{:S(2)}, u32[]{:S(2)}) collective-permute-start(bf16[528,128]{1,0:T(8,128)(2,1)S(1)} %get-tuple-element.104), channel_id=1, source_target_pairs={{0,16},{4,20},{8,24},{12,28},{16,0},{20,4},{24,8},{28,12},{1,17},{... | collective-permute-start | bytes 405512 | tf_op jit(solution)/shard_map/ppermute | solution.py:535
  69.0 1.6 %collective-permute-start.18 = (bf16[512,128]{1,0:T(8,128)(2,1)S(1)}, bf16[512,128]{1,0:T(8,128)(2,1)S(1)}, u32[]{:S(2)}, u32[]{:S(2)}) collective-permute-start(bf16[512,128]{1,0:T(8,128)(2,1)S(1)} %get-tuple-element.106), channel_id=1, source_target_pairs={{0,8},{4,12},{8,0},{12,4},{16,24},{20,28},{24,16},{28,20},{1,9},{5... | collective-permute-start | bytes 393224 | tf_op jit(solution)/shard_map/ppermute | solution.py:535
  70.7 1.8 %collective-permute-start.12 = (bf16[256,128]{1,0:T(8,128)(2,1)S(1)}, bf16[256,128]{1,0:T(8,128)(2,1)S(1)}, u32[]{:S(2)}, u32[]{:S(2)}) collective-permute-start(bf16[256,128]{1,0:T(8,128)(2,1)S(1)} %get-tuple-element.96), channel_id=1, source_target_pairs={{0,3},{1,2},{2,1},{3,0},{4,7},{5,6},{6,5},{7,4},{8,11},{9,10},{10,... | collective-permute-start | bytes 196616 | tf_op jit(solution)/shard_map/ppermute | solution.py:538
  72.5 1.5 %collective-permute-done.18.refs_4_ = bf16[512,128]{1,0:T(8,128)(2,1)S(1)} collective-permute-done((bf16[512,128]{1,0:T(8,128)(2,1)S(1)}, bf16[512,128]{1,0:T(8,128)(2,1)S(1)}, u32[]{:S(2)}, u32[]{:S(2)}) %collective-permute-start.18) | collective-permute-done | bytes 131104 | tf_op jit(solution)/shard_map/ppermute | solution.py:535
  74.2 1.8 %collective-permute-start.19 = (bf16[272,128]{1,0:T(8,128)(2,1)S(1)}, bf16[272,128]{1,0:T(8,128)(2,1)S(1)}, u32[]{:S(2)}, u32[]{:S(2)}) collective-permute-start(bf16[272,128]{1,0:T(8,128)(2,1)S(1)} %get-tuple-element.109), channel_id=1, source_target_pairs={{0,3},{1,2},{2,1},{3,0},{4,7},{5,6},{6,5},{7,4},{8,11},{9,10},{10,... | collective-permute-start | bytes 208904 | tf_op jit(solution)/shard_map/ppermute | solution.py:538
  76.0 2.6 %collective-permute-start.21 = (bf16[272,128]{1,0:T(8,128)(2,1)S(1)}, bf16[272,128]{1,0:T(8,128)(2,1)S(1)}, u32[]{:S(2)}, u32[]{:S(2)}) collective-permute-start(bf16[272,128]{1,0:T(8,128)(2,1)S(1)} %get-tuple-element.111), channel_id=1, source_target_pairs={{0,1},{1,0},{2,3},{3,2},{4,5},{5,4},{6,7},{7,6},{8,9},{9,8},{10,11... | collective-permute-start | bytes 208904 | tf_op jit(solution)/shard_map/ppermute | solution.py:538
  78.9 2.0 %collective-permute-start.14 = (bf16[256,128]{1,0:T(8,128)(2,1)S(1)}, bf16[256,128]{1,0:T(8,128)(2,1)S(1)}, u32[]{:S(2)}, u32[]{:S(2)}) collective-permute-start(bf16[256,128]{1,0:T(8,128)(2,1)S(1)} %get-tuple-element.98), channel_id=1, source_target_pairs={{0,1},{1,0},{2,3},{3,2},{4,5},{5,4},{6,7},{7,6},{8,9},{9,8},{10,11... | collective-permute-start | bytes 196616 | tf_op jit(solution)/shard_map/ppermute | solution.py:538
  81.0 3.1 %collective-permute-done.13.refs_4_ = bf16[256,128]{1,0:T(8,128)(2,1)S(1)} collective-permute-done((bf16[256,128]{1,0:T(8,128)(2,1)S(1)}, bf16[256,128]{1,0:T(8,128)(2,1)S(1)}, u32[]{:S(2)}, u32[]{:S(2)}) %collective-permute-start.13) | collective-permute-done | bytes 65568 | tf_op jit(solution)/shard_map/ppermute | solution.py:538
  (58 shorter events, 13.2 us)
Async XLA Ops:
  0.6 0.9 %copy-start.2 = (bf16[384,128]{1,0:T(8,128)(2,1)S(1)}, bf16[384,128]{1,0:T(8,128)(2,1)}, u32[]{:S(2)}) copy-start(bf16[384,128]{1,0:T(8,128)(2,1)} %k_hbm.1) | copy-start | bytes 294916
  1.5 0.9 %copy-start.3 = (bf16[384,128]{1,0:T(8,128)(2,1)S(1)}, bf16[384,128]{1,0:T(8,128)(2,1)}, u32[]{:S(2)}) copy-start(bf16[384,128]{1,0:T(8,128)(2,1)} %v_hbm.1) | copy-start | bytes 294916
  2.5 13.3 %collective-permute-start.1 = (bf16[384,256]{1,0:T(8,128)(2,1)S(1)}, bf16[384,256]{1,0:T(8,128)(2,1)S(1)}, u32[]{:S(2)}, u32[]{:S(2)}) collective-permute-start(bf16[384,256]{1,0:T(8,128)(2,1)S(1)} %join_keys_values.1.refs_4_.refs_3_.refs_0_), channel_id=1, source_target_pairs={{0,2},{1,3},{2,0},{3,1},{4,6},{5,7},{6,4},{7,5},{8,10},{9,11},{10,... | collective-permute-start | bytes 589832 | tf_op jit(solution)/shard_map/ppermute | solution.py:538
  6.6 9.8 %collective-permute-start = (bf16[384,256]{1,0:T(8,128)(2,1)S(1)}, bf16[384,256]{1,0:T(8,128)(2,1)S(1)}, u32[]{:S(2)}, u32[]{:S(2)}) collective-permute-start(bf16[384,256]{1,0:T(8,128)(2,1)S(1)} %join_keys_values.1.refs_4_.refs_3_.refs_0_), channel_id=1, source_target_pairs={{0,1},{1,0},{2,3},{3,2},{4,5},{5,4},{6,7},{7,6},{8,9},{9,8},{10,11... | collective-permute-start | bytes 589832 | tf_op jit(solution)/shard_map/ppermute | solution.py:538
  8.2 1.1 %copy-start.4 = (bf16[384,1024]{1,0:T(8,128)(2,1)S(1)}, bf16[384,1024]{1,0:T(8,128)(2,1)}, u32[]{:S(2)}) copy-start(bf16[384,1024]{1,0:T(8,128)(2,1)} %refs_2_.1) | copy-start | bytes 2359300
  9.3 1.1 %copy-start.5 = (bf16[384,1024]{1,0:T(8,128)(2,1)S(1)}, bf16[384,1024]{1,0:T(8,128)(2,1)}, u32[]{:S(2)}) copy-start(bf16[384,1024]{1,0:T(8,128)(2,1)} %refs_3_.1) | copy-start | bytes 2359300
  15.8 6.0 %collective-permute-start.2 = (bf16[384,256]{1,0:T(8,128)(2,1)S(1)}, bf16[384,256]{1,0:T(8,128)(2,1)S(1)}, u32[]{:S(2)}, u32[]{:S(2)}) collective-permute-start(bf16[384,256]{1,0:T(8,128)(2,1)S(1)} %collective-permute-done.1.refs_5_.refs_3_.refs_4_.refs_2_), channel_id=1, source_target_pairs={{0,1},{1,0},{2,3},{3,2},{4,5},{5,4},{6,7},{7,6},{8,9},{9,8},{10,11... | collective-permute-start | bytes 589832 | tf_op jit(solution)/shard_map/ppermute | solution.py:538
  24.1 12.0 %slice-start.2 = ((s8[6291456]{0:T(1024)(128)(4,1)}), s8[4194304]{0:T(1024)(128)(4,1)S(1)}, s32[]{:S(2)}) async-start(s8[6291456]{0:T(1024)(128)(4,1)} %bitcast.15), calls=%async_computation.2 | async-start | bytes 8388608
  26.8 9.2 %slice-start.3 = ((s8[6291456]{0:T(1024)(128)(4,1)}), s8[2097152]{0:T(1024)(128)(4,1)S(1)}, s32[]{:S(2)}) async-start(s8[6291456]{0:T(1024)(128)(4,1)} %bitcast.15), calls=%async_computation.3 | async-start | bytes 4194304
  26.8 15.4 %collective-permute-start.5 = (bf16[384,256]{1,0:T(8,128)(2,1)S(1)}, bf16[384,256]{1,0:T(8,128)(2,1)S(1)}, u32[]{:S(2)}, u32[]{:S(2)}) collective-permute-start(bf16[384,256]{1,0:T(8,128)(2,1)S(1)} %get-tuple-element.64.refs_5_), channel_id=1, source_target_pairs={{0,3},{1,2},{2,1},{3,0},{4,7},{5,6},{6,5},{7,4},{8,11},{9,10},{10,... | collective-permute-start | bytes 589832 | tf_op jit(solution)/shard_map/ppermute | solution.py:538
  26.9 9.1 %slice-start = ((s8[8388608]{0:T(1024)(128)(4,1)}), s8[4194304]{0:T(1024)(128)(4,1)S(1)}, s32[]{:S(2)}) async-start(s8[8388608]{0:T(1024)(128)(4,1)} %bitcast.12), calls=%async_computation | async-start | bytes 8388608
  29.9 6.2 %slice-start.1 = ((s8[8388608]{0:T(1024)(128)(4,1)}), s8[4194304]{0:T(1024)(128)(4,1)S(1)}, s32[]{:S(2)}) async-start(s8[8388608]{0:T(1024)(128)(4,1)} %bitcast.12), calls=%async_computation.1 | async-start | bytes 8388608
  29.9 17.3 %collective-permute-start.4 = (bf16[384,256]{1,0:T(8,128)(2,1)S(1)}, bf16[384,256]{1,0:T(8,128)(2,1)S(1)}, u32[]{:S(2)}, u32[]{:S(2)}) collective-permute-start(bf16[384,256]{1,0:T(8,128)(2,1)S(1)} %get-tuple-element.65.refs_5_), channel_id=1, source_target_pairs={{0,2},{1,3},{2,0},{3,1},{4,6},{5,7},{6,4},{7,5},{8,10},{9,11},{10,... | collective-permute-start | bytes 589832 | tf_op jit(solution)/shard_map/ppermute | solution.py:538
  33.3 1.4 %copy-start = (bf16[384,3072]{1,0:T(8,128)(2,1)}, bf16[384,3072]{1,0:T(8,128)(2,1)S(1)}, u32[]{:S(2)}) copy-start(bf16[384,3072]{1,0:T(8,128)(2,1)S(1)} %get-tuple-element.68.refs_5_) | copy-start | bytes 7077892
  34.7 12.4 %collective-permute-start.3 = (bf16[384,256]{1,0:T(8,128)(2,1)S(1)}, bf16[384,256]{1,0:T(8,128)(2,1)S(1)}, u32[]{:S(2)}, u32[]{:S(2)}) collective-permute-start(bf16[384,256]{1,0:T(8,128)(2,1)S(1)} %get-tuple-element.66.refs_4_._), channel_id=1, source_target_pairs={{0,1},{1,0},{2,3},{3,2},{4,5},{5,4},{6,7},{7,6},{8,9},{9,8},{10,11... | collective-permute-start | bytes 589832 | tf_op jit(solution)/shard_map/ppermute | solution.py:538
  48.4 2.9 %collective-permute-start.7 = (bf16[2048,256]{1,0:T(8,128)(2,1)S(1)}, bf16[2048,256]{1,0:T(8,128)(2,1)S(1)}, u32[]{:S(2)}, u32[]{:S(2)}) collective-permute-start(bf16[2048,256]{1,0:T(8,128)(2,1)S(1)} %get-tuple-element.85), channel_id=1, source_target_pairs={{0,4},{4,0},{8,12},{12,8},{16,20},{20,16},{24,28},{28,24},{1,5},{5... | collective-permute-start | bytes 3145736 | tf_op jit(solution)/shard_map/ppermute | solution.py:535
  50.8 3.1 %collective-permute-start.6 = (bf16[2064,256]{1,0:T(8,128)(2,1)S(1)}, bf16[2064,256]{1,0:T(8,128)(2,1)S(1)}, u32[]{:S(2)}, u32[]{:S(2)}) collective-permute-start(bf16[2064,256]{1,0:T(8,128)(2,1)S(1)} %get-tuple-element.78), channel_id=1, source_target_pairs={{0,4},{4,0},{8,12},{12,8},{16,20},{20,16},{24,28},{28,24},{1,5},{5... | collective-permute-start | bytes 3170312 | tf_op jit(solution)/shard_map/ppermute | solution.py:535
  51.6 4.8 %copy-start.1 = (bf16[384,3072]{1,0:T(8,128)(2,1)S(1)}, bf16[384,3072]{1,0:T(8,128)(2,1)}, u32[]{:S(2)}) copy-start(bf16[384,3072]{1,0:T(8,128)(2,1)} %copy-done) | copy-start | bytes 7077892
  51.6 9.2 %collective-permute-start.8 = (bf16[1024,128]{1,0:T(8,128)(2,1)S(1)}, bf16[1024,128]{1,0:T(8,128)(2,1)S(1)}, u32[]{:S(2)}, u32[]{:S(2)}) collective-permute-start(bf16[1024,128]{1,0:T(8,128)(2,1)S(1)} %get-tuple-element.87), channel_id=1, source_target_pairs={{0,8},{4,12},{8,0},{12,4},{16,24},{20,28},{24,16},{28,20},{1,9},{5... | collective-permute-start | bytes 786440 | tf_op jit(solution)/shard_map/ppermute | solution.py:535
  52.2 9.2 %collective-permute-start.9 = (bf16[1024,128]{1,0:T(8,128)(2,1)S(1)}, bf16[1024,128]{1,0:T(8,128)(2,1)S(1)}, u32[]{:S(2)}, u32[]{:S(2)}) collective-permute-start(bf16[1024,128]{1,0:T(8,128)(2,1)S(1)} %get-tuple-element.89), channel_id=1, source_target_pairs={{0,16},{4,20},{8,24},{12,28},{16,0},{20,4},{24,8},{28,12},{1,17},{... | collective-permute-start | bytes 786440 | tf_op jit(solution)/shard_map/ppermute | solution.py:535
  54.3 12.8 %collective-permute-start.15 = (bf16[1040,128]{1,0:T(8,128)(2,1)S(1)}, bf16[1040,128]{1,0:T(8,128)(2,1)S(1)}, u32[]{:S(2)}, u32[]{:S(2)}) collective-permute-start(bf16[1040,128]{1,0:T(8,128)(2,1)S(1)} %get-tuple-element.99), channel_id=1, source_target_pairs={{0,8},{4,12},{8,0},{12,4},{16,24},{20,28},{24,16},{28,20},{1,9},{5... | collective-permute-start | bytes 798728 | tf_op jit(solution)/shard_map/ppermute | solution.py:535
  56.0 11.1 %collective-permute-start.16 = (bf16[1024,128]{1,0:T(8,128)(2,1)S(1)}, bf16[1024,128]{1,0:T(8,128)(2,1)S(1)}, u32[]{:S(2)}, u32[]{:S(2)}) collective-permute-start(bf16[1024,128]{1,0:T(8,128)(2,1)S(1)} %get-tuple-element.101), channel_id=1, source_target_pairs={{0,16},{4,20},{8,24},{12,28},{16,0},{20,4},{24,8},{28,12},{1,17},{... | collective-permute-start | bytes 786440 | tf_op jit(solution)/shard_map/ppermute | solution.py:535
  61.6 9.1 %collective-permute-start.10 = (bf16[512,128]{1,0:T(8,128)(2,1)S(1)}, bf16[512,128]{1,0:T(8,128)(2,1)S(1)}, u32[]{:S(2)}, u32[]{:S(2)}) collective-permute-start(bf16[512,128]{1,0:T(8,128)(2,1)S(1)} %get-tuple-element.92), channel_id=1, source_target_pairs={{0,16},{4,20},{8,24},{12,28},{16,0},{20,4},{24,8},{28,12},{1,17},{... | collective-permute-start | bytes 393224 | tf_op jit(solution)/shard_map/ppermute | solution.py:535
  63.3 7.4 %collective-permute-start.11 = (bf16[512,128]{1,0:T(8,128)(2,1)S(1)}, bf16[512,128]{1,0:T(8,128)(2,1)S(1)}, u32[]{:S(2)}, u32[]{:S(2)}) collective-permute-start(bf16[512,128]{1,0:T(8,128)(2,1)S(1)} %get-tuple-element.94), channel_id=1, source_target_pairs={{0,8},{4,12},{8,0},{12,4},{16,24},{20,28},{24,16},{28,20},{1,9},{5... | collective-permute-start | bytes 393224 | tf_op jit(solution)/shard_map/ppermute | solution.py:535
  67.3 6.7 %collective-permute-start.17 = (bf16[528,128]{1,0:T(8,128)(2,1)S(1)}, bf16[528,128]{1,0:T(8,128)(2,1)S(1)}, u32[]{:S(2)}, u32[]{:S(2)}) collective-permute-start(bf16[528,128]{1,0:T(8,128)(2,1)S(1)} %get-tuple-element.104), channel_id=1, source_target_pairs={{0,16},{4,20},{8,24},{12,28},{16,0},{20,4},{24,8},{28,12},{1,17},{... | collective-permute-start | bytes 405512 | tf_op jit(solution)/shard_map/ppermute | solution.py:535
  69.0 5.0 %collective-permute-start.18 = (bf16[512,128]{1,0:T(8,128)(2,1)S(1)}, bf16[512,128]{1,0:T(8,128)(2,1)S(1)}, u32[]{:S(2)}, u32[]{:S(2)}) collective-permute-start(bf16[512,128]{1,0:T(8,128)(2,1)S(1)} %get-tuple-element.106), channel_id=1, source_target_pairs={{0,8},{4,12},{8,0},{12,4},{16,24},{20,28},{24,16},{28,20},{1,9},{5... | collective-permute-start | bytes 393224 | tf_op jit(solution)/shard_map/ppermute | solution.py:535
  70.7 8.2 %collective-permute-start.12 = (bf16[256,128]{1,0:T(8,128)(2,1)S(1)}, bf16[256,128]{1,0:T(8,128)(2,1)S(1)}, u32[]{:S(2)}, u32[]{:S(2)}) collective-permute-start(bf16[256,128]{1,0:T(8,128)(2,1)S(1)} %get-tuple-element.96), channel_id=1, source_target_pairs={{0,3},{1,2},{2,1},{3,0},{4,7},{5,6},{6,5},{7,4},{8,11},{9,10},{10,... | collective-permute-start | bytes 196616 | tf_op jit(solution)/shard_map/ppermute | solution.py:538
  74.2 9.9 %collective-permute-start.19 = (bf16[272,128]{1,0:T(8,128)(2,1)S(1)}, bf16[272,128]{1,0:T(8,128)(2,1)S(1)}, u32[]{:S(2)}, u32[]{:S(2)}) collective-permute-start(bf16[272,128]{1,0:T(8,128)(2,1)S(1)} %get-tuple-element.109), channel_id=1, source_target_pairs={{0,3},{1,2},{2,1},{3,0},{4,7},{5,6},{6,5},{7,4},{8,11},{9,10},{10,... | collective-permute-start | bytes 208904 | tf_op jit(solution)/shard_map/ppermute | solution.py:538
  76.0 8.1 %collective-permute-start.20 = (bf16[272,128]{1,0:T(8,128)(2,1)S(1)}, bf16[272,128]{1,0:T(8,128)(2,1)S(1)}, u32[]{:S(2)}, u32[]{:S(2)}) collective-permute-start(bf16[272,128]{1,0:T(8,128)(2,1)S(1)} %get-tuple-element.110), channel_id=1, source_target_pairs={{0,2},{1,3},{2,0},{3,1},{4,6},{5,7},{6,4},{7,5},{8,10},{9,11},{10,... | collective-permute-start | bytes 208904 | tf_op jit(solution)/shard_map/ppermute | solution.py:538
  76.0 8.1 %collective-permute-start.21 = (bf16[272,128]{1,0:T(8,128)(2,1)S(1)}, bf16[272,128]{1,0:T(8,128)(2,1)S(1)}, u32[]{:S(2)}, u32[]{:S(2)}) collective-permute-start(bf16[272,128]{1,0:T(8,128)(2,1)S(1)} %get-tuple-element.111), channel_id=1, source_target_pairs={{0,1},{1,0},{2,3},{3,2},{4,5},{5,4},{6,7},{7,6},{8,9},{9,8},{10,11... | collective-permute-start | bytes 208904 | tf_op jit(solution)/shard_map/ppermute | solution.py:538
  78.6 5.5 %collective-permute-start.13 = (bf16[256,128]{1,0:T(8,128)(2,1)S(1)}, bf16[256,128]{1,0:T(8,128)(2,1)S(1)}, u32[]{:S(2)}, u32[]{:S(2)}) collective-permute-start(bf16[256,128]{1,0:T(8,128)(2,1)S(1)} %get-tuple-element.97), channel_id=1, source_target_pairs={{0,2},{1,3},{2,0},{3,1},{4,6},{5,7},{6,4},{7,5},{8,10},{9,11},{10,... | collective-permute-start | bytes 196616 | tf_op jit(solution)/shard_map/ppermute | solution.py:538
  78.9 5.1 %collective-permute-start.14 = (bf16[256,128]{1,0:T(8,128)(2,1)S(1)}, bf16[256,128]{1,0:T(8,128)(2,1)S(1)}, u32[]{:S(2)}, u32[]{:S(2)}) collective-permute-start(bf16[256,128]{1,0:T(8,128)(2,1)S(1)} %get-tuple-element.98), channel_id=1, source_target_pairs={{0,1},{1,0},{2,3},{3,2},{4,5},{5,4},{6,7},{7,6},{8,9},{9,8},{10,11... | collective-permute-start | bytes 196616 | tf_op jit(solution)/shard_map/ppermute | solution.py:538
  (1 other events, 0.7 us)

commit v7 on v6

--- a/solution.py
+++ b/solution.py
@@ -52,73 +52,27 @@
     )(*scalars, *operands, *after)
 
 
-def copy_all(pairs_of_refs, sems):
-    copies = [pltpu.make_async_copy(src, dst, sems.at[i]) for i, (src, dst) in enumerate(pairs_of_refs)]
-    for copy in copies:
-        copy.start()
-    for copy in copies:
-        copy.wait()
-
-
-def join_kernel(k_hbm, v_hbm, out_ref, sems):
-    hd = k_hbm.shape[1]
-    copy_all([(k_hbm, out_ref.at[:, pl.ds(0, hd)]), (v_hbm, out_ref.at[:, pl.ds(hd, hd)])], sems)
-
-
-def load_call(kernel, name, operands, out_shape, mib):
-    return pl.pallas_call(
-        kernel,
-        in_specs=[pl.BlockSpec(memory_space=pltpu.HBM)] * 2,
-        out_specs=[pl.BlockSpec(memory_space=pltpu.VMEM)] * len(out_shape),
-        out_shape=out_shape,
-        scratch_shapes=[pltpu.SemaphoreType.DMA((2,))],
-        compiler_params=pltpu.CompilerParams(vmem_limit_bytes=mib * MIB),
-        cost_estimate=pl.CostEstimate(flops=0, bytes_accessed=4 * operands[0].size, transcendentals=0),
-        name=name,
-    )(*operands)
-
-
-def prepare_kernel(pieces, a_hbm, e_hbm, _, a_out, e_out, a_buf, a_sems, e_sems):
-    model = a_buf.shape[1]
-    tile = model // pieces
-    parts = [pl.ds(i * tile, tile) for i in range(pieces)]
-    a_copies = [pltpu.make_async_copy(a_hbm.at[:, p], a_buf.at[:, p], a_sems.at[i]) for i, p in enumerate(parts)]
-    e_copies = [pltpu.make_async_copy(e_hbm.at[p, :], e_out.at[p, :], e_sems.at[i]) for i, p in enumerate(parts)]
-    for copy in a_copies + e_copies:
-        copy.start()
-    for copy, part in zip(a_copies, parts):
-        copy.wait()
-        a_out[part, :] = a_buf[:, part].T
-    for copy in e_copies:
-        copy.wait()
-
-
-def prepare(activations, errors, after):
+def begin_kernel(out_ref):
+    out_ref[...] = jnp.zeros_like(out_ref)
+
+
+def begin():
+    mark = [shape((8, 128), F32)]
+    return whole_call(begin_kernel, "begin", [], [], mark, 4, (20_000_000_000, 0))[0]
+
+
+def prepare_kernel(pieces, a_ref, a_out):
+    tile = a_ref.shape[1] // pieces
+    for i in range(pieces):
+        a_out[i * tile : (i + 1) * tile, :] = a_ref[:, i * tile : (i + 1) * tile].T
+
+
+def prepare(activations, after):
     rows, model = activations.shape
-    pieces = 8
-    hbm = pl.BlockSpec(memory_space=pltpu.HBM)
-    outs = [shape((model, rows)), shape(errors.shape, F32)]
-    return pl.pallas_call(
-        functools.partial(prepare_kernel, pieces),
-        in_specs=[hbm, hbm, pl.BlockSpec(memory_space=pl.ANY)],
-        out_specs=[pl.BlockSpec(memory_space=pltpu.VMEM)] * 2,
-        out_shape=outs,
-        scratch_shapes=[
-            pltpu.VMEM((rows, model), BF16),
-            pltpu.SemaphoreType.DMA((pieces,)),
-            pltpu.SemaphoreType.DMA((pieces,)),
-        ],
-        compiler_params=pltpu.CompilerParams(vmem_limit_bytes=24 * MIB),
-        cost_estimate=pl.CostEstimate(
-            flops=0, bytes_accessed=2 * rows * model + 4 * errors.size, transcendentals=0
-        ),
-        name="prepare",
-    )(activations, errors, *after)
-
-
-def key_value(ref):
-    hd = ref.shape[1] // 2
-    return ref[:, :hd], ref[:, hd:]
+    outs = [shape((model, rows))]
+    cost = (0, 4 * rows * model)
+    kernel = functools.partial(prepare_kernel, 8)
+    return whole_call(kernel, "prepare", [], [activations], outs, 16, cost, [], after)[0]
 
 
 def head_pair(ref, i, hd):
@@ -145,8 +99,8 @@
     return jnp.max(jnp.where(lane == b, flags[...], 0.0)) > 0.5
 
 
-def stats_of_block(b, q_ref, do_ref, kv, before, out):
-    k, v = key_value(kv)
+def stats_of_block(b, q_ref, do_ref, k_ref, v_ref, before, out):
+    k, v = k_ref[...], v_ref[...]
     rows, hd = k.shape
     pair = 2 * rows
     factor = LOG2E / hd**0.5
@@ -176,7 +130,7 @@
     lax.fori_loop(0, q_ref.shape[1] // (2 * hd), heads, 0, unroll=True)
 
 
-def first_stats_kernel(n, me_ref, span_ref, q_ref, do_ref, kv, out, q_out, do_out, flags):
+def first_stats_kernel(n, me_ref, span_ref, q_ref, do_ref, k_ref, v_ref, out, q_out, do_out, k_out, v_out, flags):
     me = me_ref[0]
     lane = lax.broadcasted_iota(jnp.int32, flags.shape, 1)
     found = jnp.zeros(flags.shape, F32)
@@ -185,23 +139,25 @@
     flags[...] = found
     q_out[...] = q_ref[...]
     do_out[...] = do_ref[...]
-    stats_of_block(0, q_ref, do_ref, kv, None, out)
-
-
-def next_stats_kernel(b, flags, q_ref, do_ref, kv, before, out):
+    k_out[...] = k_ref[...]
+    v_out[...] = v_ref[...]
+    stats_of_block(0, q_ref, do_ref, k_ref, v_ref, None, out)
+
+
+def next_stats_kernel(b, flags, q_ref, do_ref, k_ref, v_ref, before, out):
     keep = counted(b, flags)
 
     @pl.when(keep)
     def _():
-        stats_of_block(b, q_ref, do_ref, kv, before, out)
+        stats_of_block(b, q_ref, do_ref, k_ref, v_ref, before, out)
 
     @pl.when(jnp.logical_not(keep))
     def _():
         out[...] = before[...]
 
 
-def block_gradients(own, stats, q_ref, do_ref, kv, p_buf, ds_ref, dk, dv):
-    k, v = key_value(kv)
+def block_gradients(own, stats, q_ref, do_ref, k_ref, v_ref, p_buf, ds_ref, dk, dv):
+    k, v = k_ref[...], v_ref[...]
     rows, hd = k.shape
     pair = 2 * rows
     factor = LOG2E / hd**0.5
@@ -230,13 +186,13 @@
     return dk[...] * inverse, dv[...]
 
 
-def other_kernel(b, flags, stats, q_ref, do_ref, kv, out_ref, ds_out, p_buf, dk, dv):
+def other_kernel(b, flags, stats, q_ref, do_ref, k_ref, v_ref, out_ref, ds_out, p_buf, dk, dv):
     keep = counted(b, flags)
     rows, hd = dk.shape
 
     @pl.when(keep)
     def _():
-        dk_sum, dv_sum = block_gradients(False, stats, q_ref, do_ref, kv, p_buf, ds_out, dk, dv)
+        dk_sum, dv_sum = block_gradients(False, stats, q_ref, do_ref, k_ref, v_ref, p_buf, ds_out, dk, dv)
         out_ref[:, :hd] = dk_sum.astype(BF16)
         out_ref[:, hd:] = dv_sum.astype(BF16)
 
@@ -246,97 +202,124 @@
         ds_out[...] = jnp.zeros_like(ds_out)
 
 
-def own_kernel(stats, q_ref, do_ref, kv, out_ref, ds_out, p_buf, dk, dv):
+def own_kernel(stats, q_ref, do_ref, k_ref, v_ref, out_ref, ds_out, p_buf, dk, dv):
     hd = dk.shape[1]
-    dk_sum, dv_sum = block_gradients(True, stats, q_ref, do_ref, kv, p_buf, ds_out, dk, dv)
+    dk_sum, dv_sum = block_gradients(True, stats, q_ref, do_ref, k_ref, v_ref, p_buf, ds_out, dk, dv)
     out_ref[:, :hd] = dk_sum
     out_ref[:, hd:] = dv_sum
 
 
 def query_kernel(n, *refs):
-    kv_refs, ds_refs, dq_ref, mark_ref = refs[:n], refs[n : 2 * n], refs[2 * n], refs[2 * n + 1]
+    k_refs, ds_refs, dq_ref, mark_ref = refs[:n], refs[n : 2 * n], refs[2 * n], refs[2 * n + 1]
     mark_ref[...] = jnp.zeros_like(mark_ref)
-    rows, hd = kv_refs[0].shape[0], kv_refs[0].shape[1] // 2
+    rows, hd = k_refs[0].shape
     for h in range(dq_ref.shape[1] // hd):
         dq = 0.0
-        for kv, ds in zip(kv_refs, ds_refs):
+        for k, ds in zip(k_refs, ds_refs):
             part = ds[:, h * rows : (h + 1) * rows]
-            dq = dq + lax.dot_general(part, kv[:, :hd], TN, preferred_element_type=F32)
+            dq = dq + lax.dot_general(part, k[...], TN, preferred_element_type=F32)
         dq_ref[:, h * hd : (h + 1) * hd] = (dq / hd**0.5).astype(BF16)
 
 
-def attention(me, spans, queries, out_grad, pairs, swap, n):
-    rows, hd = pairs.shape[0], pairs.shape[1] // 2
+def relay_kernel(block_ref, out_ref):
+    out_ref[...] = block_ref[...]
+
+
+def merge_kernel(own_ref, got_ref, out_ref):
+    out_ref[...] = (own_ref[...].astype(F32) + got_ref[...].astype(F32)).astype(BF16)
+
+
+def small_call(kernel, name, operands, after):
+    x = operands[0]
+    return whole_call(kernel, name, [], operands, [shape(x.shape)], 4, (0, 6 * x.size), [], after)[0]
+
+
+def attention(me, spans, queries, out_grad, keys, values, swap, n):
+    rows, hd = keys.shape
     columns = queries.shape[1]
     tall = columns // hd * rows
     product = 2 * rows * tall * hd
-    cost = (4 * product, 8 * rows * columns)
-
-    blocks = [pairs]
-    for b in range(1, n):
-        blocks.append(swap(blocks[b & (b - 1)], b & -b))
+    cost = (8 * product, 8 * rows * columns)
+
+    direct = [b for b in range(1, n) if b & (b - 1) == 0]
+    blocks = {b: [swap(keys, b), swap(values, b)] for b in reversed(direct)}
     stats_shape = shape((8, tall), F32)
-    stats, queries, out_grad, flags = whole_call(
+    stats, queries, out_grad, keys, values, flags = whole_call(
         functools.partial(first_stats_kernel, n),
         "first_stats",
         [me, spans],
-        [queries, out_grad, pairs],
-        [stats_shape, shape(queries.shape), shape(out_grad.shape), shape((8, 128), F32)],
+        [queries, out_grad, keys, values],
+        [stats_shape] + [shape(x.shape) for x in (queries, out_grad, keys, values)] + [shape((8, 128), F32)],
         14,
         cost,
-    )
+        [],
+        [begin()],
+    )
+    blocks[0] = [keys, values]
     for b in range(1, n):
+        if b == 2:
+            values_on = small_call(relay_kernel, "relay", [blocks[2][1]], [stats])
+            blocks[3] = [swap(blocks[2][0], 1), swap(values_on, 1)]
+        if b not in blocks:
+            blocks[b] = [swap(x, b & -b) for x in blocks[b & (b - 1)]]
         stats = whole_call(
             functools.partial(next_stats_kernel, b),
             "next_stats",
             [],
-            [flags, queries, out_grad, blocks[b], stats],
+            [flags, queries, out_grad, *blocks[b], stats],
             [stats_shape],
             12,
             cost,
             [],
-            blocks[2:3] if b == 1 else [],
+            blocks[2][:1] if b == 1 else blocks[3][:1] if b == 2 else [],
         )[0]
-    received = blocks[1:]
     p_buf = pltpu.VMEM((rows, 2 * rows), BF16)
     sums = [pltpu.VMEM((rows, hd), F32)] * 2
-    parts, score_grads, before = [None] * (n - 1), [None] * (n - 1), []
+    parts, score_grads, before = [[] for _ in range(n)], [None] * n, []
     for b in range(n - 1, 0, -1):
-        part, score_grads[b - 1] = whole_call(
+        part, score_grads[b] = whole_call(
             functools.partial(other_kernel, b),
             "block_gradients",
             [],
-            [flags, stats, queries, out_grad, received[b - 1]],
+            [flags, stats, queries, out_grad, *blocks[b]],
             [shape((rows, 2 * hd)), shape((rows, tall))],
             14,
-            (8 * product, 16 * rows * columns),
+            (11 * product, 16 * rows * columns),
             [p_buf, *sums],
             before,
         )
-        parts[b - 1] = swap(part, b)
         before = [part]
-    own, own_score_grad = whole_call(
+        parts[b].insert(0, part)
+    arrived = []
+    for b in range(n - 1, 0, -1):
+        part, *got = parts[b]
+        for other in got:
+            part = small_call(merge_kernel, "merge", [part, other], [])
+            before = [part]
+        to = b & (b - 1)
+        (parts[to] if to else arrived).append(swap(part, b & -b))
+    own, score_grads[0] = whole_call(
         own_kernel,
         "own_gradients",
         [],
-        [stats, queries, out_grad, pairs],
+        [stats, queries, out_grad, keys, values],
         [shape((rows, 2 * hd), F32), shape((rows, tall))],
         14,
         (8 * product, 16 * rows * columns),
         [p_buf, *sums],
         before,
     )
-    return own, parts, blocks, [own_score_grad, *score_grads], before
-
-
-def query_gradients(blocks, score_grads, columns, after):
-    n = len(blocks)
-    rows, width = blocks[0].shape
+    return own, arrived, [blocks[b][0] for b in range(n)], score_grads, before
+
+
+def query_gradients(key_blocks, score_grads, columns, after):
+    n = len(key_blocks)
+    rows = key_blocks[0].shape[0]
     return whole_call(
         functools.partial(query_kernel, n),
         "query_gradients",
         [],
-        [*blocks, *score_grads],
+        [*key_blocks, *score_grads],
         [shape((rows, columns)), shape((8, 128), F32)],
         5 + 3 * n,
         (2 * n * rows * rows * columns, 16 * rows * columns),
@@ -537,20 +520,19 @@
     def swap_ctx(x, mask):
         return lax.ppermute(x, "context", xor_perm(n_ctx, mask))
 
-    pairs = load_call(join_kernel, "join_keys_values", [keys, values], [shape((rows, width))], 4)[0]
-    own, parts, blocks, score_grads, last_part = attention(
-        me_ctx, span_order[0], queries, out_grad, pairs, swap_ctx, n_ctx
-    )
-    acts, errors = prepare(activations, error_feedback[0, 0], last_part)
+    own, parts, key_blocks, score_grads, last_part = attention(
+        me_ctx, span_order[0], queries, out_grad, keys, values, swap_ctx, n_ctx
+    )
+    acts = prepare(activations, last_part)
 
     shrink = 1.0 / (n_dp * n_ctx)
     acts = acts.reshape(n_dp, n_ctx, sets, rows_set, rows)
-    errors = errors.reshape(n_dp, n_ctx, sets, rows_set, width)
+    errors = error_feedback.reshape(n_dp, n_ctx, sets, rows_set, width)
     tops = shape((TOP_ROWS, TOP_LANES), F32)
     steps = n_dp // 2
     cost = (2 * steps * tall * rows * width, steps * tall * (2 * rows + 6 * width))
     out, top, key_grad, value_grad, grads = whole_call(
-        functools.partial(first_send_kernel, bits, shrink, n_ctx - 1),
+        functools.partial(first_send_kernel, bits, shrink, len(parts)),
         "send_tiles",
         [me_dp],
         [own, *parts, acts, errors],
@@ -596,7 +578,7 @@
         )
         halves.append(arrays[:4])
     gathered = [arrays[4]]
-    query_grad, mark = query_gradients(blocks, score_grads, queries.shape[1], [arrays[1]])
+    query_grad, mark = query_gradients(key_blocks, score_grads, queries.shape[1], [arrays[1]])
     groups = []
     for chosen in range(sets):
         low_away, low, high_away, high = halves[chosen]

time: 85.8 us -> 83.4 us (0.972); the launches traced: 85.6 us -> 82.3 us
  Pallas kernels: 32.9 us -> 22.2 us
  starting transfers between devices: 28.4 us -> 38.9 us
  local copies, waits for them, and re-layouts: 6.78 us -> 4.18 us
    ppermute x12 -> x15, starting transfers between devices: 16.9 us -> 31.6 us  [swap_ctx(): return lax.ppermute(x, 'context', xor_perm(n_ctx, mask))]
    pallas_call x19 -> x23, Pallas kernels: 29.4 us -> 22.2 us  [whole_call(): pl.pallas_call(body, grid_spec=pltpu.PrefetchScalarGridSpec(num_scalar_pr...]
    ppermute x10, starting transfers between devices: 11.5 us -> 7.28 us  [swap_dp(): return lax.ppermute(x, 'dp', xor_perm(n_dp, mask))]
    pallas_call x2 -> x0, Pallas kernels: 3.57 us -> none  [the longest x1 3.51 us: prepare(): pl.pallas_call(functools.partial(prepare_kernel, pieces), in_specs=[hbm,...]
    ppermute x12 -> x15, waiting for transfers between devices: 11.4 us -> 8.16 us  [swap_ctx(): return lax.ppermute(x, 'context', xor_perm(n_ctx, mask))]
    ppermute x10, waiting for transfers between devices: 5.21 us -> 8.04 us  [swap_dp(): return lax.ppermute(x, 'dp', xor_perm(n_dp, mask))]
    unnamed x22 -> x24, local copies, waits for them, and re-layouts: 6.15 us -> 3.54 us
  transfers between devices with their start and end apart: 22 -> 25, of which waited for: 8 -> 10; matrix products, arithmetic and copies ran while one was open for 0% -> 0% of each run, Pallas kernels for 30% -> 24%
where the time goes in v7:
time: 83.4 us; the launch traced here: 82.3 us
  starting transfers between devices  38.9 us (47%)
  Pallas kernels  22.2 us (27%)
  waiting for transfers between devices  16.2 us (19%)
  local copies, waits for them, and re-layouts  4.18 us (5%)
  between operations  0.85 us (1%)
    ppermute x15, starting transfers between devices, swap_ctx(): return lax.ppermute(x, 'context', xor_perm(n_ctx, mask))  31.6 us
    pallas_call x23, Pallas kernels, whole_call(): pl.pallas_call(body, grid_spec=pltpu.PrefetchScalarGridSpec(num_scalar_pr...  22.2 us
    ppermute x15, waiting for transfers between devices, swap_ctx(): return lax.ppermute(x, 'context', xor_perm(n_ctx, mask))  8.16 us
    ppermute x10, waiting for transfers between devices, swap_dp(): return lax.ppermute(x, 'dp', xor_perm(n_dp, mask))  8.04 us
    ppermute x10, starting transfers between devices, swap_dp(): return lax.ppermute(x, 'dp', xor_perm(n_dp, mask))  7.28 us
    unnamed x24, local copies, waits for them, and re-layouts  3.54 us
  transfers between devices with their start and end apart: 25, of which 10 were waited for; matrix products, arithmetic and copies ran while one was open for 0% of the time, Pallas kernels for 24%

profile of v7, /device:TPU:0, one launch (start us, length us, event | category | flops | bytes accessed | tf_op | source)
XLA Modules:
  0.0 82.3 jit_solution(6693692256806861901)
XLA Ops:
  0.6 4.1 %collective-permute-start.1 = (bf16[384,128]{1,0:T(8,128)(2,1)}, bf16[384,128]{1,0:T(8,128)(2,1)S(1)}, u32[]{:S(2)}, u32[]{:S(2)}) collective-permute-start(bf16[384,128]{1,0:T(8,128)(2,1)} %refs_4_.1), channel_id=1, source_target_pairs={{0,2},{1,3},{2,0},{3,1},{4,6},{5,7},{6,4},{7,5},{8,10},{9,11},{10,... | collective-permute-start | bytes 294920 | tf_op jit(solution)/shard_map/ppermute | solution.py:521
  4.7 1.6 %collective-permute-start = (bf16[384,128]{1,0:T(8,128)(2,1)}, bf16[384,128]{1,0:T(8,128)(2,1)S(1)}, u32[]{:S(2)}, u32[]{:S(2)}) collective-permute-start(bf16[384,128]{1,0:T(8,128)(2,1)} %refs_4_.1), channel_id=1, source_target_pairs={{0,1},{1,0},{2,3},{3,2},{4,5},{5,4},{6,7},{7,6},{8,9},{9,8},{10,11... | collective-permute-start | bytes 294920 | tf_op jit(solution)/shard_map/ppermute | solution.py:521
  6.9 1.1 %copy-done = bf16[384,1024]{1,0:T(8,128)(2,1)S(1)} copy-done((bf16[384,1024]{1,0:T(8,128)(2,1)S(1)}, bf16[384,1024]{1,0:T(8,128)(2,1)}, u32[]{:S(2)}) %copy-start) | copy-done | bytes 786456
  8.2 2.4 %first_stats.1 = (f32[8,3072]{1,0:T(8,128)S(1)}, bf16[384,1024]{1,0:T(8,128)(2,1)S(1)}, bf16[384,1024]{1,0:T(8,128)(2,1)S(1)}, bf16[384,128]{1,0:T(8,128)(2,1)S(...) custom-call(s32[1]{0:T(128)} %bitcast.refs_0_.refs_1_, s32[4]{0:T(128)S(1)} %bitcast.15, ...), custom_call_target="tpu_custom_call" | custom-call | flops 2415919104 | bytes 3145728 | tf_op jit(solution)/shard_map/first_stats/pallas_call | solution.py:39
  11.5 1.8 %collective-permute-start.2 = (bf16[384,128]{1,0:T(8,128)(2,1)S(1)}, bf16[384,128]{1,0:T(8,128)(2,1)S(1)}, u32[]{:S(2)}, u32[]{:S(2)}) collective-permute-start(bf16[384,128]{1,0:T(8,128)(2,1)S(1)} %collective-permute-done.1.refs_6_.refs_3_.refs_4_.refs_2_), channel_id=1, source_target_pairs={{0,1},{1,0},{2,3},{3,2},{4,5},{5,4},{6,7},{7,6},{8,9},{9,8},{10,11... | collective-permute-start | bytes 294920 | tf_op jit(solution)/shard_map/ppermute | solution.py:521
  13.4 2.0 %collective-permute-done.4.refs_4_.refs_5_ = bf16[384,128]{1,0:T(8,128)(2,1)S(1)} collective-permute-done((bf16[384,128]{1,0:T(8,128)(2,1)}, bf16[384,128]{1,0:T(8,128)(2,1)S(1)}, u32[]{:S(2)}, u32[]{:S(2)}) %collective-permute-start.4) | collective-permute-done | bytes 98336 | tf_op jit(solution)/shard_map/ppermute | solution.py:521
  15.4 1.1 %copy-done.6 = bf16[384,1024]{1,0:T(8,128)(2,1)S(1)} copy-done((bf16[384,1024]{1,0:T(8,128)(2,1)S(1)}, bf16[384,1024]{1,0:T(8,128)(2,1)}, u32[]{:S(2)}) %copy-start.6) | copy-done | bytes 786456
  16.7 1.7 %collective-permute-start.5 = (bf16[384,128]{1,0:T(8,128)(2,1)S(1)}, bf16[384,128]{1,0:T(8,128)(2,1)S(1)}, u32[]{:S(2)}, u32[]{:S(2)}) collective-permute-start(bf16[384,128]{1,0:T(8,128)(2,1)S(1)} %relay.1), channel_id=1, source_target_pairs={{0,1},{1,0},{2,3},{3,2},{4,5},{5,4},{6,7},{7,6},{8,9},{9,8},{10,11... | collective-permute-start | bytes 294920 | tf_op jit(solution)/shard_map/ppermute | solution.py:521
  18.4 2.1 %next_stats.4.refs_5_ = f32[8,3072]{1,0:T(8,128)S(1)} custom-call(f32[8,128]{1,0:T(8,128)S(1)} %get-tuple-element.61.refs_0_, bf16[384,1024]{1,0:T(8,128)(2,1)S(1)} %get-tuple-element.62.refs_1_.refs_2_, bf16[384,1024]{1,0:T(8,128)(2,1)S(1)} %copy-done.6, bf16[384,128]{1,0:T(8,128)(2,1)S(1)} %collective-permute-done.1.refs_6_.refs_3_.refs_4_.refs_2_, ...), custom_call_target="tpu_custom_call" | custom-call | flops 2415919104 | bytes 3145728 | tf_op jit(solution)/shard_map/next_stats/pallas_call | solution.py:39
  22.0 6.1 %collective-permute-start.6 = (bf16[384,256]{1,0:T(8,128)(2,1)S(1)}, bf16[384,256]{1,0:T(8,128)(2,1)S(1)}, u32[]{:S(2)}, u32[]{:S(2)}) collective-permute-start(bf16[384,256]{1,0:T(8,128)(2,1)S(1)} %get-tuple-element.66.refs_6_), channel_id=1, source_target_pairs={{0,1},{1,0},{2,3},{3,2},{4,5},{5,4},{6,7},{7,6},{8,9},{9,8},{10,11... | collective-permute-start | bytes 589832 | tf_op jit(solution)/shard_map/ppermute | solution.py:521
  28.0 2.9 %block_gradients.4 = (bf16[384,256]{1,0:T(8,128)(2,1)S(1)}, bf16[384,3072]{1,0:T(8,128)(2,1)S(1)}) custom-call(f32[8,128]{1,0:T(8,128)S(1)} %get-tuple-element.61.refs_0_, f32[8,3072]{1,0:T(8,128)S(1)} %next_stats.5.refs_1_.refs_0_, bf16[384,1024]{1,0:T(8,128)(2,1)S(1)} %get-tuple-element.62.refs_1_.refs_2_, bf16[384,1024]{1,0:T(8,128)(2,1)S(1)} %copy-done.7, ...), custom_call_target="tpu_custom_call" | custom-call | flops 3321888768 | bytes 6291456 | tf_op jit(solution)/shard_map/block_gradients/pallas_call | solution.py:39
  31.3 2.6 %collective-permute-start.8 = (bf16[384,256]{1,0:T(8,128)(2,1)S(1)}, bf16[384,256]{1,0:T(8,128)(2,1)S(1)}, u32[]{:S(2)}, u32[]{:S(2)}) collective-permute-start(bf16[384,256]{1,0:T(8,128)(2,1)S(1)} %get-tuple-element.73), channel_id=1, source_target_pairs={{0,1},{1,0},{2,3},{3,2},{4,5},{5,4},{6,7},{7,6},{8,9},{9,8},{10,11... | collective-permute-start | bytes 589832 | tf_op jit(solution)/shard_map/ppermute | solution.py:521
  33.9 2.6 %collective-permute-start.7 = (bf16[384,256]{1,0:T(8,128)(2,1)S(1)}, bf16[384,256]{1,0:T(8,128)(2,1)S(1)}, u32[]{:S(2)}, u32[]{:S(2)}) collective-permute-start(bf16[384,256]{1,0:T(8,128)(2,1)S(1)} %merge.1.refs_5_.refs_1_), channel_id=1, source_target_pairs={{0,2},{1,3},{2,0},{3,1},{4,6},{5,7},{6,4},{7,5},{8,10},{9,11},{10,... | collective-permute-start | bytes 589832 | tf_op jit(solution)/shard_map/ppermute | solution.py:521
  36.6 1.7 %prepare.1 = bf16[8192,384]{1,0:T(8,128)(2,1)S(1)} custom-call(bf16[384,8192]{1,0:T(8,128)(2,1)S(1)} %bitcast.14, bf16[384,256]{1,0:T(8,128)(2,1)S(1)} %merge.1.refs_5_.refs_1_), custom_call_target="tpu_custom_call" | custom-call | bytes 12582912 | tf_op jit(solution)/shard_map/prepare/pallas_call | solution.py:39
  38.2 2.6 %own_gradients.1 = (f32[384,256]{1,0:T(8,128)S(1)}, bf16[384,3072]{1,0:T(8,128)(2,1)S(1)}) custom-call(f32[8,3072]{1,0:T(8,128)S(1)} %next_stats.5.refs_1_.refs_0_, bf16[384,1024]{1,0:T(8,128)(2,1)S(1)} %get-tuple-element.62.refs_1_.refs_2_, bf16[384,1024]{1,0:T(8,128)(2,1)S(1)} %copy-done.7, bf16[384,128]{1,0:T(8,128)(2,1)S(1)} %get-tuple-element.60.refs_3_.refs_0_, ...), custom_call_target="tpu_custom_call" | custom-call | flops 2415919104 | bytes 6291456 | tf_op jit(solution)/shard_map/own_gradients/pallas_call | solution.py:39
  40.9 2.6 %collective-permute-done.7.refs_2_ = bf16[384,256]{1,0:T(8,128)(2,1)S(1)} collective-permute-done((bf16[384,256]{1,0:T(8,128)(2,1)S(1)}, bf16[384,256]{1,0:T(8,128)(2,1)S(1)}, u32[]{:S(2)}, u32[]{:S(2)}) %collective-permute-start.7) | collective-permute-done | bytes 196640 | tf_op jit(solution)/shard_map/ppermute | solution.py:521
  43.5 1.3 %send_tiles.2 = (bf16[2048,256]{1,0:T(8,128)(2,1)S(1)}, f32[16,128]{1,0:T(8,128)S(1)}, bf16[384,128]{1,0:T(8,128)(2,1)}, bf16[384,128]{1,0:T(8,128)(2,1)}, bf16[384,256]{1,0:T(8,128)(2,1)S(1)}) custom-call(s32[1]{0:T(128)} %bitcast.2.refs_0_, f32[384,256]{1,0:T(8,128)S(1)} %get-tuple-element.72.refs_1_, bf16[384,256]{1,0:T(8,128)(2,1)S(1)} %collective-permute-done.7.refs_2_, ...), custom_call_target="tpu_custom_call" | custom-call | flops 402653184 | bytes 4718592 | tf_op jit(solution)/shard_map/send_tiles/pallas_call | solution.py:39
  44.8 1.4 %kept_tiles.1 = (f32[4,512,256]{2,1,0:T(8,128)S(1)}, f32[4,512,256]{2,1,0:T(8,128)S(1)}, f32[16,128]{1,0:T(8,128)S(1)}) custom-call(s32[1]{0:T(128)} %bitcast.2.refs_0_, bf16[384,256]{1,0:T(8,128)(2,1)S(1)} %get-tuple-element.74.refs_1_, f32[16,128]{1,0:T(8,128)S(1)} %get-tuple-element.75.refs_2_, bf16[8,4,2,128,384]{4,3,2,1,0:T(8,128)(2,1)S(1)} %bitcast.6, ...), custom_call_target="tpu_custom_call" | custom-call | flops 805306368 | bytes 9437184 | tf_op jit(solution)/shard_map/kept_tiles/pallas_call | solution.py:39
  46.2 0.9 %send_tiles.3 = (bf16[2064,256]{1,0:T(8,128)(2,1)S(1)}, f32[16,128]{1,0:T(8,128)S(1)}) custom-call(s32[1]{0:T(128)} %bitcast.2.refs_0_, bf16[384,256]{1,0:T(8,128)(2,1)S(1)} %get-tuple-element.74.refs_1_, f32[16,128]{1,0:T(8,128)S(1)} %get-tuple-element.77.refs_2_, bf16[8,4,2,128,384]{4,3,2,1,0:T(8,128)(2,1)S(1)} %bitcast.7, f32[8,4,2,128,256]{4,3,2,1,0:T(8,128)S(1)} %bitcast.12), custom_call_target="tpu_custom_call" | custom-call | flops 402653184 | bytes 4718592 | tf_op jit(solution)/shard_map/send_tiles/pallas_call | solution.py:39
  48.0 1.6 %collective-permute-start.11 = (bf16[1024,128]{1,0:T(8,128)(2,1)S(1)}, bf16[1024,128]{1,0:T(8,128)(2,1)S(1)}, u32[]{:S(2)}, u32[]{:S(2)}) collective-permute-start(bf16[1024,128]{1,0:T(8,128)(2,1)S(1)} %get-tuple-element.87), channel_id=1, source_target_pairs={{0,8},{4,12},{8,0},{12,4},{16,24},{20,28},{24,16},{28,20},{1,9},{5... | collective-permute-start | bytes 786440 | tf_op jit(solution)/shard_map/ppermute | solution.py:518
  50.6 1.5 %collective-permute-start.18 = (bf16[1040,128]{1,0:T(8,128)(2,1)S(1)}, bf16[1040,128]{1,0:T(8,128)(2,1)S(1)}, u32[]{:S(2)}, u32[]{:S(2)}) collective-permute-start(bf16[1040,128]{1,0:T(8,128)(2,1)S(1)} %get-tuple-element.99), channel_id=1, source_target_pairs={{0,8},{4,12},{8,0},{12,4},{16,24},{20,28},{24,16},{28,20},{1,9},{5... | collective-permute-start | bytes 798728 | tf_op jit(solution)/shard_map/ppermute | solution.py:518
  52.6 3.8 %query_gradients.1 = (bf16[384,1024]{1,0:T(8,128)(2,1)}, f32[8,128]{1,0:T(8,128)S(1)}) custom-call(bf16[384,128]{1,0:T(8,128)(2,1)S(1)} %get-tuple-element.60.refs_3_.refs_0_, bf16[384,128]{1,0:T(8,128)(2,1)S(1)} %collective-permute-done.refs_3_.refs_4_.refs_1_, bf16[384,128]{1,0:T(8,128)(2,1)S(1)} %collective-permute-done.1.refs_6_.refs_3_.refs_4_.refs_2_, ...), custom_call_target="tpu_custom_call" | custom-call | flops 1207959552 | bytes 6291456 | tf_op jit(solution)/shard_map/query_gradients/pallas_call | solution.py:39
  57.2 1.6 %collective-permute-done.12.refs_3_ = bf16[1024,128]{1,0:T(8,128)(2,1)S(1)} collective-permute-done((bf16[1024,128]{1,0:T(8,128)(2,1)S(1)}, bf16[1024,128]{1,0:T(8,128)(2,1)S(1)}, u32[]{:S(2)}, u32[]{:S(2)}) %collective-permute-start.12) | collective-permute-done | bytes 262176 | tf_op jit(solution)/shard_map/ppermute | solution.py:518
  60.2 4.2 %collective-permute-done.19.refs_3_ = bf16[1024,128]{1,0:T(8,128)(2,1)S(1)} collective-permute-done((bf16[1024,128]{1,0:T(8,128)(2,1)S(1)}, bf16[1024,128]{1,0:T(8,128)(2,1)S(1)}, u32[]{:S(2)}, u32[]{:S(2)}) %collective-permute-start.19) | collective-permute-done | bytes 262176 | tf_op jit(solution)/shard_map/ppermute | solution.py:518
  66.0 1.0 %collective-permute-done.13.refs_2_ = bf16[512,128]{1,0:T(8,128)(2,1)S(1)} collective-permute-done((bf16[512,128]{1,0:T(8,128)(2,1)S(1)}, bf16[512,128]{1,0:T(8,128)(2,1)S(1)}, u32[]{:S(2)}, u32[]{:S(2)}) %collective-permute-start.13) | collective-permute-done | bytes 131104 | tf_op jit(solution)/shard_map/ppermute | solution.py:518
  67.0 2.9 %collective-permute-start.15 = (bf16[256,128]{1,0:T(8,128)(2,1)S(1)}, bf16[256,128]{1,0:T(8,128)(2,1)S(1)}, u32[]{:S(2)}, u32[]{:S(2)}) collective-permute-start(bf16[256,128]{1,0:T(8,128)(2,1)S(1)} %get-tuple-element.96), channel_id=1, source_target_pairs={{0,3},{1,2},{2,1},{3,0},{4,7},{5,6},{6,5},{7,4},{8,11},{9,10},{10,... | collective-permute-start | bytes 196616 | tf_op jit(solution)/shard_map/ppermute | solution.py:521
  70.5 2.8 %collective-permute-start.22 = (bf16[272,128]{1,0:T(8,128)(2,1)S(1)}, bf16[272,128]{1,0:T(8,128)(2,1)S(1)}, u32[]{:S(2)}, u32[]{:S(2)}) collective-permute-start(bf16[272,128]{1,0:T(8,128)(2,1)S(1)} %get-tuple-element.109), channel_id=1, source_target_pairs={{0,3},{1,2},{2,1},{3,0},{4,7},{5,6},{6,5},{7,4},{8,11},{9,10},{10,... | collective-permute-start | bytes 208904 | tf_op jit(solution)/shard_map/ppermute | solution.py:521
  73.3 1.6 %collective-permute-start.24 = (bf16[272,128]{1,0:T(8,128)(2,1)S(1)}, bf16[272,128]{1,0:T(8,128)(2,1)S(1)}, u32[]{:S(2)}, u32[]{:S(2)}) collective-permute-start(bf16[272,128]{1,0:T(8,128)(2,1)S(1)} %get-tuple-element.111), channel_id=1, source_target_pairs={{0,1},{1,0},{2,3},{3,2},{4,5},{5,4},{6,7},{7,6},{8,9},{9,8},{10,11... | collective-permute-start | bytes 208904 | tf_op jit(solution)/shard_map/ppermute | solution.py:521
  74.9 1.3 %collective-permute-start.16 = (bf16[256,128]{1,0:T(8,128)(2,1)S(1)}, bf16[256,128]{1,0:T(8,128)(2,1)S(1)}, u32[]{:S(2)}, u32[]{:S(2)}) collective-permute-start(bf16[256,128]{1,0:T(8,128)(2,1)S(1)} %get-tuple-element.97), channel_id=1, source_target_pairs={{0,2},{1,3},{2,0},{3,1},{4,6},{5,7},{6,4},{7,5},{8,10},{9,11},{10,... | collective-permute-start | bytes 196616 | tf_op jit(solution)/shard_map/ppermute | solution.py:521
  76.2 2.0 %collective-permute-start.17 = (bf16[256,128]{1,0:T(8,128)(2,1)S(1)}, bf16[256,128]{1,0:T(8,128)(2,1)S(1)}, u32[]{:S(2)}, u32[]{:S(2)}) collective-permute-start(bf16[256,128]{1,0:T(8,128)(2,1)S(1)} %get-tuple-element.98), channel_id=1, source_target_pairs={{0,1},{1,0},{2,3},{3,2},{4,5},{5,4},{6,7},{7,6},{8,9},{9,8},{10,11... | collective-permute-start | bytes 196616 | tf_op jit(solution)/shard_map/ppermute | solution.py:521
  78.2 2.6 %collective-permute-done.16.refs_4_ = bf16[256,128]{1,0:T(8,128)(2,1)S(1)} collective-permute-done((bf16[256,128]{1,0:T(8,128)(2,1)S(1)}, bf16[256,128]{1,0:T(8,128)(2,1)S(1)}, u32[]{:S(2)}, u32[]{:S(2)}) %collective-permute-start.16) | collective-permute-done | bytes 65568 | tf_op jit(solution)/shard_map/ppermute | solution.py:521
  80.8 0.9 %final_stage.1 = (f32[256,256]{1,0:T(8,128)}, f32[8,32]{1,0:T(8,128)S(1)}) custom-call(s32[1]{0:T(128)} %bitcast.2.refs_0_, s32[1]{0:T(128)} %bitcast.refs_0_.refs_1_, f32[256,128]{1,0:T(8,128)S(1)} %get-tuple-element.95.refs_2_, bf16[256,128]{1,0:T(8,128)(2,1)S(1)} %collective-permute-done.15.refs_3_, bf16[256,128]{1,0:T(8,128)(2,1)S(1)} %collective-permute-done.16.refs_4_, ...), custom_call_target="tpu_custom_call" | custom-call | flops 1048576 | bytes 1048576 | tf_op jit(solution)/shard_map/final_stage/pallas_call | solution.py:39
  (68 shorter events, 10.9 us)
Async XLA Ops:
  0.6 10.9 %collective-permute-start.1 = (bf16[384,128]{1,0:T(8,128)(2,1)}, bf16[384,128]{1,0:T(8,128)(2,1)S(1)}, u32[]{:S(2)}, u32[]{:S(2)}) collective-permute-start(bf16[384,128]{1,0:T(8,128)(2,1)} %refs_4_.1), channel_id=1, source_target_pairs={{0,2},{1,3},{2,0},{3,1},{4,6},{5,7},{6,4},{7,5},{8,10},{9,11},{10,... | collective-permute-start | bytes 294920 | tf_op jit(solution)/shard_map/ppermute | solution.py:521
  4.7 8.7 %collective-permute-start = (bf16[384,128]{1,0:T(8,128)(2,1)}, bf16[384,128]{1,0:T(8,128)(2,1)S(1)}, u32[]{:S(2)}, u32[]{:S(2)}) collective-permute-start(bf16[384,128]{1,0:T(8,128)(2,1)} %refs_4_.1), channel_id=1, source_target_pairs={{0,1},{1,0},{2,3},{3,2},{4,5},{5,4},{6,7},{7,6},{8,9},{9,8},{10,11... | collective-permute-start | bytes 294920 | tf_op jit(solution)/shard_map/ppermute | solution.py:521
  6.3 9.1 %collective-permute-start.4 = (bf16[384,128]{1,0:T(8,128)(2,1)}, bf16[384,128]{1,0:T(8,128)(2,1)S(1)}, u32[]{:S(2)}, u32[]{:S(2)}) collective-permute-start(bf16[384,128]{1,0:T(8,128)(2,1)} %refs_5_.1), channel_id=1, source_target_pairs={{0,1},{1,0},{2,3},{3,2},{4,5},{5,4},{6,7},{7,6},{8,9},{9,8},{10,11... | collective-permute-start | bytes 294920 | tf_op jit(solution)/shard_map/ppermute | solution.py:521
  6.8 9.9 %collective-permute-start.3 = (bf16[384,128]{1,0:T(8,128)(2,1)}, bf16[384,128]{1,0:T(8,128)(2,1)S(1)}, u32[]{:S(2)}, u32[]{:S(2)}) collective-permute-start(bf16[384,128]{1,0:T(8,128)(2,1)} %refs_5_.1), channel_id=1, source_target_pairs={{0,2},{1,3},{2,0},{3,1},{4,6},{5,7},{6,4},{7,5},{8,10},{9,11},{10,... | collective-permute-start | bytes 294920 | tf_op jit(solution)/shard_map/ppermute | solution.py:521
  6.8 1.4 %copy-start.2 = (bf16[384,128]{1,0:T(8,128)(2,1)S(1)}, bf16[384,128]{1,0:T(8,128)(2,1)}, u32[]{:S(2)}) copy-start(bf16[384,128]{1,0:T(8,128)(2,1)} %refs_4_.1) | copy-start | bytes 294916
  6.8 1.4 %copy-start.3 = (bf16[384,128]{1,0:T(8,128)(2,1)S(1)}, bf16[384,128]{1,0:T(8,128)(2,1)}, u32[]{:S(2)}) copy-start(bf16[384,128]{1,0:T(8,128)(2,1)} %refs_5_.1) | copy-start | bytes 294916
  6.9 1.4 %copy-start.4 = (s32[1,4]{1,0:T(1,128)S(1)}, s32[1,4]{1,0:T(1,128)}, u32[]{:S(2)}) copy-start(s32[1,4]{1,0:T(1,128)} %param.7) | copy-start | bytes 52
  11.5 6.9 %collective-permute-start.2 = (bf16[384,128]{1,0:T(8,128)(2,1)S(1)}, bf16[384,128]{1,0:T(8,128)(2,1)S(1)}, u32[]{:S(2)}, u32[]{:S(2)}) collective-permute-start(bf16[384,128]{1,0:T(8,128)(2,1)S(1)} %collective-permute-done.1.refs_6_.refs_3_.refs_4_.refs_2_), channel_id=1, source_target_pairs={{0,1},{1,0},{2,3},{3,2},{4,5},{5,4},{6,7},{7,6},{8,9},{9,8},{10,11... | collective-permute-start | bytes 294920 | tf_op jit(solution)/shard_map/ppermute | solution.py:521
  16.7 4.7 %collective-permute-start.5 = (bf16[384,128]{1,0:T(8,128)(2,1)S(1)}, bf16[384,128]{1,0:T(8,128)(2,1)S(1)}, u32[]{:S(2)}, u32[]{:S(2)}) collective-permute-start(bf16[384,128]{1,0:T(8,128)(2,1)S(1)} %relay.1), channel_id=1, source_target_pairs={{0,1},{1,0},{2,3},{3,2},{4,5},{5,4},{6,7},{7,6},{8,9},{9,8},{10,11... | collective-permute-start | bytes 294920 | tf_op jit(solution)/shard_map/ppermute | solution.py:521
  22.0 11.9 %collective-permute-start.6 = (bf16[384,256]{1,0:T(8,128)(2,1)S(1)}, bf16[384,256]{1,0:T(8,128)(2,1)S(1)}, u32[]{:S(2)}, u32[]{:S(2)}) collective-permute-start(bf16[384,256]{1,0:T(8,128)(2,1)S(1)} %get-tuple-element.66.refs_6_), channel_id=1, source_target_pairs={{0,1},{1,0},{2,3},{3,2},{4,5},{5,4},{6,7},{7,6},{8,9},{9,8},{10,11... | collective-permute-start | bytes 589832 | tf_op jit(solution)/shard_map/ppermute | solution.py:521
  31.0 5.6 %slice-start.2 = ((s8[6291456]{0:T(1024)(128)(4,1)}), s8[4194304]{0:T(1024)(128)(4,1)S(1)}, s32[]{:S(2)}) async-start(s8[6291456]{0:T(1024)(128)(4,1)} %bitcast.13), calls=%async_computation.2 | async-start | bytes 8388608
  31.0 5.6 %slice-start.3 = ((s8[6291456]{0:T(1024)(128)(4,1)}), s8[2097152]{0:T(1024)(128)(4,1)S(1)}, s32[]{:S(2)}) async-start(s8[6291456]{0:T(1024)(128)(4,1)} %bitcast.13), calls=%async_computation.3 | async-start | bytes 4194304
  31.3 9.6 %collective-permute-start.8 = (bf16[384,256]{1,0:T(8,128)(2,1)S(1)}, bf16[384,256]{1,0:T(8,128)(2,1)S(1)}, u32[]{:S(2)}, u32[]{:S(2)}) collective-permute-start(bf16[384,256]{1,0:T(8,128)(2,1)S(1)} %get-tuple-element.73), channel_id=1, source_target_pairs={{0,1},{1,0},{2,3},{3,2},{4,5},{5,4},{6,7},{7,6},{8,9},{9,8},{10,11... | collective-permute-start | bytes 589832 | tf_op jit(solution)/shard_map/ppermute | solution.py:521
  33.9 9.7 %slice-start = ((s8[8388608]{0:T(1024)(128)(4,1)}), s8[4194304]{0:T(1024)(128)(4,1)S(1)}, s32[]{:S(2)}) async-start(s8[8388608]{0:T(1024)(128)(4,1)} %bitcast.8), calls=%async_computation | async-start | bytes 8388608
  33.9 9.6 %slice-start.1 = ((s8[8388608]{0:T(1024)(128)(4,1)}), s8[4194304]{0:T(1024)(128)(4,1)S(1)}, s32[]{:S(2)}) async-start(s8[8388608]{0:T(1024)(128)(4,1)} %bitcast.8), calls=%async_computation.1 | async-start | bytes 8388608
  33.9 9.6 %collective-permute-start.7 = (bf16[384,256]{1,0:T(8,128)(2,1)S(1)}, bf16[384,256]{1,0:T(8,128)(2,1)S(1)}, u32[]{:S(2)}, u32[]{:S(2)}) collective-permute-start(bf16[384,256]{1,0:T(8,128)(2,1)S(1)} %merge.1.refs_5_.refs_1_), channel_id=1, source_target_pairs={{0,2},{1,3},{2,0},{3,1},{4,6},{5,7},{6,4},{7,5},{8,10},{9,11},{10,... | collective-permute-start | bytes 589832 | tf_op jit(solution)/shard_map/ppermute | solution.py:521
  44.8 2.9 %collective-permute-start.10 = (bf16[2048,256]{1,0:T(8,128)(2,1)S(1)}, bf16[2048,256]{1,0:T(8,128)(2,1)S(1)}, u32[]{:S(2)}, u32[]{:S(2)}) collective-permute-start(bf16[2048,256]{1,0:T(8,128)(2,1)S(1)} %get-tuple-element.85), channel_id=1, source_target_pairs={{0,4},{4,0},{8,12},{12,8},{16,20},{20,16},{24,28},{28,24},{1,5},{5... | collective-permute-start | bytes 3145736 | tf_op jit(solution)/shard_map/ppermute | solution.py:518
  47.2 3.0 %collective-permute-start.9 = (bf16[2064,256]{1,0:T(8,128)(2,1)S(1)}, bf16[2064,256]{1,0:T(8,128)(2,1)S(1)}, u32[]{:S(2)}, u32[]{:S(2)}) collective-permute-start(bf16[2064,256]{1,0:T(8,128)(2,1)S(1)} %get-tuple-element.78), channel_id=1, source_target_pairs={{0,4},{4,0},{8,12},{12,8},{16,20},{20,16},{24,28},{28,24},{1,5},{5... | collective-permute-start | bytes 3170312 | tf_op jit(solution)/shard_map/ppermute | solution.py:518
  48.0 9.2 %collective-permute-start.11 = (bf16[1024,128]{1,0:T(8,128)(2,1)S(1)}, bf16[1024,128]{1,0:T(8,128)(2,1)S(1)}, u32[]{:S(2)}, u32[]{:S(2)}) collective-permute-start(bf16[1024,128]{1,0:T(8,128)(2,1)S(1)} %get-tuple-element.87), channel_id=1, source_target_pairs={{0,8},{4,12},{8,0},{12,4},{16,24},{20,28},{24,16},{28,20},{1,9},{5... | collective-permute-start | bytes 786440 | tf_op jit(solution)/shard_map/ppermute | solution.py:518
  49.6 9.2 %collective-permute-start.12 = (bf16[1024,128]{1,0:T(8,128)(2,1)S(1)}, bf16[1024,128]{1,0:T(8,128)(2,1)S(1)}, u32[]{:S(2)}, u32[]{:S(2)}) collective-permute-start(bf16[1024,128]{1,0:T(8,128)(2,1)S(1)} %get-tuple-element.89), channel_id=1, source_target_pairs={{0,16},{4,20},{8,24},{12,28},{16,0},{20,4},{24,8},{28,12},{1,17},{... | collective-permute-start | bytes 786440 | tf_op jit(solution)/shard_map/ppermute | solution.py:518
  50.6 13.9 %collective-permute-start.18 = (bf16[1040,128]{1,0:T(8,128)(2,1)S(1)}, bf16[1040,128]{1,0:T(8,128)(2,1)S(1)}, u32[]{:S(2)}, u32[]{:S(2)}) collective-permute-start(bf16[1040,128]{1,0:T(8,128)(2,1)S(1)} %get-tuple-element.99), channel_id=1, source_target_pairs={{0,8},{4,12},{8,0},{12,4},{16,24},{20,28},{24,16},{28,20},{1,9},{5... | collective-permute-start | bytes 798728 | tf_op jit(solution)/shard_map/ppermute | solution.py:518
  52.1 12.4 %collective-permute-start.19 = (bf16[1024,128]{1,0:T(8,128)(2,1)S(1)}, bf16[1024,128]{1,0:T(8,128)(2,1)S(1)}, u32[]{:S(2)}, u32[]{:S(2)}) collective-permute-start(bf16[1024,128]{1,0:T(8,128)(2,1)S(1)} %get-tuple-element.101), channel_id=1, source_target_pairs={{0,16},{4,20},{8,24},{12,28},{16,0},{20,4},{24,8},{28,12},{1,17},{... | collective-permute-start | bytes 786440 | tf_op jit(solution)/shard_map/ppermute | solution.py:518
  59.0 8.0 %collective-permute-start.13 = (bf16[512,128]{1,0:T(8,128)(2,1)S(1)}, bf16[512,128]{1,0:T(8,128)(2,1)S(1)}, u32[]{:S(2)}, u32[]{:S(2)}) collective-permute-start(bf16[512,128]{1,0:T(8,128)(2,1)S(1)} %get-tuple-element.92), channel_id=1, source_target_pairs={{0,16},{4,20},{8,24},{12,28},{16,0},{20,4},{24,8},{28,12},{1,17},{... | collective-permute-start | bytes 393224 | tf_op jit(solution)/shard_map/ppermute | solution.py:518
  59.6 7.4 %collective-permute-start.14 = (bf16[512,128]{1,0:T(8,128)(2,1)S(1)}, bf16[512,128]{1,0:T(8,128)(2,1)S(1)}, u32[]{:S(2)}, u32[]{:S(2)}) collective-permute-start(bf16[512,128]{1,0:T(8,128)(2,1)S(1)} %get-tuple-element.94), channel_id=1, source_target_pairs={{0,8},{4,12},{8,0},{12,4},{16,24},{20,28},{24,16},{28,20},{1,9},{5... | collective-permute-start | bytes 393224 | tf_op jit(solution)/shard_map/ppermute | solution.py:518
  64.7 5.6 %collective-permute-start.20 = (bf16[528,128]{1,0:T(8,128)(2,1)S(1)}, bf16[528,128]{1,0:T(8,128)(2,1)S(1)}, u32[]{:S(2)}, u32[]{:S(2)}) collective-permute-start(bf16[528,128]{1,0:T(8,128)(2,1)S(1)} %get-tuple-element.104), channel_id=1, source_target_pairs={{0,16},{4,20},{8,24},{12,28},{16,0},{20,4},{24,8},{28,12},{1,17},{... | collective-permute-start | bytes 405512 | tf_op jit(solution)/shard_map/ppermute | solution.py:518
  65.3 5.0 %collective-permute-start.21 = (bf16[512,128]{1,0:T(8,128)(2,1)S(1)}, bf16[512,128]{1,0:T(8,128)(2,1)S(1)}, u32[]{:S(2)}, u32[]{:S(2)}) collective-permute-start(bf16[512,128]{1,0:T(8,128)(2,1)S(1)} %get-tuple-element.106), channel_id=1, source_target_pairs={{0,8},{4,12},{8,0},{12,4},{16,24},{20,28},{24,16},{28,20},{1,9},{5... | collective-permute-start | bytes 393224 | tf_op jit(solution)/shard_map/ppermute | solution.py:518
  67.0 9.1 %collective-permute-start.15 = (bf16[256,128]{1,0:T(8,128)(2,1)S(1)}, bf16[256,128]{1,0:T(8,128)(2,1)S(1)}, u32[]{:S(2)}, u32[]{:S(2)}) collective-permute-start(bf16[256,128]{1,0:T(8,128)(2,1)S(1)} %get-tuple-element.96), channel_id=1, source_target_pairs={{0,3},{1,2},{2,1},{3,0},{4,7},{5,6},{6,5},{7,4},{8,11},{9,10},{10,... | collective-permute-start | bytes 196616 | tf_op jit(solution)/shard_map/ppermute | solution.py:521
  70.5 10.3 %collective-permute-start.22 = (bf16[272,128]{1,0:T(8,128)(2,1)S(1)}, bf16[272,128]{1,0:T(8,128)(2,1)S(1)}, u32[]{:S(2)}, u32[]{:S(2)}) collective-permute-start(bf16[272,128]{1,0:T(8,128)(2,1)S(1)} %get-tuple-element.109), channel_id=1, source_target_pairs={{0,3},{1,2},{2,1},{3,0},{4,7},{5,6},{6,5},{7,4},{8,11},{9,10},{10,... | collective-permute-start | bytes 208904 | tf_op jit(solution)/shard_map/ppermute | solution.py:521
  73.2 7.5 %collective-permute-start.23 = (bf16[272,128]{1,0:T(8,128)(2,1)S(1)}, bf16[272,128]{1,0:T(8,128)(2,1)S(1)}, u32[]{:S(2)}, u32[]{:S(2)}) collective-permute-start(bf16[272,128]{1,0:T(8,128)(2,1)S(1)} %get-tuple-element.110), channel_id=1, source_target_pairs={{0,2},{1,3},{2,0},{3,1},{4,6},{5,7},{6,4},{7,5},{8,10},{9,11},{10,... | collective-permute-start | bytes 208904 | tf_op jit(solution)/shard_map/ppermute | solution.py:521
  73.3 7.5 %collective-permute-start.24 = (bf16[272,128]{1,0:T(8,128)(2,1)S(1)}, bf16[272,128]{1,0:T(8,128)(2,1)S(1)}, u32[]{:S(2)}, u32[]{:S(2)}) collective-permute-start(bf16[272,128]{1,0:T(8,128)(2,1)S(1)} %get-tuple-element.111), channel_id=1, source_target_pairs={{0,1},{1,0},{2,3},{3,2},{4,5},{5,4},{6,7},{7,6},{8,9},{9,8},{10,11... | collective-permute-start | bytes 208904 | tf_op jit(solution)/shard_map/ppermute | solution.py:521
  74.9 5.9 %collective-permute-start.16 = (bf16[256,128]{1,0:T(8,128)(2,1)S(1)}, bf16[256,128]{1,0:T(8,128)(2,1)S(1)}, u32[]{:S(2)}, u32[]{:S(2)}) collective-permute-start(bf16[256,128]{1,0:T(8,128)(2,1)S(1)} %get-tuple-element.97), channel_id=1, source_target_pairs={{0,2},{1,3},{2,0},{3,1},{4,6},{5,7},{6,4},{7,5},{8,10},{9,11},{10,... | collective-permute-start | bytes 196616 | tf_op jit(solution)/shard_map/ppermute | solution.py:521
  76.2 4.6 %collective-permute-start.17 = (bf16[256,128]{1,0:T(8,128)(2,1)S(1)}, bf16[256,128]{1,0:T(8,128)(2,1)S(1)}, u32[]{:S(2)}, u32[]{:S(2)}) collective-permute-start(bf16[256,128]{1,0:T(8,128)(2,1)S(1)} %get-tuple-element.98), channel_id=1, source_target_pairs={{0,1},{1,0},{2,3},{3,2},{4,5},{5,4},{6,7},{7,6},{8,9},{9,8},{10,11... | collective-permute-start | bytes 196616 | tf_op jit(solution)/shard_map/ppermute | solution.py:521
  (5 other events, 5.7 us)

commit v8 on v7

--- a/solution.py
+++ b/solution.py
@@ -70,7 +70,7 @@
 def prepare(activations, after):
     rows, model = activations.shape
     outs = [shape((model, rows))]
-    cost = (0, 4 * rows * model)
+    cost = (0, 0)
     kernel = functools.partial(prepare_kernel, 8)
     return whole_call(kernel, "prepare", [], [activations], outs, 16, cost, [], after)[0]
 
@@ -221,17 +221,15 @@
         dq_ref[:, h * hd : (h + 1) * hd] = (dq / hd**0.5).astype(BF16)
 
 
-def relay_kernel(block_ref, out_ref):
-    out_ref[...] = block_ref[...]
-
-
-def merge_kernel(own_ref, got_ref, out_ref):
-    out_ref[...] = (own_ref[...].astype(F32) + got_ref[...].astype(F32)).astype(BF16)
-
-
-def small_call(kernel, name, operands, after):
-    x = operands[0]
-    return whole_call(kernel, name, [], operands, [shape(x.shape)], 4, (0, 6 * x.size), [], after)[0]
+def merge_kernel(rows, own_ref, got_ref, out_ref):
+    out_ref[:rows, :] = (own_ref[:rows, :].astype(F32) + got_ref[:rows, :].astype(F32)).astype(BF16)
+    out_ref[rows:, :] = jnp.zeros((out_ref.shape[0] - rows, out_ref.shape[1]), BF16)
+
+
+def merge(own, got, rows, after):
+    outs = [shape((rows + TOP_ROWS, own.shape[1]))]
+    kernel = functools.partial(merge_kernel, rows)
+    return whole_call(kernel, "merge", [], [own, got], outs, 4, (0, 6 * own.size), [], after)[0]
 
 
 def attention(me, spans, queries, out_grad, keys, values, swap, n):
@@ -257,9 +255,6 @@
     )
     blocks[0] = [keys, values]
     for b in range(1, n):
-        if b == 2:
-            values_on = small_call(relay_kernel, "relay", [blocks[2][1]], [stats])
-            blocks[3] = [swap(blocks[2][0], 1), swap(values_on, 1)]
         if b not in blocks:
             blocks[b] = [swap(x, b & -b) for x in blocks[b & (b - 1)]]
         stats = whole_call(
@@ -271,10 +266,23 @@
             12,
             cost,
             [],
-            blocks[2][:1] if b == 1 else blocks[3][:1] if b == 2 else [],
+            blocks[2] if b == 1 else [],
         )[0]
     p_buf = pltpu.VMEM((rows, 2 * rows), BF16)
     sums = [pltpu.VMEM((rows, hd), F32)] * 2
+    def own_call(after):
+        return whole_call(
+            own_kernel,
+            "own_gradients",
+            [],
+            [stats, queries, out_grad, keys, values],
+            [shape((rows, 2 * hd), F32), shape((rows, tall))],
+            14,
+            (11 * product, 16 * rows * columns),
+            [p_buf, *sums],
+            after,
+        )
+
     parts, score_grads, before = [[] for _ in range(n)], [None] * n, []
     for b in range(n - 1, 0, -1):
         part, score_grads[b] = whole_call(
@@ -288,28 +296,14 @@
             [p_buf, *sums],
             before,
         )
+        if b == min(2, n - 1):
+            own, score_grads[0] = own_call([part])
+        for other in parts[b]:
+            part = merge(part, other, rows, [own] if b == 2 else [])
         before = [part]
-        parts[b].insert(0, part)
-    arrived = []
-    for b in range(n - 1, 0, -1):
-        part, *got = parts[b]
-        for other in got:
-            part = small_call(merge_kernel, "merge", [part, other], [])
-            before = [part]
         to = b & (b - 1)
-        (parts[to] if to else arrived).append(swap(part, b & -b))
-    own, score_grads[0] = whole_call(
-        own_kernel,
-        "own_gradients",
-        [],
-        [stats, queries, out_grad, keys, values],
-        [shape((rows, 2 * hd), F32), shape((rows, tall))],
-        14,
-        (8 * product, 16 * rows * columns),
-        [p_buf, *sums],
-        before,
-    )
-    return own, arrived, [blocks[b][0] for b in range(n)], score_grads, before
+        parts[to].append(swap(part, b & -b))
+    return own, parts[0], [blocks[b][0] for b in range(n)], score_grads, before
 
 
 def query_gradients(key_blocks, score_grads, columns, after):
@@ -391,7 +385,7 @@
     a_ref, e_ref, out_ref, top_ref, kg_ref, vg_ref, grads_ref = refs[n_parts:]
     total = own_ref[...]
     for part in part_refs:
-        total = total + part[...].astype(F32)
+        total = total + part[: total.shape[0], :].astype(F32)
     total = total.astype(BF16)
     hd = total.shape[1] // 2
     kg_ref[...] = total[:, :hd]
@@ -472,12 +466,13 @@
         for at, mine, got in ((0, low, low_got), (rows_set, high, high_got)):
             total = mine[part, :].astype(F32) + got[part, :].astype(F32)
             outs[b][at : at + rows_set, :] = total.astype(outs[b].dtype)
-        if b > 0 and tops:
-            outs[b][2 * rows_set :, :] = packed
+        if b > 0:
+            tail = outs[b].shape[0] - 2 * rows_set
+            outs[b][2 * rows_set :, :] = packed if tops else jnp.zeros((tail, hd), BF16)
 
 
 def final_kernel(sets, n_ctx, gain, me_dp_ref, me_ctx_ref, *refs):
-    groups = [refs[chosen * n_ctx : (chosen + 1) * n_ctx] for chosen in range(sets)]
+    groups = [refs[chosen * n_ctx : (chosen + 1) * n_ctx] for chosen in range(sets)][::-1]
     top_ref, out_ref, scale_ref, all_tops = refs[sets * n_ctx :]
     n_dp, lanes = scale_ref.shape
     rows_set, hd = groups[0][0].shape[0] // 2, groups[0][0].shape[1]
@@ -537,7 +532,7 @@
         [me_dp],
         [own, *parts, acts, errors],
         [shape((steps * tall, width)), tops, shape((rows, hd)), shape((rows, hd)), shape((rows, width))],
-        22,
+        18,
         cost,
     )
     got = [swap_dp(out, 1)]
@@ -547,7 +542,7 @@
         [me_dp],
         [grads, top, acts, errors],
         [shape((steps, tall, width), F32)] * sets + [tops],
-        24,
+        20,
         (sets * cost[0], sets * cost[1]),
     )
     for chosen in range(1, sets):
@@ -558,7 +553,7 @@
             [me_dp],
             [grads, top, acts, errors],
             [shape((steps * tall + extra, width)), tops],
-            22,
+            18,
             cost,
         )
         got.append(swap_dp(out, 1))
@@ -609,7 +604,7 @@
                     [me_ctx],
                     operands,
                     [shape((2 * rows_set, hd), F32)]
-                    + [shape((2 * rows_set + extra, hd))] * (n_ctx - 1)
+                    + [shape((2 * rows_set + (extra or 2 * TOP_ROWS), hd))] * (n_ctx - 1)
                     + [tops] * with_tops,
                     8,
                     cost,
@@ -622,7 +617,7 @@
         functools.partial(final_kernel, sets, n_ctx, 7.0 / shrink),
         "final_stage",
         [me_dp, me_ctx],
-        [x for group in groups for x in group] + gathered,
+        [x for group in groups[::-1] for x in group] + gathered,
         [shape((sets * rows_set, width), F32), shape((n_dp, sets * tall // QROWS), F32)],
         8,
         (4 * sets * tall * width, 16 * sets * rows_set * width),

time: 83.4 us -> 92.4 us (1.11)
  local copies, waits for them, and re-layouts: 4.18 us -> 13.9 us
  starting transfers between devices: 38.9 us -> 33.6 us
  Pallas kernels: 22.2 us -> 26.6 us
    unnamed x24 -> x46, local copies, waits for them, and re-layouts: 3.54 us -> 13.3 us
    ppermute x15, starting transfers between devices: 31.6 us -> 22.5 us  [swap_ctx(): return lax.ppermute(x, 'context', xor_perm(n_ctx, mask))]
    pallas_call x23 -> x22, Pallas kernels: 22.2 us -> 26.6 us  [whole_call(): pl.pallas_call(body, grid_spec=pltpu.PrefetchScalarGridSpec(num_scalar_pr...]
    ppermute x10, starting transfers between devices: 7.28 us -> 11 us  [swap_dp(): return lax.ppermute(x, 'dp', xor_perm(n_dp, mask))]
    ppermute x15, waiting for transfers between devices: 8.16 us -> 10.9 us  [swap_ctx(): return lax.ppermute(x, 'context', xor_perm(n_ctx, mask))]
    ppermute x10, waiting for transfers between devices: 8.04 us -> 6.26 us  [swap_dp(): return lax.ppermute(x, 'dp', xor_perm(n_dp, mask))]
  transfers between devices with their start and end apart: 25 -> 25, of which waited for: 10 -> 11; matrix products, arithmetic and copies ran while one was open for 0% -> 0% of each run, Pallas kernels for 24% -> 26%
where the time goes in v8:
time: 92.4 us; the launch traced here: 92.2 us
  starting transfers between devices  33.6 us (36%)
  Pallas kernels  26.6 us (29%)
  waiting for transfers between devices  17.1 us (19%)
  local copies, waits for them, and re-layouts  13.9 us (15%)
  between operations  0.95 us (1%)
    pallas_call x22, Pallas kernels, whole_call(): pl.pallas_call(body, grid_spec=pltpu.PrefetchScalarGridSpec(num_scalar_pr...  26.6 us
    ppermute x15, starting transfers between devices, swap_ctx(): return lax.ppermute(x, 'context', xor_perm(n_ctx, mask))  22.5 us
    unnamed x46, local copies, waits for them, and re-layouts  13.3 us
    ppermute x10, starting transfers between devices, swap_dp(): return lax.ppermute(x, 'dp', xor_perm(n_dp, mask))  11 us
    ppermute x15, waiting for transfers between devices, swap_ctx(): return lax.ppermute(x, 'context', xor_perm(n_ctx, mask))  10.9 us
    ppermute x10, waiting for transfers between devices, swap_dp(): return lax.ppermute(x, 'dp', xor_perm(n_dp, mask))  6.26 us
  transfers between devices with their start and end apart: 25, of which 11 were waited for; matrix products, arithmetic and copies ran while one was open for 0% of the time, Pallas kernels for 26%

profile of v8, /device:TPU:0, one launch (start us, length us, event | category | flops | bytes accessed | tf_op | source)
XLA Modules:
  0.0 92.2 jit_solution(16151010018943803651)
XLA Ops:
  0.6 4.1 %collective-permute-start.1 = (bf16[384,128]{1,0:T(8,128)(2,1)}, bf16[384,128]{1,0:T(8,128)(2,1)S(1)}, u32[]{:S(2)}, u32[]{:S(2)}) collective-permute-start(bf16[384,128]{1,0:T(8,128)(2,1)} %refs_4_.1), channel_id=1, source_target_pairs={{0,2},{1,3},{2,0},{3,1},{4,6},{5,7},{6,4},{7,5},{8,10},{9,11},{10,... | collective-permute-start | bytes 294920 | tf_op jit(solution)/shard_map/ppermute | solution.py:516
  4.7 1.6 %collective-permute-start = (bf16[384,128]{1,0:T(8,128)(2,1)}, bf16[384,128]{1,0:T(8,128)(2,1)S(1)}, u32[]{:S(2)}, u32[]{:S(2)}) collective-permute-start(bf16[384,128]{1,0:T(8,128)(2,1)} %refs_4_.1), channel_id=1, source_target_pairs={{0,1},{1,0},{2,3},{3,2},{4,5},{5,4},{6,7},{7,6},{8,9},{9,8},{10,11... | collective-permute-start | bytes 294920 | tf_op jit(solution)/shard_map/ppermute | solution.py:516
  8.2 2.4 %first_stats.1 = (f32[8,3072]{1,0:T(8,128)S(1)}, bf16[384,1024]{1,0:T(8,128)(2,1)S(1)}, bf16[384,1024]{1,0:T(8,128)(2,1)S(1)}, bf16[384,128]{1,0:T(8,128)(2,1)S(...) custom-call(s32[1]{0:T(128)} %bitcast.refs_0_.refs_1_, s32[4]{0:T(128)S(1)} %bitcast.13, ...), custom_call_target="tpu_custom_call" | custom-call | flops 2415919104 | bytes 3145728 | tf_op jit(solution)/shard_map/first_stats/pallas_call | solution.py:39
  10.6 1.9 %collective-permute-start.2 = (bf16[384,128]{1,0:T(8,128)(2,1)S(1)}, bf16[384,128]{1,0:T(8,128)(2,1)S(1)}, u32[]{:S(2)}, u32[]{:S(2)}) collective-permute-start(bf16[384,128]{1,0:T(8,128)(2,1)S(1)} %collective-permute-done.1.refs_6_.refs_3_.refs_4_.refs_2_), channel_id=1, source_target_pairs={{0,1},{1,0},{2,3},{3,2},{4,5},{5,4},{6,7},{7,6},{8,9},{9,8},{10,11... | collective-permute-start | bytes 294920 | tf_op jit(solution)/shard_map/ppermute | solution.py:516
  12.5 1.4 %collective-permute-done.3.refs_7_.refs_4_.refs_5_ = bf16[384,128]{1,0:T(8,128)(2,1)S(1)} collective-permute-done((bf16[384,128]{1,0:T(8,128)(2,1)}, bf16[384,128]{1,0:T(8,128)(2,1)S(1)}, u32[]{:S(2)}, u32[]{:S(2)}) %collective-permute-start.3) | collective-permute-done | bytes 98336 | tf_op jit(solution)/shard_map/ppermute | solution.py:516
  15.4 2.1 %next_stats.3.refs_5_ = f32[8,3072]{1,0:T(8,128)S(1)} custom-call(f32[8,128]{1,0:T(8,128)S(1)} %get-tuple-element.61.refs_0_, bf16[384,1024]{1,0:T(8,128)(2,1)S(1)} %get-tuple-element.62.refs_1_.refs_2_, bf16[384,1024]{1,0:T(8,128)(2,1)S(1)} %get-tuple-element.63.refs_2_.refs_3_, bf16[384,128]{1,0:T(8,128)(2,1)S(1)} %collective-permute-done.refs_3_.refs_4_.refs_1_, ...), custom_call_target="tpu_custom_call" | custom-call | flops 2415919104 | bytes 3145728 | tf_op jit(solution)/shard_map/next_stats/pallas_call | solution.py:39
  17.5 2.1 %next_stats.4.refs_5_ = f32[8,3072]{1,0:T(8,128)S(1)} custom-call(f32[8,128]{1,0:T(8,128)S(1)} %get-tuple-element.61.refs_0_, bf16[384,1024]{1,0:T(8,128)(2,1)S(1)} %get-tuple-element.62.refs_1_.refs_2_, bf16[384,1024]{1,0:T(8,128)(2,1)S(1)} %get-tuple-element.63.refs_2_.refs_3_, bf16[384,128]{1,0:T(8,128)(2,1)S(1)} %collective-permute-done.1.refs_6_.refs_3_.refs_4_.refs_2_, ...), custom_call_target="tpu_custom_call" | custom-call | flops 2415919104 | bytes 3145728 | tf_op jit(solution)/shard_map/next_stats/pallas_call | solution.py:39
  20.6 2.9 %block_gradients.4 = (bf16[384,256]{1,0:T(8,128)(2,1)S(1)}, bf16[384,3072]{1,0:T(8,128)(2,1)S(1)}) custom-call(f32[8,128]{1,0:T(8,128)S(1)} %get-tuple-element.61.refs_0_, f32[8,3072]{1,0:T(8,128)S(1)} %next_stats.5.refs_1_.refs_0_, bf16[384,1024]{1,0:T(8,128)(2,1)S(1)} %get-tuple-element.62.refs_1_.refs_2_, ...), custom_call_target="tpu_custom_call" | custom-call | flops 3321888768 | bytes 6291456 | tf_op jit(solution)/shard_map/block_gradients/pallas_call | solution.py:39
  23.6 1.4 %copy-done.2 = bf16[384,3072]{1,0:T(8,128)(2,1)} copy-done((bf16[384,3072]{1,0:T(8,128)(2,1)}, bf16[384,3072]{1,0:T(8,128)(2,1)S(1)}, u32[]{:S(2)}) %copy-start.2) | copy-done | bytes 2359320
  25.0 2.6 %own_gradients.1 = (f32[384,256]{1,0:T(8,128)S(1)}, bf16[384,3072]{1,0:T(8,128)(2,1)S(1)}) custom-call(f32[8,3072]{1,0:T(8,128)S(1)} %next_stats.5.refs_1_.refs_0_, bf16[384,1024]{1,0:T(8,128)(2,1)S(1)} %get-tuple-element.62.refs_1_.refs_2_, bf16[384,1024]{1,0:T(8,128)(2,1)S(1)} %get-tuple-element.63.refs_2_.refs_3_, ...), custom_call_target="tpu_custom_call" | custom-call | flops 3321888768 | bytes 6291456 | tf_op jit(solution)/shard_map/own_gradients/pallas_call | solution.py:39
  27.6 1.5 %copy-done.4 = bf16[384,3072]{1,0:T(8,128)(2,1)} copy-done((bf16[384,3072]{1,0:T(8,128)(2,1)}, bf16[384,3072]{1,0:T(8,128)(2,1)S(1)}, u32[]{:S(2)}) %copy-start.4) | copy-done | bytes 2359320
  29.1 4.8 %collective-permute-start.7 = (bf16[400,256]{1,0:T(8,128)(2,1)S(1)}, bf16[400,256]{1,0:T(8,128)(2,1)S(1)}, u32[]{:S(2)}, u32[]{:S(2)}) collective-permute-start(bf16[400,256]{1,0:T(8,128)(2,1)S(1)} %merge.1.refs_6_), channel_id=1, source_target_pairs={{0,2},{1,3},{2,0},{3,1},{4,6},{5,7},{6,4},{7,5},{8,10},{9,11},{10,... | collective-permute-start | bytes 614408 | tf_op jit(solution)/shard_map/ppermute | solution.py:516
  33.9 3.0 %block_gradients.5 = (bf16[384,256]{1,0:T(8,128)(2,1)S(1)}, bf16[384,3072]{1,0:T(8,128)(2,1)S(1)}) custom-call(f32[8,128]{1,0:T(8,128)S(1)} %get-tuple-element.61.refs_0_, f32[8,3072]{1,0:T(8,128)S(1)} %next_stats.5.refs_1_.refs_0_, bf16[384,1024]{1,0:T(8,128)(2,1)S(1)} %get-tuple-element.62.refs_1_.refs_2_, ...), custom_call_target="tpu_custom_call" | custom-call | flops 3321888768 | bytes 6291456 | tf_op jit(solution)/shard_map/block_gradients/pallas_call | solution.py:39
  37.0 1.4 %copy-done.6 = bf16[384,3072]{1,0:T(8,128)(2,1)} copy-done((bf16[384,3072]{1,0:T(8,128)(2,1)}, bf16[384,3072]{1,0:T(8,128)(2,1)S(1)}, u32[]{:S(2)}) %copy-start.6) | copy-done | bytes 2359320
  38.6 2.8 %copy-done.1 = bf16[384,8192]{1,0:T(8,128)(2,1)S(1)} copy-done((bf16[384,8192]{1,0:T(8,128)(2,1)S(1)}, bf16[384,8192]{1,0:T(8,128)(2,1)}, u32[]{:S(2)}) %copy-start.1) | copy-done | bytes 6291480
  41.4 1.7 %prepare.1 = bf16[8192,384]{1,0:T(8,128)(2,1)S(1)} custom-call(bf16[384,8192]{1,0:T(8,128)(2,1)S(1)} %copy-done.1, bf16[384,256]{1,0:T(8,128)(2,1)S(1)} %get-tuple-element.73.refs_1_), custom_call_target="tpu_custom_call" | custom-call | tf_op jit(solution)/shard_map/prepare/pallas_call | solution.py:39
  43.1 3.3 %collective-permute-done.8.refs_3_ = bf16[384,256]{1,0:T(8,128)(2,1)S(1)} collective-permute-done((bf16[384,256]{1,0:T(8,128)(2,1)S(1)}, bf16[384,256]{1,0:T(8,128)(2,1)S(1)}, u32[]{:S(2)}, u32[]{:S(2)}) %collective-permute-start.8) | collective-permute-done | bytes 196640 | tf_op jit(solution)/shard_map/ppermute | solution.py:516
  46.4 3.4 %copy-done = f32[1,1,8192,256]{3,2,1,0:T(8,128)S(1)} copy-done((f32[1,1,8192,256]{3,2,1,0:T(8,128)S(1)}, f32[1,1,8192,256]{3,2,1,0:T(8,128)}, u32[]{:S(2)}) %copy-start) | copy-done | bytes 8388632
  52.0 1.4 %kept_tiles.1 = (f32[4,512,256]{2,1,0:T(8,128)S(1)}, f32[4,512,256]{2,1,0:T(8,128)S(1)}, f32[16,128]{1,0:T(8,128)S(1)}) custom-call(s32[1]{0:T(128)} %bitcast.2.refs_0_, bf16[384,256]{1,0:T(8,128)(2,1)S(1)} %get-tuple-element.74.refs_1_, f32[16,128]{1,0:T(8,128)S(1)} %get-tuple-element.75.refs_2_, bf16[8,4,2,128,384]{4,3,2,1,0:T(8,128)(2,1)S(1)} %bitcast.6, ...), custom_call_target="tpu_custom_call" | custom-call | flops 805306368 | bytes 9437184 | tf_op jit(solution)/shard_map/kept_tiles/pallas_call | solution.py:39
  54.8 4.4 %collective-permute-start.18 = (bf16[1024,128]{1,0:T(8,128)(2,1)S(1)}, bf16[1024,128]{1,0:T(8,128)(2,1)S(1)}, u32[]{:S(2)}, u32[]{:S(2)}) collective-permute-start(bf16[1024,128]{1,0:T(8,128)(2,1)S(1)} %get-tuple-element.100), channel_id=1, source_target_pairs={{0,8},{4,12},{8,0},{12,4},{16,24},{20,28},{24,16},{28,20},{1,9},{5... | collective-permute-start | bytes 786440 | tf_op jit(solution)/shard_map/ppermute | solution.py:513
  59.7 2.2 %collective-permute-start.10 = (bf16[1040,128]{1,0:T(8,128)(2,1)S(1)}, bf16[1040,128]{1,0:T(8,128)(2,1)S(1)}, u32[]{:S(2)}, u32[]{:S(2)}) collective-permute-start(bf16[1040,128]{1,0:T(8,128)(2,1)S(1)} %get-tuple-element.84), channel_id=1, source_target_pairs={{0,8},{4,12},{8,0},{12,4},{16,24},{20,28},{24,16},{28,20},{1,9},{5... | collective-permute-start | bytes 798728 | tf_op jit(solution)/shard_map/ppermute | solution.py:513
  62.1 3.6 %query_gradients.1 = (bf16[384,1024]{1,0:T(8,128)(2,1)}, f32[8,128]{1,0:T(8,128)S(1)}) custom-call(bf16[384,128]{1,0:T(8,128)(2,1)S(1)} %copy-done.13, bf16[384,128]{1,0:T(8,128)(2,1)S(1)} %copy-done.11, bf16[384,128]{1,0:T(8,128)(2,1)S(1)} %copy-done.9, bf16[384,128]{1,0:T(8,128)(2,1)S(1)} %copy-done.15, bf16[384,3072]{1,0:T(8,128)(2,1)S(1)} %copy-done.5, ...), custom_call_target="tpu_custom_call" | custom-call | flops 1207959552 | bytes 6291456 | tf_op jit(solution)/shard_map/query_gradients/pallas_call | solution.py:39
  66.3 2.0 %collective-permute-done.19.refs_3_ = bf16[1024,128]{1,0:T(8,128)(2,1)S(1)} collective-permute-done((bf16[1024,128]{1,0:T(8,128)(2,1)S(1)}, bf16[1024,128]{1,0:T(8,128)(2,1)S(1)}, u32[]{:S(2)}, u32[]{:S(2)}) %collective-permute-start.19) | collective-permute-done | bytes 262176 | tf_op jit(solution)/shard_map/ppermute | solution.py:513
  68.6 2.0 %collective-permute-start.21 = (bf16[512,128]{1,0:T(8,128)(2,1)S(1)}, bf16[512,128]{1,0:T(8,128)(2,1)S(1)}, u32[]{:S(2)}, u32[]{:S(2)}) collective-permute-start(bf16[512,128]{1,0:T(8,128)(2,1)S(1)} %get-tuple-element.107), channel_id=1, source_target_pairs={{0,8},{4,12},{8,0},{12,4},{16,24},{20,28},{24,16},{28,20},{1,9},{5... | collective-permute-start | bytes 393224 | tf_op jit(solution)/shard_map/ppermute | solution.py:513
  70.5 3.4 %collective-permute-done.11.refs_3_ = bf16[1024,128]{1,0:T(8,128)(2,1)S(1)} collective-permute-done((bf16[1024,128]{1,0:T(8,128)(2,1)S(1)}, bf16[1024,128]{1,0:T(8,128)(2,1)S(1)}, u32[]{:S(2)}, u32[]{:S(2)}) %collective-permute-start.11) | collective-permute-done | bytes 262176 | tf_op jit(solution)/shard_map/ppermute | solution.py:513
  74.3 2.0 %collective-permute-start.13 = (bf16[512,128]{1,0:T(8,128)(2,1)S(1)}, bf16[512,128]{1,0:T(8,128)(2,1)S(1)}, u32[]{:S(2)}, u32[]{:S(2)}) collective-permute-start(bf16[512,128]{1,0:T(8,128)(2,1)S(1)} %get-tuple-element.91), channel_id=1, source_target_pairs={{0,8},{4,12},{8,0},{12,4},{16,24},{20,28},{24,16},{28,20},{1,9},{5... | collective-permute-start | bytes 393224 | tf_op jit(solution)/shard_map/ppermute | solution.py:513
  76.5 1.4 %collective-permute-start.22 = (bf16[288,128]{1,0:T(8,128)(2,1)S(1)}, bf16[288,128]{1,0:T(8,128)(2,1)S(1)}, u32[]{:S(2)}, u32[]{:S(2)}) collective-permute-start(bf16[288,128]{1,0:T(8,128)(2,1)S(1)} %get-tuple-element.109), channel_id=1, source_target_pairs={{0,3},{1,2},{2,1},{3,0},{4,7},{5,6},{6,5},{7,4},{8,11},{9,10},{10,... | collective-permute-start | bytes 221192 | tf_op jit(solution)/shard_map/ppermute | solution.py:516
  77.9 3.1 %collective-permute-start.24 = (bf16[288,128]{1,0:T(8,128)(2,1)S(1)}, bf16[288,128]{1,0:T(8,128)(2,1)S(1)}, u32[]{:S(2)}, u32[]{:S(2)}) collective-permute-start(bf16[288,128]{1,0:T(8,128)(2,1)S(1)} %get-tuple-element.111), channel_id=1, source_target_pairs={{0,1},{1,0},{2,3},{3,2},{4,5},{5,4},{6,7},{7,6},{8,9},{9,8},{10,11... | collective-permute-start | bytes 221192 | tf_op jit(solution)/shard_map/ppermute | solution.py:516
  81.2 1.4 %collective-permute-start.14 = (bf16[272,128]{1,0:T(8,128)(2,1)S(1)}, bf16[272,128]{1,0:T(8,128)(2,1)S(1)}, u32[]{:S(2)}, u32[]{:S(2)}) collective-permute-start(bf16[272,128]{1,0:T(8,128)(2,1)S(1)} %get-tuple-element.94), channel_id=1, source_target_pairs={{0,3},{1,2},{2,1},{3,0},{4,7},{5,6},{6,5},{7,4},{8,11},{9,10},{10,... | collective-permute-start | bytes 208904 | tf_op jit(solution)/shard_map/ppermute | solution.py:516
  83.2 2.4 %collective-permute-start.16 = (bf16[272,128]{1,0:T(8,128)(2,1)S(1)}, bf16[272,128]{1,0:T(8,128)(2,1)S(1)}, u32[]{:S(2)}, u32[]{:S(2)}) collective-permute-start(bf16[272,128]{1,0:T(8,128)(2,1)S(1)} %get-tuple-element.96), channel_id=1, source_target_pairs={{0,1},{1,0},{2,3},{3,2},{4,5},{5,4},{6,7},{7,6},{8,9},{9,8},{10,11... | collective-permute-start | bytes 208904 | tf_op jit(solution)/shard_map/ppermute | solution.py:516
  85.6 1.5 %collective-permute-done.23.refs_8_ = bf16[288,128]{1,0:T(8,128)(2,1)S(1)} collective-permute-done((bf16[288,128]{1,0:T(8,128)(2,1)S(1)}, bf16[288,128]{1,0:T(8,128)(2,1)S(1)}, u32[]{:S(2)}, u32[]{:S(2)}) %collective-permute-start.23) | collective-permute-done | bytes 73760 | tf_op jit(solution)/shard_map/ppermute | solution.py:516
  87.8 2.8 %collective-permute-done.15.refs_4_ = bf16[272,128]{1,0:T(8,128)(2,1)S(1)} collective-permute-done((bf16[272,128]{1,0:T(8,128)(2,1)S(1)}, bf16[272,128]{1,0:T(8,128)(2,1)S(1)}, u32[]{:S(2)}, u32[]{:S(2)}) %collective-permute-start.15) | collective-permute-done | bytes 69664 | tf_op jit(solution)/shard_map/ppermute | solution.py:516
  (88 shorter events, 13.5 us)
Async XLA Ops:
  0.6 10.0 %collective-permute-start.1 = (bf16[384,128]{1,0:T(8,128)(2,1)}, bf16[384,128]{1,0:T(8,128)(2,1)S(1)}, u32[]{:S(2)}, u32[]{:S(2)}) collective-permute-start(bf16[384,128]{1,0:T(8,128)(2,1)} %refs_4_.1), channel_id=1, source_target_pairs={{0,2},{1,3},{2,0},{3,1},{4,6},{5,7},{6,4},{7,5},{8,10},{9,11},{10,... | collective-permute-start | bytes 294920 | tf_op jit(solution)/shard_map/ppermute | solution.py:516
  4.7 10.2 %collective-permute-start = (bf16[384,128]{1,0:T(8,128)(2,1)}, bf16[384,128]{1,0:T(8,128)(2,1)S(1)}, u32[]{:S(2)}, u32[]{:S(2)}) collective-permute-start(bf16[384,128]{1,0:T(8,128)(2,1)} %refs_4_.1), channel_id=1, source_target_pairs={{0,1},{1,0},{2,3},{3,2},{4,5},{5,4},{6,7},{7,6},{8,9},{9,8},{10,11... | collective-permute-start | bytes 294920 | tf_op jit(solution)/shard_map/ppermute | solution.py:516
  6.3 7.6 %collective-permute-start.3 = (bf16[384,128]{1,0:T(8,128)(2,1)}, bf16[384,128]{1,0:T(8,128)(2,1)S(1)}, u32[]{:S(2)}, u32[]{:S(2)}) collective-permute-start(bf16[384,128]{1,0:T(8,128)(2,1)} %refs_5_.1), channel_id=1, source_target_pairs={{0,2},{1,3},{2,0},{3,1},{4,6},{5,7},{6,4},{7,5},{8,10},{9,11},{10,... | collective-permute-start | bytes 294920 | tf_op jit(solution)/shard_map/ppermute | solution.py:516
  6.6 8.8 %collective-permute-start.5 = (bf16[384,128]{1,0:T(8,128)(2,1)}, bf16[384,128]{1,0:T(8,128)(2,1)S(1)}, u32[]{:S(2)}, u32[]{:S(2)}) collective-permute-start(bf16[384,128]{1,0:T(8,128)(2,1)} %refs_5_.1), channel_id=1, source_target_pairs={{0,1},{1,0},{2,3},{3,2},{4,5},{5,4},{6,7},{7,6},{8,9},{9,8},{10,11... | collective-permute-start | bytes 294920 | tf_op jit(solution)/shard_map/ppermute | solution.py:516
  10.6 14.4 %copy-start.12 = (bf16[384,128]{1,0:T(8,128)(2,1)}, bf16[384,128]{1,0:T(8,128)(2,1)S(1)}, u32[]{:S(2)}) copy-start(bf16[384,128]{1,0:T(8,128)(2,1)S(1)} %get-tuple-element.60.refs_3_.refs_0_) | copy-start | bytes 294916
  10.6 10.0 %copy-start.8 = (bf16[384,128]{1,0:T(8,128)(2,1)}, bf16[384,128]{1,0:T(8,128)(2,1)S(1)}, u32[]{:S(2)}) copy-start(bf16[384,128]{1,0:T(8,128)(2,1)S(1)} %collective-permute-done.1.refs_6_.refs_3_.refs_4_.refs_2_) | copy-start | bytes 294916
  10.6 8.9 %collective-permute-start.2 = (bf16[384,128]{1,0:T(8,128)(2,1)S(1)}, bf16[384,128]{1,0:T(8,128)(2,1)S(1)}, u32[]{:S(2)}, u32[]{:S(2)}) collective-permute-start(bf16[384,128]{1,0:T(8,128)(2,1)S(1)} %collective-permute-done.1.refs_6_.refs_3_.refs_4_.refs_2_), channel_id=1, source_target_pairs={{0,1},{1,0},{2,3},{3,2},{4,5},{5,4},{6,7},{7,6},{8,9},{9,8},{10,11... | collective-permute-start | bytes 294920 | tf_op jit(solution)/shard_map/ppermute | solution.py:516
  13.9 5.6 %collective-permute-start.4 = (bf16[384,128]{1,0:T(8,128)(2,1)S(1)}, bf16[384,128]{1,0:T(8,128)(2,1)S(1)}, u32[]{:S(2)}, u32[]{:S(2)}) collective-permute-start(bf16[384,128]{1,0:T(8,128)(2,1)S(1)} %collective-permute-done.3.refs_7_.refs_4_.refs_5_), channel_id=1, source_target_pairs={{0,1},{1,0},{2,3},{3,2},{4,5},{5,4},{6,7},{7,6},{8,9},{9,8},{10,11... | collective-permute-start | bytes 294920 | tf_op jit(solution)/shard_map/ppermute | solution.py:516
  14.9 19.1 %copy-start.10 = (bf16[384,128]{1,0:T(8,128)(2,1)}, bf16[384,128]{1,0:T(8,128)(2,1)S(1)}, u32[]{:S(2)}) copy-start(bf16[384,128]{1,0:T(8,128)(2,1)S(1)} %collective-permute-done.refs_3_.refs_4_.refs_1_) | copy-start | bytes 294916
  20.5 8.6 %collective-permute-start.6 = (bf16[384,256]{1,0:T(8,128)(2,1)S(1)}, bf16[384,256]{1,0:T(8,128)(2,1)S(1)}, u32[]{:S(2)}, u32[]{:S(2)}) collective-permute-start(bf16[384,256]{1,0:T(8,128)(2,1)S(1)} %get-tuple-element.66.refs_6_), channel_id=1, source_target_pairs={{0,1},{1,0},{2,3},{3,2},{4,5},{5,4},{6,7},{7,6},{8,9},{9,8},{10,11... | collective-permute-start | bytes 589832 | tf_op jit(solution)/shard_map/ppermute | solution.py:516
  29.1 17.2 %collective-permute-start.7 = (bf16[400,256]{1,0:T(8,128)(2,1)S(1)}, bf16[400,256]{1,0:T(8,128)(2,1)S(1)}, u32[]{:S(2)}, u32[]{:S(2)}) collective-permute-start(bf16[400,256]{1,0:T(8,128)(2,1)S(1)} %merge.1.refs_6_), channel_id=1, source_target_pairs={{0,2},{1,3},{2,0},{3,1},{4,6},{5,7},{6,4},{7,5},{8,10},{9,11},{10,... | collective-permute-start | bytes 614408 | tf_op jit(solution)/shard_map/ppermute | solution.py:516
  38.3 8.0 %collective-permute-start.8 = (bf16[384,256]{1,0:T(8,128)(2,1)S(1)}, bf16[384,256]{1,0:T(8,128)(2,1)S(1)}, u32[]{:S(2)}, u32[]{:S(2)}) collective-permute-start(bf16[384,256]{1,0:T(8,128)(2,1)S(1)} %get-tuple-element.73.refs_1_), channel_id=1, source_target_pairs={{0,1},{1,0},{2,3},{3,2},{4,5},{5,4},{6,7},{7,6},{8,9},{9,8},{10,11... | collective-permute-start | bytes 589832 | tf_op jit(solution)/shard_map/ppermute | solution.py:516
  41.4 9.7 %slice-start = ((s8[8388608]{0:T(1024)(128)(4,1)}), s8[4194304]{0:T(1024)(128)(4,1)S(1)}, s32[]{:S(2)}) async-start(s8[8388608]{0:T(1024)(128)(4,1)} %bitcast.9), calls=%async_computation | async-start | bytes 8388608
  51.0 3.4 %collective-permute-start.17 = (bf16[2048,256]{1,0:T(8,128)(2,1)S(1)}, bf16[2048,256]{1,0:T(8,128)(2,1)S(1)}, u32[]{:S(2)}, u32[]{:S(2)}) collective-permute-start(bf16[2048,256]{1,0:T(8,128)(2,1)S(1)} %get-tuple-element.98), channel_id=1, source_target_pairs={{0,4},{4,0},{8,12},{12,8},{16,20},{20,16},{24,28},{28,24},{1,5},{5... | collective-permute-start | bytes 3145736 | tf_op jit(solution)/shard_map/ppermute | solution.py:513
  53.5 8.5 %copy-start.7 = (bf16[384,3072]{1,0:T(8,128)(2,1)S(1)}, bf16[384,3072]{1,0:T(8,128)(2,1)}, u32[]{:S(2)}) copy-start(bf16[384,3072]{1,0:T(8,128)(2,1)} %copy-done.6) | copy-start | bytes 7077892
  54.4 4.8 %collective-permute-start.9 = (bf16[2064,256]{1,0:T(8,128)(2,1)S(1)}, bf16[2064,256]{1,0:T(8,128)(2,1)S(1)}, u32[]{:S(2)}, u32[]{:S(2)}) collective-permute-start(bf16[2064,256]{1,0:T(8,128)(2,1)S(1)} %get-tuple-element.78), channel_id=1, source_target_pairs={{0,4},{4,0},{8,12},{12,8},{16,20},{20,16},{24,28},{28,24},{1,5},{5... | collective-permute-start | bytes 3170312 | tf_op jit(solution)/shard_map/ppermute | solution.py:513
  54.4 7.6 %copy-start.5 = (bf16[384,3072]{1,0:T(8,128)(2,1)S(1)}, bf16[384,3072]{1,0:T(8,128)(2,1)}, u32[]{:S(2)}) copy-start(bf16[384,3072]{1,0:T(8,128)(2,1)} %copy-done.4) | copy-start | bytes 7077892
  54.7 7.3 %copy-start.3 = (bf16[384,3072]{1,0:T(8,128)(2,1)S(1)}, bf16[384,3072]{1,0:T(8,128)(2,1)}, u32[]{:S(2)}) copy-start(bf16[384,3072]{1,0:T(8,128)(2,1)} %copy-done.2) | copy-start | bytes 7077892
  54.8 11.6 %collective-permute-start.18 = (bf16[1024,128]{1,0:T(8,128)(2,1)S(1)}, bf16[1024,128]{1,0:T(8,128)(2,1)S(1)}, u32[]{:S(2)}, u32[]{:S(2)}) collective-permute-start(bf16[1024,128]{1,0:T(8,128)(2,1)S(1)} %get-tuple-element.100), channel_id=1, source_target_pairs={{0,8},{4,12},{8,0},{12,4},{16,24},{20,28},{24,16},{28,20},{1,9},{5... | collective-permute-start | bytes 786440 | tf_op jit(solution)/shard_map/ppermute | solution.py:513
  59.2 9.1 %collective-permute-start.19 = (bf16[1024,128]{1,0:T(8,128)(2,1)S(1)}, bf16[1024,128]{1,0:T(8,128)(2,1)S(1)}, u32[]{:S(2)}, u32[]{:S(2)}) collective-permute-start(bf16[1024,128]{1,0:T(8,128)(2,1)S(1)} %get-tuple-element.102), channel_id=1, source_target_pairs={{0,16},{4,20},{8,24},{12,28},{16,0},{20,4},{24,8},{28,12},{1,17},{... | collective-permute-start | bytes 786440 | tf_op jit(solution)/shard_map/ppermute | solution.py:513
  59.7 14.3 %collective-permute-start.10 = (bf16[1040,128]{1,0:T(8,128)(2,1)S(1)}, bf16[1040,128]{1,0:T(8,128)(2,1)S(1)}, u32[]{:S(2)}, u32[]{:S(2)}) collective-permute-start(bf16[1040,128]{1,0:T(8,128)(2,1)S(1)} %get-tuple-element.84), channel_id=1, source_target_pairs={{0,8},{4,12},{8,0},{12,4},{16,24},{20,28},{24,16},{28,20},{1,9},{5... | collective-permute-start | bytes 798728 | tf_op jit(solution)/shard_map/ppermute | solution.py:513
  61.9 12.1 %collective-permute-start.11 = (bf16[1024,128]{1,0:T(8,128)(2,1)S(1)}, bf16[1024,128]{1,0:T(8,128)(2,1)S(1)}, u32[]{:S(2)}, u32[]{:S(2)}) collective-permute-start(bf16[1024,128]{1,0:T(8,128)(2,1)S(1)} %get-tuple-element.86), channel_id=1, source_target_pairs={{0,16},{4,20},{8,24},{12,28},{16,0},{20,4},{24,8},{28,12},{1,17},{... | collective-permute-start | bytes 786440 | tf_op jit(solution)/shard_map/ppermute | solution.py:513
  68.5 8.0 %collective-permute-start.20 = (bf16[512,128]{1,0:T(8,128)(2,1)S(1)}, bf16[512,128]{1,0:T(8,128)(2,1)S(1)}, u32[]{:S(2)}, u32[]{:S(2)}) collective-permute-start(bf16[512,128]{1,0:T(8,128)(2,1)S(1)} %get-tuple-element.105), channel_id=1, source_target_pairs={{0,16},{4,20},{8,24},{12,28},{16,0},{20,4},{24,8},{28,12},{1,17},{... | collective-permute-start | bytes 393224 | tf_op jit(solution)/shard_map/ppermute | solution.py:513
  68.6 7.9 %collective-permute-start.21 = (bf16[512,128]{1,0:T(8,128)(2,1)S(1)}, bf16[512,128]{1,0:T(8,128)(2,1)S(1)}, u32[]{:S(2)}, u32[]{:S(2)}) collective-permute-start(bf16[512,128]{1,0:T(8,128)(2,1)S(1)} %get-tuple-element.107), channel_id=1, source_target_pairs={{0,8},{4,12},{8,0},{12,4},{16,24},{20,28},{24,16},{28,20},{1,9},{5... | collective-permute-start | bytes 393224 | tf_op jit(solution)/shard_map/ppermute | solution.py:513
  74.2 6.8 %collective-permute-start.12 = (bf16[528,128]{1,0:T(8,128)(2,1)S(1)}, bf16[528,128]{1,0:T(8,128)(2,1)S(1)}, u32[]{:S(2)}, u32[]{:S(2)}) collective-permute-start(bf16[528,128]{1,0:T(8,128)(2,1)S(1)} %get-tuple-element.89), channel_id=1, source_target_pairs={{0,16},{4,20},{8,24},{12,28},{16,0},{20,4},{24,8},{28,12},{1,17},{... | collective-permute-start | bytes 405512 | tf_op jit(solution)/shard_map/ppermute | solution.py:513
  74.3 6.7 %collective-permute-start.13 = (bf16[512,128]{1,0:T(8,128)(2,1)S(1)}, bf16[512,128]{1,0:T(8,128)(2,1)S(1)}, u32[]{:S(2)}, u32[]{:S(2)}) collective-permute-start(bf16[512,128]{1,0:T(8,128)(2,1)S(1)} %get-tuple-element.91), channel_id=1, source_target_pairs={{0,8},{4,12},{8,0},{12,4},{16,24},{20,28},{24,16},{28,20},{1,9},{5... | collective-permute-start | bytes 393224 | tf_op jit(solution)/shard_map/ppermute | solution.py:513
  76.5 6.7 %collective-permute-start.22 = (bf16[288,128]{1,0:T(8,128)(2,1)S(1)}, bf16[288,128]{1,0:T(8,128)(2,1)S(1)}, u32[]{:S(2)}, u32[]{:S(2)}) collective-permute-start(bf16[288,128]{1,0:T(8,128)(2,1)S(1)} %get-tuple-element.109), channel_id=1, source_target_pairs={{0,3},{1,2},{2,1},{3,0},{4,7},{5,6},{6,5},{7,4},{8,11},{9,10},{10,... | collective-permute-start | bytes 221192 | tf_op jit(solution)/shard_map/ppermute | solution.py:516
  77.9 9.2 %collective-permute-start.23 = (bf16[288,128]{1,0:T(8,128)(2,1)S(1)}, bf16[288,128]{1,0:T(8,128)(2,1)S(1)}, u32[]{:S(2)}, u32[]{:S(2)}) collective-permute-start(bf16[288,128]{1,0:T(8,128)(2,1)S(1)} %get-tuple-element.110), channel_id=1, source_target_pairs={{0,2},{1,3},{2,0},{3,1},{4,6},{5,7},{6,4},{7,5},{8,10},{9,11},{10,... | collective-permute-start | bytes 221192 | tf_op jit(solution)/shard_map/ppermute | solution.py:516
  77.9 9.2 %collective-permute-start.24 = (bf16[288,128]{1,0:T(8,128)(2,1)S(1)}, bf16[288,128]{1,0:T(8,128)(2,1)S(1)}, u32[]{:S(2)}, u32[]{:S(2)}) collective-permute-start(bf16[288,128]{1,0:T(8,128)(2,1)S(1)} %get-tuple-element.111), channel_id=1, source_target_pairs={{0,1},{1,0},{2,3},{3,2},{4,5},{5,4},{6,7},{7,6},{8,9},{9,8},{10,11... | collective-permute-start | bytes 221192 | tf_op jit(solution)/shard_map/ppermute | solution.py:516
  81.2 6.7 %collective-permute-start.14 = (bf16[272,128]{1,0:T(8,128)(2,1)S(1)}, bf16[272,128]{1,0:T(8,128)(2,1)S(1)}, u32[]{:S(2)}, u32[]{:S(2)}) collective-permute-start(bf16[272,128]{1,0:T(8,128)(2,1)S(1)} %get-tuple-element.94), channel_id=1, source_target_pairs={{0,3},{1,2},{2,1},{3,0},{4,7},{5,6},{6,5},{7,4},{8,11},{9,10},{10,... | collective-permute-start | bytes 208904 | tf_op jit(solution)/shard_map/ppermute | solution.py:516
  82.5 8.1 %collective-permute-start.15 = (bf16[272,128]{1,0:T(8,128)(2,1)S(1)}, bf16[272,128]{1,0:T(8,128)(2,1)S(1)}, u32[]{:S(2)}, u32[]{:S(2)}) collective-permute-start(bf16[272,128]{1,0:T(8,128)(2,1)S(1)} %get-tuple-element.95), channel_id=1, source_target_pairs={{0,2},{1,3},{2,0},{3,1},{4,6},{5,7},{6,4},{7,5},{8,10},{9,11},{10,... | collective-permute-start | bytes 208904 | tf_op jit(solution)/shard_map/ppermute | solution.py:516
  83.2 7.4 %collective-permute-start.16 = (bf16[272,128]{1,0:T(8,128)(2,1)S(1)}, bf16[272,128]{1,0:T(8,128)(2,1)S(1)}, u32[]{:S(2)}, u32[]{:S(2)}) collective-permute-start(bf16[272,128]{1,0:T(8,128)(2,1)S(1)} %get-tuple-element.96), channel_id=1, source_target_pairs={{0,1},{1,0},{2,3},{3,2},{4,5},{5,4},{6,7},{7,6},{8,9},{9,8},{10,11... | collective-permute-start | bytes 208904 | tf_op jit(solution)/shard_map/ppermute | solution.py:516
  (16 other events, 49.2 us)

commit v9 on v8

--- a/solution.py
+++ b/solution.py
@@ -232,7 +232,7 @@
     return whole_call(kernel, "merge", [], [own, got], outs, 4, (0, 6 * own.size), [], after)[0]
 
 
-def attention(me, spans, queries, out_grad, keys, values, swap, n):
+def attention(me, spans, queries, out_grad, keys, values, activations, swap, n):
     rows, hd = keys.shape
     columns = queries.shape[1]
     tall = columns // hd * rows
@@ -248,12 +248,13 @@
         [me, spans],
         [queries, out_grad, keys, values],
         [stats_shape] + [shape(x.shape) for x in (queries, out_grad, keys, values)] + [shape((8, 128), F32)],
-        14,
+        12,
         cost,
         [],
         [begin()],
     )
     blocks[0] = [keys, values]
+    acts = prepare(activations, [stats])
     for b in range(1, n):
         if b not in blocks:
             blocks[b] = [swap(x, b & -b) for x in blocks[b & (b - 1)]]
@@ -263,10 +264,10 @@
             [],
             [flags, queries, out_grad, *blocks[b], stats],
             [stats_shape],
-            12,
+            10,
             cost,
             [],
-            blocks[2] if b == 1 else [],
+            [*blocks[2], acts] if b == 1 else [],
         )[0]
     p_buf = pltpu.VMEM((rows, 2 * rows), BF16)
     sums = [pltpu.VMEM((rows, hd), F32)] * 2
@@ -277,7 +278,7 @@
             [],
             [stats, queries, out_grad, keys, values],
             [shape((rows, 2 * hd), F32), shape((rows, tall))],
-            14,
+            10,
             (11 * product, 16 * rows * columns),
             [p_buf, *sums],
             after,
@@ -291,7 +292,7 @@
             [],
             [flags, stats, queries, out_grad, *blocks[b]],
             [shape((rows, 2 * hd)), shape((rows, tall))],
-            14,
+            10,
             (11 * product, 16 * rows * columns),
             [p_buf, *sums],
             before,
@@ -303,7 +304,7 @@
         before = [part]
         to = b & (b - 1)
         parts[to].append(swap(part, b & -b))
-    return own, parts[0], [blocks[b][0] for b in range(n)], score_grads, before
+    return own, parts[0], [blocks[b][0] for b in range(n)], score_grads, acts
 
 
 def query_gradients(key_blocks, score_grads, columns, after):
@@ -315,7 +316,7 @@
         [],
         [*key_blocks, *score_grads],
         [shape((rows, columns)), shape((8, 128), F32)],
-        5 + 3 * n,
+        2 + 3 * n,
         (2 * n * rows * rows * columns, 16 * rows * columns),
         [],
         after,
@@ -515,10 +516,9 @@
     def swap_ctx(x, mask):
         return lax.ppermute(x, "context", xor_perm(n_ctx, mask))
 
-    own, parts, key_blocks, score_grads, last_part = attention(
-        me_ctx, span_order[0], queries, out_grad, keys, values, swap_ctx, n_ctx
+    own, parts, key_blocks, score_grads, acts = attention(
+        me_ctx, span_order[0], queries, out_grad, keys, values, activations, swap_ctx, n_ctx
     )
-    acts = prepare(activations, last_part)
 
     shrink = 1.0 / (n_dp * n_ctx)
     acts = acts.reshape(n_dp, n_ctx, sets, rows_set, rows)

time: 92.4 us -> 103 us (1.11)
  local copies, waits for them, and re-layouts: 13.9 us -> 22.4 us
  Pallas kernels: 26.6 us -> 18.5 us
  starting transfers between devices: 33.6 us -> 41 us
  waiting for transfers between devices: 17.1 us -> 19.6 us
    ppermute x15, starting transfers between devices: 22.5 us -> 31.7 us  [swap_ctx(): return lax.ppermute(x, 'context', xor_perm(n_ctx, mask))]
    unnamed x46 -> x42, local copies, waits for them, and re-layouts: 13.3 us -> 21.7 us
    pallas_call x22, Pallas kernels: 26.6 us -> 18.5 us  [whole_call(): pl.pallas_call(body, grid_spec=pltpu.PrefetchScalarGridSpec(num_scalar_pr...]
    ppermute x15, waiting for transfers between devices: 10.9 us -> 14.2 us  [swap_ctx(): return lax.ppermute(x, 'context', xor_perm(n_ctx, mask))]
    ppermute x10, starting transfers between devices: 11 us -> 9.33 us  [swap_dp(): return lax.ppermute(x, 'dp', xor_perm(n_dp, mask))]
  transfers between devices with their start and end apart: 25 -> 25, of which waited for: 11 -> 10; matrix products, arithmetic and copies ran while one was open for 0% -> 0% of each run, Pallas kernels for 26% -> 15%
where the time goes in v9:
time: 103 us; the launch traced here: 102 us
  starting transfers between devices  41 us (40%)
  local copies, waits for them, and re-layouts  22.4 us (22%)
  waiting for transfers between devices  19.6 us (19%)
  Pallas kernels  18.5 us (18%)
    ppermute x15, starting transfers between devices, swap_ctx(): return lax.ppermute(x, 'context', xor_perm(n_ctx, mask))  31.7 us
    unnamed x42, local copies, waits for them, and re-layouts  21.7 us
    pallas_call x22, Pallas kernels, whole_call(): pl.pallas_call(body, grid_spec=pltpu.PrefetchScalarGridSpec(num_scalar_pr...  18.5 us
    ppermute x15, waiting for transfers between devices, swap_ctx(): return lax.ppermute(x, 'context', xor_perm(n_ctx, mask))  14.2 us
    ppermute x10, starting transfers between devices, swap_dp(): return lax.ppermute(x, 'dp', xor_perm(n_dp, mask))  9.33 us
    ppermute x10, waiting for transfers between devices, swap_dp(): return lax.ppermute(x, 'dp', xor_perm(n_dp, mask))  5.38 us
  transfers between devices with their start and end apart: 25, of which 10 were waited for; matrix products, arithmetic and copies ran while one was open for 0% of the time, Pallas kernels for 15%

profile of v9, /device:TPU:0, one launch (start us, length us, event | category | flops | bytes accessed | tf_op | source)
XLA Modules:
  0.0 102.3 jit_solution(14341660133592282876)
XLA Ops:
  0.6 4.1 %collective-permute-start.1 = (bf16[384,128]{1,0:T(8,128)(2,1)}, bf16[384,128]{1,0:T(8,128)(2,1)S(1)}, u32[]{:S(2)}, u32[]{:S(2)}) collective-permute-start(bf16[384,128]{1,0:T(8,128)(2,1)} %refs_4_.1), channel_id=1, source_target_pairs={{0,2},{1,3},{2,0},{3,1},{4,6},{5,7},{6,4},{7,5},{8,10},{9,11},{10,... | collective-permute-start | bytes 294920 | tf_op jit(solution)/shard_map/ppermute | solution.py:517
  4.7 1.6 %collective-permute-start = (bf16[384,128]{1,0:T(8,128)(2,1)}, bf16[384,128]{1,0:T(8,128)(2,1)S(1)}, u32[]{:S(2)}, u32[]{:S(2)}) collective-permute-start(bf16[384,128]{1,0:T(8,128)(2,1)} %refs_4_.1), channel_id=1, source_target_pairs={{0,1},{1,0},{2,3},{3,2},{4,5},{5,4},{6,7},{7,6},{8,9},{9,8},{10,11... | collective-permute-start | bytes 294920 | tf_op jit(solution)/shard_map/ppermute | solution.py:517
  8.2 2.4 %first_stats.1 = (f32[8,3072]{1,0:T(8,128)S(1)}, bf16[384,1024]{1,0:T(8,128)(2,1)S(1)}, bf16[384,1024]{1,0:T(8,128)(2,1)S(1)}, bf16[384,128]{1,0:T(8,128)(2,1)S(...) custom-call(s32[1]{0:T(128)} %bitcast.refs_0_.refs_1_, s32[4]{0:T(128)S(1)} %bitcast.13, ...), custom_call_target="tpu_custom_call" | custom-call | flops 2415919104 | bytes 3145728 | tf_op jit(solution)/shard_map/first_stats/pallas_call | solution.py:39
  11.0 1.7 %prepare.1.refs_8_ = bf16[8192,384]{1,0:T(8,128)(2,1)S(1)} custom-call(bf16[384,8192]{1,0:T(8,128)(2,1)S(1)} %copy-done.5, f32[8,3072]{1,0:T(8,128)S(1)} %get-tuple-element.64.refs_1_.refs_5_), custom_call_target="tpu_custom_call" | custom-call | tf_op jit(solution)/shard_map/prepare/pallas_call | solution.py:39
  12.7 1.9 %collective-permute-start.2 = (bf16[384,128]{1,0:T(8,128)(2,1)S(1)}, bf16[384,128]{1,0:T(8,128)(2,1)S(1)}, u32[]{:S(2)}, u32[]{:S(2)}) collective-permute-start(bf16[384,128]{1,0:T(8,128)(2,1)S(1)} %collective-permute-done.1.refs_6_.refs_3_.refs_4_.refs_2_), channel_id=1, source_target_pairs={{0,1},{1,0},{2,3},{3,2},{4,5},{5,4},{6,7},{7,6},{8,9},{9,8},{10,11... | collective-permute-start | bytes 294920 | tf_op jit(solution)/shard_map/ppermute | solution.py:517
  15.5 2.4 %collective-permute-done.2.refs_3_.refs_4_ = bf16[384,128]{1,0:T(8,128)(2,1)S(1)} collective-permute-done((bf16[384,128]{1,0:T(8,128)(2,1)S(1)}, bf16[384,128]{1,0:T(8,128)(2,1)S(1)}, u32[]{:S(2)}, u32[]{:S(2)}) %collective-permute-start.2) | collective-permute-done | bytes 98336 | tf_op jit(solution)/shard_map/ppermute | solution.py:517
  19.9 1.5 %copy-done.6 = bf16[384,3072]{1,0:T(8,128)(2,1)} copy-done((bf16[384,3072]{1,0:T(8,128)(2,1)}, bf16[384,3072]{1,0:T(8,128)(2,1)S(1)}, u32[]{:S(2)}) %copy-start.6) | copy-done | bytes 2359320
  21.3 1.4 %collective-permute-start.6 = (bf16[384,256]{1,0:T(8,128)(2,1)S(1)}, bf16[384,256]{1,0:T(8,128)(2,1)S(1)}, u32[]{:S(2)}, u32[]{:S(2)}) collective-permute-start(bf16[384,256]{1,0:T(8,128)(2,1)S(1)} %get-tuple-element.66.refs_6_), channel_id=1, source_target_pairs={{0,1},{1,0},{2,3},{3,2},{4,5},{5,4},{6,7},{7,6},{8,9},{9,8},{10,11... | collective-permute-start | bytes 589832 | tf_op jit(solution)/shard_map/ppermute | solution.py:517
  24.4 2.6 %own_gradients.1 = (f32[384,256]{1,0:T(8,128)S(1)}, bf16[384,3072]{1,0:T(8,128)(2,1)S(1)}) custom-call(f32[8,3072]{1,0:T(8,128)S(1)} %next_stats.5.refs_1_.refs_0_, bf16[384,1024]{1,0:T(8,128)(2,1)S(1)} %get-tuple-element.62.refs_1_.refs_2_, bf16[384,1024]{1,0:T(8,128)(2,1)S(1)} %get-tuple-element.63.refs_2_.refs_3_, ...), custom_call_target="tpu_custom_call" | custom-call | flops 3321888768 | bytes 6291456 | tf_op jit(solution)/shard_map/own_gradients/pallas_call | solution.py:39
  27.1 1.5 %copy-done.10 = bf16[384,3072]{1,0:T(8,128)(2,1)} copy-done((bf16[384,3072]{1,0:T(8,128)(2,1)}, bf16[384,3072]{1,0:T(8,128)(2,1)S(1)}, u32[]{:S(2)}) %copy-start.10) | copy-done | bytes 2359320
  28.6 10.3 %collective-permute-start.7 = (bf16[400,256]{1,0:T(8,128)(2,1)S(1)}, bf16[400,256]{1,0:T(8,128)(2,1)S(1)}, u32[]{:S(2)}, u32[]{:S(2)}) collective-permute-start(bf16[400,256]{1,0:T(8,128)(2,1)S(1)} %merge.1.refs_6_), channel_id=1, source_target_pairs={{0,2},{1,3},{2,0},{3,1},{4,6},{5,7},{6,4},{7,5},{8,10},{9,11},{10,... | collective-permute-start | bytes 614408 | tf_op jit(solution)/shard_map/ppermute | solution.py:517
  40.0 1.4 %copy-done.12 = bf16[384,3072]{1,0:T(8,128)(2,1)} copy-done((bf16[384,3072]{1,0:T(8,128)(2,1)}, bf16[384,3072]{1,0:T(8,128)(2,1)S(1)}, u32[]{:S(2)}) %copy-start.12) | copy-done | bytes 2359320
  41.5 2.8 %collective-permute-start.8 = (bf16[384,256]{1,0:T(8,128)(2,1)}, bf16[384,256]{1,0:T(8,128)(2,1)S(1)}, u32[]{:S(2)}, u32[]{:S(2)}) collective-permute-start(bf16[384,256]{1,0:T(8,128)(2,1)} %get-tuple-element.73), channel_id=1, source_target_pairs={{0,1},{1,0},{2,3},{3,2},{4,5},{5,4},{6,7},{7,6},{8,9},{9,8},{10,11... | collective-permute-start | bytes 589832 | tf_op jit(solution)/shard_map/ppermute | solution.py:517
  44.2 4.8 %collective-permute-done.8.refs_3_ = bf16[384,256]{1,0:T(8,128)(2,1)S(1)} collective-permute-done((bf16[384,256]{1,0:T(8,128)(2,1)}, bf16[384,256]{1,0:T(8,128)(2,1)S(1)}, u32[]{:S(2)}, u32[]{:S(2)}) %collective-permute-start.8) | collective-permute-done | bytes 196640 | tf_op jit(solution)/shard_map/ppermute | solution.py:517
  49.0 2.8 %copy-done.1 = bf16[8192,384]{1,0:T(8,128)(2,1)S(1)} copy-done((bf16[8192,384]{1,0:T(8,128)(2,1)S(1)}, bf16[8192,384]{1,0:T(8,128)(2,1)}, u32[]{:S(2)}) %copy-start.1) | copy-done | bytes 6291480
  51.8 3.4 %copy-done.2 = f32[1,1,8192,256]{3,2,1,0:T(8,128)S(1)} copy-done((f32[1,1,8192,256]{3,2,1,0:T(8,128)S(1)}, f32[1,1,8192,256]{3,2,1,0:T(8,128)}, u32[]{:S(2)}) %copy-start.2) | copy-done | bytes 8388632
  57.4 3.4 %copy-done.3 = f32[1,1,8192,256]{3,2,1,0:T(8,128)S(1)} copy-done((f32[1,1,8192,256]{3,2,1,0:T(8,128)S(1)}, f32[1,1,8192,256]{3,2,1,0:T(8,128)}, u32[]{:S(2)}) %copy-start.3) | copy-done | bytes 8388632
  60.8 1.5 %kept_tiles.1 = (f32[4,512,256]{2,1,0:T(8,128)S(1)}, f32[4,512,256]{2,1,0:T(8,128)S(1)}, f32[16,128]{1,0:T(8,128)S(1)}) custom-call(s32[1]{0:T(128)} %bitcast.2.refs_0_, bf16[384,256]{1,0:T(8,128)(2,1)S(1)} %get-tuple-element.74.refs_1_, f32[16,128]{1,0:T(8,128)S(1)} %get-tuple-element.75.refs_2_, bf16[8,4,2,128,384]{4,3,2,1,0:T(8,128)(2,1)S(1)} %bitcast.8, ...), custom_call_target="tpu_custom_call" | custom-call | flops 805306368 | bytes 9437184 | tf_op jit(solution)/shard_map/kept_tiles/pallas_call | solution.py:39
  62.3 3.4 %copy-done.4 = f32[1,1,8192,256]{3,2,1,0:T(8,128)S(1)} copy-done((f32[1,1,8192,256]{3,2,1,0:T(8,128)S(1)}, f32[1,1,8192,256]{3,2,1,0:T(8,128)}, u32[]{:S(2)}) %copy-start.4) | copy-done | bytes 8388632
  66.9 1.6 %collective-permute-start.18 = (bf16[1024,128]{1,0:T(8,128)(2,1)S(1)}, bf16[1024,128]{1,0:T(8,128)(2,1)S(1)}, u32[]{:S(2)}, u32[]{:S(2)}) collective-permute-start(bf16[1024,128]{1,0:T(8,128)(2,1)S(1)} %get-tuple-element.100), channel_id=1, source_target_pairs={{0,8},{4,12},{8,0},{12,4},{16,24},{20,28},{24,16},{28,20},{1,9},{5... | collective-permute-start | bytes 786440 | tf_op jit(solution)/shard_map/ppermute | solution.py:514
  69.7 1.7 %collective-permute-start.10 = (bf16[1040,128]{1,0:T(8,128)(2,1)S(1)}, bf16[1040,128]{1,0:T(8,128)(2,1)S(1)}, u32[]{:S(2)}, u32[]{:S(2)}) collective-permute-start(bf16[1040,128]{1,0:T(8,128)(2,1)S(1)} %get-tuple-element.84), channel_id=1, source_target_pairs={{0,8},{4,12},{8,0},{12,4},{16,24},{20,28},{24,16},{28,20},{1,9},{5... | collective-permute-start | bytes 798728 | tf_op jit(solution)/shard_map/ppermute | solution.py:514
  71.9 3.6 %query_gradients.1 = (bf16[384,1024]{1,0:T(8,128)(2,1)}, f32[8,128]{1,0:T(8,128)S(1)}) custom-call(bf16[384,128]{1,0:T(8,128)(2,1)S(1)} %get-tuple-element.60.refs_3_.refs_0_, bf16[384,128]{1,0:T(8,128)(2,1)S(1)} %collective-permute-done.refs_3_.refs_4_.refs_1_, bf16[384,128]{1,0:T(8,128)(2,1)S(1)} %collective-permute-done.1.refs_6_.refs_3_.refs_4_.refs_2_, ...), custom_call_target="tpu_custom_call" | custom-call | flops 1207959552 | bytes 6291456 | tf_op jit(solution)/shard_map/query_gradients/pallas_call | solution.py:39
  76.1 1.6 %collective-permute-done.19.refs_3_ = bf16[1024,128]{1,0:T(8,128)(2,1)S(1)} collective-permute-done((bf16[1024,128]{1,0:T(8,128)(2,1)S(1)}, bf16[1024,128]{1,0:T(8,128)(2,1)S(1)}, u32[]{:S(2)}, u32[]{:S(2)}) %collective-permute-start.19) | collective-permute-done | bytes 262176 | tf_op jit(solution)/shard_map/ppermute | solution.py:514
  78.4 1.8 %collective-permute-start.21 = (bf16[512,128]{1,0:T(8,128)(2,1)S(1)}, bf16[512,128]{1,0:T(8,128)(2,1)S(1)}, u32[]{:S(2)}, u32[]{:S(2)}) collective-permute-start(bf16[512,128]{1,0:T(8,128)(2,1)S(1)} %get-tuple-element.107), channel_id=1, source_target_pairs={{0,8},{4,12},{8,0},{12,4},{16,24},{20,28},{24,16},{28,20},{1,9},{5... | collective-permute-start | bytes 393224 | tf_op jit(solution)/shard_map/ppermute | solution.py:514
  80.2 3.0 %collective-permute-done.11.refs_3_ = bf16[1024,128]{1,0:T(8,128)(2,1)S(1)} collective-permute-done((bf16[1024,128]{1,0:T(8,128)(2,1)S(1)}, bf16[1024,128]{1,0:T(8,128)(2,1)S(1)}, u32[]{:S(2)}, u32[]{:S(2)}) %collective-permute-start.11) | collective-permute-done | bytes 262176 | tf_op jit(solution)/shard_map/ppermute | solution.py:514
  84.2 1.8 %collective-permute-start.13 = (bf16[512,128]{1,0:T(8,128)(2,1)S(1)}, bf16[512,128]{1,0:T(8,128)(2,1)S(1)}, u32[]{:S(2)}, u32[]{:S(2)}) collective-permute-start(bf16[512,128]{1,0:T(8,128)(2,1)S(1)} %get-tuple-element.91), channel_id=1, source_target_pairs={{0,8},{4,12},{8,0},{12,4},{16,24},{20,28},{24,16},{28,20},{1,9},{5... | collective-permute-start | bytes 393224 | tf_op jit(solution)/shard_map/ppermute | solution.py:514
  86.1 2.1 %collective-permute-start.22 = (bf16[288,128]{1,0:T(8,128)(2,1)S(1)}, bf16[288,128]{1,0:T(8,128)(2,1)S(1)}, u32[]{:S(2)}, u32[]{:S(2)}) collective-permute-start(bf16[288,128]{1,0:T(8,128)(2,1)S(1)} %get-tuple-element.109), channel_id=1, source_target_pairs={{0,3},{1,2},{2,1},{3,0},{4,7},{5,6},{6,5},{7,4},{8,11},{9,10},{10,... | collective-permute-start | bytes 221192 | tf_op jit(solution)/shard_map/ppermute | solution.py:517
  88.2 2.3 %collective-permute-start.24 = (bf16[288,128]{1,0:T(8,128)(2,1)S(1)}, bf16[288,128]{1,0:T(8,128)(2,1)S(1)}, u32[]{:S(2)}, u32[]{:S(2)}) collective-permute-start(bf16[288,128]{1,0:T(8,128)(2,1)S(1)} %get-tuple-element.111), channel_id=1, source_target_pairs={{0,1},{1,0},{2,3},{3,2},{4,5},{5,4},{6,7},{7,6},{8,9},{9,8},{10,11... | collective-permute-start | bytes 221192 | tf_op jit(solution)/shard_map/ppermute | solution.py:517
  90.7 2.1 %collective-permute-start.14 = (bf16[272,128]{1,0:T(8,128)(2,1)S(1)}, bf16[272,128]{1,0:T(8,128)(2,1)S(1)}, u32[]{:S(2)}, u32[]{:S(2)}) collective-permute-start(bf16[272,128]{1,0:T(8,128)(2,1)S(1)} %get-tuple-element.94), channel_id=1, source_target_pairs={{0,3},{1,2},{2,1},{3,0},{4,7},{5,6},{6,5},{7,4},{8,11},{9,10},{10,... | collective-permute-start | bytes 208904 | tf_op jit(solution)/shard_map/ppermute | solution.py:517
  93.1 2.2 %collective-permute-start.16 = (bf16[272,128]{1,0:T(8,128)(2,1)S(1)}, bf16[272,128]{1,0:T(8,128)(2,1)S(1)}, u32[]{:S(2)}, u32[]{:S(2)}) collective-permute-start(bf16[272,128]{1,0:T(8,128)(2,1)S(1)} %get-tuple-element.96), channel_id=1, source_target_pairs={{0,1},{1,0},{2,3},{3,2},{4,5},{5,4},{6,7},{7,6},{8,9},{9,8},{10,11... | collective-permute-start | bytes 208904 | tf_op jit(solution)/shard_map/ppermute | solution.py:517
  95.4 3.2 %collective-permute-done.23.refs_8_ = bf16[288,128]{1,0:T(8,128)(2,1)S(1)} collective-permute-done((bf16[288,128]{1,0:T(8,128)(2,1)S(1)}, bf16[288,128]{1,0:T(8,128)(2,1)S(1)}, u32[]{:S(2)}, u32[]{:S(2)}) %collective-permute-start.23) | collective-permute-done | bytes 73760 | tf_op jit(solution)/shard_map/ppermute | solution.py:517
  98.5 2.2 %collective-permute-done.15.refs_4_ = bf16[272,128]{1,0:T(8,128)(2,1)S(1)} collective-permute-done((bf16[272,128]{1,0:T(8,128)(2,1)S(1)}, bf16[272,128]{1,0:T(8,128)(2,1)S(1)}, u32[]{:S(2)}, u32[]{:S(2)}) %collective-permute-start.15) | collective-permute-done | bytes 69664 | tf_op jit(solution)/shard_map/ppermute | solution.py:517
  (84 shorter events, 17.6 us)
Async XLA Ops:
  0.6 12.1 %collective-permute-start.1 = (bf16[384,128]{1,0:T(8,128)(2,1)}, bf16[384,128]{1,0:T(8,128)(2,1)S(1)}, u32[]{:S(2)}, u32[]{:S(2)}) collective-permute-start(bf16[384,128]{1,0:T(8,128)(2,1)} %refs_4_.1), channel_id=1, source_target_pairs={{0,2},{1,3},{2,0},{3,1},{4,6},{5,7},{6,4},{7,5},{8,10},{9,11},{10,... | collective-permute-start | bytes 294920 | tf_op jit(solution)/shard_map/ppermute | solution.py:517
  4.7 10.2 %collective-permute-start = (bf16[384,128]{1,0:T(8,128)(2,1)}, bf16[384,128]{1,0:T(8,128)(2,1)S(1)}, u32[]{:S(2)}, u32[]{:S(2)}) collective-permute-start(bf16[384,128]{1,0:T(8,128)(2,1)} %refs_4_.1), channel_id=1, source_target_pairs={{0,1},{1,0},{2,3},{3,2},{4,5},{5,4},{6,7},{7,6},{8,9},{9,8},{10,11... | collective-permute-start | bytes 294920 | tf_op jit(solution)/shard_map/ppermute | solution.py:517
  6.3 8.3 %collective-permute-start.3 = (bf16[384,128]{1,0:T(8,128)(2,1)}, bf16[384,128]{1,0:T(8,128)(2,1)S(1)}, u32[]{:S(2)}, u32[]{:S(2)}) collective-permute-start(bf16[384,128]{1,0:T(8,128)(2,1)} %refs_5_.1), channel_id=1, source_target_pairs={{0,2},{1,3},{2,0},{3,1},{4,6},{5,7},{6,4},{7,5},{8,10},{9,11},{10,... | collective-permute-start | bytes 294920 | tf_op jit(solution)/shard_map/ppermute | solution.py:517
  6.6 8.2 %collective-permute-start.5 = (bf16[384,128]{1,0:T(8,128)(2,1)}, bf16[384,128]{1,0:T(8,128)(2,1)S(1)}, u32[]{:S(2)}, u32[]{:S(2)}) collective-permute-start(bf16[384,128]{1,0:T(8,128)(2,1)} %refs_5_.1), channel_id=1, source_target_pairs={{0,1},{1,0},{2,3},{3,2},{4,5},{5,4},{6,7},{7,6},{8,9},{9,8},{10,11... | collective-permute-start | bytes 294920 | tf_op jit(solution)/shard_map/ppermute | solution.py:517
  12.7 5.1 %collective-permute-start.2 = (bf16[384,128]{1,0:T(8,128)(2,1)S(1)}, bf16[384,128]{1,0:T(8,128)(2,1)S(1)}, u32[]{:S(2)}, u32[]{:S(2)}) collective-permute-start(bf16[384,128]{1,0:T(8,128)(2,1)S(1)} %collective-permute-done.1.refs_6_.refs_3_.refs_4_.refs_2_), channel_id=1, source_target_pairs={{0,1},{1,0},{2,3},{3,2},{4,5},{5,4},{6,7},{7,6},{8,9},{9,8},{10,11... | collective-permute-start | bytes 294920 | tf_op jit(solution)/shard_map/ppermute | solution.py:517
  14.6 4.6 %collective-permute-start.4 = (bf16[384,128]{1,0:T(8,128)(2,1)S(1)}, bf16[384,128]{1,0:T(8,128)(2,1)S(1)}, u32[]{:S(2)}, u32[]{:S(2)}) collective-permute-start(bf16[384,128]{1,0:T(8,128)(2,1)S(1)} %collective-permute-done.3.refs_7_.refs_4_.refs_5_), channel_id=1, source_target_pairs={{0,1},{1,0},{2,3},{3,2},{4,5},{5,4},{6,7},{7,6},{8,9},{9,8},{10,11... | collective-permute-start | bytes 294920 | tf_op jit(solution)/shard_map/ppermute | solution.py:517
  21.3 7.2 %collective-permute-start.6 = (bf16[384,256]{1,0:T(8,128)(2,1)S(1)}, bf16[384,256]{1,0:T(8,128)(2,1)S(1)}, u32[]{:S(2)}, u32[]{:S(2)}) collective-permute-start(bf16[384,256]{1,0:T(8,128)(2,1)S(1)} %get-tuple-element.66.refs_6_), channel_id=1, source_target_pairs={{0,1},{1,0},{2,3},{3,2},{4,5},{5,4},{6,7},{7,6},{8,9},{9,8},{10,11... | collective-permute-start | bytes 589832 | tf_op jit(solution)/shard_map/ppermute | solution.py:517
  28.6 20.4 %collective-permute-start.7 = (bf16[400,256]{1,0:T(8,128)(2,1)S(1)}, bf16[400,256]{1,0:T(8,128)(2,1)S(1)}, u32[]{:S(2)}, u32[]{:S(2)}) collective-permute-start(bf16[400,256]{1,0:T(8,128)(2,1)S(1)} %merge.1.refs_6_), channel_id=1, source_target_pairs={{0,2},{1,3},{2,0},{3,1},{4,6},{5,7},{6,4},{7,5},{8,10},{9,11},{10,... | collective-permute-start | bytes 614408 | tf_op jit(solution)/shard_map/ppermute | solution.py:517
  38.9 17.6 %slice-start = ((s8[6291456]{0:T(1024)(128)(4,1)}), s8[2097152]{0:T(1024)(128)(4,1)S(1)}, s32[]{:S(2)}) async-start(s8[6291456]{0:T(1024)(128)(4,1)} %bitcast.6), calls=%async_computation | async-start | bytes 4194304
  41.5 7.5 %collective-permute-start.8 = (bf16[384,256]{1,0:T(8,128)(2,1)}, bf16[384,256]{1,0:T(8,128)(2,1)S(1)}, u32[]{:S(2)}, u32[]{:S(2)}) collective-permute-start(bf16[384,256]{1,0:T(8,128)(2,1)} %get-tuple-element.73), channel_id=1, source_target_pairs={{0,1},{1,0},{2,3},{3,2},{4,5},{5,4},{6,7},{7,6},{8,9},{9,8},{10,11... | collective-permute-start | bytes 589832 | tf_op jit(solution)/shard_map/ppermute | solution.py:517
  51.8 3.4 %copy-start.2 = (f32[1,1,8192,256]{3,2,1,0:T(8,128)S(1)}, f32[1,1,8192,256]{3,2,1,0:T(8,128)}, u32[]{:S(2)}) copy-start(f32[1,1,8192,256]{3,2,1,0:T(8,128)} %param.13) | copy-start | bytes 25165828
  56.4 10.2 %collective-permute-start.17 = (bf16[2048,256]{1,0:T(8,128)(2,1)S(1)}, bf16[2048,256]{1,0:T(8,128)(2,1)S(1)}, u32[]{:S(2)}, u32[]{:S(2)}) collective-permute-start(bf16[2048,256]{1,0:T(8,128)(2,1)S(1)} %get-tuple-element.98), channel_id=1, source_target_pairs={{0,4},{4,0},{8,12},{12,8},{16,20},{20,16},{24,28},{28,24},{1,5},{5... | collective-permute-start | bytes 3145736 | tf_op jit(solution)/shard_map/ppermute | solution.py:514
  62.3 3.4 %copy-start.4 = (f32[1,1,8192,256]{3,2,1,0:T(8,128)S(1)}, f32[1,1,8192,256]{3,2,1,0:T(8,128)}, u32[]{:S(2)}) copy-start(f32[1,1,8192,256]{3,2,1,0:T(8,128)} %param.13) | copy-start | bytes 25165828
  65.6 6.3 %copy-start.11 = (bf16[384,3072]{1,0:T(8,128)(2,1)S(1)}, bf16[384,3072]{1,0:T(8,128)(2,1)}, u32[]{:S(2)}) copy-start(bf16[384,3072]{1,0:T(8,128)(2,1)} %copy-done.10) | copy-start | bytes 7077892
  65.6 6.3 %copy-start.13 = (bf16[384,3072]{1,0:T(8,128)(2,1)S(1)}, bf16[384,3072]{1,0:T(8,128)(2,1)}, u32[]{:S(2)}) copy-start(bf16[384,3072]{1,0:T(8,128)(2,1)} %copy-done.12) | copy-start | bytes 7077892
  66.6 2.7 %collective-permute-start.9 = (bf16[2064,256]{1,0:T(8,128)(2,1)S(1)}, bf16[2064,256]{1,0:T(8,128)(2,1)S(1)}, u32[]{:S(2)}, u32[]{:S(2)}) collective-permute-start(bf16[2064,256]{1,0:T(8,128)(2,1)S(1)} %get-tuple-element.78), channel_id=1, source_target_pairs={{0,4},{4,0},{8,12},{12,8},{16,20},{20,16},{24,28},{28,24},{1,5},{5... | collective-permute-start | bytes 3170312 | tf_op jit(solution)/shard_map/ppermute | solution.py:514
  66.6 5.3 %copy-start.9 = (bf16[384,3072]{1,0:T(8,128)(2,1)S(1)}, bf16[384,3072]{1,0:T(8,128)(2,1)}, u32[]{:S(2)}) copy-start(bf16[384,3072]{1,0:T(8,128)(2,1)} %copy-done.8) | copy-start | bytes 7077892
  66.9 5.0 %copy-start.7 = (bf16[384,3072]{1,0:T(8,128)(2,1)S(1)}, bf16[384,3072]{1,0:T(8,128)(2,1)}, u32[]{:S(2)}) copy-start(bf16[384,3072]{1,0:T(8,128)(2,1)} %copy-done.6) | copy-start | bytes 7077892
  66.9 9.2 %collective-permute-start.18 = (bf16[1024,128]{1,0:T(8,128)(2,1)S(1)}, bf16[1024,128]{1,0:T(8,128)(2,1)S(1)}, u32[]{:S(2)}, u32[]{:S(2)}) collective-permute-start(bf16[1024,128]{1,0:T(8,128)(2,1)S(1)} %get-tuple-element.100), channel_id=1, source_target_pairs={{0,8},{4,12},{8,0},{12,4},{16,24},{20,28},{24,16},{28,20},{1,9},{5... | collective-permute-start | bytes 786440 | tf_op jit(solution)/shard_map/ppermute | solution.py:514
  68.5 9.1 %collective-permute-start.19 = (bf16[1024,128]{1,0:T(8,128)(2,1)S(1)}, bf16[1024,128]{1,0:T(8,128)(2,1)S(1)}, u32[]{:S(2)}, u32[]{:S(2)}) collective-permute-start(bf16[1024,128]{1,0:T(8,128)(2,1)S(1)} %get-tuple-element.102), channel_id=1, source_target_pairs={{0,16},{4,20},{8,24},{12,28},{16,0},{20,4},{24,8},{28,12},{1,17},{... | collective-permute-start | bytes 786440 | tf_op jit(solution)/shard_map/ppermute | solution.py:514
  69.7 13.6 %collective-permute-start.10 = (bf16[1040,128]{1,0:T(8,128)(2,1)S(1)}, bf16[1040,128]{1,0:T(8,128)(2,1)S(1)}, u32[]{:S(2)}, u32[]{:S(2)}) collective-permute-start(bf16[1040,128]{1,0:T(8,128)(2,1)S(1)} %get-tuple-element.84), channel_id=1, source_target_pairs={{0,8},{4,12},{8,0},{12,4},{16,24},{20,28},{24,16},{28,20},{1,9},{5... | collective-permute-start | bytes 798728 | tf_op jit(solution)/shard_map/ppermute | solution.py:514
  71.4 11.9 %collective-permute-start.11 = (bf16[1024,128]{1,0:T(8,128)(2,1)S(1)}, bf16[1024,128]{1,0:T(8,128)(2,1)S(1)}, u32[]{:S(2)}, u32[]{:S(2)}) collective-permute-start(bf16[1024,128]{1,0:T(8,128)(2,1)S(1)} %get-tuple-element.86), channel_id=1, source_target_pairs={{0,16},{4,20},{8,24},{12,28},{16,0},{20,4},{24,8},{28,12},{1,17},{... | collective-permute-start | bytes 786440 | tf_op jit(solution)/shard_map/ppermute | solution.py:514
  77.8 8.2 %collective-permute-start.20 = (bf16[512,128]{1,0:T(8,128)(2,1)S(1)}, bf16[512,128]{1,0:T(8,128)(2,1)S(1)}, u32[]{:S(2)}, u32[]{:S(2)}) collective-permute-start(bf16[512,128]{1,0:T(8,128)(2,1)S(1)} %get-tuple-element.105), channel_id=1, source_target_pairs={{0,16},{4,20},{8,24},{12,28},{16,0},{20,4},{24,8},{28,12},{1,17},{... | collective-permute-start | bytes 393224 | tf_op jit(solution)/shard_map/ppermute | solution.py:514
  78.4 7.6 %collective-permute-start.21 = (bf16[512,128]{1,0:T(8,128)(2,1)S(1)}, bf16[512,128]{1,0:T(8,128)(2,1)S(1)}, u32[]{:S(2)}, u32[]{:S(2)}) collective-permute-start(bf16[512,128]{1,0:T(8,128)(2,1)S(1)} %get-tuple-element.107), channel_id=1, source_target_pairs={{0,8},{4,12},{8,0},{12,4},{16,24},{20,28},{24,16},{28,20},{1,9},{5... | collective-permute-start | bytes 393224 | tf_op jit(solution)/shard_map/ppermute | solution.py:514
  83.5 7.0 %collective-permute-start.12 = (bf16[528,128]{1,0:T(8,128)(2,1)S(1)}, bf16[528,128]{1,0:T(8,128)(2,1)S(1)}, u32[]{:S(2)}, u32[]{:S(2)}) collective-permute-start(bf16[528,128]{1,0:T(8,128)(2,1)S(1)} %get-tuple-element.89), channel_id=1, source_target_pairs={{0,16},{4,20},{8,24},{12,28},{16,0},{20,4},{24,8},{28,12},{1,17},{... | collective-permute-start | bytes 405512 | tf_op jit(solution)/shard_map/ppermute | solution.py:514
  84.2 6.3 %collective-permute-start.13 = (bf16[512,128]{1,0:T(8,128)(2,1)S(1)}, bf16[512,128]{1,0:T(8,128)(2,1)S(1)}, u32[]{:S(2)}, u32[]{:S(2)}) collective-permute-start(bf16[512,128]{1,0:T(8,128)(2,1)S(1)} %get-tuple-element.91), channel_id=1, source_target_pairs={{0,8},{4,12},{8,0},{12,4},{16,24},{20,28},{24,16},{28,20},{1,9},{5... | collective-permute-start | bytes 393224 | tf_op jit(solution)/shard_map/ppermute | solution.py:514
  86.1 7.0 %collective-permute-start.22 = (bf16[288,128]{1,0:T(8,128)(2,1)S(1)}, bf16[288,128]{1,0:T(8,128)(2,1)S(1)}, u32[]{:S(2)}, u32[]{:S(2)}) collective-permute-start(bf16[288,128]{1,0:T(8,128)(2,1)S(1)} %get-tuple-element.109), channel_id=1, source_target_pairs={{0,3},{1,2},{2,1},{3,0},{4,7},{5,6},{6,5},{7,4},{8,11},{9,10},{10,... | collective-permute-start | bytes 221192 | tf_op jit(solution)/shard_map/ppermute | solution.py:517
  88.2 10.3 %collective-permute-start.23 = (bf16[288,128]{1,0:T(8,128)(2,1)S(1)}, bf16[288,128]{1,0:T(8,128)(2,1)S(1)}, u32[]{:S(2)}, u32[]{:S(2)}) collective-permute-start(bf16[288,128]{1,0:T(8,128)(2,1)S(1)} %get-tuple-element.110), channel_id=1, source_target_pairs={{0,2},{1,3},{2,0},{3,1},{4,6},{5,7},{6,4},{7,5},{8,10},{9,11},{10,... | collective-permute-start | bytes 221192 | tf_op jit(solution)/shard_map/ppermute | solution.py:517
  88.2 10.3 %collective-permute-start.24 = (bf16[288,128]{1,0:T(8,128)(2,1)S(1)}, bf16[288,128]{1,0:T(8,128)(2,1)S(1)}, u32[]{:S(2)}, u32[]{:S(2)}) collective-permute-start(bf16[288,128]{1,0:T(8,128)(2,1)S(1)} %get-tuple-element.111), channel_id=1, source_target_pairs={{0,1},{1,0},{2,3},{3,2},{4,5},{5,4},{6,7},{7,6},{8,9},{9,8},{10,11... | collective-permute-start | bytes 221192 | tf_op jit(solution)/shard_map/ppermute | solution.py:517
  90.7 7.8 %collective-permute-start.14 = (bf16[272,128]{1,0:T(8,128)(2,1)S(1)}, bf16[272,128]{1,0:T(8,128)(2,1)S(1)}, u32[]{:S(2)}, u32[]{:S(2)}) collective-permute-start(bf16[272,128]{1,0:T(8,128)(2,1)S(1)} %get-tuple-element.94), channel_id=1, source_target_pairs={{0,3},{1,2},{2,1},{3,0},{4,7},{5,6},{6,5},{7,4},{8,11},{9,10},{10,... | collective-permute-start | bytes 208904 | tf_op jit(solution)/shard_map/ppermute | solution.py:517
  92.8 7.9 %collective-permute-start.15 = (bf16[272,128]{1,0:T(8,128)(2,1)S(1)}, bf16[272,128]{1,0:T(8,128)(2,1)S(1)}, u32[]{:S(2)}, u32[]{:S(2)}) collective-permute-start(bf16[272,128]{1,0:T(8,128)(2,1)S(1)} %get-tuple-element.95), channel_id=1, source_target_pairs={{0,2},{1,3},{2,0},{3,1},{4,6},{5,7},{6,4},{7,5},{8,10},{9,11},{10,... | collective-permute-start | bytes 208904 | tf_op jit(solution)/shard_map/ppermute | solution.py:517
  93.1 7.7 %collective-permute-start.16 = (bf16[272,128]{1,0:T(8,128)(2,1)S(1)}, bf16[272,128]{1,0:T(8,128)(2,1)S(1)}, u32[]{:S(2)}, u32[]{:S(2)}) collective-permute-start(bf16[272,128]{1,0:T(8,128)(2,1)S(1)} %get-tuple-element.96), channel_id=1, source_target_pairs={{0,1},{1,0},{2,3},{3,2},{4,5},{5,4},{6,7},{7,6},{8,9},{9,8},{10,11... | collective-permute-start | bytes 208904 | tf_op jit(solution)/shard_map/ppermute | solution.py:517
  (14 other events, 26.3 us)

commit v10 on v9

--- a/solution.py
+++ b/solution.py
@@ -52,13 +52,13 @@
     )(*scalars, *operands, *after)
 
 
-def begin_kernel(out_ref):
+def begin_kernel(me_dp_ref, me_ctx_ref, out_ref):
     out_ref[...] = jnp.zeros_like(out_ref)
 
 
-def begin():
+def begin(me_dp, me_ctx):
     mark = [shape((8, 128), F32)]
-    return whole_call(begin_kernel, "begin", [], [], mark, 4, (20_000_000_000, 0))[0]
+    return whole_call(begin_kernel, "begin", [me_dp, me_ctx], [], mark, 4, (20_000_000_000, 0))[0]
 
 
 def prepare_kernel(pieces, a_ref, a_out):
@@ -232,7 +232,7 @@
     return whole_call(kernel, "merge", [], [own, got], outs, 4, (0, 6 * own.size), [], after)[0]
 
 
-def attention(me, spans, queries, out_grad, keys, values, activations, swap, n):
+def attention(me, spans, queries, out_grad, keys, values, activations, mark, swap, n):
     rows, hd = keys.shape
     columns = queries.shape[1]
     tall = columns // hd * rows
@@ -251,7 +251,7 @@
         12,
         cost,
         [],
-        [begin()],
+        [mark],
     )
     blocks[0] = [keys, values]
     acts = prepare(activations, [stats])
@@ -517,7 +517,7 @@
         return lax.ppermute(x, "context", xor_perm(n_ctx, mask))
 
     own, parts, key_blocks, score_grads, acts = attention(
-        me_ctx, span_order[0], queries, out_grad, keys, values, activations, swap_ctx, n_ctx
+        me_ctx, span_order[0], queries, out_grad, keys, values, activations, begin(me_dp, me_ctx), swap_ctx, n_ctx
     )
 
     shrink = 1.0 / (n_dp * n_ctx)

time: 103 us -> 84.1 us (0.82)
  local copies, waits for them, and re-layouts: 22.4 us -> 2.38 us
  Pallas kernels: 18.5 us -> 27.1 us
  starting transfers between devices: 41 us -> 32.7 us
    unnamed x42 -> x16, local copies, waits for them, and re-layouts: 21.7 us -> 1.74 us
    pallas_call x22, Pallas kernels: 18.5 us -> 27.1 us  [whole_call(): pl.pallas_call(body, grid_spec=pltpu.PrefetchScalarGridSpec(num_scalar_pr...]
    ppermute x15, starting transfers between devices: 31.7 us -> 25.4 us  [swap_ctx(): return lax.ppermute(x, 'context', xor_perm(n_ctx, mask))]
    ppermute x10, starting transfers between devices: 9.33 us -> 7.3 us  [swap_dp(): return lax.ppermute(x, 'dp', xor_perm(n_dp, mask))]
  transfers between devices with their start and end apart: 25 -> 25, of which waited for: 10 -> 8; matrix products, arithmetic and copies ran while one was open for 0% -> 0% of each run, Pallas kernels for 15% -> 29%
where the time goes in v10:
time: 84.1 us; the launch traced here: 83.6 us
  starting transfers between devices  32.7 us (39%)
  Pallas kernels  27.1 us (32%)
  waiting for transfers between devices  20.5 us (24%)
  local copies, waits for them, and re-layouts  2.38 us (3%)
    pallas_call x22, Pallas kernels, whole_call(): pl.pallas_call(body, grid_spec=pltpu.PrefetchScalarGridSpec(num_scalar_pr...  27.1 us
    ppermute x15, starting transfers between devices, swap_ctx(): return lax.ppermute(x, 'context', xor_perm(n_ctx, mask))  25.4 us
    ppermute x15, waiting for transfers between devices, swap_ctx(): return lax.ppermute(x, 'context', xor_perm(n_ctx, mask))  14.5 us
    ppermute x10, starting transfers between devices, swap_dp(): return lax.ppermute(x, 'dp', xor_perm(n_dp, mask))  7.3 us
    ppermute x10, waiting for transfers between devices, swap_dp(): return lax.ppermute(x, 'dp', xor_perm(n_dp, mask))  6.09 us
    unnamed x16, local copies, waits for them, and re-layouts  1.74 us
  transfers between devices with their start and end apart: 25, of which 8 were waited for; matrix products, arithmetic and copies ran while one was open for 0% of the time, Pallas kernels for 29%

profile of v10, /device:TPU:0, one launch (start us, length us, event | category | flops | bytes accessed | tf_op | source)
XLA Modules:
  0.0 83.6 jit_solution(6999215399975954208)
XLA Ops:
  0.6 4.1 %collective-permute-start.1 = (bf16[384,128]{1,0:T(8,128)(2,1)}, bf16[384,128]{1,0:T(8,128)(2,1)S(1)}, u32[]{:S(2)}, u32[]{:S(2)}) collective-permute-start(bf16[384,128]{1,0:T(8,128)(2,1)} %refs_4_.1), channel_id=1, source_target_pairs={{0,2},{1,3},{2,0},{3,1},{4,6},{5,7},{6,4},{7,5},{8,10},{9,11},{10,... | collective-permute-start | bytes 294920 | tf_op jit(solution)/shard_map/ppermute | solution.py:517
  4.7 1.6 %collective-permute-start = (bf16[384,128]{1,0:T(8,128)(2,1)}, bf16[384,128]{1,0:T(8,128)(2,1)S(1)}, u32[]{:S(2)}, u32[]{:S(2)}) collective-permute-start(bf16[384,128]{1,0:T(8,128)(2,1)} %refs_4_.1), channel_id=1, source_target_pairs={{0,1},{1,0},{2,3},{3,2},{4,5},{5,4},{6,7},{7,6},{8,9},{9,8},{10,11... | collective-permute-start | bytes 294920 | tf_op jit(solution)/shard_map/ppermute | solution.py:517
  6.9 1.1 %copy-done.1 = bf16[384,1024]{1,0:T(8,128)(2,1)S(1)} copy-done((bf16[384,1024]{1,0:T(8,128)(2,1)S(1)}, bf16[384,1024]{1,0:T(8,128)(2,1)}, u32[]{:S(2)}) %copy-start.1) | copy-done | bytes 786456
  8.2 2.4 %first_stats.1 = (f32[8,3072]{1,0:T(8,128)S(1)}, bf16[384,1024]{1,0:T(8,128)(2,1)S(1)}, bf16[384,1024]{1,0:T(8,128)(2,1)S(1)}, bf16[384,128]{1,0:T(8,128)(2,1)S(...) custom-call(s32[1]{0:T(128)} %bitcast.refs_1_.refs_0_, s32[4]{0:T(128)S(1)} %bitcast.13, ...), custom_call_target="tpu_custom_call" | custom-call | flops 2415919104 | bytes 3145728 | tf_op jit(solution)/shard_map/first_stats/pallas_call | solution.py:39
  11.0 1.7 %prepare.1.refs_8_ = bf16[8192,384]{1,0:T(8,128)(2,1)S(1)} custom-call(bf16[384,8192]{1,0:T(8,128)(2,1)S(1)} %copy-done, f32[8,3072]{1,0:T(8,128)S(1)} %get-tuple-element.64.refs_1_.refs_5_), custom_call_target="tpu_custom_call" | custom-call | tf_op jit(solution)/shard_map/prepare/pallas_call | solution.py:39
  12.7 1.9 %collective-permute-start.2 = (bf16[384,128]{1,0:T(8,128)(2,1)S(1)}, bf16[384,128]{1,0:T(8,128)(2,1)S(1)}, u32[]{:S(2)}, u32[]{:S(2)}) collective-permute-start(bf16[384,128]{1,0:T(8,128)(2,1)S(1)} %collective-permute-done.1.refs_6_.refs_3_.refs_4_.refs_2_), channel_id=1, source_target_pairs={{0,1},{1,0},{2,3},{3,2},{4,5},{5,4},{6,7},{7,6},{8,9},{9,8},{10,11... | collective-permute-start | bytes 294920 | tf_op jit(solution)/shard_map/ppermute | solution.py:517
  14.9 2.1 %next_stats.3.refs_5_ = f32[8,3072]{1,0:T(8,128)S(1)} custom-call(f32[8,128]{1,0:T(8,128)S(1)} %get-tuple-element.61.refs_0_, bf16[384,1024]{1,0:T(8,128)(2,1)S(1)} %get-tuple-element.62.refs_1_.refs_2_, bf16[384,1024]{1,0:T(8,128)(2,1)S(1)} %get-tuple-element.63.refs_2_.refs_3_, bf16[384,128]{1,0:T(8,128)(2,1)S(1)} %collective-permute-done.refs_3_.refs_4_.refs_1_, ...), custom_call_target="tpu_custom_call" | custom-call | flops 2415919104 | bytes 3145728 | tf_op jit(solution)/shard_map/next_stats/pallas_call | solution.py:39
  17.0 2.2 %next_stats.4.refs_5_ = f32[8,3072]{1,0:T(8,128)S(1)} custom-call(f32[8,128]{1,0:T(8,128)S(1)} %get-tuple-element.61.refs_0_, bf16[384,1024]{1,0:T(8,128)(2,1)S(1)} %get-tuple-element.62.refs_1_.refs_2_, bf16[384,1024]{1,0:T(8,128)(2,1)S(1)} %get-tuple-element.63.refs_2_.refs_3_, bf16[384,128]{1,0:T(8,128)(2,1)S(1)} %collective-permute-done.1.refs_6_.refs_3_.refs_4_.refs_2_, ...), custom_call_target="tpu_custom_call" | custom-call | flops 2415919104 | bytes 3145728 | tf_op jit(solution)/shard_map/next_stats/pallas_call | solution.py:39
  19.9 6.1 %collective-permute-start.6 = (bf16[384,256]{1,0:T(8,128)(2,1)S(1)}, bf16[384,256]{1,0:T(8,128)(2,1)S(1)}, u32[]{:S(2)}, u32[]{:S(2)}) collective-permute-start(bf16[384,256]{1,0:T(8,128)(2,1)S(1)} %get-tuple-element.66.refs_6_), channel_id=1, source_target_pairs={{0,1},{1,0},{2,3},{3,2},{4,5},{5,4},{6,7},{7,6},{8,9},{9,8},{10,11... | collective-permute-start | bytes 589832 | tf_op jit(solution)/shard_map/ppermute | solution.py:517
  25.9 2.8 %block_gradients.4 = (bf16[384,256]{1,0:T(8,128)(2,1)S(1)}, bf16[384,3072]{1,0:T(8,128)(2,1)S(1)}) custom-call(f32[8,128]{1,0:T(8,128)S(1)} %get-tuple-element.61.refs_0_, f32[8,3072]{1,0:T(8,128)S(1)} %next_stats.5.refs_1_.refs_0_, bf16[384,1024]{1,0:T(8,128)(2,1)S(1)} %get-tuple-element.62.refs_1_.refs_2_, ...), custom_call_target="tpu_custom_call" | custom-call | flops 3321888768 | bytes 6291456 | tf_op jit(solution)/shard_map/block_gradients/pallas_call | solution.py:39
  28.7 2.6 %own_gradients.1 = (f32[384,256]{1,0:T(8,128)S(1)}, bf16[384,3072]{1,0:T(8,128)(2,1)S(1)}) custom-call(f32[8,3072]{1,0:T(8,128)S(1)} %next_stats.5.refs_1_.refs_0_, bf16[384,1024]{1,0:T(8,128)(2,1)S(1)} %get-tuple-element.62.refs_1_.refs_2_, bf16[384,1024]{1,0:T(8,128)(2,1)S(1)} %get-tuple-element.63.refs_2_.refs_3_, ...), custom_call_target="tpu_custom_call" | custom-call | flops 3321888768 | bytes 6291456 | tf_op jit(solution)/shard_map/own_gradients/pallas_call | solution.py:39
  31.4 2.0 %collective-permute-start.7 = (bf16[400,256]{1,0:T(8,128)(2,1)S(1)}, bf16[400,256]{1,0:T(8,128)(2,1)S(1)}, u32[]{:S(2)}, u32[]{:S(2)}) collective-permute-start(bf16[400,256]{1,0:T(8,128)(2,1)S(1)} %merge.1.refs_6_), channel_id=1, source_target_pairs={{0,2},{1,3},{2,0},{3,1},{4,6},{5,7},{6,4},{7,5},{8,10},{9,11},{10,... | collective-permute-start | bytes 614408 | tf_op jit(solution)/shard_map/ppermute | solution.py:517
  33.4 3.0 %block_gradients.5 = (bf16[384,256]{1,0:T(8,128)(2,1)S(1)}, bf16[384,3072]{1,0:T(8,128)(2,1)S(1)}) custom-call(f32[8,128]{1,0:T(8,128)S(1)} %get-tuple-element.61.refs_0_, f32[8,3072]{1,0:T(8,128)S(1)} %next_stats.5.refs_1_.refs_0_, bf16[384,1024]{1,0:T(8,128)(2,1)S(1)} %get-tuple-element.62.refs_1_.refs_2_, ...), custom_call_target="tpu_custom_call" | custom-call | flops 3321888768 | bytes 6291456 | tf_op jit(solution)/shard_map/block_gradients/pallas_call | solution.py:39
  36.5 9.4 %collective-permute-done.8.refs_3_ = bf16[384,256]{1,0:T(8,128)(2,1)S(1)} collective-permute-done((bf16[384,256]{1,0:T(8,128)(2,1)S(1)}, bf16[384,256]{1,0:T(8,128)(2,1)S(1)}, u32[]{:S(2)}, u32[]{:S(2)}) %collective-permute-start.8) | collective-permute-done | bytes 196640 | tf_op jit(solution)/shard_map/ppermute | solution.py:517
  45.9 1.3 %send_tiles.2 = (bf16[2048,256]{1,0:T(8,128)(2,1)S(1)}, f32[16,128]{1,0:T(8,128)S(1)}, bf16[384,128]{1,0:T(8,128)(2,1)}, bf16[384,128]{1,0:T(8,128)(2,1)}, bf16[384,256]{1,0:T(8,128)(2,1)S(1)}) custom-call(s32[1]{0:T(128)} %bitcast.2.refs_0_, f32[384,256]{1,0:T(8,128)S(1)} %get-tuple-element.69.refs_2_.refs_1_, ...), custom_call_target="tpu_custom_call" | custom-call | flops 402653184 | bytes 4718592 | tf_op jit(solution)/shard_map/send_tiles/pallas_call | solution.py:39
  47.2 1.4 %kept_tiles.1 = (f32[4,512,256]{2,1,0:T(8,128)S(1)}, f32[4,512,256]{2,1,0:T(8,128)S(1)}, f32[16,128]{1,0:T(8,128)S(1)}) custom-call(s32[1]{0:T(128)} %bitcast.2.refs_0_, bf16[384,256]{1,0:T(8,128)(2,1)S(1)} %get-tuple-element.74.refs_1_, f32[16,128]{1,0:T(8,128)S(1)} %get-tuple-element.75.refs_2_, bf16[8,4,2,128,384]{4,3,2,1,0:T(8,128)(2,1)S(1)} %bitcast.6, ...), custom_call_target="tpu_custom_call" | custom-call | flops 805306368 | bytes 9437184 | tf_op jit(solution)/shard_map/kept_tiles/pallas_call | solution.py:39
  48.7 0.9 %send_tiles.3 = (bf16[2064,256]{1,0:T(8,128)(2,1)S(1)}, f32[16,128]{1,0:T(8,128)S(1)}) custom-call(s32[1]{0:T(128)} %bitcast.2.refs_0_, bf16[384,256]{1,0:T(8,128)(2,1)S(1)} %get-tuple-element.74.refs_1_, f32[16,128]{1,0:T(8,128)S(1)} %get-tuple-element.77.refs_2_, bf16[8,4,2,128,384]{4,3,2,1,0:T(8,128)(2,1)S(1)} %bitcast.7, f32[8,4,2,128,256]{4,3,2,1,0:T(8,128)S(1)} %bitcast.12), custom_call_target="tpu_custom_call" | custom-call | flops 402653184 | bytes 4718592 | tf_op jit(solution)/shard_map/send_tiles/pallas_call | solution.py:39
  50.8 1.7 %collective-permute-done.9.refs_1_ = bf16[2064,256]{1,0:T(8,128)(2,1)S(1)} collective-permute-done((bf16[2064,256]{1,0:T(8,128)(2,1)S(1)}, bf16[2064,256]{1,0:T(8,128)(2,1)S(1)}, u32[]{:S(2)}, u32[]{:S(2)}) %collective-permute-start.9) | collective-permute-done | bytes 1056800 | tf_op jit(solution)/shard_map/ppermute | solution.py:514
  53.0 2.0 %collective-permute-start.11 = (bf16[1024,128]{1,0:T(8,128)(2,1)S(1)}, bf16[1024,128]{1,0:T(8,128)(2,1)S(1)}, u32[]{:S(2)}, u32[]{:S(2)}) collective-permute-start(bf16[1024,128]{1,0:T(8,128)(2,1)S(1)} %get-tuple-element.86), channel_id=1, source_target_pairs={{0,16},{4,20},{8,24},{12,28},{16,0},{20,4},{24,8},{28,12},{1,17},{... | collective-permute-start | bytes 786440 | tf_op jit(solution)/shard_map/ppermute | solution.py:514
  55.0 3.8 %query_gradients.1 = (bf16[384,1024]{1,0:T(8,128)(2,1)}, f32[8,128]{1,0:T(8,128)S(1)}) custom-call(bf16[384,128]{1,0:T(8,128)(2,1)S(1)} %get-tuple-element.60.refs_3_.refs_0_, bf16[384,128]{1,0:T(8,128)(2,1)S(1)} %collective-permute-done.refs_3_.refs_4_.refs_1_, bf16[384,128]{1,0:T(8,128)(2,1)S(1)} %collective-permute-done.1.refs_6_.refs_3_.refs_4_.refs_2_, ...), custom_call_target="tpu_custom_call" | custom-call | flops 1207959552 | bytes 6291456 | tf_op jit(solution)/shard_map/query_gradients/pallas_call | solution.py:39
  58.8 0.9 %collective-permute-done.18.refs_1_ = bf16[1024,128]{1,0:T(8,128)(2,1)S(1)} collective-permute-done((bf16[1024,128]{1,0:T(8,128)(2,1)S(1)}, bf16[1024,128]{1,0:T(8,128)(2,1)S(1)}, u32[]{:S(2)}, u32[]{:S(2)}) %collective-permute-start.18) | collective-permute-done | bytes 262176 | tf_op jit(solution)/shard_map/ppermute | solution.py:514
  60.1 1.9 %collective-permute-start.21 = (bf16[512,128]{1,0:T(8,128)(2,1)S(1)}, bf16[512,128]{1,0:T(8,128)(2,1)S(1)}, u32[]{:S(2)}, u32[]{:S(2)}) collective-permute-start(bf16[512,128]{1,0:T(8,128)(2,1)S(1)} %get-tuple-element.107), channel_id=1, source_target_pairs={{0,8},{4,12},{8,0},{12,4},{16,24},{20,28},{24,16},{28,20},{1,9},{5... | collective-permute-start | bytes 393224 | tf_op jit(solution)/shard_map/ppermute | solution.py:514
  62.0 3.4 %collective-permute-done.11.refs_3_ = bf16[1024,128]{1,0:T(8,128)(2,1)S(1)} collective-permute-done((bf16[1024,128]{1,0:T(8,128)(2,1)S(1)}, bf16[1024,128]{1,0:T(8,128)(2,1)S(1)}, u32[]{:S(2)}, u32[]{:S(2)}) %collective-permute-start.11) | collective-permute-done | bytes 262176 | tf_op jit(solution)/shard_map/ppermute | solution.py:514
  65.9 1.9 %collective-permute-start.13 = (bf16[512,128]{1,0:T(8,128)(2,1)S(1)}, bf16[512,128]{1,0:T(8,128)(2,1)S(1)}, u32[]{:S(2)}, u32[]{:S(2)}) collective-permute-start(bf16[512,128]{1,0:T(8,128)(2,1)S(1)} %get-tuple-element.91), channel_id=1, source_target_pairs={{0,8},{4,12},{8,0},{12,4},{16,24},{20,28},{24,16},{28,20},{1,9},{5... | collective-permute-start | bytes 393224 | tf_op jit(solution)/shard_map/ppermute | solution.py:514
  67.9 1.5 %collective-permute-start.22 = (bf16[288,128]{1,0:T(8,128)(2,1)S(1)}, bf16[288,128]{1,0:T(8,128)(2,1)S(1)}, u32[]{:S(2)}, u32[]{:S(2)}) collective-permute-start(bf16[288,128]{1,0:T(8,128)(2,1)S(1)} %get-tuple-element.109), channel_id=1, source_target_pairs={{0,3},{1,2},{2,1},{3,0},{4,7},{5,6},{6,5},{7,4},{8,11},{9,10},{10,... | collective-permute-start | bytes 221192 | tf_op jit(solution)/shard_map/ppermute | solution.py:517
  69.5 2.9 %collective-permute-start.24 = (bf16[288,128]{1,0:T(8,128)(2,1)S(1)}, bf16[288,128]{1,0:T(8,128)(2,1)S(1)}, u32[]{:S(2)}, u32[]{:S(2)}) collective-permute-start(bf16[288,128]{1,0:T(8,128)(2,1)S(1)} %get-tuple-element.111), channel_id=1, source_target_pairs={{0,1},{1,0},{2,3},{3,2},{4,5},{5,4},{6,7},{7,6},{8,9},{9,8},{10,11... | collective-permute-start | bytes 221192 | tf_op jit(solution)/shard_map/ppermute | solution.py:517
  72.5 1.9 %collective-permute-start.14 = (bf16[272,128]{1,0:T(8,128)(2,1)S(1)}, bf16[272,128]{1,0:T(8,128)(2,1)S(1)}, u32[]{:S(2)}, u32[]{:S(2)}) collective-permute-start(bf16[272,128]{1,0:T(8,128)(2,1)S(1)} %get-tuple-element.94), channel_id=1, source_target_pairs={{0,3},{1,2},{2,1},{3,0},{4,7},{5,6},{6,5},{7,4},{8,11},{9,10},{10,... | collective-permute-start | bytes 208904 | tf_op jit(solution)/shard_map/ppermute | solution.py:517
  74.4 2.6 %collective-permute-start.16 = (bf16[272,128]{1,0:T(8,128)(2,1)S(1)}, bf16[272,128]{1,0:T(8,128)(2,1)S(1)}, u32[]{:S(2)}, u32[]{:S(2)}) collective-permute-start(bf16[272,128]{1,0:T(8,128)(2,1)S(1)} %get-tuple-element.96), channel_id=1, source_target_pairs={{0,1},{1,0},{2,3},{3,2},{4,5},{5,4},{6,7},{7,6},{8,9},{9,8},{10,11... | collective-permute-start | bytes 208904 | tf_op jit(solution)/shard_map/ppermute | solution.py:517
  77.0 2.7 %collective-permute-done.23.refs_8_ = bf16[288,128]{1,0:T(8,128)(2,1)S(1)} collective-permute-done((bf16[288,128]{1,0:T(8,128)(2,1)S(1)}, bf16[288,128]{1,0:T(8,128)(2,1)S(1)}, u32[]{:S(2)}, u32[]{:S(2)}) %collective-permute-start.23) | collective-permute-done | bytes 73760 | tf_op jit(solution)/shard_map/ppermute | solution.py:517
  79.7 2.4 %collective-permute-done.15.refs_4_ = bf16[272,128]{1,0:T(8,128)(2,1)S(1)} collective-permute-done((bf16[272,128]{1,0:T(8,128)(2,1)S(1)}, bf16[272,128]{1,0:T(8,128)(2,1)S(1)}, u32[]{:S(2)}, u32[]{:S(2)}) %collective-permute-start.15) | collective-permute-done | bytes 69664 | tf_op jit(solution)/shard_map/ppermute | solution.py:517
  82.0 0.9 %final_stage.1 = (f32[256,256]{1,0:T(8,128)}, f32[8,32]{1,0:T(8,128)S(1)}) custom-call(s32[1]{0:T(128)} %bitcast.2.refs_0_, s32[1]{0:T(128)} %bitcast.refs_1_.refs_0_, f32[256,128]{1,0:T(8,128)S(1)} %get-tuple-element.93.refs_2_, bf16[272,128]{1,0:T(8,128)(2,1)S(1)} %collective-permute-done.14.refs_3_, bf16[272,128]{1,0:T(8,128)(2,1)S(1)} %collective-permute-done.15.refs_4_, ...), custom_call_target="tpu_custom_call" | custom-call | flops 1048576 | bytes 1048576 | tf_op jit(solution)/shard_map/final_stage/pallas_call | solution.py:39
  82.9 0.6 reshape.21
  (58 shorter events, 5.2 us)
Async XLA Ops:
  0.6 12.1 %collective-permute-start.1 = (bf16[384,128]{1,0:T(8,128)(2,1)}, bf16[384,128]{1,0:T(8,128)(2,1)S(1)}, u32[]{:S(2)}, u32[]{:S(2)}) collective-permute-start(bf16[384,128]{1,0:T(8,128)(2,1)} %refs_4_.1), channel_id=1, source_target_pairs={{0,2},{1,3},{2,0},{3,1},{4,6},{5,7},{6,4},{7,5},{8,10},{9,11},{10,... | collective-permute-start | bytes 294920 | tf_op jit(solution)/shard_map/ppermute | solution.py:517
  4.7 10.2 %collective-permute-start = (bf16[384,128]{1,0:T(8,128)(2,1)}, bf16[384,128]{1,0:T(8,128)(2,1)S(1)}, u32[]{:S(2)}, u32[]{:S(2)}) collective-permute-start(bf16[384,128]{1,0:T(8,128)(2,1)} %refs_4_.1), channel_id=1, source_target_pairs={{0,1},{1,0},{2,3},{3,2},{4,5},{5,4},{6,7},{7,6},{8,9},{9,8},{10,11... | collective-permute-start | bytes 294920 | tf_op jit(solution)/shard_map/ppermute | solution.py:517
  6.3 8.3 %collective-permute-start.3 = (bf16[384,128]{1,0:T(8,128)(2,1)}, bf16[384,128]{1,0:T(8,128)(2,1)S(1)}, u32[]{:S(2)}, u32[]{:S(2)}) collective-permute-start(bf16[384,128]{1,0:T(8,128)(2,1)} %refs_5_.1), channel_id=1, source_target_pairs={{0,2},{1,3},{2,0},{3,1},{4,6},{5,7},{6,4},{7,5},{8,10},{9,11},{10,... | collective-permute-start | bytes 294920 | tf_op jit(solution)/shard_map/ppermute | solution.py:517
  6.6 8.2 %collective-permute-start.5 = (bf16[384,128]{1,0:T(8,128)(2,1)}, bf16[384,128]{1,0:T(8,128)(2,1)S(1)}, u32[]{:S(2)}, u32[]{:S(2)}) collective-permute-start(bf16[384,128]{1,0:T(8,128)(2,1)} %refs_5_.1), channel_id=1, source_target_pairs={{0,1},{1,0},{2,3},{3,2},{4,5},{5,4},{6,7},{7,6},{8,9},{9,8},{10,11... | collective-permute-start | bytes 294920 | tf_op jit(solution)/shard_map/ppermute | solution.py:517
  6.8 1.4 %copy-start.2 = (bf16[384,1024]{1,0:T(8,128)(2,1)S(1)}, bf16[384,1024]{1,0:T(8,128)(2,1)}, u32[]{:S(2)}) copy-start(bf16[384,1024]{1,0:T(8,128)(2,1)} %refs_3_.1) | copy-start | bytes 2359300
  6.8 1.4 %copy-start.3 = (bf16[384,128]{1,0:T(8,128)(2,1)S(1)}, bf16[384,128]{1,0:T(8,128)(2,1)}, u32[]{:S(2)}) copy-start(bf16[384,128]{1,0:T(8,128)(2,1)} %refs_4_.1) | copy-start | bytes 294916
  6.8 1.4 %copy-start.4 = (bf16[384,128]{1,0:T(8,128)(2,1)S(1)}, bf16[384,128]{1,0:T(8,128)(2,1)}, u32[]{:S(2)}) copy-start(bf16[384,128]{1,0:T(8,128)(2,1)} %refs_5_.1) | copy-start | bytes 294916
  6.9 1.4 %copy-start.5 = (s32[1,4]{1,0:T(1,128)S(1)}, s32[1,4]{1,0:T(1,128)}, u32[]{:S(2)}) copy-start(s32[1,4]{1,0:T(1,128)} %param.7) | copy-start | bytes 52
  8.2 2.8 %copy-start = (bf16[384,8192]{1,0:T(8,128)(2,1)S(1)}, bf16[384,8192]{1,0:T(8,128)(2,1)}, u32[]{:S(2)}) copy-start(bf16[384,8192]{1,0:T(8,128)(2,1)} %refs_0_.1) | copy-start | bytes 18874372
  12.7 6.5 %collective-permute-start.2 = (bf16[384,128]{1,0:T(8,128)(2,1)S(1)}, bf16[384,128]{1,0:T(8,128)(2,1)S(1)}, u32[]{:S(2)}, u32[]{:S(2)}) collective-permute-start(bf16[384,128]{1,0:T(8,128)(2,1)S(1)} %collective-permute-done.1.refs_6_.refs_3_.refs_4_.refs_2_), channel_id=1, source_target_pairs={{0,1},{1,0},{2,3},{3,2},{4,5},{5,4},{6,7},{7,6},{8,9},{9,8},{10,11... | collective-permute-start | bytes 294920 | tf_op jit(solution)/shard_map/ppermute | solution.py:517
  14.6 4.6 %collective-permute-start.4 = (bf16[384,128]{1,0:T(8,128)(2,1)S(1)}, bf16[384,128]{1,0:T(8,128)(2,1)S(1)}, u32[]{:S(2)}, u32[]{:S(2)}) collective-permute-start(bf16[384,128]{1,0:T(8,128)(2,1)S(1)} %collective-permute-done.3.refs_7_.refs_4_.refs_5_), channel_id=1, source_target_pairs={{0,1},{1,0},{2,3},{3,2},{4,5},{5,4},{6,7},{7,6},{8,9},{9,8},{10,11... | collective-permute-start | bytes 294920 | tf_op jit(solution)/shard_map/ppermute | solution.py:517
  19.9 11.5 %collective-permute-start.6 = (bf16[384,256]{1,0:T(8,128)(2,1)S(1)}, bf16[384,256]{1,0:T(8,128)(2,1)S(1)}, u32[]{:S(2)}, u32[]{:S(2)}) collective-permute-start(bf16[384,256]{1,0:T(8,128)(2,1)S(1)} %get-tuple-element.66.refs_6_), channel_id=1, source_target_pairs={{0,1},{1,0},{2,3},{3,2},{4,5},{5,4},{6,7},{7,6},{8,9},{9,8},{10,11... | collective-permute-start | bytes 589832 | tf_op jit(solution)/shard_map/ppermute | solution.py:517
  28.7 17.2 %slice-start = ((s8[8388608]{0:T(1024)(128)(4,1)}), s8[4194304]{0:T(1024)(128)(4,1)S(1)}, s32[]{:S(2)}) async-start(s8[8388608]{0:T(1024)(128)(4,1)} %bitcast.8), calls=%async_computation | async-start | bytes 8388608
  31.4 14.6 %slice-start.1 = ((s8[8388608]{0:T(1024)(128)(4,1)}), s8[4194304]{0:T(1024)(128)(4,1)S(1)}, s32[]{:S(2)}) async-start(s8[8388608]{0:T(1024)(128)(4,1)} %bitcast.8), calls=%async_computation.1 | async-start | bytes 8388608
  31.4 14.5 %collective-permute-start.7 = (bf16[400,256]{1,0:T(8,128)(2,1)S(1)}, bf16[400,256]{1,0:T(8,128)(2,1)S(1)}, u32[]{:S(2)}, u32[]{:S(2)}) collective-permute-start(bf16[400,256]{1,0:T(8,128)(2,1)S(1)} %merge.1.refs_6_), channel_id=1, source_target_pairs={{0,2},{1,3},{2,0},{3,1},{4,6},{5,7},{6,4},{7,5},{8,10},{9,11},{10,... | collective-permute-start | bytes 614408 | tf_op jit(solution)/shard_map/ppermute | solution.py:517
  36.4 9.5 %collective-permute-start.8 = (bf16[384,256]{1,0:T(8,128)(2,1)S(1)}, bf16[384,256]{1,0:T(8,128)(2,1)S(1)}, u32[]{:S(2)}, u32[]{:S(2)}) collective-permute-start(bf16[384,256]{1,0:T(8,128)(2,1)S(1)} %get-tuple-element.73), channel_id=1, source_target_pairs={{0,1},{1,0},{2,3},{3,2},{4,5},{5,4},{6,7},{7,6},{8,9},{9,8},{10,11... | collective-permute-start | bytes 589832 | tf_op jit(solution)/shard_map/ppermute | solution.py:517
  47.2 2.9 %collective-permute-start.17 = (bf16[2048,256]{1,0:T(8,128)(2,1)S(1)}, bf16[2048,256]{1,0:T(8,128)(2,1)S(1)}, u32[]{:S(2)}, u32[]{:S(2)}) collective-permute-start(bf16[2048,256]{1,0:T(8,128)(2,1)S(1)} %get-tuple-element.98), channel_id=1, source_target_pairs={{0,4},{4,0},{8,12},{12,8},{16,20},{20,16},{24,28},{28,24},{1,5},{5... | collective-permute-start | bytes 3145736 | tf_op jit(solution)/shard_map/ppermute | solution.py:514
  49.6 2.8 %collective-permute-start.9 = (bf16[2064,256]{1,0:T(8,128)(2,1)S(1)}, bf16[2064,256]{1,0:T(8,128)(2,1)S(1)}, u32[]{:S(2)}, u32[]{:S(2)}) collective-permute-start(bf16[2064,256]{1,0:T(8,128)(2,1)S(1)} %get-tuple-element.78), channel_id=1, source_target_pairs={{0,4},{4,0},{8,12},{12,8},{16,20},{20,16},{24,28},{28,24},{1,5},{5... | collective-permute-start | bytes 3170312 | tf_op jit(solution)/shard_map/ppermute | solution.py:514
  50.4 9.2 %collective-permute-start.18 = (bf16[1024,128]{1,0:T(8,128)(2,1)S(1)}, bf16[1024,128]{1,0:T(8,128)(2,1)S(1)}, u32[]{:S(2)}, u32[]{:S(2)}) collective-permute-start(bf16[1024,128]{1,0:T(8,128)(2,1)S(1)} %get-tuple-element.100), channel_id=1, source_target_pairs={{0,8},{4,12},{8,0},{12,4},{16,24},{20,28},{24,16},{28,20},{1,9},{5... | collective-permute-start | bytes 786440 | tf_op jit(solution)/shard_map/ppermute | solution.py:514
  50.5 9.2 %collective-permute-start.19 = (bf16[1024,128]{1,0:T(8,128)(2,1)S(1)}, bf16[1024,128]{1,0:T(8,128)(2,1)S(1)}, u32[]{:S(2)}, u32[]{:S(2)}) collective-permute-start(bf16[1024,128]{1,0:T(8,128)(2,1)S(1)} %get-tuple-element.102), channel_id=1, source_target_pairs={{0,16},{4,20},{8,24},{12,28},{16,0},{20,4},{24,8},{28,12},{1,17},{... | collective-permute-start | bytes 786440 | tf_op jit(solution)/shard_map/ppermute | solution.py:514
  52.8 12.5 %collective-permute-start.10 = (bf16[1040,128]{1,0:T(8,128)(2,1)S(1)}, bf16[1040,128]{1,0:T(8,128)(2,1)S(1)}, u32[]{:S(2)}, u32[]{:S(2)}) collective-permute-start(bf16[1040,128]{1,0:T(8,128)(2,1)S(1)} %get-tuple-element.84), channel_id=1, source_target_pairs={{0,8},{4,12},{8,0},{12,4},{16,24},{20,28},{24,16},{28,20},{1,9},{5... | collective-permute-start | bytes 798728 | tf_op jit(solution)/shard_map/ppermute | solution.py:514
  53.0 12.4 %collective-permute-start.11 = (bf16[1024,128]{1,0:T(8,128)(2,1)S(1)}, bf16[1024,128]{1,0:T(8,128)(2,1)S(1)}, u32[]{:S(2)}, u32[]{:S(2)}) collective-permute-start(bf16[1024,128]{1,0:T(8,128)(2,1)S(1)} %get-tuple-element.86), channel_id=1, source_target_pairs={{0,16},{4,20},{8,24},{12,28},{16,0},{20,4},{24,8},{28,12},{1,17},{... | collective-permute-start | bytes 786440 | tf_op jit(solution)/shard_map/ppermute | solution.py:514
  59.8 8.0 %collective-permute-start.20 = (bf16[512,128]{1,0:T(8,128)(2,1)S(1)}, bf16[512,128]{1,0:T(8,128)(2,1)S(1)}, u32[]{:S(2)}, u32[]{:S(2)}) collective-permute-start(bf16[512,128]{1,0:T(8,128)(2,1)S(1)} %get-tuple-element.105), channel_id=1, source_target_pairs={{0,16},{4,20},{8,24},{12,28},{16,0},{20,4},{24,8},{28,12},{1,17},{... | collective-permute-start | bytes 393224 | tf_op jit(solution)/shard_map/ppermute | solution.py:514
  60.1 7.7 %collective-permute-start.21 = (bf16[512,128]{1,0:T(8,128)(2,1)S(1)}, bf16[512,128]{1,0:T(8,128)(2,1)S(1)}, u32[]{:S(2)}, u32[]{:S(2)}) collective-permute-start(bf16[512,128]{1,0:T(8,128)(2,1)S(1)} %get-tuple-element.107), channel_id=1, source_target_pairs={{0,8},{4,12},{8,0},{12,4},{16,24},{20,28},{24,16},{28,20},{1,9},{5... | collective-permute-start | bytes 393224 | tf_op jit(solution)/shard_map/ppermute | solution.py:514
  65.6 6.8 %collective-permute-start.12 = (bf16[528,128]{1,0:T(8,128)(2,1)S(1)}, bf16[528,128]{1,0:T(8,128)(2,1)S(1)}, u32[]{:S(2)}, u32[]{:S(2)}) collective-permute-start(bf16[528,128]{1,0:T(8,128)(2,1)S(1)} %get-tuple-element.89), channel_id=1, source_target_pairs={{0,16},{4,20},{8,24},{12,28},{16,0},{20,4},{24,8},{28,12},{1,17},{... | collective-permute-start | bytes 405512 | tf_op jit(solution)/shard_map/ppermute | solution.py:514
  65.9 6.5 %collective-permute-start.13 = (bf16[512,128]{1,0:T(8,128)(2,1)S(1)}, bf16[512,128]{1,0:T(8,128)(2,1)S(1)}, u32[]{:S(2)}, u32[]{:S(2)}) collective-permute-start(bf16[512,128]{1,0:T(8,128)(2,1)S(1)} %get-tuple-element.91), channel_id=1, source_target_pairs={{0,8},{4,12},{8,0},{12,4},{16,24},{20,28},{24,16},{28,20},{1,9},{5... | collective-permute-start | bytes 393224 | tf_op jit(solution)/shard_map/ppermute | solution.py:514
  67.9 6.5 %collective-permute-start.22 = (bf16[288,128]{1,0:T(8,128)(2,1)S(1)}, bf16[288,128]{1,0:T(8,128)(2,1)S(1)}, u32[]{:S(2)}, u32[]{:S(2)}) collective-permute-start(bf16[288,128]{1,0:T(8,128)(2,1)S(1)} %get-tuple-element.109), channel_id=1, source_target_pairs={{0,3},{1,2},{2,1},{3,0},{4,7},{5,6},{6,5},{7,4},{8,11},{9,10},{10,... | collective-permute-start | bytes 221192 | tf_op jit(solution)/shard_map/ppermute | solution.py:517
  69.5 10.2 %collective-permute-start.23 = (bf16[288,128]{1,0:T(8,128)(2,1)S(1)}, bf16[288,128]{1,0:T(8,128)(2,1)S(1)}, u32[]{:S(2)}, u32[]{:S(2)}) collective-permute-start(bf16[288,128]{1,0:T(8,128)(2,1)S(1)} %get-tuple-element.110), channel_id=1, source_target_pairs={{0,2},{1,3},{2,0},{3,1},{4,6},{5,7},{6,4},{7,5},{8,10},{9,11},{10,... | collective-permute-start | bytes 221192 | tf_op jit(solution)/shard_map/ppermute | solution.py:517
  69.5 10.2 %collective-permute-start.24 = (bf16[288,128]{1,0:T(8,128)(2,1)S(1)}, bf16[288,128]{1,0:T(8,128)(2,1)S(1)}, u32[]{:S(2)}, u32[]{:S(2)}) collective-permute-start(bf16[288,128]{1,0:T(8,128)(2,1)S(1)} %get-tuple-element.111), channel_id=1, source_target_pairs={{0,1},{1,0},{2,3},{3,2},{4,5},{5,4},{6,7},{7,6},{8,9},{9,8},{10,11... | collective-permute-start | bytes 221192 | tf_op jit(solution)/shard_map/ppermute | solution.py:517
  72.5 7.1 %collective-permute-start.14 = (bf16[272,128]{1,0:T(8,128)(2,1)S(1)}, bf16[272,128]{1,0:T(8,128)(2,1)S(1)}, u32[]{:S(2)}, u32[]{:S(2)}) collective-permute-start(bf16[272,128]{1,0:T(8,128)(2,1)S(1)} %get-tuple-element.94), channel_id=1, source_target_pairs={{0,3},{1,2},{2,1},{3,0},{4,7},{5,6},{6,5},{7,4},{8,11},{9,10},{10,... | collective-permute-start | bytes 208904 | tf_op jit(solution)/shard_map/ppermute | solution.py:517
  74.4 7.6 %collective-permute-start.15 = (bf16[272,128]{1,0:T(8,128)(2,1)S(1)}, bf16[272,128]{1,0:T(8,128)(2,1)S(1)}, u32[]{:S(2)}, u32[]{:S(2)}) collective-permute-start(bf16[272,128]{1,0:T(8,128)(2,1)S(1)} %get-tuple-element.95), channel_id=1, source_target_pairs={{0,2},{1,3},{2,0},{3,1},{4,6},{5,7},{6,4},{7,5},{8,10},{9,11},{10,... | collective-permute-start | bytes 208904 | tf_op jit(solution)/shard_map/ppermute | solution.py:517
  74.4 7.6 %collective-permute-start.16 = (bf16[272,128]{1,0:T(8,128)(2,1)S(1)}, bf16[272,128]{1,0:T(8,128)(2,1)S(1)}, u32[]{:S(2)}, u32[]{:S(2)}) collective-permute-start(bf16[272,128]{1,0:T(8,128)(2,1)S(1)} %get-tuple-element.96), channel_id=1, source_target_pairs={{0,1},{1,0},{2,3},{3,2},{4,5},{5,4},{6,7},{7,6},{8,9},{9,8},{10,11... | collective-permute-start | bytes 208904 | tf_op jit(solution)/shard_map/ppermute | solution.py:517
  (1 other events, 1.1 us)

commit v11 on v10

--- a/solution.py
+++ b/solution.py
@@ -186,19 +186,22 @@
     return dk[...] * inverse, dv[...]
 
 
-def other_kernel(b, flags, stats, q_ref, do_ref, k_ref, v_ref, out_ref, ds_out, p_buf, dk, dv):
+def other_kernel(b, flags, stats, q_ref, do_ref, k_ref, v_ref, *refs):
+    *outs, ds_out, p_buf, dk, dv = refs
     keep = counted(b, flags)
-    rows, hd = dk.shape
+    hd = dk.shape[1]
+    dk_out, dv_out = outs if len(outs) == 2 else (outs[0].at[:, pl.ds(0, hd)], outs[0].at[:, pl.ds(hd, hd)])
 
     @pl.when(keep)
     def _():
         dk_sum, dv_sum = block_gradients(False, stats, q_ref, do_ref, k_ref, v_ref, p_buf, ds_out, dk, dv)
-        out_ref[:, :hd] = dk_sum.astype(BF16)
-        out_ref[:, hd:] = dv_sum.astype(BF16)
+        dk_out[...] = dk_sum.astype(BF16)
+        dv_out[...] = dv_sum.astype(BF16)
 
     @pl.when(jnp.logical_not(keep))
     def _():
-        out_ref[...] = jnp.zeros_like(out_ref)
+        for out in outs:
+            out[...] = jnp.zeros_like(out)
         ds_out[...] = jnp.zeros_like(ds_out)
 
 
@@ -221,15 +224,24 @@
         dq_ref[:, h * hd : (h + 1) * hd] = (dq / hd**0.5).astype(BF16)
 
 
-def merge_kernel(rows, own_ref, got_ref, out_ref):
-    out_ref[:rows, :] = (own_ref[:rows, :].astype(F32) + got_ref[:rows, :].astype(F32)).astype(BF16)
-    out_ref[rows:, :] = jnp.zeros((out_ref.shape[0] - rows, out_ref.shape[1]), BF16)
-
-
-def merge(own, got, rows, after):
-    outs = [shape((rows + TOP_ROWS, own.shape[1]))]
-    kernel = functools.partial(merge_kernel, rows)
-    return whole_call(kernel, "merge", [], [own, got], outs, 4, (0, 6 * own.size), [], after)[0]
+def merge_kernel(n_got, own_ref, *refs):
+    got_refs, out_ref = refs[:n_got], refs[n_got]
+    rows, width = own_ref.shape
+    at = width - got_refs[0].shape[1]
+    total = own_ref[:, at:].astype(F32)
+    for got in got_refs:
+        total = total + got[...].astype(F32)
+    out_ref[:rows, at:] = total.astype(BF16)
+    if at:
+        out_ref[:rows, :at] = own_ref[:, :at]
+    if out_ref.shape[0] > rows:
+        out_ref[rows:, :] = jnp.zeros((out_ref.shape[0] - rows, width), BF16)
+
+
+def merge(own, got, extra, after):
+    outs = [shape((own.shape[0] + extra, own.shape[1]))]
+    kernel = functools.partial(merge_kernel, len(got))
+    return whole_call(kernel, "merge", [], [own, *got], outs, 4, (0, 0), [], after)[0]
 
 
 def attention(me, spans, queries, out_grad, keys, values, activations, mark, swap, n):
@@ -271,40 +283,41 @@
         )[0]
     p_buf = pltpu.VMEM((rows, 2 * rows), BF16)
     sums = [pltpu.VMEM((rows, hd), F32)] * 2
-    def own_call(after):
-        return whole_call(
-            own_kernel,
-            "own_gradients",
-            [],
-            [stats, queries, out_grad, keys, values],
-            [shape((rows, 2 * hd), F32), shape((rows, tall))],
-            10,
-            (11 * product, 16 * rows * columns),
-            [p_buf, *sums],
-            after,
-        )
-
-    parts, score_grads, before = [[] for _ in range(n)], [None] * n, []
+    parts, straight, score_grads, before = [[] for _ in range(n)], [], [None] * n, []
     for b in range(n - 1, 0, -1):
-        part, score_grads[b] = whole_call(
+        far = b & (b - 1)
+        outs = [shape((rows, hd))] * 2 if far else [shape((rows, 2 * hd))]
+        *part, score_grads[b] = whole_call(
             functools.partial(other_kernel, b),
             "block_gradients",
             [],
             [flags, stats, queries, out_grad, *blocks[b]],
-            [shape((rows, 2 * hd)), shape((rows, tall))],
+            outs + [shape((rows, tall))],
             10,
-            (11 * product, 16 * rows * columns),
+            (0, 0),
             [p_buf, *sums],
-            before,
+            before if far or b > 1 else [*before, *straight],
         )
-        if b == min(2, n - 1):
-            own, score_grads[0] = own_call([part])
-        for other in parts[b]:
-            part = merge(part, other, rows, [own] if b == 2 else [])
-        before = [part]
-        to = b & (b - 1)
-        parts[to].append(swap(part, b & -b))
-    return own, parts[0], [blocks[b][0] for b in range(n)], score_grads, acts
+        before = part[:1]
+        if far:
+            straight.append(swap(part[0], b))
+        part = part[-1]
+        if parts[b]:
+            part = merge(part, parts[b], 0 if far else TOP_ROWS, [])
+            before = [part]
+        parts[far].append(swap(part, b & -b))
+    own, score_grads[0] = whole_call(
+        own_kernel,
+        "own_gradients",
+        [],
+        [stats, queries, out_grad, keys, values],
+        [shape((rows, 2 * hd), F32), shape((rows, tall))],
+        10,
+        (0, 0),
+        [p_buf, *sums],
+        before,
+    )
+    return own, [*straight, *parts[0]], [blocks[b][0] for b in range(n)], score_grads, acts
 
 
 def query_gradients(key_blocks, score_grads, columns, after):
@@ -376,9 +389,9 @@
         dest = tile_of(step, me_ref[0], bits, 1)
         c = corrected_tile(chosen, dest, total, a_ref, e_ref, top_ref)
         out_ref[step * tall : (step + 1) * tall, :] = (c * shrink).astype(BF16)
+    out_ref[steps * tall :, :] = jnp.zeros((out_ref.shape[0] - steps * tall, out_ref.shape[1]), BF16)
     if packed:
         out_ref[steps * tall :, :TOP_LANES] = pack_top(top_ref[...])
-        out_ref[steps * tall :, TOP_LANES:] = jnp.zeros((TOP_ROWS, out_ref.shape[1] - TOP_LANES), BF16)
 
 
 def first_send_kernel(bits, shrink, n_parts, me_ref, own_ref, *refs):
@@ -386,7 +399,10 @@
     a_ref, e_ref, out_ref, top_ref, kg_ref, vg_ref, grads_ref = refs[n_parts:]
     total = own_ref[...]
     for part in part_refs:
-        total = total + part[: total.shape[0], :].astype(F32)
+        got = part[: total.shape[0], :].astype(F32)
+        if got.shape[1] < total.shape[1]:
+            got = jnp.concatenate([got, jnp.zeros_like(got)], axis=1)
+        total = total + got
     total = total.astype(BF16)
     hd = total.shape[1] // 2
     kg_ref[...] = total[:, :hd]
@@ -429,6 +445,8 @@
         top = largest(tops, got, steps * tall)
         top_out[0][...] = top
         low_away[half * tall :, :] = pack_top(top)
+    else:
+        low_away[half * tall :, :] = jnp.zeros((low_away.shape[0] - half * tall, hd), BF16)
 
 
 def largest(tops, low_got, size):
@@ -449,54 +467,73 @@
     if tops:
         top = largest(tops, low_got, size)
         top_out[0][...] = top
-        if low_away.shape[0] > half:
-            low_away[half:, :] = pack_top(top)
+        low_away[half:, :] = pack_top(top)
+    else:
+        low_away[half:, :] = jnp.zeros((low_away.shape[0] - half, low_away.shape[1]), BF16)
+
+
+def context_masks(n_ctx):
+    bits = n_ctx.bit_length() - 1
+    return [sum((1 << j) for j in range(bits) if not (step >> (bits - 1 - j)) & 1) for step in range(n_ctx)]
 
 
 def last_kernel(n_ctx, n_tops, me_ref, low, low_got, high, high_got, *refs):
     tops = refs[:n_tops]
-    outs, top_out = refs[n_tops : n_tops + n_ctx], refs[n_tops + n_ctx :]
+    away, stay, *top_out = refs[n_tops:]
     size, hd = low.shape
     rows_set = size // n_ctx
+    half = n_ctx // 2
+    for i, mask in enumerate(context_masks(n_ctx)):
+        part = pl.ds(pl.multiple_of((me_ref[0] ^ mask) * rows_set, rows_set), rows_set)
+        out, at = (away, i) if i < half else (stay, i - half)
+        at = 2 * at * rows_set
+        for mine, got in ((low, low_got), (high, high_got)):
+            total = mine[part, :].astype(F32) + got[part, :].astype(F32)
+            out[at : at + rows_set, :] = total.astype(BF16)
+            at += rows_set
     if tops:
         top = largest(tops, low_got, size)
         top_out[0][...] = top
-        packed = pack_top(top)
-    for b in range(n_ctx):
-        part = pl.ds(pl.multiple_of((me_ref[0] ^ b) * rows_set, rows_set), rows_set)
-        for at, mine, got in ((0, low, low_got), (rows_set, high, high_got)):
-            total = mine[part, :].astype(F32) + got[part, :].astype(F32)
-            outs[b][at : at + rows_set, :] = total.astype(outs[b].dtype)
-        if b > 0:
-            tail = outs[b].shape[0] - 2 * rows_set
-            outs[b][2 * rows_set :, :] = packed if tops else jnp.zeros((tail, hd), BF16)
-
-
-def final_kernel(sets, n_ctx, gain, me_dp_ref, me_ctx_ref, *refs):
-    groups = [refs[chosen * n_ctx : (chosen + 1) * n_ctx] for chosen in range(sets)][::-1]
-    top_ref, out_ref, scale_ref, all_tops = refs[sets * n_ctx :]
+        away[half * 2 * rows_set :, :] = pack_top(top)
+    else:
+        away[half * 2 * rows_set :, :] = jnp.zeros((away.shape[0] - half * 2 * rows_set, hd), BF16)
+
+
+def halve_kernel(n_tops, mine, got, *refs):
+    tops = refs[:n_tops]
+    away, stay, *top_out = refs[n_tops:]
+    size = mine.shape[0]
+    half = size // 2
+    away[:half, :] = (mine[:half, :].astype(F32) + got[:half, :].astype(F32)).astype(BF16)
+    stay[...] = (mine[half:, :].astype(F32) + got[half:size, :].astype(F32)).astype(stay.dtype)
+    if tops:
+        top = largest(tops, got, size)
+        top_out[0][...] = top
+        away[half:, :] = pack_top(top)
+    else:
+        away[half:, :] = jnp.zeros((away.shape[0] - half, away.shape[1]), BF16)
+
+
+def final_kernel(sets, gain, me_dp_ref, me_ctx_ref, *refs):
+    groups = [refs[2 * chosen : 2 * chosen + 2] for chosen in range(sets)][::-1]
+    top_ref, out_ref, scale_ref, all_tops = refs[2 * sets :]
     n_dp, lanes = scale_ref.shape
     rows_set, hd = groups[0][0].shape[0] // 2, groups[0][0].shape[1]
-    scale = top_ref[...]
-    for other in groups[-1][1:]:
-        scale = jnp.maximum(scale, unpack_top(other, 2 * rows_set))
-    scale = scale + 1e-06
+    scale = jnp.maximum(top_ref[...], unpack_top(groups[-1][1], 2 * rows_set)) + 1e-06
     all_tops[...] = scale
     scale_ref[...] = scale[:n_dp, :lanes]
     factors = gain / all_tops[pl.ds(me_dp_ref[0], 1), :]
     lane = lax.broadcasted_iota(jnp.int32, factors.shape, 1)
     per_set = rows_set // QROWS
     first = me_ctx_ref[0] * (sets * per_set)
-    for chosen, group in enumerate(groups):
+    for chosen, (mine_ref, got_ref) in enumerate(groups):
         for r in range(per_set):
             mine = jnp.where(lane == first + (chosen * per_set + r), factors, 0.0)
             factor = jnp.sum(mine, axis=1, keepdims=True)
             at = chosen * rows_set + r * QROWS
             for h in range(2):
                 part = slice(h * rows_set + r * QROWS, h * rows_set + (r + 1) * QROWS)
-                total = group[0][part, :]
-                for other in group[1:]:
-                    total = total + other[part, :].astype(F32)
+                total = mine_ref[part, :] + got_ref[part, :].astype(F32)
                 out_ref[at : at + QROWS, h * hd : (h + 1) * hd] = total * factor
 
 
@@ -531,7 +568,7 @@
         "send_tiles",
         [me_dp],
         [own, *parts, acts, errors],
-        [shape((steps * tall, width)), tops, shape((rows, hd)), shape((rows, hd)), shape((rows, width))],
+        [shape((steps * tall + 2 * TOP_ROWS, width)), tops, shape((rows, hd)), shape((rows, hd)), shape((rows, width))],
         18,
         cost,
     )
@@ -567,7 +604,7 @@
             "split_tiles",
             [],
             [kept[chosen], got[chosen]] + [top] * last,
-            [shape((half + TOP_ROWS * last, hd))] + [shape((half, hd))] * 3 + [tops] * last,
+            [shape((half + (1 if last else 2) * TOP_ROWS, hd))] + [shape((half, hd))] * 3 + [tops] * last,
             10,
             (4 * half * width, 12 * half * width),
         )
@@ -578,6 +615,7 @@
     for chosen in range(sets):
         low_away, low, high_away, high = halves[chosen]
         extra = TOP_ROWS if chosen == sets - 1 else 0
+        tail = extra or 2 * TOP_ROWS
         for stage in range(1, bits):
             low_got = swap_dp(low_away, 1 << stage)
             high_got = swap_dp(high_away, 1 << (bits - stage))
@@ -592,35 +630,49 @@
                     "add_stage",
                     [],
                     operands,
-                    [shape((size // 2 + extra, hd))] + [shape((size // 2, hd))] * 3 + [tops] * with_tops,
+                    [shape((size // 2 + tail, hd))] + [shape((size // 2, hd))] * 3 + [tops] * with_tops,
                     8,
                     cost,
                     after=[mark] if chosen == 0 and stage == 1 else [],
                 )
             else:
-                outs = whole_call(
+                chunk = 2 * rows_set
+                away, stay, *top_out = whole_call(
                     functools.partial(last_kernel, n_ctx, n_tops),
                     "last_stage",
                     [me_ctx],
                     operands,
-                    [shape((2 * rows_set, hd), F32)]
-                    + [shape((2 * rows_set + (extra or 2 * TOP_ROWS), hd))] * (n_ctx - 1)
-                    + [tops] * with_tops,
+                    [shape((n_ctx // 2 * chunk + tail, hd)), shape((n_ctx // 2 * chunk, hd))] + [tops] * with_tops,
                     8,
                     cost,
                 )
-                mine, away, top_out = outs[0], outs[1:n_ctx], outs[n_ctx:]
             if with_tops:
                 gathered = list(top_out)
-        groups.append([mine] + [swap_ctx(away[b - 1], b) for b in range(n_ctx - 1, 0, -1)])
+        mask = 1
+        while mask < n_ctx // 2:
+            size = stay.shape[0]
+            away, stay, *top_out = whole_call(
+                functools.partial(halve_kernel, int(with_tops)),
+                "halve_context",
+                [],
+                [stay, swap_ctx(away, mask)] + (gathered if with_tops else []),
+                [shape((size // 2 + tail, hd)), shape((size // 2, hd), F32 if size == 2 * chunk else BF16)]
+                + [tops] * with_tops,
+                8,
+                (0, 0),
+            )
+            if with_tops:
+                gathered = list(top_out)
+            mask *= 2
+        groups = [stay, swap_ctx(away, mask), *groups]
     payload, scale = whole_call(
-        functools.partial(final_kernel, sets, n_ctx, 7.0 / shrink),
+        functools.partial(final_kernel, sets, 7.0 / shrink),
         "final_stage",
         [me_dp, me_ctx],
-        [x for group in groups[::-1] for x in group] + gathered,
+        groups + gathered,
         [shape((sets * rows_set, width), F32), shape((n_dp, sets * tall // QROWS), F32)],
         8,
-        (4 * sets * tall * width, 16 * sets * rows_set * width),
+        (0, 0),
         [pltpu.VMEM((TOP_ROWS, TOP_LANES), F32)],
     )
     return query_grad, key_grad, value_grad, payload, scale.reshape(-1)

time: 84.1 us -> 84.6 us (level)
  waiting for transfers between devices: 20.5 us -> 26.4 us
  starting transfers between devices: 32.7 us -> 28.2 us
    ppermute x10, waiting for transfers between devices: 6.09 us -> 12.7 us  [swap_dp(): return lax.ppermute(x, 'dp', xor_perm(n_dp, mask))]
    ppermute x15 -> x14, starting transfers between devices: 25.4 us -> 21.5 us  [swap_ctx(): return lax.ppermute(x, 'context', xor_perm(n_ctx, mask))]
    ppermute x15 -> x14, waiting for transfers between devices: 14.5 us -> 13.7 us  [swap_ctx(): return lax.ppermute(x, 'context', xor_perm(n_ctx, mask))]
    pallas_call x22 -> x24, Pallas kernels: 27.1 us -> 27.1 us  [whole_call(): pl.pallas_call(body, grid_spec=pltpu.PrefetchScalarGridSpec(num_scalar_pr...]
  transfers between devices with their start and end apart: 25 -> 24, of which waited for: 8 -> 8; matrix products, arithmetic and copies ran while one was open for 0% -> 0% of each run, Pallas kernels for 29% -> 29%
where the time goes in v11:
time: 84.6 us; the launch traced here: 84.9 us
  starting transfers between devices  28.2 us (33%)
  Pallas kernels  27.1 us (32%)
  waiting for transfers between devices  26.4 us (31%)
  local copies, waits for them, and re-layouts  2.38 us (3%)
  between operations  0.86 us (1%)
    pallas_call x24, Pallas kernels, whole_call(): pl.pallas_call(body, grid_spec=pltpu.PrefetchScalarGridSpec(num_scalar_pr...  27.1 us
    ppermute x14, starting transfers between devices, swap_ctx(): return lax.ppermute(x, 'context', xor_perm(n_ctx, mask))  21.5 us
    ppermute x14, waiting for transfers between devices, swap_ctx(): return lax.ppermute(x, 'context', xor_perm(n_ctx, mask))  13.7 us
    ppermute x10, waiting for transfers between devices, swap_dp(): return lax.ppermute(x, 'dp', xor_perm(n_dp, mask))  12.7 us
    ppermute x10, starting transfers between devices, swap_dp(): return lax.ppermute(x, 'dp', xor_perm(n_dp, mask))  6.67 us
    unnamed x16, local copies, waits for them, and re-layouts  1.74 us
  transfers between devices with their start and end apart: 24, of which 8 were waited for; matrix products, arithmetic and copies ran while one was open for 0% of the time, Pallas kernels for 29%

profile of v11, /device:TPU:0, one launch (start us, length us, event | category | flops | bytes accessed | tf_op | source)
XLA Modules:
  0.0 84.9 jit_solution(17478459291143151503)
XLA Ops:
  0.6 4.1 %collective-permute-start.1 = (bf16[384,128]{1,0:T(8,128)(2,1)}, bf16[384,128]{1,0:T(8,128)(2,1)S(1)}, u32[]{:S(2)}, u32[]{:S(2)}) collective-permute-start(bf16[384,128]{1,0:T(8,128)(2,1)} %refs_4_.1), channel_id=1, source_target_pairs={{0,2},{1,3},{2,0},{3,1},{4,6},{5,7},{6,4},{7,5},{8,10},{9,11},{10,... | collective-permute-start | bytes 294920 | tf_op jit(solution)/shard_map/ppermute | solution.py:554
  4.7 1.6 %collective-permute-start = (bf16[384,128]{1,0:T(8,128)(2,1)}, bf16[384,128]{1,0:T(8,128)(2,1)S(1)}, u32[]{:S(2)}, u32[]{:S(2)}) collective-permute-start(bf16[384,128]{1,0:T(8,128)(2,1)} %refs_4_.1), channel_id=1, source_target_pairs={{0,1},{1,0},{2,3},{3,2},{4,5},{5,4},{6,7},{7,6},{8,9},{9,8},{10,11... | collective-permute-start | bytes 294920 | tf_op jit(solution)/shard_map/ppermute | solution.py:554
  6.9 1.1 %copy-done.1 = bf16[384,1024]{1,0:T(8,128)(2,1)S(1)} copy-done((bf16[384,1024]{1,0:T(8,128)(2,1)S(1)}, bf16[384,1024]{1,0:T(8,128)(2,1)}, u32[]{:S(2)}) %copy-start.1) | copy-done | bytes 786456
  8.2 2.4 %first_stats.1 = (f32[8,3072]{1,0:T(8,128)S(1)}, bf16[384,1024]{1,0:T(8,128)(2,1)S(1)}, bf16[384,1024]{1,0:T(8,128)(2,1)S(1)}, bf16[384,128]{1,0:T(8,128)(2,1)S(...) custom-call(s32[1]{0:T(128)} %bitcast.refs_1_.refs_0_, s32[4]{0:T(128)S(1)} %bitcast.13, ...), custom_call_target="tpu_custom_call" | custom-call | flops 2415919104 | bytes 3145728 | tf_op jit(solution)/shard_map/first_stats/pallas_call | solution.py:39
  11.0 1.7 %prepare.1.refs_8_ = bf16[8192,384]{1,0:T(8,128)(2,1)S(1)} custom-call(bf16[384,8192]{1,0:T(8,128)(2,1)S(1)} %copy-done, f32[8,3072]{1,0:T(8,128)S(1)} %get-tuple-element.66.refs_1_.refs_5_), custom_call_target="tpu_custom_call" | custom-call | tf_op jit(solution)/shard_map/prepare/pallas_call | solution.py:39
  12.7 1.9 %collective-permute-start.2 = (bf16[384,128]{1,0:T(8,128)(2,1)S(1)}, bf16[384,128]{1,0:T(8,128)(2,1)S(1)}, u32[]{:S(2)}, u32[]{:S(2)}) collective-permute-start(bf16[384,128]{1,0:T(8,128)(2,1)S(1)} %collective-permute-done.1.refs_6_.refs_3_.refs_4_.refs_2_), channel_id=1, source_target_pairs={{0,1},{1,0},{2,3},{3,2},{4,5},{5,4},{6,7},{7,6},{8,9},{9,8},{10,11... | collective-permute-start | bytes 294920 | tf_op jit(solution)/shard_map/ppermute | solution.py:554
  14.6 1.1 %collective-permute-start.4 = (bf16[384,128]{1,0:T(8,128)(2,1)S(1)}, bf16[384,128]{1,0:T(8,128)(2,1)S(1)}, u32[]{:S(2)}, u32[]{:S(2)}) collective-permute-start(bf16[384,128]{1,0:T(8,128)(2,1)S(1)} %collective-permute-done.3.refs_7_.refs_4_.refs_5_), channel_id=1, source_target_pairs={{0,1},{1,0},{2,3},{3,2},{4,5},{5,4},{6,7},{7,6},{8,9},{9,8},{10,11... | collective-permute-start | bytes 294920 | tf_op jit(solution)/shard_map/ppermute | solution.py:554
  15.7 2.1 %next_stats.3.refs_5_ = f32[8,3072]{1,0:T(8,128)S(1)} custom-call(f32[8,128]{1,0:T(8,128)S(1)} %get-tuple-element.63.refs_0_, bf16[384,1024]{1,0:T(8,128)(2,1)S(1)} %get-tuple-element.64.refs_1_.refs_2_, bf16[384,1024]{1,0:T(8,128)(2,1)S(1)} %get-tuple-element.65.refs_2_.refs_3_, bf16[384,128]{1,0:T(8,128)(2,1)S(1)} %collective-permute-done.refs_3_.refs_4_.refs_1_, ...), custom_call_target="tpu_custom_call" | custom-call | flops 2415919104 | bytes 3145728 | tf_op jit(solution)/shard_map/next_stats/pallas_call | solution.py:39
  17.8 2.1 %next_stats.4.refs_5_ = f32[8,3072]{1,0:T(8,128)S(1)} custom-call(f32[8,128]{1,0:T(8,128)S(1)} %get-tuple-element.63.refs_0_, bf16[384,1024]{1,0:T(8,128)(2,1)S(1)} %get-tuple-element.64.refs_1_.refs_2_, bf16[384,1024]{1,0:T(8,128)(2,1)S(1)} %get-tuple-element.65.refs_2_.refs_3_, bf16[384,128]{1,0:T(8,128)(2,1)S(1)} %collective-permute-done.1.refs_6_.refs_3_.refs_4_.refs_2_, ...), custom_call_target="tpu_custom_call" | custom-call | flops 2415919104 | bytes 3145728 | tf_op jit(solution)/shard_map/next_stats/pallas_call | solution.py:39
  21.0 7.4 %collective-permute-start.7 = (bf16[384,128]{1,0:T(8,128)(2,1)S(1)}, bf16[384,128]{1,0:T(8,128)(2,1)S(1)}, u32[]{:S(2)}, u32[]{:S(2)}) collective-permute-start(bf16[384,128]{1,0:T(8,128)(2,1)S(1)} %get-tuple-element.68.refs_6_), channel_id=1, source_target_pairs={{0,3},{1,2},{2,1},{3,0},{4,7},{5,6},{6,5},{7,4},{8,11},{9,10},{10,... | collective-permute-start | bytes 294920 | tf_op jit(solution)/shard_map/ppermute | solution.py:554
  28.4 2.8 %block_gradients.4 = (bf16[384,256]{1,0:T(8,128)(2,1)S(1)}, bf16[384,3072]{1,0:T(8,128)(2,1)S(1)}) custom-call(f32[8,128]{1,0:T(8,128)S(1)} %get-tuple-element.63.refs_0_, f32[8,3072]{1,0:T(8,128)S(1)} %next_stats.5.refs_1_.refs_0_, bf16[384,1024]{1,0:T(8,128)(2,1)S(1)} %get-tuple-element.64.refs_1_.refs_2_, ...), custom_call_target="tpu_custom_call" | custom-call | tf_op jit(solution)/shard_map/block_gradients/pallas_call | solution.py:39
  31.7 1.5 %collective-permute-done.7.refs_7_.refs_2_ = bf16[384,128]{1,0:T(8,128)(2,1)S(1)} collective-permute-done((bf16[384,128]{1,0:T(8,128)(2,1)S(1)}, bf16[384,128]{1,0:T(8,128)(2,1)S(1)}, u32[]{:S(2)}, u32[]{:S(2)}) %collective-permute-start.7) | collective-permute-done | bytes 98336 | tf_op jit(solution)/shard_map/ppermute | solution.py:554
  33.2 3.0 %block_gradients.5 = (bf16[384,256]{1,0:T(8,128)(2,1)S(1)}, bf16[384,3072]{1,0:T(8,128)(2,1)S(1)}) custom-call(f32[8,128]{1,0:T(8,128)S(1)} %get-tuple-element.63.refs_0_, f32[8,3072]{1,0:T(8,128)S(1)} %next_stats.5.refs_1_.refs_0_, bf16[384,1024]{1,0:T(8,128)(2,1)S(1)} %get-tuple-element.64.refs_1_.refs_2_, ...), custom_call_target="tpu_custom_call" | custom-call | tf_op jit(solution)/shard_map/block_gradients/pallas_call | solution.py:39
  36.6 2.6 %own_gradients.1 = (f32[384,256]{1,0:T(8,128)S(1)}, bf16[384,3072]{1,0:T(8,128)(2,1)S(1)}) custom-call(f32[8,3072]{1,0:T(8,128)S(1)} %next_stats.5.refs_1_.refs_0_, bf16[384,1024]{1,0:T(8,128)(2,1)S(1)} %get-tuple-element.64.refs_1_.refs_2_, bf16[384,1024]{1,0:T(8,128)(2,1)S(1)} %get-tuple-element.65.refs_2_.refs_3_, ...), custom_call_target="tpu_custom_call" | custom-call | tf_op jit(solution)/shard_map/own_gradients/pallas_call | solution.py:39
  39.2 3.8 %collective-permute-done.9.refs_4_ = bf16[384,256]{1,0:T(8,128)(2,1)S(1)} collective-permute-done((bf16[384,256]{1,0:T(8,128)(2,1)S(1)}, bf16[384,256]{1,0:T(8,128)(2,1)S(1)}, u32[]{:S(2)}, u32[]{:S(2)}) %collective-permute-start.9) | collective-permute-done | bytes 196640 | tf_op jit(solution)/shard_map/ppermute | solution.py:554
  43.1 1.3 %send_tiles.2 = (bf16[2080,256]{1,0:T(8,128)(2,1)S(1)}, f32[16,128]{1,0:T(8,128)S(1)}, bf16[384,128]{1,0:T(8,128)(2,1)}, bf16[384,128]{1,0:T(8,128)(2,1)}, bf16[384,256]{1,0:T(8,128)(2,1)S(1)}) custom-call(s32[1]{0:T(128)} %bitcast.2.refs_0_, f32[384,256]{1,0:T(8,128)S(1)} %get-tuple-element.76.refs_1_, ...), custom_call_target="tpu_custom_call" | custom-call | flops 402653184 | bytes 4718592 | tf_op jit(solution)/shard_map/send_tiles/pallas_call | solution.py:39
  44.4 1.4 %kept_tiles.1 = (f32[4,512,256]{2,1,0:T(8,128)S(1)}, f32[4,512,256]{2,1,0:T(8,128)S(1)}, f32[16,128]{1,0:T(8,128)S(1)}) custom-call(s32[1]{0:T(128)} %bitcast.2.refs_0_, bf16[384,256]{1,0:T(8,128)(2,1)S(1)} %get-tuple-element.77.refs_1_, f32[16,128]{1,0:T(8,128)S(1)} %get-tuple-element.78.refs_2_, bf16[8,4,2,128,384]{4,3,2,1,0:T(8,128)(2,1)S(1)} %bitcast.6, ...), custom_call_target="tpu_custom_call" | custom-call | flops 805306368 | bytes 9437184 | tf_op jit(solution)/shard_map/kept_tiles/pallas_call | solution.py:39
  45.8 0.9 %send_tiles.3 = (bf16[2064,256]{1,0:T(8,128)(2,1)S(1)}, f32[16,128]{1,0:T(8,128)S(1)}) custom-call(s32[1]{0:T(128)} %bitcast.2.refs_0_, bf16[384,256]{1,0:T(8,128)(2,1)S(1)} %get-tuple-element.77.refs_1_, f32[16,128]{1,0:T(8,128)S(1)} %get-tuple-element.80.refs_2_, bf16[8,4,2,128,384]{4,3,2,1,0:T(8,128)(2,1)S(1)} %bitcast.7, f32[8,4,2,128,256]{4,3,2,1,0:T(8,128)S(1)} %bitcast.12), custom_call_target="tpu_custom_call" | custom-call | flops 402653184 | bytes 4718592 | tf_op jit(solution)/shard_map/send_tiles/pallas_call | solution.py:39
  46.8 0.5 collective-permute-start.10
  47.6 3.4 %collective-permute-start.18 = (bf16[1056,128]{1,0:T(8,128)(2,1)S(1)}, bf16[1056,128]{1,0:T(8,128)(2,1)S(1)}, u32[]{:S(2)}, u32[]{:S(2)}) collective-permute-start(bf16[1056,128]{1,0:T(8,128)(2,1)S(1)} %get-tuple-element.104), channel_id=1, source_target_pairs={{0,8},{4,12},{8,0},{12,4},{16,24},{20,28},{24,16},{28,20},{1,9},{5... | collective-permute-start | bytes 811016 | tf_op jit(solution)/shard_map/ppermute | solution.py:551
  51.3 2.0 %collective-permute-start.11 = (bf16[1040,128]{1,0:T(8,128)(2,1)S(1)}, bf16[1040,128]{1,0:T(8,128)(2,1)S(1)}, u32[]{:S(2)}, u32[]{:S(2)}) collective-permute-start(bf16[1040,128]{1,0:T(8,128)(2,1)S(1)} %get-tuple-element.87), channel_id=1, source_target_pairs={{0,8},{4,12},{8,0},{12,4},{16,24},{20,28},{24,16},{28,20},{1,9},{5... | collective-permute-start | bytes 798728 | tf_op jit(solution)/shard_map/ppermute | solution.py:551
  53.5 3.8 %query_gradients.1 = (bf16[384,1024]{1,0:T(8,128)(2,1)}, f32[8,128]{1,0:T(8,128)S(1)}) custom-call(bf16[384,128]{1,0:T(8,128)(2,1)S(1)} %get-tuple-element.62.refs_3_.refs_0_, bf16[384,128]{1,0:T(8,128)(2,1)S(1)} %collective-permute-done.refs_3_.refs_4_.refs_1_, bf16[384,128]{1,0:T(8,128)(2,1)S(1)} %collective-permute-done.1.refs_6_.refs_3_.refs_4_.refs_2_, ...), custom_call_target="tpu_custom_call" | custom-call | flops 1207959552 | bytes 6291456 | tf_op jit(solution)/shard_map/query_gradients/pallas_call | solution.py:39
  57.3 2.8 %collective-permute-done.19.refs_3_ = bf16[1024,128]{1,0:T(8,128)(2,1)S(1)} collective-permute-done((bf16[1024,128]{1,0:T(8,128)(2,1)S(1)}, bf16[1024,128]{1,0:T(8,128)(2,1)S(1)}, u32[]{:S(2)}, u32[]{:S(2)}) %collective-permute-start.19) | collective-permute-done | bytes 262176 | tf_op jit(solution)/shard_map/ppermute | solution.py:551
  60.5 5.2 %collective-permute-done.12.refs_3_ = bf16[1024,128]{1,0:T(8,128)(2,1)S(1)} collective-permute-done((bf16[1024,128]{1,0:T(8,128)(2,1)S(1)}, bf16[1024,128]{1,0:T(8,128)(2,1)S(1)}, u32[]{:S(2)}, u32[]{:S(2)}) %collective-permute-start.12) | collective-permute-done | bytes 262176 | tf_op jit(solution)/shard_map/ppermute | solution.py:551
  66.4 2.2 %collective-permute-done.20.refs_2_ = bf16[544,128]{1,0:T(8,128)(2,1)S(1)} collective-permute-done((bf16[544,128]{1,0:T(8,128)(2,1)S(1)}, bf16[544,128]{1,0:T(8,128)(2,1)S(1)}, u32[]{:S(2)}, u32[]{:S(2)}) %collective-permute-start.20) | collective-permute-done | bytes 139296 | tf_op jit(solution)/shard_map/ppermute | solution.py:551
  68.8 2.4 %collective-permute-done.14.refs_4_ = bf16[512,128]{1,0:T(8,128)(2,1)S(1)} collective-permute-done((bf16[512,128]{1,0:T(8,128)(2,1)S(1)}, bf16[512,128]{1,0:T(8,128)(2,1)S(1)}, u32[]{:S(2)}, u32[]{:S(2)}) %collective-permute-start.14) | collective-permute-done | bytes 131104 | tf_op jit(solution)/shard_map/ppermute | solution.py:551
  71.4 3.9 %collective-permute-done.22.refs_1_ = bf16[544,128]{1,0:T(8,128)(2,1)S(1)} collective-permute-done((bf16[544,128]{1,0:T(8,128)(2,1)S(1)}, bf16[544,128]{1,0:T(8,128)(2,1)S(1)}, u32[]{:S(2)}, u32[]{:S(2)}) %collective-permute-start.22) | collective-permute-done | bytes 139296 | tf_op jit(solution)/shard_map/ppermute | solution.py:554
  75.3 1.9 %collective-permute-start.23 = (bf16[288,128]{1,0:T(8,128)(2,1)S(1)}, bf16[288,128]{1,0:T(8,128)(2,1)S(1)}, u32[]{:S(2)}, u32[]{:S(2)}) collective-permute-start(bf16[288,128]{1,0:T(8,128)(2,1)S(1)} %get-tuple-element.115), channel_id=1, source_target_pairs={{0,2},{1,3},{2,0},{3,1},{4,6},{5,7},{6,4},{7,5},{8,10},{9,11},{10,... | collective-permute-start | bytes 221192 | tf_op jit(solution)/shard_map/ppermute | solution.py:554
  77.4 1.5 %collective-permute-start.16 = (bf16[272,128]{1,0:T(8,128)(2,1)S(1)}, bf16[272,128]{1,0:T(8,128)(2,1)S(1)}, u32[]{:S(2)}, u32[]{:S(2)}) collective-permute-start(bf16[272,128]{1,0:T(8,128)(2,1)S(1)} %get-tuple-element.100), channel_id=1, source_target_pairs={{0,2},{1,3},{2,0},{3,1},{4,6},{5,7},{6,4},{7,5},{8,10},{9,11},{10,... | collective-permute-start | bytes 208904 | tf_op jit(solution)/shard_map/ppermute | solution.py:554
  78.9 4.5 %collective-permute-done.16.refs_3_ = bf16[272,128]{1,0:T(8,128)(2,1)S(1)} collective-permute-done((bf16[272,128]{1,0:T(8,128)(2,1)S(1)}, bf16[272,128]{1,0:T(8,128)(2,1)S(1)}, u32[]{:S(2)}, u32[]{:S(2)}) %collective-permute-start.16) | collective-permute-done | bytes 69664 | tf_op jit(solution)/shard_map/ppermute | solution.py:554
  83.4 0.9 %final_stage.1 = (f32[256,256]{1,0:T(8,128)}, f32[8,32]{1,0:T(8,128)S(1)}) custom-call(s32[1]{0:T(128)} %bitcast.2.refs_0_, s32[1]{0:T(128)} %bitcast.refs_1_.refs_0_, f32[256,128]{1,0:T(8,128)S(1)} %get-tuple-element.99.refs_2_, bf16[272,128]{1,0:T(8,128)(2,1)S(1)} %collective-permute-done.16.refs_3_, f32[256,128]{1,0:T(8,128)S(1)} %get-tuple-element.114.refs_4_, ...), custom_call_target="tpu_custom_call" | custom-call | tf_op jit(solution)/shard_map/final_stage/pallas_call | solution.py:39
  84.3 0.6 reshape.21
  (58 shorter events, 5.6 us)
Async XLA Ops:
  0.6 12.1 %collective-permute-start.1 = (bf16[384,128]{1,0:T(8,128)(2,1)}, bf16[384,128]{1,0:T(8,128)(2,1)S(1)}, u32[]{:S(2)}, u32[]{:S(2)}) collective-permute-start(bf16[384,128]{1,0:T(8,128)(2,1)} %refs_4_.1), channel_id=1, source_target_pairs={{0,2},{1,3},{2,0},{3,1},{4,6},{5,7},{6,4},{7,5},{8,10},{9,11},{10,... | collective-permute-start | bytes 294920 | tf_op jit(solution)/shard_map/ppermute | solution.py:554
  4.7 11.0 %collective-permute-start = (bf16[384,128]{1,0:T(8,128)(2,1)}, bf16[384,128]{1,0:T(8,128)(2,1)S(1)}, u32[]{:S(2)}, u32[]{:S(2)}) collective-permute-start(bf16[384,128]{1,0:T(8,128)(2,1)} %refs_4_.1), channel_id=1, source_target_pairs={{0,1},{1,0},{2,3},{3,2},{4,5},{5,4},{6,7},{7,6},{8,9},{9,8},{10,11... | collective-permute-start | bytes 294920 | tf_op jit(solution)/shard_map/ppermute | solution.py:554
  6.3 9.4 %collective-permute-start.5 = (bf16[384,128]{1,0:T(8,128)(2,1)}, bf16[384,128]{1,0:T(8,128)(2,1)S(1)}, u32[]{:S(2)}, u32[]{:S(2)}) collective-permute-start(bf16[384,128]{1,0:T(8,128)(2,1)} %refs_5_.1), channel_id=1, source_target_pairs={{0,1},{1,0},{2,3},{3,2},{4,5},{5,4},{6,7},{7,6},{8,9},{9,8},{10,11... | collective-permute-start | bytes 294920 | tf_op jit(solution)/shard_map/ppermute | solution.py:554
  6.8 7.8 %collective-permute-start.3 = (bf16[384,128]{1,0:T(8,128)(2,1)}, bf16[384,128]{1,0:T(8,128)(2,1)S(1)}, u32[]{:S(2)}, u32[]{:S(2)}) collective-permute-start(bf16[384,128]{1,0:T(8,128)(2,1)} %refs_5_.1), channel_id=1, source_target_pairs={{0,2},{1,3},{2,0},{3,1},{4,6},{5,7},{6,4},{7,5},{8,10},{9,11},{10,... | collective-permute-start | bytes 294920 | tf_op jit(solution)/shard_map/ppermute | solution.py:554
  6.8 1.1 %copy-start.1 = (bf16[384,1024]{1,0:T(8,128)(2,1)S(1)}, bf16[384,1024]{1,0:T(8,128)(2,1)}, u32[]{:S(2)}) copy-start(bf16[384,1024]{1,0:T(8,128)(2,1)} %refs_2_.1) | copy-start | bytes 2359300
  6.8 1.4 %copy-start.2 = (bf16[384,1024]{1,0:T(8,128)(2,1)S(1)}, bf16[384,1024]{1,0:T(8,128)(2,1)}, u32[]{:S(2)}) copy-start(bf16[384,1024]{1,0:T(8,128)(2,1)} %refs_3_.1) | copy-start | bytes 2359300
  6.8 1.4 %copy-start.3 = (bf16[384,128]{1,0:T(8,128)(2,1)S(1)}, bf16[384,128]{1,0:T(8,128)(2,1)}, u32[]{:S(2)}) copy-start(bf16[384,128]{1,0:T(8,128)(2,1)} %refs_4_.1) | copy-start | bytes 294916
  6.8 1.4 %copy-start.4 = (bf16[384,128]{1,0:T(8,128)(2,1)S(1)}, bf16[384,128]{1,0:T(8,128)(2,1)}, u32[]{:S(2)}) copy-start(bf16[384,128]{1,0:T(8,128)(2,1)} %refs_5_.1) | copy-start | bytes 294916
  6.9 1.4 %copy-start.5 = (s32[1,4]{1,0:T(1,128)S(1)}, s32[1,4]{1,0:T(1,128)}, u32[]{:S(2)}) copy-start(s32[1,4]{1,0:T(1,128)} %param.7) | copy-start | bytes 52
  8.2 2.8 %copy-start = (bf16[384,8192]{1,0:T(8,128)(2,1)S(1)}, bf16[384,8192]{1,0:T(8,128)(2,1)}, u32[]{:S(2)}) copy-start(bf16[384,8192]{1,0:T(8,128)(2,1)} %refs_0_.1) | copy-start | bytes 18874372
  12.7 7.2 %collective-permute-start.2 = (bf16[384,128]{1,0:T(8,128)(2,1)S(1)}, bf16[384,128]{1,0:T(8,128)(2,1)S(1)}, u32[]{:S(2)}, u32[]{:S(2)}) collective-permute-start(bf16[384,128]{1,0:T(8,128)(2,1)S(1)} %collective-permute-done.1.refs_6_.refs_3_.refs_4_.refs_2_), channel_id=1, source_target_pairs={{0,1},{1,0},{2,3},{3,2},{4,5},{5,4},{6,7},{7,6},{8,9},{9,8},{10,11... | collective-permute-start | bytes 294920 | tf_op jit(solution)/shard_map/ppermute | solution.py:554
  14.6 5.3 %collective-permute-start.4 = (bf16[384,128]{1,0:T(8,128)(2,1)S(1)}, bf16[384,128]{1,0:T(8,128)(2,1)S(1)}, u32[]{:S(2)}, u32[]{:S(2)}) collective-permute-start(bf16[384,128]{1,0:T(8,128)(2,1)S(1)} %collective-permute-done.3.refs_7_.refs_4_.refs_5_), channel_id=1, source_target_pairs={{0,1},{1,0},{2,3},{3,2},{4,5},{5,4},{6,7},{7,6},{8,9},{9,8},{10,11... | collective-permute-start | bytes 294920 | tf_op jit(solution)/shard_map/ppermute | solution.py:554
  17.8 25.3 %slice-start = ((s8[8388608]{0:T(1024)(128)(4,1)}), s8[4194304]{0:T(1024)(128)(4,1)S(1)}, s32[]{:S(2)}) async-start(s8[8388608]{0:T(1024)(128)(4,1)} %bitcast.8), calls=%async_computation | async-start | bytes 8388608
  19.9 23.2 %slice-start.1 = ((s8[8388608]{0:T(1024)(128)(4,1)}), s8[4194304]{0:T(1024)(128)(4,1)S(1)}, s32[]{:S(2)}) async-start(s8[8388608]{0:T(1024)(128)(4,1)} %bitcast.8), calls=%async_computation.1 | async-start | bytes 8388608
  20.5 10.6 %collective-permute-start.6 = (bf16[384,128]{1,0:T(8,128)(2,1)S(1)}, bf16[384,128]{1,0:T(8,128)(2,1)S(1)}, u32[]{:S(2)}, u32[]{:S(2)}) collective-permute-start(bf16[384,128]{1,0:T(8,128)(2,1)S(1)} %get-tuple-element.70), channel_id=1, source_target_pairs={{0,1},{1,0},{2,3},{3,2},{4,5},{5,4},{6,7},{7,6},{8,9},{9,8},{10,11... | collective-permute-start | bytes 294920 | tf_op jit(solution)/shard_map/ppermute | solution.py:554
  21.0 12.2 %collective-permute-start.7 = (bf16[384,128]{1,0:T(8,128)(2,1)S(1)}, bf16[384,128]{1,0:T(8,128)(2,1)S(1)}, u32[]{:S(2)}, u32[]{:S(2)}) collective-permute-start(bf16[384,128]{1,0:T(8,128)(2,1)S(1)} %get-tuple-element.68.refs_6_), channel_id=1, source_target_pairs={{0,3},{1,2},{2,1},{3,0},{4,7},{5,6},{6,5},{7,4},{8,11},{9,10},{10,... | collective-permute-start | bytes 294920 | tf_op jit(solution)/shard_map/ppermute | solution.py:554
  31.3 11.8 %collective-permute-start.8 = (bf16[400,256]{1,0:T(8,128)(2,1)S(1)}, bf16[400,256]{1,0:T(8,128)(2,1)S(1)}, u32[]{:S(2)}, u32[]{:S(2)}) collective-permute-start(bf16[400,256]{1,0:T(8,128)(2,1)S(1)} %merge.1.refs_6_), channel_id=1, source_target_pairs={{0,2},{1,3},{2,0},{3,1},{4,6},{5,7},{6,4},{7,5},{8,10},{9,11},{10,... | collective-permute-start | bytes 614408 | tf_op jit(solution)/shard_map/ppermute | solution.py:554
  36.2 6.9 %collective-permute-start.9 = (bf16[384,256]{1,0:T(8,128)(2,1)S(1)}, bf16[384,256]{1,0:T(8,128)(2,1)S(1)}, u32[]{:S(2)}, u32[]{:S(2)}) collective-permute-start(bf16[384,256]{1,0:T(8,128)(2,1)S(1)} %get-tuple-element.71.refs_5_), channel_id=1, source_target_pairs={{0,1},{1,0},{2,3},{3,2},{4,5},{5,4},{6,7},{7,6},{8,9},{9,8},{10,11... | collective-permute-start | bytes 589832 | tf_op jit(solution)/shard_map/ppermute | solution.py:554
  44.4 2.9 %collective-permute-start.17 = (bf16[2080,256]{1,0:T(8,128)(2,1)S(1)}, bf16[2080,256]{1,0:T(8,128)(2,1)S(1)}, u32[]{:S(2)}, u32[]{:S(2)}) collective-permute-start(bf16[2080,256]{1,0:T(8,128)(2,1)S(1)} %get-tuple-element.102), channel_id=1, source_target_pairs={{0,4},{4,0},{8,12},{12,8},{16,20},{20,16},{24,28},{28,24},{1,5},{5... | collective-permute-start | bytes 3194888 | tf_op jit(solution)/shard_map/ppermute | solution.py:551
  46.8 4.2 %collective-permute-start.10 = (bf16[2064,256]{1,0:T(8,128)(2,1)S(1)}, bf16[2064,256]{1,0:T(8,128)(2,1)S(1)}, u32[]{:S(2)}, u32[]{:S(2)}) collective-permute-start(bf16[2064,256]{1,0:T(8,128)(2,1)S(1)} %get-tuple-element.81), channel_id=1, source_target_pairs={{0,4},{4,0},{8,12},{12,8},{16,20},{20,16},{24,28},{28,24},{1,5},{5... | collective-permute-start | bytes 3170312 | tf_op jit(solution)/shard_map/ppermute | solution.py:551
  47.6 12.6 %collective-permute-start.18 = (bf16[1056,128]{1,0:T(8,128)(2,1)S(1)}, bf16[1056,128]{1,0:T(8,128)(2,1)S(1)}, u32[]{:S(2)}, u32[]{:S(2)}) collective-permute-start(bf16[1056,128]{1,0:T(8,128)(2,1)S(1)} %get-tuple-element.104), channel_id=1, source_target_pairs={{0,8},{4,12},{8,0},{12,4},{16,24},{20,28},{24,16},{28,20},{1,9},{5... | collective-permute-start | bytes 811016 | tf_op jit(solution)/shard_map/ppermute | solution.py:551
  50.9 9.2 %collective-permute-start.19 = (bf16[1024,128]{1,0:T(8,128)(2,1)S(1)}, bf16[1024,128]{1,0:T(8,128)(2,1)S(1)}, u32[]{:S(2)}, u32[]{:S(2)}) collective-permute-start(bf16[1024,128]{1,0:T(8,128)(2,1)S(1)} %get-tuple-element.106), channel_id=1, source_target_pairs={{0,16},{4,20},{8,24},{12,28},{16,0},{20,4},{24,8},{28,12},{1,17},{... | collective-permute-start | bytes 786440 | tf_op jit(solution)/shard_map/ppermute | solution.py:551
  51.3 14.4 %collective-permute-start.11 = (bf16[1040,128]{1,0:T(8,128)(2,1)S(1)}, bf16[1040,128]{1,0:T(8,128)(2,1)S(1)}, u32[]{:S(2)}, u32[]{:S(2)}) collective-permute-start(bf16[1040,128]{1,0:T(8,128)(2,1)S(1)} %get-tuple-element.87), channel_id=1, source_target_pairs={{0,8},{4,12},{8,0},{12,4},{16,24},{20,28},{24,16},{28,20},{1,9},{5... | collective-permute-start | bytes 798728 | tf_op jit(solution)/shard_map/ppermute | solution.py:551
  53.4 12.4 %collective-permute-start.12 = (bf16[1024,128]{1,0:T(8,128)(2,1)S(1)}, bf16[1024,128]{1,0:T(8,128)(2,1)S(1)}, u32[]{:S(2)}, u32[]{:S(2)}) collective-permute-start(bf16[1024,128]{1,0:T(8,128)(2,1)S(1)} %get-tuple-element.89), channel_id=1, source_target_pairs={{0,16},{4,20},{8,24},{12,28},{16,0},{20,4},{24,8},{28,12},{1,17},{... | collective-permute-start | bytes 786440 | tf_op jit(solution)/shard_map/ppermute | solution.py:551
  60.3 8.4 %collective-permute-start.20 = (bf16[544,128]{1,0:T(8,128)(2,1)S(1)}, bf16[544,128]{1,0:T(8,128)(2,1)S(1)}, u32[]{:S(2)}, u32[]{:S(2)}) collective-permute-start(bf16[544,128]{1,0:T(8,128)(2,1)S(1)} %get-tuple-element.109), channel_id=1, source_target_pairs={{0,16},{4,20},{8,24},{12,28},{16,0},{20,4},{24,8},{28,12},{1,17},{... | collective-permute-start | bytes 417800 | tf_op jit(solution)/shard_map/ppermute | solution.py:551
  60.3 6.0 %collective-permute-start.21 = (bf16[512,128]{1,0:T(8,128)(2,1)S(1)}, bf16[512,128]{1,0:T(8,128)(2,1)S(1)}, u32[]{:S(2)}, u32[]{:S(2)}) collective-permute-start(bf16[512,128]{1,0:T(8,128)(2,1)S(1)} %get-tuple-element.111), channel_id=1, source_target_pairs={{0,8},{4,12},{8,0},{12,4},{16,24},{20,28},{24,16},{28,20},{1,9},{5... | collective-permute-start | bytes 393224 | tf_op jit(solution)/shard_map/ppermute | solution.py:551
  66.0 5.1 %collective-permute-start.13 = (bf16[528,128]{1,0:T(8,128)(2,1)S(1)}, bf16[528,128]{1,0:T(8,128)(2,1)S(1)}, u32[]{:S(2)}, u32[]{:S(2)}) collective-permute-start(bf16[528,128]{1,0:T(8,128)(2,1)S(1)} %get-tuple-element.92), channel_id=1, source_target_pairs={{0,16},{4,20},{8,24},{12,28},{16,0},{20,4},{24,8},{28,12},{1,17},{... | collective-permute-start | bytes 405512 | tf_op jit(solution)/shard_map/ppermute | solution.py:551
  66.1 5.0 %collective-permute-start.14 = (bf16[512,128]{1,0:T(8,128)(2,1)S(1)}, bf16[512,128]{1,0:T(8,128)(2,1)S(1)}, u32[]{:S(2)}, u32[]{:S(2)}) collective-permute-start(bf16[512,128]{1,0:T(8,128)(2,1)S(1)} %get-tuple-element.94), channel_id=1, source_target_pairs={{0,8},{4,12},{8,0},{12,4},{16,24},{20,28},{24,16},{28,20},{1,9},{5... | collective-permute-start | bytes 393224 | tf_op jit(solution)/shard_map/ppermute | solution.py:551
  68.7 6.6 %collective-permute-start.22 = (bf16[544,128]{1,0:T(8,128)(2,1)S(1)}, bf16[544,128]{1,0:T(8,128)(2,1)S(1)}, u32[]{:S(2)}, u32[]{:S(2)}) collective-permute-start(bf16[544,128]{1,0:T(8,128)(2,1)S(1)} %get-tuple-element.113), channel_id=1, source_target_pairs={{0,1},{1,0},{2,3},{3,2},{4,5},{5,4},{6,7},{7,6},{8,9},{9,8},{10,11... | collective-permute-start | bytes 417800 | tf_op jit(solution)/shard_map/ppermute | solution.py:554
  71.3 5.9 %collective-permute-start.15 = (bf16[528,128]{1,0:T(8,128)(2,1)S(1)}, bf16[528,128]{1,0:T(8,128)(2,1)S(1)}, u32[]{:S(2)}, u32[]{:S(2)}) collective-permute-start(bf16[528,128]{1,0:T(8,128)(2,1)S(1)} %get-tuple-element.97), channel_id=1, source_target_pairs={{0,1},{1,0},{2,3},{3,2},{4,5},{5,4},{6,7},{7,6},{8,9},{9,8},{10,11... | collective-permute-start | bytes 405512 | tf_op jit(solution)/shard_map/ppermute | solution.py:554
  75.3 8.1 %collective-permute-start.23 = (bf16[288,128]{1,0:T(8,128)(2,1)S(1)}, bf16[288,128]{1,0:T(8,128)(2,1)S(1)}, u32[]{:S(2)}, u32[]{:S(2)}) collective-permute-start(bf16[288,128]{1,0:T(8,128)(2,1)S(1)} %get-tuple-element.115), channel_id=1, source_target_pairs={{0,2},{1,3},{2,0},{3,1},{4,6},{5,7},{6,4},{7,5},{8,10},{9,11},{10,... | collective-permute-start | bytes 221192 | tf_op jit(solution)/shard_map/ppermute | solution.py:554
  77.4 6.0 %collective-permute-start.16 = (bf16[272,128]{1,0:T(8,128)(2,1)S(1)}, bf16[272,128]{1,0:T(8,128)(2,1)S(1)}, u32[]{:S(2)}, u32[]{:S(2)}) collective-permute-start(bf16[272,128]{1,0:T(8,128)(2,1)S(1)} %get-tuple-element.100), channel_id=1, source_target_pairs={{0,2},{1,3},{2,0},{3,1},{4,6},{5,7},{6,4},{7,5},{8,10},{9,11},{10,... | collective-permute-start | bytes 208904 | tf_op jit(solution)/shard_map/ppermute | solution.py:554

commit v12 on v11

--- a/solution.py
+++ b/solution.py
@@ -186,22 +186,21 @@
     return dk[...] * inverse, dv[...]
 
 
-def other_kernel(b, flags, stats, q_ref, do_ref, k_ref, v_ref, *refs):
-    *outs, ds_out, p_buf, dk, dv = refs
+def other_kernel(b, flags, stats, q_ref, do_ref, k_ref, v_ref, dk_out, dv_out, ds_out, p_buf, dk, dv):
     keep = counted(b, flags)
-    hd = dk.shape[1]
-    dk_out, dv_out = outs if len(outs) == 2 else (outs[0].at[:, pl.ds(0, hd)], outs[0].at[:, pl.ds(hd, hd)])
+    rows = dk.shape[0]
 
     @pl.when(keep)
     def _():
         dk_sum, dv_sum = block_gradients(False, stats, q_ref, do_ref, k_ref, v_ref, p_buf, ds_out, dk, dv)
         dk_out[...] = dk_sum.astype(BF16)
-        dv_out[...] = dv_sum.astype(BF16)
+        dv_out[:rows, :] = dv_sum.astype(BF16)
+        dv_out[rows:, :] = jnp.zeros((dv_out.shape[0] - rows, dv.shape[1]), BF16)
 
     @pl.when(jnp.logical_not(keep))
     def _():
-        for out in outs:
-            out[...] = jnp.zeros_like(out)
+        dk_out[...] = jnp.zeros_like(dk_out)
+        dv_out[...] = jnp.zeros_like(dv_out)
         ds_out[...] = jnp.zeros_like(ds_out)
 
 
@@ -224,24 +223,17 @@
         dq_ref[:, h * hd : (h + 1) * hd] = (dq / hd**0.5).astype(BF16)
 
 
-def merge_kernel(n_got, own_ref, *refs):
-    got_refs, out_ref = refs[:n_got], refs[n_got]
-    rows, width = own_ref.shape
-    at = width - got_refs[0].shape[1]
-    total = own_ref[:, at:].astype(F32)
-    for got in got_refs:
-        total = total + got[...].astype(F32)
-    out_ref[:rows, at:] = total.astype(BF16)
-    if at:
-        out_ref[:rows, :at] = own_ref[:, :at]
+def merge_kernel(rows, *refs):
+    *terms, out_ref = refs
+    total = functools.reduce(jnp.add, [term[:rows, :].astype(F32) for term in terms])
+    out_ref[:rows, :] = total.astype(BF16)
     if out_ref.shape[0] > rows:
-        out_ref[rows:, :] = jnp.zeros((out_ref.shape[0] - rows, width), BF16)
-
-
-def merge(own, got, extra, after):
-    outs = [shape((own.shape[0] + extra, own.shape[1]))]
-    kernel = functools.partial(merge_kernel, len(got))
-    return whole_call(kernel, "merge", [], [own, *got], outs, 4, (0, 0), [], after)[0]
+        out_ref[rows:, :] = jnp.zeros((out_ref.shape[0] - rows, out_ref.shape[1]), BF16)
+
+
+def merge(rows, terms, after):
+    outs = [shape(terms[0].shape)]
+    return whole_call(functools.partial(merge_kernel, rows), "merge", [], terms, outs, 4, (0, 0), [], after)[0]
 
 
 def attention(me, spans, queries, out_grad, keys, values, activations, mark, swap, n):
@@ -283,29 +275,30 @@
         )[0]
     p_buf = pltpu.VMEM((rows, 2 * rows), BF16)
     sums = [pltpu.VMEM((rows, hd), F32)] * 2
-    parts, straight, score_grads, before = [[] for _ in range(n)], [], [None] * n, []
+    key_parts, value_parts = [[] for _ in range(n)], [[] for _ in range(n)]
+    score_grads, own_parts, before = [None] * n, {}, []
     for b in range(n - 1, 0, -1):
-        far = b & (b - 1)
-        outs = [shape((rows, hd))] * 2 if far else [shape((rows, 2 * hd))]
-        *part, score_grads[b] = whole_call(
+        dk, dv, score_grads[b] = whole_call(
             functools.partial(other_kernel, b),
             "block_gradients",
             [],
             [flags, stats, queries, out_grad, *blocks[b]],
-            outs + [shape((rows, tall))],
+            [shape((rows, hd)), shape((rows + TOP_ROWS, hd)), shape((rows, tall))],
             10,
             (0, 0),
             [p_buf, *sums],
-            before if far or b > 1 else [*before, *straight],
+            before,
         )
-        before = part[:1]
-        if far:
-            straight.append(swap(part[0], b))
-        part = part[-1]
-        if parts[b]:
-            part = merge(part, parts[b], 0 if far else TOP_ROWS, [])
-            before = [part]
-        parts[far].append(swap(part, b & -b))
+        own_parts[b] = dk
+        if value_parts[b]:
+            dv = merge(rows, [dv, *value_parts[b]], [])
+        value_parts[b & (b - 1)].append(swap(dv, b & -b))
+        before = [dv]
+    for b in range(n - 1, 0, -1):
+        dk = own_parts[b]
+        if key_parts[b]:
+            dk = merge(rows, [dk, *key_parts[b]], before)
+        key_parts[b & (b - 1)].append(swap(dk, b & -b))
     own, score_grads[0] = whole_call(
         own_kernel,
         "own_gradients",
@@ -317,7 +310,7 @@
         [p_buf, *sums],
         before,
     )
-    return own, [*straight, *parts[0]], [blocks[b][0] for b in range(n)], score_grads, acts
+    return own, key_parts[0], value_parts[0], [blocks[b][0] for b in range(n)], score_grads, acts
 
 
 def query_gradients(key_blocks, score_grads, columns, after):
@@ -363,90 +356,97 @@
     return sum(((step >> (bits - 1 - j)) & 1) << (j - 1) for j in range(1, bits))
 
 
-def corrected_tile(chosen, dest, grads, a_ref, e_ref, top_ref):
-    _, n_ctx, sets, rows_set, rows = a_ref.shape
-    tall = n_ctx * rows_set
-    a = a_ref[dest, :, chosen].reshape(tall, rows)
-    e = e_ref[dest, :, chosen].reshape(tall, e_ref.shape[4])
+def corrected_tile(at, dest, grads, a_ref, e_ref, top_ref):
+    _, n_ctx, rows_ctx, rows = a_ref.shape
+    tall = n_ctx * rows_ctx
+    hd = grads.shape[1]
+    a = a_ref[dest].reshape(tall, rows)
+    e = e_ref[dest, :, :, at : at + hd].reshape(tall, hd)
     c = jnp.dot(a, grads, preferred_element_type=F32) + e
-
-    mags = jnp.max(jnp.abs(c).reshape(tall // QROWS, QROWS, c.shape[1]), axis=1)
+    mags = jnp.max(jnp.abs(c).reshape(tall // QROWS, QROWS, hd), axis=1)
     mags = jnp.max(mags, axis=1, keepdims=True)
-    per_set = rows_set // QROWS
     block = lax.broadcasted_iota(jnp.int32, (tall // QROWS, TOP_LANES), 0)
     lane = lax.broadcasted_iota(jnp.int32, (tall // QROWS, TOP_LANES), 1)
-    shift = per_set.bit_length() - 1
-    place = ((block >> shift) * (sets * per_set)) + chosen * per_set + (block & (per_set - 1))
-    top = jnp.max(jnp.where(lane == place, mags, 0.0), axis=0, keepdims=True)
+    top = jnp.max(jnp.where(lane == block, mags, 0.0), axis=0, keepdims=True)
     top_ref[pl.ds(dest, 1), :] = jnp.maximum(top_ref[pl.ds(dest, 1), :], top)
     return c
 
 
-def send_rows(bits, shrink, chosen, me_ref, total, a_ref, e_ref, out_ref, top_ref, packed):
-    tall = a_ref.shape[1] * a_ref.shape[3]
+def summed_grads(at, own_ref, part_refs):
+    rows, hd = own_ref.shape[0], own_ref.shape[1] // 2
+    total = own_ref[:, at : at + hd]
+    for part in part_refs:
+        total = total + part[:rows, :].astype(F32)
+    return total.astype(BF16)
+
+
+def send_rows(bits, shrink, at, me_ref, total, a_ref, e_ref, out_ref, top_ref, packed):
+    tall = a_ref.shape[1] * a_ref.shape[2]
     steps = a_ref.shape[0] // 2
     for step in range(steps):
         dest = tile_of(step, me_ref[0], bits, 1)
-        c = corrected_tile(chosen, dest, total, a_ref, e_ref, top_ref)
+        c = corrected_tile(at, dest, total, a_ref, e_ref, top_ref)
         out_ref[step * tall : (step + 1) * tall, :] = (c * shrink).astype(BF16)
-    out_ref[steps * tall :, :] = jnp.zeros((out_ref.shape[0] - steps * tall, out_ref.shape[1]), BF16)
-    if packed:
-        out_ref[steps * tall :, :TOP_LANES] = pack_top(top_ref[...])
-
-
-def first_send_kernel(bits, shrink, n_parts, me_ref, own_ref, *refs):
-    part_refs = refs[:n_parts]
-    a_ref, e_ref, out_ref, top_ref, kg_ref, vg_ref, grads_ref = refs[n_parts:]
-    total = own_ref[...]
-    for part in part_refs:
-        got = part[: total.shape[0], :].astype(F32)
-        if got.shape[1] < total.shape[1]:
-            got = jnp.concatenate([got, jnp.zeros_like(got)], axis=1)
-        total = total + got
-    total = total.astype(BF16)
-    hd = total.shape[1] // 2
-    kg_ref[...] = total[:, :hd]
-    vg_ref[...] = total[:, hd:]
+    tail = jnp.zeros((out_ref.shape[0] - steps * tall, out_ref.shape[1]), BF16)
+    out_ref[steps * tall :, :] = pack_top(top_ref[...]) if packed else tail
+
+
+def kept_rows(bits, shrink, at, me_ref, total, a_ref, e_ref, out_ref, top_ref):
+    for step in range(out_ref.shape[0]):
+        dest = tile_of(step, me_ref[0], bits, 0)
+        out_ref[step] = corrected_tile(at, dest, total, a_ref, e_ref, top_ref) * shrink
+
+
+def first_send_kernel(bits, shrink, at, n_parts, me_ref, own_ref, *refs):
+    a_ref, e_ref, out_ref, top_ref, grads_ref, grads_out = refs[n_parts:]
+    total = summed_grads(at, own_ref, refs[:n_parts])
     grads_ref[...] = total
+    grads_out[...] = total
     top_ref[...] = jnp.zeros_like(top_ref)
-    send_rows(bits, shrink, 0, me_ref, total, a_ref, e_ref, out_ref, top_ref, False)
-
-
-def next_send_kernel(bits, shrink, chosen, packed, me_ref, grads_ref, before_ref, a_ref, e_ref, out_ref, top_ref):
+    send_rows(bits, shrink, at, me_ref, total, a_ref, e_ref, out_ref, top_ref, False)
+
+
+def next_kept_kernel(bits, shrink, at, me_ref, grads_ref, before_ref, a_ref, e_ref, out_ref, top_ref):
     top_ref[...] = before_ref[...]
-    send_rows(bits, shrink, chosen, me_ref, grads_ref[...], a_ref, e_ref, out_ref, top_ref, packed)
-
-
-def kept_kernel(bits, shrink, me_ref, grads_ref, before_ref, a_ref, e_ref, *outs):
-    *kept, top_ref = outs
+    kept_rows(bits, shrink, at, me_ref, grads_ref[...], a_ref, e_ref, out_ref, top_ref)
+
+
+def first_kept_kernel(bits, shrink, at, n_parts, me_ref, own_ref, *refs):
+    before_ref, a_ref, e_ref, out_ref, top_ref, grads_ref, grads_out = refs[n_parts:]
+    total = summed_grads(at, own_ref, refs[:n_parts])
+    grads_ref[...] = total
+    grads_out[...] = total
     top_ref[...] = before_ref[...]
-    total = grads_ref[...]
-    for chosen, out_ref in enumerate(kept):
-        for step in range(out_ref.shape[0]):
-            dest = tile_of(step, me_ref[0], bits, 0)
-            out_ref[step] = corrected_tile(chosen, dest, total, a_ref, e_ref, top_ref) * shrink
-
-
-def split_kernel(bits, n_tops, kept, got, *refs):
-    steps, tall, width = kept.shape
+    kept_rows(bits, shrink, at, me_ref, total, a_ref, e_ref, out_ref, top_ref)
+
+
+def next_send_kernel(bits, shrink, at, me_ref, grads_ref, before_ref, a_ref, e_ref, out_ref, top_ref):
+    top_ref[...] = before_ref[...]
+    send_rows(bits, shrink, at, me_ref, grads_ref[...], a_ref, e_ref, out_ref, top_ref, True)
+
+
+def split_kernel(bits, n_ctx, n_tops, kept, got, *refs):
+    steps, tall, hd = kept.shape
     half = steps // 2
-    hd = width // 2
+    part_tall = tall // 2
     tops = refs[:n_tops]
     low_away, low_stay, high_away, high_stay, *top_out = refs[n_tops:]
     for step in range(steps):
         c = (kept[step] + got[step * tall : (step + 1) * tall, :].astype(F32)).astype(BF16)
+        c = c.reshape(n_ctx, 2, part_tall // n_ctx, hd)
         back = reversed_step(step, bits)
-        for at, part, away, stay in ((step, c[:, :hd], low_away, low_stay), (back, c[:, hd:], high_away, high_stay)):
+        for at, i, away, stay in ((step, 0, low_away, low_stay), (back, 1, high_away, high_stay)):
+            part = c[:, i].reshape(part_tall, hd)
             if at < half:
-                away[at * tall : (at + 1) * tall, :] = part
+                away[at * part_tall : (at + 1) * part_tall, :] = part
             else:
-                stay[(at - half) * tall : (at - half + 1) * tall, :] = part
+                stay[(at - half) * part_tall : (at - half + 1) * part_tall, :] = part
     if tops:
         top = largest(tops, got, steps * tall)
         top_out[0][...] = top
-        low_away[half * tall :, :] = pack_top(top)
+        low_away[half * part_tall :, :] = pack_top(top)
     else:
-        low_away[half * tall :, :] = jnp.zeros((low_away.shape[0] - half * tall, hd), BF16)
+        low_away[half * part_tall :, :] = jnp.zeros((low_away.shape[0] - half * part_tall, hd), BF16)
 
 
 def largest(tops, low_got, size):
@@ -514,35 +514,32 @@
         away[half:, :] = jnp.zeros((away.shape[0] - half, away.shape[1]), BF16)
 
 
-def final_kernel(sets, gain, me_dp_ref, me_ctx_ref, *refs):
-    groups = [refs[2 * chosen : 2 * chosen + 2] for chosen in range(sets)][::-1]
+def final_kernel(columns, gain, me_dp_ref, me_ctx_ref, *refs):
+    sets = len(columns)
+    groups = [refs[2 * chosen : 2 * chosen + 2] for chosen in range(sets)]
     top_ref, out_ref, scale_ref, all_tops = refs[2 * sets :]
     n_dp, lanes = scale_ref.shape
-    rows_set, hd = groups[0][0].shape[0] // 2, groups[0][0].shape[1]
-    scale = jnp.maximum(top_ref[...], unpack_top(groups[-1][1], 2 * rows_set)) + 1e-06
+    rows_ctx, hd = groups[0][0].shape
+    scale = jnp.maximum(top_ref[...], unpack_top(groups[0][1], rows_ctx)) + 1e-06
     all_tops[...] = scale
     scale_ref[...] = scale[:n_dp, :lanes]
     factors = gain / all_tops[pl.ds(me_dp_ref[0], 1), :]
     lane = lax.broadcasted_iota(jnp.int32, factors.shape, 1)
-    per_set = rows_set // QROWS
-    first = me_ctx_ref[0] * (sets * per_set)
-    for chosen, (mine_ref, got_ref) in enumerate(groups):
-        for r in range(per_set):
-            mine = jnp.where(lane == first + (chosen * per_set + r), factors, 0.0)
-            factor = jnp.sum(mine, axis=1, keepdims=True)
-            at = chosen * rows_set + r * QROWS
-            for h in range(2):
-                part = slice(h * rows_set + r * QROWS, h * rows_set + (r + 1) * QROWS)
-                total = mine_ref[part, :] + got_ref[part, :].astype(F32)
-                out_ref[at : at + QROWS, h * hd : (h + 1) * hd] = total * factor
-
-
-def local(n_dp, n_ctx, sets, span_order, queries, keys, values, out_grad, activations, error_feedback):
+    blocks = rows_ctx // QROWS
+    for r in range(blocks):
+        mine = jnp.where(lane == me_ctx_ref[0] * blocks + r, factors, 0.0)
+        factor = jnp.sum(mine, axis=1, keepdims=True)
+        part = slice(r * QROWS, (r + 1) * QROWS)
+        for at, (mine_ref, got_ref) in zip(columns, groups):
+            out_ref[part, at : at + hd] = (mine_ref[part, :] + got_ref[part, :].astype(F32)) * factor
+
+
+def local(n_dp, n_ctx, span_order, queries, keys, values, out_grad, activations, error_feedback):
     rows, hd = keys.shape
     width = 2 * hd
     model = activations.shape[1]
-    rows_set = model // (n_dp * n_ctx * sets)
-    tall = n_ctx * rows_set
+    rows_ctx = model // (n_dp * n_ctx)
+    tall = n_ctx * rows_ctx
     me_dp = lax.axis_index("dp").astype(jnp.int32)[None]
     me_ctx = lax.axis_index("context").astype(jnp.int32)[None]
     bits = n_dp.bit_length() - 1
@@ -553,62 +550,61 @@
     def swap_ctx(x, mask):
         return lax.ppermute(x, "context", xor_perm(n_ctx, mask))
 
-    own, parts, key_blocks, score_grads, acts = attention(
+    own, key_parts, value_parts, key_blocks, score_grads, acts = attention(
         me_ctx, span_order[0], queries, out_grad, keys, values, activations, begin(me_dp, me_ctx), swap_ctx, n_ctx
     )
 
     shrink = 1.0 / (n_dp * n_ctx)
-    acts = acts.reshape(n_dp, n_ctx, sets, rows_set, rows)
-    errors = error_feedback.reshape(n_dp, n_ctx, sets, rows_set, width)
+    acts = acts.reshape(n_dp, n_ctx, rows_ctx, rows)
+    errors = error_feedback.reshape(n_dp, n_ctx, rows_ctx, width)
     tops = shape((TOP_ROWS, TOP_LANES), F32)
     steps = n_dp // 2
-    cost = (2 * steps * tall * rows * width, steps * tall * (2 * rows + 6 * width))
-    out, top, key_grad, value_grad, grads = whole_call(
-        functools.partial(first_send_kernel, bits, shrink, len(parts)),
-        "send_tiles",
-        [me_dp],
-        [own, *parts, acts, errors],
-        [shape((steps * tall + 2 * TOP_ROWS, width)), tops, shape((rows, hd)), shape((rows, hd)), shape((rows, width))],
-        18,
-        cost,
-    )
-    got = [swap_dp(out, 1)]
-    *kept, top = whole_call(
-        functools.partial(kept_kernel, bits, shrink),
-        "kept_tiles",
-        [me_dp],
-        [grads, top, acts, errors],
-        [shape((steps, tall, width), F32)] * sets + [tops],
-        20,
-        (sets * cost[0], sets * cost[1]),
-    )
-    for chosen in range(1, sets):
-        extra = TOP_ROWS if chosen == sets - 1 else 0
-        out, top = whole_call(
-            functools.partial(next_send_kernel, bits, shrink, chosen, extra > 0),
-            "send_tiles",
-            [me_dp],
-            [grads, top, acts, errors],
-            [shape((steps * tall + extra, width)), tops],
-            18,
+    cost = (0, 0)
+    kept_shape, grad_shape = shape((steps, tall, hd), F32), shape((rows, hd))
+
+    def tiles(kernel, name, operands, outs, after=()):
+        return whole_call(kernel, name, [me_dp], [*operands, acts, errors], outs, 18, cost, [], after)
+
+    sets = 2
+    half = steps // 2 * (tall // 2)
+
+    def split(last, kept, got, top):
+        return whole_call(
+            functools.partial(split_kernel, bits, n_ctx, int(last)),
+            "split_tiles",
+            [],
+            [kept, got] + [top] * last,
+            [shape((half + (1 if last else 2) * TOP_ROWS, hd))] + [shape((half, hd))] * 3 + [tops] * last,
+            10,
             cost,
         )
-        got.append(swap_dp(out, 1))
-
-    halves = []
-    for chosen in range(sets):
-        half = steps // 2 * tall
-        last = chosen == sets - 1
-        arrays = whole_call(
-            functools.partial(split_kernel, bits, int(last)),
-            "split_tiles",
-            [],
-            [kept[chosen], got[chosen]] + [top] * last,
-            [shape((half + (1 if last else 2) * TOP_ROWS, hd))] + [shape((half, hd))] * 3 + [tops] * last,
-            10,
-            (4 * half * width, 12 * half * width),
-        )
-        halves.append(arrays[:4])
+
+    out, top, grads, value_grad = tiles(
+        functools.partial(first_send_kernel, bits, shrink, hd, len(value_parts)),
+        "send_tiles",
+        [own, *value_parts],
+        [shape((steps * tall + 2 * TOP_ROWS, hd)), tops, grad_shape, grad_shape],
+    )
+    got = swap_dp(out, 1)
+    kept, top = tiles(
+        functools.partial(next_kept_kernel, bits, shrink, hd), "kept_tiles", [grads, top], [kept_shape, tops]
+    )
+    halves = [split(False, kept, got, None)]
+    kept, top, grads, key_grad = tiles(
+        functools.partial(first_kept_kernel, bits, shrink, 0, len(key_parts)),
+        "kept_tiles",
+        [own, *key_parts, top],
+        [kept_shape, tops, grad_shape, grad_shape],
+        halves[0][1:2],
+    )
+    out, top = tiles(
+        functools.partial(next_send_kernel, bits, shrink, 0),
+        "send_tiles",
+        [grads, top],
+        [shape((steps * tall + TOP_ROWS, hd)), tops],
+    )
+    arrays = split(True, kept, swap_dp(out, 1), top)
+    halves.append(arrays[:4])
     gathered = [arrays[4]]
     query_grad, mark = query_gradients(key_blocks, score_grads, queries.shape[1], [arrays[1]])
     groups = []
@@ -623,7 +619,6 @@
             operands = [low, low_got, high, high_got] + (gathered if with_tops else [])
             n_tops = len(operands) - 4
             size = low.shape[0]
-            cost = (4 * size * hd, 12 * size * hd)
             if stage < bits - 1:
                 low_away, low, high_away, high, *top_out = whole_call(
                     functools.partial(add_kernel, n_tops),
@@ -636,7 +631,7 @@
                     after=[mark] if chosen == 0 and stage == 1 else [],
                 )
             else:
-                chunk = 2 * rows_set
+                chunk = rows_ctx
                 away, stay, *top_out = whole_call(
                     functools.partial(last_kernel, n_ctx, n_tops),
                     "last_stage",
@@ -666,11 +661,11 @@
             mask *= 2
         groups = [stay, swap_ctx(away, mask), *groups]
     payload, scale = whole_call(
-        functools.partial(final_kernel, sets, 7.0 / shrink),
+        functools.partial(final_kernel, (0, hd), 7.0 / shrink),
         "final_stage",
         [me_dp, me_ctx],
         groups + gathered,
-        [shape((sets * rows_set, width), F32), shape((n_dp, sets * tall // QROWS), F32)],
+        [shape((rows_ctx, width), F32), shape((n_dp, tall // QROWS), F32)],
         8,
         (0, 0),
         [pltpu.VMEM((TOP_ROWS, TOP_LANES), F32)],
@@ -681,7 +676,7 @@
 def solution(mesh):
     tokens = P(("dp", "context"), None)
     return jax.shard_map(
-        functools.partial(local, mesh.shape["dp"], mesh.shape["context"], 2),
+        functools.partial(local, mesh.shape["dp"], mesh.shape["context"]),
         mesh=mesh,
         in_specs=(P("dp", None), tokens, tokens, tokens, tokens, tokens, P("dp", "context", None, None)),
         out_specs=(tokens, tokens, tokens, tokens, P()),

time: 84.6 us -> 92.3 us (1.091)
  starting transfers between devices: 28.2 us -> 38.1 us
  Pallas kernels: 27.1 us -> 19.9 us
  waiting for transfers between devices: 26.4 us -> 31.2 us
    ppermute x14 -> x16, waiting for transfers between devices: 13.7 us -> 26.1 us  [swap_ctx(): return lax.ppermute(x, 'context', xor_perm(n_ctx, mask))]
    ppermute x10, waiting for transfers between devices: 12.7 us -> 5.16 us  [swap_dp(): return lax.ppermute(x, 'dp', xor_perm(n_dp, mask))]
    pallas_call x24 -> x26, Pallas kernels: 27.1 us -> 19.9 us  [whole_call(): pl.pallas_call(body, grid_spec=pltpu.PrefetchScalarGridSpec(num_scalar_pr...]
    ppermute x10, starting transfers between devices: 6.67 us -> 12.4 us  [swap_dp(): return lax.ppermute(x, 'dp', xor_perm(n_dp, mask))]
    ppermute x14 -> x16, starting transfers between devices: 21.5 us -> 25.7 us  [swap_ctx(): return lax.ppermute(x, 'context', xor_perm(n_ctx, mask))]
  transfers between devices with their start and end apart: 24 -> 26, of which waited for: 8 -> 14; matrix products, arithmetic and copies ran while one was open for 0% -> 0% of each run, Pallas kernels for 29% -> 15%
where the time goes in v12:
time: 92.3 us; the launch traced here: 92.5 us
  starting transfers between devices  38.1 us (41%)
  waiting for transfers between devices  31.2 us (34%)
  Pallas kernels  19.9 us (22%)
  local copies, waits for them, and re-layouts  2.37 us (3%)
    ppermute x16, waiting for transfers between devices, swap_ctx(): return lax.ppermute(x, 'context', xor_perm(n_ctx, mask))  26.1 us
    ppermute x16, starting transfers between devices, swap_ctx(): return lax.ppermute(x, 'context', xor_perm(n_ctx, mask))  25.7 us
    pallas_call x26, Pallas kernels, whole_call(): pl.pallas_call(body, grid_spec=pltpu.PrefetchScalarGridSpec(num_scalar_pr...  19.9 us
    ppermute x10, starting transfers between devices, swap_dp(): return lax.ppermute(x, 'dp', xor_perm(n_dp, mask))  12.4 us
    ppermute x10, waiting for transfers between devices, swap_dp(): return lax.ppermute(x, 'dp', xor_perm(n_dp, mask))  5.16 us
  transfers between devices with their start and end apart: 26, of which 14 were waited for; matrix products, arithmetic and copies ran while one was open for 0% of the time, Pallas kernels for 15%

profile of v12, /device:TPU:0, one launch (start us, length us, event | category | flops | bytes accessed | tf_op | source)
XLA Modules:
  0.0 92.5 jit_solution(8521895789183485170)
XLA Ops:
  0.6 4.1 %collective-permute-start.1 = (bf16[384,128]{1,0:T(8,128)(2,1)}, bf16[384,128]{1,0:T(8,128)(2,1)S(1)}, u32[]{:S(2)}, u32[]{:S(2)}) collective-permute-start(bf16[384,128]{1,0:T(8,128)(2,1)} %refs_4_.1), channel_id=1, source_target_pairs={{0,2},{1,3},{2,0},{3,1},{4,6},{5,7},{6,4},{7,5},{8,10},{9,11},{10,... | collective-permute-start | bytes 294920 | tf_op jit(solution)/shard_map/ppermute | solution.py:551
  4.7 1.6 %collective-permute-start = (bf16[384,128]{1,0:T(8,128)(2,1)}, bf16[384,128]{1,0:T(8,128)(2,1)S(1)}, u32[]{:S(2)}, u32[]{:S(2)}) collective-permute-start(bf16[384,128]{1,0:T(8,128)(2,1)} %refs_4_.1), channel_id=1, source_target_pairs={{0,1},{1,0},{2,3},{3,2},{4,5},{5,4},{6,7},{7,6},{8,9},{9,8},{10,11... | collective-permute-start | bytes 294920 | tf_op jit(solution)/shard_map/ppermute | solution.py:551
  8.2 2.4 %first_stats.1 = (f32[8,3072]{1,0:T(8,128)S(1)}, bf16[384,1024]{1,0:T(8,128)(2,1)S(1)}, bf16[384,1024]{1,0:T(8,128)(2,1)S(1)}, bf16[384,128]{1,0:T(8,128)(2,1)S(...) custom-call(s32[1]{0:T(128)} %bitcast.refs_1_.refs_0_, s32[4]{0:T(128)S(1)} %bitcast.15, ...), custom_call_target="tpu_custom_call" | custom-call | flops 2415919104 | bytes 3145728 | tf_op jit(solution)/shard_map/first_stats/pallas_call | solution.py:39
  11.0 1.7 %prepare.1.refs_8_ = bf16[8192,384]{1,0:T(8,128)(2,1)S(1)} custom-call(bf16[384,8192]{1,0:T(8,128)(2,1)S(1)} %copy-done, f32[8,3072]{1,0:T(8,128)S(1)} %get-tuple-element.70.refs_1_.refs_5_), custom_call_target="tpu_custom_call" | custom-call | tf_op jit(solution)/shard_map/prepare/pallas_call | solution.py:39
  12.7 1.9 %collective-permute-start.2 = (bf16[384,128]{1,0:T(8,128)(2,1)S(1)}, bf16[384,128]{1,0:T(8,128)(2,1)S(1)}, u32[]{:S(2)}, u32[]{:S(2)}) collective-permute-start(bf16[384,128]{1,0:T(8,128)(2,1)S(1)} %collective-permute-done.1.refs_6_.refs_3_.refs_4_.refs_2_), channel_id=1, source_target_pairs={{0,1},{1,0},{2,3},{3,2},{4,5},{5,4},{6,7},{7,6},{8,9},{9,8},{10,11... | collective-permute-start | bytes 294920 | tf_op jit(solution)/shard_map/ppermute | solution.py:551
  14.6 1.1 %collective-permute-start.4 = (bf16[384,128]{1,0:T(8,128)(2,1)S(1)}, bf16[384,128]{1,0:T(8,128)(2,1)S(1)}, u32[]{:S(2)}, u32[]{:S(2)}) collective-permute-start(bf16[384,128]{1,0:T(8,128)(2,1)S(1)} %collective-permute-done.3.refs_7_.refs_4_.refs_5_), channel_id=1, source_target_pairs={{0,1},{1,0},{2,3},{3,2},{4,5},{5,4},{6,7},{7,6},{8,9},{9,8},{10,11... | collective-permute-start | bytes 294920 | tf_op jit(solution)/shard_map/ppermute | solution.py:551
  16.0 1.7 %collective-permute-done.2.refs_3_.refs_4_ = bf16[384,128]{1,0:T(8,128)(2,1)S(1)} collective-permute-done((bf16[384,128]{1,0:T(8,128)(2,1)S(1)}, bf16[384,128]{1,0:T(8,128)(2,1)S(1)}, u32[]{:S(2)}, u32[]{:S(2)}) %collective-permute-start.2) | collective-permute-done | bytes 98336 | tf_op jit(solution)/shard_map/ppermute | solution.py:551
  17.8 1.5 %collective-permute-done.4.refs_4_.refs_5_ = bf16[384,128]{1,0:T(8,128)(2,1)S(1)} collective-permute-done((bf16[384,128]{1,0:T(8,128)(2,1)S(1)}, bf16[384,128]{1,0:T(8,128)(2,1)S(1)}, u32[]{:S(2)}, u32[]{:S(2)}) %collective-permute-start.4) | collective-permute-done | bytes 98336 | tf_op jit(solution)/shard_map/ppermute | solution.py:551
  19.9 1.2 %collective-permute-start.6 = (bf16[400,128]{1,0:T(8,128)(2,1)S(1)}, bf16[400,128]{1,0:T(8,128)(2,1)S(1)}, u32[]{:S(2)}, u32[]{:S(2)}) collective-permute-start(bf16[400,128]{1,0:T(8,128)(2,1)S(1)} %get-tuple-element.72.refs_6_), channel_id=1, source_target_pairs={{0,1},{1,0},{2,3},{3,2},{4,5},{5,4},{6,7},{7,6},{8,9},{9,8},{10,11... | collective-permute-start | bytes 307208 | tf_op jit(solution)/shard_map/ppermute | solution.py:551
  21.4 3.2 %collective-permute-done.6.refs_1_ = bf16[400,128]{1,0:T(8,128)(2,1)S(1)} collective-permute-done((bf16[400,128]{1,0:T(8,128)(2,1)S(1)}, bf16[400,128]{1,0:T(8,128)(2,1)S(1)}, u32[]{:S(2)}, u32[]{:S(2)}) %collective-permute-start.6) | collective-permute-done | bytes 102432 | tf_op jit(solution)/shard_map/ppermute | solution.py:551
  24.6 7.3 %collective-permute-start.10 = (bf16[400,128]{1,0:T(8,128)(2,1)S(1)}, bf16[400,128]{1,0:T(8,128)(2,1)S(1)}, u32[]{:S(2)}, u32[]{:S(2)}) collective-permute-start(bf16[400,128]{1,0:T(8,128)(2,1)S(1)} %merge.2.refs_6_), channel_id=1, source_target_pairs={{0,2},{1,3},{2,0},{3,1},{4,6},{5,7},{6,4},{7,5},{8,10},{9,11},{10,... | collective-permute-start | bytes 307208 | tf_op jit(solution)/shard_map/ppermute | solution.py:551
  32.4 4.0 %collective-permute-start.11 = (bf16[400,128]{1,0:T(8,128)(2,1)S(1)}, bf16[400,128]{1,0:T(8,128)(2,1)S(1)}, u32[]{:S(2)}, u32[]{:S(2)}) collective-permute-start(bf16[400,128]{1,0:T(8,128)(2,1)S(1)} %get-tuple-element.74.refs_5_.refs_2_), channel_id=1, source_target_pairs={{0,1},{1,0},{2,3},{3,2},{4,5},{5,4},{6,7},{7,6},{8,9},{9,8},{10,11... | collective-permute-start | bytes 307208 | tf_op jit(solution)/shard_map/ppermute | solution.py:551
  36.4 2.6 %own_gradients.1 = (f32[384,256]{1,0:T(8,128)S(1)}, bf16[384,3072]{1,0:T(8,128)(2,1)S(1)}) custom-call(f32[8,3072]{1,0:T(8,128)S(1)} %next_stats.5.refs_1_.refs_0_, bf16[384,1024]{1,0:T(8,128)(2,1)S(1)} %get-tuple-element.68.refs_1_.refs_2_, bf16[384,1024]{1,0:T(8,128)(2,1)S(1)} %get-tuple-element.69.refs_2_.refs_3_, ...), custom_call_target="tpu_custom_call" | custom-call | tf_op jit(solution)/shard_map/own_gradients/pallas_call | solution.py:39
  39.1 1.5 %send_tiles.2 = (bf16[4128,128]{1,0:T(8,128)(2,1)S(1)}, f32[16,128]{1,0:T(8,128)S(1)}, bf16[384,128]{1,0:T(8,128)(2,1)S(1)}, bf16[384,128]{1,0:T(8,128)(2,1)}) custom-call(s32[1]{0:T(128)} %bitcast.2.refs_0_, f32[384,256]{1,0:T(8,128)S(1)} %get-tuple-element.79.refs_1_, bf16[400,128]{1,0:T(8,128)(2,1)S(1)} %collective-permute-done.10.refs_2_, ...), custom_call_target="tpu_custom_call" | custom-call | tf_op jit(solution)/shard_map/send_tiles/pallas_call | solution.py:39
  40.6 2.0 %collective-permute-start.7 = (bf16[384,128]{1,0:T(8,128)(2,1)S(1)}, bf16[384,128]{1,0:T(8,128)(2,1)S(1)}, u32[]{:S(2)}, u32[]{:S(2)}) collective-permute-start(bf16[384,128]{1,0:T(8,128)(2,1)S(1)} %get-tuple-element.81), channel_id=1, source_target_pairs={{0,1},{1,0},{2,3},{3,2},{4,5},{5,4},{6,7},{7,6},{8,9},{9,8},{10,11... | collective-permute-start | bytes 294920 | tf_op jit(solution)/shard_map/ppermute | solution.py:551
  42.7 3.6 %collective-permute-done.7.refs_1_ = bf16[384,128]{1,0:T(8,128)(2,1)S(1)} collective-permute-done((bf16[384,128]{1,0:T(8,128)(2,1)S(1)}, bf16[384,128]{1,0:T(8,128)(2,1)S(1)}, u32[]{:S(2)}, u32[]{:S(2)}) %collective-permute-start.7) | collective-permute-done | bytes 98336 | tf_op jit(solution)/shard_map/ppermute | solution.py:551
  48.2 5.6 %collective-permute-done.8.refs_2_ = bf16[384,128]{1,0:T(8,128)(2,1)S(1)} collective-permute-done((bf16[384,128]{1,0:T(8,128)(2,1)S(1)}, bf16[384,128]{1,0:T(8,128)(2,1)S(1)}, u32[]{:S(2)}, u32[]{:S(2)}) %collective-permute-start.8) | collective-permute-done | bytes 98336 | tf_op jit(solution)/shard_map/ppermute | solution.py:551
  53.7 1.6 %kept_tiles.3 = (f32[4,1024,128]{2,1,0:T(8,128)S(1)}, f32[16,128]{1,0:T(8,128)S(1)}, bf16[384,128]{1,0:T(8,128)(2,1)S(1)}, bf16[384,128]{1,0:T(8,128)(2,1)}) custom-call(s32[1]{0:T(128)} %bitcast.2.refs_0_, f32[384,256]{1,0:T(8,128)S(1)} %get-tuple-element.79.refs_1_, bf16[384,128]{1,0:T(8,128)(2,1)S(1)} %collective-permute-done.8.refs_2_, ...), custom_call_target="tpu_custom_call" | custom-call | tf_op jit(solution)/shard_map/kept_tiles/pallas_call | solution.py:39
  55.3 1.2 %send_tiles.3 = (bf16[4112,128]{1,0:T(8,128)(2,1)S(1)}, f32[16,128]{1,0:T(8,128)S(1)}) custom-call(s32[1]{0:T(128)} %bitcast.2.refs_0_, bf16[384,128]{1,0:T(8,128)(2,1)S(1)} %get-tuple-element.90.refs_1_, f32[16,128]{1,0:T(8,128)S(1)} %get-tuple-element.91.refs_2_, bf16[8,4,256,384]{3,2,1,0:T(8,128)(2,1)S(1)} %bitcast.8, f32[8,4,256,256]{3,2,1,0:T(8,128)S(1)} %bitcast.14), custom_call_target="tpu_custom_call" | custom-call | tf_op jit(solution)/shard_map/send_tiles/pallas_call | solution.py:39
  56.8 2.0 %collective-permute-start.21 = (bf16[1024,128]{1,0:T(8,128)(2,1)S(1)}, bf16[1024,128]{1,0:T(8,128)(2,1)S(1)}, u32[]{:S(2)}, u32[]{:S(2)}) collective-permute-start(bf16[1024,128]{1,0:T(8,128)(2,1)S(1)} %get-tuple-element.114), channel_id=1, source_target_pairs={{0,16},{4,20},{8,24},{12,28},{16,0},{20,4},{24,8},{28,12},{1,17},{... | collective-permute-start | bytes 786440 | tf_op jit(solution)/shard_map/ppermute | solution.py:548
  59.6 1.6 %collective-permute-start.14 = (bf16[1040,128]{1,0:T(8,128)(2,1)S(1)}, bf16[1040,128]{1,0:T(8,128)(2,1)S(1)}, u32[]{:S(2)}, u32[]{:S(2)}) collective-permute-start(bf16[1040,128]{1,0:T(8,128)(2,1)S(1)} %get-tuple-element.98), channel_id=1, source_target_pairs={{0,8},{4,12},{8,0},{12,4},{16,24},{20,28},{24,16},{28,20},{1,9},{5... | collective-permute-start | bytes 798728 | tf_op jit(solution)/shard_map/ppermute | solution.py:548
  61.8 3.8 %query_gradients.1 = (bf16[384,1024]{1,0:T(8,128)(2,1)}, f32[8,128]{1,0:T(8,128)S(1)}) custom-call(bf16[384,128]{1,0:T(8,128)(2,1)S(1)} %get-tuple-element.66.refs_3_.refs_0_, bf16[384,128]{1,0:T(8,128)(2,1)S(1)} %collective-permute-done.refs_3_.refs_4_.refs_1_, bf16[384,128]{1,0:T(8,128)(2,1)S(1)} %collective-permute-done.1.refs_6_.refs_3_.refs_4_.refs_2_, ...), custom_call_target="tpu_custom_call" | custom-call | flops 1207959552 | bytes 6291456 | tf_op jit(solution)/shard_map/query_gradients/pallas_call | solution.py:39
  66.0 2.1 %collective-permute-start.22 = (bf16[544,128]{1,0:T(8,128)(2,1)S(1)}, bf16[544,128]{1,0:T(8,128)(2,1)S(1)}, u32[]{:S(2)}, u32[]{:S(2)}) collective-permute-start(bf16[544,128]{1,0:T(8,128)(2,1)S(1)} %get-tuple-element.117), channel_id=1, source_target_pairs={{0,16},{4,20},{8,24},{12,28},{16,0},{20,4},{24,8},{28,12},{1,17},{... | collective-permute-start | bytes 417800 | tf_op jit(solution)/shard_map/ppermute | solution.py:548
  68.1 1.9 %collective-permute-start.23 = (bf16[512,128]{1,0:T(8,128)(2,1)S(1)}, bf16[512,128]{1,0:T(8,128)(2,1)S(1)}, u32[]{:S(2)}, u32[]{:S(2)}) collective-permute-start(bf16[512,128]{1,0:T(8,128)(2,1)S(1)} %get-tuple-element.119), channel_id=1, source_target_pairs={{0,8},{4,12},{8,0},{12,4},{16,24},{20,28},{24,16},{28,20},{1,9},{5... | collective-permute-start | bytes 393224 | tf_op jit(solution)/shard_map/ppermute | solution.py:548
  70.0 1.4 %collective-permute-done.15.refs_3_ = bf16[1024,128]{1,0:T(8,128)(2,1)S(1)} collective-permute-done((bf16[1024,128]{1,0:T(8,128)(2,1)S(1)}, bf16[1024,128]{1,0:T(8,128)(2,1)S(1)}, u32[]{:S(2)}, u32[]{:S(2)}) %collective-permute-start.15) | collective-permute-done | bytes 262176 | tf_op jit(solution)/shard_map/ppermute | solution.py:548
  71.8 2.1 %collective-permute-start.16 = (bf16[528,128]{1,0:T(8,128)(2,1)S(1)}, bf16[528,128]{1,0:T(8,128)(2,1)S(1)}, u32[]{:S(2)}, u32[]{:S(2)}) collective-permute-start(bf16[528,128]{1,0:T(8,128)(2,1)S(1)} %get-tuple-element.103), channel_id=1, source_target_pairs={{0,16},{4,20},{8,24},{12,28},{16,0},{20,4},{24,8},{28,12},{1,17},{... | collective-permute-start | bytes 405512 | tf_op jit(solution)/shard_map/ppermute | solution.py:548
  74.0 1.8 %collective-permute-start.17 = (bf16[512,128]{1,0:T(8,128)(2,1)S(1)}, bf16[512,128]{1,0:T(8,128)(2,1)S(1)}, u32[]{:S(2)}, u32[]{:S(2)}) collective-permute-start(bf16[512,128]{1,0:T(8,128)(2,1)S(1)} %get-tuple-element.105), channel_id=1, source_target_pairs={{0,8},{4,12},{8,0},{12,4},{16,24},{20,28},{24,16},{28,20},{1,9},{5... | collective-permute-start | bytes 393224 | tf_op jit(solution)/shard_map/ppermute | solution.py:548
  76.1 2.8 %collective-permute-done.17.refs_4_ = bf16[512,128]{1,0:T(8,128)(2,1)S(1)} collective-permute-done((bf16[512,128]{1,0:T(8,128)(2,1)S(1)}, bf16[512,128]{1,0:T(8,128)(2,1)S(1)}, u32[]{:S(2)}, u32[]{:S(2)}) %collective-permute-start.17) | collective-permute-done | bytes 131104 | tf_op jit(solution)/shard_map/ppermute | solution.py:548
  79.3 3.2 %collective-permute-done.24.refs_1_ = bf16[544,128]{1,0:T(8,128)(2,1)S(1)} collective-permute-done((bf16[544,128]{1,0:T(8,128)(2,1)S(1)}, bf16[544,128]{1,0:T(8,128)(2,1)S(1)}, u32[]{:S(2)}, u32[]{:S(2)}) %collective-permute-start.24) | collective-permute-done | bytes 139296 | tf_op jit(solution)/shard_map/ppermute | solution.py:551
  82.7 2.0 %collective-permute-done.18.refs_1_ = bf16[528,128]{1,0:T(8,128)(2,1)S(1)} collective-permute-done((bf16[528,128]{1,0:T(8,128)(2,1)S(1)}, bf16[528,128]{1,0:T(8,128)(2,1)S(1)}, u32[]{:S(2)}, u32[]{:S(2)}) %collective-permute-start.18) | collective-permute-done | bytes 135200 | tf_op jit(solution)/shard_map/ppermute | solution.py:551
  85.8 3.7 %collective-permute-done.25.refs_5_ = bf16[288,128]{1,0:T(8,128)(2,1)S(1)} collective-permute-done((bf16[288,128]{1,0:T(8,128)(2,1)S(1)}, bf16[288,128]{1,0:T(8,128)(2,1)S(1)}, u32[]{:S(2)}, u32[]{:S(2)}) %collective-permute-start.25) | collective-permute-done | bytes 73760 | tf_op jit(solution)/shard_map/ppermute | solution.py:551
  89.5 1.5 %collective-permute-done.19.refs_3_ = bf16[272,128]{1,0:T(8,128)(2,1)S(1)} collective-permute-done((bf16[272,128]{1,0:T(8,128)(2,1)S(1)}, bf16[272,128]{1,0:T(8,128)(2,1)S(1)}, u32[]{:S(2)}, u32[]{:S(2)}) %collective-permute-start.19) | collective-permute-done | bytes 69664 | tf_op jit(solution)/shard_map/ppermute | solution.py:551
  (64 shorter events, 11.9 us)
Async XLA Ops:
  0.6 12.1 %collective-permute-start.1 = (bf16[384,128]{1,0:T(8,128)(2,1)}, bf16[384,128]{1,0:T(8,128)(2,1)S(1)}, u32[]{:S(2)}, u32[]{:S(2)}) collective-permute-start(bf16[384,128]{1,0:T(8,128)(2,1)} %refs_4_.1), channel_id=1, source_target_pairs={{0,2},{1,3},{2,0},{3,1},{4,6},{5,7},{6,4},{7,5},{8,10},{9,11},{10,... | collective-permute-start | bytes 294920 | tf_op jit(solution)/shard_map/ppermute | solution.py:551
  4.7 11.0 %collective-permute-start = (bf16[384,128]{1,0:T(8,128)(2,1)}, bf16[384,128]{1,0:T(8,128)(2,1)S(1)}, u32[]{:S(2)}, u32[]{:S(2)}) collective-permute-start(bf16[384,128]{1,0:T(8,128)(2,1)} %refs_4_.1), channel_id=1, source_target_pairs={{0,1},{1,0},{2,3},{3,2},{4,5},{5,4},{6,7},{7,6},{8,9},{9,8},{10,11... | collective-permute-start | bytes 294920 | tf_op jit(solution)/shard_map/ppermute | solution.py:551
  6.3 9.4 %collective-permute-start.5 = (bf16[384,128]{1,0:T(8,128)(2,1)}, bf16[384,128]{1,0:T(8,128)(2,1)S(1)}, u32[]{:S(2)}, u32[]{:S(2)}) collective-permute-start(bf16[384,128]{1,0:T(8,128)(2,1)} %refs_5_.1), channel_id=1, source_target_pairs={{0,1},{1,0},{2,3},{3,2},{4,5},{5,4},{6,7},{7,6},{8,9},{9,8},{10,11... | collective-permute-start | bytes 294920 | tf_op jit(solution)/shard_map/ppermute | solution.py:551
  6.8 7.8 %collective-permute-start.3 = (bf16[384,128]{1,0:T(8,128)(2,1)}, bf16[384,128]{1,0:T(8,128)(2,1)S(1)}, u32[]{:S(2)}, u32[]{:S(2)}) collective-permute-start(bf16[384,128]{1,0:T(8,128)(2,1)} %refs_5_.1), channel_id=1, source_target_pairs={{0,2},{1,3},{2,0},{3,1},{4,6},{5,7},{6,4},{7,5},{8,10},{9,11},{10,... | collective-permute-start | bytes 294920 | tf_op jit(solution)/shard_map/ppermute | solution.py:551
  6.8 1.4 %copy-start.3 = (bf16[384,128]{1,0:T(8,128)(2,1)S(1)}, bf16[384,128]{1,0:T(8,128)(2,1)}, u32[]{:S(2)}) copy-start(bf16[384,128]{1,0:T(8,128)(2,1)} %refs_4_.1) | copy-start | bytes 294916
  6.8 1.4 %copy-start.4 = (bf16[384,128]{1,0:T(8,128)(2,1)S(1)}, bf16[384,128]{1,0:T(8,128)(2,1)}, u32[]{:S(2)}) copy-start(bf16[384,128]{1,0:T(8,128)(2,1)} %refs_5_.1) | copy-start | bytes 294916
  6.9 1.4 %copy-start.5 = (s32[1,4]{1,0:T(1,128)S(1)}, s32[1,4]{1,0:T(1,128)}, u32[]{:S(2)}) copy-start(s32[1,4]{1,0:T(1,128)} %param.7) | copy-start | bytes 52
  8.2 2.8 %copy-start = (bf16[384,8192]{1,0:T(8,128)(2,1)S(1)}, bf16[384,8192]{1,0:T(8,128)(2,1)}, u32[]{:S(2)}) copy-start(bf16[384,8192]{1,0:T(8,128)(2,1)} %refs_0_.1) | copy-start | bytes 18874372
  12.7 5.1 %collective-permute-start.2 = (bf16[384,128]{1,0:T(8,128)(2,1)S(1)}, bf16[384,128]{1,0:T(8,128)(2,1)S(1)}, u32[]{:S(2)}, u32[]{:S(2)}) collective-permute-start(bf16[384,128]{1,0:T(8,128)(2,1)S(1)} %collective-permute-done.1.refs_6_.refs_3_.refs_4_.refs_2_), channel_id=1, source_target_pairs={{0,1},{1,0},{2,3},{3,2},{4,5},{5,4},{6,7},{7,6},{8,9},{9,8},{10,11... | collective-permute-start | bytes 294920 | tf_op jit(solution)/shard_map/ppermute | solution.py:551
  14.6 4.6 %collective-permute-start.4 = (bf16[384,128]{1,0:T(8,128)(2,1)S(1)}, bf16[384,128]{1,0:T(8,128)(2,1)S(1)}, u32[]{:S(2)}, u32[]{:S(2)}) collective-permute-start(bf16[384,128]{1,0:T(8,128)(2,1)S(1)} %collective-permute-done.3.refs_7_.refs_4_.refs_5_), channel_id=1, source_target_pairs={{0,1},{1,0},{2,3},{3,2},{4,5},{5,4},{6,7},{7,6},{8,9},{9,8},{10,11... | collective-permute-start | bytes 294920 | tf_op jit(solution)/shard_map/ppermute | solution.py:551
  15.9 23.2 %slice-start = ((s8[8388608]{0:T(1024)(128)(4,1)}), s8[4194304]{0:T(1024)(128)(4,1)S(1)}, s32[]{:S(2)}) async-start(s8[8388608]{0:T(1024)(128)(4,1)} %bitcast.9), calls=%async_computation | async-start | bytes 8388608
  16.0 23.1 %slice-start.1 = ((s8[8388608]{0:T(1024)(128)(4,1)}), s8[4194304]{0:T(1024)(128)(4,1)S(1)}, s32[]{:S(2)}) async-start(s8[8388608]{0:T(1024)(128)(4,1)} %bitcast.9), calls=%async_computation.1 | async-start | bytes 8388608
  19.9 4.7 %collective-permute-start.6 = (bf16[400,128]{1,0:T(8,128)(2,1)S(1)}, bf16[400,128]{1,0:T(8,128)(2,1)S(1)}, u32[]{:S(2)}, u32[]{:S(2)}) collective-permute-start(bf16[400,128]{1,0:T(8,128)(2,1)S(1)} %get-tuple-element.72.refs_6_), channel_id=1, source_target_pairs={{0,1},{1,0},{2,3},{3,2},{4,5},{5,4},{6,7},{7,6},{8,9},{9,8},{10,11... | collective-permute-start | bytes 307208 | tf_op jit(solution)/shard_map/ppermute | solution.py:551
  24.6 14.5 %collective-permute-start.10 = (bf16[400,128]{1,0:T(8,128)(2,1)S(1)}, bf16[400,128]{1,0:T(8,128)(2,1)S(1)}, u32[]{:S(2)}, u32[]{:S(2)}) collective-permute-start(bf16[400,128]{1,0:T(8,128)(2,1)S(1)} %merge.2.refs_6_), channel_id=1, source_target_pairs={{0,2},{1,3},{2,0},{3,1},{4,6},{5,7},{6,4},{7,5},{8,10},{9,11},{10,... | collective-permute-start | bytes 307208 | tf_op jit(solution)/shard_map/ppermute | solution.py:551
  32.4 6.7 %collective-permute-start.11 = (bf16[400,128]{1,0:T(8,128)(2,1)S(1)}, bf16[400,128]{1,0:T(8,128)(2,1)S(1)}, u32[]{:S(2)}, u32[]{:S(2)}) collective-permute-start(bf16[400,128]{1,0:T(8,128)(2,1)S(1)} %get-tuple-element.74.refs_5_.refs_2_), channel_id=1, source_target_pairs={{0,1},{1,0},{2,3},{3,2},{4,5},{5,4},{6,7},{7,6},{8,9},{9,8},{10,11... | collective-permute-start | bytes 307208 | tf_op jit(solution)/shard_map/ppermute | solution.py:551
  40.6 7.3 %collective-permute-start.12 = (bf16[4128,128]{1,0:T(8,128)(2,1)S(1)}, bf16[4128,128]{1,0:T(8,128)(2,1)S(1)}, u32[]{:S(2)}, u32[]{:S(2)}) collective-permute-start(bf16[4128,128]{1,0:T(8,128)(2,1)S(1)} %get-tuple-element.87), channel_id=1, source_target_pairs={{0,4},{4,0},{8,12},{12,8},{16,20},{20,16},{24,28},{28,24},{1,5},{5... | collective-permute-start | bytes 3170312 | tf_op jit(solution)/shard_map/ppermute | solution.py:548
  40.6 5.7 %collective-permute-start.7 = (bf16[384,128]{1,0:T(8,128)(2,1)S(1)}, bf16[384,128]{1,0:T(8,128)(2,1)S(1)}, u32[]{:S(2)}, u32[]{:S(2)}) collective-permute-start(bf16[384,128]{1,0:T(8,128)(2,1)S(1)} %get-tuple-element.81), channel_id=1, source_target_pairs={{0,1},{1,0},{2,3},{3,2},{4,5},{5,4},{6,7},{7,6},{8,9},{9,8},{10,11... | collective-permute-start | bytes 294920 | tf_op jit(solution)/shard_map/ppermute | solution.py:551
  42.6 5.6 %collective-permute-start.9 = (bf16[384,128]{1,0:T(8,128)(2,1)S(1)}, bf16[384,128]{1,0:T(8,128)(2,1)S(1)}, u32[]{:S(2)}, u32[]{:S(2)}) collective-permute-start(bf16[384,128]{1,0:T(8,128)(2,1)S(1)} %get-tuple-element.82), channel_id=1, source_target_pairs={{0,1},{1,0},{2,3},{3,2},{4,5},{5,4},{6,7},{7,6},{8,9},{9,8},{10,11... | collective-permute-start | bytes 294920 | tf_op jit(solution)/shard_map/ppermute | solution.py:551
  46.3 7.4 %collective-permute-start.8 = (bf16[384,128]{1,0:T(8,128)(2,1)S(1)}, bf16[384,128]{1,0:T(8,128)(2,1)S(1)}, u32[]{:S(2)}, u32[]{:S(2)}) collective-permute-start(bf16[384,128]{1,0:T(8,128)(2,1)S(1)} %merge.3), channel_id=1, source_target_pairs={{0,2},{1,3},{2,0},{3,1},{4,6},{5,7},{6,4},{7,5},{8,10},{9,11},{10,... | collective-permute-start | bytes 294920 | tf_op jit(solution)/shard_map/ppermute | solution.py:551
  56.5 2.7 %collective-permute-start.13 = (bf16[4112,128]{1,0:T(8,128)(2,1)S(1)}, bf16[4112,128]{1,0:T(8,128)(2,1)S(1)}, u32[]{:S(2)}, u32[]{:S(2)}) collective-permute-start(bf16[4112,128]{1,0:T(8,128)(2,1)S(1)} %get-tuple-element.92), channel_id=1, source_target_pairs={{0,4},{4,0},{8,12},{12,8},{16,20},{20,16},{24,28},{28,24},{1,5},{5... | collective-permute-start | bytes 3158024 | tf_op jit(solution)/shard_map/ppermute | solution.py:548
  56.5 9.4 %collective-permute-start.20 = (bf16[1056,128]{1,0:T(8,128)(2,1)S(1)}, bf16[1056,128]{1,0:T(8,128)(2,1)S(1)}, u32[]{:S(2)}, u32[]{:S(2)}) collective-permute-start(bf16[1056,128]{1,0:T(8,128)(2,1)S(1)} %get-tuple-element.112), channel_id=1, source_target_pairs={{0,8},{4,12},{8,0},{12,4},{16,24},{20,28},{24,16},{28,20},{1,9},{5... | collective-permute-start | bytes 811016 | tf_op jit(solution)/shard_map/ppermute | solution.py:548
  56.8 9.1 %collective-permute-start.21 = (bf16[1024,128]{1,0:T(8,128)(2,1)S(1)}, bf16[1024,128]{1,0:T(8,128)(2,1)S(1)}, u32[]{:S(2)}, u32[]{:S(2)}) collective-permute-start(bf16[1024,128]{1,0:T(8,128)(2,1)S(1)} %get-tuple-element.114), channel_id=1, source_target_pairs={{0,16},{4,20},{8,24},{12,28},{16,0},{20,4},{24,8},{28,12},{1,17},{... | collective-permute-start | bytes 786440 | tf_op jit(solution)/shard_map/ppermute | solution.py:548
  59.6 12.0 %collective-permute-start.14 = (bf16[1040,128]{1,0:T(8,128)(2,1)S(1)}, bf16[1040,128]{1,0:T(8,128)(2,1)S(1)}, u32[]{:S(2)}, u32[]{:S(2)}) collective-permute-start(bf16[1040,128]{1,0:T(8,128)(2,1)S(1)} %get-tuple-element.98), channel_id=1, source_target_pairs={{0,8},{4,12},{8,0},{12,4},{16,24},{20,28},{24,16},{28,20},{1,9},{5... | collective-permute-start | bytes 798728 | tf_op jit(solution)/shard_map/ppermute | solution.py:548
  61.2 10.3 %collective-permute-start.15 = (bf16[1024,128]{1,0:T(8,128)(2,1)S(1)}, bf16[1024,128]{1,0:T(8,128)(2,1)S(1)}, u32[]{:S(2)}, u32[]{:S(2)}) collective-permute-start(bf16[1024,128]{1,0:T(8,128)(2,1)S(1)} %get-tuple-element.100), channel_id=1, source_target_pairs={{0,16},{4,20},{8,24},{12,28},{16,0},{20,4},{24,8},{28,12},{1,17},{... | collective-permute-start | bytes 786440 | tf_op jit(solution)/shard_map/ppermute | solution.py:548
  66.0 9.8 %collective-permute-start.22 = (bf16[544,128]{1,0:T(8,128)(2,1)S(1)}, bf16[544,128]{1,0:T(8,128)(2,1)S(1)}, u32[]{:S(2)}, u32[]{:S(2)}) collective-permute-start(bf16[544,128]{1,0:T(8,128)(2,1)S(1)} %get-tuple-element.117), channel_id=1, source_target_pairs={{0,16},{4,20},{8,24},{12,28},{16,0},{20,4},{24,8},{28,12},{1,17},{... | collective-permute-start | bytes 417800 | tf_op jit(solution)/shard_map/ppermute | solution.py:548
  68.1 7.6 %collective-permute-start.23 = (bf16[512,128]{1,0:T(8,128)(2,1)S(1)}, bf16[512,128]{1,0:T(8,128)(2,1)S(1)}, u32[]{:S(2)}, u32[]{:S(2)}) collective-permute-start(bf16[512,128]{1,0:T(8,128)(2,1)S(1)} %get-tuple-element.119), channel_id=1, source_target_pairs={{0,8},{4,12},{8,0},{12,4},{16,24},{20,28},{24,16},{28,20},{1,9},{5... | collective-permute-start | bytes 393224 | tf_op jit(solution)/shard_map/ppermute | solution.py:548
  71.8 7.1 %collective-permute-start.16 = (bf16[528,128]{1,0:T(8,128)(2,1)S(1)}, bf16[528,128]{1,0:T(8,128)(2,1)S(1)}, u32[]{:S(2)}, u32[]{:S(2)}) collective-permute-start(bf16[528,128]{1,0:T(8,128)(2,1)S(1)} %get-tuple-element.103), channel_id=1, source_target_pairs={{0,16},{4,20},{8,24},{12,28},{16,0},{20,4},{24,8},{28,12},{1,17},{... | collective-permute-start | bytes 405512 | tf_op jit(solution)/shard_map/ppermute | solution.py:548
  74.0 5.0 %collective-permute-start.17 = (bf16[512,128]{1,0:T(8,128)(2,1)S(1)}, bf16[512,128]{1,0:T(8,128)(2,1)S(1)}, u32[]{:S(2)}, u32[]{:S(2)}) collective-permute-start(bf16[512,128]{1,0:T(8,128)(2,1)S(1)} %get-tuple-element.105), channel_id=1, source_target_pairs={{0,8},{4,12},{8,0},{12,4},{16,24},{20,28},{24,16},{28,20},{1,9},{5... | collective-permute-start | bytes 393224 | tf_op jit(solution)/shard_map/ppermute | solution.py:548
  75.9 6.7 %collective-permute-start.24 = (bf16[544,128]{1,0:T(8,128)(2,1)S(1)}, bf16[544,128]{1,0:T(8,128)(2,1)S(1)}, u32[]{:S(2)}, u32[]{:S(2)}) collective-permute-start(bf16[544,128]{1,0:T(8,128)(2,1)S(1)} %get-tuple-element.121), channel_id=1, source_target_pairs={{0,1},{1,0},{2,3},{3,2},{4,5},{5,4},{6,7},{7,6},{8,9},{9,8},{10,11... | collective-permute-start | bytes 417800 | tf_op jit(solution)/shard_map/ppermute | solution.py:551
  79.1 5.6 %collective-permute-start.18 = (bf16[528,128]{1,0:T(8,128)(2,1)S(1)}, bf16[528,128]{1,0:T(8,128)(2,1)S(1)}, u32[]{:S(2)}, u32[]{:S(2)}) collective-permute-start(bf16[528,128]{1,0:T(8,128)(2,1)S(1)} %get-tuple-element.108), channel_id=1, source_target_pairs={{0,1},{1,0},{2,3},{3,2},{4,5},{5,4},{6,7},{7,6},{8,9},{9,8},{10,11... | collective-permute-start | bytes 405512 | tf_op jit(solution)/shard_map/ppermute | solution.py:551
  82.6 6.9 %collective-permute-start.25 = (bf16[288,128]{1,0:T(8,128)(2,1)S(1)}, bf16[288,128]{1,0:T(8,128)(2,1)S(1)}, u32[]{:S(2)}, u32[]{:S(2)}) collective-permute-start(bf16[288,128]{1,0:T(8,128)(2,1)S(1)} %get-tuple-element.123), channel_id=1, source_target_pairs={{0,2},{1,3},{2,0},{3,1},{4,6},{5,7},{6,4},{7,5},{8,10},{9,11},{10,... | collective-permute-start | bytes 221192 | tf_op jit(solution)/shard_map/ppermute | solution.py:551
  84.8 6.1 %collective-permute-start.19 = (bf16[272,128]{1,0:T(8,128)(2,1)S(1)}, bf16[272,128]{1,0:T(8,128)(2,1)S(1)}, u32[]{:S(2)}, u32[]{:S(2)}) collective-permute-start(bf16[272,128]{1,0:T(8,128)(2,1)S(1)} %get-tuple-element.111), channel_id=1, source_target_pairs={{0,2},{1,3},{2,0},{3,1},{4,6},{5,7},{6,4},{7,5},{8,10},{9,11},{10,... | collective-permute-start | bytes 208904 | tf_op jit(solution)/shard_map/ppermute | solution.py:551
  (2 other events, 2.5 us)

commit v13 on v12

--- a/solution.py
+++ b/solution.py
@@ -276,7 +276,7 @@
     p_buf = pltpu.VMEM((rows, 2 * rows), BF16)
     sums = [pltpu.VMEM((rows, hd), F32)] * 2
     key_parts, value_parts = [[] for _ in range(n)], [[] for _ in range(n)]
-    score_grads, own_parts, before = [None] * n, {}, []
+    score_grads, before = [None] * n, []
     for b in range(n - 1, 0, -1):
         dk, dv, score_grads[b] = whole_call(
             functools.partial(other_kernel, b),
@@ -289,16 +289,13 @@
             [p_buf, *sums],
             before,
         )
-        own_parts[b] = dk
         if value_parts[b]:
             dv = merge(rows, [dv, *value_parts[b]], [])
         value_parts[b & (b - 1)].append(swap(dv, b & -b))
-        before = [dv]
-    for b in range(n - 1, 0, -1):
-        dk = own_parts[b]
         if key_parts[b]:
-            dk = merge(rows, [dk, *key_parts[b]], before)
+            dk = merge(rows, [dk, *key_parts[b]], [dv])
         key_parts[b & (b - 1)].append(swap(dk, b & -b))
+        before = [dv, dk]
     own, score_grads[0] = whole_call(
         own_kernel,
         "own_gradients",
@@ -595,7 +592,6 @@
         "kept_tiles",
         [own, *key_parts, top],
         [kept_shape, tops, grad_shape, grad_shape],
-        halves[0][1:2],
     )
     out, top = tiles(
         functools.partial(next_send_kernel, bits, shrink, 0),

time: 92.3 us -> 83.2 us (0.901)
  waiting for transfers between devices: 31.2 us -> 20 us
  starting transfers between devices: 38.1 us -> 40.2 us
    ppermute x16, waiting for transfers between devices: 26.1 us -> 13.8 us  [swap_ctx(): return lax.ppermute(x, 'context', xor_perm(n_ctx, mask))]
    ppermute x16, starting transfers between devices: 25.7 us -> 28 us  [swap_ctx(): return lax.ppermute(x, 'context', xor_perm(n_ctx, mask))]
    ppermute x10, waiting for transfers between devices: 5.16 us -> 6.16 us  [swap_dp(): return lax.ppermute(x, 'dp', xor_perm(n_dp, mask))]
  transfers between devices with their start and end apart: 26 -> 26, of which waited for: 14 -> 10; matrix products, arithmetic and copies ran while one was open for 0% -> 0% of each run, Pallas kernels for 15% -> 22%
where the time goes in v13:
time: 83.2 us
  starting transfers between devices  40.2 us (48%)
  waiting for transfers between devices  20 us (24%)
  Pallas kernels  19.9 us (24%)
  local copies, waits for them, and re-layouts  2.38 us (3%)
    ppermute x16, starting transfers between devices, swap_ctx(): return lax.ppermute(x, 'context', xor_perm(n_ctx, mask))  28 us
    pallas_call x26, Pallas kernels, whole_call(): pl.pallas_call(body, grid_spec=pltpu.PrefetchScalarGridSpec(num_scalar_pr...  19.9 us
    ppermute x16, waiting for transfers between devices, swap_ctx(): return lax.ppermute(x, 'context', xor_perm(n_ctx, mask))  13.8 us
    ppermute x10, starting transfers between devices, swap_dp(): return lax.ppermute(x, 'dp', xor_perm(n_dp, mask))  12.1 us
    ppermute x10, waiting for transfers between devices, swap_dp(): return lax.ppermute(x, 'dp', xor_perm(n_dp, mask))  6.16 us
    unnamed x16, local copies, waits for them, and re-layouts  1.74 us
  transfers between devices with their start and end apart: 26, of which 10 were waited for; matrix products, arithmetic and copies ran while one was open for 0% of the time, Pallas kernels for 22%

profile of v13, /device:TPU:0, one launch (start us, length us, event | category | flops | bytes accessed | tf_op | source)
XLA Modules:
  0.0 83.2 jit_solution(10951652548650580398)
XLA Ops:
  0.6 4.1 %collective-permute-start.1 = (bf16[384,128]{1,0:T(8,128)(2,1)}, bf16[384,128]{1,0:T(8,128)(2,1)S(1)}, u32[]{:S(2)}, u32[]{:S(2)}) collective-permute-start(bf16[384,128]{1,0:T(8,128)(2,1)} %refs_4_.1), channel_id=1, source_target_pairs={{0,2},{1,3},{2,0},{3,1},{4,6},{5,7},{6,4},{7,5},{8,10},{9,11},{10,... | collective-permute-start | bytes 294920 | tf_op jit(solution)/shard_map/ppermute | solution.py:548
  4.7 1.6 %collective-permute-start = (bf16[384,128]{1,0:T(8,128)(2,1)}, bf16[384,128]{1,0:T(8,128)(2,1)S(1)}, u32[]{:S(2)}, u32[]{:S(2)}) collective-permute-start(bf16[384,128]{1,0:T(8,128)(2,1)} %refs_4_.1), channel_id=1, source_target_pairs={{0,1},{1,0},{2,3},{3,2},{4,5},{5,4},{6,7},{7,6},{8,9},{9,8},{10,11... | collective-permute-start | bytes 294920 | tf_op jit(solution)/shard_map/ppermute | solution.py:548
  6.9 1.1 %copy-done.1 = bf16[384,1024]{1,0:T(8,128)(2,1)S(1)} copy-done((bf16[384,1024]{1,0:T(8,128)(2,1)S(1)}, bf16[384,1024]{1,0:T(8,128)(2,1)}, u32[]{:S(2)}) %copy-start.1) | copy-done | bytes 786456
  8.2 2.4 %first_stats.1 = (f32[8,3072]{1,0:T(8,128)S(1)}, bf16[384,1024]{1,0:T(8,128)(2,1)S(1)}, bf16[384,1024]{1,0:T(8,128)(2,1)S(1)}, bf16[384,128]{1,0:T(8,128)(2,1)S(...) custom-call(s32[1]{0:T(128)} %bitcast.refs_1_.refs_0_, s32[4]{0:T(128)S(1)} %bitcast.15, ...), custom_call_target="tpu_custom_call" | custom-call | flops 2415919104 | bytes 3145728 | tf_op jit(solution)/shard_map/first_stats/pallas_call | solution.py:39
  11.0 1.7 %prepare.1.refs_8_ = bf16[8192,384]{1,0:T(8,128)(2,1)S(1)} custom-call(bf16[384,8192]{1,0:T(8,128)(2,1)S(1)} %copy-done, f32[8,3072]{1,0:T(8,128)S(1)} %get-tuple-element.70.refs_1_.refs_5_), custom_call_target="tpu_custom_call" | custom-call | tf_op jit(solution)/shard_map/prepare/pallas_call | solution.py:39
  12.7 1.9 %collective-permute-start.2 = (bf16[384,128]{1,0:T(8,128)(2,1)S(1)}, bf16[384,128]{1,0:T(8,128)(2,1)S(1)}, u32[]{:S(2)}, u32[]{:S(2)}) collective-permute-start(bf16[384,128]{1,0:T(8,128)(2,1)S(1)} %collective-permute-done.1.refs_6_.refs_3_.refs_4_.refs_2_), channel_id=1, source_target_pairs={{0,1},{1,0},{2,3},{3,2},{4,5},{5,4},{6,7},{7,6},{8,9},{9,8},{10,11... | collective-permute-start | bytes 294920 | tf_op jit(solution)/shard_map/ppermute | solution.py:548
  14.6 1.1 %collective-permute-start.4 = (bf16[384,128]{1,0:T(8,128)(2,1)S(1)}, bf16[384,128]{1,0:T(8,128)(2,1)S(1)}, u32[]{:S(2)}, u32[]{:S(2)}) collective-permute-start(bf16[384,128]{1,0:T(8,128)(2,1)S(1)} %collective-permute-done.3.refs_7_.refs_4_.refs_5_), channel_id=1, source_target_pairs={{0,1},{1,0},{2,3},{3,2},{4,5},{5,4},{6,7},{7,6},{8,9},{9,8},{10,11... | collective-permute-start | bytes 294920 | tf_op jit(solution)/shard_map/ppermute | solution.py:548
  16.0 1.7 %collective-permute-done.2.refs_3_.refs_4_ = bf16[384,128]{1,0:T(8,128)(2,1)S(1)} collective-permute-done((bf16[384,128]{1,0:T(8,128)(2,1)S(1)}, bf16[384,128]{1,0:T(8,128)(2,1)S(1)}, u32[]{:S(2)}, u32[]{:S(2)}) %collective-permute-start.2) | collective-permute-done | bytes 98336 | tf_op jit(solution)/shard_map/ppermute | solution.py:548
  17.8 1.5 %collective-permute-done.4.refs_4_.refs_5_ = bf16[384,128]{1,0:T(8,128)(2,1)S(1)} collective-permute-done((bf16[384,128]{1,0:T(8,128)(2,1)S(1)}, bf16[384,128]{1,0:T(8,128)(2,1)S(1)}, u32[]{:S(2)}, u32[]{:S(2)}) %collective-permute-start.4) | collective-permute-done | bytes 98336 | tf_op jit(solution)/shard_map/ppermute | solution.py:548
  19.9 6.1 %collective-permute-start.6 = (bf16[400,128]{1,0:T(8,128)(2,1)S(1)}, bf16[400,128]{1,0:T(8,128)(2,1)S(1)}, u32[]{:S(2)}, u32[]{:S(2)}) collective-permute-start(bf16[400,128]{1,0:T(8,128)(2,1)S(1)} %get-tuple-element.72.refs_6_), channel_id=1, source_target_pairs={{0,1},{1,0},{2,3},{3,2},{4,5},{5,4},{6,7},{7,6},{8,9},{9,8},{10,11... | collective-permute-start | bytes 307208 | tf_op jit(solution)/shard_map/ppermute | solution.py:548
  26.3 2.3 %collective-permute-done.6.refs_1_ = bf16[400,128]{1,0:T(8,128)(2,1)S(1)} collective-permute-done((bf16[400,128]{1,0:T(8,128)(2,1)S(1)}, bf16[400,128]{1,0:T(8,128)(2,1)S(1)}, u32[]{:S(2)}, u32[]{:S(2)}) %collective-permute-start.6) | collective-permute-done | bytes 102432 | tf_op jit(solution)/shard_map/ppermute | solution.py:548
  28.6 3.2 %collective-permute-start.10 = (bf16[400,128]{1,0:T(8,128)(2,1)S(1)}, bf16[400,128]{1,0:T(8,128)(2,1)S(1)}, u32[]{:S(2)}, u32[]{:S(2)}) collective-permute-start(bf16[400,128]{1,0:T(8,128)(2,1)S(1)} %merge.2.refs_2_.refs_6_), channel_id=1, source_target_pairs={{0,2},{1,3},{2,0},{3,1},{4,6},{5,7},{6,4},{7,5},{8,10},{9,11},{10,... | collective-permute-start | bytes 307208 | tf_op jit(solution)/shard_map/ppermute | solution.py:548
  32.4 3.5 %collective-permute-start.11 = (bf16[400,128]{1,0:T(8,128)(2,1)S(1)}, bf16[400,128]{1,0:T(8,128)(2,1)S(1)}, u32[]{:S(2)}, u32[]{:S(2)}) collective-permute-start(bf16[400,128]{1,0:T(8,128)(2,1)S(1)} %get-tuple-element.76.refs_5_), channel_id=1, source_target_pairs={{0,1},{1,0},{2,3},{3,2},{4,5},{5,4},{6,7},{7,6},{8,9},{9,8},{10,11... | collective-permute-start | bytes 307208 | tf_op jit(solution)/shard_map/ppermute | solution.py:548
  36.9 2.6 %own_gradients.1 = (f32[384,256]{1,0:T(8,128)S(1)}, bf16[384,3072]{1,0:T(8,128)(2,1)S(1)}) custom-call(f32[8,3072]{1,0:T(8,128)S(1)} %next_stats.5.refs_1_.refs_0_, bf16[384,1024]{1,0:T(8,128)(2,1)S(1)} %get-tuple-element.68.refs_1_.refs_2_, bf16[384,1024]{1,0:T(8,128)(2,1)S(1)} %get-tuple-element.69.refs_2_.refs_3_, ...), custom_call_target="tpu_custom_call" | custom-call | tf_op jit(solution)/shard_map/own_gradients/pallas_call | solution.py:39
  40.0 1.5 %send_tiles.2 = (bf16[4128,128]{1,0:T(8,128)(2,1)S(1)}, f32[16,128]{1,0:T(8,128)S(1)}, bf16[384,128]{1,0:T(8,128)(2,1)S(1)}, bf16[384,128]{1,0:T(8,128)(2,1)}) custom-call(s32[1]{0:T(128)} %bitcast.2.refs_0_, f32[384,256]{1,0:T(8,128)S(1)} %get-tuple-element.82.refs_1_, bf16[400,128]{1,0:T(8,128)(2,1)S(1)} %collective-permute-done.10.refs_2_, ...), custom_call_target="tpu_custom_call" | custom-call | tf_op jit(solution)/shard_map/send_tiles/pallas_call | solution.py:39
  41.5 1.1 %kept_tiles.2 = (f32[4,1024,128]{2,1,0:T(8,128)S(1)}, f32[16,128]{1,0:T(8,128)S(1)}) custom-call(s32[1]{0:T(128)} %bitcast.2.refs_0_, bf16[384,128]{1,0:T(8,128)(2,1)S(1)} %get-tuple-element.83.refs_1_, f32[16,128]{1,0:T(8,128)S(1)} %get-tuple-element.84.refs_2_, bf16[8,4,256,384]{3,2,1,0:T(8,128)(2,1)S(1)} %bitcast.6, f32[8,4,256,256]{3,2,1,0:T(8,128)S(1)} %bitcast.12), custom_call_target="tpu_custom_call" | custom-call | tf_op jit(solution)/shard_map/kept_tiles/pallas_call | solution.py:39
  42.6 1.6 %kept_tiles.3 = (f32[4,1024,128]{2,1,0:T(8,128)S(1)}, f32[16,128]{1,0:T(8,128)S(1)}, bf16[384,128]{1,0:T(8,128)(2,1)S(1)}, bf16[384,128]{1,0:T(8,128)(2,1)}) custom-call(s32[1]{0:T(128)} %bitcast.2.refs_0_, f32[384,256]{1,0:T(8,128)S(1)} %get-tuple-element.82.refs_1_, bf16[384,128]{1,0:T(8,128)(2,1)S(1)} %collective-permute-done.8.refs_2_, ...), custom_call_target="tpu_custom_call" | custom-call | tf_op jit(solution)/shard_map/kept_tiles/pallas_call | solution.py:39
  44.2 1.2 %send_tiles.3 = (bf16[4112,128]{1,0:T(8,128)(2,1)S(1)}, f32[16,128]{1,0:T(8,128)S(1)}) custom-call(s32[1]{0:T(128)} %bitcast.2.refs_0_, bf16[384,128]{1,0:T(8,128)(2,1)S(1)} %get-tuple-element.87.refs_1_, f32[16,128]{1,0:T(8,128)S(1)} %get-tuple-element.88.refs_2_, bf16[8,4,256,384]{3,2,1,0:T(8,128)(2,1)S(1)} %bitcast.8, f32[8,4,256,256]{3,2,1,0:T(8,128)S(1)} %bitcast.14), custom_call_target="tpu_custom_call" | custom-call | tf_op jit(solution)/shard_map/send_tiles/pallas_call | solution.py:39
  46.0 2.2 %collective-permute-start.20 = (bf16[1056,128]{1,0:T(8,128)(2,1)S(1)}, bf16[1056,128]{1,0:T(8,128)(2,1)S(1)}, u32[]{:S(2)}, u32[]{:S(2)}) collective-permute-start(bf16[1056,128]{1,0:T(8,128)(2,1)S(1)} %get-tuple-element.112), channel_id=1, source_target_pairs={{0,8},{4,12},{8,0},{12,4},{16,24},{20,28},{24,16},{28,20},{1,9},{5... | collective-permute-start | bytes 811016 | tf_op jit(solution)/shard_map/ppermute | solution.py:545
  48.3 2.0 %collective-permute-start.21 = (bf16[1024,128]{1,0:T(8,128)(2,1)S(1)}, bf16[1024,128]{1,0:T(8,128)(2,1)S(1)}, u32[]{:S(2)}, u32[]{:S(2)}) collective-permute-start(bf16[1024,128]{1,0:T(8,128)(2,1)S(1)} %get-tuple-element.114), channel_id=1, source_target_pairs={{0,16},{4,20},{8,24},{12,28},{16,0},{20,4},{24,8},{28,12},{1,17},{... | collective-permute-start | bytes 786440 | tf_op jit(solution)/shard_map/ppermute | solution.py:545
  51.3 1.6 %collective-permute-start.14 = (bf16[1024,128]{1,0:T(8,128)(2,1)S(1)}, bf16[1024,128]{1,0:T(8,128)(2,1)S(1)}, u32[]{:S(2)}, u32[]{:S(2)}) collective-permute-start(bf16[1024,128]{1,0:T(8,128)(2,1)S(1)} %get-tuple-element.97), channel_id=1, source_target_pairs={{0,16},{4,20},{8,24},{12,28},{16,0},{20,4},{24,8},{28,12},{1,17},{... | collective-permute-start | bytes 786440 | tf_op jit(solution)/shard_map/ppermute | solution.py:545
  52.9 3.8 %query_gradients.1 = (bf16[384,1024]{1,0:T(8,128)(2,1)}, f32[8,128]{1,0:T(8,128)S(1)}) custom-call(bf16[384,128]{1,0:T(8,128)(2,1)S(1)} %get-tuple-element.66.refs_3_.refs_0_, bf16[384,128]{1,0:T(8,128)(2,1)S(1)} %collective-permute-done.refs_3_.refs_4_.refs_1_, bf16[384,128]{1,0:T(8,128)(2,1)S(1)} %collective-permute-done.1.refs_6_.refs_3_.refs_4_.refs_2_, ...), custom_call_target="tpu_custom_call" | custom-call | flops 1207959552 | bytes 6291456 | tf_op jit(solution)/shard_map/query_gradients/pallas_call | solution.py:39
  57.6 2.1 %collective-permute-start.22 = (bf16[544,128]{1,0:T(8,128)(2,1)S(1)}, bf16[544,128]{1,0:T(8,128)(2,1)S(1)}, u32[]{:S(2)}, u32[]{:S(2)}) collective-permute-start(bf16[544,128]{1,0:T(8,128)(2,1)S(1)} %get-tuple-element.117), channel_id=1, source_target_pairs={{0,16},{4,20},{8,24},{12,28},{16,0},{20,4},{24,8},{28,12},{1,17},{... | collective-permute-start | bytes 417800 | tf_op jit(solution)/shard_map/ppermute | solution.py:545
  60.2 2.9 %collective-permute-done.14.refs_3_ = bf16[1024,128]{1,0:T(8,128)(2,1)S(1)} collective-permute-done((bf16[1024,128]{1,0:T(8,128)(2,1)S(1)}, bf16[1024,128]{1,0:T(8,128)(2,1)S(1)}, u32[]{:S(2)}, u32[]{:S(2)}) %collective-permute-start.14) | collective-permute-done | bytes 262176 | tf_op jit(solution)/shard_map/ppermute | solution.py:545
  63.4 2.1 %collective-permute-start.15 = (bf16[528,128]{1,0:T(8,128)(2,1)S(1)}, bf16[528,128]{1,0:T(8,128)(2,1)S(1)}, u32[]{:S(2)}, u32[]{:S(2)}) collective-permute-start(bf16[528,128]{1,0:T(8,128)(2,1)S(1)} %get-tuple-element.100), channel_id=1, source_target_pairs={{0,16},{4,20},{8,24},{12,28},{16,0},{20,4},{24,8},{28,12},{1,17},{... | collective-permute-start | bytes 405512 | tf_op jit(solution)/shard_map/ppermute | solution.py:545
  66.0 2.0 %collective-permute-start.24 = (bf16[544,128]{1,0:T(8,128)(2,1)S(1)}, bf16[544,128]{1,0:T(8,128)(2,1)S(1)}, u32[]{:S(2)}, u32[]{:S(2)}) collective-permute-start(bf16[544,128]{1,0:T(8,128)(2,1)S(1)} %get-tuple-element.121), channel_id=1, source_target_pairs={{0,1},{1,0},{2,3},{3,2},{4,5},{5,4},{6,7},{7,6},{8,9},{9,8},{10,11... | collective-permute-start | bytes 417800 | tf_op jit(solution)/shard_map/ppermute | solution.py:548
  68.1 2.4 %collective-permute-done.16.refs_4_ = bf16[512,128]{1,0:T(8,128)(2,1)S(1)} collective-permute-done((bf16[512,128]{1,0:T(8,128)(2,1)S(1)}, bf16[512,128]{1,0:T(8,128)(2,1)S(1)}, u32[]{:S(2)}, u32[]{:S(2)}) %collective-permute-start.16) | collective-permute-done | bytes 131104 | tf_op jit(solution)/shard_map/ppermute | solution.py:545
  70.9 2.3 %collective-permute-done.24.refs_1_ = bf16[544,128]{1,0:T(8,128)(2,1)S(1)} collective-permute-done((bf16[544,128]{1,0:T(8,128)(2,1)S(1)}, bf16[544,128]{1,0:T(8,128)(2,1)S(1)}, u32[]{:S(2)}, u32[]{:S(2)}) %collective-permute-start.24) | collective-permute-done | bytes 139296 | tf_op jit(solution)/shard_map/ppermute | solution.py:548
  73.2 1.3 %collective-permute-start.25 = (bf16[288,128]{1,0:T(8,128)(2,1)S(1)}, bf16[288,128]{1,0:T(8,128)(2,1)S(1)}, u32[]{:S(2)}, u32[]{:S(2)}) collective-permute-start(bf16[288,128]{1,0:T(8,128)(2,1)S(1)} %get-tuple-element.123), channel_id=1, source_target_pairs={{0,2},{1,3},{2,0},{3,1},{4,6},{5,7},{6,4},{7,5},{8,10},{9,11},{10,... | collective-permute-start | bytes 221192 | tf_op jit(solution)/shard_map/ppermute | solution.py:548
  74.5 1.1 %collective-permute-done.17.refs_1_ = bf16[528,128]{1,0:T(8,128)(2,1)S(1)} collective-permute-done((bf16[528,128]{1,0:T(8,128)(2,1)S(1)}, bf16[528,128]{1,0:T(8,128)(2,1)S(1)}, u32[]{:S(2)}, u32[]{:S(2)}) %collective-permute-start.17) | collective-permute-done | bytes 135200 | tf_op jit(solution)/shard_map/ppermute | solution.py:548
  75.8 1.2 %collective-permute-start.18 = (bf16[272,128]{1,0:T(8,128)(2,1)S(1)}, bf16[272,128]{1,0:T(8,128)(2,1)S(1)}, u32[]{:S(2)}, u32[]{:S(2)}) collective-permute-start(bf16[272,128]{1,0:T(8,128)(2,1)S(1)} %get-tuple-element.108), channel_id=1, source_target_pairs={{0,2},{1,3},{2,0},{3,1},{4,6},{5,7},{6,4},{7,5},{8,10},{9,11},{10,... | collective-permute-start | bytes 208904 | tf_op jit(solution)/shard_map/ppermute | solution.py:548
  77.1 4.6 %collective-permute-done.18.refs_3_ = bf16[272,128]{1,0:T(8,128)(2,1)S(1)} collective-permute-done((bf16[272,128]{1,0:T(8,128)(2,1)S(1)}, bf16[272,128]{1,0:T(8,128)(2,1)S(1)}, u32[]{:S(2)}, u32[]{:S(2)}) %collective-permute-start.18) | collective-permute-done | bytes 69664 | tf_op jit(solution)/shard_map/ppermute | solution.py:548
  (64 shorter events, 10.5 us)
Async XLA Ops:
  0.6 12.1 %collective-permute-start.1 = (bf16[384,128]{1,0:T(8,128)(2,1)}, bf16[384,128]{1,0:T(8,128)(2,1)S(1)}, u32[]{:S(2)}, u32[]{:S(2)}) collective-permute-start(bf16[384,128]{1,0:T(8,128)(2,1)} %refs_4_.1), channel_id=1, source_target_pairs={{0,2},{1,3},{2,0},{3,1},{4,6},{5,7},{6,4},{7,5},{8,10},{9,11},{10,... | collective-permute-start | bytes 294920 | tf_op jit(solution)/shard_map/ppermute | solution.py:548
  4.7 11.0 %collective-permute-start = (bf16[384,128]{1,0:T(8,128)(2,1)}, bf16[384,128]{1,0:T(8,128)(2,1)S(1)}, u32[]{:S(2)}, u32[]{:S(2)}) collective-permute-start(bf16[384,128]{1,0:T(8,128)(2,1)} %refs_4_.1), channel_id=1, source_target_pairs={{0,1},{1,0},{2,3},{3,2},{4,5},{5,4},{6,7},{7,6},{8,9},{9,8},{10,11... | collective-permute-start | bytes 294920 | tf_op jit(solution)/shard_map/ppermute | solution.py:548
  6.3 9.4 %collective-permute-start.5 = (bf16[384,128]{1,0:T(8,128)(2,1)}, bf16[384,128]{1,0:T(8,128)(2,1)S(1)}, u32[]{:S(2)}, u32[]{:S(2)}) collective-permute-start(bf16[384,128]{1,0:T(8,128)(2,1)} %refs_5_.1), channel_id=1, source_target_pairs={{0,1},{1,0},{2,3},{3,2},{4,5},{5,4},{6,7},{7,6},{8,9},{9,8},{10,11... | collective-permute-start | bytes 294920 | tf_op jit(solution)/shard_map/ppermute | solution.py:548
  6.8 7.8 %collective-permute-start.3 = (bf16[384,128]{1,0:T(8,128)(2,1)}, bf16[384,128]{1,0:T(8,128)(2,1)S(1)}, u32[]{:S(2)}, u32[]{:S(2)}) collective-permute-start(bf16[384,128]{1,0:T(8,128)(2,1)} %refs_5_.1), channel_id=1, source_target_pairs={{0,2},{1,3},{2,0},{3,1},{4,6},{5,7},{6,4},{7,5},{8,10},{9,11},{10,... | collective-permute-start | bytes 294920 | tf_op jit(solution)/shard_map/ppermute | solution.py:548
  6.8 1.4 %copy-start.3 = (bf16[384,128]{1,0:T(8,128)(2,1)S(1)}, bf16[384,128]{1,0:T(8,128)(2,1)}, u32[]{:S(2)}) copy-start(bf16[384,128]{1,0:T(8,128)(2,1)} %refs_4_.1) | copy-start | bytes 294916
  6.8 1.4 %copy-start.4 = (bf16[384,128]{1,0:T(8,128)(2,1)S(1)}, bf16[384,128]{1,0:T(8,128)(2,1)}, u32[]{:S(2)}) copy-start(bf16[384,128]{1,0:T(8,128)(2,1)} %refs_5_.1) | copy-start | bytes 294916
  6.9 1.4 %copy-start.5 = (s32[1,4]{1,0:T(1,128)S(1)}, s32[1,4]{1,0:T(1,128)}, u32[]{:S(2)}) copy-start(s32[1,4]{1,0:T(1,128)} %param.7) | copy-start | bytes 52
  8.2 2.8 %copy-start = (bf16[384,8192]{1,0:T(8,128)(2,1)S(1)}, bf16[384,8192]{1,0:T(8,128)(2,1)}, u32[]{:S(2)}) copy-start(bf16[384,8192]{1,0:T(8,128)(2,1)} %refs_0_.1) | copy-start | bytes 18874372
  12.7 5.1 %collective-permute-start.2 = (bf16[384,128]{1,0:T(8,128)(2,1)S(1)}, bf16[384,128]{1,0:T(8,128)(2,1)S(1)}, u32[]{:S(2)}, u32[]{:S(2)}) collective-permute-start(bf16[384,128]{1,0:T(8,128)(2,1)S(1)} %collective-permute-done.1.refs_6_.refs_3_.refs_4_.refs_2_), channel_id=1, source_target_pairs={{0,1},{1,0},{2,3},{3,2},{4,5},{5,4},{6,7},{7,6},{8,9},{9,8},{10,11... | collective-permute-start | bytes 294920 | tf_op jit(solution)/shard_map/ppermute | solution.py:548
  14.6 4.6 %collective-permute-start.4 = (bf16[384,128]{1,0:T(8,128)(2,1)S(1)}, bf16[384,128]{1,0:T(8,128)(2,1)S(1)}, u32[]{:S(2)}, u32[]{:S(2)}) collective-permute-start(bf16[384,128]{1,0:T(8,128)(2,1)S(1)} %collective-permute-done.3.refs_7_.refs_4_.refs_5_), channel_id=1, source_target_pairs={{0,1},{1,0},{2,3},{3,2},{4,5},{5,4},{6,7},{7,6},{8,9},{9,8},{10,11... | collective-permute-start | bytes 294920 | tf_op jit(solution)/shard_map/ppermute | solution.py:548
  15.9 24.1 %slice-start = ((s8[8388608]{0:T(1024)(128)(4,1)}), s8[4194304]{0:T(1024)(128)(4,1)S(1)}, s32[]{:S(2)}) async-start(s8[8388608]{0:T(1024)(128)(4,1)} %bitcast.9), calls=%async_computation | async-start | bytes 8388608
  16.0 23.9 %slice-start.1 = ((s8[8388608]{0:T(1024)(128)(4,1)}), s8[4194304]{0:T(1024)(128)(4,1)S(1)}, s32[]{:S(2)}) async-start(s8[8388608]{0:T(1024)(128)(4,1)} %bitcast.9), calls=%async_computation.1 | async-start | bytes 8388608
  19.9 8.7 %collective-permute-start.6 = (bf16[400,128]{1,0:T(8,128)(2,1)S(1)}, bf16[400,128]{1,0:T(8,128)(2,1)S(1)}, u32[]{:S(2)}, u32[]{:S(2)}) collective-permute-start(bf16[400,128]{1,0:T(8,128)(2,1)S(1)} %get-tuple-element.72.refs_6_), channel_id=1, source_target_pairs={{0,1},{1,0},{2,3},{3,2},{4,5},{5,4},{6,7},{7,6},{8,9},{9,8},{10,11... | collective-permute-start | bytes 307208 | tf_op jit(solution)/shard_map/ppermute | solution.py:548
  25.9 5.9 %collective-permute-start.7 = (bf16[384,128]{1,0:T(8,128)(2,1)S(1)}, bf16[384,128]{1,0:T(8,128)(2,1)S(1)}, u32[]{:S(2)}, u32[]{:S(2)}) collective-permute-start(bf16[384,128]{1,0:T(8,128)(2,1)S(1)} %get-tuple-element.73.refs_7_), channel_id=1, source_target_pairs={{0,1},{1,0},{2,3},{3,2},{4,5},{5,4},{6,7},{7,6},{8,9},{9,8},{10,11... | collective-permute-start | bytes 294920 | tf_op jit(solution)/shard_map/ppermute | solution.py:548
  28.6 11.0 %collective-permute-start.10 = (bf16[400,128]{1,0:T(8,128)(2,1)S(1)}, bf16[400,128]{1,0:T(8,128)(2,1)S(1)}, u32[]{:S(2)}, u32[]{:S(2)}) collective-permute-start(bf16[400,128]{1,0:T(8,128)(2,1)S(1)} %merge.2.refs_2_.refs_6_), channel_id=1, source_target_pairs={{0,2},{1,3},{2,0},{3,1},{4,6},{5,7},{6,4},{7,5},{8,10},{9,11},{10,... | collective-permute-start | bytes 307208 | tf_op jit(solution)/shard_map/ppermute | solution.py:548
  32.4 7.6 %collective-permute-start.11 = (bf16[400,128]{1,0:T(8,128)(2,1)S(1)}, bf16[400,128]{1,0:T(8,128)(2,1)S(1)}, u32[]{:S(2)}, u32[]{:S(2)}) collective-permute-start(bf16[400,128]{1,0:T(8,128)(2,1)S(1)} %get-tuple-element.76.refs_5_), channel_id=1, source_target_pairs={{0,1},{1,0},{2,3},{3,2},{4,5},{5,4},{6,7},{7,6},{8,9},{9,8},{10,11... | collective-permute-start | bytes 307208 | tf_op jit(solution)/shard_map/ppermute | solution.py:548
  35.8 6.7 %collective-permute-start.8 = (bf16[384,128]{1,0:T(8,128)(2,1)S(1)}, bf16[384,128]{1,0:T(8,128)(2,1)S(1)}, u32[]{:S(2)}, u32[]{:S(2)}) collective-permute-start(bf16[384,128]{1,0:T(8,128)(2,1)S(1)} %merge.3.refs_7_), channel_id=1, source_target_pairs={{0,2},{1,3},{2,0},{3,1},{4,6},{5,7},{6,4},{7,5},{8,10},{9,11},{10,... | collective-permute-start | bytes 294920 | tf_op jit(solution)/shard_map/ppermute | solution.py:548
  36.9 5.7 %collective-permute-start.9 = (bf16[384,128]{1,0:T(8,128)(2,1)S(1)}, bf16[384,128]{1,0:T(8,128)(2,1)S(1)}, u32[]{:S(2)}, u32[]{:S(2)}) collective-permute-start(bf16[384,128]{1,0:T(8,128)(2,1)S(1)} %get-tuple-element.77.refs_6_), channel_id=1, source_target_pairs={{0,1},{1,0},{2,3},{3,2},{4,5},{5,4},{6,7},{7,6},{8,9},{9,8},{10,11... | collective-permute-start | bytes 294920 | tf_op jit(solution)/shard_map/ppermute | solution.py:548
  41.5 4.4 %collective-permute-start.19 = (bf16[4128,128]{1,0:T(8,128)(2,1)S(1)}, bf16[4128,128]{1,0:T(8,128)(2,1)S(1)}, u32[]{:S(2)}, u32[]{:S(2)}) collective-permute-start(bf16[4128,128]{1,0:T(8,128)(2,1)S(1)} %get-tuple-element.110), channel_id=1, source_target_pairs={{0,4},{4,0},{8,12},{12,8},{16,20},{20,16},{24,28},{28,24},{1,5},{5... | collective-permute-start | bytes 3170312 | tf_op jit(solution)/shard_map/ppermute | solution.py:545
  45.3 5.0 %collective-permute-start.12 = (bf16[4112,128]{1,0:T(8,128)(2,1)S(1)}, bf16[4112,128]{1,0:T(8,128)(2,1)S(1)}, u32[]{:S(2)}, u32[]{:S(2)}) collective-permute-start(bf16[4112,128]{1,0:T(8,128)(2,1)S(1)} %get-tuple-element.89), channel_id=1, source_target_pairs={{0,4},{4,0},{8,12},{12,8},{16,20},{20,16},{24,28},{28,24},{1,5},{5... | collective-permute-start | bytes 3158024 | tf_op jit(solution)/shard_map/ppermute | solution.py:545
  46.0 11.4 %collective-permute-start.20 = (bf16[1056,128]{1,0:T(8,128)(2,1)S(1)}, bf16[1056,128]{1,0:T(8,128)(2,1)S(1)}, u32[]{:S(2)}, u32[]{:S(2)}) collective-permute-start(bf16[1056,128]{1,0:T(8,128)(2,1)S(1)} %get-tuple-element.112), channel_id=1, source_target_pairs={{0,8},{4,12},{8,0},{12,4},{16,24},{20,28},{24,16},{28,20},{1,9},{5... | collective-permute-start | bytes 811016 | tf_op jit(solution)/shard_map/ppermute | solution.py:545
  48.3 9.2 %collective-permute-start.21 = (bf16[1024,128]{1,0:T(8,128)(2,1)S(1)}, bf16[1024,128]{1,0:T(8,128)(2,1)S(1)}, u32[]{:S(2)}, u32[]{:S(2)}) collective-permute-start(bf16[1024,128]{1,0:T(8,128)(2,1)S(1)} %get-tuple-element.114), channel_id=1, source_target_pairs={{0,16},{4,20},{8,24},{12,28},{16,0},{20,4},{24,8},{28,12},{1,17},{... | collective-permute-start | bytes 786440 | tf_op jit(solution)/shard_map/ppermute | solution.py:545
  50.7 12.4 %collective-permute-start.13 = (bf16[1040,128]{1,0:T(8,128)(2,1)S(1)}, bf16[1040,128]{1,0:T(8,128)(2,1)S(1)}, u32[]{:S(2)}, u32[]{:S(2)}) collective-permute-start(bf16[1040,128]{1,0:T(8,128)(2,1)S(1)} %get-tuple-element.95), channel_id=1, source_target_pairs={{0,8},{4,12},{8,0},{12,4},{16,24},{20,28},{24,16},{28,20},{1,9},{5... | collective-permute-start | bytes 798728 | tf_op jit(solution)/shard_map/ppermute | solution.py:545
  51.3 11.8 %collective-permute-start.14 = (bf16[1024,128]{1,0:T(8,128)(2,1)S(1)}, bf16[1024,128]{1,0:T(8,128)(2,1)S(1)}, u32[]{:S(2)}, u32[]{:S(2)}) collective-permute-start(bf16[1024,128]{1,0:T(8,128)(2,1)S(1)} %get-tuple-element.97), channel_id=1, source_target_pairs={{0,16},{4,20},{8,24},{12,28},{16,0},{20,4},{24,8},{28,12},{1,17},{... | collective-permute-start | bytes 786440 | tf_op jit(solution)/shard_map/ppermute | solution.py:545
  57.6 8.4 %collective-permute-start.22 = (bf16[544,128]{1,0:T(8,128)(2,1)S(1)}, bf16[544,128]{1,0:T(8,128)(2,1)S(1)}, u32[]{:S(2)}, u32[]{:S(2)}) collective-permute-start(bf16[544,128]{1,0:T(8,128)(2,1)S(1)} %get-tuple-element.117), channel_id=1, source_target_pairs={{0,16},{4,20},{8,24},{12,28},{16,0},{20,4},{24,8},{28,12},{1,17},{... | collective-permute-start | bytes 417800 | tf_op jit(solution)/shard_map/ppermute | solution.py:545
  59.7 6.2 %collective-permute-start.23 = (bf16[512,128]{1,0:T(8,128)(2,1)S(1)}, bf16[512,128]{1,0:T(8,128)(2,1)S(1)}, u32[]{:S(2)}, u32[]{:S(2)}) collective-permute-start(bf16[512,128]{1,0:T(8,128)(2,1)S(1)} %get-tuple-element.119), channel_id=1, source_target_pairs={{0,8},{4,12},{8,0},{12,4},{16,24},{20,28},{24,16},{28,20},{1,9},{5... | collective-permute-start | bytes 393224 | tf_op jit(solution)/shard_map/ppermute | solution.py:545
  63.4 7.1 %collective-permute-start.15 = (bf16[528,128]{1,0:T(8,128)(2,1)S(1)}, bf16[528,128]{1,0:T(8,128)(2,1)S(1)}, u32[]{:S(2)}, u32[]{:S(2)}) collective-permute-start(bf16[528,128]{1,0:T(8,128)(2,1)S(1)} %get-tuple-element.100), channel_id=1, source_target_pairs={{0,16},{4,20},{8,24},{12,28},{16,0},{20,4},{24,8},{28,12},{1,17},{... | collective-permute-start | bytes 405512 | tf_op jit(solution)/shard_map/ppermute | solution.py:545
  65.5 5.0 %collective-permute-start.16 = (bf16[512,128]{1,0:T(8,128)(2,1)S(1)}, bf16[512,128]{1,0:T(8,128)(2,1)S(1)}, u32[]{:S(2)}, u32[]{:S(2)}) collective-permute-start(bf16[512,128]{1,0:T(8,128)(2,1)S(1)} %get-tuple-element.102), channel_id=1, source_target_pairs={{0,8},{4,12},{8,0},{12,4},{16,24},{20,28},{24,16},{28,20},{1,9},{5... | collective-permute-start | bytes 393224 | tf_op jit(solution)/shard_map/ppermute | solution.py:545
  66.0 7.1 %collective-permute-start.24 = (bf16[544,128]{1,0:T(8,128)(2,1)S(1)}, bf16[544,128]{1,0:T(8,128)(2,1)S(1)}, u32[]{:S(2)}, u32[]{:S(2)}) collective-permute-start(bf16[544,128]{1,0:T(8,128)(2,1)S(1)} %get-tuple-element.121), channel_id=1, source_target_pairs={{0,1},{1,0},{2,3},{3,2},{4,5},{5,4},{6,7},{7,6},{8,9},{9,8},{10,11... | collective-permute-start | bytes 417800 | tf_op jit(solution)/shard_map/ppermute | solution.py:548
  70.6 5.1 %collective-permute-start.17 = (bf16[528,128]{1,0:T(8,128)(2,1)S(1)}, bf16[528,128]{1,0:T(8,128)(2,1)S(1)}, u32[]{:S(2)}, u32[]{:S(2)}) collective-permute-start(bf16[528,128]{1,0:T(8,128)(2,1)S(1)} %get-tuple-element.105), channel_id=1, source_target_pairs={{0,1},{1,0},{2,3},{3,2},{4,5},{5,4},{6,7},{7,6},{8,9},{9,8},{10,11... | collective-permute-start | bytes 405512 | tf_op jit(solution)/shard_map/ppermute | solution.py:548
  73.2 8.5 %collective-permute-start.25 = (bf16[288,128]{1,0:T(8,128)(2,1)S(1)}, bf16[288,128]{1,0:T(8,128)(2,1)S(1)}, u32[]{:S(2)}, u32[]{:S(2)}) collective-permute-start(bf16[288,128]{1,0:T(8,128)(2,1)S(1)} %get-tuple-element.123), channel_id=1, source_target_pairs={{0,2},{1,3},{2,0},{3,1},{4,6},{5,7},{6,4},{7,5},{8,10},{9,11},{10,... | collective-permute-start | bytes 221192 | tf_op jit(solution)/shard_map/ppermute | solution.py:548
  75.8 5.8 %collective-permute-start.18 = (bf16[272,128]{1,0:T(8,128)(2,1)S(1)}, bf16[272,128]{1,0:T(8,128)(2,1)S(1)}, u32[]{:S(2)}, u32[]{:S(2)}) collective-permute-start(bf16[272,128]{1,0:T(8,128)(2,1)S(1)} %get-tuple-element.108), channel_id=1, source_target_pairs={{0,2},{1,3},{2,0},{3,1},{4,6},{5,7},{6,4},{7,5},{8,10},{9,11},{10,... | collective-permute-start | bytes 208904 | tf_op jit(solution)/shard_map/ppermute | solution.py:548
  (2 other events, 2.5 us)

commit v14 on v12

--- a/solution.py
+++ b/solution.py
@@ -289,10 +289,10 @@
             [p_buf, *sums],
             before,
         )
-        own_parts[b] = dk
         if value_parts[b]:
             dv = merge(rows, [dv, *value_parts[b]], [])
         value_parts[b & (b - 1)].append(swap(dv, b & -b))
+        own_parts[b] = dk
         before = [dv]
     for b in range(n - 1, 0, -1):
         dk = own_parts[b]
@@ -514,18 +514,24 @@
         away[half:, :] = jnp.zeros((away.shape[0] - half, away.shape[1]), BF16)
 
 
-def final_kernel(columns, gain, me_dp_ref, me_ctx_ref, *refs):
+def final_kernel(columns, n_ctx, gain, me_dp_ref, me_ctx_ref, *refs):
     sets = len(columns)
     groups = [refs[2 * chosen : 2 * chosen + 2] for chosen in range(sets)]
     top_ref, out_ref, scale_ref, all_tops = refs[2 * sets :]
-    n_dp, lanes = scale_ref.shape
     rows_ctx, hd = groups[0][0].shape
     scale = jnp.maximum(top_ref[...], unpack_top(groups[0][1], rows_ctx)) + 1e-06
     all_tops[...] = scale
-    scale_ref[...] = scale[:n_dp, :lanes]
+    blocks = rows_ctx // QROWS
+    lanes = n_ctx * blocks
+    per_row = TOP_LANES // lanes
+    lane = lax.broadcasted_iota(jnp.int32, scale.shape, 1)
+    group = jnp.where(lane < lanes, scale, 0.0)
+    moved = [group] + [pltpu.roll(group, k * lanes, 1) for k in range(1, per_row)]
+    for r in range(scale_ref.shape[0]):
+        row = [moved[k][r * per_row + k : r * per_row + k + 1, :] for k in range(per_row)]
+        scale_ref[r : r + 1, :] = functools.reduce(jnp.add, row)
     factors = gain / all_tops[pl.ds(me_dp_ref[0], 1), :]
     lane = lax.broadcasted_iota(jnp.int32, factors.shape, 1)
-    blocks = rows_ctx // QROWS
     for r in range(blocks):
         mine = jnp.where(lane == me_ctx_ref[0] * blocks + r, factors, 0.0)
         factor = jnp.sum(mine, axis=1, keepdims=True)
@@ -595,7 +601,6 @@
         "kept_tiles",
         [own, *key_parts, top],
         [kept_shape, tops, grad_shape, grad_shape],
-        halves[0][1:2],
     )
     out, top = tiles(
         functools.partial(next_send_kernel, bits, shrink, 0),
@@ -661,11 +666,11 @@
             mask *= 2
         groups = [stay, swap_ctx(away, mask), *groups]
     payload, scale = whole_call(
-        functools.partial(final_kernel, (0, hd), 7.0 / shrink),
+        functools.partial(final_kernel, (0, hd), n_ctx, 7.0 / shrink),
         "final_stage",
         [me_dp, me_ctx],
         groups + gathered,
-        [shape((rows_ctx, width), F32), shape((n_dp, tall // QROWS), F32)],
+        [shape((rows_ctx, width), F32), shape((model // QROWS // TOP_LANES, TOP_LANES), F32)],
         8,
         (0, 0),
         [pltpu.VMEM((TOP_ROWS, TOP_LANES), F32)],

time: 92.3 us -> 82.2 us (0.89)
  waiting for transfers between devices: 31.2 us -> 13.3 us
  Pallas kernels: 19.9 us -> 33.2 us
  starting transfers between devices: 38.1 us -> 33 us
    ppermute x16, waiting for transfers between devices: 26.1 us -> 5.12 us  [swap_ctx(): return lax.ppermute(x, 'context', xor_perm(n_ctx, mask))]
    pallas_call x26, Pallas kernels: 19.9 us -> 33.2 us  [whole_call(): pl.pallas_call(body, grid_spec=pltpu.PrefetchScalarGridSpec(num_scalar_pr...]
    ppermute x10, waiting for transfers between devices: 5.16 us -> 8.15 us  [swap_dp(): return lax.ppermute(x, 'dp', xor_perm(n_dp, mask))]
    ppermute x16, starting transfers between devices: 25.7 us -> 22.7 us  [swap_ctx(): return lax.ppermute(x, 'context', xor_perm(n_ctx, mask))]
    ppermute x10, starting transfers between devices: 12.4 us -> 10.2 us  [swap_dp(): return lax.ppermute(x, 'dp', xor_perm(n_dp, mask))]
  transfers between devices with their start and end apart: 26 -> 26, of which waited for: 14 -> 7; matrix products, arithmetic and copies ran while one was open for 0% -> 0% of each run, Pallas kernels for 15% -> 33%
where the time goes in v14:
time: 82.2 us; the launch traced here: 82.1 us
  Pallas kernels  33.2 us (40%)
  starting transfers between devices  33 us (40%)
  waiting for transfers between devices  13.3 us (16%)
  local copies, waits for them, and re-layouts  1.73 us (2%)
  between operations  0.89 us (1%)
    pallas_call x26, Pallas kernels, whole_call(): pl.pallas_call(body, grid_spec=pltpu.PrefetchScalarGridSpec(num_scalar_pr...  33.2 us
    ppermute x16, starting transfers between devices, swap_ctx(): return lax.ppermute(x, 'context', xor_perm(n_ctx, mask))  22.7 us
    ppermute x10, starting transfers between devices, swap_dp(): return lax.ppermute(x, 'dp', xor_perm(n_dp, mask))  10.2 us
    ppermute x10, waiting for transfers between devices, swap_dp(): return lax.ppermute(x, 'dp', xor_perm(n_dp, mask))  8.15 us
    ppermute x16, waiting for transfers between devices, swap_ctx(): return lax.ppermute(x, 'context', xor_perm(n_ctx, mask))  5.12 us
    unnamed x16, local copies, waits for them, and re-layouts  1.73 us
  transfers between devices with their start and end apart: 26, of which 7 were waited for; matrix products, arithmetic and copies ran while one was open for 0% of the time, Pallas kernels for 33%

profile of v14, /device:TPU:0, one launch (start us, length us, event | category | flops | bytes accessed | tf_op | source)
XLA Modules:
  0.0 82.1 jit_solution(15792170064881048736)
XLA Ops:
  0.6 4.1 %collective-permute-start.1 = (bf16[384,128]{1,0:T(8,128)(2,1)}, bf16[384,128]{1,0:T(8,128)(2,1)S(1)}, u32[]{:S(2)}, u32[]{:S(2)}) collective-permute-start(bf16[384,128]{1,0:T(8,128)(2,1)} %refs_4_.1), channel_id=1, source_target_pairs={{0,2},{1,3},{2,0},{3,1},{4,6},{5,7},{6,4},{7,5},{8,10},{9,11},{10,... | collective-permute-start | bytes 294920 | tf_op jit(solution)/shard_map/ppermute | solution.py:557
  4.7 1.6 %collective-permute-start = (bf16[384,128]{1,0:T(8,128)(2,1)}, bf16[384,128]{1,0:T(8,128)(2,1)S(1)}, u32[]{:S(2)}, u32[]{:S(2)}) collective-permute-start(bf16[384,128]{1,0:T(8,128)(2,1)} %refs_4_.1), channel_id=1, source_target_pairs={{0,1},{1,0},{2,3},{3,2},{4,5},{5,4},{6,7},{7,6},{8,9},{9,8},{10,11... | collective-permute-start | bytes 294920 | tf_op jit(solution)/shard_map/ppermute | solution.py:557
  6.9 1.1 %copy-done.1 = bf16[384,1024]{1,0:T(8,128)(2,1)S(1)} copy-done((bf16[384,1024]{1,0:T(8,128)(2,1)S(1)}, bf16[384,1024]{1,0:T(8,128)(2,1)}, u32[]{:S(2)}) %copy-start.1) | copy-done | bytes 786456
  8.2 2.4 %first_stats.1 = (f32[8,3072]{1,0:T(8,128)S(1)}, bf16[384,1024]{1,0:T(8,128)(2,1)S(1)}, bf16[384,1024]{1,0:T(8,128)(2,1)S(1)}, bf16[384,128]{1,0:T(8,128)(2,1)S(...) custom-call(s32[1]{0:T(128)} %bitcast.refs_1_.refs_0_, s32[4]{0:T(128)S(1)} %bitcast.16, ...), custom_call_target="tpu_custom_call" | custom-call | flops 2415919104 | bytes 3145728 | tf_op jit(solution)/shard_map/first_stats/pallas_call | solution.py:39
  11.0 1.7 %prepare.1.refs_8_ = bf16[8192,384]{1,0:T(8,128)(2,1)S(1)} custom-call(bf16[384,8192]{1,0:T(8,128)(2,1)S(1)} %copy-done, f32[8,3072]{1,0:T(8,128)S(1)} %get-tuple-element.70.refs_1_.refs_5_), custom_call_target="tpu_custom_call" | custom-call | tf_op jit(solution)/shard_map/prepare/pallas_call | solution.py:39
  12.7 1.9 %collective-permute-start.2 = (bf16[384,128]{1,0:T(8,128)(2,1)S(1)}, bf16[384,128]{1,0:T(8,128)(2,1)S(1)}, u32[]{:S(2)}, u32[]{:S(2)}) collective-permute-start(bf16[384,128]{1,0:T(8,128)(2,1)S(1)} %collective-permute-done.1.refs_6_.refs_3_.refs_4_.refs_2_), channel_id=1, source_target_pairs={{0,1},{1,0},{2,3},{3,2},{4,5},{5,4},{6,7},{7,6},{8,9},{9,8},{10,11... | collective-permute-start | bytes 294920 | tf_op jit(solution)/shard_map/ppermute | solution.py:557
  14.6 1.1 %collective-permute-start.4 = (bf16[384,128]{1,0:T(8,128)(2,1)S(1)}, bf16[384,128]{1,0:T(8,128)(2,1)S(1)}, u32[]{:S(2)}, u32[]{:S(2)}) collective-permute-start(bf16[384,128]{1,0:T(8,128)(2,1)S(1)} %collective-permute-done.3.refs_7_.refs_4_.refs_5_), channel_id=1, source_target_pairs={{0,1},{1,0},{2,3},{3,2},{4,5},{5,4},{6,7},{7,6},{8,9},{9,8},{10,11... | collective-permute-start | bytes 294920 | tf_op jit(solution)/shard_map/ppermute | solution.py:557
  15.7 2.1 %next_stats.3.refs_5_ = f32[8,3072]{1,0:T(8,128)S(1)} custom-call(f32[8,128]{1,0:T(8,128)S(1)} %get-tuple-element.67.refs_0_, bf16[384,1024]{1,0:T(8,128)(2,1)S(1)} %get-tuple-element.68.refs_1_.refs_2_, bf16[384,1024]{1,0:T(8,128)(2,1)S(1)} %get-tuple-element.69.refs_2_.refs_3_, bf16[384,128]{1,0:T(8,128)(2,1)S(1)} %collective-permute-done.refs_3_.refs_4_.refs_1_, ...), custom_call_target="tpu_custom_call" | custom-call | flops 2415919104 | bytes 3145728 | tf_op jit(solution)/shard_map/next_stats/pallas_call | solution.py:39
  17.8 2.1 %next_stats.4.refs_5_ = f32[8,3072]{1,0:T(8,128)S(1)} custom-call(f32[8,128]{1,0:T(8,128)S(1)} %get-tuple-element.67.refs_0_, bf16[384,1024]{1,0:T(8,128)(2,1)S(1)} %get-tuple-element.68.refs_1_.refs_2_, bf16[384,1024]{1,0:T(8,128)(2,1)S(1)} %get-tuple-element.69.refs_2_.refs_3_, bf16[384,128]{1,0:T(8,128)(2,1)S(1)} %collective-permute-done.1.refs_6_.refs_3_.refs_4_.refs_2_, ...), custom_call_target="tpu_custom_call" | custom-call | flops 2415919104 | bytes 3145728 | tf_op jit(solution)/shard_map/next_stats/pallas_call | solution.py:39
  19.9 2.2 %next_stats.5.refs_1_.refs_0_ = f32[8,3072]{1,0:T(8,128)S(1)} custom-call(f32[8,128]{1,0:T(8,128)S(1)} %get-tuple-element.67.refs_0_, bf16[384,1024]{1,0:T(8,128)(2,1)S(1)} %get-tuple-element.68.refs_1_.refs_2_, bf16[384,1024]{1,0:T(8,128)(2,1)S(1)} %get-tuple-element.69.refs_2_.refs_3_, bf16[384,128]{1,0:T(8,128)(2,1)S(1)} %collective-permute-done.2.refs_3_.refs_4_, ...), custom_call_target="tpu_custom_call" | custom-call | flops 2415919104 | bytes 3145728 | tf_op jit(solution)/shard_map/next_stats/pallas_call | solution.py:39
  22.1 3.0 %block_gradients.3 = (bf16[384,128]{1,0:T(8,128)(2,1)S(1)}, bf16[400,128]{1,0:T(8,128)(2,1)S(1)}, bf16[384,3072]{1,0:T(8,128)(2,1)S(1)}) custom-call(f32[8,128]{1,0:T(8,128)S(1)} %get-tuple-element.67.refs_0_, f32[8,3072]{1,0:T(8,128)S(1)} %next_stats.5.refs_1_.refs_0_, bf16[384,1024]{1,0:T(8,128)(2,1)S(1)} %get-tuple-element.68.refs_1_.refs_2_, ...), custom_call_target="tpu_custom_call" | custom-call | tf_op jit(solution)/shard_map/block_gradients/pallas_call | solution.py:39
  25.1 2.0 %collective-permute-start.7 = (bf16[384,128]{1,0:T(8,128)(2,1)S(1)}, bf16[384,128]{1,0:T(8,128)(2,1)S(1)}, u32[]{:S(2)}, u32[]{:S(2)}) collective-permute-start(bf16[384,128]{1,0:T(8,128)(2,1)S(1)} %get-tuple-element.81), channel_id=1, source_target_pairs={{0,1},{1,0},{2,3},{3,2},{4,5},{5,4},{6,7},{7,6},{8,9},{9,8},{10,11... | collective-permute-start | bytes 294920 | tf_op jit(solution)/shard_map/ppermute | solution.py:557
  27.2 2.8 %block_gradients.4 = (bf16[384,128]{1,0:T(8,128)(2,1)S(1)}, bf16[400,128]{1,0:T(8,128)(2,1)S(1)}, bf16[384,3072]{1,0:T(8,128)(2,1)S(1)}) custom-call(f32[8,128]{1,0:T(8,128)S(1)} %get-tuple-element.67.refs_0_, f32[8,3072]{1,0:T(8,128)S(1)} %next_stats.5.refs_1_.refs_0_, bf16[384,1024]{1,0:T(8,128)(2,1)S(1)} %get-tuple-element.68.refs_1_.refs_2_, ...), custom_call_target="tpu_custom_call" | custom-call | tf_op jit(solution)/shard_map/block_gradients/pallas_call | solution.py:39
  30.0 1.8 %collective-permute-start.10 = (bf16[400,128]{1,0:T(8,128)(2,1)S(1)}, bf16[400,128]{1,0:T(8,128)(2,1)S(1)}, u32[]{:S(2)}, u32[]{:S(2)}) collective-permute-start(bf16[400,128]{1,0:T(8,128)(2,1)S(1)} %merge.2.refs_6_), channel_id=1, source_target_pairs={{0,2},{1,3},{2,0},{3,1},{4,6},{5,7},{6,4},{7,5},{8,10},{9,11},{10,... | collective-permute-start | bytes 307208 | tf_op jit(solution)/shard_map/ppermute | solution.py:557
  31.8 3.0 %block_gradients.5 = (bf16[384,128]{1,0:T(8,128)(2,1)S(1)}, bf16[400,128]{1,0:T(8,128)(2,1)S(1)}, bf16[384,3072]{1,0:T(8,128)(2,1)S(1)}) custom-call(f32[8,128]{1,0:T(8,128)S(1)} %get-tuple-element.67.refs_0_, f32[8,3072]{1,0:T(8,128)S(1)} %next_stats.5.refs_1_.refs_0_, bf16[384,1024]{1,0:T(8,128)(2,1)S(1)} %get-tuple-element.68.refs_1_.refs_2_, ...), custom_call_target="tpu_custom_call" | custom-call | tf_op jit(solution)/shard_map/block_gradients/pallas_call | solution.py:39
  34.8 2.0 %collective-permute-start.9 = (bf16[384,128]{1,0:T(8,128)(2,1)S(1)}, bf16[384,128]{1,0:T(8,128)(2,1)S(1)}, u32[]{:S(2)}, u32[]{:S(2)}) collective-permute-start(bf16[384,128]{1,0:T(8,128)(2,1)S(1)} %get-tuple-element.82), channel_id=1, source_target_pairs={{0,1},{1,0},{2,3},{3,2},{4,5},{5,4},{6,7},{7,6},{8,9},{9,8},{10,11... | collective-permute-start | bytes 294920 | tf_op jit(solution)/shard_map/ppermute | solution.py:557
  36.9 1.3 %collective-permute-start.8 = (bf16[384,128]{1,0:T(8,128)(2,1)S(1)}, bf16[384,128]{1,0:T(8,128)(2,1)S(1)}, u32[]{:S(2)}, u32[]{:S(2)}) collective-permute-start(bf16[384,128]{1,0:T(8,128)(2,1)S(1)} %merge.3), channel_id=1, source_target_pairs={{0,2},{1,3},{2,0},{3,1},{4,6},{5,7},{6,4},{7,5},{8,10},{9,11},{10,... | collective-permute-start | bytes 294920 | tf_op jit(solution)/shard_map/ppermute | solution.py:557
  38.2 2.6 %own_gradients.1 = (f32[384,256]{1,0:T(8,128)S(1)}, bf16[384,3072]{1,0:T(8,128)(2,1)S(1)}) custom-call(f32[8,3072]{1,0:T(8,128)S(1)} %next_stats.5.refs_1_.refs_0_, bf16[384,1024]{1,0:T(8,128)(2,1)S(1)} %get-tuple-element.68.refs_1_.refs_2_, bf16[384,1024]{1,0:T(8,128)(2,1)S(1)} %get-tuple-element.69.refs_2_.refs_3_, ...), custom_call_target="tpu_custom_call" | custom-call | tf_op jit(solution)/shard_map/own_gradients/pallas_call | solution.py:39
  40.9 1.5 %send_tiles.2 = (bf16[4128,128]{1,0:T(8,128)(2,1)S(1)}, f32[16,128]{1,0:T(8,128)S(1)}, bf16[384,128]{1,0:T(8,128)(2,1)S(1)}, bf16[384,128]{1,0:T(8,128)(2,1)}) custom-call(s32[1]{0:T(128)} %bitcast.2.refs_0_, f32[384,256]{1,0:T(8,128)S(1)} %get-tuple-element.79.refs_1_, bf16[400,128]{1,0:T(8,128)(2,1)S(1)} %collective-permute-done.10.refs_2_, ...), custom_call_target="tpu_custom_call" | custom-call | tf_op jit(solution)/shard_map/send_tiles/pallas_call | solution.py:39
  43.5 1.6 %kept_tiles.3 = (f32[4,1024,128]{2,1,0:T(8,128)S(1)}, f32[16,128]{1,0:T(8,128)S(1)}, bf16[384,128]{1,0:T(8,128)(2,1)S(1)}, bf16[384,128]{1,0:T(8,128)(2,1)}) custom-call(s32[1]{0:T(128)} %bitcast.2.refs_0_, f32[384,256]{1,0:T(8,128)S(1)} %get-tuple-element.79.refs_1_, bf16[384,128]{1,0:T(8,128)(2,1)S(1)} %collective-permute-done.8.refs_2_, ...), custom_call_target="tpu_custom_call" | custom-call | tf_op jit(solution)/shard_map/kept_tiles/pallas_call | solution.py:39
  45.1 1.2 %send_tiles.3 = (bf16[4112,128]{1,0:T(8,128)(2,1)S(1)}, f32[16,128]{1,0:T(8,128)S(1)}) custom-call(s32[1]{0:T(128)} %bitcast.2.refs_0_, bf16[384,128]{1,0:T(8,128)(2,1)S(1)} %get-tuple-element.87.refs_1_, f32[16,128]{1,0:T(8,128)S(1)} %get-tuple-element.88.refs_2_, bf16[8,4,256,384]{3,2,1,0:T(8,128)(2,1)S(1)} %bitcast.9, f32[8,4,256,256]{3,2,1,0:T(8,128)S(1)} %bitcast.15), custom_call_target="tpu_custom_call" | custom-call | tf_op jit(solution)/shard_map/send_tiles/pallas_call | solution.py:39
  48.0 2.0 %collective-permute-start.21 = (bf16[1024,128]{1,0:T(8,128)(2,1)S(1)}, bf16[1024,128]{1,0:T(8,128)(2,1)S(1)}, u32[]{:S(2)}, u32[]{:S(2)}) collective-permute-start(bf16[1024,128]{1,0:T(8,128)(2,1)S(1)} %get-tuple-element.114), channel_id=1, source_target_pairs={{0,16},{4,20},{8,24},{12,28},{16,0},{20,4},{24,8},{28,12},{1,17},{... | collective-permute-start | bytes 786440 | tf_op jit(solution)/shard_map/ppermute | solution.py:554
  50.9 1.6 %collective-permute-start.14 = (bf16[1024,128]{1,0:T(8,128)(2,1)S(1)}, bf16[1024,128]{1,0:T(8,128)(2,1)S(1)}, u32[]{:S(2)}, u32[]{:S(2)}) collective-permute-start(bf16[1024,128]{1,0:T(8,128)(2,1)S(1)} %get-tuple-element.97), channel_id=1, source_target_pairs={{0,16},{4,20},{8,24},{12,28},{16,0},{20,4},{24,8},{28,12},{1,17},{... | collective-permute-start | bytes 786440 | tf_op jit(solution)/shard_map/ppermute | solution.py:554
  52.5 3.8 %query_gradients.1 = (bf16[384,1024]{1,0:T(8,128)(2,1)}, f32[8,128]{1,0:T(8,128)S(1)}) custom-call(bf16[384,128]{1,0:T(8,128)(2,1)S(1)} %get-tuple-element.66.refs_3_.refs_0_, bf16[384,128]{1,0:T(8,128)(2,1)S(1)} %collective-permute-done.refs_3_.refs_4_.refs_1_, bf16[384,128]{1,0:T(8,128)(2,1)S(1)} %collective-permute-done.1.refs_6_.refs_3_.refs_4_.refs_2_, ...), custom_call_target="tpu_custom_call" | custom-call | flops 1207959552 | bytes 6291456 | tf_op jit(solution)/shard_map/query_gradients/pallas_call | solution.py:39
  57.3 2.1 %collective-permute-start.22 = (bf16[544,128]{1,0:T(8,128)(2,1)S(1)}, bf16[544,128]{1,0:T(8,128)(2,1)S(1)}, u32[]{:S(2)}, u32[]{:S(2)}) collective-permute-start(bf16[544,128]{1,0:T(8,128)(2,1)S(1)} %get-tuple-element.117), channel_id=1, source_target_pairs={{0,16},{4,20},{8,24},{12,28},{16,0},{20,4},{24,8},{28,12},{1,17},{... | collective-permute-start | bytes 417800 | tf_op jit(solution)/shard_map/ppermute | solution.py:554
  59.6 3.2 %collective-permute-done.14.refs_3_ = bf16[1024,128]{1,0:T(8,128)(2,1)S(1)} collective-permute-done((bf16[1024,128]{1,0:T(8,128)(2,1)S(1)}, bf16[1024,128]{1,0:T(8,128)(2,1)S(1)}, u32[]{:S(2)}, u32[]{:S(2)}) %collective-permute-start.14) | collective-permute-done | bytes 262176 | tf_op jit(solution)/shard_map/ppermute | solution.py:554
  63.0 2.1 %collective-permute-start.15 = (bf16[528,128]{1,0:T(8,128)(2,1)S(1)}, bf16[528,128]{1,0:T(8,128)(2,1)S(1)}, u32[]{:S(2)}, u32[]{:S(2)}) collective-permute-start(bf16[528,128]{1,0:T(8,128)(2,1)S(1)} %get-tuple-element.100), channel_id=1, source_target_pairs={{0,16},{4,20},{8,24},{12,28},{16,0},{20,4},{24,8},{28,12},{1,17},{... | collective-permute-start | bytes 405512 | tf_op jit(solution)/shard_map/ppermute | solution.py:554
  66.4 3.7 %collective-permute-done.16.refs_4_ = bf16[512,128]{1,0:T(8,128)(2,1)S(1)} collective-permute-done((bf16[512,128]{1,0:T(8,128)(2,1)S(1)}, bf16[512,128]{1,0:T(8,128)(2,1)S(1)}, u32[]{:S(2)}, u32[]{:S(2)}) %collective-permute-start.16) | collective-permute-done | bytes 131104 | tf_op jit(solution)/shard_map/ppermute | solution.py:554
  70.6 1.5 %collective-permute-done.24.refs_1_ = bf16[544,128]{1,0:T(8,128)(2,1)S(1)} collective-permute-done((bf16[544,128]{1,0:T(8,128)(2,1)S(1)}, bf16[544,128]{1,0:T(8,128)(2,1)S(1)}, u32[]{:S(2)}, u32[]{:S(2)}) %collective-permute-start.24) | collective-permute-done | bytes 139296 | tf_op jit(solution)/shard_map/ppermute | solution.py:557
  72.1 2.8 %collective-permute-start.25 = (bf16[288,128]{1,0:T(8,128)(2,1)S(1)}, bf16[288,128]{1,0:T(8,128)(2,1)S(1)}, u32[]{:S(2)}, u32[]{:S(2)}) collective-permute-start(bf16[288,128]{1,0:T(8,128)(2,1)S(1)} %get-tuple-element.123), channel_id=1, source_target_pairs={{0,2},{1,3},{2,0},{3,1},{4,6},{5,7},{6,4},{7,5},{8,10},{9,11},{10,... | collective-permute-start | bytes 221192 | tf_op jit(solution)/shard_map/ppermute | solution.py:557
  75.5 2.6 %collective-permute-start.18 = (bf16[272,128]{1,0:T(8,128)(2,1)S(1)}, bf16[272,128]{1,0:T(8,128)(2,1)S(1)}, u32[]{:S(2)}, u32[]{:S(2)}) collective-permute-start(bf16[272,128]{1,0:T(8,128)(2,1)S(1)} %get-tuple-element.108), channel_id=1, source_target_pairs={{0,2},{1,3},{2,0},{3,1},{4,6},{5,7},{6,4},{7,5},{8,10},{9,11},{10,... | collective-permute-start | bytes 208904 | tf_op jit(solution)/shard_map/ppermute | solution.py:557
  78.0 3.1 %collective-permute-done.18.refs_3_ = bf16[272,128]{1,0:T(8,128)(2,1)S(1)} collective-permute-done((bf16[272,128]{1,0:T(8,128)(2,1)S(1)}, bf16[272,128]{1,0:T(8,128)(2,1)S(1)}, u32[]{:S(2)}, u32[]{:S(2)}) %collective-permute-start.18) | collective-permute-done | bytes 69664 | tf_op jit(solution)/shard_map/ppermute | solution.py:557
  (63 shorter events, 9.8 us)
Async XLA Ops:
  0.6 12.1 %collective-permute-start.1 = (bf16[384,128]{1,0:T(8,128)(2,1)}, bf16[384,128]{1,0:T(8,128)(2,1)S(1)}, u32[]{:S(2)}, u32[]{:S(2)}) collective-permute-start(bf16[384,128]{1,0:T(8,128)(2,1)} %refs_4_.1), channel_id=1, source_target_pairs={{0,2},{1,3},{2,0},{3,1},{4,6},{5,7},{6,4},{7,5},{8,10},{9,11},{10,... | collective-permute-start | bytes 294920 | tf_op jit(solution)/shard_map/ppermute | solution.py:557
  4.7 11.0 %collective-permute-start = (bf16[384,128]{1,0:T(8,128)(2,1)}, bf16[384,128]{1,0:T(8,128)(2,1)S(1)}, u32[]{:S(2)}, u32[]{:S(2)}) collective-permute-start(bf16[384,128]{1,0:T(8,128)(2,1)} %refs_4_.1), channel_id=1, source_target_pairs={{0,1},{1,0},{2,3},{3,2},{4,5},{5,4},{6,7},{7,6},{8,9},{9,8},{10,11... | collective-permute-start | bytes 294920 | tf_op jit(solution)/shard_map/ppermute | solution.py:557
  6.3 9.4 %collective-permute-start.5 = (bf16[384,128]{1,0:T(8,128)(2,1)}, bf16[384,128]{1,0:T(8,128)(2,1)S(1)}, u32[]{:S(2)}, u32[]{:S(2)}) collective-permute-start(bf16[384,128]{1,0:T(8,128)(2,1)} %refs_5_.1), channel_id=1, source_target_pairs={{0,1},{1,0},{2,3},{3,2},{4,5},{5,4},{6,7},{7,6},{8,9},{9,8},{10,11... | collective-permute-start | bytes 294920 | tf_op jit(solution)/shard_map/ppermute | solution.py:557
  6.8 7.8 %collective-permute-start.3 = (bf16[384,128]{1,0:T(8,128)(2,1)}, bf16[384,128]{1,0:T(8,128)(2,1)S(1)}, u32[]{:S(2)}, u32[]{:S(2)}) collective-permute-start(bf16[384,128]{1,0:T(8,128)(2,1)} %refs_5_.1), channel_id=1, source_target_pairs={{0,2},{1,3},{2,0},{3,1},{4,6},{5,7},{6,4},{7,5},{8,10},{9,11},{10,... | collective-permute-start | bytes 294920 | tf_op jit(solution)/shard_map/ppermute | solution.py:557
  6.8 1.4 %copy-start.3 = (bf16[384,128]{1,0:T(8,128)(2,1)S(1)}, bf16[384,128]{1,0:T(8,128)(2,1)}, u32[]{:S(2)}) copy-start(bf16[384,128]{1,0:T(8,128)(2,1)} %refs_4_.1) | copy-start | bytes 294916
  6.8 1.4 %copy-start.4 = (bf16[384,128]{1,0:T(8,128)(2,1)S(1)}, bf16[384,128]{1,0:T(8,128)(2,1)}, u32[]{:S(2)}) copy-start(bf16[384,128]{1,0:T(8,128)(2,1)} %refs_5_.1) | copy-start | bytes 294916
  6.9 1.4 %copy-start.5 = (s32[1,4]{1,0:T(1,128)S(1)}, s32[1,4]{1,0:T(1,128)}, u32[]{:S(2)}) copy-start(s32[1,4]{1,0:T(1,128)} %param.7) | copy-start | bytes 52
  8.2 2.8 %copy-start = (bf16[384,8192]{1,0:T(8,128)(2,1)S(1)}, bf16[384,8192]{1,0:T(8,128)(2,1)}, u32[]{:S(2)}) copy-start(bf16[384,8192]{1,0:T(8,128)(2,1)} %refs_0_.1) | copy-start | bytes 18874372
  12.7 7.2 %collective-permute-start.2 = (bf16[384,128]{1,0:T(8,128)(2,1)S(1)}, bf16[384,128]{1,0:T(8,128)(2,1)S(1)}, u32[]{:S(2)}, u32[]{:S(2)}) collective-permute-start(bf16[384,128]{1,0:T(8,128)(2,1)S(1)} %collective-permute-done.1.refs_6_.refs_3_.refs_4_.refs_2_), channel_id=1, source_target_pairs={{0,1},{1,0},{2,3},{3,2},{4,5},{5,4},{6,7},{7,6},{8,9},{9,8},{10,11... | collective-permute-start | bytes 294920 | tf_op jit(solution)/shard_map/ppermute | solution.py:557
  14.6 5.3 %collective-permute-start.4 = (bf16[384,128]{1,0:T(8,128)(2,1)S(1)}, bf16[384,128]{1,0:T(8,128)(2,1)S(1)}, u32[]{:S(2)}, u32[]{:S(2)}) collective-permute-start(bf16[384,128]{1,0:T(8,128)(2,1)S(1)} %collective-permute-done.3.refs_7_.refs_4_.refs_5_), channel_id=1, source_target_pairs={{0,1},{1,0},{2,3},{3,2},{4,5},{5,4},{6,7},{7,6},{8,9},{9,8},{10,11... | collective-permute-start | bytes 294920 | tf_op jit(solution)/shard_map/ppermute | solution.py:557
  17.8 23.0 %slice-start = ((s8[8388608]{0:T(1024)(128)(4,1)}), s8[4194304]{0:T(1024)(128)(4,1)S(1)}, s32[]{:S(2)}) async-start(s8[8388608]{0:T(1024)(128)(4,1)} %bitcast.10), calls=%async_computation | async-start | bytes 8388608
  19.9 20.9 %slice-start.1 = ((s8[8388608]{0:T(1024)(128)(4,1)}), s8[4194304]{0:T(1024)(128)(4,1)S(1)}, s32[]{:S(2)}) async-start(s8[8388608]{0:T(1024)(128)(4,1)} %bitcast.10), calls=%async_computation.1 | async-start | bytes 8388608
  25.1 4.9 %collective-permute-start.6 = (bf16[400,128]{1,0:T(8,128)(2,1)S(1)}, bf16[400,128]{1,0:T(8,128)(2,1)S(1)}, u32[]{:S(2)}, u32[]{:S(2)}) collective-permute-start(bf16[400,128]{1,0:T(8,128)(2,1)S(1)} %get-tuple-element.72.refs_6_), channel_id=1, source_target_pairs={{0,1},{1,0},{2,3},{3,2},{4,5},{5,4},{6,7},{7,6},{8,9},{9,8},{10,11... | collective-permute-start | bytes 307208 | tf_op jit(solution)/shard_map/ppermute | solution.py:557
  25.1 11.7 %collective-permute-start.7 = (bf16[384,128]{1,0:T(8,128)(2,1)S(1)}, bf16[384,128]{1,0:T(8,128)(2,1)S(1)}, u32[]{:S(2)}, u32[]{:S(2)}) collective-permute-start(bf16[384,128]{1,0:T(8,128)(2,1)S(1)} %get-tuple-element.81), channel_id=1, source_target_pairs={{0,1},{1,0},{2,3},{3,2},{4,5},{5,4},{6,7},{7,6},{8,9},{9,8},{10,11... | collective-permute-start | bytes 294920 | tf_op jit(solution)/shard_map/ppermute | solution.py:557
  30.0 10.8 %collective-permute-start.10 = (bf16[400,128]{1,0:T(8,128)(2,1)S(1)}, bf16[400,128]{1,0:T(8,128)(2,1)S(1)}, u32[]{:S(2)}, u32[]{:S(2)}) collective-permute-start(bf16[400,128]{1,0:T(8,128)(2,1)S(1)} %merge.2.refs_6_), channel_id=1, source_target_pairs={{0,2},{1,3},{2,0},{3,1},{4,6},{5,7},{6,4},{7,5},{8,10},{9,11},{10,... | collective-permute-start | bytes 307208 | tf_op jit(solution)/shard_map/ppermute | solution.py:557
  34.8 6.1 %collective-permute-start.11 = (bf16[400,128]{1,0:T(8,128)(2,1)S(1)}, bf16[400,128]{1,0:T(8,128)(2,1)S(1)}, u32[]{:S(2)}, u32[]{:S(2)}) collective-permute-start(bf16[400,128]{1,0:T(8,128)(2,1)S(1)} %get-tuple-element.74.refs_5_.refs_2_), channel_id=1, source_target_pairs={{0,1},{1,0},{2,3},{3,2},{4,5},{5,4},{6,7},{7,6},{8,9},{9,8},{10,11... | collective-permute-start | bytes 307208 | tf_op jit(solution)/shard_map/ppermute | solution.py:557
  34.8 8.6 %collective-permute-start.9 = (bf16[384,128]{1,0:T(8,128)(2,1)S(1)}, bf16[384,128]{1,0:T(8,128)(2,1)S(1)}, u32[]{:S(2)}, u32[]{:S(2)}) collective-permute-start(bf16[384,128]{1,0:T(8,128)(2,1)S(1)} %get-tuple-element.82), channel_id=1, source_target_pairs={{0,1},{1,0},{2,3},{3,2},{4,5},{5,4},{6,7},{7,6},{8,9},{9,8},{10,11... | collective-permute-start | bytes 294920 | tf_op jit(solution)/shard_map/ppermute | solution.py:557
  36.9 6.6 %collective-permute-start.8 = (bf16[384,128]{1,0:T(8,128)(2,1)S(1)}, bf16[384,128]{1,0:T(8,128)(2,1)S(1)}, u32[]{:S(2)}, u32[]{:S(2)}) collective-permute-start(bf16[384,128]{1,0:T(8,128)(2,1)S(1)} %merge.3), channel_id=1, source_target_pairs={{0,2},{1,3},{2,0},{3,1},{4,6},{5,7},{6,4},{7,5},{8,10},{9,11},{10,... | collective-permute-start | bytes 294920 | tf_op jit(solution)/shard_map/ppermute | solution.py:557
  42.4 4.4 %collective-permute-start.19 = (bf16[4128,128]{1,0:T(8,128)(2,1)S(1)}, bf16[4128,128]{1,0:T(8,128)(2,1)S(1)}, u32[]{:S(2)}, u32[]{:S(2)}) collective-permute-start(bf16[4128,128]{1,0:T(8,128)(2,1)S(1)} %get-tuple-element.110), channel_id=1, source_target_pairs={{0,4},{4,0},{8,12},{12,8},{16,20},{20,16},{24,28},{28,24},{1,5},{5... | collective-permute-start | bytes 3170312 | tf_op jit(solution)/shard_map/ppermute | solution.py:554
  46.3 3.7 %collective-permute-start.12 = (bf16[4112,128]{1,0:T(8,128)(2,1)S(1)}, bf16[4112,128]{1,0:T(8,128)(2,1)S(1)}, u32[]{:S(2)}, u32[]{:S(2)}) collective-permute-start(bf16[4112,128]{1,0:T(8,128)(2,1)S(1)} %get-tuple-element.89), channel_id=1, source_target_pairs={{0,4},{4,0},{8,12},{12,8},{16,20},{20,16},{24,28},{28,24},{1,5},{5... | collective-permute-start | bytes 3158024 | tf_op jit(solution)/shard_map/ppermute | solution.py:554
  46.9 10.2 %collective-permute-start.20 = (bf16[1056,128]{1,0:T(8,128)(2,1)S(1)}, bf16[1056,128]{1,0:T(8,128)(2,1)S(1)}, u32[]{:S(2)}, u32[]{:S(2)}) collective-permute-start(bf16[1056,128]{1,0:T(8,128)(2,1)S(1)} %get-tuple-element.112), channel_id=1, source_target_pairs={{0,8},{4,12},{8,0},{12,4},{16,24},{20,28},{24,16},{28,20},{1,9},{5... | collective-permute-start | bytes 811016 | tf_op jit(solution)/shard_map/ppermute | solution.py:554
  48.0 9.1 %collective-permute-start.21 = (bf16[1024,128]{1,0:T(8,128)(2,1)S(1)}, bf16[1024,128]{1,0:T(8,128)(2,1)S(1)}, u32[]{:S(2)}, u32[]{:S(2)}) collective-permute-start(bf16[1024,128]{1,0:T(8,128)(2,1)S(1)} %get-tuple-element.114), channel_id=1, source_target_pairs={{0,16},{4,20},{8,24},{12,28},{16,0},{20,4},{24,8},{28,12},{1,17},{... | collective-permute-start | bytes 786440 | tf_op jit(solution)/shard_map/ppermute | solution.py:554
  50.4 12.4 %collective-permute-start.13 = (bf16[1040,128]{1,0:T(8,128)(2,1)S(1)}, bf16[1040,128]{1,0:T(8,128)(2,1)S(1)}, u32[]{:S(2)}, u32[]{:S(2)}) collective-permute-start(bf16[1040,128]{1,0:T(8,128)(2,1)S(1)} %get-tuple-element.95), channel_id=1, source_target_pairs={{0,8},{4,12},{8,0},{12,4},{16,24},{20,28},{24,16},{28,20},{1,9},{5... | collective-permute-start | bytes 798728 | tf_op jit(solution)/shard_map/ppermute | solution.py:554
  50.9 11.9 %collective-permute-start.14 = (bf16[1024,128]{1,0:T(8,128)(2,1)S(1)}, bf16[1024,128]{1,0:T(8,128)(2,1)S(1)}, u32[]{:S(2)}, u32[]{:S(2)}) collective-permute-start(bf16[1024,128]{1,0:T(8,128)(2,1)S(1)} %get-tuple-element.97), channel_id=1, source_target_pairs={{0,16},{4,20},{8,24},{12,28},{16,0},{20,4},{24,8},{28,12},{1,17},{... | collective-permute-start | bytes 786440 | tf_op jit(solution)/shard_map/ppermute | solution.py:554
  57.3 8.4 %collective-permute-start.22 = (bf16[544,128]{1,0:T(8,128)(2,1)S(1)}, bf16[544,128]{1,0:T(8,128)(2,1)S(1)}, u32[]{:S(2)}, u32[]{:S(2)}) collective-permute-start(bf16[544,128]{1,0:T(8,128)(2,1)S(1)} %get-tuple-element.117), channel_id=1, source_target_pairs={{0,16},{4,20},{8,24},{12,28},{16,0},{20,4},{24,8},{28,12},{1,17},{... | collective-permute-start | bytes 417800 | tf_op jit(solution)/shard_map/ppermute | solution.py:554
  59.4 6.0 %collective-permute-start.23 = (bf16[512,128]{1,0:T(8,128)(2,1)S(1)}, bf16[512,128]{1,0:T(8,128)(2,1)S(1)}, u32[]{:S(2)}, u32[]{:S(2)}) collective-permute-start(bf16[512,128]{1,0:T(8,128)(2,1)S(1)} %get-tuple-element.119), channel_id=1, source_target_pairs={{0,8},{4,12},{8,0},{12,4},{16,24},{20,28},{24,16},{28,20},{1,9},{5... | collective-permute-start | bytes 393224 | tf_op jit(solution)/shard_map/ppermute | solution.py:554
  63.0 7.1 %collective-permute-start.15 = (bf16[528,128]{1,0:T(8,128)(2,1)S(1)}, bf16[528,128]{1,0:T(8,128)(2,1)S(1)}, u32[]{:S(2)}, u32[]{:S(2)}) collective-permute-start(bf16[528,128]{1,0:T(8,128)(2,1)S(1)} %get-tuple-element.100), channel_id=1, source_target_pairs={{0,16},{4,20},{8,24},{12,28},{16,0},{20,4},{24,8},{28,12},{1,17},{... | collective-permute-start | bytes 405512 | tf_op jit(solution)/shard_map/ppermute | solution.py:554
  65.1 5.0 %collective-permute-start.16 = (bf16[512,128]{1,0:T(8,128)(2,1)S(1)}, bf16[512,128]{1,0:T(8,128)(2,1)S(1)}, u32[]{:S(2)}, u32[]{:S(2)}) collective-permute-start(bf16[512,128]{1,0:T(8,128)(2,1)S(1)} %get-tuple-element.102), channel_id=1, source_target_pairs={{0,8},{4,12},{8,0},{12,4},{16,24},{20,28},{24,16},{28,20},{1,9},{5... | collective-permute-start | bytes 393224 | tf_op jit(solution)/shard_map/ppermute | solution.py:554
  65.7 6.3 %collective-permute-start.24 = (bf16[544,128]{1,0:T(8,128)(2,1)S(1)}, bf16[544,128]{1,0:T(8,128)(2,1)S(1)}, u32[]{:S(2)}, u32[]{:S(2)}) collective-permute-start(bf16[544,128]{1,0:T(8,128)(2,1)S(1)} %get-tuple-element.121), channel_id=1, source_target_pairs={{0,1},{1,0},{2,3},{3,2},{4,5},{5,4},{6,7},{7,6},{8,9},{9,8},{10,11... | collective-permute-start | bytes 417800 | tf_op jit(solution)/shard_map/ppermute | solution.py:557
  70.3 5.1 %collective-permute-start.17 = (bf16[528,128]{1,0:T(8,128)(2,1)S(1)}, bf16[528,128]{1,0:T(8,128)(2,1)S(1)}, u32[]{:S(2)}, u32[]{:S(2)}) collective-permute-start(bf16[528,128]{1,0:T(8,128)(2,1)S(1)} %get-tuple-element.105), channel_id=1, source_target_pairs={{0,1},{1,0},{2,3},{3,2},{4,5},{5,4},{6,7},{7,6},{8,9},{9,8},{10,11... | collective-permute-start | bytes 405512 | tf_op jit(solution)/shard_map/ppermute | solution.py:557
  72.1 9.1 %collective-permute-start.25 = (bf16[288,128]{1,0:T(8,128)(2,1)S(1)}, bf16[288,128]{1,0:T(8,128)(2,1)S(1)}, u32[]{:S(2)}, u32[]{:S(2)}) collective-permute-start(bf16[288,128]{1,0:T(8,128)(2,1)S(1)} %get-tuple-element.123), channel_id=1, source_target_pairs={{0,2},{1,3},{2,0},{3,1},{4,6},{5,7},{6,4},{7,5},{8,10},{9,11},{10,... | collective-permute-start | bytes 221192 | tf_op jit(solution)/shard_map/ppermute | solution.py:557
  75.5 5.7 %collective-permute-start.18 = (bf16[272,128]{1,0:T(8,128)(2,1)S(1)}, bf16[272,128]{1,0:T(8,128)(2,1)S(1)}, u32[]{:S(2)}, u32[]{:S(2)}) collective-permute-start(bf16[272,128]{1,0:T(8,128)(2,1)S(1)} %get-tuple-element.108), channel_id=1, source_target_pairs={{0,2},{1,3},{2,0},{3,1},{4,6},{5,7},{6,4},{7,5},{8,10},{9,11},{10,... | collective-permute-start | bytes 208904 | tf_op jit(solution)/shard_map/ppermute | solution.py:557
  (2 other events, 2.5 us)

commit v15 on v14

--- a/solution.py
+++ b/solution.py
@@ -99,7 +99,7 @@
     return jnp.max(jnp.where(lane == b, flags[...], 0.0)) > 0.5
 
 
-def stats_of_block(b, q_ref, do_ref, k_ref, v_ref, before, out):
+def stats_of_block(b, q_ref, do_ref, k_ref, v_ref, before, out, held=None):
     k, v = k_ref[...], v_ref[...]
     rows, hd = k.shape
     pair = 2 * rows
@@ -111,6 +111,9 @@
             part = slice(t * CHUNK, (t + 1) * CHUNK)
             lanes = pl.ds(pl.multiple_of(i * pair + t * CHUNK, CHUNK), CHUNK)
             s, dp = score_chunk(k, v, q[part], do[part], b == 0, t * CHUNK)
+            if held:
+                held[0][:, lanes] = s
+                held[1][:, lanes] = dp
             top = jnp.max(s, axis=0, keepdims=True) * factor
             e = jnp.exp2(s * factor - top)
             total = jnp.sum(e, axis=0, keepdims=True)
@@ -156,7 +159,7 @@
         out[...] = before[...]
 
 
-def block_gradients(own, stats, q_ref, do_ref, k_ref, v_ref, p_buf, ds_ref, dk, dv):
+def block_gradients(own, stats, q_ref, do_ref, k_ref, v_ref, p_buf, ds_ref, dk, dv, held=None):
     k, v = k_ref[...], v_ref[...]
     rows, hd = k.shape
     pair = 2 * rows
@@ -169,7 +172,10 @@
         for t in range(pair // CHUNK):
             part = slice(t * CHUNK, (t + 1) * CHUNK)
             lanes = pl.ds(pl.multiple_of(i * pair + t * CHUNK, CHUNK), CHUNK)
-            s, dp = score_chunk(k, v, q[part], do[part], own, t * CHUNK)
+            if held:
+                s, dp = held[0][:, lanes], held[1][:, lanes]
+            else:
+                s, dp = score_chunk(k, v, q[part], do[part], own, t * CHUNK)
             total = stats[1:2, lanes]
             level = stats[0:1, lanes] + jnp.log(total) * LOG2E
             p = jnp.exp2(s * factor - level)
@@ -186,19 +192,27 @@
     return dk[...] * inverse, dv[...]
 
 
-def other_kernel(b, flags, stats, q_ref, do_ref, k_ref, v_ref, dk_out, dv_out, ds_out, p_buf, dk, dv):
+def other_kernel(b, flags, stats, q_ref, do_ref, k_ref, v_ref, dk_out, dv_out, ds_out, *refs):
+    *refs, p_buf, dk, dv = refs
     keep = counted(b, flags)
     rows = dk.shape[0]
+    held, before = None, stats
+    if refs:
+        stats, *held = refs
 
     @pl.when(keep)
     def _():
-        dk_sum, dv_sum = block_gradients(False, stats, q_ref, do_ref, k_ref, v_ref, p_buf, ds_out, dk, dv)
+        if held:
+            stats_of_block(b, q_ref, do_ref, k_ref, v_ref, before, stats, held)
+        dk_sum, dv_sum = block_gradients(False, stats, q_ref, do_ref, k_ref, v_ref, p_buf, ds_out, dk, dv, held)
         dk_out[...] = dk_sum.astype(BF16)
         dv_out[:rows, :] = dv_sum.astype(BF16)
         dv_out[rows:, :] = jnp.zeros((dv_out.shape[0] - rows, dv.shape[1]), BF16)
 
     @pl.when(jnp.logical_not(keep))
     def _():
+        if held:
+            stats[...] = before[...]
         dk_out[...] = jnp.zeros_like(dk_out)
         dv_out[...] = jnp.zeros_like(dv_out)
         ds_out[...] = jnp.zeros_like(ds_out)
@@ -262,6 +276,8 @@
     for b in range(1, n):
         if b not in blocks:
             blocks[b] = [swap(x, b & -b) for x in blocks[b & (b - 1)]]
+        if b == n - 1:
+            break
         stats = whole_call(
             functools.partial(next_stats_kernel, b),
             "next_stats",
@@ -278,17 +294,21 @@
     key_parts, value_parts = [[] for _ in range(n)], [[] for _ in range(n)]
     score_grads, own_parts, before = [None] * n, {}, []
     for b in range(n - 1, 0, -1):
-        dk, dv, score_grads[b] = whole_call(
+        last = b == n - 1
+        held = pltpu.VMEM((rows, tall), F32)
+        dk, dv, score_grads[b], *total = whole_call(
             functools.partial(other_kernel, b),
             "block_gradients",
             [],
             [flags, stats, queries, out_grad, *blocks[b]],
-            [shape((rows, hd)), shape((rows + TOP_ROWS, hd)), shape((rows, tall))],
-            10,
+            [shape((rows, hd)), shape((rows + TOP_ROWS, hd)), shape((rows, tall))] + [stats_shape] * last,
+            20 if last else 10,
             (0, 0),
-            [p_buf, *sums],
+            [held, held] * last + [p_buf, *sums],
             before,
         )
+        if last:
+            stats = total[0]
         if value_parts[b]:
             dv = merge(rows, [dv, *value_parts[b]], [])
         value_parts[b & (b - 1)].append(swap(dv, b & -b))

time: 82.2 us -> 81.3 us (0.989)
  waiting for transfers between devices: 13.3 us -> 17.7 us
  Pallas kernels: 33.2 us -> 29.2 us
  starting transfers between devices: 33 us -> 31.6 us
    ppermute x10, starting transfers between devices: 10.2 us -> 6.07 us  [swap_dp(): return lax.ppermute(x, 'dp', xor_perm(n_dp, mask))]
    pallas_call x26 -> x25, Pallas kernels: 33.2 us -> 29.2 us  [whole_call(): pl.pallas_call(body, grid_spec=pltpu.PrefetchScalarGridSpec(num_scalar_pr...]
    ppermute x16, starting transfers between devices: 22.7 us -> 25.6 us  [swap_ctx(): return lax.ppermute(x, 'context', xor_perm(n_ctx, mask))]
    ppermute x16, waiting for transfers between devices: 5.12 us -> 7.84 us  [swap_ctx(): return lax.ppermute(x, 'context', xor_perm(n_ctx, mask))]
    ppermute x10, waiting for transfers between devices: 8.15 us -> 9.86 us  [swap_dp(): return lax.ppermute(x, 'dp', xor_perm(n_dp, mask))]
  transfers between devices with their start and end apart: 26 -> 26, of which waited for: 7 -> 12; matrix products, arithmetic and copies ran while one was open for 0% -> 0% of each run, Pallas kernels for 33% -> 29%
where the time goes in v15:
time: 81.3 us; the launch traced here: 81.1 us
  starting transfers between devices  31.6 us (39%)
  Pallas kernels  29.2 us (36%)
  waiting for transfers between devices  17.7 us (22%)
  local copies, waits for them, and re-layouts  1.72 us (2%)
  between operations  0.82 us (1%)
    pallas_call x25, Pallas kernels, whole_call(): pl.pallas_call(body, grid_spec=pltpu.PrefetchScalarGridSpec(num_scalar_pr...  29.2 us
    ppermute x16, starting transfers between devices, swap_ctx(): return lax.ppermute(x, 'context', xor_perm(n_ctx, mask))  25.6 us
    ppermute x10, waiting for transfers between devices, swap_dp(): return lax.ppermute(x, 'dp', xor_perm(n_dp, mask))  9.86 us
    ppermute x16, waiting for transfers between devices, swap_ctx(): return lax.ppermute(x, 'context', xor_perm(n_ctx, mask))  7.84 us
    ppermute x10, starting transfers between devices, swap_dp(): return lax.ppermute(x, 'dp', xor_perm(n_dp, mask))  6.07 us
    unnamed x16, local copies, waits for them, and re-layouts  1.72 us
  transfers between devices with their start and end apart: 26, of which 12 were waited for; matrix products, arithmetic and copies ran while one was open for 0% of the time, Pallas kernels for 29%

profile of v15, /device:TPU:0, one launch (start us, length us, event | category | flops | bytes accessed | tf_op | source)
XLA Modules:
  0.0 81.1 jit_solution(14986113530661895479)
XLA Ops:
  0.6 4.1 %collective-permute-start.1 = (bf16[384,128]{1,0:T(8,128)(2,1)}, bf16[384,128]{1,0:T(8,128)(2,1)S(1)}, u32[]{:S(2)}, u32[]{:S(2)}) collective-permute-start(bf16[384,128]{1,0:T(8,128)(2,1)} %refs_4_.1), channel_id=1, source_target_pairs={{0,2},{1,3},{2,0},{3,1},{4,6},{5,7},{6,4},{7,5},{8,10},{9,11},{10,... | collective-permute-start | bytes 294920 | tf_op jit(solution)/shard_map/ppermute | solution.py:577
  4.7 1.6 %collective-permute-start = (bf16[384,128]{1,0:T(8,128)(2,1)}, bf16[384,128]{1,0:T(8,128)(2,1)S(1)}, u32[]{:S(2)}, u32[]{:S(2)}) collective-permute-start(bf16[384,128]{1,0:T(8,128)(2,1)} %refs_4_.1), channel_id=1, source_target_pairs={{0,1},{1,0},{2,3},{3,2},{4,5},{5,4},{6,7},{7,6},{8,9},{9,8},{10,11... | collective-permute-start | bytes 294920 | tf_op jit(solution)/shard_map/ppermute | solution.py:577
  6.9 1.1 %copy-done.1 = bf16[384,1024]{1,0:T(8,128)(2,1)S(1)} copy-done((bf16[384,1024]{1,0:T(8,128)(2,1)S(1)}, bf16[384,1024]{1,0:T(8,128)(2,1)}, u32[]{:S(2)}) %copy-start.1) | copy-done | bytes 786456
  8.2 2.4 %first_stats.1 = (f32[8,3072]{1,0:T(8,128)S(1)}, bf16[384,1024]{1,0:T(8,128)(2,1)S(1)}, bf16[384,1024]{1,0:T(8,128)(2,1)S(1)}, bf16[384,128]{1,0:T(8,128)(2,1)S(...) custom-call(s32[1]{0:T(128)} %bitcast.refs_1_.refs_0_, s32[4]{0:T(128)S(1)} %bitcast.16, ...), custom_call_target="tpu_custom_call" | custom-call | flops 2415919104 | bytes 3145728 | tf_op jit(solution)/shard_map/first_stats/pallas_call | solution.py:39
  11.0 1.7 %prepare.1.refs_8_ = bf16[8192,384]{1,0:T(8,128)(2,1)S(1)} custom-call(bf16[384,8192]{1,0:T(8,128)(2,1)S(1)} %copy-done, f32[8,3072]{1,0:T(8,128)S(1)} %get-tuple-element.71.refs_1_.refs_5_), custom_call_target="tpu_custom_call" | custom-call | tf_op jit(solution)/shard_map/prepare/pallas_call | solution.py:39
  12.7 1.9 %collective-permute-start.2 = (bf16[384,128]{1,0:T(8,128)(2,1)S(1)}, bf16[384,128]{1,0:T(8,128)(2,1)S(1)}, u32[]{:S(2)}, u32[]{:S(2)}) collective-permute-start(bf16[384,128]{1,0:T(8,128)(2,1)S(1)} %collective-permute-done.1.refs_6_.refs_3_.refs_4_.refs_2_), channel_id=1, source_target_pairs={{0,1},{1,0},{2,3},{3,2},{4,5},{5,4},{6,7},{7,6},{8,9},{9,8},{10,11... | collective-permute-start | bytes 294920 | tf_op jit(solution)/shard_map/ppermute | solution.py:577
  14.6 1.1 %collective-permute-start.5 = (bf16[384,128]{1,0:T(8,128)(2,1)S(1)}, bf16[384,128]{1,0:T(8,128)(2,1)S(1)}, u32[]{:S(2)}, u32[]{:S(2)}) collective-permute-start(bf16[384,128]{1,0:T(8,128)(2,1)S(1)} %collective-permute-done.3.refs_7_.refs_4_.refs_5_), channel_id=1, source_target_pairs={{0,1},{1,0},{2,3},{3,2},{4,5},{5,4},{6,7},{7,6},{8,9},{9,8},{10,11... | collective-permute-start | bytes 294920 | tf_op jit(solution)/shard_map/ppermute | solution.py:577
  15.7 2.2 %next_stats.2.refs_5_ = f32[8,3072]{1,0:T(8,128)S(1)} custom-call(f32[8,128]{1,0:T(8,128)S(1)} %get-tuple-element.68.refs_0_, bf16[384,1024]{1,0:T(8,128)(2,1)S(1)} %get-tuple-element.69.refs_1_.refs_2_, bf16[384,1024]{1,0:T(8,128)(2,1)S(1)} %get-tuple-element.70.refs_2_.refs_3_, bf16[384,128]{1,0:T(8,128)(2,1)S(1)} %collective-permute-done.refs_3_.refs_4_.refs_1_, ...), custom_call_target="tpu_custom_call" | custom-call | flops 2415919104 | bytes 3145728 | tf_op jit(solution)/shard_map/next_stats/pallas_call | solution.py:39
  18.1 1.2 %collective-permute-done.5.refs_5_ = bf16[384,128]{1,0:T(8,128)(2,1)S(1)} collective-permute-done((bf16[384,128]{1,0:T(8,128)(2,1)S(1)}, bf16[384,128]{1,0:T(8,128)(2,1)S(1)}, u32[]{:S(2)}, u32[]{:S(2)}) %collective-permute-start.5) | collective-permute-done | bytes 98336 | tf_op jit(solution)/shard_map/ppermute | solution.py:577
  19.2 5.1 %block_gradients.3 = (bf16[384,128]{1,0:T(8,128)(2,1)S(1)}, bf16[400,128]{1,0:T(8,128)(2,1)S(1)}, bf16[384,3072]{1,0:T(8,128)(2,1)S(1)}, f32[8,3072]{1,0:T(8,128)S(1)}) custom-call(f32[8,128]{1,0:T(8,128)S(1)} %get-tuple-element.68.refs_0_, f32[8,3072]{1,0:T(8,128)S(1)} %next_stats.3.refs_1_, bf16[384,1024]{1,0:T(8,128)(2,1)S(1)} %get-tuple-element.69.refs_1_.refs_2_, ...), custom_call_target="tpu_custom_call" | custom-call | tf_op jit(solution)/shard_map/block_gradients/pallas_call | solution.py:39
  24.4 2.0 %collective-permute-start.7 = (bf16[384,128]{1,0:T(8,128)(2,1)S(1)}, bf16[384,128]{1,0:T(8,128)(2,1)S(1)}, u32[]{:S(2)}, u32[]{:S(2)}) collective-permute-start(bf16[384,128]{1,0:T(8,128)(2,1)S(1)} %get-tuple-element.83), channel_id=1, source_target_pairs={{0,1},{1,0},{2,3},{3,2},{4,5},{5,4},{6,7},{7,6},{8,9},{9,8},{10,11... | collective-permute-start | bytes 294920 | tf_op jit(solution)/shard_map/ppermute | solution.py:577
  26.7 2.3 %collective-permute-done.6.refs_1_ = bf16[400,128]{1,0:T(8,128)(2,1)S(1)} collective-permute-done((bf16[400,128]{1,0:T(8,128)(2,1)S(1)}, bf16[400,128]{1,0:T(8,128)(2,1)S(1)}, u32[]{:S(2)}, u32[]{:S(2)}) %collective-permute-start.6) | collective-permute-done | bytes 102432 | tf_op jit(solution)/shard_map/ppermute | solution.py:577
  29.1 4.0 %collective-permute-start.10 = (bf16[400,128]{1,0:T(8,128)(2,1)S(1)}, bf16[400,128]{1,0:T(8,128)(2,1)S(1)}, u32[]{:S(2)}, u32[]{:S(2)}) collective-permute-start(bf16[400,128]{1,0:T(8,128)(2,1)S(1)} %merge.2.refs_6_), channel_id=1, source_target_pairs={{0,2},{1,3},{2,0},{3,1},{4,6},{5,7},{6,4},{7,5},{8,10},{9,11},{10,... | collective-permute-start | bytes 307208 | tf_op jit(solution)/shard_map/ppermute | solution.py:577
  33.1 3.0 %block_gradients.5 = (bf16[384,128]{1,0:T(8,128)(2,1)S(1)}, bf16[400,128]{1,0:T(8,128)(2,1)S(1)}, bf16[384,3072]{1,0:T(8,128)(2,1)S(1)}) custom-call(f32[8,128]{1,0:T(8,128)S(1)} %get-tuple-element.68.refs_0_, f32[8,3072]{1,0:T(8,128)S(1)} %get-tuple-element.72.refs_1_.refs_0_, bf16[384,1024]{1,0:T(8,128)(2,1)S(1)} %get-tuple-element.69.refs_1_.refs_2_, ...), custom_call_target="tpu_custom_call" | custom-call | tf_op jit(solution)/shard_map/block_gradients/pallas_call | solution.py:39
  36.2 2.0 %collective-permute-start.9 = (bf16[384,128]{1,0:T(8,128)(2,1)S(1)}, bf16[384,128]{1,0:T(8,128)(2,1)S(1)}, u32[]{:S(2)}, u32[]{:S(2)}) collective-permute-start(bf16[384,128]{1,0:T(8,128)(2,1)S(1)} %get-tuple-element.84), channel_id=1, source_target_pairs={{0,1},{1,0},{2,3},{3,2},{4,5},{5,4},{6,7},{7,6},{8,9},{9,8},{10,11... | collective-permute-start | bytes 294920 | tf_op jit(solution)/shard_map/ppermute | solution.py:577
  38.3 2.7 %own_gradients.1 = (f32[384,256]{1,0:T(8,128)S(1)}, bf16[384,3072]{1,0:T(8,128)(2,1)S(1)}) custom-call(f32[8,3072]{1,0:T(8,128)S(1)} %get-tuple-element.72.refs_1_.refs_0_, bf16[384,1024]{1,0:T(8,128)(2,1)S(1)} %get-tuple-element.69.refs_1_.refs_2_, bf16[384,1024]{1,0:T(8,128)(2,1)S(1)} %get-tuple-element.70.refs_2_.refs_3_, ...), custom_call_target="tpu_custom_call" | custom-call | tf_op jit(solution)/shard_map/own_gradients/pallas_call | solution.py:39
  41.3 1.5 %send_tiles.2 = (bf16[4128,128]{1,0:T(8,128)(2,1)S(1)}, f32[16,128]{1,0:T(8,128)S(1)}, bf16[384,128]{1,0:T(8,128)(2,1)S(1)}, bf16[384,128]{1,0:T(8,128)(2,1)}) custom-call(s32[1]{0:T(128)} %bitcast.2.refs_0_, f32[384,256]{1,0:T(8,128)S(1)} %get-tuple-element.81.refs_1_, bf16[400,128]{1,0:T(8,128)(2,1)S(1)} %collective-permute-done.10.refs_2_, ...), custom_call_target="tpu_custom_call" | custom-call | tf_op jit(solution)/shard_map/send_tiles/pallas_call | solution.py:39
  42.8 1.1 %kept_tiles.2 = (f32[4,1024,128]{2,1,0:T(8,128)S(1)}, f32[16,128]{1,0:T(8,128)S(1)}) custom-call(s32[1]{0:T(128)} %bitcast.2.refs_0_, bf16[384,128]{1,0:T(8,128)(2,1)S(1)} %get-tuple-element.85.refs_1_, f32[16,128]{1,0:T(8,128)S(1)} %get-tuple-element.86.refs_2_, bf16[8,4,256,384]{3,2,1,0:T(8,128)(2,1)S(1)} %bitcast.7, f32[8,4,256,256]{3,2,1,0:T(8,128)S(1)} %bitcast.13), custom_call_target="tpu_custom_call" | custom-call | tf_op jit(solution)/shard_map/kept_tiles/pallas_call | solution.py:39
  44.4 1.6 %kept_tiles.3 = (f32[4,1024,128]{2,1,0:T(8,128)S(1)}, f32[16,128]{1,0:T(8,128)S(1)}, bf16[384,128]{1,0:T(8,128)(2,1)S(1)}, bf16[384,128]{1,0:T(8,128)(2,1)}) custom-call(s32[1]{0:T(128)} %bitcast.2.refs_0_, f32[384,256]{1,0:T(8,128)S(1)} %get-tuple-element.81.refs_1_, bf16[384,128]{1,0:T(8,128)(2,1)S(1)} %collective-permute-done.8.refs_2_, ...), custom_call_target="tpu_custom_call" | custom-call | tf_op jit(solution)/shard_map/kept_tiles/pallas_call | solution.py:39
  46.0 1.2 %send_tiles.3 = (bf16[4112,128]{1,0:T(8,128)(2,1)S(1)}, f32[16,128]{1,0:T(8,128)S(1)}) custom-call(s32[1]{0:T(128)} %bitcast.2.refs_0_, bf16[384,128]{1,0:T(8,128)(2,1)S(1)} %get-tuple-element.89.refs_1_, f32[16,128]{1,0:T(8,128)S(1)} %get-tuple-element.90.refs_2_, bf16[8,4,256,384]{3,2,1,0:T(8,128)(2,1)S(1)} %bitcast.9, f32[8,4,256,256]{3,2,1,0:T(8,128)S(1)} %bitcast.15), custom_call_target="tpu_custom_call" | custom-call | tf_op jit(solution)/shard_map/send_tiles/pallas_call | solution.py:39
  47.5 1.2 %collective-permute-start.20 = (bf16[1056,128]{1,0:T(8,128)(2,1)S(1)}, bf16[1056,128]{1,0:T(8,128)(2,1)S(1)}, u32[]{:S(2)}, u32[]{:S(2)}) collective-permute-start(bf16[1056,128]{1,0:T(8,128)(2,1)S(1)} %get-tuple-element.114), channel_id=1, source_target_pairs={{0,8},{4,12},{8,0},{12,4},{16,24},{20,28},{24,16},{28,20},{1,9},{5... | collective-permute-start | bytes 811016 | tf_op jit(solution)/shard_map/ppermute | solution.py:574
  52.1 4.0 %query_gradients.1 = (bf16[384,1024]{1,0:T(8,128)(2,1)}, f32[8,128]{1,0:T(8,128)S(1)}) custom-call(bf16[384,128]{1,0:T(8,128)(2,1)S(1)} %get-tuple-element.67.refs_3_.refs_0_, bf16[384,128]{1,0:T(8,128)(2,1)S(1)} %collective-permute-done.refs_3_.refs_4_.refs_1_, bf16[384,128]{1,0:T(8,128)(2,1)S(1)} %collective-permute-done.1.refs_6_.refs_3_.refs_4_.refs_2_, ...), custom_call_target="tpu_custom_call" | custom-call | flops 1207959552 | bytes 6291456 | tf_op jit(solution)/shard_map/query_gradients/pallas_call | solution.py:39
  56.1 1.8 %collective-permute-done.21.refs_3_ = bf16[1024,128]{1,0:T(8,128)(2,1)S(1)} collective-permute-done((bf16[1024,128]{1,0:T(8,128)(2,1)S(1)}, bf16[1024,128]{1,0:T(8,128)(2,1)S(1)}, u32[]{:S(2)}, u32[]{:S(2)}) %collective-permute-start.21) | collective-permute-done | bytes 262176 | tf_op jit(solution)/shard_map/ppermute | solution.py:574
  58.3 1.1 %collective-permute-start.23 = (bf16[512,128]{1,0:T(8,128)(2,1)S(1)}, bf16[512,128]{1,0:T(8,128)(2,1)S(1)}, u32[]{:S(2)}, u32[]{:S(2)}) collective-permute-start(bf16[512,128]{1,0:T(8,128)(2,1)S(1)} %get-tuple-element.121), channel_id=1, source_target_pairs={{0,8},{4,12},{8,0},{12,4},{16,24},{20,28},{24,16},{28,20},{1,9},{5... | collective-permute-start | bytes 393224 | tf_op jit(solution)/shard_map/ppermute | solution.py:574
  59.4 4.1 %collective-permute-done.14.refs_3_ = bf16[1024,128]{1,0:T(8,128)(2,1)S(1)} collective-permute-done((bf16[1024,128]{1,0:T(8,128)(2,1)S(1)}, bf16[1024,128]{1,0:T(8,128)(2,1)S(1)}, u32[]{:S(2)}, u32[]{:S(2)}) %collective-permute-start.14) | collective-permute-done | bytes 262176 | tf_op jit(solution)/shard_map/ppermute | solution.py:574
  64.1 1.1 %collective-permute-start.16 = (bf16[512,128]{1,0:T(8,128)(2,1)S(1)}, bf16[512,128]{1,0:T(8,128)(2,1)S(1)}, u32[]{:S(2)}, u32[]{:S(2)}) collective-permute-start(bf16[512,128]{1,0:T(8,128)(2,1)S(1)} %get-tuple-element.104), channel_id=1, source_target_pairs={{0,8},{4,12},{8,0},{12,4},{16,24},{20,28},{24,16},{28,20},{1,9},{5... | collective-permute-start | bytes 393224 | tf_op jit(solution)/shard_map/ppermute | solution.py:574
  66.6 2.4 %collective-permute-done.16.refs_4_ = bf16[512,128]{1,0:T(8,128)(2,1)S(1)} collective-permute-done((bf16[512,128]{1,0:T(8,128)(2,1)S(1)}, bf16[512,128]{1,0:T(8,128)(2,1)S(1)}, u32[]{:S(2)}, u32[]{:S(2)}) %collective-permute-start.16) | collective-permute-done | bytes 131104 | tf_op jit(solution)/shard_map/ppermute | solution.py:574
  69.2 2.0 %collective-permute-start.17 = (bf16[528,128]{1,0:T(8,128)(2,1)S(1)}, bf16[528,128]{1,0:T(8,128)(2,1)S(1)}, u32[]{:S(2)}, u32[]{:S(2)}) collective-permute-start(bf16[528,128]{1,0:T(8,128)(2,1)S(1)} %get-tuple-element.107), channel_id=1, source_target_pairs={{0,1},{1,0},{2,3},{3,2},{4,5},{5,4},{6,7},{7,6},{8,9},{9,8},{10,11... | collective-permute-start | bytes 405512 | tf_op jit(solution)/shard_map/ppermute | solution.py:577
  71.2 1.1 %collective-permute-done.24.refs_1_ = bf16[544,128]{1,0:T(8,128)(2,1)S(1)} collective-permute-done((bf16[544,128]{1,0:T(8,128)(2,1)S(1)}, bf16[544,128]{1,0:T(8,128)(2,1)S(1)}, u32[]{:S(2)}, u32[]{:S(2)}) %collective-permute-start.24) | collective-permute-done | bytes 139296 | tf_op jit(solution)/shard_map/ppermute | solution.py:577
  72.3 2.3 %collective-permute-start.25 = (bf16[288,128]{1,0:T(8,128)(2,1)S(1)}, bf16[288,128]{1,0:T(8,128)(2,1)S(1)}, u32[]{:S(2)}, u32[]{:S(2)}) collective-permute-start(bf16[288,128]{1,0:T(8,128)(2,1)S(1)} %get-tuple-element.125), channel_id=1, source_target_pairs={{0,2},{1,3},{2,0},{3,1},{4,6},{5,7},{6,4},{7,5},{8,10},{9,11},{10,... | collective-permute-start | bytes 221192 | tf_op jit(solution)/shard_map/ppermute | solution.py:577
  74.9 3.0 %collective-permute-start.18 = (bf16[272,128]{1,0:T(8,128)(2,1)S(1)}, bf16[272,128]{1,0:T(8,128)(2,1)S(1)}, u32[]{:S(2)}, u32[]{:S(2)}) collective-permute-start(bf16[272,128]{1,0:T(8,128)(2,1)S(1)} %get-tuple-element.110), channel_id=1, source_target_pairs={{0,2},{1,3},{2,0},{3,1},{4,6},{5,7},{6,4},{7,5},{8,10},{9,11},{10,... | collective-permute-start | bytes 208904 | tf_op jit(solution)/shard_map/ppermute | solution.py:577
  77.9 2.3 %collective-permute-done.18.refs_3_ = bf16[272,128]{1,0:T(8,128)(2,1)S(1)} collective-permute-done((bf16[272,128]{1,0:T(8,128)(2,1)S(1)}, bf16[272,128]{1,0:T(8,128)(2,1)S(1)}, u32[]{:S(2)}, u32[]{:S(2)}) %collective-permute-start.18) | collective-permute-done | bytes 69664 | tf_op jit(solution)/shard_map/ppermute | solution.py:577
  (62 shorter events, 10.1 us)
Async XLA Ops:
  0.6 12.1 %collective-permute-start.1 = (bf16[384,128]{1,0:T(8,128)(2,1)}, bf16[384,128]{1,0:T(8,128)(2,1)S(1)}, u32[]{:S(2)}, u32[]{:S(2)}) collective-permute-start(bf16[384,128]{1,0:T(8,128)(2,1)} %refs_4_.1), channel_id=1, source_target_pairs={{0,2},{1,3},{2,0},{3,1},{4,6},{5,7},{6,4},{7,5},{8,10},{9,11},{10,... | collective-permute-start | bytes 294920 | tf_op jit(solution)/shard_map/ppermute | solution.py:577
  4.7 11.0 %collective-permute-start = (bf16[384,128]{1,0:T(8,128)(2,1)}, bf16[384,128]{1,0:T(8,128)(2,1)S(1)}, u32[]{:S(2)}, u32[]{:S(2)}) collective-permute-start(bf16[384,128]{1,0:T(8,128)(2,1)} %refs_4_.1), channel_id=1, source_target_pairs={{0,1},{1,0},{2,3},{3,2},{4,5},{5,4},{6,7},{7,6},{8,9},{9,8},{10,11... | collective-permute-start | bytes 294920 | tf_op jit(solution)/shard_map/ppermute | solution.py:577
  6.3 9.4 %collective-permute-start.4 = (bf16[384,128]{1,0:T(8,128)(2,1)}, bf16[384,128]{1,0:T(8,128)(2,1)S(1)}, u32[]{:S(2)}, u32[]{:S(2)}) collective-permute-start(bf16[384,128]{1,0:T(8,128)(2,1)} %refs_5_.1), channel_id=1, source_target_pairs={{0,1},{1,0},{2,3},{3,2},{4,5},{5,4},{6,7},{7,6},{8,9},{9,8},{10,11... | collective-permute-start | bytes 294920 | tf_op jit(solution)/shard_map/ppermute | solution.py:577
  6.8 7.8 %collective-permute-start.3 = (bf16[384,128]{1,0:T(8,128)(2,1)}, bf16[384,128]{1,0:T(8,128)(2,1)S(1)}, u32[]{:S(2)}, u32[]{:S(2)}) collective-permute-start(bf16[384,128]{1,0:T(8,128)(2,1)} %refs_5_.1), channel_id=1, source_target_pairs={{0,2},{1,3},{2,0},{3,1},{4,6},{5,7},{6,4},{7,5},{8,10},{9,11},{10,... | collective-permute-start | bytes 294920 | tf_op jit(solution)/shard_map/ppermute | solution.py:577
  6.8 1.4 %copy-start.3 = (bf16[384,128]{1,0:T(8,128)(2,1)S(1)}, bf16[384,128]{1,0:T(8,128)(2,1)}, u32[]{:S(2)}) copy-start(bf16[384,128]{1,0:T(8,128)(2,1)} %refs_4_.1) | copy-start | bytes 294916
  6.8 1.4 %copy-start.4 = (bf16[384,128]{1,0:T(8,128)(2,1)S(1)}, bf16[384,128]{1,0:T(8,128)(2,1)}, u32[]{:S(2)}) copy-start(bf16[384,128]{1,0:T(8,128)(2,1)} %refs_5_.1) | copy-start | bytes 294916
  6.9 1.4 %copy-start.5 = (s32[1,4]{1,0:T(1,128)S(1)}, s32[1,4]{1,0:T(1,128)}, u32[]{:S(2)}) copy-start(s32[1,4]{1,0:T(1,128)} %param.7) | copy-start | bytes 52
  8.2 2.8 %copy-start = (bf16[384,8192]{1,0:T(8,128)(2,1)S(1)}, bf16[384,8192]{1,0:T(8,128)(2,1)}, u32[]{:S(2)}) copy-start(bf16[384,8192]{1,0:T(8,128)(2,1)} %refs_0_.1) | copy-start | bytes 18874372
  12.7 5.3 %collective-permute-start.2 = (bf16[384,128]{1,0:T(8,128)(2,1)S(1)}, bf16[384,128]{1,0:T(8,128)(2,1)S(1)}, u32[]{:S(2)}, u32[]{:S(2)}) collective-permute-start(bf16[384,128]{1,0:T(8,128)(2,1)S(1)} %collective-permute-done.1.refs_6_.refs_3_.refs_4_.refs_2_), channel_id=1, source_target_pairs={{0,1},{1,0},{2,3},{3,2},{4,5},{5,4},{6,7},{7,6},{8,9},{9,8},{10,11... | collective-permute-start | bytes 294920 | tf_op jit(solution)/shard_map/ppermute | solution.py:577
  14.6 4.6 %collective-permute-start.5 = (bf16[384,128]{1,0:T(8,128)(2,1)S(1)}, bf16[384,128]{1,0:T(8,128)(2,1)S(1)}, u32[]{:S(2)}, u32[]{:S(2)}) collective-permute-start(bf16[384,128]{1,0:T(8,128)(2,1)S(1)} %collective-permute-done.3.refs_7_.refs_4_.refs_5_), channel_id=1, source_target_pairs={{0,1},{1,0},{2,3},{3,2},{4,5},{5,4},{6,7},{7,6},{8,9},{9,8},{10,11... | collective-permute-start | bytes 294920 | tf_op jit(solution)/shard_map/ppermute | solution.py:577
  15.7 25.6 %slice-start = ((s8[8388608]{0:T(1024)(128)(4,1)}), s8[4194304]{0:T(1024)(128)(4,1)S(1)}, s32[]{:S(2)}) async-start(s8[8388608]{0:T(1024)(128)(4,1)} %bitcast.10), calls=%async_computation | async-start | bytes 8388608
  17.9 23.4 %slice-start.1 = ((s8[8388608]{0:T(1024)(128)(4,1)}), s8[4194304]{0:T(1024)(128)(4,1)S(1)}, s32[]{:S(2)}) async-start(s8[8388608]{0:T(1024)(128)(4,1)} %bitcast.10), calls=%async_computation.1 | async-start | bytes 8388608
  24.3 4.7 %collective-permute-start.6 = (bf16[400,128]{1,0:T(8,128)(2,1)S(1)}, bf16[400,128]{1,0:T(8,128)(2,1)S(1)}, u32[]{:S(2)}, u32[]{:S(2)}) collective-permute-start(bf16[400,128]{1,0:T(8,128)(2,1)S(1)} %get-tuple-element.74.refs_6_), channel_id=1, source_target_pairs={{0,1},{1,0},{2,3},{3,2},{4,5},{5,4},{6,7},{7,6},{8,9},{9,8},{10,11... | collective-permute-start | bytes 307208 | tf_op jit(solution)/shard_map/ppermute | solution.py:577
  24.4 13.8 %collective-permute-start.7 = (bf16[384,128]{1,0:T(8,128)(2,1)S(1)}, bf16[384,128]{1,0:T(8,128)(2,1)S(1)}, u32[]{:S(2)}, u32[]{:S(2)}) collective-permute-start(bf16[384,128]{1,0:T(8,128)(2,1)S(1)} %get-tuple-element.83), channel_id=1, source_target_pairs={{0,1},{1,0},{2,3},{3,2},{4,5},{5,4},{6,7},{7,6},{8,9},{9,8},{10,11... | collective-permute-start | bytes 294920 | tf_op jit(solution)/shard_map/ppermute | solution.py:577
  29.1 11.9 %collective-permute-start.10 = (bf16[400,128]{1,0:T(8,128)(2,1)S(1)}, bf16[400,128]{1,0:T(8,128)(2,1)S(1)}, u32[]{:S(2)}, u32[]{:S(2)}) collective-permute-start(bf16[400,128]{1,0:T(8,128)(2,1)S(1)} %merge.2.refs_6_), channel_id=1, source_target_pairs={{0,2},{1,3},{2,0},{3,1},{4,6},{5,7},{6,4},{7,5},{8,10},{9,11},{10,... | collective-permute-start | bytes 307208 | tf_op jit(solution)/shard_map/ppermute | solution.py:577
  36.1 5.2 %collective-permute-start.11 = (bf16[400,128]{1,0:T(8,128)(2,1)S(1)}, bf16[400,128]{1,0:T(8,128)(2,1)S(1)}, u32[]{:S(2)}, u32[]{:S(2)}) collective-permute-start(bf16[400,128]{1,0:T(8,128)(2,1)S(1)} %get-tuple-element.76.refs_5_.refs_2_), channel_id=1, source_target_pairs={{0,1},{1,0},{2,3},{3,2},{4,5},{5,4},{6,7},{7,6},{8,9},{9,8},{10,11... | collective-permute-start | bytes 307208 | tf_op jit(solution)/shard_map/ppermute | solution.py:577
  36.2 7.7 %collective-permute-start.9 = (bf16[384,128]{1,0:T(8,128)(2,1)S(1)}, bf16[384,128]{1,0:T(8,128)(2,1)S(1)}, u32[]{:S(2)}, u32[]{:S(2)}) collective-permute-start(bf16[384,128]{1,0:T(8,128)(2,1)S(1)} %get-tuple-element.84), channel_id=1, source_target_pairs={{0,1},{1,0},{2,3},{3,2},{4,5},{5,4},{6,7},{7,6},{8,9},{9,8},{10,11... | collective-permute-start | bytes 294920 | tf_op jit(solution)/shard_map/ppermute | solution.py:577
  38.2 6.1 %collective-permute-start.8 = (bf16[384,128]{1,0:T(8,128)(2,1)S(1)}, bf16[384,128]{1,0:T(8,128)(2,1)S(1)}, u32[]{:S(2)}, u32[]{:S(2)}) collective-permute-start(bf16[384,128]{1,0:T(8,128)(2,1)S(1)} %merge.3), channel_id=1, source_target_pairs={{0,2},{1,3},{2,0},{3,1},{4,6},{5,7},{6,4},{7,5},{8,10},{9,11},{10,... | collective-permute-start | bytes 294920 | tf_op jit(solution)/shard_map/ppermute | solution.py:577
  42.8 4.4 %collective-permute-start.19 = (bf16[4128,128]{1,0:T(8,128)(2,1)S(1)}, bf16[4128,128]{1,0:T(8,128)(2,1)S(1)}, u32[]{:S(2)}, u32[]{:S(2)}) collective-permute-start(bf16[4128,128]{1,0:T(8,128)(2,1)S(1)} %get-tuple-element.112), channel_id=1, source_target_pairs={{0,4},{4,0},{8,12},{12,8},{16,20},{20,16},{24,28},{28,24},{1,5},{5... | collective-permute-start | bytes 3170312 | tf_op jit(solution)/shard_map/ppermute | solution.py:574
  47.2 2.7 %collective-permute-start.12 = (bf16[4112,128]{1,0:T(8,128)(2,1)S(1)}, bf16[4112,128]{1,0:T(8,128)(2,1)S(1)}, u32[]{:S(2)}, u32[]{:S(2)}) collective-permute-start(bf16[4112,128]{1,0:T(8,128)(2,1)S(1)} %get-tuple-element.91), channel_id=1, source_target_pairs={{0,4},{4,0},{8,12},{12,8},{16,20},{20,16},{24,28},{28,24},{1,5},{5... | collective-permute-start | bytes 3158024 | tf_op jit(solution)/shard_map/ppermute | solution.py:574
  47.5 10.4 %collective-permute-start.20 = (bf16[1056,128]{1,0:T(8,128)(2,1)S(1)}, bf16[1056,128]{1,0:T(8,128)(2,1)S(1)}, u32[]{:S(2)}, u32[]{:S(2)}) collective-permute-start(bf16[1056,128]{1,0:T(8,128)(2,1)S(1)} %get-tuple-element.114), channel_id=1, source_target_pairs={{0,8},{4,12},{8,0},{12,4},{16,24},{20,28},{24,16},{28,20},{1,9},{5... | collective-permute-start | bytes 811016 | tf_op jit(solution)/shard_map/ppermute | solution.py:574
  48.7 9.2 %collective-permute-start.21 = (bf16[1024,128]{1,0:T(8,128)(2,1)S(1)}, bf16[1024,128]{1,0:T(8,128)(2,1)S(1)}, u32[]{:S(2)}, u32[]{:S(2)}) collective-permute-start(bf16[1024,128]{1,0:T(8,128)(2,1)S(1)} %get-tuple-element.116), channel_id=1, source_target_pairs={{0,16},{4,20},{8,24},{12,28},{16,0},{20,4},{24,8},{28,12},{1,17},{... | collective-permute-start | bytes 786440 | tf_op jit(solution)/shard_map/ppermute | solution.py:574
  50.2 13.3 %collective-permute-start.13 = (bf16[1040,128]{1,0:T(8,128)(2,1)S(1)}, bf16[1040,128]{1,0:T(8,128)(2,1)S(1)}, u32[]{:S(2)}, u32[]{:S(2)}) collective-permute-start(bf16[1040,128]{1,0:T(8,128)(2,1)S(1)} %get-tuple-element.97), channel_id=1, source_target_pairs={{0,8},{4,12},{8,0},{12,4},{16,24},{20,28},{24,16},{28,20},{1,9},{5... | collective-permute-start | bytes 798728 | tf_op jit(solution)/shard_map/ppermute | solution.py:574
  51.1 12.4 %collective-permute-start.14 = (bf16[1024,128]{1,0:T(8,128)(2,1)S(1)}, bf16[1024,128]{1,0:T(8,128)(2,1)S(1)}, u32[]{:S(2)}, u32[]{:S(2)}) collective-permute-start(bf16[1024,128]{1,0:T(8,128)(2,1)S(1)} %get-tuple-element.99), channel_id=1, source_target_pairs={{0,16},{4,20},{8,24},{12,28},{16,0},{20,4},{24,8},{28,12},{1,17},{... | collective-permute-start | bytes 786440 | tf_op jit(solution)/shard_map/ppermute | solution.py:574
  58.1 7.7 %collective-permute-start.22 = (bf16[544,128]{1,0:T(8,128)(2,1)S(1)}, bf16[544,128]{1,0:T(8,128)(2,1)S(1)}, u32[]{:S(2)}, u32[]{:S(2)}) collective-permute-start(bf16[544,128]{1,0:T(8,128)(2,1)S(1)} %get-tuple-element.119), channel_id=1, source_target_pairs={{0,16},{4,20},{8,24},{12,28},{16,0},{20,4},{24,8},{28,12},{1,17},{... | collective-permute-start | bytes 417800 | tf_op jit(solution)/shard_map/ppermute | solution.py:574
  58.3 6.9 %collective-permute-start.23 = (bf16[512,128]{1,0:T(8,128)(2,1)S(1)}, bf16[512,128]{1,0:T(8,128)(2,1)S(1)}, u32[]{:S(2)}, u32[]{:S(2)}) collective-permute-start(bf16[512,128]{1,0:T(8,128)(2,1)S(1)} %get-tuple-element.121), channel_id=1, source_target_pairs={{0,8},{4,12},{8,0},{12,4},{16,24},{20,28},{24,16},{28,20},{1,9},{5... | collective-permute-start | bytes 393224 | tf_op jit(solution)/shard_map/ppermute | solution.py:574
  63.8 5.2 %collective-permute-start.15 = (bf16[528,128]{1,0:T(8,128)(2,1)S(1)}, bf16[528,128]{1,0:T(8,128)(2,1)S(1)}, u32[]{:S(2)}, u32[]{:S(2)}) collective-permute-start(bf16[528,128]{1,0:T(8,128)(2,1)S(1)} %get-tuple-element.102), channel_id=1, source_target_pairs={{0,16},{4,20},{8,24},{12,28},{16,0},{20,4},{24,8},{28,12},{1,17},{... | collective-permute-start | bytes 405512 | tf_op jit(solution)/shard_map/ppermute | solution.py:574
  64.1 5.0 %collective-permute-start.16 = (bf16[512,128]{1,0:T(8,128)(2,1)S(1)}, bf16[512,128]{1,0:T(8,128)(2,1)S(1)}, u32[]{:S(2)}, u32[]{:S(2)}) collective-permute-start(bf16[512,128]{1,0:T(8,128)(2,1)S(1)} %get-tuple-element.104), channel_id=1, source_target_pairs={{0,8},{4,12},{8,0},{12,4},{16,24},{20,28},{24,16},{28,20},{1,9},{5... | collective-permute-start | bytes 393224 | tf_op jit(solution)/shard_map/ppermute | solution.py:574
  65.8 6.5 %collective-permute-start.24 = (bf16[544,128]{1,0:T(8,128)(2,1)S(1)}, bf16[544,128]{1,0:T(8,128)(2,1)S(1)}, u32[]{:S(2)}, u32[]{:S(2)}) collective-permute-start(bf16[544,128]{1,0:T(8,128)(2,1)S(1)} %get-tuple-element.123), channel_id=1, source_target_pairs={{0,1},{1,0},{2,3},{3,2},{4,5},{5,4},{6,7},{7,6},{8,9},{9,8},{10,11... | collective-permute-start | bytes 417800 | tf_op jit(solution)/shard_map/ppermute | solution.py:577
  69.2 5.6 %collective-permute-start.17 = (bf16[528,128]{1,0:T(8,128)(2,1)S(1)}, bf16[528,128]{1,0:T(8,128)(2,1)S(1)}, u32[]{:S(2)}, u32[]{:S(2)}) collective-permute-start(bf16[528,128]{1,0:T(8,128)(2,1)S(1)} %get-tuple-element.107), channel_id=1, source_target_pairs={{0,1},{1,0},{2,3},{3,2},{4,5},{5,4},{6,7},{7,6},{8,9},{9,8},{10,11... | collective-permute-start | bytes 405512 | tf_op jit(solution)/shard_map/ppermute | solution.py:577
  72.3 7.9 %collective-permute-start.25 = (bf16[288,128]{1,0:T(8,128)(2,1)S(1)}, bf16[288,128]{1,0:T(8,128)(2,1)S(1)}, u32[]{:S(2)}, u32[]{:S(2)}) collective-permute-start(bf16[288,128]{1,0:T(8,128)(2,1)S(1)} %get-tuple-element.125), channel_id=1, source_target_pairs={{0,2},{1,3},{2,0},{3,1},{4,6},{5,7},{6,4},{7,5},{8,10},{9,11},{10,... | collective-permute-start | bytes 221192 | tf_op jit(solution)/shard_map/ppermute | solution.py:577
  74.9 5.2 %collective-permute-start.18 = (bf16[272,128]{1,0:T(8,128)(2,1)S(1)}, bf16[272,128]{1,0:T(8,128)(2,1)S(1)}, u32[]{:S(2)}, u32[]{:S(2)}) collective-permute-start(bf16[272,128]{1,0:T(8,128)(2,1)S(1)} %get-tuple-element.110), channel_id=1, source_target_pairs={{0,2},{1,3},{2,0},{3,1},{4,6},{5,7},{6,4},{7,5},{8,10},{9,11},{10,... | collective-permute-start | bytes 208904 | tf_op jit(solution)/shard_map/ppermute | solution.py:577
  (2 other events, 2.5 us)

commit v16 on v15

--- a/solution.py
+++ b/solution.py
@@ -400,49 +400,31 @@
     return total.astype(BF16)
 
 
-def send_rows(bits, shrink, at, me_ref, total, a_ref, e_ref, out_ref, top_ref, packed):
+def kept_rows(bits, shrink, at, me_ref, total, a_ref, e_ref, out_ref, top_ref):
+    for step in range(out_ref.shape[0]):
+        dest = tile_of(step, me_ref[0], bits, 0)
+        out_ref[step] = corrected_tile(at, dest, total, a_ref, e_ref, top_ref) * shrink
+
+
+def send_kernel(bits, shrink, at, n_parts, me_ref, own_ref, *refs):
+    *before, a_ref, e_ref, out_ref, top_ref, grads_ref, grads_out = refs[n_parts:]
+    total = summed_grads(at, own_ref, refs[:n_parts])
+    grads_ref[...] = total
+    grads_out[...] = total
+    top_ref[...] = before[0][...] if before else jnp.zeros_like(top_ref)
+    steps = a_ref.shape[0] // 2
     tall = a_ref.shape[1] * a_ref.shape[2]
-    steps = a_ref.shape[0] // 2
     for step in range(steps):
         dest = tile_of(step, me_ref[0], bits, 1)
         c = corrected_tile(at, dest, total, a_ref, e_ref, top_ref)
         out_ref[step * tall : (step + 1) * tall, :] = (c * shrink).astype(BF16)
-    tail = jnp.zeros((out_ref.shape[0] - steps * tall, out_ref.shape[1]), BF16)
-    out_ref[steps * tall :, :] = pack_top(top_ref[...]) if packed else tail
-
-
-def kept_rows(bits, shrink, at, me_ref, total, a_ref, e_ref, out_ref, top_ref):
-    for step in range(out_ref.shape[0]):
-        dest = tile_of(step, me_ref[0], bits, 0)
-        out_ref[step] = corrected_tile(at, dest, total, a_ref, e_ref, top_ref) * shrink
-
-
-def first_send_kernel(bits, shrink, at, n_parts, me_ref, own_ref, *refs):
-    a_ref, e_ref, out_ref, top_ref, grads_ref, grads_out = refs[n_parts:]
-    total = summed_grads(at, own_ref, refs[:n_parts])
-    grads_ref[...] = total
-    grads_out[...] = total
-    top_ref[...] = jnp.zeros_like(top_ref)
-    send_rows(bits, shrink, at, me_ref, total, a_ref, e_ref, out_ref, top_ref, False)
-
-
-def next_kept_kernel(bits, shrink, at, me_ref, grads_ref, before_ref, a_ref, e_ref, out_ref, top_ref):
+    if out_ref.shape[0] > steps * tall:
+        out_ref[steps * tall :, :] = jnp.zeros((out_ref.shape[0] - steps * tall, out_ref.shape[1]), BF16)
+
+
+def kept_kernel(bits, shrink, at, me_ref, grads_ref, before_ref, a_ref, e_ref, out_ref, top_ref):
     top_ref[...] = before_ref[...]
     kept_rows(bits, shrink, at, me_ref, grads_ref[...], a_ref, e_ref, out_ref, top_ref)
-
-
-def first_kept_kernel(bits, shrink, at, n_parts, me_ref, own_ref, *refs):
-    before_ref, a_ref, e_ref, out_ref, top_ref, grads_ref, grads_out = refs[n_parts:]
-    total = summed_grads(at, own_ref, refs[:n_parts])
-    grads_ref[...] = total
-    grads_out[...] = total
-    top_ref[...] = before_ref[...]
-    kept_rows(bits, shrink, at, me_ref, total, a_ref, e_ref, out_ref, top_ref)
-
-
-def next_send_kernel(bits, shrink, at, me_ref, grads_ref, before_ref, a_ref, e_ref, out_ref, top_ref):
-    top_ref[...] = before_ref[...]
-    send_rows(bits, shrink, at, me_ref, grads_ref[...], a_ref, e_ref, out_ref, top_ref, True)
 
 
 def split_kernel(bits, n_ctx, n_tops, kept, got, *refs):
@@ -466,7 +448,9 @@
         top_out[0][...] = top
         low_away[half * part_tall :, :] = pack_top(top)
     else:
-        low_away[half * part_tall :, :] = jnp.zeros((low_away.shape[0] - half * part_tall, hd), BF16)
+        tail = jnp.zeros((low_away.shape[0] - half * part_tall, hd), BF16)
+        low_away[half * part_tall :, :] = tail
+        high_away[half * part_tall :, :] = tail
 
 
 def largest(tops, low_got, size):
@@ -596,39 +580,47 @@
 
     def split(last, kept, got, top):
         return whole_call(
-            functools.partial(split_kernel, bits, n_ctx, int(last)),
+            functools.partial(split_kernel, bits, n_ctx, len(top)),
             "split_tiles",
             [],
-            [kept, got] + [top] * last,
-            [shape((half + (1 if last else 2) * TOP_ROWS, hd))] + [shape((half, hd))] * 3 + [tops] * last,
+            [kept, got, *top],
+            [
+                shape((half + (1 if last else 2) * TOP_ROWS, hd)),
+                shape((half, hd)),
+                shape((half + (0 if last else 2) * TOP_ROWS, hd)),
+                shape((half, hd)),
+            ]
+            + [tops] * last,
             10,
             cost,
         )
 
     out, top, grads, value_grad = tiles(
-        functools.partial(first_send_kernel, bits, shrink, hd, len(value_parts)),
+        functools.partial(send_kernel, bits, shrink, hd, len(value_parts)),
         "send_tiles",
         [own, *value_parts],
         [shape((steps * tall + 2 * TOP_ROWS, hd)), tops, grad_shape, grad_shape],
     )
     got = swap_dp(out, 1)
     kept, top = tiles(
-        functools.partial(next_kept_kernel, bits, shrink, hd), "kept_tiles", [grads, top], [kept_shape, tops]
-    )
-    halves = [split(False, kept, got, None)]
-    kept, top, grads, key_grad = tiles(
-        functools.partial(first_kept_kernel, bits, shrink, 0, len(key_parts)),
+        functools.partial(kept_kernel, bits, shrink, hd), "kept_tiles", [grads, top], [kept_shape, tops]
+    )
+    out, top, grads, key_grad = tiles(
+        functools.partial(send_kernel, bits, shrink, 0, len(key_parts)),
+        "send_tiles",
+        [own, *key_parts, top],
+        [shape((steps * tall, hd)), tops, grad_shape, grad_shape],
+    )
+    halves = [split(False, kept, got, [])]
+    got = swap_dp(out, 1)
+    kept, top = tiles(
+        functools.partial(kept_kernel, bits, shrink, 0),
         "kept_tiles",
-        [own, *key_parts, top],
-        [kept_shape, tops, grad_shape, grad_shape],
-    )
-    out, top = tiles(
-        functools.partial(next_send_kernel, bits, shrink, 0),
-        "send_tiles",
         [grads, top],
-        [shape((steps * tall + TOP_ROWS, hd)), tops],
-    )
-    arrays = split(True, kept, swap_dp(out, 1), top)
+        [kept_shape, tops],
+        halves[0][1:2],
+    )
+    arrays = split(True, kept, got, [top, swap_dp(top, 1)])
     halves.append(arrays[:4])
     gathered = [arrays[4]]
     query_grad, mark = query_gradients(key_blocks, score_grads, queries.shape[1], [arrays[1]])

time: 81.3 us -> 81.1 us (level)
  Pallas kernels: 29.2 us -> 19.9 us
  starting transfers between devices: 31.6 us -> 40.1 us
    pallas_call x25, Pallas kernels: 29.2 us -> 19.9 us  [whole_call(): pl.pallas_call(body, grid_spec=pltpu.PrefetchScalarGridSpec(num_scalar_pr...]
    ppermute x16, waiting for transfers between devices: 7.84 us -> 13.1 us  [swap_ctx(): return lax.ppermute(x, 'context', xor_perm(n_ctx, mask))]
    ppermute x10 -> x11, starting transfers between devices: 6.07 us -> 11 us  [swap_dp(): return lax.ppermute(x, 'dp', xor_perm(n_dp, mask))]
    ppermute x10 -> x11, waiting for transfers between devices: 9.86 us -> 5.21 us  [swap_dp(): return lax.ppermute(x, 'dp', xor_perm(n_dp, mask))]
    ppermute x16, starting transfers between devices: 25.6 us -> 29.1 us  [swap_ctx(): return lax.ppermute(x, 'context', xor_perm(n_ctx, mask))]
  transfers between devices with their start and end apart: 26 -> 27, of which waited for: 12 -> 9; matrix products, arithmetic and copies ran while one was open for 0% -> 0% of each run, Pallas kernels for 29% -> 23%
where the time goes in v16:
time: 81.1 us; the launch traced here: 81 us
  starting transfers between devices  40.1 us (49%)
  Pallas kernels  19.9 us (25%)
  waiting for transfers between devices  18.4 us (23%)
  local copies, waits for them, and re-layouts  1.72 us (2%)
  between operations  0.85 us (1%)
    ppermute x16, starting transfers between devices, swap_ctx(): return lax.ppermute(x, 'context', xor_perm(n_ctx, mask))  29.1 us
    pallas_call x25, Pallas kernels, whole_call(): pl.pallas_call(body, grid_spec=pltpu.PrefetchScalarGridSpec(num_scalar_pr...  19.9 us
    ppermute x16, waiting for transfers between devices, swap_ctx(): return lax.ppermute(x, 'context', xor_perm(n_ctx, mask))  13.1 us
    ppermute x11, starting transfers between devices, swap_dp(): return lax.ppermute(x, 'dp', xor_perm(n_dp, mask))  11 us
    ppermute x11, waiting for transfers between devices, swap_dp(): return lax.ppermute(x, 'dp', xor_perm(n_dp, mask))  5.21 us
    unnamed x16, local copies, waits for them, and re-layouts  1.72 us
  transfers between devices with their start and end apart: 27, of which 9 were waited for; matrix products, arithmetic and copies ran while one was open for 0% of the time, Pallas kernels for 23%

profile of v16, /device:TPU:0, one launch (start us, length us, event | category | flops | bytes accessed | tf_op | source)
XLA Modules:
  0.0 81.0 jit_solution(6424806547530528652)
XLA Ops:
  0.6 4.1 %collective-permute-start.1 = (bf16[384,128]{1,0:T(8,128)(2,1)}, bf16[384,128]{1,0:T(8,128)(2,1)S(1)}, u32[]{:S(2)}, u32[]{:S(2)}) collective-permute-start(bf16[384,128]{1,0:T(8,128)(2,1)} %refs_4_.1), channel_id=1, source_target_pairs={{0,2},{1,3},{2,0},{3,1},{4,6},{5,7},{6,4},{7,5},{8,10},{9,11},{10,... | collective-permute-start | bytes 294920 | tf_op jit(solution)/shard_map/ppermute | solution.py:561
  4.7 1.6 %collective-permute-start = (bf16[384,128]{1,0:T(8,128)(2,1)}, bf16[384,128]{1,0:T(8,128)(2,1)S(1)}, u32[]{:S(2)}, u32[]{:S(2)}) collective-permute-start(bf16[384,128]{1,0:T(8,128)(2,1)} %refs_4_.1), channel_id=1, source_target_pairs={{0,1},{1,0},{2,3},{3,2},{4,5},{5,4},{6,7},{7,6},{8,9},{9,8},{10,11... | collective-permute-start | bytes 294920 | tf_op jit(solution)/shard_map/ppermute | solution.py:561
  6.9 1.1 %copy-done.1 = bf16[384,1024]{1,0:T(8,128)(2,1)S(1)} copy-done((bf16[384,1024]{1,0:T(8,128)(2,1)S(1)}, bf16[384,1024]{1,0:T(8,128)(2,1)}, u32[]{:S(2)}) %copy-start.1) | copy-done | bytes 786456
  8.2 2.4 %first_stats.1 = (f32[8,3072]{1,0:T(8,128)S(1)}, bf16[384,1024]{1,0:T(8,128)(2,1)S(1)}, bf16[384,1024]{1,0:T(8,128)(2,1)S(1)}, bf16[384,128]{1,0:T(8,128)(2,1)S(...) custom-call(s32[1]{0:T(128)} %bitcast.refs_1_.refs_0_, s32[4]{0:T(128)S(1)} %bitcast.16, ...), custom_call_target="tpu_custom_call" | custom-call | flops 2415919104 | bytes 3145728 | tf_op jit(solution)/shard_map/first_stats/pallas_call | solution.py:39
  11.0 1.7 %prepare.1.refs_8_ = bf16[8192,384]{1,0:T(8,128)(2,1)S(1)} custom-call(bf16[384,8192]{1,0:T(8,128)(2,1)S(1)} %copy-done, f32[8,3072]{1,0:T(8,128)S(1)} %get-tuple-element.71.refs_1_.refs_5_), custom_call_target="tpu_custom_call" | custom-call | tf_op jit(solution)/shard_map/prepare/pallas_call | solution.py:39
  12.7 1.9 %collective-permute-start.2 = (bf16[384,128]{1,0:T(8,128)(2,1)S(1)}, bf16[384,128]{1,0:T(8,128)(2,1)S(1)}, u32[]{:S(2)}, u32[]{:S(2)}) collective-permute-start(bf16[384,128]{1,0:T(8,128)(2,1)S(1)} %collective-permute-done.1.refs_6_.refs_3_.refs_4_.refs_2_), channel_id=1, source_target_pairs={{0,1},{1,0},{2,3},{3,2},{4,5},{5,4},{6,7},{7,6},{8,9},{9,8},{10,11... | collective-permute-start | bytes 294920 | tf_op jit(solution)/shard_map/ppermute | solution.py:561
  14.6 1.1 %collective-permute-start.5 = (bf16[384,128]{1,0:T(8,128)(2,1)S(1)}, bf16[384,128]{1,0:T(8,128)(2,1)S(1)}, u32[]{:S(2)}, u32[]{:S(2)}) collective-permute-start(bf16[384,128]{1,0:T(8,128)(2,1)S(1)} %collective-permute-done.3.refs_7_.refs_4_.refs_5_), channel_id=1, source_target_pairs={{0,1},{1,0},{2,3},{3,2},{4,5},{5,4},{6,7},{7,6},{8,9},{9,8},{10,11... | collective-permute-start | bytes 294920 | tf_op jit(solution)/shard_map/ppermute | solution.py:561
  16.0 1.7 %collective-permute-done.2.refs_4_.refs_3_ = bf16[384,128]{1,0:T(8,128)(2,1)S(1)} collective-permute-done((bf16[384,128]{1,0:T(8,128)(2,1)S(1)}, bf16[384,128]{1,0:T(8,128)(2,1)S(1)}, u32[]{:S(2)}, u32[]{:S(2)}) %collective-permute-start.2) | collective-permute-done | bytes 98336 | tf_op jit(solution)/shard_map/ppermute | solution.py:561
  17.8 1.5 %collective-permute-done.5.refs_5_ = bf16[384,128]{1,0:T(8,128)(2,1)S(1)} collective-permute-done((bf16[384,128]{1,0:T(8,128)(2,1)S(1)}, bf16[384,128]{1,0:T(8,128)(2,1)S(1)}, u32[]{:S(2)}, u32[]{:S(2)}) %collective-permute-start.5) | collective-permute-done | bytes 98336 | tf_op jit(solution)/shard_map/ppermute | solution.py:561
  19.7 1.8 %collective-permute-start.6 = (bf16[400,128]{1,0:T(8,128)(2,1)S(1)}, bf16[400,128]{1,0:T(8,128)(2,1)S(1)}, u32[]{:S(2)}, u32[]{:S(2)}) collective-permute-start(bf16[400,128]{1,0:T(8,128)(2,1)S(1)} %get-tuple-element.74.refs_6_), channel_id=1, source_target_pairs={{0,1},{1,0},{2,3},{3,2},{4,5},{5,4},{6,7},{7,6},{8,9},{9,8},{10,11... | collective-permute-start | bytes 307208 | tf_op jit(solution)/shard_map/ppermute | solution.py:561
  22.1 2.3 %collective-permute-done.6.refs_1_ = bf16[400,128]{1,0:T(8,128)(2,1)S(1)} collective-permute-done((bf16[400,128]{1,0:T(8,128)(2,1)S(1)}, bf16[400,128]{1,0:T(8,128)(2,1)S(1)}, u32[]{:S(2)}, u32[]{:S(2)}) %collective-permute-start.6) | collective-permute-done | bytes 102432 | tf_op jit(solution)/shard_map/ppermute | solution.py:561
  24.5 7.8 %collective-permute-start.10 = (bf16[400,128]{1,0:T(8,128)(2,1)S(1)}, bf16[400,128]{1,0:T(8,128)(2,1)S(1)}, u32[]{:S(2)}, u32[]{:S(2)}) collective-permute-start(bf16[400,128]{1,0:T(8,128)(2,1)S(1)} %merge.2.refs_6_), channel_id=1, source_target_pairs={{0,2},{1,3},{2,0},{3,1},{4,6},{5,7},{6,4},{7,5},{8,10},{9,11},{10,... | collective-permute-start | bytes 307208 | tf_op jit(solution)/shard_map/ppermute | solution.py:561
  32.8 3.0 %collective-permute-start.11 = (bf16[400,128]{1,0:T(8,128)(2,1)S(1)}, bf16[400,128]{1,0:T(8,128)(2,1)S(1)}, u32[]{:S(2)}, u32[]{:S(2)}) collective-permute-start(bf16[400,128]{1,0:T(8,128)(2,1)S(1)} %get-tuple-element.76.refs_5_.refs_2_), channel_id=1, source_target_pairs={{0,1},{1,0},{2,3},{3,2},{4,5},{5,4},{6,7},{7,6},{8,9},{9,8},{10,11... | collective-permute-start | bytes 307208 | tf_op jit(solution)/shard_map/ppermute | solution.py:561
  35.9 1.6 %collective-permute-start.8 = (bf16[384,128]{1,0:T(8,128)(2,1)S(1)}, bf16[384,128]{1,0:T(8,128)(2,1)S(1)}, u32[]{:S(2)}, u32[]{:S(2)}) collective-permute-start(bf16[384,128]{1,0:T(8,128)(2,1)S(1)} %merge.3), channel_id=1, source_target_pairs={{0,2},{1,3},{2,0},{3,1},{4,6},{5,7},{6,4},{7,5},{8,10},{9,11},{10,... | collective-permute-start | bytes 294920 | tf_op jit(solution)/shard_map/ppermute | solution.py:561
  37.5 2.7 %own_gradients.1 = (f32[384,256]{1,0:T(8,128)S(1)}, bf16[384,3072]{1,0:T(8,128)(2,1)S(1)}) custom-call(f32[8,3072]{1,0:T(8,128)S(1)} %get-tuple-element.72.refs_1_.refs_0_, bf16[384,1024]{1,0:T(8,128)(2,1)S(1)} %get-tuple-element.69.refs_1_.refs_2_, bf16[384,1024]{1,0:T(8,128)(2,1)S(1)} %get-tuple-element.70.refs_2_.refs_3_, ...), custom_call_target="tpu_custom_call" | custom-call | tf_op jit(solution)/shard_map/own_gradients/pallas_call | solution.py:39
  40.2 1.5 %send_tiles.2 = (bf16[4128,128]{1,0:T(8,128)(2,1)S(1)}, f32[16,128]{1,0:T(8,128)S(1)}, bf16[384,128]{1,0:T(8,128)(2,1)S(1)}, bf16[384,128]{1,0:T(8,128)(2,1)}) custom-call(s32[1]{0:T(128)} %bitcast.2.refs_0_, f32[384,256]{1,0:T(8,128)S(1)} %get-tuple-element.81.refs_1_, bf16[400,128]{1,0:T(8,128)(2,1)S(1)} %collective-permute-done.10.refs_2_, ...), custom_call_target="tpu_custom_call" | custom-call | tf_op jit(solution)/shard_map/send_tiles/pallas_call | solution.py:39
  41.8 1.1 %kept_tiles.2 = (f32[4,1024,128]{2,1,0:T(8,128)S(1)}, f32[16,128]{1,0:T(8,128)S(1)}) custom-call(s32[1]{0:T(128)} %bitcast.2.refs_0_, bf16[384,128]{1,0:T(8,128)(2,1)S(1)} %get-tuple-element.85.refs_1_, f32[16,128]{1,0:T(8,128)S(1)} %get-tuple-element.86.refs_2_, bf16[8,4,256,384]{3,2,1,0:T(8,128)(2,1)S(1)} %bitcast.7, f32[8,4,256,256]{3,2,1,0:T(8,128)S(1)} %bitcast.13), custom_call_target="tpu_custom_call" | custom-call | tf_op jit(solution)/shard_map/kept_tiles/pallas_call | solution.py:39
  42.9 1.5 %send_tiles.3 = (bf16[4096,128]{1,0:T(8,128)(2,1)S(1)}, f32[16,128]{1,0:T(8,128)S(1)}, bf16[384,128]{1,0:T(8,128)(2,1)S(1)}, bf16[384,128]{1,0:T(8,128)(2,1)}) custom-call(s32[1]{0:T(128)} %bitcast.2.refs_0_, f32[384,256]{1,0:T(8,128)S(1)} %get-tuple-element.81.refs_1_, bf16[384,128]{1,0:T(8,128)(2,1)S(1)} %collective-permute-done.8.refs_2_, ...), custom_call_target="tpu_custom_call" | custom-call | tf_op jit(solution)/shard_map/send_tiles/pallas_call | solution.py:39
  45.2 1.3 %collective-permute-start.21 = (bf16[1056,128]{1,0:T(8,128)(2,1)S(1)}, bf16[1056,128]{1,0:T(8,128)(2,1)S(1)}, u32[]{:S(2)}, u32[]{:S(2)}) collective-permute-start(bf16[1056,128]{1,0:T(8,128)(2,1)S(1)} %get-tuple-element.114), channel_id=1, source_target_pairs={{0,8},{4,12},{8,0},{12,4},{16,24},{20,28},{24,16},{28,20},{1,9},{5... | collective-permute-start | bytes 811016 | tf_op jit(solution)/shard_map/ppermute | solution.py:558
  46.5 1.9 %collective-permute-start.22 = (bf16[1056,128]{1,0:T(8,128)(2,1)S(1)}, bf16[1056,128]{1,0:T(8,128)(2,1)S(1)}, u32[]{:S(2)}, u32[]{:S(2)}) collective-permute-start(bf16[1056,128]{1,0:T(8,128)(2,1)S(1)} %get-tuple-element.116), channel_id=1, source_target_pairs={{0,16},{4,20},{8,24},{12,28},{16,0},{20,4},{24,8},{28,12},{1,17},{... | collective-permute-start | bytes 811016 | tf_op jit(solution)/shard_map/ppermute | solution.py:558
  48.4 1.1 %kept_tiles.3 = (f32[4,1024,128]{2,1,0:T(8,128)S(1)}, f32[16,128]{1,0:T(8,128)S(1)}) custom-call(s32[1]{0:T(128)} %bitcast.2.refs_0_, bf16[384,128]{1,0:T(8,128)(2,1)S(1)} %get-tuple-element.88.refs_1_, f32[16,128]{1,0:T(8,128)S(1)} %get-tuple-element.89.refs_2_, bf16[8,4,256,384]{3,2,1,0:T(8,128)(2,1)S(1)} %bitcast.9, f32[8,4,256,256]{3,2,1,0:T(8,128)S(1)} %bitcast.15, ...), custom_call_target="tpu_custom_call" | custom-call | tf_op jit(solution)/shard_map/kept_tiles/pallas_call | solution.py:39
  49.5 1.1 %collective-permute-done.14.refs_3_ = f32[16,128]{1,0:T(8,128)S(1)} collective-permute-done((f32[16,128]{1,0:T(8,128)S(1)}, f32[16,128]{1,0:T(8,128)S(1)}, u32[]{:S(2)}, u32[]{:S(2)}) %collective-permute-start.14) | collective-permute-done | bytes 8224 | tf_op jit(solution)/shard_map/ppermute | solution.py:558
  52.1 4.0 %query_gradients.1 = (bf16[384,1024]{1,0:T(8,128)(2,1)}, f32[8,128]{1,0:T(8,128)S(1)}) custom-call(bf16[384,128]{1,0:T(8,128)(2,1)S(1)} %get-tuple-element.67.refs_3_.refs_0_, bf16[384,128]{1,0:T(8,128)(2,1)S(1)} %collective-permute-done.refs_3_.refs_4_.refs_1_, bf16[384,128]{1,0:T(8,128)(2,1)S(1)} %collective-permute-done.1.refs_6_.refs_3_.refs_4_.refs_2_, ...), custom_call_target="tpu_custom_call" | custom-call | flops 1207959552 | bytes 6291456 | tf_op jit(solution)/shard_map/query_gradients/pallas_call | solution.py:39
  56.2 2.1 %collective-permute-start.23 = (bf16[544,128]{1,0:T(8,128)(2,1)S(1)}, bf16[544,128]{1,0:T(8,128)(2,1)S(1)}, u32[]{:S(2)}, u32[]{:S(2)}) collective-permute-start(bf16[544,128]{1,0:T(8,128)(2,1)S(1)} %get-tuple-element.119), channel_id=1, source_target_pairs={{0,16},{4,20},{8,24},{12,28},{16,0},{20,4},{24,8},{28,12},{1,17},{... | collective-permute-start | bytes 417800 | tf_op jit(solution)/shard_map/ppermute | solution.py:558
  59.3 1.9 %collective-permute-done.16.refs_3_ = bf16[1024,128]{1,0:T(8,128)(2,1)S(1)} collective-permute-done((bf16[1024,128]{1,0:T(8,128)(2,1)S(1)}, bf16[1024,128]{1,0:T(8,128)(2,1)S(1)}, u32[]{:S(2)}, u32[]{:S(2)}) %collective-permute-start.16) | collective-permute-done | bytes 262176 | tf_op jit(solution)/shard_map/ppermute | solution.py:558
  61.5 2.2 %collective-permute-start.17 = (bf16[528,128]{1,0:T(8,128)(2,1)S(1)}, bf16[528,128]{1,0:T(8,128)(2,1)S(1)}, u32[]{:S(2)}, u32[]{:S(2)}) collective-permute-start(bf16[528,128]{1,0:T(8,128)(2,1)S(1)} %get-tuple-element.105), channel_id=1, source_target_pairs={{0,16},{4,20},{8,24},{12,28},{16,0},{20,4},{24,8},{28,12},{1,17},{... | collective-permute-start | bytes 405512 | tf_op jit(solution)/shard_map/ppermute | solution.py:558
  64.7 1.9 %collective-permute-start.25 = (bf16[544,128]{1,0:T(8,128)(2,1)S(1)}, bf16[544,128]{1,0:T(8,128)(2,1)S(1)}, u32[]{:S(2)}, u32[]{:S(2)}) collective-permute-start(bf16[544,128]{1,0:T(8,128)(2,1)S(1)} %get-tuple-element.123), channel_id=1, source_target_pairs={{0,1},{1,0},{2,3},{3,2},{4,5},{5,4},{6,7},{7,6},{8,9},{9,8},{10,11... | collective-permute-start | bytes 417800 | tf_op jit(solution)/shard_map/ppermute | solution.py:561
  66.6 2.1 %collective-permute-done.18.refs_4_ = bf16[512,128]{1,0:T(8,128)(2,1)S(1)} collective-permute-done((bf16[512,128]{1,0:T(8,128)(2,1)S(1)}, bf16[512,128]{1,0:T(8,128)(2,1)S(1)}, u32[]{:S(2)}, u32[]{:S(2)}) %collective-permute-start.18) | collective-permute-done | bytes 131104 | tf_op jit(solution)/shard_map/ppermute | solution.py:558
  69.6 2.2 %collective-permute-done.25.refs_1_ = bf16[544,128]{1,0:T(8,128)(2,1)S(1)} collective-permute-done((bf16[544,128]{1,0:T(8,128)(2,1)S(1)}, bf16[544,128]{1,0:T(8,128)(2,1)S(1)}, u32[]{:S(2)}, u32[]{:S(2)}) %collective-permute-start.25) | collective-permute-done | bytes 139296 | tf_op jit(solution)/shard_map/ppermute | solution.py:561
  71.8 1.5 %collective-permute-start.26 = (bf16[288,128]{1,0:T(8,128)(2,1)S(1)}, bf16[288,128]{1,0:T(8,128)(2,1)S(1)}, u32[]{:S(2)}, u32[]{:S(2)}) collective-permute-start(bf16[288,128]{1,0:T(8,128)(2,1)S(1)} %get-tuple-element.125), channel_id=1, source_target_pairs={{0,2},{1,3},{2,0},{3,1},{4,6},{5,7},{6,4},{7,5},{8,10},{9,11},{10,... | collective-permute-start | bytes 221192 | tf_op jit(solution)/shard_map/ppermute | solution.py:561
  74.1 1.2 %collective-permute-start.20 = (bf16[272,128]{1,0:T(8,128)(2,1)S(1)}, bf16[272,128]{1,0:T(8,128)(2,1)S(1)}, u32[]{:S(2)}, u32[]{:S(2)}) collective-permute-start(bf16[272,128]{1,0:T(8,128)(2,1)S(1)} %get-tuple-element.113), channel_id=1, source_target_pairs={{0,2},{1,3},{2,0},{3,1},{4,6},{5,7},{6,4},{7,5},{8,10},{9,11},{10,... | collective-permute-start | bytes 208904 | tf_op jit(solution)/shard_map/ppermute | solution.py:561
  75.2 4.8 %collective-permute-done.20.refs_3_ = bf16[272,128]{1,0:T(8,128)(2,1)S(1)} collective-permute-done((bf16[272,128]{1,0:T(8,128)(2,1)S(1)}, bf16[272,128]{1,0:T(8,128)(2,1)S(1)}, u32[]{:S(2)}, u32[]{:S(2)}) %collective-permute-start.20) | collective-permute-done | bytes 69664 | tf_op jit(solution)/shard_map/ppermute | solution.py:561
  (64 shorter events, 10.3 us)
Async XLA Ops:
  0.6 12.1 %collective-permute-start.1 = (bf16[384,128]{1,0:T(8,128)(2,1)}, bf16[384,128]{1,0:T(8,128)(2,1)S(1)}, u32[]{:S(2)}, u32[]{:S(2)}) collective-permute-start(bf16[384,128]{1,0:T(8,128)(2,1)} %refs_4_.1), channel_id=1, source_target_pairs={{0,2},{1,3},{2,0},{3,1},{4,6},{5,7},{6,4},{7,5},{8,10},{9,11},{10,... | collective-permute-start | bytes 294920 | tf_op jit(solution)/shard_map/ppermute | solution.py:561
  4.7 11.0 %collective-permute-start = (bf16[384,128]{1,0:T(8,128)(2,1)}, bf16[384,128]{1,0:T(8,128)(2,1)S(1)}, u32[]{:S(2)}, u32[]{:S(2)}) collective-permute-start(bf16[384,128]{1,0:T(8,128)(2,1)} %refs_4_.1), channel_id=1, source_target_pairs={{0,1},{1,0},{2,3},{3,2},{4,5},{5,4},{6,7},{7,6},{8,9},{9,8},{10,11... | collective-permute-start | bytes 294920 | tf_op jit(solution)/shard_map/ppermute | solution.py:561
  6.3 9.4 %collective-permute-start.4 = (bf16[384,128]{1,0:T(8,128)(2,1)}, bf16[384,128]{1,0:T(8,128)(2,1)S(1)}, u32[]{:S(2)}, u32[]{:S(2)}) collective-permute-start(bf16[384,128]{1,0:T(8,128)(2,1)} %refs_5_.1), channel_id=1, source_target_pairs={{0,1},{1,0},{2,3},{3,2},{4,5},{5,4},{6,7},{7,6},{8,9},{9,8},{10,11... | collective-permute-start | bytes 294920 | tf_op jit(solution)/shard_map/ppermute | solution.py:561
  6.8 7.8 %collective-permute-start.3 = (bf16[384,128]{1,0:T(8,128)(2,1)}, bf16[384,128]{1,0:T(8,128)(2,1)S(1)}, u32[]{:S(2)}, u32[]{:S(2)}) collective-permute-start(bf16[384,128]{1,0:T(8,128)(2,1)} %refs_5_.1), channel_id=1, source_target_pairs={{0,2},{1,3},{2,0},{3,1},{4,6},{5,7},{6,4},{7,5},{8,10},{9,11},{10,... | collective-permute-start | bytes 294920 | tf_op jit(solution)/shard_map/ppermute | solution.py:561
  6.8 1.4 %copy-start.4 = (bf16[384,128]{1,0:T(8,128)(2,1)S(1)}, bf16[384,128]{1,0:T(8,128)(2,1)}, u32[]{:S(2)}) copy-start(bf16[384,128]{1,0:T(8,128)(2,1)} %refs_5_.1) | copy-start | bytes 294916
  6.9 1.4 %copy-start.5 = (s32[1,4]{1,0:T(1,128)S(1)}, s32[1,4]{1,0:T(1,128)}, u32[]{:S(2)}) copy-start(s32[1,4]{1,0:T(1,128)} %param.7) | copy-start | bytes 52
  8.2 2.8 %copy-start = (bf16[384,8192]{1,0:T(8,128)(2,1)S(1)}, bf16[384,8192]{1,0:T(8,128)(2,1)}, u32[]{:S(2)}) copy-start(bf16[384,8192]{1,0:T(8,128)(2,1)} %refs_0_.1) | copy-start | bytes 18874372
  12.7 5.1 %collective-permute-start.2 = (bf16[384,128]{1,0:T(8,128)(2,1)S(1)}, bf16[384,128]{1,0:T(8,128)(2,1)S(1)}, u32[]{:S(2)}, u32[]{:S(2)}) collective-permute-start(bf16[384,128]{1,0:T(8,128)(2,1)S(1)} %collective-permute-done.1.refs_6_.refs_3_.refs_4_.refs_2_), channel_id=1, source_target_pairs={{0,1},{1,0},{2,3},{3,2},{4,5},{5,4},{6,7},{7,6},{8,9},{9,8},{10,11... | collective-permute-start | bytes 294920 | tf_op jit(solution)/shard_map/ppermute | solution.py:561
  14.6 4.6 %collective-permute-start.5 = (bf16[384,128]{1,0:T(8,128)(2,1)S(1)}, bf16[384,128]{1,0:T(8,128)(2,1)S(1)}, u32[]{:S(2)}, u32[]{:S(2)}) collective-permute-start(bf16[384,128]{1,0:T(8,128)(2,1)S(1)} %collective-permute-done.3.refs_7_.refs_4_.refs_5_), channel_id=1, source_target_pairs={{0,1},{1,0},{2,3},{3,2},{4,5},{5,4},{6,7},{7,6},{8,9},{9,8},{10,11... | collective-permute-start | bytes 294920 | tf_op jit(solution)/shard_map/ppermute | solution.py:561
  15.7 24.5 %slice-start = ((s8[8388608]{0:T(1024)(128)(4,1)}), s8[4194304]{0:T(1024)(128)(4,1)S(1)}, s32[]{:S(2)}) async-start(s8[8388608]{0:T(1024)(128)(4,1)} %bitcast.10), calls=%async_computation | async-start | bytes 8388608
  15.9 24.3 %slice-start.1 = ((s8[8388608]{0:T(1024)(128)(4,1)}), s8[4194304]{0:T(1024)(128)(4,1)S(1)}, s32[]{:S(2)}) async-start(s8[8388608]{0:T(1024)(128)(4,1)} %bitcast.10), calls=%async_computation.1 | async-start | bytes 8388608
  19.7 4.7 %collective-permute-start.6 = (bf16[400,128]{1,0:T(8,128)(2,1)S(1)}, bf16[400,128]{1,0:T(8,128)(2,1)S(1)}, u32[]{:S(2)}, u32[]{:S(2)}) collective-permute-start(bf16[400,128]{1,0:T(8,128)(2,1)S(1)} %get-tuple-element.74.refs_6_), channel_id=1, source_target_pairs={{0,1},{1,0},{2,3},{3,2},{4,5},{5,4},{6,7},{7,6},{8,9},{9,8},{10,11... | collective-permute-start | bytes 307208 | tf_op jit(solution)/shard_map/ppermute | solution.py:561
  21.6 14.3 %collective-permute-start.7 = (bf16[384,128]{1,0:T(8,128)(2,1)S(1)}, bf16[384,128]{1,0:T(8,128)(2,1)S(1)}, u32[]{:S(2)}, u32[]{:S(2)}) collective-permute-start(bf16[384,128]{1,0:T(8,128)(2,1)S(1)} %get-tuple-element.83), channel_id=1, source_target_pairs={{0,1},{1,0},{2,3},{3,2},{4,5},{5,4},{6,7},{7,6},{8,9},{9,8},{10,11... | collective-permute-start | bytes 294920 | tf_op jit(solution)/shard_map/ppermute | solution.py:561
  24.5 15.7 %collective-permute-start.10 = (bf16[400,128]{1,0:T(8,128)(2,1)S(1)}, bf16[400,128]{1,0:T(8,128)(2,1)S(1)}, u32[]{:S(2)}, u32[]{:S(2)}) collective-permute-start(bf16[400,128]{1,0:T(8,128)(2,1)S(1)} %merge.2.refs_6_), channel_id=1, source_target_pairs={{0,2},{1,3},{2,0},{3,1},{4,6},{5,7},{6,4},{7,5},{8,10},{9,11},{10,... | collective-permute-start | bytes 307208 | tf_op jit(solution)/shard_map/ppermute | solution.py:561
  32.8 7.4 %collective-permute-start.11 = (bf16[400,128]{1,0:T(8,128)(2,1)S(1)}, bf16[400,128]{1,0:T(8,128)(2,1)S(1)}, u32[]{:S(2)}, u32[]{:S(2)}) collective-permute-start(bf16[400,128]{1,0:T(8,128)(2,1)S(1)} %get-tuple-element.76.refs_5_.refs_2_), channel_id=1, source_target_pairs={{0,1},{1,0},{2,3},{3,2},{4,5},{5,4},{6,7},{7,6},{8,9},{9,8},{10,11... | collective-permute-start | bytes 307208 | tf_op jit(solution)/shard_map/ppermute | solution.py:561
  35.8 7.0 %collective-permute-start.9 = (bf16[384,128]{1,0:T(8,128)(2,1)S(1)}, bf16[384,128]{1,0:T(8,128)(2,1)S(1)}, u32[]{:S(2)}, u32[]{:S(2)}) collective-permute-start(bf16[384,128]{1,0:T(8,128)(2,1)S(1)} %get-tuple-element.84), channel_id=1, source_target_pairs={{0,1},{1,0},{2,3},{3,2},{4,5},{5,4},{6,7},{7,6},{8,9},{9,8},{10,11... | collective-permute-start | bytes 294920 | tf_op jit(solution)/shard_map/ppermute | solution.py:561
  35.9 6.9 %collective-permute-start.8 = (bf16[384,128]{1,0:T(8,128)(2,1)S(1)}, bf16[384,128]{1,0:T(8,128)(2,1)S(1)}, u32[]{:S(2)}, u32[]{:S(2)}) collective-permute-start(bf16[384,128]{1,0:T(8,128)(2,1)S(1)} %merge.3), channel_id=1, source_target_pairs={{0,2},{1,3},{2,0},{3,1},{4,6},{5,7},{6,4},{7,5},{8,10},{9,11},{10,... | collective-permute-start | bytes 294920 | tf_op jit(solution)/shard_map/ppermute | solution.py:561
  41.7 3.2 %collective-permute-start.12 = (bf16[4128,128]{1,0:T(8,128)(2,1)S(1)}, bf16[4128,128]{1,0:T(8,128)(2,1)S(1)}, u32[]{:S(2)}, u32[]{:S(2)}) collective-permute-start(bf16[4128,128]{1,0:T(8,128)(2,1)S(1)} %get-tuple-element.91), channel_id=1, source_target_pairs={{0,4},{4,0},{8,12},{12,8},{16,20},{20,16},{24,28},{28,24},{1,5},{5... | collective-permute-start | bytes 3170312 | tf_op jit(solution)/shard_map/ppermute | solution.py:558
  44.4 5.1 %collective-permute-start.13 = (bf16[4096,128]{1,0:T(8,128)(2,1)S(1)}, bf16[4096,128]{1,0:T(8,128)(2,1)S(1)}, u32[]{:S(2)}, u32[]{:S(2)}) collective-permute-start(bf16[4096,128]{1,0:T(8,128)(2,1)S(1)} %get-tuple-element.94), channel_id=1, source_target_pairs={{0,4},{4,0},{8,12},{12,8},{16,20},{20,16},{24,28},{28,24},{1,5},{5... | collective-permute-start | bytes 3145736 | tf_op jit(solution)/shard_map/ppermute | solution.py:558
  45.2 10.8 %collective-permute-start.21 = (bf16[1056,128]{1,0:T(8,128)(2,1)S(1)}, bf16[1056,128]{1,0:T(8,128)(2,1)S(1)}, u32[]{:S(2)}, u32[]{:S(2)}) collective-permute-start(bf16[1056,128]{1,0:T(8,128)(2,1)S(1)} %get-tuple-element.114), channel_id=1, source_target_pairs={{0,8},{4,12},{8,0},{12,4},{16,24},{20,28},{24,16},{28,20},{1,9},{5... | collective-permute-start | bytes 811016 | tf_op jit(solution)/shard_map/ppermute | solution.py:558
  46.5 9.6 %collective-permute-start.22 = (bf16[1056,128]{1,0:T(8,128)(2,1)S(1)}, bf16[1056,128]{1,0:T(8,128)(2,1)S(1)}, u32[]{:S(2)}, u32[]{:S(2)}) collective-permute-start(bf16[1056,128]{1,0:T(8,128)(2,1)S(1)} %get-tuple-element.116), channel_id=1, source_target_pairs={{0,16},{4,20},{8,24},{12,28},{16,0},{20,4},{24,8},{28,12},{1,17},{... | collective-permute-start | bytes 811016 | tf_op jit(solution)/shard_map/ppermute | solution.py:558
  49.5 1.2 %collective-permute-start.14 = (f32[16,128]{1,0:T(8,128)S(1)}, f32[16,128]{1,0:T(8,128)S(1)}, u32[]{:S(2)}, u32[]{:S(2)}) collective-permute-start(f32[16,128]{1,0:T(8,128)S(1)} %get-tuple-element.95.refs_2_), channel_id=1, source_target_pairs={{0,4},{4,0},{8,12},{12,8},{16,20},{20,16},{24,28},{28,24},{1,5},{5... | collective-permute-start | bytes 24584 | tf_op jit(solution)/shard_map/ppermute | solution.py:558
  51.0 10.2 %collective-permute-start.15 = (bf16[1040,128]{1,0:T(8,128)(2,1)S(1)}, bf16[1040,128]{1,0:T(8,128)(2,1)S(1)}, u32[]{:S(2)}, u32[]{:S(2)}) collective-permute-start(bf16[1040,128]{1,0:T(8,128)(2,1)S(1)} %get-tuple-element.100), channel_id=1, source_target_pairs={{0,8},{4,12},{8,0},{12,4},{16,24},{20,28},{24,16},{28,20},{1,9},{5... | collective-permute-start | bytes 798728 | tf_op jit(solution)/shard_map/ppermute | solution.py:558
  52.0 9.2 %collective-permute-start.16 = (bf16[1024,128]{1,0:T(8,128)(2,1)S(1)}, bf16[1024,128]{1,0:T(8,128)(2,1)S(1)}, u32[]{:S(2)}, u32[]{:S(2)}) collective-permute-start(bf16[1024,128]{1,0:T(8,128)(2,1)S(1)} %get-tuple-element.102), channel_id=1, source_target_pairs={{0,16},{4,20},{8,24},{12,28},{16,0},{20,4},{24,8},{28,12},{1,17},{... | collective-permute-start | bytes 786440 | tf_op jit(solution)/shard_map/ppermute | solution.py:558
  56.2 8.4 %collective-permute-start.23 = (bf16[544,128]{1,0:T(8,128)(2,1)S(1)}, bf16[544,128]{1,0:T(8,128)(2,1)S(1)}, u32[]{:S(2)}, u32[]{:S(2)}) collective-permute-start(bf16[544,128]{1,0:T(8,128)(2,1)S(1)} %get-tuple-element.119), channel_id=1, source_target_pairs={{0,16},{4,20},{8,24},{12,28},{16,0},{20,4},{24,8},{28,12},{1,17},{... | collective-permute-start | bytes 417800 | tf_op jit(solution)/shard_map/ppermute | solution.py:558
  58.3 6.3 %collective-permute-start.24 = (bf16[512,128]{1,0:T(8,128)(2,1)S(1)}, bf16[512,128]{1,0:T(8,128)(2,1)S(1)}, u32[]{:S(2)}, u32[]{:S(2)}) collective-permute-start(bf16[512,128]{1,0:T(8,128)(2,1)S(1)} %get-tuple-element.121), channel_id=1, source_target_pairs={{0,8},{4,12},{8,0},{12,4},{16,24},{20,28},{24,16},{28,20},{1,9},{5... | collective-permute-start | bytes 393224 | tf_op jit(solution)/shard_map/ppermute | solution.py:558
  61.5 7.2 %collective-permute-start.17 = (bf16[528,128]{1,0:T(8,128)(2,1)S(1)}, bf16[528,128]{1,0:T(8,128)(2,1)S(1)}, u32[]{:S(2)}, u32[]{:S(2)}) collective-permute-start(bf16[528,128]{1,0:T(8,128)(2,1)S(1)} %get-tuple-element.105), channel_id=1, source_target_pairs={{0,16},{4,20},{8,24},{12,28},{16,0},{20,4},{24,8},{28,12},{1,17},{... | collective-permute-start | bytes 405512 | tf_op jit(solution)/shard_map/ppermute | solution.py:558
  63.7 5.0 %collective-permute-start.18 = (bf16[512,128]{1,0:T(8,128)(2,1)S(1)}, bf16[512,128]{1,0:T(8,128)(2,1)S(1)}, u32[]{:S(2)}, u32[]{:S(2)}) collective-permute-start(bf16[512,128]{1,0:T(8,128)(2,1)S(1)} %get-tuple-element.107), channel_id=1, source_target_pairs={{0,8},{4,12},{8,0},{12,4},{16,24},{20,28},{24,16},{28,20},{1,9},{5... | collective-permute-start | bytes 393224 | tf_op jit(solution)/shard_map/ppermute | solution.py:558
  64.7 7.1 %collective-permute-start.25 = (bf16[544,128]{1,0:T(8,128)(2,1)S(1)}, bf16[544,128]{1,0:T(8,128)(2,1)S(1)}, u32[]{:S(2)}, u32[]{:S(2)}) collective-permute-start(bf16[544,128]{1,0:T(8,128)(2,1)S(1)} %get-tuple-element.123), channel_id=1, source_target_pairs={{0,1},{1,0},{2,3},{3,2},{4,5},{5,4},{6,7},{7,6},{8,9},{9,8},{10,11... | collective-permute-start | bytes 417800 | tf_op jit(solution)/shard_map/ppermute | solution.py:561
  68.8 5.1 %collective-permute-start.19 = (bf16[528,128]{1,0:T(8,128)(2,1)S(1)}, bf16[528,128]{1,0:T(8,128)(2,1)S(1)}, u32[]{:S(2)}, u32[]{:S(2)}) collective-permute-start(bf16[528,128]{1,0:T(8,128)(2,1)S(1)} %get-tuple-element.110), channel_id=1, source_target_pairs={{0,1},{1,0},{2,3},{3,2},{4,5},{5,4},{6,7},{7,6},{8,9},{9,8},{10,11... | collective-permute-start | bytes 405512 | tf_op jit(solution)/shard_map/ppermute | solution.py:561
  71.8 8.3 %collective-permute-start.26 = (bf16[288,128]{1,0:T(8,128)(2,1)S(1)}, bf16[288,128]{1,0:T(8,128)(2,1)S(1)}, u32[]{:S(2)}, u32[]{:S(2)}) collective-permute-start(bf16[288,128]{1,0:T(8,128)(2,1)S(1)} %get-tuple-element.125), channel_id=1, source_target_pairs={{0,2},{1,3},{2,0},{3,1},{4,6},{5,7},{6,4},{7,5},{8,10},{9,11},{10,... | collective-permute-start | bytes 221192 | tf_op jit(solution)/shard_map/ppermute | solution.py:561
  74.1 6.0 %collective-permute-start.20 = (bf16[272,128]{1,0:T(8,128)(2,1)S(1)}, bf16[272,128]{1,0:T(8,128)(2,1)S(1)}, u32[]{:S(2)}, u32[]{:S(2)}) collective-permute-start(bf16[272,128]{1,0:T(8,128)(2,1)S(1)} %get-tuple-element.113), channel_id=1, source_target_pairs={{0,2},{1,3},{2,0},{3,1},{4,6},{5,7},{6,4},{7,5},{8,10},{9,11},{10,... | collective-permute-start | bytes 208904 | tf_op jit(solution)/shard_map/ppermute | solution.py:561
  (3 other events, 3.9 us)

commit v17 on v16

--- a/solution.py
+++ b/solution.py
@@ -226,10 +226,15 @@
 
 
 def query_kernel(n, *refs):
-    k_refs, ds_refs, dq_ref, mark_ref = refs[:n], refs[n : 2 * n], refs[2 * n], refs[2 * n + 1]
+    k_refs, ds_refs = refs[:n], refs[n : 2 * n]
+    *done, dq_ref, mark_ref = refs[2 * n :]
     mark_ref[...] = jnp.zeros_like(mark_ref)
     rows, hd = k_refs[0].shape
-    for h in range(dq_ref.shape[1] // hd):
+    first = 0
+    if done:
+        first = done[0].shape[1] // hd
+        dq_ref[:, : first * hd] = done[0][...]
+    for h in range(first, dq_ref.shape[1] // hd):
         dq = 0.0
         for k, ds in zip(k_refs, ds_refs):
             part = ds[:, h * rows : (h + 1) * rows]
@@ -333,17 +338,17 @@
     return own, key_parts[0], value_parts[0], [blocks[b][0] for b in range(n)], score_grads, acts
 
 
-def query_gradients(key_blocks, score_grads, columns, after):
+def query_gradients(key_blocks, score_grads, done, columns, after):
     n = len(key_blocks)
     rows = key_blocks[0].shape[0]
     return whole_call(
         functools.partial(query_kernel, n),
         "query_gradients",
         [],
-        [*key_blocks, *score_grads],
+        [*key_blocks, *score_grads, *done],
         [shape((rows, columns)), shape((8, 128), F32)],
         2 + 3 * n,
-        (2 * n * rows * rows * columns, 16 * rows * columns),
+        (0, 0),
         [],
         after,
     )
@@ -623,7 +628,7 @@
     arrays = split(True, kept, got, [top, swap_dp(top, 1)])
     halves.append(arrays[:4])
     gathered = [arrays[4]]
-    query_grad, mark = query_gradients(key_blocks, score_grads, queries.shape[1], [arrays[1]])
+    query_half, mark = query_gradients(key_blocks, score_grads, [], queries.shape[1] // 2, [arrays[1]])
     groups = []
     for chosen in range(sets):
         low_away, low, high_away, high = halves[chosen]
@@ -645,8 +650,12 @@
                     [shape((size // 2 + tail, hd))] + [shape((size // 2, hd))] * 3 + [tops] * with_tops,
                     8,
                     cost,
-                    after=[mark] if chosen == 0 and stage == 1 else [],
+                    after=[mark] if stage == 1 else [],
                 )
+                if chosen == 0 and stage == 1:
+                    query_grad, mark = query_gradients(
+                        key_blocks, score_grads, [query_half], queries.shape[1], [low]
+                    )
             else:
                 chunk = rows_ctx
                 away, stay, *top_out = whole_call(

time: 81.1 us -> 81.4 us (level)
  Pallas kernels: 19.9 us -> 33.7 us
  starting transfers between devices: 40.1 us -> 28.2 us
  waiting for transfers between devices: 18.4 us -> 16.7 us
    pallas_call x25 -> x26, Pallas kernels: 19.9 us -> 33.7 us  [whole_call(): pl.pallas_call(body, grid_spec=pltpu.PrefetchScalarGridSpec(num_scalar_pr...]
    ppermute x16, starting transfers between devices: 29.1 us -> 21.9 us  [swap_ctx(): return lax.ppermute(x, 'context', xor_perm(n_ctx, mask))]
    ppermute x16, waiting for transfers between devices: 13.1 us -> 6.16 us  [swap_ctx(): return lax.ppermute(x, 'context', xor_perm(n_ctx, mask))]
    ppermute x11, waiting for transfers between devices: 5.21 us -> 10.6 us  [swap_dp(): return lax.ppermute(x, 'dp', xor_perm(n_dp, mask))]
    ppermute x11, starting transfers between devices: 11 us -> 6.27 us  [swap_dp(): return lax.ppermute(x, 'dp', xor_perm(n_dp, mask))]
  transfers between devices with their start and end apart: 27 -> 27, of which waited for: 9 -> 10; matrix products, arithmetic and copies ran while one was open for 0% -> 0% of each run, Pallas kernels for 23% -> 34%
where the time goes in v17:
time: 81.4 us; the launch traced here: 81.2 us
  Pallas kernels  33.7 us (41%)
  starting transfers between devices  28.2 us (35%)
  waiting for transfers between devices  16.7 us (21%)
  local copies, waits for them, and re-layouts  1.72 us (2%)
  between operations  0.87 us (1%)
    pallas_call x26, Pallas kernels, whole_call(): pl.pallas_call(body, grid_spec=pltpu.PrefetchScalarGridSpec(num_scalar_pr...  33.7 us
    ppermute x16, starting transfers between devices, swap_ctx(): return lax.ppermute(x, 'context', xor_perm(n_ctx, mask))  21.9 us
    ppermute x11, waiting for transfers between devices, swap_dp(): return lax.ppermute(x, 'dp', xor_perm(n_dp, mask))  10.6 us
    ppermute x11, starting transfers between devices, swap_dp(): return lax.ppermute(x, 'dp', xor_perm(n_dp, mask))  6.27 us
    ppermute x16, waiting for transfers between devices, swap_ctx(): return lax.ppermute(x, 'context', xor_perm(n_ctx, mask))  6.16 us
    unnamed x16, local copies, waits for them, and re-layouts  1.72 us
  transfers between devices with their start and end apart: 27, of which 10 were waited for; matrix products, arithmetic and copies ran while one was open for 0% of the time, Pallas kernels for 34%

profile of v17, /device:TPU:0, one launch (start us, length us, event | category | flops | bytes accessed | tf_op | source)
XLA Modules:
  0.0 81.2 jit_solution(17869894697827406997)
XLA Ops:
  0.6 4.1 %collective-permute-start.1 = (bf16[384,128]{1,0:T(8,128)(2,1)}, bf16[384,128]{1,0:T(8,128)(2,1)S(1)}, u32[]{:S(2)}, u32[]{:S(2)}) collective-permute-start(bf16[384,128]{1,0:T(8,128)(2,1)} %refs_4_.1), channel_id=1, source_target_pairs={{0,2},{1,3},{2,0},{3,1},{4,6},{5,7},{6,4},{7,5},{8,10},{9,11},{10,... | collective-permute-start | bytes 294920 | tf_op jit(solution)/shard_map/ppermute | solution.py:566
  4.7 1.6 %collective-permute-start = (bf16[384,128]{1,0:T(8,128)(2,1)}, bf16[384,128]{1,0:T(8,128)(2,1)S(1)}, u32[]{:S(2)}, u32[]{:S(2)}) collective-permute-start(bf16[384,128]{1,0:T(8,128)(2,1)} %refs_4_.1), channel_id=1, source_target_pairs={{0,1},{1,0},{2,3},{3,2},{4,5},{5,4},{6,7},{7,6},{8,9},{9,8},{10,11... | collective-permute-start | bytes 294920 | tf_op jit(solution)/shard_map/ppermute | solution.py:566
  6.9 1.1 %copy-done.1 = bf16[384,1024]{1,0:T(8,128)(2,1)S(1)} copy-done((bf16[384,1024]{1,0:T(8,128)(2,1)S(1)}, bf16[384,1024]{1,0:T(8,128)(2,1)}, u32[]{:S(2)}) %copy-start.1) | copy-done | bytes 786456
  8.2 2.4 %first_stats.1 = (f32[8,3072]{1,0:T(8,128)S(1)}, bf16[384,1024]{1,0:T(8,128)(2,1)S(1)}, bf16[384,1024]{1,0:T(8,128)(2,1)S(1)}, bf16[384,128]{1,0:T(8,128)(2,1)S(...) custom-call(s32[1]{0:T(128)} %bitcast.refs_1_.refs_0_, s32[4]{0:T(128)S(1)} %bitcast.16, ...), custom_call_target="tpu_custom_call" | custom-call | flops 2415919104 | bytes 3145728 | tf_op jit(solution)/shard_map/first_stats/pallas_call | solution.py:39
  11.0 1.7 %prepare.1.refs_8_ = bf16[8192,384]{1,0:T(8,128)(2,1)S(1)} custom-call(bf16[384,8192]{1,0:T(8,128)(2,1)S(1)} %copy-done, f32[8,3072]{1,0:T(8,128)S(1)} %get-tuple-element.73.refs_1_.refs_5_), custom_call_target="tpu_custom_call" | custom-call | tf_op jit(solution)/shard_map/prepare/pallas_call | solution.py:39
  12.7 1.9 %collective-permute-start.2 = (bf16[384,128]{1,0:T(8,128)(2,1)S(1)}, bf16[384,128]{1,0:T(8,128)(2,1)S(1)}, u32[]{:S(2)}, u32[]{:S(2)}) collective-permute-start(bf16[384,128]{1,0:T(8,128)(2,1)S(1)} %collective-permute-done.1.refs_6_.refs_3_.refs_4_.refs_2_), channel_id=1, source_target_pairs={{0,1},{1,0},{2,3},{3,2},{4,5},{5,4},{6,7},{7,6},{8,9},{9,8},{10,11... | collective-permute-start | bytes 294920 | tf_op jit(solution)/shard_map/ppermute | solution.py:566
  14.6 1.1 %collective-permute-start.5 = (bf16[384,128]{1,0:T(8,128)(2,1)S(1)}, bf16[384,128]{1,0:T(8,128)(2,1)S(1)}, u32[]{:S(2)}, u32[]{:S(2)}) collective-permute-start(bf16[384,128]{1,0:T(8,128)(2,1)S(1)} %collective-permute-done.3.refs_7_.refs_4_.refs_5_), channel_id=1, source_target_pairs={{0,1},{1,0},{2,3},{3,2},{4,5},{5,4},{6,7},{7,6},{8,9},{9,8},{10,11... | collective-permute-start | bytes 294920 | tf_op jit(solution)/shard_map/ppermute | solution.py:566
  15.7 2.2 %next_stats.2.refs_5_ = f32[8,3072]{1,0:T(8,128)S(1)} custom-call(f32[8,128]{1,0:T(8,128)S(1)} %get-tuple-element.70.refs_0_, bf16[384,1024]{1,0:T(8,128)(2,1)S(1)} %get-tuple-element.71.refs_1_.refs_2_, bf16[384,1024]{1,0:T(8,128)(2,1)S(1)} %get-tuple-element.72.refs_2_.refs_3_, bf16[384,128]{1,0:T(8,128)(2,1)S(1)} %collective-permute-done.refs_3_.refs_4_.refs_1_, ...), custom_call_target="tpu_custom_call" | custom-call | flops 2415919104 | bytes 3145728 | tf_op jit(solution)/shard_map/next_stats/pallas_call | solution.py:39
  17.9 2.2 %next_stats.3.refs_1_ = f32[8,3072]{1,0:T(8,128)S(1)} custom-call(f32[8,128]{1,0:T(8,128)S(1)} %get-tuple-element.70.refs_0_, bf16[384,1024]{1,0:T(8,128)(2,1)S(1)} %get-tuple-element.71.refs_1_.refs_2_, bf16[384,1024]{1,0:T(8,128)(2,1)S(1)} %get-tuple-element.72.refs_2_.refs_3_, bf16[384,128]{1,0:T(8,128)(2,1)S(1)} %collective-permute-done.1.refs_6_.refs_3_.refs_4_.refs_2_, ...), custom_call_target="tpu_custom_call" | custom-call | flops 2415919104 | bytes 3145728 | tf_op jit(solution)/shard_map/next_stats/pallas_call | solution.py:39
  20.1 5.1 %block_gradients.3 = (bf16[384,128]{1,0:T(8,128)(2,1)S(1)}, bf16[400,128]{1,0:T(8,128)(2,1)S(1)}, bf16[384,3072]{1,0:T(8,128)(2,1)S(1)}, f32[8,3072]{1,0:T(8,128)S(1)}) custom-call(f32[8,128]{1,0:T(8,128)S(1)} %get-tuple-element.70.refs_0_, f32[8,3072]{1,0:T(8,128)S(1)} %next_stats.3.refs_1_, bf16[384,1024]{1,0:T(8,128)(2,1)S(1)} %get-tuple-element.71.refs_1_.refs_2_, ...), custom_call_target="tpu_custom_call" | custom-call | tf_op jit(solution)/shard_map/block_gradients/pallas_call | solution.py:39
  25.2 2.0 %collective-permute-start.7 = (bf16[384,128]{1,0:T(8,128)(2,1)S(1)}, bf16[384,128]{1,0:T(8,128)(2,1)S(1)}, u32[]{:S(2)}, u32[]{:S(2)}) collective-permute-start(bf16[384,128]{1,0:T(8,128)(2,1)S(1)} %get-tuple-element.85), channel_id=1, source_target_pairs={{0,1},{1,0},{2,3},{3,2},{4,5},{5,4},{6,7},{7,6},{8,9},{9,8},{10,11... | collective-permute-start | bytes 294920 | tf_op jit(solution)/shard_map/ppermute | solution.py:566
  27.3 2.8 %block_gradients.4 = (bf16[384,128]{1,0:T(8,128)(2,1)S(1)}, bf16[400,128]{1,0:T(8,128)(2,1)S(1)}, bf16[384,3072]{1,0:T(8,128)(2,1)S(1)}) custom-call(f32[8,128]{1,0:T(8,128)S(1)} %get-tuple-element.70.refs_0_, f32[8,3072]{1,0:T(8,128)S(1)} %get-tuple-element.74.refs_1_.refs_0_, bf16[384,1024]{1,0:T(8,128)(2,1)S(1)} %get-tuple-element.71.refs_1_.refs_2_, ...), custom_call_target="tpu_custom_call" | custom-call | tf_op jit(solution)/shard_map/block_gradients/pallas_call | solution.py:39
  30.1 1.7 %collective-permute-start.10 = (bf16[400,128]{1,0:T(8,128)(2,1)S(1)}, bf16[400,128]{1,0:T(8,128)(2,1)S(1)}, u32[]{:S(2)}, u32[]{:S(2)}) collective-permute-start(bf16[400,128]{1,0:T(8,128)(2,1)S(1)} %merge.2.refs_6_), channel_id=1, source_target_pairs={{0,2},{1,3},{2,0},{3,1},{4,6},{5,7},{6,4},{7,5},{8,10},{9,11},{10,... | collective-permute-start | bytes 307208 | tf_op jit(solution)/shard_map/ppermute | solution.py:566
  31.8 3.0 %block_gradients.5 = (bf16[384,128]{1,0:T(8,128)(2,1)S(1)}, bf16[400,128]{1,0:T(8,128)(2,1)S(1)}, bf16[384,3072]{1,0:T(8,128)(2,1)S(1)}) custom-call(f32[8,128]{1,0:T(8,128)S(1)} %get-tuple-element.70.refs_0_, f32[8,3072]{1,0:T(8,128)S(1)} %get-tuple-element.74.refs_1_.refs_0_, bf16[384,1024]{1,0:T(8,128)(2,1)S(1)} %get-tuple-element.71.refs_1_.refs_2_, ...), custom_call_target="tpu_custom_call" | custom-call | tf_op jit(solution)/shard_map/block_gradients/pallas_call | solution.py:39
  34.9 2.0 %collective-permute-start.9 = (bf16[384,128]{1,0:T(8,128)(2,1)S(1)}, bf16[384,128]{1,0:T(8,128)(2,1)S(1)}, u32[]{:S(2)}, u32[]{:S(2)}) collective-permute-start(bf16[384,128]{1,0:T(8,128)(2,1)S(1)} %get-tuple-element.86), channel_id=1, source_target_pairs={{0,1},{1,0},{2,3},{3,2},{4,5},{5,4},{6,7},{7,6},{8,9},{9,8},{10,11... | collective-permute-start | bytes 294920 | tf_op jit(solution)/shard_map/ppermute | solution.py:566
  37.0 2.7 %own_gradients.1 = (f32[384,256]{1,0:T(8,128)S(1)}, bf16[384,3072]{1,0:T(8,128)(2,1)S(1)}) custom-call(f32[8,3072]{1,0:T(8,128)S(1)} %get-tuple-element.74.refs_1_.refs_0_, bf16[384,1024]{1,0:T(8,128)(2,1)S(1)} %get-tuple-element.71.refs_1_.refs_2_, bf16[384,1024]{1,0:T(8,128)(2,1)S(1)} %get-tuple-element.72.refs_2_.refs_3_, ...), custom_call_target="tpu_custom_call" | custom-call | tf_op jit(solution)/shard_map/own_gradients/pallas_call | solution.py:39
  40.4 1.5 %send_tiles.2 = (bf16[4128,128]{1,0:T(8,128)(2,1)S(1)}, f32[16,128]{1,0:T(8,128)S(1)}, bf16[384,128]{1,0:T(8,128)(2,1)S(1)}, bf16[384,128]{1,0:T(8,128)(2,1)}) custom-call(s32[1]{0:T(128)} %bitcast.2.refs_0_, f32[384,256]{1,0:T(8,128)S(1)} %get-tuple-element.83.refs_1_, bf16[400,128]{1,0:T(8,128)(2,1)S(1)} %collective-permute-done.10.refs_2_, ...), custom_call_target="tpu_custom_call" | custom-call | tf_op jit(solution)/shard_map/send_tiles/pallas_call | solution.py:39
  43.1 1.5 %send_tiles.3 = (bf16[4096,128]{1,0:T(8,128)(2,1)S(1)}, f32[16,128]{1,0:T(8,128)S(1)}, bf16[384,128]{1,0:T(8,128)(2,1)S(1)}, bf16[384,128]{1,0:T(8,128)(2,1)}) custom-call(s32[1]{0:T(128)} %bitcast.2.refs_0_, f32[384,256]{1,0:T(8,128)S(1)} %get-tuple-element.83.refs_1_, bf16[384,128]{1,0:T(8,128)(2,1)S(1)} %collective-permute-done.8.refs_2_, ...), custom_call_target="tpu_custom_call" | custom-call | tf_op jit(solution)/shard_map/send_tiles/pallas_call | solution.py:39
  45.4 2.0 %collective-permute-start.15 = (bf16[1056,128]{1,0:T(8,128)(2,1)S(1)}, bf16[1056,128]{1,0:T(8,128)(2,1)S(1)}, u32[]{:S(2)}, u32[]{:S(2)}) collective-permute-start(bf16[1056,128]{1,0:T(8,128)(2,1)S(1)} %get-tuple-element.100), channel_id=1, source_target_pairs={{0,8},{4,12},{8,0},{12,4},{16,24},{20,28},{24,16},{28,20},{1,9},{5... | collective-permute-start | bytes 811016 | tf_op jit(solution)/shard_map/ppermute | solution.py:563
  48.9 1.1 %collective-permute-done.14.refs_3_ = f32[16,128]{1,0:T(8,128)S(1)} collective-permute-done((f32[16,128]{1,0:T(8,128)S(1)}, f32[16,128]{1,0:T(8,128)S(1)}, u32[]{:S(2)}, u32[]{:S(2)}) %collective-permute-start.14) | collective-permute-done | bytes 8224 | tf_op jit(solution)/shard_map/ppermute | solution.py:563
  50.8 1.4 %collective-permute-start.18 = (bf16[1024,128]{1,0:T(8,128)(2,1)S(1)}, bf16[1024,128]{1,0:T(8,128)(2,1)S(1)}, u32[]{:S(2)}, u32[]{:S(2)}) collective-permute-start(bf16[1024,128]{1,0:T(8,128)(2,1)S(1)} %get-tuple-element.110), channel_id=1, source_target_pairs={{0,16},{4,20},{8,24},{12,28},{16,0},{20,4},{24,8},{28,12},{1,17},{... | collective-permute-start | bytes 786440 | tf_op jit(solution)/shard_map/ppermute | solution.py:563
  52.2 1.6 %query_gradients.2 = (bf16[384,512]{1,0:T(8,128)(2,1)S(1)}, f32[8,128]{1,0:T(8,128)S(1)}) custom-call(bf16[384,128]{1,0:T(8,128)(2,1)S(1)} %get-tuple-element.69.refs_3_.refs_0_, bf16[384,128]{1,0:T(8,128)(2,1)S(1)} %collective-permute-done.refs_3_.refs_4_.refs_1_, bf16[384,128]{1,0:T(8,128)(2,1)S(1)} %collective-permute-done.1.refs_6_.refs_3_.refs_4_.refs_2_, ...), custom_call_target="tpu_custom_call" | custom-call | tf_op jit(solution)/shard_map/query_gradients/pallas_call | solution.py:39
  54.7 2.0 %collective-permute-done.16.refs_3_ = bf16[1056,128]{1,0:T(8,128)(2,1)S(1)} collective-permute-done((bf16[1056,128]{1,0:T(8,128)(2,1)S(1)}, bf16[1056,128]{1,0:T(8,128)(2,1)S(1)}, u32[]{:S(2)}, u32[]{:S(2)}) %collective-permute-start.16) | collective-permute-done | bytes 270368 | tf_op jit(solution)/shard_map/ppermute | solution.py:563
  57.3 2.5 %query_gradients.3 = (bf16[384,1024]{1,0:T(8,128)(2,1)}, f32[8,128]{1,0:T(8,128)S(1)}) custom-call(bf16[384,128]{1,0:T(8,128)(2,1)S(1)} %get-tuple-element.69.refs_3_.refs_0_, bf16[384,128]{1,0:T(8,128)(2,1)S(1)} %collective-permute-done.refs_3_.refs_4_.refs_1_, bf16[384,128]{1,0:T(8,128)(2,1)S(1)} %collective-permute-done.1.refs_6_.refs_3_.refs_4_.refs_2_, ...), custom_call_target="tpu_custom_call" | custom-call | tf_op jit(solution)/shard_map/query_gradients/pallas_call | solution.py:39
  59.8 2.5 %collective-permute-done.18.refs_3_ = bf16[1024,128]{1,0:T(8,128)(2,1)S(1)} collective-permute-done((bf16[1024,128]{1,0:T(8,128)(2,1)S(1)}, bf16[1024,128]{1,0:T(8,128)(2,1)S(1)}, u32[]{:S(2)}, u32[]{:S(2)}) %collective-permute-start.18) | collective-permute-done | bytes 262176 | tf_op jit(solution)/shard_map/ppermute | solution.py:563
  63.8 1.4 %collective-permute-done.23.refs_2_ = bf16[544,128]{1,0:T(8,128)(2,1)S(1)} collective-permute-done((bf16[544,128]{1,0:T(8,128)(2,1)S(1)}, bf16[544,128]{1,0:T(8,128)(2,1)S(1)}, u32[]{:S(2)}, u32[]{:S(2)}) %collective-permute-start.23) | collective-permute-done | bytes 139296 | tf_op jit(solution)/shard_map/ppermute | solution.py:563
  65.4 2.6 %collective-permute-done.20.refs_4_ = bf16[512,128]{1,0:T(8,128)(2,1)S(1)} collective-permute-done((bf16[512,128]{1,0:T(8,128)(2,1)S(1)}, bf16[512,128]{1,0:T(8,128)(2,1)S(1)}, u32[]{:S(2)}, u32[]{:S(2)}) %collective-permute-start.20) | collective-permute-done | bytes 131104 | tf_op jit(solution)/shard_map/ppermute | solution.py:563
  68.1 1.6 %collective-permute-start.21 = (bf16[528,128]{1,0:T(8,128)(2,1)S(1)}, bf16[528,128]{1,0:T(8,128)(2,1)S(1)}, u32[]{:S(2)}, u32[]{:S(2)}) collective-permute-start(bf16[528,128]{1,0:T(8,128)(2,1)S(1)} %get-tuple-element.119), channel_id=1, source_target_pairs={{0,1},{1,0},{2,3},{3,2},{4,5},{5,4},{6,7},{7,6},{8,9},{9,8},{10,11... | collective-permute-start | bytes 405512 | tf_op jit(solution)/shard_map/ppermute | solution.py:566
  69.7 1.5 %collective-permute-done.25.refs_1_ = bf16[544,128]{1,0:T(8,128)(2,1)S(1)} collective-permute-done((bf16[544,128]{1,0:T(8,128)(2,1)S(1)}, bf16[544,128]{1,0:T(8,128)(2,1)S(1)}, u32[]{:S(2)}, u32[]{:S(2)}) %collective-permute-start.25) | collective-permute-done | bytes 139296 | tf_op jit(solution)/shard_map/ppermute | solution.py:566
  71.3 3.0 %collective-permute-start.26 = (bf16[288,128]{1,0:T(8,128)(2,1)S(1)}, bf16[288,128]{1,0:T(8,128)(2,1)S(1)}, u32[]{:S(2)}, u32[]{:S(2)}) collective-permute-start(bf16[288,128]{1,0:T(8,128)(2,1)S(1)} %get-tuple-element.129), channel_id=1, source_target_pairs={{0,2},{1,3},{2,0},{3,1},{4,6},{5,7},{6,4},{7,5},{8,10},{9,11},{10,... | collective-permute-start | bytes 221192 | tf_op jit(solution)/shard_map/ppermute | solution.py:566
  74.5 2.0 %collective-permute-start.22 = (bf16[272,128]{1,0:T(8,128)(2,1)S(1)}, bf16[272,128]{1,0:T(8,128)(2,1)S(1)}, u32[]{:S(2)}, u32[]{:S(2)}) collective-permute-start(bf16[272,128]{1,0:T(8,128)(2,1)S(1)} %get-tuple-element.122), channel_id=1, source_target_pairs={{0,2},{1,3},{2,0},{3,1},{4,6},{5,7},{6,4},{7,5},{8,10},{9,11},{10,... | collective-permute-start | bytes 208904 | tf_op jit(solution)/shard_map/ppermute | solution.py:566
  76.5 3.8 %collective-permute-done.22.refs_3_ = bf16[272,128]{1,0:T(8,128)(2,1)S(1)} collective-permute-done((bf16[272,128]{1,0:T(8,128)(2,1)S(1)}, bf16[272,128]{1,0:T(8,128)(2,1)S(1)}, u32[]{:S(2)}, u32[]{:S(2)}) %collective-permute-start.22) | collective-permute-done | bytes 69664 | tf_op jit(solution)/shard_map/ppermute | solution.py:566
  (65 shorter events, 10.6 us)
Async XLA Ops:
  0.6 12.1 %collective-permute-start.1 = (bf16[384,128]{1,0:T(8,128)(2,1)}, bf16[384,128]{1,0:T(8,128)(2,1)S(1)}, u32[]{:S(2)}, u32[]{:S(2)}) collective-permute-start(bf16[384,128]{1,0:T(8,128)(2,1)} %refs_4_.1), channel_id=1, source_target_pairs={{0,2},{1,3},{2,0},{3,1},{4,6},{5,7},{6,4},{7,5},{8,10},{9,11},{10,... | collective-permute-start | bytes 294920 | tf_op jit(solution)/shard_map/ppermute | solution.py:566
  4.7 11.0 %collective-permute-start = (bf16[384,128]{1,0:T(8,128)(2,1)}, bf16[384,128]{1,0:T(8,128)(2,1)S(1)}, u32[]{:S(2)}, u32[]{:S(2)}) collective-permute-start(bf16[384,128]{1,0:T(8,128)(2,1)} %refs_4_.1), channel_id=1, source_target_pairs={{0,1},{1,0},{2,3},{3,2},{4,5},{5,4},{6,7},{7,6},{8,9},{9,8},{10,11... | collective-permute-start | bytes 294920 | tf_op jit(solution)/shard_map/ppermute | solution.py:566
  6.3 9.4 %collective-permute-start.4 = (bf16[384,128]{1,0:T(8,128)(2,1)}, bf16[384,128]{1,0:T(8,128)(2,1)S(1)}, u32[]{:S(2)}, u32[]{:S(2)}) collective-permute-start(bf16[384,128]{1,0:T(8,128)(2,1)} %refs_5_.1), channel_id=1, source_target_pairs={{0,1},{1,0},{2,3},{3,2},{4,5},{5,4},{6,7},{7,6},{8,9},{9,8},{10,11... | collective-permute-start | bytes 294920 | tf_op jit(solution)/shard_map/ppermute | solution.py:566
  6.8 7.8 %collective-permute-start.3 = (bf16[384,128]{1,0:T(8,128)(2,1)}, bf16[384,128]{1,0:T(8,128)(2,1)S(1)}, u32[]{:S(2)}, u32[]{:S(2)}) collective-permute-start(bf16[384,128]{1,0:T(8,128)(2,1)} %refs_5_.1), channel_id=1, source_target_pairs={{0,2},{1,3},{2,0},{3,1},{4,6},{5,7},{6,4},{7,5},{8,10},{9,11},{10,... | collective-permute-start | bytes 294920 | tf_op jit(solution)/shard_map/ppermute | solution.py:566
  6.8 1.4 %copy-start.4 = (bf16[384,128]{1,0:T(8,128)(2,1)S(1)}, bf16[384,128]{1,0:T(8,128)(2,1)}, u32[]{:S(2)}) copy-start(bf16[384,128]{1,0:T(8,128)(2,1)} %refs_5_.1) | copy-start | bytes 294916
  6.9 1.4 %copy-start.5 = (s32[1,4]{1,0:T(1,128)S(1)}, s32[1,4]{1,0:T(1,128)}, u32[]{:S(2)}) copy-start(s32[1,4]{1,0:T(1,128)} %param.7) | copy-start | bytes 52
  8.2 2.8 %copy-start = (bf16[384,8192]{1,0:T(8,128)(2,1)S(1)}, bf16[384,8192]{1,0:T(8,128)(2,1)}, u32[]{:S(2)}) copy-start(bf16[384,8192]{1,0:T(8,128)(2,1)} %refs_0_.1) | copy-start | bytes 18874372
  12.7 7.4 %collective-permute-start.2 = (bf16[384,128]{1,0:T(8,128)(2,1)S(1)}, bf16[384,128]{1,0:T(8,128)(2,1)S(1)}, u32[]{:S(2)}, u32[]{:S(2)}) collective-permute-start(bf16[384,128]{1,0:T(8,128)(2,1)S(1)} %collective-permute-done.1.refs_6_.refs_3_.refs_4_.refs_2_), channel_id=1, source_target_pairs={{0,1},{1,0},{2,3},{3,2},{4,5},{5,4},{6,7},{7,6},{8,9},{9,8},{10,11... | collective-permute-start | bytes 294920 | tf_op jit(solution)/shard_map/ppermute | solution.py:566
  14.6 5.5 %collective-permute-start.5 = (bf16[384,128]{1,0:T(8,128)(2,1)S(1)}, bf16[384,128]{1,0:T(8,128)(2,1)S(1)}, u32[]{:S(2)}, u32[]{:S(2)}) collective-permute-start(bf16[384,128]{1,0:T(8,128)(2,1)S(1)} %collective-permute-done.3.refs_7_.refs_4_.refs_5_), channel_id=1, source_target_pairs={{0,1},{1,0},{2,3},{3,2},{4,5},{5,4},{6,7},{7,6},{8,9},{9,8},{10,11... | collective-permute-start | bytes 294920 | tf_op jit(solution)/shard_map/ppermute | solution.py:566
  15.7 24.7 %slice-start = ((s8[8388608]{0:T(1024)(128)(4,1)}), s8[4194304]{0:T(1024)(128)(4,1)S(1)}, s32[]{:S(2)}) async-start(s8[8388608]{0:T(1024)(128)(4,1)} %bitcast.10), calls=%async_computation | async-start | bytes 8388608
  17.9 22.5 %slice-start.1 = ((s8[8388608]{0:T(1024)(128)(4,1)}), s8[4194304]{0:T(1024)(128)(4,1)S(1)}, s32[]{:S(2)}) async-start(s8[8388608]{0:T(1024)(128)(4,1)} %bitcast.10), calls=%async_computation.1 | async-start | bytes 8388608
  25.2 4.9 %collective-permute-start.6 = (bf16[400,128]{1,0:T(8,128)(2,1)S(1)}, bf16[400,128]{1,0:T(8,128)(2,1)S(1)}, u32[]{:S(2)}, u32[]{:S(2)}) collective-permute-start(bf16[400,128]{1,0:T(8,128)(2,1)S(1)} %get-tuple-element.76.refs_6_), channel_id=1, source_target_pairs={{0,1},{1,0},{2,3},{3,2},{4,5},{5,4},{6,7},{7,6},{8,9},{9,8},{10,11... | collective-permute-start | bytes 307208 | tf_op jit(solution)/shard_map/ppermute | solution.py:566
  25.2 11.7 %collective-permute-start.7 = (bf16[384,128]{1,0:T(8,128)(2,1)S(1)}, bf16[384,128]{1,0:T(8,128)(2,1)S(1)}, u32[]{:S(2)}, u32[]{:S(2)}) collective-permute-start(bf16[384,128]{1,0:T(8,128)(2,1)S(1)} %get-tuple-element.85), channel_id=1, source_target_pairs={{0,1},{1,0},{2,3},{3,2},{4,5},{5,4},{6,7},{7,6},{8,9},{9,8},{10,11... | collective-permute-start | bytes 294920 | tf_op jit(solution)/shard_map/ppermute | solution.py:566
  30.1 9.6 %collective-permute-start.10 = (bf16[400,128]{1,0:T(8,128)(2,1)S(1)}, bf16[400,128]{1,0:T(8,128)(2,1)S(1)}, u32[]{:S(2)}, u32[]{:S(2)}) collective-permute-start(bf16[400,128]{1,0:T(8,128)(2,1)S(1)} %merge.2.refs_6_), channel_id=1, source_target_pairs={{0,2},{1,3},{2,0},{3,1},{4,6},{5,7},{6,4},{7,5},{8,10},{9,11},{10,... | collective-permute-start | bytes 307208 | tf_op jit(solution)/shard_map/ppermute | solution.py:566
  34.8 5.6 %collective-permute-start.11 = (bf16[400,128]{1,0:T(8,128)(2,1)S(1)}, bf16[400,128]{1,0:T(8,128)(2,1)S(1)}, u32[]{:S(2)}, u32[]{:S(2)}) collective-permute-start(bf16[400,128]{1,0:T(8,128)(2,1)S(1)} %get-tuple-element.78.refs_5_.refs_2_), channel_id=1, source_target_pairs={{0,1},{1,0},{2,3},{3,2},{4,5},{5,4},{6,7},{7,6},{8,9},{9,8},{10,11... | collective-permute-start | bytes 307208 | tf_op jit(solution)/shard_map/ppermute | solution.py:566
  34.9 8.1 %collective-permute-start.9 = (bf16[384,128]{1,0:T(8,128)(2,1)S(1)}, bf16[384,128]{1,0:T(8,128)(2,1)S(1)}, u32[]{:S(2)}, u32[]{:S(2)}) collective-permute-start(bf16[384,128]{1,0:T(8,128)(2,1)S(1)} %get-tuple-element.86), channel_id=1, source_target_pairs={{0,1},{1,0},{2,3},{3,2},{4,5},{5,4},{6,7},{7,6},{8,9},{9,8},{10,11... | collective-permute-start | bytes 294920 | tf_op jit(solution)/shard_map/ppermute | solution.py:566
  37.0 6.2 %collective-permute-start.8 = (bf16[384,128]{1,0:T(8,128)(2,1)S(1)}, bf16[384,128]{1,0:T(8,128)(2,1)S(1)}, u32[]{:S(2)}, u32[]{:S(2)}) collective-permute-start(bf16[384,128]{1,0:T(8,128)(2,1)S(1)} %merge.3), channel_id=1, source_target_pairs={{0,2},{1,3},{2,0},{3,1},{4,6},{5,7},{6,4},{7,5},{8,10},{9,11},{10,... | collective-permute-start | bytes 294920 | tf_op jit(solution)/shard_map/ppermute | solution.py:566
  41.9 3.2 %collective-permute-start.12 = (bf16[4128,128]{1,0:T(8,128)(2,1)S(1)}, bf16[4128,128]{1,0:T(8,128)(2,1)S(1)}, u32[]{:S(2)}, u32[]{:S(2)}) collective-permute-start(bf16[4128,128]{1,0:T(8,128)(2,1)S(1)} %get-tuple-element.93), channel_id=1, source_target_pairs={{0,4},{4,0},{8,12},{12,8},{16,20},{20,16},{24,28},{28,24},{1,5},{5... | collective-permute-start | bytes 3170312 | tf_op jit(solution)/shard_map/ppermute | solution.py:563
  44.7 4.2 %collective-permute-start.13 = (bf16[4096,128]{1,0:T(8,128)(2,1)S(1)}, bf16[4096,128]{1,0:T(8,128)(2,1)S(1)}, u32[]{:S(2)}, u32[]{:S(2)}) collective-permute-start(bf16[4096,128]{1,0:T(8,128)(2,1)S(1)} %get-tuple-element.96), channel_id=1, source_target_pairs={{0,4},{4,0},{8,12},{12,8},{16,20},{20,16},{24,28},{28,24},{1,5},{5... | collective-permute-start | bytes 3145736 | tf_op jit(solution)/shard_map/ppermute | solution.py:563
  45.4 9.4 %collective-permute-start.15 = (bf16[1056,128]{1,0:T(8,128)(2,1)S(1)}, bf16[1056,128]{1,0:T(8,128)(2,1)S(1)}, u32[]{:S(2)}, u32[]{:S(2)}) collective-permute-start(bf16[1056,128]{1,0:T(8,128)(2,1)S(1)} %get-tuple-element.100), channel_id=1, source_target_pairs={{0,8},{4,12},{8,0},{12,4},{16,24},{20,28},{24,16},{28,20},{1,9},{5... | collective-permute-start | bytes 811016 | tf_op jit(solution)/shard_map/ppermute | solution.py:563
  47.3 9.4 %collective-permute-start.16 = (bf16[1056,128]{1,0:T(8,128)(2,1)S(1)}, bf16[1056,128]{1,0:T(8,128)(2,1)S(1)}, u32[]{:S(2)}, u32[]{:S(2)}) collective-permute-start(bf16[1056,128]{1,0:T(8,128)(2,1)S(1)} %get-tuple-element.102), channel_id=1, source_target_pairs={{0,16},{4,20},{8,24},{12,28},{16,0},{20,4},{24,8},{28,12},{1,17},{... | collective-permute-start | bytes 811016 | tf_op jit(solution)/shard_map/ppermute | solution.py:563
  48.9 1.2 %collective-permute-start.14 = (f32[16,128]{1,0:T(8,128)S(1)}, f32[16,128]{1,0:T(8,128)S(1)}, u32[]{:S(2)}, u32[]{:S(2)}) collective-permute-start(f32[16,128]{1,0:T(8,128)S(1)} %get-tuple-element.97.refs_2_), channel_id=1, source_target_pairs={{0,4},{4,0},{8,12},{12,8},{16,20},{20,16},{24,28},{28,24},{1,5},{5... | collective-permute-start | bytes 24584 | tf_op jit(solution)/shard_map/ppermute | solution.py:563
  50.4 11.9 %collective-permute-start.17 = (bf16[1040,128]{1,0:T(8,128)(2,1)S(1)}, bf16[1040,128]{1,0:T(8,128)(2,1)S(1)}, u32[]{:S(2)}, u32[]{:S(2)}) collective-permute-start(bf16[1040,128]{1,0:T(8,128)(2,1)S(1)} %get-tuple-element.108), channel_id=1, source_target_pairs={{0,8},{4,12},{8,0},{12,4},{16,24},{20,28},{24,16},{28,20},{1,9},{5... | collective-permute-start | bytes 798728 | tf_op jit(solution)/shard_map/ppermute | solution.py:563
  50.8 11.6 %collective-permute-start.18 = (bf16[1024,128]{1,0:T(8,128)(2,1)S(1)}, bf16[1024,128]{1,0:T(8,128)(2,1)S(1)}, u32[]{:S(2)}, u32[]{:S(2)}) collective-permute-start(bf16[1024,128]{1,0:T(8,128)(2,1)S(1)} %get-tuple-element.110), channel_id=1, source_target_pairs={{0,16},{4,20},{8,24},{12,28},{16,0},{20,4},{24,8},{28,12},{1,17},{... | collective-permute-start | bytes 786440 | tf_op jit(solution)/shard_map/ppermute | solution.py:563
  56.8 8.4 %collective-permute-start.23 = (bf16[544,128]{1,0:T(8,128)(2,1)S(1)}, bf16[544,128]{1,0:T(8,128)(2,1)S(1)}, u32[]{:S(2)}, u32[]{:S(2)}) collective-permute-start(bf16[544,128]{1,0:T(8,128)(2,1)S(1)} %get-tuple-element.123), channel_id=1, source_target_pairs={{0,16},{4,20},{8,24},{12,28},{16,0},{20,4},{24,8},{28,12},{1,17},{... | collective-permute-start | bytes 417800 | tf_op jit(solution)/shard_map/ppermute | solution.py:563
  57.3 6.5 %collective-permute-start.24 = (bf16[512,128]{1,0:T(8,128)(2,1)S(1)}, bf16[512,128]{1,0:T(8,128)(2,1)S(1)}, u32[]{:S(2)}, u32[]{:S(2)}) collective-permute-start(bf16[512,128]{1,0:T(8,128)(2,1)S(1)} %get-tuple-element.125), channel_id=1, source_target_pairs={{0,8},{4,12},{8,0},{12,4},{16,24},{20,28},{24,16},{28,20},{1,9},{5... | collective-permute-start | bytes 393224 | tf_op jit(solution)/shard_map/ppermute | solution.py:563
  62.6 5.4 %collective-permute-start.19 = (bf16[528,128]{1,0:T(8,128)(2,1)S(1)}, bf16[528,128]{1,0:T(8,128)(2,1)S(1)}, u32[]{:S(2)}, u32[]{:S(2)}) collective-permute-start(bf16[528,128]{1,0:T(8,128)(2,1)S(1)} %get-tuple-element.114), channel_id=1, source_target_pairs={{0,16},{4,20},{8,24},{12,28},{16,0},{20,4},{24,8},{28,12},{1,17},{... | collective-permute-start | bytes 405512 | tf_op jit(solution)/shard_map/ppermute | solution.py:563
  63.0 5.0 %collective-permute-start.20 = (bf16[512,128]{1,0:T(8,128)(2,1)S(1)}, bf16[512,128]{1,0:T(8,128)(2,1)S(1)}, u32[]{:S(2)}, u32[]{:S(2)}) collective-permute-start(bf16[512,128]{1,0:T(8,128)(2,1)S(1)} %get-tuple-element.116), channel_id=1, source_target_pairs={{0,8},{4,12},{8,0},{12,4},{16,24},{20,28},{24,16},{28,20},{1,9},{5... | collective-permute-start | bytes 393224 | tf_op jit(solution)/shard_map/ppermute | solution.py:563
  65.3 6.0 %collective-permute-start.25 = (bf16[544,128]{1,0:T(8,128)(2,1)S(1)}, bf16[544,128]{1,0:T(8,128)(2,1)S(1)}, u32[]{:S(2)}, u32[]{:S(2)}) collective-permute-start(bf16[544,128]{1,0:T(8,128)(2,1)S(1)} %get-tuple-element.127), channel_id=1, source_target_pairs={{0,1},{1,0},{2,3},{3,2},{4,5},{5,4},{6,7},{7,6},{8,9},{9,8},{10,11... | collective-permute-start | bytes 417800 | tf_op jit(solution)/shard_map/ppermute | solution.py:566
  68.1 6.2 %collective-permute-start.21 = (bf16[528,128]{1,0:T(8,128)(2,1)S(1)}, bf16[528,128]{1,0:T(8,128)(2,1)S(1)}, u32[]{:S(2)}, u32[]{:S(2)}) collective-permute-start(bf16[528,128]{1,0:T(8,128)(2,1)S(1)} %get-tuple-element.119), channel_id=1, source_target_pairs={{0,1},{1,0},{2,3},{3,2},{4,5},{5,4},{6,7},{7,6},{8,9},{9,8},{10,11... | collective-permute-start | bytes 405512 | tf_op jit(solution)/shard_map/ppermute | solution.py:566
  71.3 9.1 %collective-permute-start.26 = (bf16[288,128]{1,0:T(8,128)(2,1)S(1)}, bf16[288,128]{1,0:T(8,128)(2,1)S(1)}, u32[]{:S(2)}, u32[]{:S(2)}) collective-permute-start(bf16[288,128]{1,0:T(8,128)(2,1)S(1)} %get-tuple-element.129), channel_id=1, source_target_pairs={{0,2},{1,3},{2,0},{3,1},{4,6},{5,7},{6,4},{7,5},{8,10},{9,11},{10,... | collective-permute-start | bytes 221192 | tf_op jit(solution)/shard_map/ppermute | solution.py:566
  74.5 5.9 %collective-permute-start.22 = (bf16[272,128]{1,0:T(8,128)(2,1)S(1)}, bf16[272,128]{1,0:T(8,128)(2,1)S(1)}, u32[]{:S(2)}, u32[]{:S(2)}) collective-permute-start(bf16[272,128]{1,0:T(8,128)(2,1)S(1)} %get-tuple-element.122), channel_id=1, source_target_pairs={{0,2},{1,3},{2,0},{3,1},{4,6},{5,7},{6,4},{7,5},{8,10},{9,11},{10,... | collective-permute-start | bytes 208904 | tf_op jit(solution)/shard_map/ppermute | solution.py:566
  (3 other events, 3.9 us)

commit v18 on v17

--- a/solution.py
+++ b/solution.py
@@ -192,7 +192,13 @@
     return dk[...] * inverse, dv[...]
 
 
-def other_kernel(b, flags, stats, q_ref, do_ref, k_ref, v_ref, dk_out, dv_out, ds_out, *refs):
+def other_kernel(b, flags, stats, q_ref, do_ref, k_ref, v_ref, *refs):
+    if b & (b - 1):
+        both, ds_out, *refs = refs
+        hd = both.shape[1] // 2
+        dk_out, dv_out = both.at[:, pl.ds(0, hd)], both.at[:, pl.ds(hd, hd)]
+    else:
+        dk_out, dv_out, ds_out, *refs = refs
     *refs, p_buf, dk, dv = refs
     keep = counted(b, flags)
     rows = dk.shape[0]
@@ -205,16 +211,17 @@
         if held:
             stats_of_block(b, q_ref, do_ref, k_ref, v_ref, before, stats, held)
         dk_sum, dv_sum = block_gradients(False, stats, q_ref, do_ref, k_ref, v_ref, p_buf, ds_out, dk, dv, held)
-        dk_out[...] = dk_sum.astype(BF16)
-        dv_out[:rows, :] = dv_sum.astype(BF16)
-        dv_out[rows:, :] = jnp.zeros((dv_out.shape[0] - rows, dv.shape[1]), BF16)
+        for out, total in ((dk_out, dk_sum), (dv_out, dv_sum)):
+            out[:rows, :] = total.astype(BF16)
+            if out.shape[0] > rows:
+                out[rows:, :] = jnp.zeros((out.shape[0] - rows, total.shape[1]), BF16)
 
     @pl.when(jnp.logical_not(keep))
     def _():
         if held:
             stats[...] = before[...]
-        dk_out[...] = jnp.zeros_like(dk_out)
-        dv_out[...] = jnp.zeros_like(dv_out)
+        dk_out[...] = jnp.zeros(dk_out.shape, BF16)
+        dv_out[...] = jnp.zeros(dv_out.shape, BF16)
         ds_out[...] = jnp.zeros_like(ds_out)
 
 
@@ -242,17 +249,20 @@
         dq_ref[:, h * hd : (h + 1) * hd] = (dq / hd**0.5).astype(BF16)
 
 
-def merge_kernel(rows, *refs):
-    *terms, out_ref = refs
-    total = functools.reduce(jnp.add, [term[:rows, :].astype(F32) for term in terms])
+def merge_kernel(rows, at, own, *refs):
+    *got, out_ref = refs
+    total = own[:rows, :].astype(F32)
+    for part in got:
+        total = total + part[:rows, at : at + total.shape[1]].astype(F32)
     out_ref[:rows, :] = total.astype(BF16)
     if out_ref.shape[0] > rows:
         out_ref[rows:, :] = jnp.zeros((out_ref.shape[0] - rows, out_ref.shape[1]), BF16)
 
 
-def merge(rows, terms, after):
-    outs = [shape(terms[0].shape)]
-    return whole_call(functools.partial(merge_kernel, rows), "merge", [], terms, outs, 4, (0, 0), [], after)[0]
+def merge(rows, at, own, got, after):
+    outs = [shape(own.shape)]
+    kernel = functools.partial(merge_kernel, rows, at)
+    return whole_call(kernel, "merge", [], [own, *got], outs, 4, (0, 0), [], after)[0]
 
 
 def attention(me, spans, queries, out_grad, keys, values, activations, mark, swap, n):
@@ -296,34 +306,42 @@
         )[0]
     p_buf = pltpu.VMEM((rows, 2 * rows), BF16)
     sums = [pltpu.VMEM((rows, hd), F32)] * 2
-    key_parts, value_parts = [[] for _ in range(n)], [[] for _ in range(n)]
-    score_grads, own_parts, before = [None] * n, {}, []
+    far_parts, key_parts, value_parts = [[] for _ in range(n)], [], []
+    score_grads, made, before = [None] * n, {}, []
     for b in range(n - 1, 0, -1):
         last = b == n - 1
         held = pltpu.VMEM((rows, tall), F32)
-        dk, dv, score_grads[b], *total = whole_call(
+        longer = rows + TOP_ROWS
+        outs = [shape((longer, 2 * hd))] if b & (b - 1) else [shape((rows, hd)), shape((longer, hd))]
+        results = whole_call(
             functools.partial(other_kernel, b),
             "block_gradients",
             [],
             [flags, stats, queries, out_grad, *blocks[b]],
-            [shape((rows, hd)), shape((rows + TOP_ROWS, hd)), shape((rows, tall))] + [stats_shape] * last,
+            outs + [shape((rows, tall))] + [stats_shape] * last,
             20 if last else 10,
             (0, 0),
             [held, held] * last + [p_buf, *sums],
             before,
         )
+        made[b] = results[: len(outs)]
+        score_grads[b] = results[len(outs)]
         if last:
-            stats = total[0]
-        if value_parts[b]:
-            dv = merge(rows, [dv, *value_parts[b]], [])
-        value_parts[b & (b - 1)].append(swap(dv, b & -b))
-        own_parts[b] = dk
-        before = [dv]
+            stats = results[-1]
+        before = made[b][-1:]
     for b in range(n - 1, 0, -1):
-        dk = own_parts[b]
-        if key_parts[b]:
-            dk = merge(rows, [dk, *key_parts[b]], before)
-        key_parts[b & (b - 1)].append(swap(dk, b & -b))
+        got, to = far_parts[b], b & (b - 1)
+        if to:
+            part = merge(rows, 0, made[b][0], got, before) if got else made[b][0]
+            far_parts[to].append(swap(part, b & -b))
+            continue
+        dk, dv = made[b]
+        if got:
+            dv = merge(rows, hd, dv, got, before)
+        value_parts.append(swap(dv, b))
+        if got:
+            dk = merge(rows, 0, dk, got, [dv])
+        key_parts.append(swap(dk, b))
     own, score_grads[0] = whole_call(
         own_kernel,
         "own_gradients",
@@ -335,7 +353,7 @@
         [p_buf, *sums],
         before,
     )
-    return own, key_parts[0], value_parts[0], [blocks[b][0] for b in range(n)], score_grads, acts
+    return own, key_parts, value_parts, [blocks[b][0] for b in range(n)], score_grads, acts
 
 
 def query_gradients(key_blocks, score_grads, done, columns, after):

time: 81.4 us -> 81.1 us (level)
    ppermute x11, waiting for transfers between devices: 10.6 us -> 6.87 us  [swap_dp(): return lax.ppermute(x, 'dp', xor_perm(n_dp, mask))]
    ppermute x16 -> x15, waiting for transfers between devices: 6.16 us -> 9.35 us  [swap_ctx(): return lax.ppermute(x, 'context', xor_perm(n_ctx, mask))]
    ppermute x11, starting transfers between devices: 6.27 us -> 9.41 us  [swap_dp(): return lax.ppermute(x, 'dp', xor_perm(n_dp, mask))]
    ppermute x16 -> x15, starting transfers between devices: 21.9 us -> 19.5 us  [swap_ctx(): return lax.ppermute(x, 'context', xor_perm(n_ctx, mask))]
  transfers between devices with their start and end apart: 27 -> 26, of which waited for: 10 -> 10; matrix products, arithmetic and copies ran while one was open for 0% -> 0% of each run, Pallas kernels for 34% -> 34%
where the time goes in v18:
time: 81.1 us
  Pallas kernels  33.4 us (41%)
  starting transfers between devices  28.9 us (36%)
  waiting for transfers between devices  16.2 us (20%)
  local copies, waits for them, and re-layouts  1.73 us (2%)
  between operations  0.86 us (1%)
    pallas_call x26, Pallas kernels, whole_call(): pl.pallas_call(body, grid_spec=pltpu.PrefetchScalarGridSpec(num_scalar_pr...  33.4 us
    ppermute x15, starting transfers between devices, swap_ctx(): return lax.ppermute(x, 'context', xor_perm(n_ctx, mask))  19.5 us
    ppermute x11, starting transfers between devices, swap_dp(): return lax.ppermute(x, 'dp', xor_perm(n_dp, mask))  9.41 us
    ppermute x15, waiting for transfers between devices, swap_ctx(): return lax.ppermute(x, 'context', xor_perm(n_ctx, mask))  9.35 us
    ppermute x11, waiting for transfers between devices, swap_dp(): return lax.ppermute(x, 'dp', xor_perm(n_dp, mask))  6.87 us
    unnamed x16, local copies, waits for them, and re-layouts  1.73 us
  transfers between devices with their start and end apart: 26, of which 10 were waited for; matrix products, arithmetic and copies ran while one was open for 0% of the time, Pallas kernels for 34%

profile of v18, /device:TPU:0, one launch (start us, length us, event | category | flops | bytes accessed | tf_op | source)
XLA Modules:
  0.0 81.1 jit_solution(5544766747982223945)
XLA Ops:
  0.6 4.1 %collective-permute-start.1 = (bf16[384,128]{1,0:T(8,128)(2,1)}, bf16[384,128]{1,0:T(8,128)(2,1)S(1)}, u32[]{:S(2)}, u32[]{:S(2)}) collective-permute-start(bf16[384,128]{1,0:T(8,128)(2,1)} %refs_4_.1), channel_id=1, source_target_pairs={{0,2},{1,3},{2,0},{3,1},{4,6},{5,7},{6,4},{7,5},{8,10},{9,11},{10,... | collective-permute-start | bytes 294920 | tf_op jit(solution)/shard_map/ppermute | solution.py:584
  4.7 1.6 %collective-permute-start = (bf16[384,128]{1,0:T(8,128)(2,1)}, bf16[384,128]{1,0:T(8,128)(2,1)S(1)}, u32[]{:S(2)}, u32[]{:S(2)}) collective-permute-start(bf16[384,128]{1,0:T(8,128)(2,1)} %refs_4_.1), channel_id=1, source_target_pairs={{0,1},{1,0},{2,3},{3,2},{4,5},{5,4},{6,7},{7,6},{8,9},{9,8},{10,11... | collective-permute-start | bytes 294920 | tf_op jit(solution)/shard_map/ppermute | solution.py:584
  6.9 1.1 %copy-done.1 = bf16[384,1024]{1,0:T(8,128)(2,1)S(1)} copy-done((bf16[384,1024]{1,0:T(8,128)(2,1)S(1)}, bf16[384,1024]{1,0:T(8,128)(2,1)}, u32[]{:S(2)}) %copy-start.1) | copy-done | bytes 786456
  8.2 2.4 %first_stats.1 = (f32[8,3072]{1,0:T(8,128)S(1)}, bf16[384,1024]{1,0:T(8,128)(2,1)S(1)}, bf16[384,1024]{1,0:T(8,128)(2,1)S(1)}, bf16[384,128]{1,0:T(8,128)(2,1)S(...) custom-call(s32[1]{0:T(128)} %bitcast.refs_1_.refs_0_, s32[4]{0:T(128)S(1)} %bitcast.16, ...), custom_call_target="tpu_custom_call" | custom-call | flops 2415919104 | bytes 3145728 | tf_op jit(solution)/shard_map/first_stats/pallas_call | solution.py:39
  11.0 1.7 %prepare.1.refs_8_ = bf16[8192,384]{1,0:T(8,128)(2,1)S(1)} custom-call(bf16[384,8192]{1,0:T(8,128)(2,1)S(1)} %copy-done, f32[8,3072]{1,0:T(8,128)S(1)} %get-tuple-element.72.refs_1_.refs_5_), custom_call_target="tpu_custom_call" | custom-call | tf_op jit(solution)/shard_map/prepare/pallas_call | solution.py:39
  12.7 1.9 %collective-permute-start.2 = (bf16[384,128]{1,0:T(8,128)(2,1)S(1)}, bf16[384,128]{1,0:T(8,128)(2,1)S(1)}, u32[]{:S(2)}, u32[]{:S(2)}) collective-permute-start(bf16[384,128]{1,0:T(8,128)(2,1)S(1)} %collective-permute-done.1.refs_6_.refs_3_.refs_4_.refs_2_), channel_id=1, source_target_pairs={{0,1},{1,0},{2,3},{3,2},{4,5},{5,4},{6,7},{7,6},{8,9},{9,8},{10,11... | collective-permute-start | bytes 294920 | tf_op jit(solution)/shard_map/ppermute | solution.py:584
  14.6 1.1 %collective-permute-start.5 = (bf16[384,128]{1,0:T(8,128)(2,1)S(1)}, bf16[384,128]{1,0:T(8,128)(2,1)S(1)}, u32[]{:S(2)}, u32[]{:S(2)}) collective-permute-start(bf16[384,128]{1,0:T(8,128)(2,1)S(1)} %collective-permute-done.3.refs_7_.refs_4_.refs_5_), channel_id=1, source_target_pairs={{0,1},{1,0},{2,3},{3,2},{4,5},{5,4},{6,7},{7,6},{8,9},{9,8},{10,11... | collective-permute-start | bytes 294920 | tf_op jit(solution)/shard_map/ppermute | solution.py:584
  15.7 2.2 %next_stats.2.refs_5_ = f32[8,3072]{1,0:T(8,128)S(1)} custom-call(f32[8,128]{1,0:T(8,128)S(1)} %get-tuple-element.69.refs_0_, bf16[384,1024]{1,0:T(8,128)(2,1)S(1)} %get-tuple-element.70.refs_1_.refs_2_, bf16[384,1024]{1,0:T(8,128)(2,1)S(1)} %get-tuple-element.71.refs_2_.refs_3_, bf16[384,128]{1,0:T(8,128)(2,1)S(1)} %collective-permute-done.refs_3_.refs_4_.refs_1_, ...), custom_call_target="tpu_custom_call" | custom-call | flops 2415919104 | bytes 3145728 | tf_op jit(solution)/shard_map/next_stats/pallas_call | solution.py:39
  17.9 2.2 %next_stats.3.refs_1_ = f32[8,3072]{1,0:T(8,128)S(1)} custom-call(f32[8,128]{1,0:T(8,128)S(1)} %get-tuple-element.69.refs_0_, bf16[384,1024]{1,0:T(8,128)(2,1)S(1)} %get-tuple-element.70.refs_1_.refs_2_, bf16[384,1024]{1,0:T(8,128)(2,1)S(1)} %get-tuple-element.71.refs_2_.refs_3_, bf16[384,128]{1,0:T(8,128)(2,1)S(1)} %collective-permute-done.1.refs_6_.refs_3_.refs_4_.refs_2_, ...), custom_call_target="tpu_custom_call" | custom-call | flops 2415919104 | bytes 3145728 | tf_op jit(solution)/shard_map/next_stats/pallas_call | solution.py:39
  20.1 5.1 %block_gradients.3 = (bf16[400,256]{1,0:T(8,128)(2,1)S(1)}, bf16[384,3072]{1,0:T(8,128)(2,1)S(1)}, f32[8,3072]{1,0:T(8,128)S(1)}) custom-call(f32[8,128]{1,0:T(8,128)S(1)} %get-tuple-element.69.refs_0_, f32[8,3072]{1,0:T(8,128)S(1)} %next_stats.3.refs_1_, bf16[384,1024]{1,0:T(8,128)(2,1)S(1)} %get-tuple-element.70.refs_1_.refs_2_, ...), custom_call_target="tpu_custom_call" | custom-call | tf_op jit(solution)/shard_map/block_gradients/pallas_call | solution.py:39
  25.3 2.8 %block_gradients.4 = (bf16[384,128]{1,0:T(8,128)(2,1)S(1)}, bf16[400,128]{1,0:T(8,128)(2,1)S(1)}, bf16[384,3072]{1,0:T(8,128)(2,1)S(1)}) custom-call(f32[8,128]{1,0:T(8,128)S(1)} %get-tuple-element.69.refs_0_, f32[8,3072]{1,0:T(8,128)S(1)} %get-tuple-element.73.refs_1_.refs_0_, bf16[384,1024]{1,0:T(8,128)(2,1)S(1)} %get-tuple-element.70.refs_1_.refs_2_, ...), custom_call_target="tpu_custom_call" | custom-call | tf_op jit(solution)/shard_map/block_gradients/pallas_call | solution.py:39
  28.1 3.0 %block_gradients.5 = (bf16[384,128]{1,0:T(8,128)(2,1)S(1)}, bf16[400,128]{1,0:T(8,128)(2,1)S(1)}, bf16[384,3072]{1,0:T(8,128)(2,1)S(1)}) custom-call(f32[8,128]{1,0:T(8,128)S(1)} %get-tuple-element.69.refs_0_, f32[8,3072]{1,0:T(8,128)S(1)} %get-tuple-element.73.refs_1_.refs_0_, bf16[384,1024]{1,0:T(8,128)(2,1)S(1)} %get-tuple-element.70.refs_1_.refs_2_, ...), custom_call_target="tpu_custom_call" | custom-call | tf_op jit(solution)/shard_map/block_gradients/pallas_call | solution.py:39
  31.2 2.0 %collective-permute-start.9 = (bf16[400,128]{1,0:T(8,128)(2,1)S(1)}, bf16[400,128]{1,0:T(8,128)(2,1)S(1)}, u32[]{:S(2)}, u32[]{:S(2)}) collective-permute-start(bf16[400,128]{1,0:T(8,128)(2,1)S(1)} %merge.2.refs_2_), channel_id=1, source_target_pairs={{0,2},{1,3},{2,0},{3,1},{4,6},{5,7},{6,4},{7,5},{8,10},{9,11},{10,... | collective-permute-start | bytes 307208 | tf_op jit(solution)/shard_map/ppermute | solution.py:584
  33.5 2.8 %collective-permute-start.7 = (bf16[384,128]{1,0:T(8,128)(2,1)S(1)}, bf16[384,128]{1,0:T(8,128)(2,1)S(1)}, u32[]{:S(2)}, u32[]{:S(2)}) collective-permute-start(bf16[384,128]{1,0:T(8,128)(2,1)S(1)} %merge.3), channel_id=1, source_target_pairs={{0,2},{1,3},{2,0},{3,1},{4,6},{5,7},{6,4},{7,5},{8,10},{9,11},{10,... | collective-permute-start | bytes 294920 | tf_op jit(solution)/shard_map/ppermute | solution.py:584
  36.3 2.6 %own_gradients.1 = (f32[384,256]{1,0:T(8,128)S(1)}, bf16[384,3072]{1,0:T(8,128)(2,1)S(1)}) custom-call(f32[8,3072]{1,0:T(8,128)S(1)} %get-tuple-element.73.refs_1_.refs_0_, bf16[384,1024]{1,0:T(8,128)(2,1)S(1)} %get-tuple-element.70.refs_1_.refs_2_, bf16[384,1024]{1,0:T(8,128)(2,1)S(1)} %get-tuple-element.71.refs_2_.refs_3_, ...), custom_call_target="tpu_custom_call" | custom-call | tf_op jit(solution)/shard_map/own_gradients/pallas_call | solution.py:39
  38.9 1.8 %collective-permute-done.9.refs_2_ = bf16[400,128]{1,0:T(8,128)(2,1)S(1)} collective-permute-done((bf16[400,128]{1,0:T(8,128)(2,1)S(1)}, bf16[400,128]{1,0:T(8,128)(2,1)S(1)}, u32[]{:S(2)}, u32[]{:S(2)}) %collective-permute-start.9) | collective-permute-done | bytes 102432 | tf_op jit(solution)/shard_map/ppermute | solution.py:584
  40.8 1.5 %send_tiles.2 = (bf16[4128,128]{1,0:T(8,128)(2,1)S(1)}, f32[16,128]{1,0:T(8,128)S(1)}, bf16[384,128]{1,0:T(8,128)(2,1)S(1)}, bf16[384,128]{1,0:T(8,128)(2,1)}) custom-call(s32[1]{0:T(128)} %bitcast.2.refs_0_, f32[384,256]{1,0:T(8,128)S(1)} %get-tuple-element.82.refs_1_, bf16[400,128]{1,0:T(8,128)(2,1)S(1)} %collective-permute-done.9.refs_2_, ...), custom_call_target="tpu_custom_call" | custom-call | tf_op jit(solution)/shard_map/send_tiles/pallas_call | solution.py:39
  42.3 1.1 %kept_tiles.2 = (f32[4,1024,128]{2,1,0:T(8,128)S(1)}, f32[16,128]{1,0:T(8,128)S(1)}) custom-call(s32[1]{0:T(128)} %bitcast.2.refs_0_, bf16[384,128]{1,0:T(8,128)(2,1)S(1)} %get-tuple-element.85.refs_1_, f32[16,128]{1,0:T(8,128)S(1)} %get-tuple-element.86.refs_2_, bf16[8,4,256,384]{3,2,1,0:T(8,128)(2,1)S(1)} %bitcast.7, f32[8,4,256,256]{3,2,1,0:T(8,128)S(1)} %bitcast.13), custom_call_target="tpu_custom_call" | custom-call | tf_op jit(solution)/shard_map/kept_tiles/pallas_call | solution.py:39
  43.4 1.5 %send_tiles.3 = (bf16[4096,128]{1,0:T(8,128)(2,1)S(1)}, f32[16,128]{1,0:T(8,128)S(1)}, bf16[384,128]{1,0:T(8,128)(2,1)S(1)}, bf16[384,128]{1,0:T(8,128)(2,1)}) custom-call(s32[1]{0:T(128)} %bitcast.2.refs_0_, f32[384,256]{1,0:T(8,128)S(1)} %get-tuple-element.82.refs_1_, bf16[384,128]{1,0:T(8,128)(2,1)S(1)} %collective-permute-done.7.refs_2_, ...), custom_call_target="tpu_custom_call" | custom-call | tf_op jit(solution)/shard_map/send_tiles/pallas_call | solution.py:39
  46.2 2.3 %collective-permute-start.15 = (bf16[1056,128]{1,0:T(8,128)(2,1)S(1)}, bf16[1056,128]{1,0:T(8,128)(2,1)S(1)}, u32[]{:S(2)}, u32[]{:S(2)}) collective-permute-start(bf16[1056,128]{1,0:T(8,128)(2,1)S(1)} %get-tuple-element.100), channel_id=1, source_target_pairs={{0,16},{4,20},{8,24},{12,28},{16,0},{20,4},{24,8},{28,12},{1,17},{... | collective-permute-start | bytes 811016 | tf_op jit(solution)/shard_map/ppermute | solution.py:581
  49.7 1.1 %collective-permute-done.13.refs_3_ = f32[16,128]{1,0:T(8,128)S(1)} collective-permute-done((f32[16,128]{1,0:T(8,128)S(1)}, f32[16,128]{1,0:T(8,128)S(1)}, u32[]{:S(2)}, u32[]{:S(2)}) %collective-permute-start.13) | collective-permute-done | bytes 8224 | tf_op jit(solution)/shard_map/ppermute | solution.py:581
  52.5 1.5 %query_gradients.2 = (bf16[384,512]{1,0:T(8,128)(2,1)S(1)}, f32[8,128]{1,0:T(8,128)S(1)}) custom-call(bf16[384,128]{1,0:T(8,128)(2,1)S(1)} %get-tuple-element.68.refs_3_.refs_0_, bf16[384,128]{1,0:T(8,128)(2,1)S(1)} %collective-permute-done.refs_3_.refs_4_.refs_1_, bf16[384,128]{1,0:T(8,128)(2,1)S(1)} %collective-permute-done.1.refs_6_.refs_3_.refs_4_.refs_2_, ...), custom_call_target="tpu_custom_call" | custom-call | tf_op jit(solution)/shard_map/query_gradients/pallas_call | solution.py:39
  54.2 1.5 %collective-permute-done.15.refs_3_ = bf16[1056,128]{1,0:T(8,128)(2,1)S(1)} collective-permute-done((bf16[1056,128]{1,0:T(8,128)(2,1)S(1)}, bf16[1056,128]{1,0:T(8,128)(2,1)S(1)}, u32[]{:S(2)}, u32[]{:S(2)}) %collective-permute-start.15) | collective-permute-done | bytes 270368 | tf_op jit(solution)/shard_map/ppermute | solution.py:581
  55.8 2.3 %collective-permute-start.22 = (bf16[544,128]{1,0:T(8,128)(2,1)S(1)}, bf16[544,128]{1,0:T(8,128)(2,1)S(1)}, u32[]{:S(2)}, u32[]{:S(2)}) collective-permute-start(bf16[544,128]{1,0:T(8,128)(2,1)S(1)} %get-tuple-element.121), channel_id=1, source_target_pairs={{0,16},{4,20},{8,24},{12,28},{16,0},{20,4},{24,8},{28,12},{1,17},{... | collective-permute-start | bytes 417800 | tf_op jit(solution)/shard_map/ppermute | solution.py:581
  58.1 2.4 %query_gradients.3 = (bf16[384,1024]{1,0:T(8,128)(2,1)}, f32[8,128]{1,0:T(8,128)S(1)}) custom-call(bf16[384,128]{1,0:T(8,128)(2,1)S(1)} %get-tuple-element.68.refs_3_.refs_0_, bf16[384,128]{1,0:T(8,128)(2,1)S(1)} %collective-permute-done.refs_3_.refs_4_.refs_1_, bf16[384,128]{1,0:T(8,128)(2,1)S(1)} %collective-permute-done.1.refs_6_.refs_3_.refs_4_.refs_2_, ...), custom_call_target="tpu_custom_call" | custom-call | tf_op jit(solution)/shard_map/query_gradients/pallas_call | solution.py:39
  61.5 2.3 %collective-permute-start.18 = (bf16[528,128]{1,0:T(8,128)(2,1)S(1)}, bf16[528,128]{1,0:T(8,128)(2,1)S(1)}, u32[]{:S(2)}, u32[]{:S(2)}) collective-permute-start(bf16[528,128]{1,0:T(8,128)(2,1)S(1)} %get-tuple-element.112), channel_id=1, source_target_pairs={{0,16},{4,20},{8,24},{12,28},{16,0},{20,4},{24,8},{28,12},{1,17},{... | collective-permute-start | bytes 405512 | tf_op jit(solution)/shard_map/ppermute | solution.py:581
  64.2 1.5 %collective-permute-start.24 = (bf16[544,128]{1,0:T(8,128)(2,1)S(1)}, bf16[544,128]{1,0:T(8,128)(2,1)S(1)}, u32[]{:S(2)}, u32[]{:S(2)}) collective-permute-start(bf16[544,128]{1,0:T(8,128)(2,1)S(1)} %get-tuple-element.125), channel_id=1, source_target_pairs={{0,1},{1,0},{2,3},{3,2},{4,5},{5,4},{6,7},{7,6},{8,9},{9,8},{10,11... | collective-permute-start | bytes 417800 | tf_op jit(solution)/shard_map/ppermute | solution.py:584
  65.7 3.1 %collective-permute-done.19.refs_4_ = bf16[512,128]{1,0:T(8,128)(2,1)S(1)} collective-permute-done((bf16[512,128]{1,0:T(8,128)(2,1)S(1)}, bf16[512,128]{1,0:T(8,128)(2,1)S(1)}, u32[]{:S(2)}, u32[]{:S(2)}) %collective-permute-start.19) | collective-permute-done | bytes 131104 | tf_op jit(solution)/shard_map/ppermute | solution.py:581
  69.1 2.4 %collective-permute-done.24.refs_1_ = bf16[544,128]{1,0:T(8,128)(2,1)S(1)} collective-permute-done((bf16[544,128]{1,0:T(8,128)(2,1)S(1)}, bf16[544,128]{1,0:T(8,128)(2,1)S(1)}, u32[]{:S(2)}, u32[]{:S(2)}) %collective-permute-start.24) | collective-permute-done | bytes 139296 | tf_op jit(solution)/shard_map/ppermute | solution.py:584
  71.5 2.1 %collective-permute-start.25 = (bf16[288,128]{1,0:T(8,128)(2,1)S(1)}, bf16[288,128]{1,0:T(8,128)(2,1)S(1)}, u32[]{:S(2)}, u32[]{:S(2)}) collective-permute-start(bf16[288,128]{1,0:T(8,128)(2,1)S(1)} %get-tuple-element.127), channel_id=1, source_target_pairs={{0,2},{1,3},{2,0},{3,1},{4,6},{5,7},{6,4},{7,5},{8,10},{9,11},{10,... | collective-permute-start | bytes 221192 | tf_op jit(solution)/shard_map/ppermute | solution.py:584
  74.2 1.3 %collective-permute-start.21 = (bf16[272,128]{1,0:T(8,128)(2,1)S(1)}, bf16[272,128]{1,0:T(8,128)(2,1)S(1)}, u32[]{:S(2)}, u32[]{:S(2)}) collective-permute-start(bf16[272,128]{1,0:T(8,128)(2,1)S(1)} %get-tuple-element.120), channel_id=1, source_target_pairs={{0,2},{1,3},{2,0},{3,1},{4,6},{5,7},{6,4},{7,5},{8,10},{9,11},{10,... | collective-permute-start | bytes 208904 | tf_op jit(solution)/shard_map/ppermute | solution.py:584
  75.5 4.7 %collective-permute-done.21.refs_3_ = bf16[272,128]{1,0:T(8,128)(2,1)S(1)} collective-permute-done((bf16[272,128]{1,0:T(8,128)(2,1)S(1)}, bf16[272,128]{1,0:T(8,128)(2,1)S(1)}, u32[]{:S(2)}, u32[]{:S(2)}) %collective-permute-start.21) | collective-permute-done | bytes 69664 | tf_op jit(solution)/shard_map/ppermute | solution.py:584
  (63 shorter events, 9.2 us)
Async XLA Ops:
  0.6 12.1 %collective-permute-start.1 = (bf16[384,128]{1,0:T(8,128)(2,1)}, bf16[384,128]{1,0:T(8,128)(2,1)S(1)}, u32[]{:S(2)}, u32[]{:S(2)}) collective-permute-start(bf16[384,128]{1,0:T(8,128)(2,1)} %refs_4_.1), channel_id=1, source_target_pairs={{0,2},{1,3},{2,0},{3,1},{4,6},{5,7},{6,4},{7,5},{8,10},{9,11},{10,... | collective-permute-start | bytes 294920 | tf_op jit(solution)/shard_map/ppermute | solution.py:584
  4.7 11.0 %collective-permute-start = (bf16[384,128]{1,0:T(8,128)(2,1)}, bf16[384,128]{1,0:T(8,128)(2,1)S(1)}, u32[]{:S(2)}, u32[]{:S(2)}) collective-permute-start(bf16[384,128]{1,0:T(8,128)(2,1)} %refs_4_.1), channel_id=1, source_target_pairs={{0,1},{1,0},{2,3},{3,2},{4,5},{5,4},{6,7},{7,6},{8,9},{9,8},{10,11... | collective-permute-start | bytes 294920 | tf_op jit(solution)/shard_map/ppermute | solution.py:584
  6.3 9.4 %collective-permute-start.4 = (bf16[384,128]{1,0:T(8,128)(2,1)}, bf16[384,128]{1,0:T(8,128)(2,1)S(1)}, u32[]{:S(2)}, u32[]{:S(2)}) collective-permute-start(bf16[384,128]{1,0:T(8,128)(2,1)} %refs_5_.1), channel_id=1, source_target_pairs={{0,1},{1,0},{2,3},{3,2},{4,5},{5,4},{6,7},{7,6},{8,9},{9,8},{10,11... | collective-permute-start | bytes 294920 | tf_op jit(solution)/shard_map/ppermute | solution.py:584
  6.8 7.8 %collective-permute-start.3 = (bf16[384,128]{1,0:T(8,128)(2,1)}, bf16[384,128]{1,0:T(8,128)(2,1)S(1)}, u32[]{:S(2)}, u32[]{:S(2)}) collective-permute-start(bf16[384,128]{1,0:T(8,128)(2,1)} %refs_5_.1), channel_id=1, source_target_pairs={{0,2},{1,3},{2,0},{3,1},{4,6},{5,7},{6,4},{7,5},{8,10},{9,11},{10,... | collective-permute-start | bytes 294920 | tf_op jit(solution)/shard_map/ppermute | solution.py:584
  6.8 1.4 %copy-start.3 = (bf16[384,128]{1,0:T(8,128)(2,1)S(1)}, bf16[384,128]{1,0:T(8,128)(2,1)}, u32[]{:S(2)}) copy-start(bf16[384,128]{1,0:T(8,128)(2,1)} %refs_4_.1) | copy-start | bytes 294916
  6.8 1.4 %copy-start.4 = (bf16[384,128]{1,0:T(8,128)(2,1)S(1)}, bf16[384,128]{1,0:T(8,128)(2,1)}, u32[]{:S(2)}) copy-start(bf16[384,128]{1,0:T(8,128)(2,1)} %refs_5_.1) | copy-start | bytes 294916
  6.9 1.4 %copy-start.5 = (s32[1,4]{1,0:T(1,128)S(1)}, s32[1,4]{1,0:T(1,128)}, u32[]{:S(2)}) copy-start(s32[1,4]{1,0:T(1,128)} %param.7) | copy-start | bytes 52
  8.2 2.8 %copy-start = (bf16[384,8192]{1,0:T(8,128)(2,1)S(1)}, bf16[384,8192]{1,0:T(8,128)(2,1)}, u32[]{:S(2)}) copy-start(bf16[384,8192]{1,0:T(8,128)(2,1)} %refs_0_.1) | copy-start | bytes 18874372
  12.7 7.4 %collective-permute-start.2 = (bf16[384,128]{1,0:T(8,128)(2,1)S(1)}, bf16[384,128]{1,0:T(8,128)(2,1)S(1)}, u32[]{:S(2)}, u32[]{:S(2)}) collective-permute-start(bf16[384,128]{1,0:T(8,128)(2,1)S(1)} %collective-permute-done.1.refs_6_.refs_3_.refs_4_.refs_2_), channel_id=1, source_target_pairs={{0,1},{1,0},{2,3},{3,2},{4,5},{5,4},{6,7},{7,6},{8,9},{9,8},{10,11... | collective-permute-start | bytes 294920 | tf_op jit(solution)/shard_map/ppermute | solution.py:584
  14.6 5.5 %collective-permute-start.5 = (bf16[384,128]{1,0:T(8,128)(2,1)S(1)}, bf16[384,128]{1,0:T(8,128)(2,1)S(1)}, u32[]{:S(2)}, u32[]{:S(2)}) collective-permute-start(bf16[384,128]{1,0:T(8,128)(2,1)S(1)} %collective-permute-done.3.refs_7_.refs_4_.refs_5_), channel_id=1, source_target_pairs={{0,1},{1,0},{2,3},{3,2},{4,5},{5,4},{6,7},{7,6},{8,9},{9,8},{10,11... | collective-permute-start | bytes 294920 | tf_op jit(solution)/shard_map/ppermute | solution.py:584
  15.7 25.0 %slice-start = ((s8[8388608]{0:T(1024)(128)(4,1)}), s8[4194304]{0:T(1024)(128)(4,1)S(1)}, s32[]{:S(2)}) async-start(s8[8388608]{0:T(1024)(128)(4,1)} %bitcast.10), calls=%async_computation | async-start | bytes 8388608
  17.9 22.9 %slice-start.1 = ((s8[8388608]{0:T(1024)(128)(4,1)}), s8[4194304]{0:T(1024)(128)(4,1)S(1)}, s32[]{:S(2)}) async-start(s8[8388608]{0:T(1024)(128)(4,1)} %bitcast.10), calls=%async_computation.1 | async-start | bytes 8388608
  25.2 5.9 %collective-permute-start.6 = (bf16[400,256]{1,0:T(8,128)(2,1)S(1)}, bf16[400,256]{1,0:T(8,128)(2,1)S(1)}, u32[]{:S(2)}, u32[]{:S(2)}) collective-permute-start(bf16[400,256]{1,0:T(8,128)(2,1)S(1)} %get-tuple-element.75.refs_6_), channel_id=1, source_target_pairs={{0,1},{1,0},{2,3},{3,2},{4,5},{5,4},{6,7},{7,6},{8,9},{9,8},{10,11... | collective-permute-start | bytes 614408 | tf_op jit(solution)/shard_map/ppermute | solution.py:584
  31.1 7.9 %collective-permute-start.10 = (bf16[400,128]{1,0:T(8,128)(2,1)S(1)}, bf16[400,128]{1,0:T(8,128)(2,1)S(1)}, u32[]{:S(2)}, u32[]{:S(2)}) collective-permute-start(bf16[400,128]{1,0:T(8,128)(2,1)S(1)} %get-tuple-element.77.refs_5_.refs_2_), channel_id=1, source_target_pairs={{0,1},{1,0},{2,3},{3,2},{4,5},{5,4},{6,7},{7,6},{8,9},{9,8},{10,11... | collective-permute-start | bytes 307208 | tf_op jit(solution)/shard_map/ppermute | solution.py:584
  31.2 9.6 %collective-permute-start.9 = (bf16[400,128]{1,0:T(8,128)(2,1)S(1)}, bf16[400,128]{1,0:T(8,128)(2,1)S(1)}, u32[]{:S(2)}, u32[]{:S(2)}) collective-permute-start(bf16[400,128]{1,0:T(8,128)(2,1)S(1)} %merge.2.refs_2_), channel_id=1, source_target_pairs={{0,2},{1,3},{2,0},{3,1},{4,6},{5,7},{6,4},{7,5},{8,10},{9,11},{10,... | collective-permute-start | bytes 307208 | tf_op jit(solution)/shard_map/ppermute | solution.py:584
  33.2 10.2 %collective-permute-start.8 = (bf16[384,128]{1,0:T(8,128)(2,1)S(1)}, bf16[384,128]{1,0:T(8,128)(2,1)S(1)}, u32[]{:S(2)}, u32[]{:S(2)}) collective-permute-start(bf16[384,128]{1,0:T(8,128)(2,1)S(1)} %get-tuple-element.84), channel_id=1, source_target_pairs={{0,1},{1,0},{2,3},{3,2},{4,5},{5,4},{6,7},{7,6},{8,9},{9,8},{10,11... | collective-permute-start | bytes 294920 | tf_op jit(solution)/shard_map/ppermute | solution.py:584
  33.5 9.9 %collective-permute-start.7 = (bf16[384,128]{1,0:T(8,128)(2,1)S(1)}, bf16[384,128]{1,0:T(8,128)(2,1)S(1)}, u32[]{:S(2)}, u32[]{:S(2)}) collective-permute-start(bf16[384,128]{1,0:T(8,128)(2,1)S(1)} %merge.3), channel_id=1, source_target_pairs={{0,2},{1,3},{2,0},{3,1},{4,6},{5,7},{6,4},{7,5},{8,10},{9,11},{10,... | collective-permute-start | bytes 294920 | tf_op jit(solution)/shard_map/ppermute | solution.py:584
  42.3 3.2 %collective-permute-start.11 = (bf16[4128,128]{1,0:T(8,128)(2,1)S(1)}, bf16[4128,128]{1,0:T(8,128)(2,1)S(1)}, u32[]{:S(2)}, u32[]{:S(2)}) collective-permute-start(bf16[4128,128]{1,0:T(8,128)(2,1)S(1)} %get-tuple-element.91), channel_id=1, source_target_pairs={{0,4},{4,0},{8,12},{12,8},{16,20},{20,16},{24,28},{28,24},{1,5},{5... | collective-permute-start | bytes 3170312 | tf_op jit(solution)/shard_map/ppermute | solution.py:581
  44.9 4.7 %collective-permute-start.12 = (bf16[4096,128]{1,0:T(8,128)(2,1)S(1)}, bf16[4096,128]{1,0:T(8,128)(2,1)S(1)}, u32[]{:S(2)}, u32[]{:S(2)}) collective-permute-start(bf16[4096,128]{1,0:T(8,128)(2,1)S(1)} %get-tuple-element.94), channel_id=1, source_target_pairs={{0,4},{4,0},{8,12},{12,8},{16,20},{20,16},{24,28},{28,24},{1,5},{5... | collective-permute-start | bytes 3145736 | tf_op jit(solution)/shard_map/ppermute | solution.py:581
  45.7 8.5 %collective-permute-start.14 = (bf16[1056,128]{1,0:T(8,128)(2,1)S(1)}, bf16[1056,128]{1,0:T(8,128)(2,1)S(1)}, u32[]{:S(2)}, u32[]{:S(2)}) collective-permute-start(bf16[1056,128]{1,0:T(8,128)(2,1)S(1)} %get-tuple-element.98), channel_id=1, source_target_pairs={{0,8},{4,12},{8,0},{12,4},{16,24},{20,28},{24,16},{28,20},{1,9},{5... | collective-permute-start | bytes 811016 | tf_op jit(solution)/shard_map/ppermute | solution.py:581
  46.2 9.4 %collective-permute-start.15 = (bf16[1056,128]{1,0:T(8,128)(2,1)S(1)}, bf16[1056,128]{1,0:T(8,128)(2,1)S(1)}, u32[]{:S(2)}, u32[]{:S(2)}) collective-permute-start(bf16[1056,128]{1,0:T(8,128)(2,1)S(1)} %get-tuple-element.100), channel_id=1, source_target_pairs={{0,16},{4,20},{8,24},{12,28},{16,0},{20,4},{24,8},{28,12},{1,17},{... | collective-permute-start | bytes 811016 | tf_op jit(solution)/shard_map/ppermute | solution.py:581
  49.6 1.2 %collective-permute-start.13 = (f32[16,128]{1,0:T(8,128)S(1)}, f32[16,128]{1,0:T(8,128)S(1)}, u32[]{:S(2)}, u32[]{:S(2)}) collective-permute-start(f32[16,128]{1,0:T(8,128)S(1)} %get-tuple-element.95.refs_2_), channel_id=1, source_target_pairs={{0,4},{4,0},{8,12},{12,8},{16,20},{20,16},{24,28},{28,24},{1,5},{5... | collective-permute-start | bytes 24584 | tf_op jit(solution)/shard_map/ppermute | solution.py:581
  51.2 10.1 %collective-permute-start.16 = (bf16[1040,128]{1,0:T(8,128)(2,1)S(1)}, bf16[1040,128]{1,0:T(8,128)(2,1)S(1)}, u32[]{:S(2)}, u32[]{:S(2)}) collective-permute-start(bf16[1040,128]{1,0:T(8,128)(2,1)S(1)} %get-tuple-element.106), channel_id=1, source_target_pairs={{0,8},{4,12},{8,0},{12,4},{16,24},{20,28},{24,16},{28,20},{1,9},{5... | collective-permute-start | bytes 798728 | tf_op jit(solution)/shard_map/ppermute | solution.py:581
  51.5 9.8 %collective-permute-start.17 = (bf16[1024,128]{1,0:T(8,128)(2,1)S(1)}, bf16[1024,128]{1,0:T(8,128)(2,1)S(1)}, u32[]{:S(2)}, u32[]{:S(2)}) collective-permute-start(bf16[1024,128]{1,0:T(8,128)(2,1)S(1)} %get-tuple-element.108), channel_id=1, source_target_pairs={{0,16},{4,20},{8,24},{12,28},{16,0},{20,4},{24,8},{28,12},{1,17},{... | collective-permute-start | bytes 786440 | tf_op jit(solution)/shard_map/ppermute | solution.py:581
  55.8 8.4 %collective-permute-start.22 = (bf16[544,128]{1,0:T(8,128)(2,1)S(1)}, bf16[544,128]{1,0:T(8,128)(2,1)S(1)}, u32[]{:S(2)}, u32[]{:S(2)}) collective-permute-start(bf16[544,128]{1,0:T(8,128)(2,1)S(1)} %get-tuple-element.121), channel_id=1, source_target_pairs={{0,16},{4,20},{8,24},{12,28},{16,0},{20,4},{24,8},{28,12},{1,17},{... | collective-permute-start | bytes 417800 | tf_op jit(solution)/shard_map/ppermute | solution.py:581
  58.1 5.8 %collective-permute-start.23 = (bf16[512,128]{1,0:T(8,128)(2,1)S(1)}, bf16[512,128]{1,0:T(8,128)(2,1)S(1)}, u32[]{:S(2)}, u32[]{:S(2)}) collective-permute-start(bf16[512,128]{1,0:T(8,128)(2,1)S(1)} %get-tuple-element.123), channel_id=1, source_target_pairs={{0,8},{4,12},{8,0},{12,4},{16,24},{20,28},{24,16},{28,20},{1,9},{5... | collective-permute-start | bytes 393224 | tf_op jit(solution)/shard_map/ppermute | solution.py:581
  61.5 7.3 %collective-permute-start.18 = (bf16[528,128]{1,0:T(8,128)(2,1)S(1)}, bf16[528,128]{1,0:T(8,128)(2,1)S(1)}, u32[]{:S(2)}, u32[]{:S(2)}) collective-permute-start(bf16[528,128]{1,0:T(8,128)(2,1)S(1)} %get-tuple-element.112), channel_id=1, source_target_pairs={{0,16},{4,20},{8,24},{12,28},{16,0},{20,4},{24,8},{28,12},{1,17},{... | collective-permute-start | bytes 405512 | tf_op jit(solution)/shard_map/ppermute | solution.py:581
  63.9 5.0 %collective-permute-start.19 = (bf16[512,128]{1,0:T(8,128)(2,1)S(1)}, bf16[512,128]{1,0:T(8,128)(2,1)S(1)}, u32[]{:S(2)}, u32[]{:S(2)}) collective-permute-start(bf16[512,128]{1,0:T(8,128)(2,1)S(1)} %get-tuple-element.114), channel_id=1, source_target_pairs={{0,8},{4,12},{8,0},{12,4},{16,24},{20,28},{24,16},{28,20},{1,9},{5... | collective-permute-start | bytes 393224 | tf_op jit(solution)/shard_map/ppermute | solution.py:581
  64.2 7.3 %collective-permute-start.24 = (bf16[544,128]{1,0:T(8,128)(2,1)S(1)}, bf16[544,128]{1,0:T(8,128)(2,1)S(1)}, u32[]{:S(2)}, u32[]{:S(2)}) collective-permute-start(bf16[544,128]{1,0:T(8,128)(2,1)S(1)} %get-tuple-element.125), channel_id=1, source_target_pairs={{0,1},{1,0},{2,3},{3,2},{4,5},{5,4},{6,7},{7,6},{8,9},{9,8},{10,11... | collective-permute-start | bytes 417800 | tf_op jit(solution)/shard_map/ppermute | solution.py:584
  69.0 5.1 %collective-permute-start.20 = (bf16[528,128]{1,0:T(8,128)(2,1)S(1)}, bf16[528,128]{1,0:T(8,128)(2,1)S(1)}, u32[]{:S(2)}, u32[]{:S(2)}) collective-permute-start(bf16[528,128]{1,0:T(8,128)(2,1)S(1)} %get-tuple-element.117), channel_id=1, source_target_pairs={{0,1},{1,0},{2,3},{3,2},{4,5},{5,4},{6,7},{7,6},{8,9},{9,8},{10,11... | collective-permute-start | bytes 405512 | tf_op jit(solution)/shard_map/ppermute | solution.py:584
  71.5 8.7 %collective-permute-start.25 = (bf16[288,128]{1,0:T(8,128)(2,1)S(1)}, bf16[288,128]{1,0:T(8,128)(2,1)S(1)}, u32[]{:S(2)}, u32[]{:S(2)}) collective-permute-start(bf16[288,128]{1,0:T(8,128)(2,1)S(1)} %get-tuple-element.127), channel_id=1, source_target_pairs={{0,2},{1,3},{2,0},{3,1},{4,6},{5,7},{6,4},{7,5},{8,10},{9,11},{10,... | collective-permute-start | bytes 221192 | tf_op jit(solution)/shard_map/ppermute | solution.py:584
  74.2 6.0 %collective-permute-start.21 = (bf16[272,128]{1,0:T(8,128)(2,1)S(1)}, bf16[272,128]{1,0:T(8,128)(2,1)S(1)}, u32[]{:S(2)}, u32[]{:S(2)}) collective-permute-start(bf16[272,128]{1,0:T(8,128)(2,1)S(1)} %get-tuple-element.120), channel_id=1, source_target_pairs={{0,2},{1,3},{2,0},{3,1},{4,6},{5,7},{6,4},{7,5},{8,10},{9,11},{10,... | collective-permute-start | bytes 208904 | tf_op jit(solution)/shard_map/ppermute | solution.py:584
  (2 other events, 2.5 us)

commit v19 on v18

--- a/solution.py
+++ b/solution.py
@@ -329,7 +329,6 @@
         if last:
             stats = results[-1]
         before = made[b][-1:]
-    for b in range(n - 1, 0, -1):
         got, to = far_parts[b], b & (b - 1)
         if to:
             part = merge(rows, 0, made[b][0], got, before) if got else made[b][0]
@@ -342,6 +341,7 @@
         if got:
             dk = merge(rows, 0, dk, got, [dv])
         key_parts.append(swap(dk, b))
+        before = [dv, dk]
     own, score_grads[0] = whole_call(
         own_kernel,
         "own_gradients",

time: 81.1 us -> 82.3 us (1.015)
  Pallas kernels: 33.4 us -> 19.9 us
  starting transfers between devices: 28.9 us -> 39.8 us
  waiting for transfers between devices: 16.2 us -> 20.1 us
    pallas_call x26, Pallas kernels: 33.4 us -> 19.9 us  [whole_call(): pl.pallas_call(body, grid_spec=pltpu.PrefetchScalarGridSpec(num_scalar_pr...]
    ppermute x15, starting transfers between devices: 19.5 us -> 27.5 us  [swap_ctx(): return lax.ppermute(x, 'context', xor_perm(n_ctx, mask))]
    ppermute x15, waiting for transfers between devices: 9.35 us -> 15.4 us  [swap_ctx(): return lax.ppermute(x, 'context', xor_perm(n_ctx, mask))]
    ppermute x11, starting transfers between devices: 9.41 us -> 12.4 us  [swap_dp(): return lax.ppermute(x, 'dp', xor_perm(n_dp, mask))]
    ppermute x11, waiting for transfers between devices: 6.87 us -> 4.67 us  [swap_dp(): return lax.ppermute(x, 'dp', xor_perm(n_dp, mask))]
  transfers between devices with their start and end apart: 26 -> 26, of which waited for: 10 -> 10; matrix products, arithmetic and copies ran while one was open for 0% -> 0% of each run, Pallas kernels for 34% -> 22%
where the time goes in v19:
time: 82.3 us; the launch traced here: 82.4 us
  starting transfers between devices  39.8 us (48%)
  waiting for transfers between devices  20.1 us (24%)
  Pallas kernels  19.9 us (24%)
  local copies, waits for them, and re-layouts  1.73 us (2%)
  between operations  0.86 us (1%)
    ppermute x15, starting transfers between devices, swap_ctx(): return lax.ppermute(x, 'context', xor_perm(n_ctx, mask))  27.5 us
    pallas_call x26, Pallas kernels, whole_call(): pl.pallas_call(body, grid_spec=pltpu.PrefetchScalarGridSpec(num_scalar_pr...  19.9 us
    ppermute x15, waiting for transfers between devices, swap_ctx(): return lax.ppermute(x, 'context', xor_perm(n_ctx, mask))  15.4 us
    ppermute x11, starting transfers between devices, swap_dp(): return lax.ppermute(x, 'dp', xor_perm(n_dp, mask))  12.4 us
    ppermute x11, waiting for transfers between devices, swap_dp(): return lax.ppermute(x, 'dp', xor_perm(n_dp, mask))  4.67 us
    unnamed x16, local copies, waits for them, and re-layouts  1.73 us
  transfers between devices with their start and end apart: 26, of which 10 were waited for; matrix products, arithmetic and copies ran while one was open for 0% of the time, Pallas kernels for 22%

profile of v19, /device:TPU:0, one launch (start us, length us, event | category | flops | bytes accessed | tf_op | source)
XLA Modules:
  0.0 82.4 jit_solution(12990933441586476742)
XLA Ops:
  0.6 4.1 %collective-permute-start.1 = (bf16[384,128]{1,0:T(8,128)(2,1)}, bf16[384,128]{1,0:T(8,128)(2,1)S(1)}, u32[]{:S(2)}, u32[]{:S(2)}) collective-permute-start(bf16[384,128]{1,0:T(8,128)(2,1)} %refs_4_.1), channel_id=1, source_target_pairs={{0,2},{1,3},{2,0},{3,1},{4,6},{5,7},{6,4},{7,5},{8,10},{9,11},{10,... | collective-permute-start | bytes 294920 | tf_op jit(solution)/shard_map/ppermute | solution.py:584
  4.7 1.6 %collective-permute-start = (bf16[384,128]{1,0:T(8,128)(2,1)}, bf16[384,128]{1,0:T(8,128)(2,1)S(1)}, u32[]{:S(2)}, u32[]{:S(2)}) collective-permute-start(bf16[384,128]{1,0:T(8,128)(2,1)} %refs_4_.1), channel_id=1, source_target_pairs={{0,1},{1,0},{2,3},{3,2},{4,5},{5,4},{6,7},{7,6},{8,9},{9,8},{10,11... | collective-permute-start | bytes 294920 | tf_op jit(solution)/shard_map/ppermute | solution.py:584
  6.9 1.1 %copy-done.1 = bf16[384,1024]{1,0:T(8,128)(2,1)S(1)} copy-done((bf16[384,1024]{1,0:T(8,128)(2,1)S(1)}, bf16[384,1024]{1,0:T(8,128)(2,1)}, u32[]{:S(2)}) %copy-start.1) | copy-done | bytes 786456
  8.2 2.4 %first_stats.1 = (f32[8,3072]{1,0:T(8,128)S(1)}, bf16[384,1024]{1,0:T(8,128)(2,1)S(1)}, bf16[384,1024]{1,0:T(8,128)(2,1)S(1)}, bf16[384,128]{1,0:T(8,128)(2,1)S(...) custom-call(s32[1]{0:T(128)} %bitcast.refs_1_.refs_0_, s32[4]{0:T(128)S(1)} %bitcast.16, ...), custom_call_target="tpu_custom_call" | custom-call | flops 2415919104 | bytes 3145728 | tf_op jit(solution)/shard_map/first_stats/pallas_call | solution.py:39
  11.0 1.7 %prepare.1.refs_8_ = bf16[8192,384]{1,0:T(8,128)(2,1)S(1)} custom-call(bf16[384,8192]{1,0:T(8,128)(2,1)S(1)} %copy-done, f32[8,3072]{1,0:T(8,128)S(1)} %get-tuple-element.72.refs_1_.refs_5_), custom_call_target="tpu_custom_call" | custom-call | tf_op jit(solution)/shard_map/prepare/pallas_call | solution.py:39
  12.7 1.9 %collective-permute-start.2 = (bf16[384,128]{1,0:T(8,128)(2,1)S(1)}, bf16[384,128]{1,0:T(8,128)(2,1)S(1)}, u32[]{:S(2)}, u32[]{:S(2)}) collective-permute-start(bf16[384,128]{1,0:T(8,128)(2,1)S(1)} %collective-permute-done.1.refs_6_.refs_3_.refs_4_.refs_2_), channel_id=1, source_target_pairs={{0,1},{1,0},{2,3},{3,2},{4,5},{5,4},{6,7},{7,6},{8,9},{9,8},{10,11... | collective-permute-start | bytes 294920 | tf_op jit(solution)/shard_map/ppermute | solution.py:584
  14.6 1.1 %collective-permute-start.5 = (bf16[384,128]{1,0:T(8,128)(2,1)S(1)}, bf16[384,128]{1,0:T(8,128)(2,1)S(1)}, u32[]{:S(2)}, u32[]{:S(2)}) collective-permute-start(bf16[384,128]{1,0:T(8,128)(2,1)S(1)} %collective-permute-done.3.refs_7_.refs_4_.refs_5_), channel_id=1, source_target_pairs={{0,1},{1,0},{2,3},{3,2},{4,5},{5,4},{6,7},{7,6},{8,9},{9,8},{10,11... | collective-permute-start | bytes 294920 | tf_op jit(solution)/shard_map/ppermute | solution.py:584
  16.0 1.7 %collective-permute-done.2.refs_4_.refs_3_ = bf16[384,128]{1,0:T(8,128)(2,1)S(1)} collective-permute-done((bf16[384,128]{1,0:T(8,128)(2,1)S(1)}, bf16[384,128]{1,0:T(8,128)(2,1)S(1)}, u32[]{:S(2)}, u32[]{:S(2)}) %collective-permute-start.2) | collective-permute-done | bytes 98336 | tf_op jit(solution)/shard_map/ppermute | solution.py:584
  17.8 1.5 %collective-permute-done.5.refs_5_ = bf16[384,128]{1,0:T(8,128)(2,1)S(1)} collective-permute-done((bf16[384,128]{1,0:T(8,128)(2,1)S(1)}, bf16[384,128]{1,0:T(8,128)(2,1)S(1)}, u32[]{:S(2)}, u32[]{:S(2)}) %collective-permute-start.5) | collective-permute-done | bytes 98336 | tf_op jit(solution)/shard_map/ppermute | solution.py:584
  19.7 1.2 %collective-permute-start.6 = (bf16[400,256]{1,0:T(8,128)(2,1)S(1)}, bf16[400,256]{1,0:T(8,128)(2,1)S(1)}, u32[]{:S(2)}, u32[]{:S(2)}) collective-permute-start(bf16[400,256]{1,0:T(8,128)(2,1)S(1)} %get-tuple-element.75.refs_6_), channel_id=1, source_target_pairs={{0,1},{1,0},{2,3},{3,2},{4,5},{5,4},{6,7},{7,6},{8,9},{9,8},{10,11... | collective-permute-start | bytes 614408 | tf_op jit(solution)/shard_map/ppermute | solution.py:584
  21.2 4.3 %collective-permute-done.6.refs_1_ = bf16[400,256]{1,0:T(8,128)(2,1)S(1)} collective-permute-done((bf16[400,256]{1,0:T(8,128)(2,1)S(1)}, bf16[400,256]{1,0:T(8,128)(2,1)S(1)}, u32[]{:S(2)}, u32[]{:S(2)}) %collective-permute-start.6) | collective-permute-done | bytes 204832 | tf_op jit(solution)/shard_map/ppermute | solution.py:584
  25.6 7.7 %collective-permute-start.9 = (bf16[400,128]{1,0:T(8,128)(2,1)S(1)}, bf16[400,128]{1,0:T(8,128)(2,1)S(1)}, u32[]{:S(2)}, u32[]{:S(2)}) collective-permute-start(bf16[400,128]{1,0:T(8,128)(2,1)S(1)} %merge.2.refs_2_.refs_6_), channel_id=1, source_target_pairs={{0,2},{1,3},{2,0},{3,1},{4,6},{5,7},{6,4},{7,5},{8,10},{9,11},{10,... | collective-permute-start | bytes 307208 | tf_op jit(solution)/shard_map/ppermute | solution.py:584
  33.8 5.0 %collective-permute-start.10 = (bf16[400,128]{1,0:T(8,128)(2,1)S(1)}, bf16[400,128]{1,0:T(8,128)(2,1)S(1)}, u32[]{:S(2)}, u32[]{:S(2)}) collective-permute-start(bf16[400,128]{1,0:T(8,128)(2,1)S(1)} %get-tuple-element.78.refs_5_), channel_id=1, source_target_pairs={{0,1},{1,0},{2,3},{3,2},{4,5},{5,4},{6,7},{7,6},{8,9},{9,8},{10,11... | collective-permute-start | bytes 307208 | tf_op jit(solution)/shard_map/ppermute | solution.py:584
  39.0 2.7 %own_gradients.1 = (f32[384,256]{1,0:T(8,128)S(1)}, bf16[384,3072]{1,0:T(8,128)(2,1)S(1)}) custom-call(f32[8,3072]{1,0:T(8,128)S(1)} %get-tuple-element.73.refs_1_.refs_0_, bf16[384,1024]{1,0:T(8,128)(2,1)S(1)} %get-tuple-element.70.refs_1_.refs_2_, bf16[384,1024]{1,0:T(8,128)(2,1)S(1)} %get-tuple-element.71.refs_2_.refs_3_, ...), custom_call_target="tpu_custom_call" | custom-call | tf_op jit(solution)/shard_map/own_gradients/pallas_call | solution.py:39
  41.7 1.5 %send_tiles.2 = (bf16[4128,128]{1,0:T(8,128)(2,1)S(1)}, f32[16,128]{1,0:T(8,128)S(1)}, bf16[384,128]{1,0:T(8,128)(2,1)S(1)}, bf16[384,128]{1,0:T(8,128)(2,1)}) custom-call(s32[1]{0:T(128)} %bitcast.2.refs_0_, f32[384,256]{1,0:T(8,128)S(1)} %get-tuple-element.84.refs_1_, bf16[400,128]{1,0:T(8,128)(2,1)S(1)} %collective-permute-done.9.refs_2_, ...), custom_call_target="tpu_custom_call" | custom-call | tf_op jit(solution)/shard_map/send_tiles/pallas_call | solution.py:39
  43.2 1.1 %kept_tiles.2 = (f32[4,1024,128]{2,1,0:T(8,128)S(1)}, f32[16,128]{1,0:T(8,128)S(1)}) custom-call(s32[1]{0:T(128)} %bitcast.2.refs_0_, bf16[384,128]{1,0:T(8,128)(2,1)S(1)} %get-tuple-element.85.refs_1_, f32[16,128]{1,0:T(8,128)S(1)} %get-tuple-element.86.refs_2_, bf16[8,4,256,384]{3,2,1,0:T(8,128)(2,1)S(1)} %bitcast.7, f32[8,4,256,256]{3,2,1,0:T(8,128)S(1)} %bitcast.13), custom_call_target="tpu_custom_call" | custom-call | tf_op jit(solution)/shard_map/kept_tiles/pallas_call | solution.py:39
  44.9 1.5 %send_tiles.3 = (bf16[4096,128]{1,0:T(8,128)(2,1)S(1)}, f32[16,128]{1,0:T(8,128)S(1)}, bf16[384,128]{1,0:T(8,128)(2,1)S(1)}, bf16[384,128]{1,0:T(8,128)(2,1)}) custom-call(s32[1]{0:T(128)} %bitcast.2.refs_0_, f32[384,256]{1,0:T(8,128)S(1)} %get-tuple-element.84.refs_1_, bf16[384,128]{1,0:T(8,128)(2,1)S(1)} %collective-permute-done.7.refs_2_, ...), custom_call_target="tpu_custom_call" | custom-call | tf_op jit(solution)/shard_map/send_tiles/pallas_call | solution.py:39
  47.5 1.9 %collective-permute-start.15 = (bf16[1056,128]{1,0:T(8,128)(2,1)S(1)}, bf16[1056,128]{1,0:T(8,128)(2,1)S(1)}, u32[]{:S(2)}, u32[]{:S(2)}) collective-permute-start(bf16[1056,128]{1,0:T(8,128)(2,1)S(1)} %get-tuple-element.100), channel_id=1, source_target_pairs={{0,16},{4,20},{8,24},{12,28},{16,0},{20,4},{24,8},{28,12},{1,17},{... | collective-permute-start | bytes 811016 | tf_op jit(solution)/shard_map/ppermute | solution.py:581
  49.4 1.1 %kept_tiles.3 = (f32[4,1024,128]{2,1,0:T(8,128)S(1)}, f32[16,128]{1,0:T(8,128)S(1)}) custom-call(s32[1]{0:T(128)} %bitcast.2.refs_0_, bf16[384,128]{1,0:T(8,128)(2,1)S(1)} %get-tuple-element.88.refs_1_, f32[16,128]{1,0:T(8,128)S(1)} %get-tuple-element.89.refs_2_, bf16[8,4,256,384]{3,2,1,0:T(8,128)(2,1)S(1)} %bitcast.9, f32[8,4,256,256]{3,2,1,0:T(8,128)S(1)} %bitcast.15, ...), custom_call_target="tpu_custom_call" | custom-call | tf_op jit(solution)/shard_map/kept_tiles/pallas_call | solution.py:39
  50.5 1.1 %collective-permute-done.13.refs_3_ = f32[16,128]{1,0:T(8,128)S(1)} collective-permute-done((f32[16,128]{1,0:T(8,128)S(1)}, f32[16,128]{1,0:T(8,128)S(1)}, u32[]{:S(2)}, u32[]{:S(2)}) %collective-permute-start.13) | collective-permute-done | bytes 8224 | tf_op jit(solution)/shard_map/ppermute | solution.py:581
  52.0 2.0 %collective-permute-start.16 = (bf16[1040,128]{1,0:T(8,128)(2,1)S(1)}, bf16[1040,128]{1,0:T(8,128)(2,1)S(1)}, u32[]{:S(2)}, u32[]{:S(2)}) collective-permute-start(bf16[1040,128]{1,0:T(8,128)(2,1)S(1)} %get-tuple-element.106), channel_id=1, source_target_pairs={{0,8},{4,12},{8,0},{12,4},{16,24},{20,28},{24,16},{28,20},{1,9},{5... | collective-permute-start | bytes 798728 | tf_op jit(solution)/shard_map/ppermute | solution.py:581
  54.1 1.5 %query_gradients.2 = (bf16[384,512]{1,0:T(8,128)(2,1)S(1)}, f32[8,128]{1,0:T(8,128)S(1)}) custom-call(bf16[384,128]{1,0:T(8,128)(2,1)S(1)} %get-tuple-element.68.refs_3_.refs_0_, bf16[384,128]{1,0:T(8,128)(2,1)S(1)} %collective-permute-done.refs_3_.refs_4_.refs_1_, bf16[384,128]{1,0:T(8,128)(2,1)S(1)} %collective-permute-done.1.refs_6_.refs_3_.refs_4_.refs_2_, ...), custom_call_target="tpu_custom_call" | custom-call | tf_op jit(solution)/shard_map/query_gradients/pallas_call | solution.py:39
  56.4 2.5 %collective-permute-start.22 = (bf16[544,128]{1,0:T(8,128)(2,1)S(1)}, bf16[544,128]{1,0:T(8,128)(2,1)S(1)}, u32[]{:S(2)}, u32[]{:S(2)}) collective-permute-start(bf16[544,128]{1,0:T(8,128)(2,1)S(1)} %get-tuple-element.121), channel_id=1, source_target_pairs={{0,16},{4,20},{8,24},{12,28},{16,0},{20,4},{24,8},{28,12},{1,17},{... | collective-permute-start | bytes 417800 | tf_op jit(solution)/shard_map/ppermute | solution.py:581
  59.0 2.0 %collective-permute-start.23 = (bf16[512,128]{1,0:T(8,128)(2,1)S(1)}, bf16[512,128]{1,0:T(8,128)(2,1)S(1)}, u32[]{:S(2)}, u32[]{:S(2)}) collective-permute-start(bf16[512,128]{1,0:T(8,128)(2,1)S(1)} %get-tuple-element.123), channel_id=1, source_target_pairs={{0,8},{4,12},{8,0},{12,4},{16,24},{20,28},{24,16},{28,20},{1,9},{5... | collective-permute-start | bytes 393224 | tf_op jit(solution)/shard_map/ppermute | solution.py:581
  60.9 2.4 %query_gradients.3 = (bf16[384,1024]{1,0:T(8,128)(2,1)}, f32[8,128]{1,0:T(8,128)S(1)}) custom-call(bf16[384,128]{1,0:T(8,128)(2,1)S(1)} %get-tuple-element.68.refs_3_.refs_0_, bf16[384,128]{1,0:T(8,128)(2,1)S(1)} %collective-permute-done.refs_3_.refs_4_.refs_1_, bf16[384,128]{1,0:T(8,128)(2,1)S(1)} %collective-permute-done.1.refs_6_.refs_3_.refs_4_.refs_2_, ...), custom_call_target="tpu_custom_call" | custom-call | tf_op jit(solution)/shard_map/query_gradients/pallas_call | solution.py:39
  63.6 1.1 %collective-permute-start.18 = (bf16[528,128]{1,0:T(8,128)(2,1)S(1)}, bf16[528,128]{1,0:T(8,128)(2,1)S(1)}, u32[]{:S(2)}, u32[]{:S(2)}) collective-permute-start(bf16[528,128]{1,0:T(8,128)(2,1)S(1)} %get-tuple-element.112), channel_id=1, source_target_pairs={{0,16},{4,20},{8,24},{12,28},{16,0},{20,4},{24,8},{28,12},{1,17},{... | collective-permute-start | bytes 405512 | tf_op jit(solution)/shard_map/ppermute | solution.py:581
  64.7 2.0 %collective-permute-start.19 = (bf16[512,128]{1,0:T(8,128)(2,1)S(1)}, bf16[512,128]{1,0:T(8,128)(2,1)S(1)}, u32[]{:S(2)}, u32[]{:S(2)}) collective-permute-start(bf16[512,128]{1,0:T(8,128)(2,1)S(1)} %get-tuple-element.114), channel_id=1, source_target_pairs={{0,8},{4,12},{8,0},{12,4},{16,24},{20,28},{24,16},{28,20},{1,9},{5... | collective-permute-start | bytes 393224 | tf_op jit(solution)/shard_map/ppermute | solution.py:581
  66.8 2.8 %collective-permute-done.19.refs_4_ = bf16[512,128]{1,0:T(8,128)(2,1)S(1)} collective-permute-done((bf16[512,128]{1,0:T(8,128)(2,1)S(1)}, bf16[512,128]{1,0:T(8,128)(2,1)S(1)}, u32[]{:S(2)}, u32[]{:S(2)}) %collective-permute-start.19) | collective-permute-done | bytes 131104 | tf_op jit(solution)/shard_map/ppermute | solution.py:581
  70.1 2.9 %collective-permute-done.24.refs_1_ = bf16[544,128]{1,0:T(8,128)(2,1)S(1)} collective-permute-done((bf16[544,128]{1,0:T(8,128)(2,1)S(1)}, bf16[544,128]{1,0:T(8,128)(2,1)S(1)}, u32[]{:S(2)}, u32[]{:S(2)}) %collective-permute-start.24) | collective-permute-done | bytes 139296 | tf_op jit(solution)/shard_map/ppermute | solution.py:584
  73.0 2.4 %collective-permute-start.25 = (bf16[288,128]{1,0:T(8,128)(2,1)S(1)}, bf16[288,128]{1,0:T(8,128)(2,1)S(1)}, u32[]{:S(2)}, u32[]{:S(2)}) collective-permute-start(bf16[288,128]{1,0:T(8,128)(2,1)S(1)} %get-tuple-element.127), channel_id=1, source_target_pairs={{0,2},{1,3},{2,0},{3,1},{4,6},{5,7},{6,4},{7,5},{8,10},{9,11},{10,... | collective-permute-start | bytes 221192 | tf_op jit(solution)/shard_map/ppermute | solution.py:584
  75.5 1.5 %collective-permute-start.21 = (bf16[272,128]{1,0:T(8,128)(2,1)S(1)}, bf16[272,128]{1,0:T(8,128)(2,1)S(1)}, u32[]{:S(2)}, u32[]{:S(2)}) collective-permute-start(bf16[272,128]{1,0:T(8,128)(2,1)S(1)} %get-tuple-element.120), channel_id=1, source_target_pairs={{0,2},{1,3},{2,0},{3,1},{4,6},{5,7},{6,4},{7,5},{8,10},{9,11},{10,... | collective-permute-start | bytes 208904 | tf_op jit(solution)/shard_map/ppermute | solution.py:584
  77.0 4.4 %collective-permute-done.21.refs_3_ = bf16[272,128]{1,0:T(8,128)(2,1)S(1)} collective-permute-done((bf16[272,128]{1,0:T(8,128)(2,1)S(1)}, bf16[272,128]{1,0:T(8,128)(2,1)S(1)}, u32[]{:S(2)}, u32[]{:S(2)}) %collective-permute-start.21) | collective-permute-done | bytes 69664 | tf_op jit(solution)/shard_map/ppermute | solution.py:584
  (63 shorter events, 7.7 us)
Async XLA Ops:
  0.6 12.1 %collective-permute-start.1 = (bf16[384,128]{1,0:T(8,128)(2,1)}, bf16[384,128]{1,0:T(8,128)(2,1)S(1)}, u32[]{:S(2)}, u32[]{:S(2)}) collective-permute-start(bf16[384,128]{1,0:T(8,128)(2,1)} %refs_4_.1), channel_id=1, source_target_pairs={{0,2},{1,3},{2,0},{3,1},{4,6},{5,7},{6,4},{7,5},{8,10},{9,11},{10,... | collective-permute-start | bytes 294920 | tf_op jit(solution)/shard_map/ppermute | solution.py:584
  4.7 11.0 %collective-permute-start = (bf16[384,128]{1,0:T(8,128)(2,1)}, bf16[384,128]{1,0:T(8,128)(2,1)S(1)}, u32[]{:S(2)}, u32[]{:S(2)}) collective-permute-start(bf16[384,128]{1,0:T(8,128)(2,1)} %refs_4_.1), channel_id=1, source_target_pairs={{0,1},{1,0},{2,3},{3,2},{4,5},{5,4},{6,7},{7,6},{8,9},{9,8},{10,11... | collective-permute-start | bytes 294920 | tf_op jit(solution)/shard_map/ppermute | solution.py:584
  6.3 9.4 %collective-permute-start.4 = (bf16[384,128]{1,0:T(8,128)(2,1)}, bf16[384,128]{1,0:T(8,128)(2,1)S(1)}, u32[]{:S(2)}, u32[]{:S(2)}) collective-permute-start(bf16[384,128]{1,0:T(8,128)(2,1)} %refs_5_.1), channel_id=1, source_target_pairs={{0,1},{1,0},{2,3},{3,2},{4,5},{5,4},{6,7},{7,6},{8,9},{9,8},{10,11... | collective-permute-start | bytes 294920 | tf_op jit(solution)/shard_map/ppermute | solution.py:584
  6.8 7.8 %collective-permute-start.3 = (bf16[384,128]{1,0:T(8,128)(2,1)}, bf16[384,128]{1,0:T(8,128)(2,1)S(1)}, u32[]{:S(2)}, u32[]{:S(2)}) collective-permute-start(bf16[384,128]{1,0:T(8,128)(2,1)} %refs_5_.1), channel_id=1, source_target_pairs={{0,2},{1,3},{2,0},{3,1},{4,6},{5,7},{6,4},{7,5},{8,10},{9,11},{10,... | collective-permute-start | bytes 294920 | tf_op jit(solution)/shard_map/ppermute | solution.py:584
  6.8 1.4 %copy-start.3 = (bf16[384,128]{1,0:T(8,128)(2,1)S(1)}, bf16[384,128]{1,0:T(8,128)(2,1)}, u32[]{:S(2)}) copy-start(bf16[384,128]{1,0:T(8,128)(2,1)} %refs_4_.1) | copy-start | bytes 294916
  6.8 1.4 %copy-start.4 = (bf16[384,128]{1,0:T(8,128)(2,1)S(1)}, bf16[384,128]{1,0:T(8,128)(2,1)}, u32[]{:S(2)}) copy-start(bf16[384,128]{1,0:T(8,128)(2,1)} %refs_5_.1) | copy-start | bytes 294916
  6.9 1.4 %copy-start.5 = (s32[1,4]{1,0:T(1,128)S(1)}, s32[1,4]{1,0:T(1,128)}, u32[]{:S(2)}) copy-start(s32[1,4]{1,0:T(1,128)} %param.7) | copy-start | bytes 52
  8.2 2.8 %copy-start = (bf16[384,8192]{1,0:T(8,128)(2,1)S(1)}, bf16[384,8192]{1,0:T(8,128)(2,1)}, u32[]{:S(2)}) copy-start(bf16[384,8192]{1,0:T(8,128)(2,1)} %refs_0_.1) | copy-start | bytes 18874372
  12.7 5.1 %collective-permute-start.2 = (bf16[384,128]{1,0:T(8,128)(2,1)S(1)}, bf16[384,128]{1,0:T(8,128)(2,1)S(1)}, u32[]{:S(2)}, u32[]{:S(2)}) collective-permute-start(bf16[384,128]{1,0:T(8,128)(2,1)S(1)} %collective-permute-done.1.refs_6_.refs_3_.refs_4_.refs_2_), channel_id=1, source_target_pairs={{0,1},{1,0},{2,3},{3,2},{4,5},{5,4},{6,7},{7,6},{8,9},{9,8},{10,11... | collective-permute-start | bytes 294920 | tf_op jit(solution)/shard_map/ppermute | solution.py:584
  14.6 4.6 %collective-permute-start.5 = (bf16[384,128]{1,0:T(8,128)(2,1)S(1)}, bf16[384,128]{1,0:T(8,128)(2,1)S(1)}, u32[]{:S(2)}, u32[]{:S(2)}) collective-permute-start(bf16[384,128]{1,0:T(8,128)(2,1)S(1)} %collective-permute-done.3.refs_7_.refs_4_.refs_5_), channel_id=1, source_target_pairs={{0,1},{1,0},{2,3},{3,2},{4,5},{5,4},{6,7},{7,6},{8,9},{9,8},{10,11... | collective-permute-start | bytes 294920 | tf_op jit(solution)/shard_map/ppermute | solution.py:584
  15.9 25.8 %slice-start = ((s8[8388608]{0:T(1024)(128)(4,1)}), s8[4194304]{0:T(1024)(128)(4,1)S(1)}, s32[]{:S(2)}) async-start(s8[8388608]{0:T(1024)(128)(4,1)} %bitcast.10), calls=%async_computation | async-start | bytes 8388608
  16.0 25.7 %slice-start.1 = ((s8[8388608]{0:T(1024)(128)(4,1)}), s8[4194304]{0:T(1024)(128)(4,1)S(1)}, s32[]{:S(2)}) async-start(s8[8388608]{0:T(1024)(128)(4,1)} %bitcast.10), calls=%async_computation.1 | async-start | bytes 8388608
  19.7 5.8 %collective-permute-start.6 = (bf16[400,256]{1,0:T(8,128)(2,1)S(1)}, bf16[400,256]{1,0:T(8,128)(2,1)S(1)}, u32[]{:S(2)}, u32[]{:S(2)}) collective-permute-start(bf16[400,256]{1,0:T(8,128)(2,1)S(1)} %get-tuple-element.75.refs_6_), channel_id=1, source_target_pairs={{0,1},{1,0},{2,3},{3,2},{4,5},{5,4},{6,7},{7,6},{8,9},{9,8},{10,11... | collective-permute-start | bytes 614408 | tf_op jit(solution)/shard_map/ppermute | solution.py:584
  25.6 16.1 %collective-permute-start.9 = (bf16[400,128]{1,0:T(8,128)(2,1)S(1)}, bf16[400,128]{1,0:T(8,128)(2,1)S(1)}, u32[]{:S(2)}, u32[]{:S(2)}) collective-permute-start(bf16[400,128]{1,0:T(8,128)(2,1)S(1)} %merge.2.refs_2_.refs_6_), channel_id=1, source_target_pairs={{0,2},{1,3},{2,0},{3,1},{4,6},{5,7},{6,4},{7,5},{8,10},{9,11},{10,... | collective-permute-start | bytes 307208 | tf_op jit(solution)/shard_map/ppermute | solution.py:584
  33.8 7.8 %collective-permute-start.10 = (bf16[400,128]{1,0:T(8,128)(2,1)S(1)}, bf16[400,128]{1,0:T(8,128)(2,1)S(1)}, u32[]{:S(2)}, u32[]{:S(2)}) collective-permute-start(bf16[400,128]{1,0:T(8,128)(2,1)S(1)} %get-tuple-element.78.refs_5_), channel_id=1, source_target_pairs={{0,1},{1,0},{2,3},{3,2},{4,5},{5,4},{6,7},{7,6},{8,9},{9,8},{10,11... | collective-permute-start | bytes 307208 | tf_op jit(solution)/shard_map/ppermute | solution.py:584
  38.8 6.1 %collective-permute-start.7 = (bf16[384,128]{1,0:T(8,128)(2,1)S(1)}, bf16[384,128]{1,0:T(8,128)(2,1)S(1)}, u32[]{:S(2)}, u32[]{:S(2)}) collective-permute-start(bf16[384,128]{1,0:T(8,128)(2,1)S(1)} %merge.3.refs_7_), channel_id=1, source_target_pairs={{0,2},{1,3},{2,0},{3,1},{4,6},{5,7},{6,4},{7,5},{8,10},{9,11},{10,... | collective-permute-start | bytes 294920 | tf_op jit(solution)/shard_map/ppermute | solution.py:584
  38.8 6.1 %collective-permute-start.8 = (bf16[384,128]{1,0:T(8,128)(2,1)S(1)}, bf16[384,128]{1,0:T(8,128)(2,1)S(1)}, u32[]{:S(2)}, u32[]{:S(2)}) collective-permute-start(bf16[384,128]{1,0:T(8,128)(2,1)S(1)} %get-tuple-element.79.refs_6_), channel_id=1, source_target_pairs={{0,1},{1,0},{2,3},{3,2},{4,5},{5,4},{6,7},{7,6},{8,9},{9,8},{10,11... | collective-permute-start | bytes 294920 | tf_op jit(solution)/shard_map/ppermute | solution.py:584
  43.2 3.3 %collective-permute-start.11 = (bf16[4128,128]{1,0:T(8,128)(2,1)S(1)}, bf16[4128,128]{1,0:T(8,128)(2,1)S(1)}, u32[]{:S(2)}, u32[]{:S(2)}) collective-permute-start(bf16[4128,128]{1,0:T(8,128)(2,1)S(1)} %get-tuple-element.91), channel_id=1, source_target_pairs={{0,4},{4,0},{8,12},{12,8},{16,20},{20,16},{24,28},{28,24},{1,5},{5... | collective-permute-start | bytes 3170312 | tf_op jit(solution)/shard_map/ppermute | solution.py:581
  46.5 4.1 %collective-permute-start.12 = (bf16[4096,128]{1,0:T(8,128)(2,1)S(1)}, bf16[4096,128]{1,0:T(8,128)(2,1)S(1)}, u32[]{:S(2)}, u32[]{:S(2)}) collective-permute-start(bf16[4096,128]{1,0:T(8,128)(2,1)S(1)} %get-tuple-element.94), channel_id=1, source_target_pairs={{0,4},{4,0},{8,12},{12,8},{16,20},{20,16},{24,28},{28,24},{1,5},{5... | collective-permute-start | bytes 3145736 | tf_op jit(solution)/shard_map/ppermute | solution.py:581
  46.7 9.3 %collective-permute-start.14 = (bf16[1056,128]{1,0:T(8,128)(2,1)S(1)}, bf16[1056,128]{1,0:T(8,128)(2,1)S(1)}, u32[]{:S(2)}, u32[]{:S(2)}) collective-permute-start(bf16[1056,128]{1,0:T(8,128)(2,1)S(1)} %get-tuple-element.98), channel_id=1, source_target_pairs={{0,8},{4,12},{8,0},{12,4},{16,24},{20,28},{24,16},{28,20},{1,9},{5... | collective-permute-start | bytes 811016 | tf_op jit(solution)/shard_map/ppermute | solution.py:581
  47.5 8.8 %collective-permute-start.15 = (bf16[1056,128]{1,0:T(8,128)(2,1)S(1)}, bf16[1056,128]{1,0:T(8,128)(2,1)S(1)}, u32[]{:S(2)}, u32[]{:S(2)}) collective-permute-start(bf16[1056,128]{1,0:T(8,128)(2,1)S(1)} %get-tuple-element.100), channel_id=1, source_target_pairs={{0,16},{4,20},{8,24},{12,28},{16,0},{20,4},{24,8},{28,12},{1,17},{... | collective-permute-start | bytes 811016 | tf_op jit(solution)/shard_map/ppermute | solution.py:581
  50.5 1.2 %collective-permute-start.13 = (f32[16,128]{1,0:T(8,128)S(1)}, f32[16,128]{1,0:T(8,128)S(1)}, u32[]{:S(2)}, u32[]{:S(2)}) collective-permute-start(f32[16,128]{1,0:T(8,128)S(1)} %get-tuple-element.95.refs_2_), channel_id=1, source_target_pairs={{0,4},{4,0},{8,12},{12,8},{16,20},{20,16},{24,28},{28,24},{1,5},{5... | collective-permute-start | bytes 24584 | tf_op jit(solution)/shard_map/ppermute | solution.py:581
  52.0 11.3 %collective-permute-start.16 = (bf16[1040,128]{1,0:T(8,128)(2,1)S(1)}, bf16[1040,128]{1,0:T(8,128)(2,1)S(1)}, u32[]{:S(2)}, u32[]{:S(2)}) collective-permute-start(bf16[1040,128]{1,0:T(8,128)(2,1)S(1)} %get-tuple-element.106), channel_id=1, source_target_pairs={{0,8},{4,12},{8,0},{12,4},{16,24},{20,28},{24,16},{28,20},{1,9},{5... | collective-permute-start | bytes 798728 | tf_op jit(solution)/shard_map/ppermute | solution.py:581
  54.1 9.3 %collective-permute-start.17 = (bf16[1024,128]{1,0:T(8,128)(2,1)S(1)}, bf16[1024,128]{1,0:T(8,128)(2,1)S(1)}, u32[]{:S(2)}, u32[]{:S(2)}) collective-permute-start(bf16[1024,128]{1,0:T(8,128)(2,1)S(1)} %get-tuple-element.108), channel_id=1, source_target_pairs={{0,16},{4,20},{8,24},{12,28},{16,0},{20,4},{24,8},{28,12},{1,17},{... | collective-permute-start | bytes 786440 | tf_op jit(solution)/shard_map/ppermute | solution.py:581
  56.4 10.3 %collective-permute-start.22 = (bf16[544,128]{1,0:T(8,128)(2,1)S(1)}, bf16[544,128]{1,0:T(8,128)(2,1)S(1)}, u32[]{:S(2)}, u32[]{:S(2)}) collective-permute-start(bf16[544,128]{1,0:T(8,128)(2,1)S(1)} %get-tuple-element.121), channel_id=1, source_target_pairs={{0,16},{4,20},{8,24},{12,28},{16,0},{20,4},{24,8},{28,12},{1,17},{... | collective-permute-start | bytes 417800 | tf_op jit(solution)/shard_map/ppermute | solution.py:581
  59.0 7.7 %collective-permute-start.23 = (bf16[512,128]{1,0:T(8,128)(2,1)S(1)}, bf16[512,128]{1,0:T(8,128)(2,1)S(1)}, u32[]{:S(2)}, u32[]{:S(2)}) collective-permute-start(bf16[512,128]{1,0:T(8,128)(2,1)S(1)} %get-tuple-element.123), channel_id=1, source_target_pairs={{0,8},{4,12},{8,0},{12,4},{16,24},{20,28},{24,16},{28,20},{1,9},{5... | collective-permute-start | bytes 393224 | tf_op jit(solution)/shard_map/ppermute | solution.py:581
  63.6 6.0 %collective-permute-start.18 = (bf16[528,128]{1,0:T(8,128)(2,1)S(1)}, bf16[528,128]{1,0:T(8,128)(2,1)S(1)}, u32[]{:S(2)}, u32[]{:S(2)}) collective-permute-start(bf16[528,128]{1,0:T(8,128)(2,1)S(1)} %get-tuple-element.112), channel_id=1, source_target_pairs={{0,16},{4,20},{8,24},{12,28},{16,0},{20,4},{24,8},{28,12},{1,17},{... | collective-permute-start | bytes 405512 | tf_op jit(solution)/shard_map/ppermute | solution.py:581
  64.7 5.0 %collective-permute-start.19 = (bf16[512,128]{1,0:T(8,128)(2,1)S(1)}, bf16[512,128]{1,0:T(8,128)(2,1)S(1)}, u32[]{:S(2)}, u32[]{:S(2)}) collective-permute-start(bf16[512,128]{1,0:T(8,128)(2,1)S(1)} %get-tuple-element.114), channel_id=1, source_target_pairs={{0,8},{4,12},{8,0},{12,4},{16,24},{20,28},{24,16},{28,20},{1,9},{5... | collective-permute-start | bytes 393224 | tf_op jit(solution)/shard_map/ppermute | solution.py:581
  66.8 6.2 %collective-permute-start.24 = (bf16[544,128]{1,0:T(8,128)(2,1)S(1)}, bf16[544,128]{1,0:T(8,128)(2,1)S(1)}, u32[]{:S(2)}, u32[]{:S(2)}) collective-permute-start(bf16[544,128]{1,0:T(8,128)(2,1)S(1)} %get-tuple-element.125), channel_id=1, source_target_pairs={{0,1},{1,0},{2,3},{3,2},{4,5},{5,4},{6,7},{7,6},{8,9},{9,8},{10,11... | collective-permute-start | bytes 417800 | tf_op jit(solution)/shard_map/ppermute | solution.py:584
  69.8 5.6 %collective-permute-start.20 = (bf16[528,128]{1,0:T(8,128)(2,1)S(1)}, bf16[528,128]{1,0:T(8,128)(2,1)S(1)}, u32[]{:S(2)}, u32[]{:S(2)}) collective-permute-start(bf16[528,128]{1,0:T(8,128)(2,1)S(1)} %get-tuple-element.117), channel_id=1, source_target_pairs={{0,1},{1,0},{2,3},{3,2},{4,5},{5,4},{6,7},{7,6},{8,9},{9,8},{10,11... | collective-permute-start | bytes 405512 | tf_op jit(solution)/shard_map/ppermute | solution.py:584
  73.0 8.4 %collective-permute-start.25 = (bf16[288,128]{1,0:T(8,128)(2,1)S(1)}, bf16[288,128]{1,0:T(8,128)(2,1)S(1)}, u32[]{:S(2)}, u32[]{:S(2)}) collective-permute-start(bf16[288,128]{1,0:T(8,128)(2,1)S(1)} %get-tuple-element.127), channel_id=1, source_target_pairs={{0,2},{1,3},{2,0},{3,1},{4,6},{5,7},{6,4},{7,5},{8,10},{9,11},{10,... | collective-permute-start | bytes 221192 | tf_op jit(solution)/shard_map/ppermute | solution.py:584
  75.5 5.9 %collective-permute-start.21 = (bf16[272,128]{1,0:T(8,128)(2,1)S(1)}, bf16[272,128]{1,0:T(8,128)(2,1)S(1)}, u32[]{:S(2)}, u32[]{:S(2)}) collective-permute-start(bf16[272,128]{1,0:T(8,128)(2,1)S(1)} %get-tuple-element.120), channel_id=1, source_target_pairs={{0,2},{1,3},{2,0},{3,1},{4,6},{5,7},{6,4},{7,5},{8,10},{9,11},{10,... | collective-permute-start | bytes 208904 | tf_op jit(solution)/shard_map/ppermute | solution.py:584
  (2 other events, 2.5 us)
